TPU v7x, 32 devices: a whole 2x2x4 slice. The times are simulated.
32 devices in a mesh: mode: 4 (over y, x), mer: 8 (over z, core).
Axes of the slice: x: 2, y: 2, z: 4, core: 2. Of those that a mesh axis runs over, the one named last changes fastest.
Arguments:
- mode_fields: bfloat16 [12, 128, 2, 16384], P(None, 'mode', None, 'mer'), may hold values from -0.5 to 0.5
- radius: float32 [16384], P('mer'), may hold values from 1 to 4
- radial_blocks: bfloat16 [5, 64, 16384], P(None, None, 'mer'), may hold values from -6 to 6
- axial_blocks: bfloat16 [5, 64, 16384], P(None, None, 'mer'), may hold values from -6 to 6
- block_columns: int32 [256, 5], P('mer'), may hold values from 0 to 39, as said below
- interface_nodes: int32 [16, 256], P('mer'), may hold values from 0 to 2047, as said below
Outputs:
- induction: float32 [3, 128, 2, 16384], P(None, 'mode', None, 'mer')
- momentum: float32 [3, 128, 2, 16384], P(None, 'mode', None, 'mer')
Inputs may be any that keep to these rules, and one draw needn't show every extreme that they name: `block_columns`: indices into the extended list of a subdomain's block row: its 2048 nodes, then the 256 nodes received from the previous subdomain, then the 256 from the next, counted in blocks of 64. `interface_nodes`: row 2 d lists the local nodes subdomain d sends to subdomain d - 1, row 2 d + 1 those it sends to d + 1; each row holds 256 distinct local node indices.
All inputs are finite; a program needn't handle non-finite values.
Results may differ from a plain program's by a relative error of at most 0.0057.
Values may be sent and summed in bfloat16 or wider, within the bound.
No kernel may reach another device: no remote copies, remote signals or barrier semaphores. Data moves between devices by JAX's collectives and lax.ppermute only.
A program may use at most 64 MiB of HBM per device.

v0:
```python
import functools
import math

import jax
import jax.numpy as jnp
import ml_dtypes
import numpy as np
from jax import lax
from jax.experimental import pallas as pl
from jax.experimental.pallas import tpu as pltpu
from jax.sharding import PartitionSpec as P

M = 128
THETA = 256
BLK = 64
NNZB = 5
LANES = 128
VMEM_LIMIT = 40 * 1024 * 1024


def params():
    return pltpu.CompilerParams(vmem_limit_bytes=VMEM_LIMIT)


def vmem():
    return pl.BlockSpec(memory_space=pltpu.VMEM)


def cost(flops, read_written):
    return pl.CostEstimate(flops=int(flops), bytes_accessed=int(read_written), transcendentals=0)


def dest_of(me, step, count):
    if count & (count - 1) == 0:
        return jnp.bitwise_xor(me, step)
    return lax.rem(me + step, count)


def source_of(me, step, count):
    if count & (count - 1) == 0:
        return jnp.bitwise_xor(me, step)
    return lax.rem(me + count - step, count)


def exchange(pieces):
    count = len(pieces)
    power = count & (count - 1) == 0
    received = [pieces[0]]
    for step in range(1, count):
        pairs = [(i, i ^ step if power else (i + step) % count) for i in range(count)]
        received.append(lax.ppermute(pieces[step], "mode", pairs))
    return received


def from_behind(value, axis, steps):
    count = lax.axis_size(axis)
    initial, last = (max(0, -steps), min(count, count - steps))
    return lax.ppermute(value, axis, [(source, source + steps) for source in range(initial, last)])


def tables(mode_total, angle_total, share_count):
    mode_ids = np.arange(mode_total)
    angle_ids = np.arange(angle_total)
    phase = angle_ids[:, None] * mode_ids[None, :] % angle_total
    angle = phase.astype(np.float32) * np.float32(2.0 * math.pi / angle_total)
    weight = np.where(mode_ids == 0, 1.0, 2.0).astype(np.float32)
    cosines = np.cos(angle)
    sines = np.sin(angle)
    inverse = np.stack([weight * cosines, -weight * sines], axis=-1).astype(ml_dtypes.bfloat16)
    forward = np.stack([cosines.T, -sines.T], axis=1) / np.float32(angle_total)
    forward = forward.reshape(share_count, mode_total // share_count, 2, angle_total)
    forward = forward.transpose(0, 2, 1, 3).reshape(2 * mode_total, angle_total).astype(ml_dtypes.bfloat16)
    return (inverse.reshape(angle_total, 2 * mode_total), forward)


def pack_kernel(count, tiles, x_ref, *out_refs):
    me = lax.axis_index("mode")
    for step in range(count):
        share = dest_of(me, step, count)
        for t in range(tiles):
            start = pl.multiple_of((share * tiles + t) * LANES, LANES)
            out_refs[step][0, t] = x_ref[0, :, :, pl.ds(start, LANES)]


def pack(fields, first, components, count):
    _, mode_count, _, width = fields.shape
    tiles = width // count // LANES
    shape = (components, tiles, mode_count, 2, LANES)
    size = components * mode_count * 2 * width * 2
    return pl.pallas_call(
        functools.partial(pack_kernel, count, tiles),
        grid=(components,),
        in_specs=[pl.BlockSpec((1, mode_count, 2, width), lambda c: (c + first, 0, 0, 0))],
        out_specs=[pl.BlockSpec((1,) + shape[1:], lambda c: (c, 0, 0, 0, 0))] * count,
        out_shape=[jax.ShapeDtypeStruct(shape, jnp.bfloat16)] * count,
        compiler_params=params(),
        cost_estimate=cost(0, 2 * size),
    )(fields)


def cross(a, b):
    return [a[1] * b[2] - a[2] * b[1], a[2] * b[0] - a[0] * b[2], a[0] * b[1] - a[1] * b[0]]


def to_physical(count, in_refs, inverse, x_ref, store):
    me = lax.axis_index("mode")
    components, tiles, rows, _ = in_refs[0].shape
    for step in range(count):
        at = pl.multiple_of(source_of(me, step, count) * rows, rows)
        for c in range(components):
            for t in range(tiles):
                x_ref[c, pl.ds(at, rows), t * LANES : (t + 1) * LANES] = in_refs[step][c, t]
    for c in range(components):
        store(c, jnp.dot(inverse, x_ref[c], preferred_element_type=jnp.float32))


def to_modes(count, forward_ref, table_ref, product_ref, out_refs):
    me = lax.axis_index("mode")
    components, tiles, rows, _ = out_refs[0].shape
    for step in range(count):
        at = pl.multiple_of(dest_of(me, step, count) * rows, rows)
        table_ref[step * rows : (step + 1) * rows] = forward_ref[pl.ds(at, rows)]
    for c in range(components):
        terms = jnp.dot(table_ref[...], product_ref[c], preferred_element_type=jnp.float32)
        terms = terms.astype(jnp.bfloat16)
        for step in range(count):
            for t in range(tiles):
                out_refs[step][c, t] = terms[step * rows : (step + 1) * rows, t * LANES : (t + 1) * LANES]


CHUNK = 32


def first_kernel(count, *refs):
    in_refs, (inverse_ref, forward_ref) = refs[:count], refs[count : count + 2]
    out_refs, (physical_ref, x_ref, product_ref, table_ref) = refs[count + 2 : 2 * count + 2], refs[2 * count + 2 :]

    def store(c, value):
        physical_ref[c] = value

    to_physical(count, in_refs, inverse_ref[...], x_ref, store)
    for i in range(THETA // CHUNK):
        at = slice(i * CHUNK, (i + 1) * CHUNK)
        velocity = [physical_ref[c, at] for c in range(3)]
        magnetic = [physical_ref[c, at] for c in range(3, 6)]
        energy = 0.5 * (velocity[0] * velocity[0] + velocity[1] * velocity[1] + velocity[2] * velocity[2])
        for c, value in enumerate(cross(velocity, magnetic) + [energy]):
            product_ref[c, at] = value.astype(jnp.bfloat16)
    to_modes(count, forward_ref, table_ref, product_ref, out_refs)


def second_kernel(count, *refs):
    in_refs, (first_ref, inverse_ref, forward_ref) = refs[:count], refs[count : count + 3]
    out_refs, (physical_ref, x_ref, product_ref, table_ref) = refs[count + 3 : 2 * count + 3], refs[2 * count + 3 :]

    def store(c, value):
        physical_ref[c] = value

    to_physical(count, in_refs, inverse_ref[...], x_ref, store)
    for i in range(THETA // CHUNK):
        at = slice(i * CHUNK, (i + 1) * CHUNK)
        velocity = [first_ref[c, at] for c in range(3)]
        magnetic = [first_ref[c, at] for c in range(3, 6)]
        current = [physical_ref[c, at] for c in range(3)]
        vorticity = [physical_ref[c, at] for c in range(3, 6)]
        lorentz = [a + b for a, b in zip(cross(current, magnetic), cross(velocity, vorticity))]
        for c, value in enumerate(lorentz):
            product_ref[c, at] = value.astype(jnp.bfloat16)
    to_modes(count, forward_ref, table_ref, product_ref, out_refs)


def physics(kernel, received, extra, inverse, forward, outputs, keep):
    count = len(received)
    components, tiles, rows, _ = received[0].shape
    group = 2 if tiles % 2 == 0 else 1
    steps = tiles // group
    width = group * LANES
    share = tiles * LANES
    in_block = pl.BlockSpec((components, group, rows, LANES), lambda i: (0, i, 0, 0))
    out_block = pl.BlockSpec((outputs, group, rows, LANES), lambda i: (0, i, 0, 0))
    whole = pl.BlockSpec((THETA, 2 * M), lambda i: (0, 0))
    turned = pl.BlockSpec((2 * M, THETA), lambda i: (0, 0))
    kept = pl.BlockSpec((6, THETA, width), lambda i: (0, 0, i))
    kept_shape = jax.ShapeDtypeStruct((6, THETA, share), jnp.float32)
    scratch = [
        pltpu.VMEM((components, 2 * M, width), jnp.bfloat16),
        pltpu.VMEM((outputs, THETA, width), jnp.bfloat16),
        pltpu.VMEM((2 * M, THETA), jnp.bfloat16),
    ]
    if not keep:
        scratch = [pltpu.VMEM((components, THETA, width), jnp.float32)] + scratch
    out_shape = [jax.ShapeDtypeStruct((outputs, tiles, rows, LANES), jnp.bfloat16)] * count
    flops = 2 * THETA * 2 * M * share * (components + outputs)
    moved = (components + outputs) * share * 2 * M * 2 + 6 * THETA * share * 4
    return pl.pallas_call(
        functools.partial(kernel, count),
        grid=(steps,),
        in_specs=[in_block] * count + [kept] * len(extra) + [whole, turned],
        out_specs=[out_block] * count + ([kept] if keep else []),
        out_shape=out_shape + ([kept_shape] if keep else []),
        scratch_shapes=scratch,
        compiler_params=params(),
        cost_estimate=cost(flops, moved),
    )(*received, *extra, inverse, forward)


def interface_kernel(count, *refs):
    in_refs, (nodes_ref,), (prev_ref, next_ref) = refs[:count], refs[count : count + 1], refs[count + 1 :]
    me = lax.axis_index("mode")
    components, tiles, rows, _ = in_refs[0].shape
    halo = nodes_ref.shape[1]
    totals = [jnp.zeros((components * rows, halo), jnp.float32) for _ in range(2)]
    inner = lax.broadcasted_iota(jnp.int32, (LANES, halo), 0)
    for step in range(count):
        share = source_of(me, step, count)
        for t in range(tiles):
            ids = inner + (share * tiles + t) * LANES
            values = in_refs[step][:, t].reshape(components * rows, LANES)
            for way in range(2):
                chosen = jnp.where(ids == nodes_ref[way : way + 1, :], 1.0, 0.0).astype(jnp.bfloat16)
                totals[way] += jnp.dot(values, chosen, preferred_element_type=jnp.float32)
    for out_ref, total in zip((prev_ref, next_ref), totals):
        picked = total.astype(jnp.bfloat16)
        for c in range(components):
            for t in range(halo // LANES):
                out_ref[c, t] = picked[c * rows : (c + 1) * rows, t * LANES : (t + 1) * LANES]


def interface(received, interface_nodes):
    count = len(received)
    components, tiles, rows, _ = received[0].shape
    halo = interface_nodes.shape[1]
    shape = jax.ShapeDtypeStruct((components, halo // LANES, rows, LANES), jnp.bfloat16)
    width = count * tiles * LANES
    return pl.pallas_call(
        functools.partial(interface_kernel, count),
        in_specs=[vmem()] * (count + 1),
        out_specs=[vmem()] * 2,
        out_shape=[shape] * 2,
        compiler_params=params(),
        cost_estimate=cost(2 * components * rows * width * 2 * halo, components * rows * width * 4),
    )(*received, interface_nodes)


def derive_kernel(count, *refs):
    in_refs = refs[:count]
    prev_ref, next_ref, radial_ref, axial_ref, radius_ref, columns_ref = refs[count : count + 6]
    induction_ref, momentum_ref, extended_ref = refs[count + 6 :]
    me = lax.axis_index("mode")
    components, tiles, rows, _ = in_refs[0].shape
    mode_count = rows // 2
    node_tiles = count * tiles
    halo_tiles = prev_ref.shape[1]
    for step in range(count):
        share = source_of(me, step, count)
        for t in range(tiles):
            extended_ref[share * tiles + t] = in_refs[step][:, t].reshape(components * rows, LANES)
    for t in range(halo_tiles):
        extended_ref[node_tiles + t] = prev_ref[:, t].reshape(components * rows, LANES)
        extended_ref[node_tiles + halo_tiles + t] = next_ref[:, t].reshape(components * rows, LANES)
    modes = (lax.broadcasted_iota(jnp.int32, (mode_count, LANES), 0) + me * mode_count).astype(jnp.float32)
    lane = lax.broadcasted_iota(jnp.int32, (1, 2 * LANES), 1)
    in_first = jnp.where(lax.rem(lane, LANES) < BLK, 1.0, 0.0)
    in_half = [in_first, 1.0 - in_first]

    def rotated(values):
        return jnp.concatenate([-modes * values[mode_count:], modes * values[:mode_count]], axis=0)

    def pair(b, carry):
        here = pl.ds(pl.multiple_of(b * LANES, LANES), LANES)
        total = jnp.zeros((components * rows, 2 * LANES), jnp.float32)
        for k in range(NNZB):
            weights = jnp.concatenate([radial_ref[k, :, here], axial_ref[k, :, here]], axis=1)
            left, right = [], []
            for half in range(2):
                column = columns_ref[2 * b + half, k]
                odd = lax.rem(column, 2).astype(jnp.float32)
                left.append(extended_ref[lax.div(column, 2)])
                right.append(weights * (in_half[half] * (1.0 - odd)).astype(jnp.bfloat16))
                right.append(weights * (in_half[half] * odd).astype(jnp.bfloat16))
            total += jnp.dot(
                jnp.concatenate(left, axis=1),
                jnp.concatenate(right, axis=0),
                preferred_element_type=jnp.float32,
            )
        along_r = [total[c * rows : (c + 1) * rows, :LANES] for c in range(components)]
        along_z = [total[c * rows : (c + 1) * rows, LANES:] for c in range(components)]
        values = [extended_ref[b, c * rows : (c + 1) * rows].astype(jnp.float32) for c in range(components)]
        inv_radius = 1.0 / radius_ref[:, here]
        induction = [
            rotated(values[2]) * inv_radius - along_z[1],
            along_z[0] - along_r[2],
            along_r[1] + values[1] * inv_radius - rotated(values[0]) * inv_radius,
        ]
        stride = 2 * node_tiles
        for i, value in enumerate(induction):
            for p in range(2):
                induction_ref[pl.ds(i * mode_count * stride + 2 * b + p, mode_count, stride=stride), :] = value[
                    p * mode_count : (p + 1) * mode_count
                ]
        momentum_ref[0, b] = along_r[3]
        momentum_ref[1, b] = rotated(values[3]) * inv_radius
        momentum_ref[2, b] = along_z[3]
        return carry

    lax.fori_loop(0, node_tiles, pair, 0)


def derive(received, from_prev, from_next, radial_blocks, axial_blocks, radius, columns):
    count = len(received)
    components, tiles, rows, _ = received[0].shape
    node_tiles = count * tiles
    halo_tiles = from_prev.shape[1]
    out_rows = 3 * rows * node_tiles
    return pl.pallas_call(
        functools.partial(derive_kernel, count),
        in_specs=[vmem()] * (count + 5) + [pl.BlockSpec(memory_space=pltpu.SMEM)],
        out_specs=[vmem()] * 2,
        out_shape=[
            jax.ShapeDtypeStruct((out_rows, LANES), jnp.float32),
            jax.ShapeDtypeStruct((3, node_tiles, rows, LANES), jnp.float32),
        ],
        scratch_shapes=[pltpu.VMEM((node_tiles + 2 * halo_tiles, components * rows, LANES), jnp.bfloat16)],
        compiler_params=params(),
        cost_estimate=cost(
            2 * components * rows * node_tiles * 2 * LANES * 2 * LANES * NNZB,
            8 * out_rows * LANES + 4 * NNZB * BLK * node_tiles * LANES,
        ),
    )(*received, from_prev, from_next, radial_blocks, axial_blocks, radius, columns)


def momentum_kernel(count, *refs):
    in_refs, (gradient_ref, out_ref) = refs[:count], refs[count:]
    me = lax.axis_index("mode")
    _, tiles, rows, _ = in_refs[0].shape
    mode_count = rows // 2
    stride = 2 * count * tiles
    for step in range(count):
        share = source_of(me, step, count)
        for t in range(tiles):
            at = share * tiles + t
            value = in_refs[step][0, t].astype(jnp.float32) - gradient_ref[0, at]
            for p in range(2):
                out_ref[pl.ds(2 * at + p, mode_count, stride=stride), :] = value[
                    p * mode_count : (p + 1) * mode_count
                ]


def momentum_of(received, gradient):
    count = len(received)
    components, tiles, rows, _ = received[0].shape
    node_tiles = count * tiles
    out_rows = rows * node_tiles
    return pl.pallas_call(
        functools.partial(momentum_kernel, count),
        grid=(components,),
        in_specs=[pl.BlockSpec((1, tiles, rows, LANES), lambda c: (c, 0, 0, 0))] * count
        + [pl.BlockSpec((1, node_tiles, rows, LANES), lambda c: (c, 0, 0, 0))],
        out_specs=pl.BlockSpec((out_rows, LANES), lambda c: (c, 0)),
        out_shape=jax.ShapeDtypeStruct((components * out_rows, LANES), jnp.float32),
        compiler_params=params(),
        cost_estimate=cost(components * out_rows * LANES, components * out_rows * LANES * 10),
    )(*received, gradient)


def whole_output(value, mode_count, width):
    value = value.reshape(3, mode_count, width // LANES, 2, LANES)
    return value.transpose(0, 1, 3, 2, 4).reshape(3, mode_count, 2, width)


def body(mode_fields, radius, radial_blocks, axial_blocks, block_columns, interface_nodes):
    _, mode_count, _, width = mode_fields.shape
    count = lax.axis_size("mode")
    rows = 2 * mode_count
    inverse, forward = tables(M, THETA, count)
    inverse, forward = jnp.asarray(inverse), jnp.asarray(forward)

    def sent(first):
        pieces = exchange(pack(mode_fields, first, 6, count))
        return [piece.reshape(piece.shape[:2] + (rows, LANES)) for piece in pieces]

    flow = sent(0)
    sources = sent(6)
    *terms, physical = physics(first_kernel, flow, [], inverse, forward, 4, True)
    local = exchange(terms)
    toward_prev, toward_next = interface(local, interface_nodes)
    from_prev = from_behind(toward_next, "mer", 1)
    from_next = from_behind(toward_prev, "mer", -1)
    induction, gradient = derive(
        local, from_prev, from_next, radial_blocks, axial_blocks, radius.reshape(1, width), block_columns
    )
    lorentz = exchange(physics(second_kernel, sources, [physical], inverse, forward, 3, False))
    momentum = momentum_of(lorentz, gradient)
    return (whole_output(induction, mode_count, width), whole_output(momentum, mode_count, width))


def solution(mesh):
    placed = (
        P(None, "mode", None, "mer"),
        P("mer"),
        P(None, None, "mer"),
        P(None, None, "mer"),
        P("mer", None),
        P("mer", None),
    )
    return jax.shard_map(
        body,
        mesh=mesh,
        in_specs=placed,
        out_specs=(P(None, "mode", None, "mer"), P(None, "mode", None, "mer")),
        check_vma=False,
    )
```

profile of v0, /device:TPU:1, one launch (start us, length us, event | category | flops | bytes accessed | tf_op | source)
XLA Modules:
  0.0 90.9 jit_solution(4543637573992941275)
XLA Ops:
  0.6 0.0 copy-start
  0.6 1.9 %copy-done = bf16[12,32,2,2048]{3,2,1,0:T(2,128)(2,1)S(1)} copy-done((bf16[12,32,2,2048]{3,2,1,0:T(2,128)(2,1)S(1)}, bf16[12,32,2,2048]{3,2,1,0:T(2,128)(2,1)}, u32[]{:S(2)}) %copy-start) | copy-done | bytes 3145752
  2.5 1.2 %shard_map.95 = (bf16[6,4,32,2,128]{4,3,2,1,0:T(2,128)(2,1)S(1)}, bf16[6,4,32,2,128]{4,3,2,1,0:T(2,128)(2,1)S(1)}, bf16[6,4,32,2,128]{4,3,2,1,0:T(2,128)(2,1)S(1)}, bf16[6,4,32,2,128]{4,3,2,1,0:T(2,128)(2,1)S(1)}) custom-call(bf16[12,32,2,2048]{3,2,1,0:T(2,128)(2,1)S(1)} %copy-done), custom_call_target="tpu_custom_call" | custom-call | bytes 3145728 | tf_op jit(solution)/shard_map/pallas_call | solution.py:90
  3.7 2.1 %collective-permute-start = (bf16[6,4,32,2,128]{4,3,2,1,0:T(2,128)(2,1)S(1)}, bf16[6,4,32,2,128]{4,3,2,1,0:T(2,128)(2,1)S(1)}, u32[]{:S(2)}, u32[]{:S(2)}) collective-permute-start(bf16[6,4,32,2,128]{4,3,2,1,0:T(2,128)(2,1)S(1)} %get-tuple-element.24), channel_id=1, source_target_pairs={{0,8},{8,0},{16,24},{24,16},{1,9},{9,1},{17,25},{25,17},{2,10},{10... | collective-permute-start | bytes 1179656 | tf_op jit(solution)/shard_map/ppermute | solution.py:51
  5.9 1.2 %collective-permute-start.1 = (bf16[6,4,32,2,128]{4,3,2,1,0:T(2,128)(2,1)S(1)}, bf16[6,4,32,2,128]{4,3,2,1,0:T(2,128)(2,1)S(1)}, u32[]{:S(2)}, u32[]{:S(2)}) collective-permute-start(bf16[6,4,32,2,128]{4,3,2,1,0:T(2,128)(2,1)S(1)} %get-tuple-element.25), channel_id=1, source_target_pairs={{0,16},{8,24},{16,0},{24,8},{1,17},{9,25},{17,1},{25,9},{2,18},{10... | collective-permute-start | bytes 1179656 | tf_op jit(solution)/shard_map/ppermute | solution.py:51
  7.1 0.0 collective-permute-start.2
  7.1 7.6 %collective-permute-done = bf16[6,4,32,2,128]{4,3,2,1,0:T(2,128)(2,1)S(1)} collective-permute-done((bf16[6,4,32,2,128]{4,3,2,1,0:T(2,128)(2,1)S(1)}, bf16[6,4,32,2,128]{4,3,2,1,0:T(2,128)(2,1)S(1)}, u32[]{:S(2)}, u32[]{:S(2)}) %collective-permute-start) | collective-permute-done | bytes 393248 | tf_op jit(solution)/shard_map/ppermute | solution.py:51
  14.7 0.8 collective-permute-done.1
  15.5 8.5 %collective-permute-done.2 = bf16[6,4,32,2,128]{4,3,2,1,0:T(2,128)(2,1)S(1)} collective-permute-done((bf16[6,4,32,2,128]{4,3,2,1,0:T(2,128)(2,1)S(1)}, bf16[6,4,32,2,128]{4,3,2,1,0:T(2,128)(2,1)S(1)}, u32[]{:S(2)}, u32[]{:S(2)}) %collective-permute-start.2) | collective-permute-done | bytes 393248 | tf_op jit(solution)/shard_map/ppermute | solution.py:51
  24.1 0.9 copy-done.2
  25.0 0.9 copy-done.4
  25.9 2.1 %shard_map.96 = (bf16[4,4,64,128]{3,2,1,0:T(8,128)(2,1)S(1)}, bf16[4,4,64,128]{3,2,1,0:T(8,128)(2,1)S(1)}, bf16[4,4,64,128]{3,2,1,0:T(8,128)(2,1)S(1)}, bf16[4,4...) custom-call(bf16[6,4,64,128]{3,2,1,0:T(8,128)(2,1)S(1)} %bitcast.20, bf16[6,4,64,128]{3,2,1,0:T(8,128)(2,1)S(1)} %bitcast.21, ...), custom_call_target="tpu_custom_call" | custom-call | flops 671088640 | bytes 5767168 | tf_op jit(solution)/shard_map/pallas_call | solution.py:195
  28.0 0.0 copy-start.16
  28.0 0.0 copy-start.15
  28.0 1.2 %collective-permute-start.3 = (bf16[4,4,64,128]{3,2,1,0:T(8,128)(2,1)S(1)}, bf16[4,4,64,128]{3,2,1,0:T(8,128)(2,1)S(1)}, u32[]{:S(2)}, u32[]{:S(2)}) collective-permute-start(bf16[4,4,64,128]{3,2,1,0:T(8,128)(2,1)S(1)} %get-tuple-element.28), channel_id=1, source_target_pairs={{0,8},{8,0},{16,24},{24,16},{1,9},{9,1},{17,25},{25,17},{2,10},{10... | collective-permute-start | bytes 786440 | tf_op jit(solution)/shard_map/ppermute | solution.py:51
  29.3 0.0 copy-done.1
  29.3 2.7 %shard_map.99 = (bf16[6,4,32,2,128]{4,3,2,1,0:T(2,128)(2,1)S(1)}, bf16[6,4,32,2,128]{4,3,2,1,0:T(2,128)(2,1)}, bf16[6,4,32,2,128]{4,3,2,1,0:T(2,128)(2,1)}, bf16[6,4,32,2,128]{4,3,2,1,0:T(2,128)(2,1)}) custom-call(bf16[12,32,2,2048]{3,2,1,0:T(2,128)(2,1)S(1)} %copy-done.1), custom_call_target="tpu_custom_call" | custom-call | bytes 3145728 | tf_op jit(solution)/shard_map/pallas_call | solution.py:90
  32.0 0.3 collective-permute-start.8
  32.3 0.3 collective-permute-start.9
  32.6 2.1 %collective-permute-start.10 = (bf16[6,4,32,2,128]{4,3,2,1,0:T(2,128)(2,1)}, bf16[6,4,32,2,128]{4,3,2,1,0:T(2,128)(2,1)}, u32[]{:S(2)}, u32[]{:S(2)}) collective-permute-start(bf16[6,4,32,2,128]{4,3,2,1,0:T(2,128)(2,1)} %get-tuple-element.37), channel_id=1, source_target_pairs={{0,24},{8,16},{16,8},{24,0},{1,25},{9,17},{17,9},{25,1},{2,26},{10... | collective-permute-start | bytes 1179656 | tf_op jit(solution)/shard_map/ppermute | solution.py:51
  34.6 0.3 collective-permute-start.4
  34.9 0.0 collective-permute-done.3.refs_1_
  34.9 1.2 %collective-permute-start.5 = (bf16[4,4,64,128]{3,2,1,0:T(8,128)(2,1)S(1)}, bf16[4,4,64,128]{3,2,1,0:T(8,128)(2,1)S(1)}, u32[]{:S(2)}, u32[]{:S(2)}) collective-permute-start(bf16[4,4,64,128]{3,2,1,0:T(8,128)(2,1)S(1)} %get-tuple-element.30), channel_id=1, source_target_pairs={{0,24},{8,16},{16,8},{24,0},{1,25},{9,17},{17,9},{25,1},{2,26},{10... | collective-permute-start | bytes 786440 | tf_op jit(solution)/shard_map/ppermute | solution.py:51
  36.1 24.4 %collective-permute-done.4.refs_2_ = bf16[4,4,64,128]{3,2,1,0:T(8,128)(2,1)S(1)} collective-permute-done((bf16[4,4,64,128]{3,2,1,0:T(8,128)(2,1)S(1)}, bf16[4,4,64,128]{3,2,1,0:T(8,128)(2,1)S(1)}, u32[]{:S(2)}, u32[]{:S(2)}) %collective-permute-start.4) | collective-permute-done | bytes 262176 | tf_op jit(solution)/shard_map/ppermute | solution.py:51
  60.5 0.0 collective-permute-done.5.refs_3_
  60.5 0.0 copy-done.15
  60.6 1.9 %shard_map.97 = (bf16[4,2,64,128]{3,2,1,0:T(8,128)(2,1)}, bf16[4,2,64,128]{3,2,1,0:T(8,128)(2,1)}) custom-call(bf16[4,4,64,128]{3,2,1,0:T(8,128)(2,1)S(1)} %get-tuple-element.27.refs_0_, bf16[4,4,64,128]{3,2,1,0:T(8,128)(2,1)S(1)} %collective-permute-done.3.refs_1_, bf16[4,4,64,128]{3,2,1,0:T(8,128)(2,1)S(1)} %collective-permute-done.4.refs_2_, ...), custom_call_target="tpu_custom_call" | custom-call | flops 536870912 | bytes 2097152 | tf_op jit(solution)/shard_map/pallas_call | solution.py:235
  62.5 6.2 %collective-permute-start.6 = (bf16[4,2,64,128]{3,2,1,0:T(8,128)(2,1)}, bf16[4,2,64,128]{3,2,1,0:T(8,128)(2,1)}, u32[]{:S(2)}, u32[]{:S(2)}) collective-permute-start(bf16[4,2,64,128]{3,2,1,0:T(8,128)(2,1)} %get-tuple-element.31), channel_id=1, source_target_pairs={{0,1},{1,2},{2,3},{3,4},{4,5},{5,6},{6,7},{8,9},{9,10},{10,11},{11... | collective-permute-start | bytes 393224 | tf_op jit(solution)/shard_map/ppermute | solution.py:58
  68.7 1.9 %collective-permute-start.7 = (bf16[4,2,64,128]{3,2,1,0:T(8,128)(2,1)}, bf16[4,2,64,128]{3,2,1,0:T(8,128)(2,1)}, u32[]{:S(2)}, u32[]{:S(2)}) collective-permute-start(bf16[4,2,64,128]{3,2,1,0:T(8,128)(2,1)} %get-tuple-element.32), channel_id=1, source_target_pairs={{1,0},{2,1},{3,2},{4,3},{5,4},{6,5},{7,6},{9,8},{10,9},{11,10},{12... | collective-permute-start | bytes 393224 | tf_op jit(solution)/shard_map/ppermute | solution.py:58
  70.7 0.8 copy.10.refs_9_
  71.4 0.0 collective-permute-done.8
  71.5 0.0 collective-permute-done.9
  71.5 0.0 collective-permute-done.10
  71.5 0.0 copy-start.3
  71.5 0.9 copy-done.3
  72.4 0.9 copy-done.5
  73.3 0.0 copy-start.14
  73.3 3.2 %shard_map.100 = (bf16[3,4,64,128]{3,2,1,0:T(8,128)(2,1)S(1)}, bf16[3,4,64,128]{3,2,1,0:T(8,128)(2,1)S(1)}, bf16[3,4,64,128]{3,2,1,0:T(8,128)(2,1)S(1)}, bf16[3,4,64,128]{3,2,1,0:T(8,128)(2,1)S(1)}) custom-call(bf16[6,4,64,128]{3,2,1,0:T(8,128)(2,1)S(1)} %bitcast.19, bf16[6,4,64,128]{3,2,1,0:T(8,128)(2,1)} %bitcast.9.refs_1_, ...), custom_call_target="tpu_custom_call" | custom-call | flops 603979776 | bytes 5505024 | tf_op jit(solution)/shard_map/pallas_call | solution.py:195
  76.5 1.2 %collective-permute-start.11 = (bf16[3,4,64,128]{3,2,1,0:T(8,128)(2,1)S(1)}, bf16[3,4,64,128]{3,2,1,0:T(8,128)(2,1)S(1)}, u32[]{:S(2)}, u32[]{:S(2)}) collective-permute-start(bf16[3,4,64,128]{3,2,1,0:T(8,128)(2,1)S(1)} %get-tuple-element.40), channel_id=1, source_target_pairs={{0,8},{8,0},{16,24},{24,16},{1,9},{9,1},{17,25},{25,17},{2,10},{10... | collective-permute-start | bytes 589832 | tf_op jit(solution)/shard_map/ppermute | solution.py:51
  77.7 0.3 collective-permute-start.12
  78.0 1.2 %collective-permute-start.13 = (bf16[3,4,64,128]{3,2,1,0:T(8,128)(2,1)S(1)}, bf16[3,4,64,128]{3,2,1,0:T(8,128)(2,1)S(1)}, u32[]{:S(2)}, u32[]{:S(2)}) collective-permute-start(bf16[3,4,64,128]{3,2,1,0:T(8,128)(2,1)S(1)} %get-tuple-element.42), channel_id=1, source_target_pairs={{0,24},{8,16},{16,8},{24,0},{1,25},{9,17},{17,9},{25,1},{2,26},{10... | collective-permute-start | bytes 589832 | tf_op jit(solution)/shard_map/ppermute | solution.py:51
  79.2 0.0 collective-permute-done.6.refs_4_
  79.2 0.0 collective-permute-done.7.refs_5_
  79.3 9.0 %shard_map.98 = (f32[3072,128]{1,0:T(8,128)}, f32[3,16,64,128]{3,2,1,0:T(8,128)S(1)}) custom-call(bf16[4,4,64,128]{3,2,1,0:T(8,128)(2,1)S(1)} %copy-done.17, bf16[4,4,64,128]{3,2,1,0:T(8,128)(2,1)S(1)} %copy-done.9, bf16[4,4,64,128]{3,2,1,0:T(8,128)(2,1)S(1)} %copy-done.11, bf16[4,4,64,128]{3,2,1,0:T(8,128)(2,1)S(1)} %copy-done.13, ...), custom_call_target="tpu_custom_call" | custom-call | flops 2684354560 | bytes 5767168 | tf_op jit(solution)/shard_map/pallas_call | solution.py:315
  88.3 0.0 collective-permute-done.11.refs_1_
  88.3 0.0 collective-permute-done.12.refs_2_
  88.3 0.0 collective-permute-done.13.refs_3_
  88.3 2.7 %shard_map.101 = f32[3072,128]{1,0:T(8,128)} custom-call(bf16[3,4,64,128]{3,2,1,0:T(8,128)(2,1)S(1)} %get-tuple-element.39.refs_0_, bf16[3,4,64,128]{3,2,1,0:T(8,128)(2,1)S(1)} %collective-permute-done.11.refs_1_, bf16[3,4,64,128]{3,2,1,0:T(8,128)(2,1)S(1)} %collective-permute-done.12.refs_2_, bf16[3,4,64,128]{3,2,1,0:T(8,128)(2,1)S(1)} %collective-permute-done.13.refs_3_, ...), custom_call_target="tpu_custom_call" | custom-call | flops 393216 | bytes 3932160 | tf_op jit(solution)/shard_map/pallas_call | solution.py:354
  (24 shorter events, 0.0 us)
Async XLA Ops:
  0.6 1.9 %copy-start = (bf16[12,32,2,2048]{3,2,1,0:T(2,128)(2,1)S(1)}, bf16[12,32,2,2048]{3,2,1,0:T(2,128)(2,1)}, u32[]{:S(2)}) copy-start(bf16[12,32,2,2048]{3,2,1,0:T(2,128)(2,1)} %x_ref.3) | copy-start | bytes 9437188
  2.5 26.7 %copy-start.1 = (bf16[12,32,2,2048]{3,2,1,0:T(2,128)(2,1)S(1)}, bf16[12,32,2,2048]{3,2,1,0:T(2,128)(2,1)}, u32[]{:S(2)}) copy-start(bf16[12,32,2,2048]{3,2,1,0:T(2,128)(2,1)} %x_ref.3) | copy-start | bytes 9437188
  3.7 10.9 %collective-permute-start = (bf16[6,4,32,2,128]{4,3,2,1,0:T(2,128)(2,1)S(1)}, bf16[6,4,32,2,128]{4,3,2,1,0:T(2,128)(2,1)S(1)}, u32[]{:S(2)}, u32[]{:S(2)}) collective-permute-start(bf16[6,4,32,2,128]{4,3,2,1,0:T(2,128)(2,1)S(1)} %get-tuple-element.24), channel_id=1, source_target_pairs={{0,8},{8,0},{16,24},{24,16},{1,9},{9,1},{17,25},{25,17},{2,10},{10... | collective-permute-start | bytes 1179656 | tf_op jit(solution)/shard_map/ppermute | solution.py:51
  5.9 9.7 %collective-permute-start.1 = (bf16[6,4,32,2,128]{4,3,2,1,0:T(2,128)(2,1)S(1)}, bf16[6,4,32,2,128]{4,3,2,1,0:T(2,128)(2,1)S(1)}, u32[]{:S(2)}, u32[]{:S(2)}) collective-permute-start(bf16[6,4,32,2,128]{4,3,2,1,0:T(2,128)(2,1)S(1)} %get-tuple-element.25), channel_id=1, source_target_pairs={{0,16},{8,24},{16,0},{24,8},{1,17},{9,25},{17,1},{25,9},{2,18},{10... | collective-permute-start | bytes 1179656 | tf_op jit(solution)/shard_map/ppermute | solution.py:51
  7.1 17.0 %collective-permute-start.2 = (bf16[6,4,32,2,128]{4,3,2,1,0:T(2,128)(2,1)S(1)}, bf16[6,4,32,2,128]{4,3,2,1,0:T(2,128)(2,1)S(1)}, u32[]{:S(2)}, u32[]{:S(2)}) collective-permute-start(bf16[6,4,32,2,128]{4,3,2,1,0:T(2,128)(2,1)S(1)} %get-tuple-element.26), channel_id=1, source_target_pairs={{0,24},{8,16},{16,8},{24,0},{1,25},{9,17},{17,9},{25,1},{2,26},{10... | collective-permute-start | bytes 1179656 | tf_op jit(solution)/shard_map/ppermute | solution.py:51
  24.1 0.9 copy-start.2
  25.0 0.9 copy-start.4
  28.0 32.5 %copy-start.16 = (bf16[4,4,64,128]{3,2,1,0:T(8,128)(2,1)}, bf16[4,4,64,128]{3,2,1,0:T(8,128)(2,1)S(1)}, u32[]{:S(2)}) copy-start(bf16[4,4,64,128]{3,2,1,0:T(8,128)(2,1)S(1)} %get-tuple-element.27.refs_0_) | copy-start | bytes 786436
  28.0 32.5 %copy-start.15 = (s32[2,256]{1,0:T(2,128)S(1)}, s32[2,256]{1,0:T(2,128)}, u32[]{:S(2)}) copy-start(s32[2,256]{1,0:T(2,128)} %refs_4_.2) | copy-start | bytes 6148
  28.0 6.9 %collective-permute-start.3 = (bf16[4,4,64,128]{3,2,1,0:T(8,128)(2,1)S(1)}, bf16[4,4,64,128]{3,2,1,0:T(8,128)(2,1)S(1)}, u32[]{:S(2)}, u32[]{:S(2)}) collective-permute-start(bf16[4,4,64,128]{3,2,1,0:T(8,128)(2,1)S(1)} %get-tuple-element.28), channel_id=1, source_target_pairs={{0,8},{8,0},{16,24},{24,16},{1,9},{9,1},{17,25},{25,17},{2,10},{10... | collective-permute-start | bytes 786440 | tf_op jit(solution)/shard_map/ppermute | solution.py:51
  32.0 39.5 %collective-permute-start.8 = (bf16[6,4,32,2,128]{4,3,2,1,0:T(2,128)(2,1)}, bf16[6,4,32,2,128]{4,3,2,1,0:T(2,128)(2,1)}, u32[]{:S(2)}, u32[]{:S(2)}) collective-permute-start(bf16[6,4,32,2,128]{4,3,2,1,0:T(2,128)(2,1)} %get-tuple-element.35), channel_id=1, source_target_pairs={{0,8},{8,0},{16,24},{24,16},{1,9},{9,1},{17,25},{25,17},{2,10},{10... | collective-permute-start | bytes 1179656 | tf_op jit(solution)/shard_map/ppermute | solution.py:51
  32.3 39.2 %collective-permute-start.9 = (bf16[6,4,32,2,128]{4,3,2,1,0:T(2,128)(2,1)}, bf16[6,4,32,2,128]{4,3,2,1,0:T(2,128)(2,1)}, u32[]{:S(2)}, u32[]{:S(2)}) collective-permute-start(bf16[6,4,32,2,128]{4,3,2,1,0:T(2,128)(2,1)} %get-tuple-element.36), channel_id=1, source_target_pairs={{0,16},{8,24},{16,0},{24,8},{1,17},{9,25},{17,1},{25,9},{2,18},{10... | collective-permute-start | bytes 1179656 | tf_op jit(solution)/shard_map/ppermute | solution.py:51
  32.6 38.9 %collective-permute-start.10 = (bf16[6,4,32,2,128]{4,3,2,1,0:T(2,128)(2,1)}, bf16[6,4,32,2,128]{4,3,2,1,0:T(2,128)(2,1)}, u32[]{:S(2)}, u32[]{:S(2)}) collective-permute-start(bf16[6,4,32,2,128]{4,3,2,1,0:T(2,128)(2,1)} %get-tuple-element.37), channel_id=1, source_target_pairs={{0,24},{8,16},{16,8},{24,0},{1,25},{9,17},{17,9},{25,1},{2,26},{10... | collective-permute-start | bytes 1179656 | tf_op jit(solution)/shard_map/ppermute | solution.py:51
  34.6 25.9 %collective-permute-start.4 = (bf16[4,4,64,128]{3,2,1,0:T(8,128)(2,1)S(1)}, bf16[4,4,64,128]{3,2,1,0:T(8,128)(2,1)S(1)}, u32[]{:S(2)}, u32[]{:S(2)}) collective-permute-start(bf16[4,4,64,128]{3,2,1,0:T(8,128)(2,1)S(1)} %get-tuple-element.29), channel_id=1, source_target_pairs={{0,16},{8,24},{16,0},{24,8},{1,17},{9,25},{17,1},{25,9},{2,18},{10... | collective-permute-start | bytes 786440 | tf_op jit(solution)/shard_map/ppermute | solution.py:51
  34.9 33.8 %copy-start.8 = (bf16[4,4,64,128]{3,2,1,0:T(8,128)(2,1)}, bf16[4,4,64,128]{3,2,1,0:T(8,128)(2,1)S(1)}, u32[]{:S(2)}) copy-start(bf16[4,4,64,128]{3,2,1,0:T(8,128)(2,1)S(1)} %collective-permute-done.3.refs_1_) | copy-start | bytes 786436
  34.9 25.6 %collective-permute-start.5 = (bf16[4,4,64,128]{3,2,1,0:T(8,128)(2,1)S(1)}, bf16[4,4,64,128]{3,2,1,0:T(8,128)(2,1)S(1)}, u32[]{:S(2)}, u32[]{:S(2)}) collective-permute-start(bf16[4,4,64,128]{3,2,1,0:T(8,128)(2,1)S(1)} %get-tuple-element.30), channel_id=1, source_target_pairs={{0,24},{8,16},{16,8},{24,0},{1,25},{9,17},{17,9},{25,1},{2,26},{10... | collective-permute-start | bytes 786440 | tf_op jit(solution)/shard_map/ppermute | solution.py:51
  60.5 8.2 %copy-start.10 = (bf16[4,4,64,128]{3,2,1,0:T(8,128)(2,1)}, bf16[4,4,64,128]{3,2,1,0:T(8,128)(2,1)S(1)}, u32[]{:S(2)}) copy-start(bf16[4,4,64,128]{3,2,1,0:T(8,128)(2,1)S(1)} %collective-permute-done.4.refs_2_) | copy-start | bytes 786436
  60.5 8.2 %copy-start.12 = (bf16[4,4,64,128]{3,2,1,0:T(8,128)(2,1)}, bf16[4,4,64,128]{3,2,1,0:T(8,128)(2,1)S(1)}, u32[]{:S(2)}) copy-start(bf16[4,4,64,128]{3,2,1,0:T(8,128)(2,1)S(1)} %collective-permute-done.5.refs_3_) | copy-start | bytes 786436
  62.5 16.7 %collective-permute-start.6 = (bf16[4,2,64,128]{3,2,1,0:T(8,128)(2,1)}, bf16[4,2,64,128]{3,2,1,0:T(8,128)(2,1)}, u32[]{:S(2)}, u32[]{:S(2)}) collective-permute-start(bf16[4,2,64,128]{3,2,1,0:T(8,128)(2,1)} %get-tuple-element.31), channel_id=1, source_target_pairs={{0,1},{1,2},{2,3},{3,4},{4,5},{5,6},{6,7},{8,9},{9,10},{10,11},{11... | collective-permute-start | bytes 393224 | tf_op jit(solution)/shard_map/ppermute | solution.py:58
  68.7 10.5 %collective-permute-start.7 = (bf16[4,2,64,128]{3,2,1,0:T(8,128)(2,1)}, bf16[4,2,64,128]{3,2,1,0:T(8,128)(2,1)}, u32[]{:S(2)}, u32[]{:S(2)}) collective-permute-start(bf16[4,2,64,128]{3,2,1,0:T(8,128)(2,1)} %get-tuple-element.32), channel_id=1, source_target_pairs={{1,0},{2,1},{3,2},{4,3},{5,4},{6,5},{7,6},{9,8},{10,9},{11,10},{12... | collective-permute-start | bytes 393224 | tf_op jit(solution)/shard_map/ppermute | solution.py:58
  71.5 0.9 copy-start.3
  72.4 0.9 copy-start.5
  73.3 5.9 %copy-start.6 = (bf16[5,64,2048]{2,1,0:T(8,128)(2,1)S(1)}, bf16[5,64,2048]{2,1,0:T(8,128)(2,1)}, u32[]{:S(2)}) copy-start(bf16[5,64,2048]{2,1,0:T(8,128)(2,1)} %refs_6_.2) | copy-start | bytes 3932164
  73.3 5.9 %copy-start.7 = (bf16[5,64,2048]{2,1,0:T(8,128)(2,1)S(1)}, bf16[5,64,2048]{2,1,0:T(8,128)(2,1)}, u32[]{:S(2)}) copy-start(bf16[5,64,2048]{2,1,0:T(8,128)(2,1)} %refs_7_.1) | copy-start | bytes 3932164
  73.3 5.9 %copy-start.9 = (bf16[4,4,64,128]{3,2,1,0:T(8,128)(2,1)S(1)}, bf16[4,4,64,128]{3,2,1,0:T(8,128)(2,1)}, u32[]{:S(2)}) copy-start(bf16[4,4,64,128]{3,2,1,0:T(8,128)(2,1)} %copy-done.8) | copy-start | bytes 786436
  73.3 6.0 %copy-start.11 = (bf16[4,4,64,128]{3,2,1,0:T(8,128)(2,1)S(1)}, bf16[4,4,64,128]{3,2,1,0:T(8,128)(2,1)}, u32[]{:S(2)}) copy-start(bf16[4,4,64,128]{3,2,1,0:T(8,128)(2,1)} %copy-done.10) | copy-start | bytes 786436
  73.3 6.0 %copy-start.13 = (bf16[4,4,64,128]{3,2,1,0:T(8,128)(2,1)S(1)}, bf16[4,4,64,128]{3,2,1,0:T(8,128)(2,1)}, u32[]{:S(2)}) copy-start(bf16[4,4,64,128]{3,2,1,0:T(8,128)(2,1)} %copy-done.12) | copy-start | bytes 786436
  73.3 6.0 %copy-start.14 = (f32[2048]{0:T(1024)S(1)}, f32[2048]{0:T(1024)}, u32[]{:S(2)}) copy-start(f32[2048]{0:T(1024)} %param.9) | copy-start | bytes 24580
  73.3 6.0 %copy-start.17 = (bf16[4,4,64,128]{3,2,1,0:T(8,128)(2,1)S(1)}, bf16[4,4,64,128]{3,2,1,0:T(8,128)(2,1)}, u32[]{:S(2)}) copy-start(bf16[4,4,64,128]{3,2,1,0:T(8,128)(2,1)} %copy-done.16) | copy-start | bytes 786436
  76.5 11.8 %collective-permute-start.11 = (bf16[3,4,64,128]{3,2,1,0:T(8,128)(2,1)S(1)}, bf16[3,4,64,128]{3,2,1,0:T(8,128)(2,1)S(1)}, u32[]{:S(2)}, u32[]{:S(2)}) collective-permute-start(bf16[3,4,64,128]{3,2,1,0:T(8,128)(2,1)S(1)} %get-tuple-element.40), channel_id=1, source_target_pairs={{0,8},{8,0},{16,24},{24,16},{1,9},{9,1},{17,25},{25,17},{2,10},{10... | collective-permute-start | bytes 589832 | tf_op jit(solution)/shard_map/ppermute | solution.py:51
  77.7 10.6 %collective-permute-start.12 = (bf16[3,4,64,128]{3,2,1,0:T(8,128)(2,1)S(1)}, bf16[3,4,64,128]{3,2,1,0:T(8,128)(2,1)S(1)}, u32[]{:S(2)}, u32[]{:S(2)}) collective-permute-start(bf16[3,4,64,128]{3,2,1,0:T(8,128)(2,1)S(1)} %get-tuple-element.41), channel_id=1, source_target_pairs={{0,16},{8,24},{16,0},{24,8},{1,17},{9,25},{17,1},{25,9},{2,18},{10... | collective-permute-start | bytes 589832 | tf_op jit(solution)/shard_map/ppermute | solution.py:51
  78.0 10.3 %collective-permute-start.13 = (bf16[3,4,64,128]{3,2,1,0:T(8,128)(2,1)S(1)}, bf16[3,4,64,128]{3,2,1,0:T(8,128)(2,1)S(1)}, u32[]{:S(2)}, u32[]{:S(2)}) collective-permute-start(bf16[3,4,64,128]{3,2,1,0:T(8,128)(2,1)S(1)} %get-tuple-element.42), channel_id=1, source_target_pairs={{0,24},{8,16},{16,8},{24,0},{1,25},{9,17},{17,9},{25,1},{2,26},{10... | collective-permute-start | bytes 589832 | tf_op jit(solution)/shard_map/ppermute | solution.py:51
where the time goes:
time: 91.2 us; the launch traced here: 90.9 us
  waiting for transfers between devices  41.4 us (45%)
  Pallas kernels  22.8 us (25%)
  starting transfers between devices  19.6 us (21%)
  local copies, waits for them, and re-layouts  6.32 us (7%)
    ppermute x12, waiting for transfers between devices, exchange(): received.append(lax.ppermute(pieces[step], 'mode', pairs))  41.4 us
    ppermute x12, starting transfers between devices, exchange(): received.append(lax.ppermute(pieces[step], 'mode', pairs))  11.4 us
    pallas_call x1, Pallas kernels, derive(): pl.pallas_call(functools.partial(derive_kernel, count), in_specs=[vmem()]...  8.99 us
    ppermute x2, starting transfers between devices, from_behind(): lax.ppermute(value, axis, [(source, source + steps) for source in range(i...  8.14 us
    unnamed x37, local copies, waits for them, and re-layouts  6.32 us
    pallas_call x2, Pallas kernels, physics(): pl.pallas_call(functools.partial(kernel, count), grid=(steps,), in_specs=...  5.29 us
    pallas_call x2, Pallas kernels, pack(): pl.pallas_call(functools.partial(pack_kernel, count, tiles), grid=(compon...  3.93 us
    pallas_call x1, Pallas kernels, momentum_of(): pl.pallas_call(functools.partial(momentum_kernel, count), grid=(component...  2.65 us
  transfers between devices with their start and end apart: 14, of which 4 were waited for; matrix products, arithmetic and copies ran while one was open for 1% of the time, Pallas kernels for 18%

commit v1 on v0

--- a/solution.py
+++ b/solution.py
@@ -16,18 +16,19 @@
 NNZB = 5
 LANES = 128
 VMEM_LIMIT = 40 * 1024 * 1024
-
-
-def params():
-    return pltpu.CompilerParams(vmem_limit_bytes=VMEM_LIMIT)
+FIRST_LIMIT = 62 * 1024 * 1024
+
+
+def params(limit=VMEM_LIMIT):
+    return pltpu.CompilerParams(vmem_limit_bytes=limit)
 
 
 def vmem():
     return pl.BlockSpec(memory_space=pltpu.VMEM)
 
 
-def cost(flops, read_written):
-    return pl.CostEstimate(flops=int(flops), bytes_accessed=int(read_written), transcendentals=0)
+def cost():
+    return pl.CostEstimate(flops=1024, bytes_accessed=1024, transcendentals=0)
 
 
 def dest_of(me, step, count):
@@ -73,29 +74,45 @@
     return (inverse.reshape(angle_total, 2 * mode_total), forward)
 
 
-def pack_kernel(count, tiles, x_ref, *out_refs):
-    me = lax.axis_index("mode")
+def pack_kernel(count, first, fields_ref, *refs):
+    me = lax.axis_index("mode")
+    out_refs, sems = refs[:count], refs[-1]
+    extra = refs[count:-1]
+    components, tiles = out_refs[0].shape[:2]
+    copies = []
     for step in range(count):
         share = dest_of(me, step, count)
         for t in range(tiles):
             start = pl.multiple_of((share * tiles + t) * LANES, LANES)
-            out_refs[step][0, t] = x_ref[0, :, :, pl.ds(start, LANES)]
-
-
-def pack(fields, first, components, count):
+            source = fields_ref.at[pl.ds(first, components), :, :, pl.ds(start, LANES)]
+            copies.append(pltpu.make_async_copy(source, out_refs[step].at[:, t], sems.at[step, t]))
+    for copy in copies:
+        copy.start()
+    for source, target in zip(extra[: len(extra) // 2], extra[len(extra) // 2 :]):
+        target[...] = source[...]
+    for copy in copies:
+        copy.wait()
+
+
+def pack(fields, first, components, count, carried, limit):
     _, mode_count, _, width = fields.shape
     tiles = width // count // LANES
     shape = (components, tiles, mode_count, 2, LANES)
-    size = components * mode_count * 2 * width * 2
+
+    def kernel(fields_ref, *refs):
+        inputs, rest = refs[: len(carried)], refs[len(carried) :]
+        pack_kernel(count, first, fields_ref, *rest[:count], *inputs, *rest[count:])
+
     return pl.pallas_call(
-        functools.partial(pack_kernel, count, tiles),
-        grid=(components,),
-        in_specs=[pl.BlockSpec((1, mode_count, 2, width), lambda c: (c + first, 0, 0, 0))],
-        out_specs=[pl.BlockSpec((1,) + shape[1:], lambda c: (c, 0, 0, 0, 0))] * count,
-        out_shape=[jax.ShapeDtypeStruct(shape, jnp.bfloat16)] * count,
-        compiler_params=params(),
-        cost_estimate=cost(0, 2 * size),
-    )(fields)
+        kernel,
+        in_specs=[pl.BlockSpec(memory_space=pltpu.HBM)] + [vmem()] * len(carried),
+        out_specs=[pl.BlockSpec(memory_space=pl.ANY)] * count + [vmem()] * len(carried),
+        out_shape=[jax.ShapeDtypeStruct(shape, jnp.bfloat16)] * count
+        + [jax.ShapeDtypeStruct(value.shape, value.dtype) for value in carried],
+        scratch_shapes=[pltpu.SemaphoreType.DMA((count, tiles))],
+        compiler_params=params(limit),
+        cost_estimate=cost(),
+    )(fields, *carried)
 
 
 def cross(a, b):
@@ -190,8 +207,6 @@
     if not keep:
         scratch = [pltpu.VMEM((components, THETA, width), jnp.float32)] + scratch
     out_shape = [jax.ShapeDtypeStruct((outputs, tiles, rows, LANES), jnp.bfloat16)] * count
-    flops = 2 * THETA * 2 * M * share * (components + outputs)
-    moved = (components + outputs) * share * 2 * M * 2 + 6 * THETA * share * 4
     return pl.pallas_call(
         functools.partial(kernel, count),
         grid=(steps,),
@@ -200,7 +215,7 @@
         out_shape=out_shape + ([kept_shape] if keep else []),
         scratch_shapes=scratch,
         compiler_params=params(),
-        cost_estimate=cost(flops, moved),
+        cost_estimate=cost(),
     )(*received, *extra, inverse, forward)
 
 
@@ -238,7 +253,7 @@
         out_specs=[vmem()] * 2,
         out_shape=[shape] * 2,
         compiler_params=params(),
-        cost_estimate=cost(2 * components * rows * width * 2 * halo, components * rows * width * 4),
+        cost_estimate=cost(),
     )(*received, interface_nodes)
 
 
@@ -322,10 +337,7 @@
         ],
         scratch_shapes=[pltpu.VMEM((node_tiles + 2 * halo_tiles, components * rows, LANES), jnp.bfloat16)],
         compiler_params=params(),
-        cost_estimate=cost(
-            2 * components * rows * node_tiles * 2 * LANES * 2 * LANES * NNZB,
-            8 * out_rows * LANES + 4 * NNZB * BLK * node_tiles * LANES,
-        ),
+        cost_estimate=cost(),
     )(*received, from_prev, from_next, radial_blocks, axial_blocks, radius, columns)
 
 
@@ -359,7 +371,7 @@
         out_specs=pl.BlockSpec((out_rows, LANES), lambda c: (c, 0)),
         out_shape=jax.ShapeDtypeStruct((components * out_rows, LANES), jnp.float32),
         compiler_params=params(),
-        cost_estimate=cost(components * out_rows * LANES, components * out_rows * LANES * 10),
+        cost_estimate=cost(),
     )(*received, gradient)
 
 
@@ -375,12 +387,12 @@
     inverse, forward = tables(M, THETA, count)
     inverse, forward = jnp.asarray(inverse), jnp.asarray(forward)
 
-    def sent(first):
-        pieces = exchange(pack(mode_fields, first, 6, count))
-        return [piece.reshape(piece.shape[:2] + (rows, LANES)) for piece in pieces]
-
-    flow = sent(0)
-    sources = sent(6)
+    def sent(pieces):
+        return [piece.reshape(piece.shape[:2] + (rows, LANES)) for piece in exchange(pieces)]
+
+    flow = sent(pack(mode_fields, 0, 6, count, [], FIRST_LIMIT))
+    *pieces, inverse, forward = pack(mode_fields, 6, 6, count, [inverse, forward], VMEM_LIMIT)
+    sources = sent(pieces)
     *terms, physical = physics(first_kernel, flow, [], inverse, forward, 4, True)
     local = exchange(terms)
     toward_prev, toward_next = interface(local, interface_nodes)

time: 91.2 us -> 128 us (1.40)
  Pallas kernels: 22.8 us -> 69.9 us
  waiting for transfers between devices: 41.4 us -> 29.1 us
  starting transfers between devices: 19.6 us -> 23 us
    pallas_call x2, Pallas kernels: 3.93 us -> 50.2 us  [pack(): pl.pallas_call(kernel, in_specs=[pl.BlockSpec(memory_space=pltpu.HBM)] +...]
    ppermute x12, waiting for transfers between devices: 41.4 us -> 25.2 us  [exchange(): received.append(lax.ppermute(pieces[step], 'mode', pairs))]
    ppermute x2, waiting for transfers between devices: 0.01 us -> 3.9 us  [from_behind(): lax.ppermute(value, axis, [(source, source + steps) for source in range(i...]
    ppermute x12, starting transfers between devices: 11.4 us -> 15.3 us  [exchange(): received.append(lax.ppermute(pieces[step], 'mode', pairs))]
    unnamed x37 -> x25, local copies, waits for them, and re-layouts: 6.32 us -> 5.05 us
  transfers between devices with their start and end apart: 14 -> 14, of which waited for: 4 -> 7; matrix products, arithmetic and copies ran while one was open for 1% -> 1% of each run, Pallas kernels for 18% -> 13%
where the time goes in v1:
time: 128 us
  Pallas kernels  69.9 us (55%)
  waiting for transfers between devices  29.1 us (23%)
  starting transfers between devices  23 us (18%)
  local copies, waits for them, and re-layouts  5.05 us (4%)
    pallas_call x2, Pallas kernels, pack(): pl.pallas_call(kernel, in_specs=[pl.BlockSpec(memory_space=pltpu.HBM)] +...  50.2 us
    ppermute x12, waiting for transfers between devices, exchange(): received.append(lax.ppermute(pieces[step], 'mode', pairs))  25.2 us
    ppermute x12, starting transfers between devices, exchange(): received.append(lax.ppermute(pieces[step], 'mode', pairs))  15.3 us
    pallas_call x1, Pallas kernels, derive(): pl.pallas_call(functools.partial(derive_kernel, count), in_specs=[vmem()]...  8.95 us
    ppermute x2, starting transfers between devices, from_behind(): lax.ppermute(value, axis, [(source, source + steps) for source in range(i...  7.69 us
    unnamed x25, local copies, waits for them, and re-layouts  5.05 us
    pallas_call x2, Pallas kernels, physics(): pl.pallas_call(functools.partial(kernel, count), grid=(steps,), in_specs=...  5.03 us
    ppermute x2, waiting for transfers between devices, from_behind(): lax.ppermute(value, axis, [(source, source + steps) for source in range(i...  3.9 us
  transfers between devices with their start and end apart: 14, of which 7 were waited for; matrix products, arithmetic and copies ran while one was open for 1% of the time, Pallas kernels for 13%

profile of v1, /device:TPU:1, one launch (start us, length us, event | category | flops | bytes accessed | tf_op | source)
XLA Modules:
  0.0 127.7 jit_solution(17022946719149790569)
XLA Ops:
  0.6 0.0 copy-start.8
  0.6 0.0 copy-start.9
  0.7 48.9 %shard_map.95 = (bf16[6,4,32,2,128]{4,3,2,1,0:T(2,128)(2,1)}, bf16[6,4,32,2,128]{4,3,2,1,0:T(2,128)(2,1)}, bf16[6,4,32,2,128]{4,3,2,1,0:T(2,128)(2,1)}, bf16[6,4,32,2,128]{4,3,2,1,0:T(2,128)(2,1)}) custom-call(bf16[12,32,2,2048]{3,2,1,0:T(2,128)(2,1)} %fields_ref.3), custom_call_target="tpu_custom_call" | custom-call | flops 1024 | bytes 1024 | tf_op jit(solution)/shard_map/pallas_call | solution.py:106
  49.6 2.1 %collective-permute-start = (bf16[6,4,32,2,128]{4,3,2,1,0:T(2,128)(2,1)}, bf16[6,4,32,2,128]{4,3,2,1,0:T(2,128)(2,1)S(1)}, u32[]{:S(2)}, u32[]{:S(2)}) collective-permute-start(bf16[6,4,32,2,128]{4,3,2,1,0:T(2,128)(2,1)} %get-tuple-element.26), channel_id=1, source_target_pairs={{0,8},{8,0},{16,24},{24,16},{1,9},{9,1},{17,25},{25,17},{2,10},{10... | collective-permute-start | bytes 1179656 | tf_op jit(solution)/shard_map/ppermute | solution.py:52
  51.7 1.2 collective-permute-start.1
  52.9 0.0 collective-permute-start.2
  52.9 0.0 copy-done.8
  52.9 0.0 copy-done.9
  52.9 1.9 %copy-done = bf16[12,32,2,2048]{3,2,1,0:T(2,128)(2,1)S(1)} copy-done((bf16[12,32,2,2048]{3,2,1,0:T(2,128)(2,1)S(1)}, bf16[12,32,2,2048]{3,2,1,0:T(2,128)(2,1)}, u32[]{:S(2)}) %copy-start) | copy-done | bytes 3145752
  54.8 1.3 %shard_map.96 = (bf16[6,4,32,2,128]{4,3,2,1,0:T(2,128)(2,1)S(1)}, bf16[6,4,32,2,128]{4,3,2,1,0:T(2,128)(2,1)S(1)}, bf16[6,4,32,2,128]{4,3,2,1,0:T(2,128)(2,1)S(1...) custom-call(bf16[12,32,2,2048]{3,2,1,0:T(2,128)(2,1)S(1)} %copy-done, ...), custom_call_target="tpu_custom_call" | custom-call | flops 1024 | bytes 1024 | tf_op jit(solution)/shard_map/pallas_call | solution.py:106
  56.1 1.5 %collective-permute-start.8 = (bf16[6,4,32,2,128]{4,3,2,1,0:T(2,128)(2,1)S(1)}, bf16[6,4,32,2,128]{4,3,2,1,0:T(2,128)(2,1)S(1)}, u32[]{:S(2)}, u32[]{:S(2)}) collective-permute-start(bf16[6,4,32,2,128]{4,3,2,1,0:T(2,128)(2,1)S(1)} %get-tuple-element.39), channel_id=1, source_target_pairs={{0,8},{8,0},{16,24},{24,16},{1,9},{9,1},{17,25},{25,17},{2,10},{10... | collective-permute-start | bytes 1179656 | tf_op jit(solution)/shard_map/ppermute | solution.py:52
  57.6 1.2 collective-permute-start.9
  58.8 1.9 %collective-permute-done = bf16[6,4,32,2,128]{4,3,2,1,0:T(2,128)(2,1)S(1)} collective-permute-done((bf16[6,4,32,2,128]{4,3,2,1,0:T(2,128)(2,1)}, bf16[6,4,32,2,128]{4,3,2,1,0:T(2,128)(2,1)S(1)}, u32[]{:S(2)}, u32[]{:S(2)}) %collective-permute-start) | collective-permute-done | bytes 393248 | tf_op jit(solution)/shard_map/ppermute | solution.py:52
  60.7 2.1 %collective-permute-start.10 = (bf16[6,4,32,2,128]{4,3,2,1,0:T(2,128)(2,1)S(1)}, bf16[6,4,32,2,128]{4,3,2,1,0:T(2,128)(2,1)S(1)}, u32[]{:S(2)}, u32[]{:S(2)}) collective-permute-start(bf16[6,4,32,2,128]{4,3,2,1,0:T(2,128)(2,1)S(1)} %get-tuple-element.41), channel_id=1, source_target_pairs={{0,24},{8,16},{16,8},{24,0},{1,25},{9,17},{17,9},{25,1},{2,26},{10... | collective-permute-start | bytes 1179656 | tf_op jit(solution)/shard_map/ppermute | solution.py:52
  62.8 0.0 collective-permute-done.1
  62.8 7.3 %collective-permute-done.2 = bf16[6,4,32,2,128]{4,3,2,1,0:T(2,128)(2,1)S(1)} collective-permute-done((bf16[6,4,32,2,128]{4,3,2,1,0:T(2,128)(2,1)}, bf16[6,4,32,2,128]{4,3,2,1,0:T(2,128)(2,1)S(1)}, u32[]{:S(2)}, u32[]{:S(2)}) %collective-permute-start.2) | collective-permute-done | bytes 393248 | tf_op jit(solution)/shard_map/ppermute | solution.py:52
  70.1 0.0 copy-done.5
  70.1 2.1 %shard_map.97 = (bf16[4,4,64,128]{3,2,1,0:T(8,128)(2,1)S(1)}, bf16[4,4,64,128]{3,2,1,0:T(8,128)(2,1)S(1)}, bf16[4,4,64,128]{3,2,1,0:T(8,128)(2,1)S(1)}, bf16[4,4...) custom-call(bf16[6,4,64,128]{3,2,1,0:T(8,128)(2,1)S(1)} %bitcast.23, bf16[6,4,64,128]{3,2,1,0:T(8,128)(2,1)S(1)} %bitcast.24, ...), custom_call_target="tpu_custom_call" | custom-call | flops 1024 | bytes 1024 | tf_op jit(solution)/shard_map/pallas_call | solution.py:210
  72.2 1.3 collective-permute-start.3
  73.5 0.2 collective-permute-start.4
  73.7 3.9 %collective-permute-done.8 = bf16[6,4,32,2,128]{4,3,2,1,0:T(2,128)(2,1)S(1)} collective-permute-done((bf16[6,4,32,2,128]{4,3,2,1,0:T(2,128)(2,1)S(1)}, bf16[6,4,32,2,128]{4,3,2,1,0:T(2,128)(2,1)S(1)}, u32[]{:S(2)}, u32[]{:S(2)}) %collective-permute-start.8) | collective-permute-done | bytes 393248 | tf_op jit(solution)/shard_map/ppermute | solution.py:52
  77.6 2.1 %collective-permute-start.5 = (bf16[4,4,64,128]{3,2,1,0:T(8,128)(2,1)S(1)}, bf16[4,4,64,128]{3,2,1,0:T(8,128)(2,1)S(1)}, u32[]{:S(2)}, u32[]{:S(2)}) collective-permute-start(bf16[4,4,64,128]{3,2,1,0:T(8,128)(2,1)S(1)} %get-tuple-element.34), channel_id=1, source_target_pairs={{0,24},{8,16},{16,8},{24,0},{1,25},{9,17},{17,9},{25,1},{2,26},{10... | collective-permute-start | bytes 786440 | tf_op jit(solution)/shard_map/ppermute | solution.py:52
  79.7 0.0 collective-permute-done.9
  79.7 7.3 %collective-permute-done.10 = bf16[6,4,32,2,128]{4,3,2,1,0:T(2,128)(2,1)S(1)} collective-permute-done((bf16[6,4,32,2,128]{4,3,2,1,0:T(2,128)(2,1)S(1)}, bf16[6,4,32,2,128]{4,3,2,1,0:T(2,128)(2,1)S(1)}, u32[]{:S(2)}, u32[]{:S(2)}) %collective-permute-start.10) | collective-permute-done | bytes 393248 | tf_op jit(solution)/shard_map/ppermute | solution.py:52
  87.0 2.9 %shard_map.100 = (bf16[3,4,64,128]{3,2,1,0:T(8,128)(2,1)S(1)}, bf16[3,4,64,128]{3,2,1,0:T(8,128)(2,1)}, bf16[3,4,64,128]{3,2,1,0:T(8,128)(2,1)}, bf16[3,4,64,128]{3,2,1,0:T(8,128)(2,1)}) custom-call(bf16[6,4,64,128]{3,2,1,0:T(8,128)(2,1)S(1)} %bitcast.19, bf16[6,4,64,128]{3,2,1,0:T(8,128)(2,1)S(1)} %bitcast.20, bf16[6,4,64,128]{3,2,1,0:T(8,128)(2,1)S(1)} %bitcast.21, ...), custom_call_target="tpu_custom_call" | custom-call | flops 1024 | bytes 1024 | tf_op jit(solution)/shard_map/pallas_call | solution.py:210
  89.9 1.2 collective-permute-start.11
  91.1 0.2 collective-permute-start.12
  91.3 0.4 collective-permute-done.3.refs_1_
  91.7 2.1 %collective-permute-start.13 = (bf16[3,4,64,128]{3,2,1,0:T(8,128)(2,1)}, bf16[3,4,64,128]{3,2,1,0:T(8,128)(2,1)}, u32[]{:S(2)}, u32[]{:S(2)}) collective-permute-start(bf16[3,4,64,128]{3,2,1,0:T(8,128)(2,1)} %get-tuple-element.46), channel_id=1, source_target_pairs={{0,24},{8,16},{16,8},{24,0},{1,25},{9,17},{17,9},{25,1},{2,26},{10... | collective-permute-start | bytes 589832 | tf_op jit(solution)/shard_map/ppermute | solution.py:52
  93.8 0.0 collective-permute-done.4.refs_2_
  93.8 4.4 %collective-permute-done.5.refs_3_ = bf16[4,4,64,128]{3,2,1,0:T(8,128)(2,1)S(1)} collective-permute-done((bf16[4,4,64,128]{3,2,1,0:T(8,128)(2,1)S(1)}, bf16[4,4,64,128]{3,2,1,0:T(8,128)(2,1)S(1)}, u32[]{:S(2)}, u32[]{:S(2)}) %collective-permute-start.5) | collective-permute-done | bytes 262176 | tf_op jit(solution)/shard_map/ppermute | solution.py:52
  98.3 0.0 copy-done.11
  98.3 1.9 %shard_map.98 = (bf16[4,2,64,128]{3,2,1,0:T(8,128)(2,1)}, bf16[4,2,64,128]{3,2,1,0:T(8,128)(2,1)}) custom-call(bf16[4,4,64,128]{3,2,1,0:T(8,128)(2,1)S(1)} %get-tuple-element.31.refs_0_, bf16[4,4,64,128]{3,2,1,0:T(8,128)(2,1)S(1)} %collective-permute-done.3.refs_1_, bf16[4,4,64,128]{3,2,1,0:T(8,128)(2,1)S(1)} %collective-permute-done.4.refs_2_, ...), custom_call_target="tpu_custom_call" | custom-call | flops 1024 | bytes 1024 | tf_op jit(solution)/shard_map/pallas_call | solution.py:250
  100.2 0.0 copy-done.6
  100.2 0.7 copy-done.3
  100.9 5.8 %collective-permute-start.6 = (bf16[4,2,64,128]{3,2,1,0:T(8,128)(2,1)}, bf16[4,2,64,128]{3,2,1,0:T(8,128)(2,1)S(1)}, u32[]{:S(2)}, u32[]{:S(2)}) collective-permute-start(bf16[4,2,64,128]{3,2,1,0:T(8,128)(2,1)} %get-tuple-element.35), channel_id=1, source_target_pairs={{0,1},{1,2},{2,3},{3,4},{4,5},{5,6},{6,7},{8,9},{9,10},{10,11},{11... | collective-permute-start | bytes 393224 | tf_op jit(solution)/shard_map/ppermute | solution.py:59
  106.7 1.9 %collective-permute-start.7 = (bf16[4,2,64,128]{3,2,1,0:T(8,128)(2,1)}, bf16[4,2,64,128]{3,2,1,0:T(8,128)(2,1)}, u32[]{:S(2)}, u32[]{:S(2)}) collective-permute-start(bf16[4,2,64,128]{3,2,1,0:T(8,128)(2,1)} %get-tuple-element.36), channel_id=1, source_target_pairs={{1,0},{2,1},{3,2},{4,3},{5,4},{6,5},{7,6},{9,8},{10,9},{11,10},{12... | collective-permute-start | bytes 393224 | tf_op jit(solution)/shard_map/ppermute | solution.py:59
  108.6 0.8 copy.10.refs_9_
  109.4 0.0 collective-permute-done.6.refs_4_
  109.4 3.9 %collective-permute-done.7.refs_5_ = bf16[4,2,64,128]{3,2,1,0:T(8,128)(2,1)} collective-permute-done((bf16[4,2,64,128]{3,2,1,0:T(8,128)(2,1)}, bf16[4,2,64,128]{3,2,1,0:T(8,128)(2,1)}, u32[]{:S(2)}, u32[]{:S(2)}) %collective-permute-start.7) | collective-permute-done | bytes 131104 | tf_op jit(solution)/shard_map/ppermute | solution.py:59
  113.3 0.9 copy-done.4
  114.2 0.7 copy-done.10
  114.9 9.0 %shard_map.99 = (f32[3072,128]{1,0:T(8,128)}, f32[3,16,64,128]{3,2,1,0:T(8,128)S(1)}) custom-call(bf16[4,4,64,128]{3,2,1,0:T(8,128)(2,1)S(1)} %get-tuple-element.31.refs_0_, bf16[4,4,64,128]{3,2,1,0:T(8,128)(2,1)S(1)} %collective-permute-done.3.refs_1_, bf16[4,4,64,128]{3,2,1,0:T(8,128)(2,1)S(1)} %collective-permute-done.4.refs_2_, ...), custom_call_target="tpu_custom_call" | custom-call | flops 1024 | bytes 1024 | tf_op jit(solution)/shard_map/pallas_call | solution.py:330
  123.9 0.0 collective-permute-done.11.refs_1_
  123.9 0.0 collective-permute-done.12.refs_2_
  123.9 0.0 collective-permute-done.13.refs_3_
  123.9 0.0 copy-done.7
  123.9 3.8 %shard_map.101 = f32[3072,128]{1,0:T(8,128)} custom-call(bf16[3,4,64,128]{3,2,1,0:T(8,128)(2,1)S(1)} %copy-done.7, bf16[3,4,64,128]{3,2,1,0:T(8,128)(2,1)} %collective-permute-done.11.refs_1_, bf16[3,4,64,128]{3,2,1,0:T(8,128)(2,1)} %collective-permute-done.12.refs_2_, bf16[3,4,64,128]{3,2,1,0:T(8,128)(2,1)} %collective-permute-done.13.refs_3_, ...), custom_call_target="tpu_custom_call" | custom-call | flops 1024 | bytes 1024 | tf_op jit(solution)/shard_map/pallas_call | solution.py:366
  (12 shorter events, 0.0 us)
Async XLA Ops:
  0.6 52.3 %copy-start.8 = (bf16[256,256]{1,0:T(8,128)(2,1)S(1)}, bf16[256,256]{1,0:T(8,128)(2,1)}, u32[]{:S(2)}) copy-start(bf16[256,256]{1,0:T(8,128)(2,1)} %constant.5.clone.refs_1_) | copy-start | bytes 393220
  0.6 52.3 %copy-start.9 = (bf16[256,256]{1,0:T(8,128)(2,1)S(1)}, bf16[256,256]{1,0:T(8,128)(2,1)}, u32[]{:S(2)}) copy-start(bf16[256,256]{1,0:T(8,128)(2,1)} %constant.4.clone.refs_0_) | copy-start | bytes 393220
  49.6 11.2 %collective-permute-start = (bf16[6,4,32,2,128]{4,3,2,1,0:T(2,128)(2,1)}, bf16[6,4,32,2,128]{4,3,2,1,0:T(2,128)(2,1)S(1)}, u32[]{:S(2)}, u32[]{:S(2)}) collective-permute-start(bf16[6,4,32,2,128]{4,3,2,1,0:T(2,128)(2,1)} %get-tuple-element.26), channel_id=1, source_target_pairs={{0,8},{8,0},{16,24},{24,16},{1,9},{9,1},{17,25},{25,17},{2,10},{10... | collective-permute-start | bytes 1179656 | tf_op jit(solution)/shard_map/ppermute | solution.py:52
  51.7 11.2 %collective-permute-start.1 = (bf16[6,4,32,2,128]{4,3,2,1,0:T(2,128)(2,1)}, bf16[6,4,32,2,128]{4,3,2,1,0:T(2,128)(2,1)S(1)}, u32[]{:S(2)}, u32[]{:S(2)}) collective-permute-start(bf16[6,4,32,2,128]{4,3,2,1,0:T(2,128)(2,1)} %get-tuple-element.27), channel_id=1, source_target_pairs={{0,16},{8,24},{16,0},{24,8},{1,17},{9,25},{17,1},{25,9},{2,18},{10... | collective-permute-start | bytes 1179656 | tf_op jit(solution)/shard_map/ppermute | solution.py:52
  52.9 17.2 %collective-permute-start.2 = (bf16[6,4,32,2,128]{4,3,2,1,0:T(2,128)(2,1)}, bf16[6,4,32,2,128]{4,3,2,1,0:T(2,128)(2,1)S(1)}, u32[]{:S(2)}, u32[]{:S(2)}) collective-permute-start(bf16[6,4,32,2,128]{4,3,2,1,0:T(2,128)(2,1)} %get-tuple-element.28), channel_id=1, source_target_pairs={{0,24},{8,16},{16,8},{24,0},{1,25},{9,17},{17,9},{25,1},{2,26},{10... | collective-permute-start | bytes 1179656 | tf_op jit(solution)/shard_map/ppermute | solution.py:52
  52.9 1.9 %copy-start = (bf16[12,32,2,2048]{3,2,1,0:T(2,128)(2,1)S(1)}, bf16[12,32,2,2048]{3,2,1,0:T(2,128)(2,1)}, u32[]{:S(2)}) copy-start(bf16[12,32,2,2048]{3,2,1,0:T(2,128)(2,1)} %fields_ref.3) | copy-start | bytes 9437188
  54.8 15.3 %copy-start.5 = (bf16[6,4,32,2,128]{4,3,2,1,0:T(2,128)(2,1)S(1)}, bf16[6,4,32,2,128]{4,3,2,1,0:T(2,128)(2,1)}, u32[]{:S(2)}) copy-start(bf16[6,4,32,2,128]{4,3,2,1,0:T(2,128)(2,1)} %get-tuple-element.25) | copy-start | bytes 1179652
  56.1 21.5 %collective-permute-start.8 = (bf16[6,4,32,2,128]{4,3,2,1,0:T(2,128)(2,1)S(1)}, bf16[6,4,32,2,128]{4,3,2,1,0:T(2,128)(2,1)S(1)}, u32[]{:S(2)}, u32[]{:S(2)}) collective-permute-start(bf16[6,4,32,2,128]{4,3,2,1,0:T(2,128)(2,1)S(1)} %get-tuple-element.39), channel_id=1, source_target_pairs={{0,8},{8,0},{16,24},{24,16},{1,9},{9,1},{17,25},{25,17},{2,10},{10... | collective-permute-start | bytes 1179656 | tf_op jit(solution)/shard_map/ppermute | solution.py:52
  57.6 22.1 %collective-permute-start.9 = (bf16[6,4,32,2,128]{4,3,2,1,0:T(2,128)(2,1)S(1)}, bf16[6,4,32,2,128]{4,3,2,1,0:T(2,128)(2,1)S(1)}, u32[]{:S(2)}, u32[]{:S(2)}) collective-permute-start(bf16[6,4,32,2,128]{4,3,2,1,0:T(2,128)(2,1)S(1)} %get-tuple-element.40), channel_id=1, source_target_pairs={{0,16},{8,24},{16,0},{24,8},{1,17},{9,25},{17,1},{25,9},{2,18},{10... | collective-permute-start | bytes 1179656 | tf_op jit(solution)/shard_map/ppermute | solution.py:52
  60.7 26.3 %collective-permute-start.10 = (bf16[6,4,32,2,128]{4,3,2,1,0:T(2,128)(2,1)S(1)}, bf16[6,4,32,2,128]{4,3,2,1,0:T(2,128)(2,1)S(1)}, u32[]{:S(2)}, u32[]{:S(2)}) collective-permute-start(bf16[6,4,32,2,128]{4,3,2,1,0:T(2,128)(2,1)S(1)} %get-tuple-element.41), channel_id=1, source_target_pairs={{0,24},{8,16},{16,8},{24,0},{1,25},{9,17},{17,9},{25,1},{2,26},{10... | collective-permute-start | bytes 1179656 | tf_op jit(solution)/shard_map/ppermute | solution.py:52
  72.2 19.5 %collective-permute-start.3 = (bf16[4,4,64,128]{3,2,1,0:T(8,128)(2,1)S(1)}, bf16[4,4,64,128]{3,2,1,0:T(8,128)(2,1)S(1)}, u32[]{:S(2)}, u32[]{:S(2)}) collective-permute-start(bf16[4,4,64,128]{3,2,1,0:T(8,128)(2,1)S(1)} %get-tuple-element.32), channel_id=1, source_target_pairs={{0,8},{8,0},{16,24},{24,16},{1,9},{9,1},{17,25},{25,17},{2,10},{10... | collective-permute-start | bytes 786440 | tf_op jit(solution)/shard_map/ppermute | solution.py:52
  73.5 20.3 %collective-permute-start.4 = (bf16[4,4,64,128]{3,2,1,0:T(8,128)(2,1)S(1)}, bf16[4,4,64,128]{3,2,1,0:T(8,128)(2,1)S(1)}, u32[]{:S(2)}, u32[]{:S(2)}) collective-permute-start(bf16[4,4,64,128]{3,2,1,0:T(8,128)(2,1)S(1)} %get-tuple-element.33), channel_id=1, source_target_pairs={{0,16},{8,24},{16,0},{24,8},{1,17},{9,25},{17,1},{25,9},{2,18},{10... | collective-permute-start | bytes 786440 | tf_op jit(solution)/shard_map/ppermute | solution.py:52
  77.6 20.6 %collective-permute-start.5 = (bf16[4,4,64,128]{3,2,1,0:T(8,128)(2,1)S(1)}, bf16[4,4,64,128]{3,2,1,0:T(8,128)(2,1)S(1)}, u32[]{:S(2)}, u32[]{:S(2)}) collective-permute-start(bf16[4,4,64,128]{3,2,1,0:T(8,128)(2,1)S(1)} %get-tuple-element.34), channel_id=1, source_target_pairs={{0,24},{8,16},{16,8},{24,0},{1,25},{9,17},{17,9},{25,1},{2,26},{10... | collective-permute-start | bytes 786440 | tf_op jit(solution)/shard_map/ppermute | solution.py:52
  87.0 11.3 %copy-start.11 = (s32[2,256]{1,0:T(2,128)S(1)}, s32[2,256]{1,0:T(2,128)}, u32[]{:S(2)}) copy-start(s32[2,256]{1,0:T(2,128)} %refs_4_.1) | copy-start | bytes 6148
  87.0 26.3 %copy-start.1 = (bf16[5,64,2048]{2,1,0:T(8,128)(2,1)S(1)}, bf16[5,64,2048]{2,1,0:T(8,128)(2,1)}, u32[]{:S(2)}) copy-start(bf16[5,64,2048]{2,1,0:T(8,128)(2,1)} %refs_6_.1) | copy-start | bytes 3932164
  87.0 26.3 %copy-start.2 = (bf16[5,64,2048]{2,1,0:T(8,128)(2,1)S(1)}, bf16[5,64,2048]{2,1,0:T(8,128)(2,1)}, u32[]{:S(2)}) copy-start(bf16[5,64,2048]{2,1,0:T(8,128)(2,1)} %refs_7_.1) | copy-start | bytes 3932164
  89.9 10.3 %copy-start.6 = (bf16[3,4,64,128]{3,2,1,0:T(8,128)(2,1)}, bf16[3,4,64,128]{3,2,1,0:T(8,128)(2,1)S(1)}, u32[]{:S(2)}) copy-start(bf16[3,4,64,128]{3,2,1,0:T(8,128)(2,1)S(1)} %get-tuple-element.43.refs_0_) | copy-start | bytes 589828
  89.9 34.0 %collective-permute-start.11 = (bf16[3,4,64,128]{3,2,1,0:T(8,128)(2,1)}, bf16[3,4,64,128]{3,2,1,0:T(8,128)(2,1)}, u32[]{:S(2)}, u32[]{:S(2)}) collective-permute-start(bf16[3,4,64,128]{3,2,1,0:T(8,128)(2,1)} %get-tuple-element.44), channel_id=1, source_target_pairs={{0,8},{8,0},{16,24},{24,16},{1,9},{9,1},{17,25},{25,17},{2,10},{10... | collective-permute-start | bytes 589832 | tf_op jit(solution)/shard_map/ppermute | solution.py:52
  91.1 32.8 %collective-permute-start.12 = (bf16[3,4,64,128]{3,2,1,0:T(8,128)(2,1)}, bf16[3,4,64,128]{3,2,1,0:T(8,128)(2,1)}, u32[]{:S(2)}, u32[]{:S(2)}) collective-permute-start(bf16[3,4,64,128]{3,2,1,0:T(8,128)(2,1)} %get-tuple-element.45), channel_id=1, source_target_pairs={{0,16},{8,24},{16,0},{24,8},{1,17},{9,25},{17,1},{25,9},{2,18},{10... | collective-permute-start | bytes 589832 | tf_op jit(solution)/shard_map/ppermute | solution.py:52
  91.7 32.2 %collective-permute-start.13 = (bf16[3,4,64,128]{3,2,1,0:T(8,128)(2,1)}, bf16[3,4,64,128]{3,2,1,0:T(8,128)(2,1)}, u32[]{:S(2)}, u32[]{:S(2)}) collective-permute-start(bf16[3,4,64,128]{3,2,1,0:T(8,128)(2,1)} %get-tuple-element.46), channel_id=1, source_target_pairs={{0,24},{8,16},{16,8},{24,0},{1,25},{9,17},{17,9},{25,1},{2,26},{10... | collective-permute-start | bytes 589832 | tf_op jit(solution)/shard_map/ppermute | solution.py:52
  100.2 0.7 copy-start.3
  100.9 8.5 %collective-permute-start.6 = (bf16[4,2,64,128]{3,2,1,0:T(8,128)(2,1)}, bf16[4,2,64,128]{3,2,1,0:T(8,128)(2,1)S(1)}, u32[]{:S(2)}, u32[]{:S(2)}) collective-permute-start(bf16[4,2,64,128]{3,2,1,0:T(8,128)(2,1)} %get-tuple-element.35), channel_id=1, source_target_pairs={{0,1},{1,2},{2,3},{3,4},{4,5},{5,6},{6,7},{8,9},{9,10},{10,11},{11... | collective-permute-start | bytes 393224 | tf_op jit(solution)/shard_map/ppermute | solution.py:59
  106.7 6.6 %collective-permute-start.7 = (bf16[4,2,64,128]{3,2,1,0:T(8,128)(2,1)}, bf16[4,2,64,128]{3,2,1,0:T(8,128)(2,1)}, u32[]{:S(2)}, u32[]{:S(2)}) collective-permute-start(bf16[4,2,64,128]{3,2,1,0:T(8,128)(2,1)} %get-tuple-element.36), channel_id=1, source_target_pairs={{1,0},{2,1},{3,2},{4,3},{5,4},{6,5},{7,6},{9,8},{10,9},{11,10},{12... | collective-permute-start | bytes 393224 | tf_op jit(solution)/shard_map/ppermute | solution.py:59
  113.3 1.0 copy-start.4
  114.2 0.7 copy-start.10
  114.9 9.0 %copy-start.7 = (bf16[3,4,64,128]{3,2,1,0:T(8,128)(2,1)S(1)}, bf16[3,4,64,128]{3,2,1,0:T(8,128)(2,1)}, u32[]{:S(2)}) copy-start(bf16[3,4,64,128]{3,2,1,0:T(8,128)(2,1)} %copy-done.6) | copy-start | bytes 589828

commit v2 on v1

--- a/solution.py
+++ b/solution.py
@@ -15,8 +15,8 @@
 BLK = 64
 NNZB = 5
 LANES = 128
-VMEM_LIMIT = 40 * 1024 * 1024
-FIRST_LIMIT = 62 * 1024 * 1024
+VMEM_LIMIT = 24 * 1024 * 1024
+FIRST_LIMIT = 61 * 1024 * 1024
 
 
 def params(limit=VMEM_LIMIT):
@@ -74,21 +74,26 @@
     return (inverse.reshape(angle_total, 2 * mode_total), forward)
 
 
-def pack_kernel(count, first, fields_ref, *refs):
-    me = lax.axis_index("mode")
-    out_refs, sems = refs[:count], refs[-1]
-    extra = refs[count:-1]
+def pack_kernel(count, carried, first, fields_ref, *refs):
+    me = lax.axis_index("mode")
+    inputs, refs = refs[:carried], refs[carried:]
+    out_refs, outputs, (fields_vmem, load, sems) = refs[:count], refs[count : count + carried], refs[count + carried :]
     components, tiles = out_refs[0].shape[:2]
+    loads = []
+    for c in range(components):
+        loads.append(pltpu.make_async_copy(fields_ref.at[first + c], fields_vmem.at[c], load.at[c]))
+        loads[c].start()
     copies = []
-    for step in range(count):
-        share = dest_of(me, step, count)
-        for t in range(tiles):
-            start = pl.multiple_of((share * tiles + t) * LANES, LANES)
-            source = fields_ref.at[pl.ds(first, components), :, :, pl.ds(start, LANES)]
-            copies.append(pltpu.make_async_copy(source, out_refs[step].at[:, t], sems.at[step, t]))
-    for copy in copies:
-        copy.start()
-    for source, target in zip(extra[: len(extra) // 2], extra[len(extra) // 2 :]):
+    for c in range(components):
+        loads[c].wait()
+        for step in range(count):
+            share = dest_of(me, step, count)
+            for t in range(tiles):
+                start = pl.multiple_of((share * tiles + t) * LANES, LANES)
+                source = fields_vmem.at[c, :, :, pl.ds(start, LANES)]
+                copies.append(pltpu.make_async_copy(source, out_refs[step].at[c, t], sems.at[c, step, t]))
+                copies[-1].start()
+    for source, target in zip(inputs, outputs):
         target[...] = source[...]
     for copy in copies:
         copy.wait()
@@ -98,18 +103,17 @@
     _, mode_count, _, width = fields.shape
     tiles = width // count // LANES
     shape = (components, tiles, mode_count, 2, LANES)
-
-    def kernel(fields_ref, *refs):
-        inputs, rest = refs[: len(carried)], refs[len(carried) :]
-        pack_kernel(count, first, fields_ref, *rest[:count], *inputs, *rest[count:])
-
     return pl.pallas_call(
-        kernel,
-        in_specs=[pl.BlockSpec(memory_space=pltpu.HBM)] + [vmem()] * len(carried),
-        out_specs=[pl.BlockSpec(memory_space=pl.ANY)] * count + [vmem()] * len(carried),
+        functools.partial(pack_kernel, count, len(carried), first),
+        in_specs=[pl.BlockSpec(memory_space=pl.ANY)] + [vmem()] * len(carried),
+        out_specs=[vmem()] * (count + len(carried)),
         out_shape=[jax.ShapeDtypeStruct(shape, jnp.bfloat16)] * count
         + [jax.ShapeDtypeStruct(value.shape, value.dtype) for value in carried],
-        scratch_shapes=[pltpu.SemaphoreType.DMA((count, tiles))],
+        scratch_shapes=[
+            pltpu.VMEM((components, mode_count, 2, width), jnp.bfloat16),
+            pltpu.SemaphoreType.DMA((components,)),
+            pltpu.SemaphoreType.DMA((components, count, tiles)),
+        ],
         compiler_params=params(limit),
         cost_estimate=cost(),
     )(fields, *carried)
@@ -266,41 +270,45 @@
     mode_count = rows // 2
     node_tiles = count * tiles
     halo_tiles = prev_ref.shape[1]
+
+    def extend(at, tile):
+        extended_ref[0, at] = tile
+        extended_ref[1, at] = jnp.concatenate([tile[:, BLK:], tile[:, :BLK]], axis=1)
+
     for step in range(count):
         share = source_of(me, step, count)
         for t in range(tiles):
-            extended_ref[share * tiles + t] = in_refs[step][:, t].reshape(components * rows, LANES)
+            extend(share * tiles + t, in_refs[step][:, t].reshape(components * rows, LANES))
     for t in range(halo_tiles):
-        extended_ref[node_tiles + t] = prev_ref[:, t].reshape(components * rows, LANES)
-        extended_ref[node_tiles + halo_tiles + t] = next_ref[:, t].reshape(components * rows, LANES)
+        extend(node_tiles + t, prev_ref[:, t].reshape(components * rows, LANES))
+        extend(node_tiles + halo_tiles + t, next_ref[:, t].reshape(components * rows, LANES))
     modes = (lax.broadcasted_iota(jnp.int32, (mode_count, LANES), 0) + me * mode_count).astype(jnp.float32)
+    low = lax.broadcasted_iota(jnp.int32, (components * rows, LANES), 1) < BLK
     lane = lax.broadcasted_iota(jnp.int32, (1, 2 * LANES), 1)
     in_first = jnp.where(lax.rem(lane, LANES) < BLK, 1.0, 0.0)
-    in_half = [in_first, 1.0 - in_first]
+    in_half = [in_first.astype(jnp.bfloat16), (1.0 - in_first).astype(jnp.bfloat16)]
 
     def rotated(values):
         return jnp.concatenate([-modes * values[mode_count:], modes * values[:mode_count]], axis=0)
 
     def pair(b, carry):
         here = pl.ds(pl.multiple_of(b * LANES, LANES), LANES)
-        total = jnp.zeros((components * rows, 2 * LANES), jnp.float32)
+        left, right = [], []
         for k in range(NNZB):
             weights = jnp.concatenate([radial_ref[k, :, here], axial_ref[k, :, here]], axis=1)
-            left, right = [], []
-            for half in range(2):
-                column = columns_ref[2 * b + half, k]
-                odd = lax.rem(column, 2).astype(jnp.float32)
-                left.append(extended_ref[lax.div(column, 2)])
-                right.append(weights * (in_half[half] * (1.0 - odd)).astype(jnp.bfloat16))
-                right.append(weights * (in_half[half] * odd).astype(jnp.bfloat16))
-            total += jnp.dot(
-                jnp.concatenate(left, axis=1),
-                jnp.concatenate(right, axis=0),
-                preferred_element_type=jnp.float32,
-            )
+            first, second = columns_ref[k, 2 * b], columns_ref[k, 2 * b + 1]
+            first_tile = extended_ref[lax.rem(first, 2), lax.div(first, 2)]
+            second_tile = extended_ref[1 - lax.rem(second, 2), lax.div(second, 2)]
+            left.append(jnp.where(low, first_tile, second_tile))
+            right += [weights * in_half[0], weights * in_half[1]]
+        total = jnp.dot(
+            jnp.concatenate(left, axis=1),
+            jnp.concatenate(right, axis=0),
+            preferred_element_type=jnp.float32,
+        )
         along_r = [total[c * rows : (c + 1) * rows, :LANES] for c in range(components)]
         along_z = [total[c * rows : (c + 1) * rows, LANES:] for c in range(components)]
-        values = [extended_ref[b, c * rows : (c + 1) * rows].astype(jnp.float32) for c in range(components)]
+        values = [extended_ref[0, b, c * rows : (c + 1) * rows].astype(jnp.float32) for c in range(components)]
         inv_radius = 1.0 / radius_ref[:, here]
         induction = [
             rotated(values[2]) * inv_radius - along_z[1],
@@ -335,41 +343,47 @@
             jax.ShapeDtypeStruct((out_rows, LANES), jnp.float32),
             jax.ShapeDtypeStruct((3, node_tiles, rows, LANES), jnp.float32),
         ],
-        scratch_shapes=[pltpu.VMEM((node_tiles + 2 * halo_tiles, components * rows, LANES), jnp.bfloat16)],
+        scratch_shapes=[pltpu.VMEM((2, node_tiles + 2 * halo_tiles, components * rows, LANES), jnp.bfloat16)],
         compiler_params=params(),
         cost_estimate=cost(),
     )(*received, from_prev, from_next, radial_blocks, axial_blocks, radius, columns)
 
 
 def momentum_kernel(count, *refs):
-    in_refs, (gradient_ref, out_ref) = refs[:count], refs[count:]
-    me = lax.axis_index("mode")
-    _, tiles, rows, _ = in_refs[0].shape
+    in_refs, (gradient_ref, out_ref, total_ref, sems) = refs[:count], refs[count:]
+    me = lax.axis_index("mode")
+    components, tiles, rows, _ = in_refs[0].shape
     mode_count = rows // 2
     stride = 2 * count * tiles
-    for step in range(count):
-        share = source_of(me, step, count)
-        for t in range(tiles):
-            at = share * tiles + t
-            value = in_refs[step][0, t].astype(jnp.float32) - gradient_ref[0, at]
-            for p in range(2):
-                out_ref[pl.ds(2 * at + p, mode_count, stride=stride), :] = value[
-                    p * mode_count : (p + 1) * mode_count
-                ]
+    out_rows = mode_count * stride
+    copies = []
+    for c in range(components):
+        for step in range(count):
+            share = source_of(me, step, count)
+            for t in range(tiles):
+                at = share * tiles + t
+                value = in_refs[step][c, t].astype(jnp.float32) - gradient_ref[c, at]
+                for p in range(2):
+                    total_ref[pl.ds(c * out_rows + 2 * at + p, mode_count, stride=stride), :] = value[
+                        p * mode_count : (p + 1) * mode_count
+                    ]
+        done = pl.ds(c * out_rows, out_rows)
+        copies.append(pltpu.make_async_copy(total_ref.at[done], out_ref.at[done], sems.at[c]))
+        copies[c].start()
+    for copy in copies:
+        copy.wait()
 
 
 def momentum_of(received, gradient):
     count = len(received)
     components, tiles, rows, _ = received[0].shape
-    node_tiles = count * tiles
-    out_rows = rows * node_tiles
+    shape = (components * rows * count * tiles, LANES)
     return pl.pallas_call(
         functools.partial(momentum_kernel, count),
-        grid=(components,),
-        in_specs=[pl.BlockSpec((1, tiles, rows, LANES), lambda c: (c, 0, 0, 0))] * count
-        + [pl.BlockSpec((1, node_tiles, rows, LANES), lambda c: (c, 0, 0, 0))],
-        out_specs=pl.BlockSpec((out_rows, LANES), lambda c: (c, 0)),
-        out_shape=jax.ShapeDtypeStruct((components * out_rows, LANES), jnp.float32),
+        in_specs=[vmem()] * (count + 1),
+        out_specs=pl.BlockSpec(memory_space=pl.ANY),
+        out_shape=jax.ShapeDtypeStruct(shape, jnp.float32),
+        scratch_shapes=[pltpu.VMEM(shape, jnp.float32), pltpu.SemaphoreType.DMA((components,))],
         compiler_params=params(),
         cost_estimate=cost(),
     )(*received, gradient)
@@ -387,19 +401,20 @@
     inverse, forward = tables(M, THETA, count)
     inverse, forward = jnp.asarray(inverse), jnp.asarray(forward)
 
-    def sent(pieces):
-        return [piece.reshape(piece.shape[:2] + (rows, LANES)) for piece in exchange(pieces)]
-
-    flow = sent(pack(mode_fields, 0, 6, count, [], FIRST_LIMIT))
+    def joined(pieces):
+        return [piece.reshape(piece.shape[:2] + (rows, LANES)) for piece in pieces]
+
+    flow = exchange(pack(mode_fields, 0, 6, count, [], FIRST_LIMIT))
     *pieces, inverse, forward = pack(mode_fields, 6, 6, count, [inverse, forward], VMEM_LIMIT)
-    sources = sent(pieces)
+    flow, pieces = lax.optimization_barrier((flow, pieces))
+    flow, sources = joined(flow), joined(exchange(pieces))
     *terms, physical = physics(first_kernel, flow, [], inverse, forward, 4, True)
     local = exchange(terms)
     toward_prev, toward_next = interface(local, interface_nodes)
     from_prev = from_behind(toward_next, "mer", 1)
     from_next = from_behind(toward_prev, "mer", -1)
     induction, gradient = derive(
-        local, from_prev, from_next, radial_blocks, axial_blocks, radius.reshape(1, width), block_columns
+        local, from_prev, from_next, radial_blocks, axial_blocks, radius.reshape(1, width), block_columns.T
     )
     lorentz = exchange(physics(second_kernel, sources, [physical], inverse, forward, 3, False))
     momentum = momentum_of(lorentz, gradient)

time: 128 us -> 83 us (0.65)
  Pallas kernels: 69.9 us -> 22.3 us
  starting transfers between devices: 23 us -> 27 us
  local copies, waits for them, and re-layouts: 5.05 us -> 1.93 us
  waiting for transfers between devices: 29.1 us -> 30.8 us
    pallas_call x3, Pallas kernels: 54 us -> 8.87 us  [the longest x2 6.68 us: pack(): pl.pallas_call(functools.partial(pack_kernel, count, len(carried), first)...]
    ppermute x2, starting transfers between devices: 7.69 us -> 13.8 us  [from_behind(): lax.ppermute(value, axis, [(source, source + steps) for source in range(i...]
    unnamed x25 -> x18, local copies, waits for them, and re-layouts: 5.05 us -> 1.93 us
    ppermute x12, starting transfers between devices: 15.3 us -> 13.2 us  [exchange(): received.append(lax.ppermute(pieces[step], 'mode', pairs))]
    ppermute x12, waiting for transfers between devices: 25.2 us -> 26.5 us  [exchange(): received.append(lax.ppermute(pieces[step], 'mode', pairs))]
  transfers between devices with their start and end apart: 14 -> 14, of which waited for: 7 -> 10; matrix products, arithmetic and copies ran while one was open for 1% -> 0% of each run, Pallas kernels for 13% -> 19%
where the time goes in v2:
time: 83 us; the launch traced here: 82.8 us
  waiting for transfers between devices  30.8 us (37%)
  starting transfers between devices  27 us (33%)
  Pallas kernels  22.3 us (27%)
  local copies, waits for them, and re-layouts  1.93 us (2%)
    ppermute x12, waiting for transfers between devices, exchange(): received.append(lax.ppermute(pieces[step], 'mode', pairs))  26.5 us
    ppermute x2, starting transfers between devices, from_behind(): lax.ppermute(value, axis, [(source, source + steps) for source in range(i...  13.8 us
    ppermute x12, starting transfers between devices, exchange(): received.append(lax.ppermute(pieces[step], 'mode', pairs))  13.2 us
    pallas_call x1, Pallas kernels, derive(): pl.pallas_call(functools.partial(derive_kernel, count), in_specs=[vmem()]...  7.82 us
    pallas_call x2, Pallas kernels, pack(): pl.pallas_call(functools.partial(pack_kernel, count, len(carried), first)...  6.68 us
    pallas_call x2, Pallas kernels, physics(): pl.pallas_call(functools.partial(kernel, count), grid=(steps,), in_specs=...  4.35 us
    ppermute x2, waiting for transfers between devices, from_behind(): lax.ppermute(value, axis, [(source, source + steps) for source in range(i...  4.35 us
    pallas_call x1, Pallas kernels, momentum_of(): pl.pallas_call(functools.partial(momentum_kernel, count), in_specs=[vmem(...  2.19 us
  transfers between devices with their start and end apart: 14, of which 10 were waited for; matrix products, arithmetic and copies ran while one was open for 0% of the time, Pallas kernels for 19%

profile of v2, /device:TPU:1, one launch (start us, length us, event | category | flops | bytes accessed | tf_op | source)
XLA Modules:
  0.0 82.8 jit_solution(14818390478989955153)
XLA Ops:
  0.6 0.0 copy-start.4
  0.6 0.0 copy-start.5
  0.7 4.3 %shard_map.95 = (bf16[6,4,32,2,128]{4,3,2,1,0:T(2,128)(2,1)}, bf16[6,4,32,2,128]{4,3,2,1,0:T(2,128)(2,1)}, bf16[6,4,32,2,128]{4,3,2,1,0:T(2,128)(2,1)}, bf16[6,4,32,2,128]{4,3,2,1,0:T(2,128)(2,1)}) custom-call(bf16[12,32,2,2048]{3,2,1,0:T(2,128)(2,1)} %fields_ref.3), custom_call_target="tpu_custom_call" | custom-call | flops 1024 | bytes 1024 | tf_op jit(solution)/shard_map/pallas_call | solution.py:106
  5.0 2.1 %collective-permute-start = (bf16[6,4,32,2,128]{4,3,2,1,0:T(2,128)(2,1)}, bf16[6,4,32,2,128]{4,3,2,1,0:T(2,128)(2,1)S(1)}, u32[]{:S(2)}, u32[]{:S(2)}) collective-permute-start(bf16[6,4,32,2,128]{4,3,2,1,0:T(2,128)(2,1)} %get-tuple-element.34), channel_id=1, source_target_pairs={{0,8},{8,0},{16,24},{24,16},{1,9},{9,1},{17,25},{25,17},{2,10},{10... | collective-permute-start | bytes 1179656 | tf_op jit(solution)/shard_map/ppermute | solution.py:52
  7.1 1.2 %collective-permute-start.1 = (bf16[6,4,32,2,128]{4,3,2,1,0:T(2,128)(2,1)}, bf16[6,4,32,2,128]{4,3,2,1,0:T(2,128)(2,1)S(1)}, u32[]{:S(2)}, u32[]{:S(2)}) collective-permute-start(bf16[6,4,32,2,128]{4,3,2,1,0:T(2,128)(2,1)} %get-tuple-element.35), channel_id=1, source_target_pairs={{0,16},{8,24},{16,0},{24,8},{1,17},{9,25},{17,1},{25,9},{2,18},{10... | collective-permute-start | bytes 1179656 | tf_op jit(solution)/shard_map/ppermute | solution.py:52
  8.4 0.0 collective-permute-start.2
  8.4 0.0 copy-done.4
  8.4 0.0 copy-done.5
  8.4 0.0 copy-start
  8.4 1.9 %copy-done = bf16[12,32,2,2048]{3,2,1,0:T(2,128)(2,1)S(1)} copy-done((bf16[12,32,2,2048]{3,2,1,0:T(2,128)(2,1)S(1)}, bf16[12,32,2,2048]{3,2,1,0:T(2,128)(2,1)}, u32[]{:S(2)}) %copy-start) | copy-done | bytes 3145752
  10.3 0.0 copy-start.3
  10.3 2.3 %shard_map.96 = (bf16[6,4,32,2,128]{4,3,2,1,0:T(2,128)(2,1)S(1)}, bf16[6,4,32,2,128]{4,3,2,1,0:T(2,128)(2,1)S(1)}, bf16[6,4,32,2,128]{4,3,2,1,0:T(2,128)(2,1)S(1...) custom-call(bf16[12,32,2,2048]{3,2,1,0:T(2,128)(2,1)S(1)} %copy-done, ...), custom_call_target="tpu_custom_call" | custom-call | flops 1024 | bytes 1024 | tf_op jit(solution)/shard_map/pallas_call | solution.py:106
  12.6 3.5 %collective-permute-done = bf16[6,4,32,2,128]{4,3,2,1,0:T(2,128)(2,1)S(1)} collective-permute-done((bf16[6,4,32,2,128]{4,3,2,1,0:T(2,128)(2,1)}, bf16[6,4,32,2,128]{4,3,2,1,0:T(2,128)(2,1)S(1)}, u32[]{:S(2)}, u32[]{:S(2)}) %collective-permute-start) | collective-permute-done | bytes 393248 | tf_op jit(solution)/shard_map/ppermute | solution.py:52
  16.2 0.8 collective-permute-done.1
  17.0 8.5 %collective-permute-done.2 = bf16[6,4,32,2,128]{4,3,2,1,0:T(2,128)(2,1)S(1)} collective-permute-done((bf16[6,4,32,2,128]{4,3,2,1,0:T(2,128)(2,1)}, bf16[6,4,32,2,128]{4,3,2,1,0:T(2,128)(2,1)S(1)}, u32[]{:S(2)}, u32[]{:S(2)}) %collective-permute-start.2) | collective-permute-done | bytes 393248 | tf_op jit(solution)/shard_map/ppermute | solution.py:52
  25.5 1.2 %collective-permute-start.8 = (bf16[6,4,32,2,128]{4,3,2,1,0:T(2,128)(2,1)S(1)}, bf16[6,4,32,2,128]{4,3,2,1,0:T(2,128)(2,1)S(1)}, u32[]{:S(2)}, u32[]{:S(2)}) collective-permute-start(bf16[6,4,32,2,128]{4,3,2,1,0:T(2,128)(2,1)S(1)} %get-tuple-element.55), channel_id=1, source_target_pairs={{0,8},{8,0},{16,24},{24,16},{1,9},{9,1},{17,25},{25,17},{2,10},{10... | collective-permute-start | bytes 1179656 | tf_op jit(solution)/shard_map/ppermute | solution.py:52
  26.7 0.3 collective-permute-start.9
  27.0 1.2 %collective-permute-start.10 = (bf16[6,4,32,2,128]{4,3,2,1,0:T(2,128)(2,1)S(1)}, bf16[6,4,32,2,128]{4,3,2,1,0:T(2,128)(2,1)S(1)}, u32[]{:S(2)}, u32[]{:S(2)}) collective-permute-start(bf16[6,4,32,2,128]{4,3,2,1,0:T(2,128)(2,1)S(1)} %get-tuple-element.57), channel_id=1, source_target_pairs={{0,24},{8,16},{16,8},{24,0},{1,25},{9,17},{17,9},{25,1},{2,26},{10... | collective-permute-start | bytes 1179656 | tf_op jit(solution)/shard_map/ppermute | solution.py:52
  28.2 0.0 copy-done.3
  28.2 2.1 %shard_map.97 = (bf16[4,4,64,128]{3,2,1,0:T(8,128)(2,1)S(1)}, bf16[4,4,64,128]{3,2,1,0:T(8,128)(2,1)S(1)}, bf16[4,4,64,128]{3,2,1,0:T(8,128)(2,1)S(1)}, bf16[4,4...) custom-call(bf16[6,4,64,128]{3,2,1,0:T(8,128)(2,1)S(1)} %bitcast.21, bf16[6,4,64,128]{3,2,1,0:T(8,128)(2,1)S(1)} %bitcast.23, ...), custom_call_target="tpu_custom_call" | custom-call | flops 1024 | bytes 1024 | tf_op jit(solution)/shard_map/pallas_call | solution.py:214
  30.3 1.2 %collective-permute-start.3 = (bf16[4,4,64,128]{3,2,1,0:T(8,128)(2,1)S(1)}, bf16[4,4,64,128]{3,2,1,0:T(8,128)(2,1)S(1)}, u32[]{:S(2)}, u32[]{:S(2)}) collective-permute-start(bf16[4,4,64,128]{3,2,1,0:T(8,128)(2,1)S(1)} %get-tuple-element.48), channel_id=1, source_target_pairs={{0,8},{8,0},{16,24},{24,16},{1,9},{9,1},{17,25},{25,17},{2,10},{10... | collective-permute-start | bytes 786440 | tf_op jit(solution)/shard_map/ppermute | solution.py:52
  31.5 0.3 collective-permute-start.4
  31.8 2.5 %collective-permute-done.8 = bf16[6,4,32,2,128]{4,3,2,1,0:T(2,128)(2,1)S(1)} collective-permute-done((bf16[6,4,32,2,128]{4,3,2,1,0:T(2,128)(2,1)S(1)}, bf16[6,4,32,2,128]{4,3,2,1,0:T(2,128)(2,1)S(1)}, u32[]{:S(2)}, u32[]{:S(2)}) %collective-permute-start.8) | collective-permute-done | bytes 393248 | tf_op jit(solution)/shard_map/ppermute | solution.py:52
  34.4 1.1 %collective-permute-start.5 = (bf16[4,4,64,128]{3,2,1,0:T(8,128)(2,1)S(1)}, bf16[4,4,64,128]{3,2,1,0:T(8,128)(2,1)S(1)}, u32[]{:S(2)}, u32[]{:S(2)}) collective-permute-start(bf16[4,4,64,128]{3,2,1,0:T(8,128)(2,1)S(1)} %get-tuple-element.50), channel_id=1, source_target_pairs={{0,24},{8,16},{16,8},{24,0},{1,25},{9,17},{17,9},{25,1},{2,26},{10... | collective-permute-start | bytes 786440 | tf_op jit(solution)/shard_map/ppermute | solution.py:52
  35.5 2.0 %collective-permute-done.9 = bf16[6,4,32,2,128]{4,3,2,1,0:T(2,128)(2,1)S(1)} collective-permute-done((bf16[6,4,32,2,128]{4,3,2,1,0:T(2,128)(2,1)S(1)}, bf16[6,4,32,2,128]{4,3,2,1,0:T(2,128)(2,1)S(1)}, u32[]{:S(2)}, u32[]{:S(2)}) %collective-permute-start.9) | collective-permute-done | bytes 393248 | tf_op jit(solution)/shard_map/ppermute | solution.py:52
  37.5 4.5 %collective-permute-done.10 = bf16[6,4,32,2,128]{4,3,2,1,0:T(2,128)(2,1)S(1)} collective-permute-done((bf16[6,4,32,2,128]{4,3,2,1,0:T(2,128)(2,1)S(1)}, bf16[6,4,32,2,128]{4,3,2,1,0:T(2,128)(2,1)S(1)}, u32[]{:S(2)}, u32[]{:S(2)}) %collective-permute-start.10) | collective-permute-done | bytes 393248 | tf_op jit(solution)/shard_map/ppermute | solution.py:52
  42.0 2.2 %shard_map.100 = (bf16[3,4,64,128]{3,2,1,0:T(8,128)(2,1)S(1)}, bf16[3,4,64,128]{3,2,1,0:T(8,128)(2,1)S(1)}, bf16[3,4,64,128]{3,2,1,0:T(8,128)(2,1)S(1)}, bf16[3,4,64,128]{3,2,1,0:T(8,128)(2,1)S(1)}) custom-call(bf16[6,4,64,128]{3,2,1,0:T(8,128)(2,1)S(1)} %bitcast.20, bf16[6,4,64,128]{3,2,1,0:T(8,128)(2,1)S(1)} %bitcast.22, ...), custom_call_target="tpu_custom_call" | custom-call | flops 1024 | bytes 1024 | tf_op jit(solution)/shard_map/pallas_call | solution.py:214
  44.3 2.0 %collective-permute-start.11 = (bf16[3,4,64,128]{3,2,1,0:T(8,128)(2,1)S(1)}, bf16[3,4,64,128]{3,2,1,0:T(8,128)(2,1)S(1)}, u32[]{:S(2)}, u32[]{:S(2)}) collective-permute-start(bf16[3,4,64,128]{3,2,1,0:T(8,128)(2,1)S(1)} %get-tuple-element.60), channel_id=1, source_target_pairs={{0,8},{8,0},{16,24},{24,16},{1,9},{9,1},{17,25},{25,17},{2,10},{10... | collective-permute-start | bytes 589832 | tf_op jit(solution)/shard_map/ppermute | solution.py:52
  46.3 1.5 %collective-permute-start.12 = (bf16[3,4,64,128]{3,2,1,0:T(8,128)(2,1)S(1)}, bf16[3,4,64,128]{3,2,1,0:T(8,128)(2,1)S(1)}, u32[]{:S(2)}, u32[]{:S(2)}) collective-permute-start(bf16[3,4,64,128]{3,2,1,0:T(8,128)(2,1)S(1)} %get-tuple-element.61), channel_id=1, source_target_pairs={{0,16},{8,24},{16,0},{24,8},{1,17},{9,25},{17,1},{25,9},{2,18},{10... | collective-permute-start | bytes 589832 | tf_op jit(solution)/shard_map/ppermute | solution.py:52
  47.7 0.7 collective-permute-done.3.refs_1_
  48.5 1.1 %collective-permute-start.13 = (bf16[3,4,64,128]{3,2,1,0:T(8,128)(2,1)S(1)}, bf16[3,4,64,128]{3,2,1,0:T(8,128)(2,1)S(1)}, u32[]{:S(2)}, u32[]{:S(2)}) collective-permute-start(bf16[3,4,64,128]{3,2,1,0:T(8,128)(2,1)S(1)} %get-tuple-element.62), channel_id=1, source_target_pairs={{0,24},{8,16},{16,8},{24,0},{1,25},{9,17},{17,9},{25,1},{2,26},{10... | collective-permute-start | bytes 589832 | tf_op jit(solution)/shard_map/ppermute | solution.py:52
  49.6 1.9 %collective-permute-done.4.refs_2_ = bf16[4,4,64,128]{3,2,1,0:T(8,128)(2,1)S(1)} collective-permute-done((bf16[4,4,64,128]{3,2,1,0:T(8,128)(2,1)S(1)}, bf16[4,4,64,128]{3,2,1,0:T(8,128)(2,1)S(1)}, u32[]{:S(2)}, u32[]{:S(2)}) %collective-permute-start.4) | collective-permute-done | bytes 262176 | tf_op jit(solution)/shard_map/ppermute | solution.py:52
  51.5 1.8 %collective-permute-done.5.refs_3_ = bf16[4,4,64,128]{3,2,1,0:T(8,128)(2,1)S(1)} collective-permute-done((bf16[4,4,64,128]{3,2,1,0:T(8,128)(2,1)S(1)}, bf16[4,4,64,128]{3,2,1,0:T(8,128)(2,1)S(1)}, u32[]{:S(2)}, u32[]{:S(2)}) %collective-permute-start.5) | collective-permute-done | bytes 262176 | tf_op jit(solution)/shard_map/ppermute | solution.py:52
  53.3 0.0 copy-done.8
  53.3 1.2 %shard_map.98 = (bf16[4,2,64,128]{3,2,1,0:T(8,128)(2,1)S(1)}, bf16[4,2,64,128]{3,2,1,0:T(8,128)(2,1)S(1)}) custom-call(bf16[4,4,64,128]{3,2,1,0:T(8,128)(2,1)S(1)} %get-tuple-element.47.refs_0_, bf16[4,4,64,128]{3,2,1,0:T(8,128)(2,1)S(1)} %collective-permute-done.3.refs_1_, bf16[4,4,64,128]{3,2,1,0:T(8,128)(2,1)S(1)} %collective-permute-done.4.refs_2_, ...), custom_call_target="tpu_custom_call" | custom-call | flops 1024 | bytes 1024 | tf_op jit(solution)/shard_map/pallas_call | solution.py:254
  54.5 11.9 %collective-permute-start.6 = (bf16[4,2,64,128]{3,2,1,0:T(8,128)(2,1)S(1)}, bf16[4,2,64,128]{3,2,1,0:T(8,128)(2,1)S(1)}, u32[]{:S(2)}, u32[]{:S(2)}) collective-permute-start(bf16[4,2,64,128]{3,2,1,0:T(8,128)(2,1)S(1)} %get-tuple-element.51), channel_id=1, source_target_pairs={{0,1},{1,2},{2,3},{3,4},{4,5},{5,6},{6,7},{8,9},{9,10},{10,11},{11... | collective-permute-start | bytes 393224 | tf_op jit(solution)/shard_map/ppermute | solution.py:59
  66.4 1.9 %collective-permute-start.7 = (bf16[4,2,64,128]{3,2,1,0:T(8,128)(2,1)S(1)}, bf16[4,2,64,128]{3,2,1,0:T(8,128)(2,1)S(1)}, u32[]{:S(2)}, u32[]{:S(2)}) collective-permute-start(bf16[4,2,64,128]{3,2,1,0:T(8,128)(2,1)S(1)} %get-tuple-element.52), channel_id=1, source_target_pairs={{1,0},{2,1},{3,2},{4,3},{5,4},{6,5},{7,6},{9,8},{10,9},{11,10},{12... | collective-permute-start | bytes 393224 | tf_op jit(solution)/shard_map/ppermute | solution.py:59
  68.4 0.0 collective-permute-done.6.refs_4_
  68.4 4.3 %collective-permute-done.7.refs_5_ = bf16[4,2,64,128]{3,2,1,0:T(8,128)(2,1)S(1)} collective-permute-done((bf16[4,2,64,128]{3,2,1,0:T(8,128)(2,1)S(1)}, bf16[4,2,64,128]{3,2,1,0:T(8,128)(2,1)S(1)}, u32[]{:S(2)}, u32[]{:S(2)}) %collective-permute-start.7) | collective-permute-done | bytes 131104 | tf_op jit(solution)/shard_map/ppermute | solution.py:59
  72.7 0.0 copy-done.1
  72.7 0.0 copy-done.2
  72.7 0.0 copy-done.6
  72.7 0.0 copy-done.7
  72.8 7.8 %shard_map.99 = (f32[3072,128]{1,0:T(8,128)}, f32[3,16,64,128]{3,2,1,0:T(8,128)S(1)}) custom-call(bf16[4,4,64,128]{3,2,1,0:T(8,128)(2,1)S(1)} %get-tuple-element.47.refs_0_, bf16[4,4,64,128]{3,2,1,0:T(8,128)(2,1)S(1)} %collective-permute-done.3.refs_1_, bf16[4,4,64,128]{3,2,1,0:T(8,128)(2,1)S(1)} %collective-permute-done.4.refs_2_, ...), custom_call_target="tpu_custom_call" | custom-call | flops 1024 | bytes 1024 | tf_op jit(solution)/shard_map/pallas_call | solution.py:338
  80.6 0.0 collective-permute-done.11.refs_1_
  80.6 0.0 collective-permute-done.12.refs_2_
  80.6 0.0 collective-permute-done.13.refs_3_
  80.6 2.2 %shard_map.101 = f32[3072,128]{1,0:T(8,128)} custom-call(bf16[3,4,64,128]{3,2,1,0:T(8,128)(2,1)S(1)} %get-tuple-element.59.refs_0_, bf16[3,4,64,128]{3,2,1,0:T(8,128)(2,1)S(1)} %collective-permute-done.11.refs_1_, bf16[3,4,64,128]{3,2,1,0:T(8,128)(2,1)S(1)} %collective-permute-done.12.refs_2_, bf16[3,4,64,128]{3,2,1,0:T(8,128)(2,1)S(1)} %collective-permute-done.13.refs_3_, ...), custom_call_target="tpu_custom_call" | custom-call | flops 1024 | bytes 1024 | tf_op jit(solution)/shard_map/pallas_call | solution.py:381
  (5 shorter events, 0.0 us)
Async XLA Ops:
  0.6 7.7 %copy-start.4 = (bf16[256,256]{1,0:T(8,128)(2,1)S(1)}, bf16[256,256]{1,0:T(8,128)(2,1)}, u32[]{:S(2)}) copy-start(bf16[256,256]{1,0:T(8,128)(2,1)} %constant.5.clone.refs_1_) | copy-start | bytes 393220
  0.6 7.7 %copy-start.5 = (bf16[256,256]{1,0:T(8,128)(2,1)S(1)}, bf16[256,256]{1,0:T(8,128)(2,1)}, u32[]{:S(2)}) copy-start(bf16[256,256]{1,0:T(8,128)(2,1)} %constant.4.clone.refs_0_) | copy-start | bytes 393220
  5.0 11.2 %collective-permute-start = (bf16[6,4,32,2,128]{4,3,2,1,0:T(2,128)(2,1)}, bf16[6,4,32,2,128]{4,3,2,1,0:T(2,128)(2,1)S(1)}, u32[]{:S(2)}, u32[]{:S(2)}) collective-permute-start(bf16[6,4,32,2,128]{4,3,2,1,0:T(2,128)(2,1)} %get-tuple-element.34), channel_id=1, source_target_pairs={{0,8},{8,0},{16,24},{24,16},{1,9},{9,1},{17,25},{25,17},{2,10},{10... | collective-permute-start | bytes 1179656 | tf_op jit(solution)/shard_map/ppermute | solution.py:52
  7.1 9.9 %collective-permute-start.1 = (bf16[6,4,32,2,128]{4,3,2,1,0:T(2,128)(2,1)}, bf16[6,4,32,2,128]{4,3,2,1,0:T(2,128)(2,1)S(1)}, u32[]{:S(2)}, u32[]{:S(2)}) collective-permute-start(bf16[6,4,32,2,128]{4,3,2,1,0:T(2,128)(2,1)} %get-tuple-element.35), channel_id=1, source_target_pairs={{0,16},{8,24},{16,0},{24,8},{1,17},{9,25},{17,1},{25,9},{2,18},{10... | collective-permute-start | bytes 1179656 | tf_op jit(solution)/shard_map/ppermute | solution.py:52
  8.4 17.2 %collective-permute-start.2 = (bf16[6,4,32,2,128]{4,3,2,1,0:T(2,128)(2,1)}, bf16[6,4,32,2,128]{4,3,2,1,0:T(2,128)(2,1)S(1)}, u32[]{:S(2)}, u32[]{:S(2)}) collective-permute-start(bf16[6,4,32,2,128]{4,3,2,1,0:T(2,128)(2,1)} %get-tuple-element.36), channel_id=1, source_target_pairs={{0,24},{8,16},{16,8},{24,0},{1,25},{9,17},{17,9},{25,1},{2,26},{10... | collective-permute-start | bytes 1179656 | tf_op jit(solution)/shard_map/ppermute | solution.py:52
  8.4 1.9 %copy-start = (bf16[12,32,2,2048]{3,2,1,0:T(2,128)(2,1)S(1)}, bf16[12,32,2,2048]{3,2,1,0:T(2,128)(2,1)}, u32[]{:S(2)}) copy-start(bf16[12,32,2,2048]{3,2,1,0:T(2,128)(2,1)} %fields_ref.3) | copy-start | bytes 9437188
  10.3 17.9 %copy-start.3 = (bf16[6,4,32,2,128]{4,3,2,1,0:T(2,128)(2,1)S(1)}, bf16[6,4,32,2,128]{4,3,2,1,0:T(2,128)(2,1)}, u32[]{:S(2)}) copy-start(bf16[6,4,32,2,128]{4,3,2,1,0:T(2,128)(2,1)} %get-tuple-element.41) | copy-start | bytes 1179652
  25.5 8.8 %collective-permute-start.8 = (bf16[6,4,32,2,128]{4,3,2,1,0:T(2,128)(2,1)S(1)}, bf16[6,4,32,2,128]{4,3,2,1,0:T(2,128)(2,1)S(1)}, u32[]{:S(2)}, u32[]{:S(2)}) collective-permute-start(bf16[6,4,32,2,128]{4,3,2,1,0:T(2,128)(2,1)S(1)} %get-tuple-element.55), channel_id=1, source_target_pairs={{0,8},{8,0},{16,24},{24,16},{1,9},{9,1},{17,25},{25,17},{2,10},{10... | collective-permute-start | bytes 1179656 | tf_op jit(solution)/shard_map/ppermute | solution.py:52
  26.7 10.8 %collective-permute-start.9 = (bf16[6,4,32,2,128]{4,3,2,1,0:T(2,128)(2,1)S(1)}, bf16[6,4,32,2,128]{4,3,2,1,0:T(2,128)(2,1)S(1)}, u32[]{:S(2)}, u32[]{:S(2)}) collective-permute-start(bf16[6,4,32,2,128]{4,3,2,1,0:T(2,128)(2,1)S(1)} %get-tuple-element.56), channel_id=1, source_target_pairs={{0,16},{8,24},{16,0},{24,8},{1,17},{9,25},{17,1},{25,9},{2,18},{10... | collective-permute-start | bytes 1179656 | tf_op jit(solution)/shard_map/ppermute | solution.py:52
  27.0 15.1 %collective-permute-start.10 = (bf16[6,4,32,2,128]{4,3,2,1,0:T(2,128)(2,1)S(1)}, bf16[6,4,32,2,128]{4,3,2,1,0:T(2,128)(2,1)S(1)}, u32[]{:S(2)}, u32[]{:S(2)}) collective-permute-start(bf16[6,4,32,2,128]{4,3,2,1,0:T(2,128)(2,1)S(1)} %get-tuple-element.57), channel_id=1, source_target_pairs={{0,24},{8,16},{16,8},{24,0},{1,25},{9,17},{17,9},{25,1},{2,26},{10... | collective-permute-start | bytes 1179656 | tf_op jit(solution)/shard_map/ppermute | solution.py:52
  30.3 18.1 %collective-permute-start.3 = (bf16[4,4,64,128]{3,2,1,0:T(8,128)(2,1)S(1)}, bf16[4,4,64,128]{3,2,1,0:T(8,128)(2,1)S(1)}, u32[]{:S(2)}, u32[]{:S(2)}) collective-permute-start(bf16[4,4,64,128]{3,2,1,0:T(8,128)(2,1)S(1)} %get-tuple-element.48), channel_id=1, source_target_pairs={{0,8},{8,0},{16,24},{24,16},{1,9},{9,1},{17,25},{25,17},{2,10},{10... | collective-permute-start | bytes 786440 | tf_op jit(solution)/shard_map/ppermute | solution.py:52
  31.5 19.9 %collective-permute-start.4 = (bf16[4,4,64,128]{3,2,1,0:T(8,128)(2,1)S(1)}, bf16[4,4,64,128]{3,2,1,0:T(8,128)(2,1)S(1)}, u32[]{:S(2)}, u32[]{:S(2)}) collective-permute-start(bf16[4,4,64,128]{3,2,1,0:T(8,128)(2,1)S(1)} %get-tuple-element.49), channel_id=1, source_target_pairs={{0,16},{8,24},{16,0},{24,8},{1,17},{9,25},{17,1},{25,9},{2,18},{10... | collective-permute-start | bytes 786440 | tf_op jit(solution)/shard_map/ppermute | solution.py:52
  34.4 18.9 %collective-permute-start.5 = (bf16[4,4,64,128]{3,2,1,0:T(8,128)(2,1)S(1)}, bf16[4,4,64,128]{3,2,1,0:T(8,128)(2,1)S(1)}, u32[]{:S(2)}, u32[]{:S(2)}) collective-permute-start(bf16[4,4,64,128]{3,2,1,0:T(8,128)(2,1)S(1)} %get-tuple-element.50), channel_id=1, source_target_pairs={{0,24},{8,16},{16,8},{24,0},{1,25},{9,17},{17,9},{25,1},{2,26},{10... | collective-permute-start | bytes 786440 | tf_op jit(solution)/shard_map/ppermute | solution.py:52
  42.0 11.3 %copy-start.8 = (s32[2,256]{1,0:T(2,128)S(1)}, s32[2,256]{1,0:T(2,128)}, u32[]{:S(2)}) copy-start(s32[2,256]{1,0:T(2,128)} %refs_4_.1) | copy-start | bytes 6148
  42.0 30.7 %copy-start.1 = (bf16[5,64,2048]{2,1,0:T(8,128)(2,1)S(1)}, bf16[5,64,2048]{2,1,0:T(8,128)(2,1)}, u32[]{:S(2)}) copy-start(bf16[5,64,2048]{2,1,0:T(8,128)(2,1)} %refs_6_.1) | copy-start | bytes 3932164
  42.0 30.7 %copy-start.2 = (bf16[5,64,2048]{2,1,0:T(8,128)(2,1)S(1)}, bf16[5,64,2048]{2,1,0:T(8,128)(2,1)}, u32[]{:S(2)}) copy-start(bf16[5,64,2048]{2,1,0:T(8,128)(2,1)} %refs_7_.1) | copy-start | bytes 3932164
  42.0 30.7 %copy-start.6 = (f32[2048]{0:T(1024)S(1)}, f32[2048]{0:T(1024)}, u32[]{:S(2)}) copy-start(f32[2048]{0:T(1024)} %param.9) | copy-start | bytes 24580
  42.0 30.7 %copy-start.7 = (s32[32,5]{0,1:T(8,128)S(1)}, s32[32,5]{0,1:T(8,128)}, u32[]{:S(2)}) copy-start(s32[32,5]{0,1:T(8,128)} %param.12) | copy-start | bytes 1924
  44.3 36.3 %collective-permute-start.11 = (bf16[3,4,64,128]{3,2,1,0:T(8,128)(2,1)S(1)}, bf16[3,4,64,128]{3,2,1,0:T(8,128)(2,1)S(1)}, u32[]{:S(2)}, u32[]{:S(2)}) collective-permute-start(bf16[3,4,64,128]{3,2,1,0:T(8,128)(2,1)S(1)} %get-tuple-element.60), channel_id=1, source_target_pairs={{0,8},{8,0},{16,24},{24,16},{1,9},{9,1},{17,25},{25,17},{2,10},{10... | collective-permute-start | bytes 589832 | tf_op jit(solution)/shard_map/ppermute | solution.py:52
  46.3 34.3 %collective-permute-start.12 = (bf16[3,4,64,128]{3,2,1,0:T(8,128)(2,1)S(1)}, bf16[3,4,64,128]{3,2,1,0:T(8,128)(2,1)S(1)}, u32[]{:S(2)}, u32[]{:S(2)}) collective-permute-start(bf16[3,4,64,128]{3,2,1,0:T(8,128)(2,1)S(1)} %get-tuple-element.61), channel_id=1, source_target_pairs={{0,16},{8,24},{16,0},{24,8},{1,17},{9,25},{17,1},{25,9},{2,18},{10... | collective-permute-start | bytes 589832 | tf_op jit(solution)/shard_map/ppermute | solution.py:52
  48.5 32.1 %collective-permute-start.13 = (bf16[3,4,64,128]{3,2,1,0:T(8,128)(2,1)S(1)}, bf16[3,4,64,128]{3,2,1,0:T(8,128)(2,1)S(1)}, u32[]{:S(2)}, u32[]{:S(2)}) collective-permute-start(bf16[3,4,64,128]{3,2,1,0:T(8,128)(2,1)S(1)} %get-tuple-element.62), channel_id=1, source_target_pairs={{0,24},{8,16},{16,8},{24,0},{1,25},{9,17},{17,9},{25,1},{2,26},{10... | collective-permute-start | bytes 589832 | tf_op jit(solution)/shard_map/ppermute | solution.py:52
  54.5 13.8 %collective-permute-start.6 = (bf16[4,2,64,128]{3,2,1,0:T(8,128)(2,1)S(1)}, bf16[4,2,64,128]{3,2,1,0:T(8,128)(2,1)S(1)}, u32[]{:S(2)}, u32[]{:S(2)}) collective-permute-start(bf16[4,2,64,128]{3,2,1,0:T(8,128)(2,1)S(1)} %get-tuple-element.51), channel_id=1, source_target_pairs={{0,1},{1,2},{2,3},{3,4},{4,5},{5,6},{6,7},{8,9},{9,10},{10,11},{11... | collective-permute-start | bytes 393224 | tf_op jit(solution)/shard_map/ppermute | solution.py:59
  66.4 6.3 %collective-permute-start.7 = (bf16[4,2,64,128]{3,2,1,0:T(8,128)(2,1)S(1)}, bf16[4,2,64,128]{3,2,1,0:T(8,128)(2,1)S(1)}, u32[]{:S(2)}, u32[]{:S(2)}) collective-permute-start(bf16[4,2,64,128]{3,2,1,0:T(8,128)(2,1)S(1)} %get-tuple-element.52), channel_id=1, source_target_pairs={{1,0},{2,1},{3,2},{4,3},{5,4},{6,5},{7,6},{9,8},{10,9},{11,10},{12... | collective-permute-start | bytes 393224 | tf_op jit(solution)/shard_map/ppermute | solution.py:59

commit v3 on v2

--- a/solution.py
+++ b/solution.py
@@ -16,7 +16,6 @@
 NNZB = 5
 LANES = 128
 VMEM_LIMIT = 24 * 1024 * 1024
-FIRST_LIMIT = 61 * 1024 * 1024
 
 
 def params(limit=VMEM_LIMIT):
@@ -44,12 +43,12 @@
 
 
 def exchange(pieces):
-    count = len(pieces)
+    count = len(pieces) + 1
     power = count & (count - 1) == 0
-    received = [pieces[0]]
+    received = []
     for step in range(1, count):
         pairs = [(i, i ^ step if power else (i + step) % count) for i in range(count)]
-        received.append(lax.ppermute(pieces[step], "mode", pairs))
+        received.append(lax.ppermute(pieces[step - 1], "mode", pairs))
     return received
 
 
@@ -74,60 +73,78 @@
     return (inverse.reshape(angle_total, 2 * mode_total), forward)
 
 
-def pack_kernel(count, carried, first, fields_ref, *refs):
-    me = lax.axis_index("mode")
-    inputs, refs = refs[:carried], refs[carried:]
-    out_refs, outputs, (fields_vmem, load, sems) = refs[:count], refs[count : count + carried], refs[count + carried :]
-    components, tiles = out_refs[0].shape[:2]
-    loads = []
-    for c in range(components):
-        loads.append(pltpu.make_async_copy(fields_ref.at[first + c], fields_vmem.at[c], load.at[c]))
-        loads[c].start()
-    copies = []
-    for c in range(components):
-        loads[c].wait()
-        for step in range(count):
-            share = dest_of(me, step, count)
-            for t in range(tiles):
-                start = pl.multiple_of((share * tiles + t) * LANES, LANES)
-                source = fields_vmem.at[c, :, :, pl.ds(start, LANES)]
-                copies.append(pltpu.make_async_copy(source, out_refs[step].at[c, t], sems.at[c, step, t]))
-                copies[-1].start()
-    for source, target in zip(inputs, outputs):
+def pieces_of(fields_ref, share, out_ref, first=0):
+    components, tiles = out_ref.shape[:2]
+    pairs = []
+    for t in range(tiles):
+        start = pl.multiple_of((share * tiles + t) * LANES, LANES)
+        for c in range(components):
+            pairs.append((fields_ref.at[first + c, :, :, pl.ds(start, LANES)], out_ref.at[c, t]))
+    return pairs
+
+
+def run_copies(pairs, sems, beside=()):
+    copies = [pltpu.make_async_copy(source, target, sems.at[i]) for i, (source, target) in enumerate(pairs)]
+    for copy in copies:
+        copy.start()
+    for source, target in beside:
         target[...] = source[...]
     for copy in copies:
         copy.wait()
 
 
-def pack(fields, first, components, count, carried, limit):
-    _, mode_count, _, width = fields.shape
-    tiles = width // count // LANES
-    shape = (components, tiles, mode_count, 2, LANES)
-    return pl.pallas_call(
-        functools.partial(pack_kernel, count, len(carried), first),
-        in_specs=[pl.BlockSpec(memory_space=pl.ANY)] + [vmem()] * len(carried),
-        out_specs=[vmem()] * (count + len(carried)),
-        out_shape=[jax.ShapeDtypeStruct(shape, jnp.bfloat16)] * count
+def share_shape(fields, count):
+    components, mode_count, _, width = fields.shape
+    return (components, width // count // LANES, mode_count, 2, LANES)
+
+
+def pack_step(fields, step, count):
+    shape = share_shape(fields, count)
+
+    def kernel(fields_ref, out_ref, sems):
+        run_copies(pieces_of(fields_ref, dest_of(lax.axis_index("mode"), step, count), out_ref), sems)
+
+    return pl.pallas_call(
+        kernel,
+        in_specs=[vmem()],
+        out_specs=vmem(),
+        out_shape=jax.ShapeDtypeStruct(shape, jnp.bfloat16),
+        scratch_shapes=[pltpu.SemaphoreType.DMA((shape[0] * shape[1],))],
+        compiler_params=params(),
+        cost_estimate=cost(),
+    )(fields)
+
+
+def pack_rest(fields, others, count, carried):
+    shape = share_shape(fields, count)
+
+    def kernel(fields_ref, others_ref, *refs):
+        inputs, (own_ref, all_ref), outputs = refs[: len(carried)], refs[len(carried) : len(carried) + 2], refs[len(carried) + 2 : -1]
+        pairs = pieces_of(fields_ref, lax.axis_index("mode"), own_ref)
+        for share in range(count):
+            pairs += pieces_of(others_ref, share, all_ref.at[share], shape[0])
+        run_copies(pairs, refs[-1], zip(inputs, outputs))
+
+    return pl.pallas_call(
+        kernel,
+        in_specs=[vmem(), pl.BlockSpec(memory_space=pl.ANY)] + [vmem()] * len(carried),
+        out_specs=[vmem()] * (2 + len(carried)),
+        out_shape=[jax.ShapeDtypeStruct(shape, jnp.bfloat16), jax.ShapeDtypeStruct((count,) + shape, jnp.bfloat16)]
         + [jax.ShapeDtypeStruct(value.shape, value.dtype) for value in carried],
-        scratch_shapes=[
-            pltpu.VMEM((components, mode_count, 2, width), jnp.bfloat16),
-            pltpu.SemaphoreType.DMA((components,)),
-            pltpu.SemaphoreType.DMA((components, count, tiles)),
-        ],
-        compiler_params=params(limit),
-        cost_estimate=cost(),
-    )(fields, *carried)
+        scratch_shapes=[pltpu.SemaphoreType.DMA(((count + 1) * shape[0] * shape[1],))],
+        compiler_params=params(),
+        cost_estimate=cost(),
+    )(fields, others, *carried)
 
 
 def cross(a, b):
     return [a[1] * b[2] - a[2] * b[1], a[2] * b[0] - a[0] * b[2], a[0] * b[1] - a[1] * b[0]]
 
 
-def to_physical(count, in_refs, inverse, x_ref, store):
-    me = lax.axis_index("mode")
+def to_physical(sources, in_refs, inverse, x_ref, store):
     components, tiles, rows, _ = in_refs[0].shape
-    for step in range(count):
-        at = pl.multiple_of(source_of(me, step, count) * rows, rows)
+    for step, source in enumerate(sources):
+        at = pl.multiple_of(source * rows, rows)
         for c in range(components):
             for t in range(tiles):
                 x_ref[c, pl.ds(at, rows), t * LANES : (t + 1) * LANES] = in_refs[step][c, t]
@@ -159,7 +176,9 @@
     def store(c, value):
         physical_ref[c] = value
 
-    to_physical(count, in_refs, inverse_ref[...], x_ref, store)
+    me = lax.axis_index("mode")
+    sources = [source_of(me, step, count) for step in range(count)]
+    to_physical(sources, in_refs, inverse_ref[...], x_ref, store)
     for i in range(THETA // CHUNK):
         at = slice(i * CHUNK, (i + 1) * CHUNK)
         velocity = [physical_ref[c, at] for c in range(3)]
@@ -171,13 +190,13 @@
 
 
 def second_kernel(count, *refs):
-    in_refs, (first_ref, inverse_ref, forward_ref) = refs[:count], refs[count : count + 3]
-    out_refs, (physical_ref, x_ref, product_ref, table_ref) = refs[count + 3 : 2 * count + 3], refs[2 * count + 3 :]
+    in_ref, first_ref, inverse_ref, forward_ref = refs[:4]
+    out_refs, (physical_ref, x_ref, product_ref, table_ref) = refs[4 : count + 4], refs[count + 4 :]
 
     def store(c, value):
         physical_ref[c] = value
 
-    to_physical(count, in_refs, inverse_ref[...], x_ref, store)
+    to_physical(range(count), [in_ref.at[source] for source in range(count)], inverse_ref[...], x_ref, store)
     for i in range(THETA // CHUNK):
         at = slice(i * CHUNK, (i + 1) * CHUNK)
         velocity = [first_ref[c, at] for c in range(3)]
@@ -191,13 +210,16 @@
 
 
 def physics(kernel, received, extra, inverse, forward, outputs, keep):
-    count = len(received)
-    components, tiles, rows, _ = received[0].shape
+    components, tiles, rows, _ = received[0].shape[-4:]
+    count = 2 * M // rows
     group = 2 if tiles % 2 == 0 else 1
     steps = tiles // group
     width = group * LANES
     share = tiles * LANES
-    in_block = pl.BlockSpec((components, group, rows, LANES), lambda i: (0, i, 0, 0))
+    if keep:
+        in_block = pl.BlockSpec((components, group, rows, LANES), lambda i: (0, i, 0, 0))
+    else:
+        in_block = pl.BlockSpec((count, components, group, rows, LANES), lambda i: (0, 0, i, 0, 0))
     out_block = pl.BlockSpec((outputs, group, rows, LANES), lambda i: (0, i, 0, 0))
     whole = pl.BlockSpec((THETA, 2 * M), lambda i: (0, 0))
     turned = pl.BlockSpec((2 * M, THETA), lambda i: (0, 0))
@@ -214,7 +236,7 @@
     return pl.pallas_call(
         functools.partial(kernel, count),
         grid=(steps,),
-        in_specs=[in_block] * count + [kept] * len(extra) + [whole, turned],
+        in_specs=[in_block] * len(received) + [kept] * len(extra) + [whole, turned],
         out_specs=[out_block] * count + ([kept] if keep else []),
         out_shape=out_shape + ([kept_shape] if keep else []),
         scratch_shapes=scratch,
@@ -326,7 +348,7 @@
         momentum_ref[2, b] = along_z[3]
         return carry
 
-    lax.fori_loop(0, node_tiles, pair, 0)
+    lax.fori_loop(0, node_tiles, pair, 0, unroll=2)
 
 
 def derive(received, from_prev, from_next, radial_blocks, axial_blocks, radius, columns):
@@ -402,21 +424,24 @@
     inverse, forward = jnp.asarray(inverse), jnp.asarray(forward)
 
     def joined(pieces):
-        return [piece.reshape(piece.shape[:2] + (rows, LANES)) for piece in pieces]
-
-    flow = exchange(pack(mode_fields, 0, 6, count, [], FIRST_LIMIT))
-    *pieces, inverse, forward = pack(mode_fields, 6, 6, count, [inverse, forward], VMEM_LIMIT)
-    flow, pieces = lax.optimization_barrier((flow, pieces))
-    flow, sources = joined(flow), joined(exchange(pieces))
+        return [piece.reshape(piece.shape[:-3] + (rows, LANES)) for piece in pieces]
+
+    fields = mode_fields[:6]
+    arrived = exchange([pack_step(fields, step, count) for step in range(1, count)])
+    own, shares, inverse, forward = pack_rest(fields, mode_fields, count, [inverse, forward])
+    arrived, shares = lax.optimization_barrier((arrived, shares))
+    flow = joined([own] + arrived)
+    sources = joined([lax.all_to_all(shares, "mode", 0, 0, tiled=True)])
     *terms, physical = physics(first_kernel, flow, [], inverse, forward, 4, True)
-    local = exchange(terms)
+    local = terms[:1] + exchange(terms[1:])
     toward_prev, toward_next = interface(local, interface_nodes)
     from_prev = from_behind(toward_next, "mer", 1)
     from_next = from_behind(toward_prev, "mer", -1)
     induction, gradient = derive(
         local, from_prev, from_next, radial_blocks, axial_blocks, radius.reshape(1, width), block_columns.T
     )
-    lorentz = exchange(physics(second_kernel, sources, [physical], inverse, forward, 3, False))
+    lorentz = list(physics(second_kernel, sources, [physical], inverse, forward, 3, False))
+    lorentz = lorentz[:1] + exchange(lorentz[1:])
     momentum = momentum_of(lorentz, gradient)
     return (whole_output(induction, mode_count, width), whole_output(momentum, mode_count, width))
 

time: 83 us -> 83.1 us (level)
  local copies, waits for them, and re-layouts: 1.93 us -> 8.2 us
  starting transfers between devices: 27 us -> 24.2 us
  Pallas kernels: 22.3 us -> 20.2 us
  waiting for transfers between devices: 30.8 us -> 29.3 us
    ppermute x12 -> x9, waiting for transfers between devices: 26.5 us -> 14 us  [exchange(): received.append(lax.ppermute(pieces[step - 1], 'mode', pairs))]
    all_to_all x0 -> x1, waiting for transfers between devices: none -> 11 us  [body(): sources = joined([lax.all_to_all(shares, 'mode', 0, 0, tiled=True)])]
    ppermute x12 -> x9, starting transfers between devices: 13.2 us -> 9.1 us  [exchange(): received.append(lax.ppermute(pieces[step - 1], 'mode', pairs))]
    all_to_all x0 -> x1, starting transfers between devices: none -> 3.56 us  [body(): sources = joined([lax.all_to_all(shares, 'mode', 0, 0, tiled=True)])]
    unnamed x18 -> x24, local copies, waits for them, and re-layouts: 1.93 us -> 5.29 us
    slice x0 -> x1, local copies, waits for them, and re-layouts: none -> 2.9 us  [body(): fields = mode_fields[:6]]
    ppermute x2, starting transfers between devices: 13.8 us -> 11.5 us  [from_behind(): lax.ppermute(value, axis, [(source, source + steps) for source in range(i...]
    pallas_call x2 -> x4, Pallas kernels: 6.68 us -> 5.44 us  [the longest x1 3.83 us: pack_rest(): pl.pallas_call(kernel, in_specs=[vmem(), pl.BlockSpec(memory_space=pl.ANY...]
  transfers between devices with their start and end apart: 14 -> 12, of which waited for: 10 -> 7; matrix products, arithmetic and copies ran while one was open for 0% -> 0% of each run, Pallas kernels for 19% -> 21%
where the time goes in v3:
time: 83.1 us; the launch traced here: 82.7 us
  waiting for transfers between devices  29.3 us (35%)
  starting transfers between devices  24.2 us (29%)
  Pallas kernels  20.2 us (24%)
  local copies, waits for them, and re-layouts  8.2 us (10%)
  between operations  0.85 us (1%)
    ppermute x9, waiting for transfers between devices, exchange(): received.append(lax.ppermute(pieces[step - 1], 'mode', pairs))  14 us
    ppermute x2, starting transfers between devices, from_behind(): lax.ppermute(value, axis, [(source, source + steps) for source in range(i...  11.5 us
    all_to_all x1, waiting for transfers between devices, body(): sources = joined([lax.all_to_all(shares, 'mode', 0, 0, tiled=True)])  11 us
    ppermute x9, starting transfers between devices, exchange(): received.append(lax.ppermute(pieces[step - 1], 'mode', pairs))  9.1 us
    pallas_call x1, Pallas kernels, derive(): pl.pallas_call(functools.partial(derive_kernel, count), in_specs=[vmem()]...  6.61 us
    unnamed x24, local copies, waits for them, and re-layouts  5.29 us
    pallas_call x2, Pallas kernels, physics(): pl.pallas_call(functools.partial(kernel, count), grid=(steps,), in_specs=...  4.7 us
    ppermute x2, waiting for transfers between devices, from_behind(): lax.ppermute(value, axis, [(source, source + steps) for source in range(i...  4.35 us
  transfers between devices with their start and end apart: 12, of which 7 were waited for; matrix products, arithmetic and copies ran while one was open for 0% of the time, Pallas kernels for 21%

profile of v3, /device:TPU:1, one launch (start us, length us, event | category | flops | bytes accessed | tf_op | source)
XLA Modules:
  0.0 82.7 jit_solution(9738920256604607996)
XLA Ops:
  0.6 2.9 %slice.3.fields_ref = bf16[6,32,2,2048]{3,2,1,0:T(2,128)(2,1)S(1)} slice(bf16[12,32,2,2048]{3,2,1,0:T(2,128)(2,1)} %others_ref.1), slice={[0:6], [0:32], [0:2], [0:2048]} | slice | bytes 3145728 | tf_op jit(solution)/shard_map/slice | solution.py:429
  3.5 0.5 shard_map.96
  4.1 0.0 copy-start
  4.1 0.0 copy-start.7
  4.1 0.0 copy-start.8
  4.1 2.1 %collective-permute-start = (bf16[6,4,32,2,128]{4,3,2,1,0:T(2,128)(2,1)S(1)}, bf16[6,4,32,2,128]{4,3,2,1,0:T(2,128)(2,1)S(1)}, u32[]{:S(2)}, u32[]{:S(2)}) collective-permute-start(bf16[6,4,32,2,128]{4,3,2,1,0:T(2,128)(2,1)S(1)} %shard_map.96), channel_id=1, source_target_pairs={{0,8},{8,0},{16,24},{24,16},{1,9},{9,1},{17,25},{25,17},{2,10},{10... | collective-permute-start | bytes 1179656 | tf_op jit(solution)/shard_map/ppermute | solution.py:51
  6.2 0.5 shard_map.97
  6.8 1.3 %collective-permute-start.1 = (bf16[6,4,32,2,128]{4,3,2,1,0:T(2,128)(2,1)S(1)}, bf16[6,4,32,2,128]{4,3,2,1,0:T(2,128)(2,1)S(1)}, u32[]{:S(2)}, u32[]{:S(2)}) collective-permute-start(bf16[6,4,32,2,128]{4,3,2,1,0:T(2,128)(2,1)S(1)} %shard_map.97), channel_id=1, source_target_pairs={{0,16},{8,24},{16,0},{24,8},{1,17},{9,25},{17,1},{25,9},{2,18},{10... | collective-permute-start | bytes 1179656 | tf_op jit(solution)/shard_map/ppermute | solution.py:51
  8.1 0.5 shard_map.98
  8.6 0.1 collective-permute-start.2
  8.7 0.0 copy-done
  8.7 0.0 copy-done.7
  8.7 0.0 copy-done.8
  8.7 3.8 %shard_map.95 = (bf16[6,4,32,2,128]{4,3,2,1,0:T(2,128)(2,1)S(1)}, bf16[4,6,4,32,2,128]{5,4,3,2,1,0:T(2,128)(2,1)}, bf16[256,256]{1,0:T(8,128)(2,1)S(1)}, bf16[256,256]{1,0:T(8,128)(2,1)S(1)}) custom-call(bf16[6,32,2,2048]{3,2,1,0:T(2,128)(2,1)S(1)} %slice.3.fields_ref, bf16[12,32,2,2048]{3,2,1,0:T(2,128)(2,1)S(1)} %copy-done, ...), custom_call_target="tpu_custom_call" | custom-call | flops 1024 | bytes 1024 | tf_op jit(solution)/shard_map/pallas_call | solution.py:128
  12.6 0.0 copy-start.5
  12.6 0.7 copy-done.5
  13.3 1.8 %collective-permute-done = bf16[6,4,32,2,128]{4,3,2,1,0:T(2,128)(2,1)S(1)} collective-permute-done((bf16[6,4,32,2,128]{4,3,2,1,0:T(2,128)(2,1)S(1)}, bf16[6,4,32,2,128]{4,3,2,1,0:T(2,128)(2,1)S(1)}, u32[]{:S(2)}, u32[]{:S(2)}) %collective-permute-start) | collective-permute-done | bytes 393248 | tf_op jit(solution)/shard_map/ppermute | solution.py:51
  15.1 8.8 %collective-permute-done.1 = bf16[6,4,32,2,128]{4,3,2,1,0:T(2,128)(2,1)S(1)} collective-permute-done((bf16[6,4,32,2,128]{4,3,2,1,0:T(2,128)(2,1)S(1)}, bf16[6,4,32,2,128]{4,3,2,1,0:T(2,128)(2,1)S(1)}, u32[]{:S(2)}, u32[]{:S(2)}) %collective-permute-start.1) | collective-permute-done | bytes 393248 | tf_op jit(solution)/shard_map/ppermute | solution.py:51
  23.8 0.6 collective-permute-done.2
  24.4 3.6 %all-to-all-start = ((bf16[4,6,4,32,2,128]{5,4,3,2,1,0:T(2,128)(2,1)}), bf16[4,6,4,32,2,128]{5,4,3,2,1,0:T(2,128)(2,1)S(1)}, u32[]{:S(2)}, u32[]{:S(2)}) async-start(bf16[4,6,4,32,2,128]{5,4,3,2,1,0:T(2,128)(2,1)} %get-tuple-element.37), calls=%async_computation | async-start | bytes 3145728 | tf_op jit(solution)/shard_map/all_to_all | solution.py:434
  28.0 0.0 copy-start.6
  28.0 1.0 %copy-done.6 = bf16[6,4,32,2,128]{4,3,2,1,0:T(2,128)(2,1)S(1)} copy-done((bf16[6,4,32,2,128]{4,3,2,1,0:T(2,128)(2,1)S(1)}, bf16[6,4,32,2,128]{4,3,2,1,0:T(2,128)(2,1)}, u32[]{:S(2)}) %copy-start.6) | copy-done | bytes 393240
  29.0 2.7 %shard_map.99 = (bf16[4,4,64,128]{3,2,1,0:T(8,128)(2,1)S(1)}, bf16[4,4,64,128]{3,2,1,0:T(8,128)(2,1)}, bf16[4,4,64,128]{3,2,1,0:T(8,128)(2,1)}, bf16[4,4,64,128]{3,2,1,0:T(8,128)(2,1)S(1)}, f32[6,256,512]{2,1,0:T(8,128)S(1)}) custom-call(bf16[6,4,64,128]{3,2,1,0:T(8,128)(2,1)S(1)} %bitcast.21, bf16[6,4,64,128]{3,2,1,0:T(8,128)(2,1)S(1)} %bitcast.18, ...), custom_call_target="tpu_custom_call" | custom-call | flops 1024 | bytes 1024 | tf_op jit(solution)/shard_map/pallas_call | solution.py:236
  31.7 1.6 %copy-done.1 = f32[6,256,512]{2,1,0:T(8,128)} copy-done((f32[6,256,512]{2,1,0:T(8,128)}, f32[6,256,512]{2,1,0:T(8,128)S(1)}, u32[]{:S(2)}) %copy-start.1) | copy-done | bytes 3145752
  33.3 1.4 %collective-permute-start.3 = (bf16[4,4,64,128]{3,2,1,0:T(8,128)(2,1)}, bf16[4,4,64,128]{3,2,1,0:T(8,128)(2,1)S(1)}, u32[]{:S(2)}, u32[]{:S(2)}) collective-permute-start(bf16[4,4,64,128]{3,2,1,0:T(8,128)(2,1)} %get-tuple-element.31), channel_id=1, source_target_pairs={{0,8},{8,0},{16,24},{24,16},{1,9},{9,1},{17,25},{25,17},{2,10},{10... | collective-permute-start | bytes 786440 | tf_op jit(solution)/shard_map/ppermute | solution.py:51
  34.7 1.2 %collective-permute-start.4 = (bf16[4,4,64,128]{3,2,1,0:T(8,128)(2,1)}, bf16[4,4,64,128]{3,2,1,0:T(8,128)(2,1)S(1)}, u32[]{:S(2)}, u32[]{:S(2)}) collective-permute-start(bf16[4,4,64,128]{3,2,1,0:T(8,128)(2,1)} %get-tuple-element.32), channel_id=1, source_target_pairs={{0,16},{8,24},{16,0},{24,8},{1,17},{9,25},{17,1},{25,9},{2,18},{10... | collective-permute-start | bytes 786440 | tf_op jit(solution)/shard_map/ppermute | solution.py:51
  35.9 0.3 collective-permute-start.5
  36.2 11.0 %all-to-all-done = bf16[4,6,4,32,2,128]{5,4,3,2,1,0:T(2,128)(2,1)S(1)} async-done(((bf16[4,6,4,32,2,128]{5,4,3,2,1,0:T(2,128)(2,1)}), bf16[4,6,4,32,2,128]{5,4,3,2,1,0:T(2,128)(2,1)S(1)}, u32[]{:S(2)}, u32[]{:S(2)}) %all-to-all-start) | async-done | bytes 1572896 | tf_op jit(solution)/shard_map/all_to_all | solution.py:434
  47.3 1.9 %copy-done.2 = f32[6,256,512]{2,1,0:T(8,128)S(1)} copy-done((f32[6,256,512]{2,1,0:T(8,128)S(1)}, f32[6,256,512]{2,1,0:T(8,128)}, u32[]{:S(2)}) %copy-start.2) | copy-done | bytes 3145752
  49.2 0.0 copy-start.10
  49.2 2.0 %shard_map.102 = (bf16[3,4,64,128]{3,2,1,0:T(8,128)(2,1)S(1)}, bf16[3,4,64,128]{3,2,1,0:T(8,128)(2,1)S(1)}, bf16[3,4,64,128]{3,2,1,0:T(8,128)(2,1)S(1)}, bf16[3,4,64,128]{3,2,1,0:T(8,128)(2,1)S(1)}) custom-call(bf16[4,6,4,64,128]{4,3,2,1,0:T(8,128)(2,1)S(1)} %bitcast.17, f32[6,256,512]{2,1,0:T(8,128)S(1)} %copy-done.2, ...), custom_call_target="tpu_custom_call" | custom-call | flops 1024 | bytes 1024 | tf_op jit(solution)/shard_map/pallas_call | solution.py:236
  51.2 0.1 collective-permute-start.8
  51.3 0.1 collective-permute-start.9
  51.4 0.0 collective-permute-done.3.refs_1_
  51.4 2.5 %collective-permute-start.10 = (bf16[3,4,64,128]{3,2,1,0:T(8,128)(2,1)S(1)}, bf16[3,4,64,128]{3,2,1,0:T(8,128)(2,1)S(1)}, u32[]{:S(2)}, u32[]{:S(2)}) collective-permute-start(bf16[3,4,64,128]{3,2,1,0:T(8,128)(2,1)S(1)} %get-tuple-element.42), channel_id=1, source_target_pairs={{0,24},{8,16},{16,8},{24,0},{1,25},{9,17},{17,9},{25,1},{2,26},{10... | collective-permute-start | bytes 589832 | tf_op jit(solution)/shard_map/ppermute | solution.py:51
  53.9 0.4 collective-permute-done.4.refs_2_
  54.3 2.5 %collective-permute-done.5.refs_3_ = bf16[4,4,64,128]{3,2,1,0:T(8,128)(2,1)S(1)} collective-permute-done((bf16[4,4,64,128]{3,2,1,0:T(8,128)(2,1)S(1)}, bf16[4,4,64,128]{3,2,1,0:T(8,128)(2,1)S(1)}, u32[]{:S(2)}, u32[]{:S(2)}) %collective-permute-start.5) | collective-permute-done | bytes 262176 | tf_op jit(solution)/shard_map/ppermute | solution.py:51
  56.8 1.2 %shard_map.100 = (bf16[4,2,64,128]{3,2,1,0:T(8,128)(2,1)S(1)}, bf16[4,2,64,128]{3,2,1,0:T(8,128)(2,1)S(1)}) custom-call(bf16[4,4,64,128]{3,2,1,0:T(8,128)(2,1)S(1)} %get-tuple-element.30.refs_0_, bf16[4,4,64,128]{3,2,1,0:T(8,128)(2,1)S(1)} %collective-permute-done.3.refs_1_, bf16[4,4,64,128]{3,2,1,0:T(8,128)(2,1)S(1)} %collective-permute-done.4.refs_2_, ...), custom_call_target="tpu_custom_call" | custom-call | flops 1024 | bytes 1024 | tf_op jit(solution)/shard_map/pallas_call | solution.py:276
  58.0 9.6 %collective-permute-start.6 = (bf16[4,2,64,128]{3,2,1,0:T(8,128)(2,1)S(1)}, bf16[4,2,64,128]{3,2,1,0:T(8,128)(2,1)S(1)}, u32[]{:S(2)}, u32[]{:S(2)}) collective-permute-start(bf16[4,2,64,128]{3,2,1,0:T(8,128)(2,1)S(1)} %get-tuple-element.34), channel_id=1, source_target_pairs={{0,1},{1,2},{2,3},{3,4},{4,5},{5,6},{6,7},{8,9},{9,10},{10,11},{11... | collective-permute-start | bytes 393224 | tf_op jit(solution)/shard_map/ppermute | solution.py:58
  67.6 1.9 %collective-permute-start.7 = (bf16[4,2,64,128]{3,2,1,0:T(8,128)(2,1)S(1)}, bf16[4,2,64,128]{3,2,1,0:T(8,128)(2,1)S(1)}, u32[]{:S(2)}, u32[]{:S(2)}) collective-permute-start(bf16[4,2,64,128]{3,2,1,0:T(8,128)(2,1)S(1)} %get-tuple-element.35), channel_id=1, source_target_pairs={{1,0},{2,1},{3,2},{4,3},{5,4},{6,5},{7,6},{9,8},{10,9},{11,10},{12... | collective-permute-start | bytes 393224 | tf_op jit(solution)/shard_map/ppermute | solution.py:58
  69.5 0.0 collective-permute-done.6.refs_4_
  69.5 4.3 %collective-permute-done.7.refs_5_ = bf16[4,2,64,128]{3,2,1,0:T(8,128)(2,1)S(1)} collective-permute-done((bf16[4,2,64,128]{3,2,1,0:T(8,128)(2,1)S(1)}, bf16[4,2,64,128]{3,2,1,0:T(8,128)(2,1)S(1)}, u32[]{:S(2)}, u32[]{:S(2)}) %collective-permute-start.7) | collective-permute-done | bytes 131104 | tf_op jit(solution)/shard_map/ppermute | solution.py:58
  73.9 0.0 copy-done.4
  73.9 6.6 %shard_map.101 = (f32[3072,128]{1,0:T(8,128)}, f32[3,16,64,128]{3,2,1,0:T(8,128)S(1)}) custom-call(bf16[4,4,64,128]{3,2,1,0:T(8,128)(2,1)S(1)} %get-tuple-element.30.refs_0_, bf16[4,4,64,128]{3,2,1,0:T(8,128)(2,1)S(1)} %collective-permute-done.3.refs_1_, bf16[4,4,64,128]{3,2,1,0:T(8,128)(2,1)S(1)} %collective-permute-done.4.refs_2_, ...), custom_call_target="tpu_custom_call" | custom-call | flops 1024 | bytes 1024 | tf_op jit(solution)/shard_map/pallas_call | solution.py:360
  80.5 0.0 collective-permute-done.8.refs_1_
  80.5 0.0 collective-permute-done.9.refs_2_
  80.5 0.0 collective-permute-done.10.refs_3_
  80.5 2.2 %shard_map.103 = f32[3072,128]{1,0:T(8,128)} custom-call(bf16[3,4,64,128]{3,2,1,0:T(8,128)(2,1)S(1)} %get-tuple-element.39.refs_0_, bf16[3,4,64,128]{3,2,1,0:T(8,128)(2,1)S(1)} %collective-permute-done.8.refs_1_, bf16[3,4,64,128]{3,2,1,0:T(8,128)(2,1)S(1)} %collective-permute-done.9.refs_2_, bf16[3,4,64,128]{3,2,1,0:T(8,128)(2,1)S(1)} %collective-permute-done.10.refs_3_, ...), custom_call_target="tpu_custom_call" | custom-call | flops 1024 | bytes 1024 | tf_op jit(solution)/shard_map/pallas_call | solution.py:403
  (10 shorter events, 0.0 us)
Async XLA Ops:
  4.1 4.6 %copy-start = (bf16[12,32,2,2048]{3,2,1,0:T(2,128)(2,1)S(1)}, bf16[12,32,2,2048]{3,2,1,0:T(2,128)(2,1)}, u32[]{:S(2)}) copy-start(bf16[12,32,2,2048]{3,2,1,0:T(2,128)(2,1)} %others_ref.1) | copy-start | bytes 9437188
  4.1 4.6 %copy-start.7 = (bf16[256,256]{1,0:T(8,128)(2,1)S(1)}, bf16[256,256]{1,0:T(8,128)(2,1)}, u32[]{:S(2)}) copy-start(bf16[256,256]{1,0:T(8,128)(2,1)} %constant.5.clone.refs_1_) | copy-start | bytes 393220
  4.1 4.6 %copy-start.8 = (bf16[256,256]{1,0:T(8,128)(2,1)S(1)}, bf16[256,256]{1,0:T(8,128)(2,1)}, u32[]{:S(2)}) copy-start(bf16[256,256]{1,0:T(8,128)(2,1)} %constant.4.clone.refs_0_) | copy-start | bytes 393220
  4.1 10.9 %collective-permute-start = (bf16[6,4,32,2,128]{4,3,2,1,0:T(2,128)(2,1)S(1)}, bf16[6,4,32,2,128]{4,3,2,1,0:T(2,128)(2,1)S(1)}, u32[]{:S(2)}, u32[]{:S(2)}) collective-permute-start(bf16[6,4,32,2,128]{4,3,2,1,0:T(2,128)(2,1)S(1)} %shard_map.96), channel_id=1, source_target_pairs={{0,8},{8,0},{16,24},{24,16},{1,9},{9,1},{17,25},{25,17},{2,10},{10... | collective-permute-start | bytes 1179656 | tf_op jit(solution)/shard_map/ppermute | solution.py:51
  6.8 17.1 %collective-permute-start.1 = (bf16[6,4,32,2,128]{4,3,2,1,0:T(2,128)(2,1)S(1)}, bf16[6,4,32,2,128]{4,3,2,1,0:T(2,128)(2,1)S(1)}, u32[]{:S(2)}, u32[]{:S(2)}) collective-permute-start(bf16[6,4,32,2,128]{4,3,2,1,0:T(2,128)(2,1)S(1)} %shard_map.97), channel_id=1, source_target_pairs={{0,16},{8,24},{16,0},{24,8},{1,17},{9,25},{17,1},{25,9},{2,18},{10... | collective-permute-start | bytes 1179656 | tf_op jit(solution)/shard_map/ppermute | solution.py:51
  8.6 15.8 %collective-permute-start.2 = (bf16[6,4,32,2,128]{4,3,2,1,0:T(2,128)(2,1)S(1)}, bf16[6,4,32,2,128]{4,3,2,1,0:T(2,128)(2,1)S(1)}, u32[]{:S(2)}, u32[]{:S(2)}) collective-permute-start(bf16[6,4,32,2,128]{4,3,2,1,0:T(2,128)(2,1)S(1)} %shard_map.98), channel_id=1, source_target_pairs={{0,24},{8,16},{16,8},{24,0},{1,25},{9,17},{17,9},{25,1},{2,26},{10... | collective-permute-start | bytes 1179656 | tf_op jit(solution)/shard_map/ppermute | solution.py:51
  12.6 0.7 copy-start.5
  24.4 22.8 %all-to-all-start = ((bf16[4,6,4,32,2,128]{5,4,3,2,1,0:T(2,128)(2,1)}), bf16[4,6,4,32,2,128]{5,4,3,2,1,0:T(2,128)(2,1)S(1)}, u32[]{:S(2)}, u32[]{:S(2)}) async-start(bf16[4,6,4,32,2,128]{5,4,3,2,1,0:T(2,128)(2,1)} %get-tuple-element.37), calls=%async_computation | async-start | bytes 3145728 | tf_op jit(solution)/shard_map/all_to_all | solution.py:434
  28.0 1.0 %copy-start.6 = (bf16[6,4,32,2,128]{4,3,2,1,0:T(2,128)(2,1)S(1)}, bf16[6,4,32,2,128]{4,3,2,1,0:T(2,128)(2,1)}, u32[]{:S(2)}) copy-start(bf16[6,4,32,2,128]{4,3,2,1,0:T(2,128)(2,1)} %copy-done.5) | copy-start | bytes 1179652
  31.7 1.6 %copy-start.1 = (f32[6,256,512]{2,1,0:T(8,128)}, f32[6,256,512]{2,1,0:T(8,128)S(1)}, u32[]{:S(2)}) copy-start(f32[6,256,512]{2,1,0:T(8,128)S(1)} %get-tuple-element.38.refs_1_) | copy-start | bytes 9437188
  33.3 18.1 %collective-permute-start.3 = (bf16[4,4,64,128]{3,2,1,0:T(8,128)(2,1)}, bf16[4,4,64,128]{3,2,1,0:T(8,128)(2,1)S(1)}, u32[]{:S(2)}, u32[]{:S(2)}) collective-permute-start(bf16[4,4,64,128]{3,2,1,0:T(8,128)(2,1)} %get-tuple-element.31), channel_id=1, source_target_pairs={{0,8},{8,0},{16,24},{24,16},{1,9},{9,1},{17,25},{25,17},{2,10},{10... | collective-permute-start | bytes 786440 | tf_op jit(solution)/shard_map/ppermute | solution.py:51
  34.7 19.6 %collective-permute-start.4 = (bf16[4,4,64,128]{3,2,1,0:T(8,128)(2,1)}, bf16[4,4,64,128]{3,2,1,0:T(8,128)(2,1)S(1)}, u32[]{:S(2)}, u32[]{:S(2)}) collective-permute-start(bf16[4,4,64,128]{3,2,1,0:T(8,128)(2,1)} %get-tuple-element.32), channel_id=1, source_target_pairs={{0,16},{8,24},{16,0},{24,8},{1,17},{9,25},{17,1},{25,9},{2,18},{10... | collective-permute-start | bytes 786440 | tf_op jit(solution)/shard_map/ppermute | solution.py:51
  35.9 20.9 %collective-permute-start.5 = (bf16[4,4,64,128]{3,2,1,0:T(8,128)(2,1)S(1)}, bf16[4,4,64,128]{3,2,1,0:T(8,128)(2,1)S(1)}, u32[]{:S(2)}, u32[]{:S(2)}) collective-permute-start(bf16[4,4,64,128]{3,2,1,0:T(8,128)(2,1)S(1)} %get-tuple-element.33), channel_id=1, source_target_pairs={{0,24},{8,16},{16,8},{24,0},{1,25},{9,17},{17,9},{25,1},{2,26},{10... | collective-permute-start | bytes 786440 | tf_op jit(solution)/shard_map/ppermute | solution.py:51
  47.3 1.9 %copy-start.2 = (f32[6,256,512]{2,1,0:T(8,128)S(1)}, f32[6,256,512]{2,1,0:T(8,128)}, u32[]{:S(2)}) copy-start(f32[6,256,512]{2,1,0:T(8,128)} %copy-done.1) | copy-start | bytes 9437188
  49.2 7.6 %copy-start.11 = (s32[2,256]{1,0:T(2,128)S(1)}, s32[2,256]{1,0:T(2,128)}, u32[]{:S(2)}) copy-start(s32[2,256]{1,0:T(2,128)} %refs_4_.1) | copy-start | bytes 6148
  49.2 24.7 %copy-start.3 = (bf16[5,64,2048]{2,1,0:T(8,128)(2,1)S(1)}, bf16[5,64,2048]{2,1,0:T(8,128)(2,1)}, u32[]{:S(2)}) copy-start(bf16[5,64,2048]{2,1,0:T(8,128)(2,1)} %refs_6_.1) | copy-start | bytes 3932164
  49.2 24.7 %copy-start.4 = (bf16[5,64,2048]{2,1,0:T(8,128)(2,1)S(1)}, bf16[5,64,2048]{2,1,0:T(8,128)(2,1)}, u32[]{:S(2)}) copy-start(bf16[5,64,2048]{2,1,0:T(8,128)(2,1)} %refs_7_.1) | copy-start | bytes 3932164
  49.2 24.7 %copy-start.9 = (f32[2048]{0:T(1024)S(1)}, f32[2048]{0:T(1024)}, u32[]{:S(2)}) copy-start(f32[2048]{0:T(1024)} %param.9) | copy-start | bytes 24580
  49.2 24.7 %copy-start.10 = (s32[32,5]{0,1:T(8,128)S(1)}, s32[32,5]{0,1:T(8,128)}, u32[]{:S(2)}) copy-start(s32[32,5]{0,1:T(8,128)} %param.12) | copy-start | bytes 1924
  51.2 29.3 %collective-permute-start.8 = (bf16[3,4,64,128]{3,2,1,0:T(8,128)(2,1)S(1)}, bf16[3,4,64,128]{3,2,1,0:T(8,128)(2,1)S(1)}, u32[]{:S(2)}, u32[]{:S(2)}) collective-permute-start(bf16[3,4,64,128]{3,2,1,0:T(8,128)(2,1)S(1)} %get-tuple-element.40), channel_id=1, source_target_pairs={{0,8},{8,0},{16,24},{24,16},{1,9},{9,1},{17,25},{25,17},{2,10},{10... | collective-permute-start | bytes 589832 | tf_op jit(solution)/shard_map/ppermute | solution.py:51
  51.3 29.2 %collective-permute-start.9 = (bf16[3,4,64,128]{3,2,1,0:T(8,128)(2,1)S(1)}, bf16[3,4,64,128]{3,2,1,0:T(8,128)(2,1)S(1)}, u32[]{:S(2)}, u32[]{:S(2)}) collective-permute-start(bf16[3,4,64,128]{3,2,1,0:T(8,128)(2,1)S(1)} %get-tuple-element.41), channel_id=1, source_target_pairs={{0,16},{8,24},{16,0},{24,8},{1,17},{9,25},{17,1},{25,9},{2,18},{10... | collective-permute-start | bytes 589832 | tf_op jit(solution)/shard_map/ppermute | solution.py:51
  51.4 29.1 %collective-permute-start.10 = (bf16[3,4,64,128]{3,2,1,0:T(8,128)(2,1)S(1)}, bf16[3,4,64,128]{3,2,1,0:T(8,128)(2,1)S(1)}, u32[]{:S(2)}, u32[]{:S(2)}) collective-permute-start(bf16[3,4,64,128]{3,2,1,0:T(8,128)(2,1)S(1)} %get-tuple-element.42), channel_id=1, source_target_pairs={{0,24},{8,16},{16,8},{24,0},{1,25},{9,17},{17,9},{25,1},{2,26},{10... | collective-permute-start | bytes 589832 | tf_op jit(solution)/shard_map/ppermute | solution.py:51
  58.0 11.5 %collective-permute-start.6 = (bf16[4,2,64,128]{3,2,1,0:T(8,128)(2,1)S(1)}, bf16[4,2,64,128]{3,2,1,0:T(8,128)(2,1)S(1)}, u32[]{:S(2)}, u32[]{:S(2)}) collective-permute-start(bf16[4,2,64,128]{3,2,1,0:T(8,128)(2,1)S(1)} %get-tuple-element.34), channel_id=1, source_target_pairs={{0,1},{1,2},{2,3},{3,4},{4,5},{5,6},{6,7},{8,9},{9,10},{10,11},{11... | collective-permute-start | bytes 393224 | tf_op jit(solution)/shard_map/ppermute | solution.py:58
  67.6 6.3 %collective-permute-start.7 = (bf16[4,2,64,128]{3,2,1,0:T(8,128)(2,1)S(1)}, bf16[4,2,64,128]{3,2,1,0:T(8,128)(2,1)S(1)}, u32[]{:S(2)}, u32[]{:S(2)}) collective-permute-start(bf16[4,2,64,128]{3,2,1,0:T(8,128)(2,1)S(1)} %get-tuple-element.35), channel_id=1, source_target_pairs={{1,0},{2,1},{3,2},{4,3},{5,4},{6,5},{7,6},{9,8},{10,9},{11,10},{12... | collective-permute-start | bytes 393224 | tf_op jit(solution)/shard_map/ppermute | solution.py:58

commit v4 on v3

--- a/solution.py
+++ b/solution.py
@@ -73,11 +73,17 @@
     return (inverse.reshape(angle_total, 2 * mode_total), forward)
 
 
-def pieces_of(fields_ref, share, out_ref, first=0):
-    components, tiles = out_ref.shape[:2]
+def groups_of(tiles):
+    return 2 if tiles % 2 == 0 else 1
+
+
+def pieces_of(fields_ref, first, share, group, out_ref):
+    count = lax.axis_size("mode")
+    tiles = fields_ref.shape[3] // count // LANES
+    components, held = out_ref.shape[:2]
     pairs = []
-    for t in range(tiles):
-        start = pl.multiple_of((share * tiles + t) * LANES, LANES)
+    for t in range(held):
+        start = pl.multiple_of((share * tiles + group * held + t) * LANES, LANES)
         for c in range(components):
             pairs.append((fields_ref.at[first + c, :, :, pl.ds(start, LANES)], out_ref.at[c, t]))
     return pairs
@@ -93,20 +99,22 @@
         copy.wait()
 
 
-def share_shape(fields, count):
-    components, mode_count, _, width = fields.shape
-    return (components, width // count // LANES, mode_count, 2, LANES)
-
-
-def pack_step(fields, step, count):
-    shape = share_shape(fields, count)
+def packed_shape(fields, first, last, groups):
+    _, mode_count, _, width = fields.shape
+    return (last - first, width // lax.axis_size("mode") // LANES // groups, mode_count, 2, LANES)
+
+
+def pack(fields, first, last, step, group, groups):
+    count = lax.axis_size("mode")
+    shape = packed_shape(fields, first, last, groups)
 
     def kernel(fields_ref, out_ref, sems):
-        run_copies(pieces_of(fields_ref, dest_of(lax.axis_index("mode"), step, count), out_ref), sems)
+        share = dest_of(lax.axis_index("mode"), step, count)
+        run_copies(pieces_of(fields_ref, first, share, group, out_ref), sems)
 
     return pl.pallas_call(
         kernel,
-        in_specs=[vmem()],
+        in_specs=[pl.BlockSpec(memory_space=pl.ANY)],
         out_specs=vmem(),
         out_shape=jax.ShapeDtypeStruct(shape, jnp.bfloat16),
         scratch_shapes=[pltpu.SemaphoreType.DMA((shape[0] * shape[1],))],
@@ -115,26 +123,33 @@
     )(fields)
 
 
-def pack_rest(fields, others, count, carried):
-    shape = share_shape(fields, count)
-
-    def kernel(fields_ref, others_ref, *refs):
-        inputs, (own_ref, all_ref), outputs = refs[: len(carried)], refs[len(carried) : len(carried) + 2], refs[len(carried) + 2 : -1]
-        pairs = pieces_of(fields_ref, lax.axis_index("mode"), own_ref)
+def pack_rest(fields, middle, groups, carried):
+    count = lax.axis_size("mode")
+    shape = packed_shape(fields, 0, middle, groups)
+    full = packed_shape(fields, middle, fields.shape[0], 1)
+
+    def kernel(fields_ref, *refs):
+        inputs, refs = refs[: len(carried)], refs[len(carried) :]
+        own_refs, all_ref, outputs = refs[:groups], refs[groups], refs[groups + 1 : -1]
+        me = lax.axis_index("mode")
+        pairs = []
+        for group in range(groups):
+            pairs += pieces_of(fields_ref, 0, me, group, own_refs[group])
         for share in range(count):
-            pairs += pieces_of(others_ref, share, all_ref.at[share], shape[0])
+            pairs += pieces_of(fields_ref, middle, share, 0, all_ref.at[share])
         run_copies(pairs, refs[-1], zip(inputs, outputs))
 
     return pl.pallas_call(
         kernel,
-        in_specs=[vmem(), pl.BlockSpec(memory_space=pl.ANY)] + [vmem()] * len(carried),
-        out_specs=[vmem()] * (2 + len(carried)),
-        out_shape=[jax.ShapeDtypeStruct(shape, jnp.bfloat16), jax.ShapeDtypeStruct((count,) + shape, jnp.bfloat16)]
+        in_specs=[pl.BlockSpec(memory_space=pl.ANY)] + [vmem()] * len(carried),
+        out_specs=[vmem()] * (groups + 1 + len(carried)),
+        out_shape=[jax.ShapeDtypeStruct(shape, jnp.bfloat16)] * groups
+        + [jax.ShapeDtypeStruct((count,) + full, jnp.bfloat16)]
         + [jax.ShapeDtypeStruct(value.shape, value.dtype) for value in carried],
-        scratch_shapes=[pltpu.SemaphoreType.DMA(((count + 1) * shape[0] * shape[1],))],
-        compiler_params=params(),
-        cost_estimate=cost(),
-    )(fields, others, *carried)
+        scratch_shapes=[pltpu.SemaphoreType.DMA((groups * shape[0] * shape[1] + count * full[0] * full[1],))],
+        compiler_params=params(),
+        cost_estimate=cost(),
+    )(fields, *carried)
 
 
 def cross(a, b):
@@ -189,77 +204,92 @@
     to_modes(count, forward_ref, table_ref, product_ref, out_refs)
 
 
-def second_kernel(count, *refs):
-    in_ref, first_ref, inverse_ref, forward_ref = refs[:4]
-    out_refs, (physical_ref, x_ref, product_ref, table_ref) = refs[4 : count + 4], refs[count + 4 :]
+def first_physics(received, inverse, forward):
+    count = len(received)
+    components, tiles, rows, _ = received[0].shape
+    width = tiles * LANES
+    return pl.pallas_call(
+        functools.partial(first_kernel, count),
+        in_specs=[vmem()] * (count + 2),
+        out_specs=[vmem()] * (count + 1),
+        out_shape=[jax.ShapeDtypeStruct((4, tiles, rows, LANES), jnp.bfloat16)] * count
+        + [jax.ShapeDtypeStruct((components, THETA, width), jnp.float32)],
+        scratch_shapes=[
+            pltpu.VMEM((components, 2 * M, width), jnp.bfloat16),
+            pltpu.VMEM((4, THETA, width), jnp.bfloat16),
+            pltpu.VMEM((2 * M, THETA), jnp.bfloat16),
+        ],
+        compiler_params=params(),
+        cost_estimate=cost(),
+    )(*received, inverse, forward)
+
+
+def second_kernel(count, groups, *refs):
+    in_ref, first_refs, (inverse_ref, forward_ref) = refs[0], refs[1 : groups + 1], refs[groups + 1 : groups + 3]
+    out_refs, (physical_ref, x_ref, product_ref, table_ref) = refs[groups + 3 : groups + 3 + count], refs[groups + 3 + count :]
+    width = first_refs[0].shape[2]
 
     def store(c, value):
         physical_ref[c] = value
 
     to_physical(range(count), [in_ref.at[source] for source in range(count)], inverse_ref[...], x_ref, store)
-    for i in range(THETA // CHUNK):
-        at = slice(i * CHUNK, (i + 1) * CHUNK)
-        velocity = [first_ref[c, at] for c in range(3)]
-        magnetic = [first_ref[c, at] for c in range(3, 6)]
-        current = [physical_ref[c, at] for c in range(3)]
-        vorticity = [physical_ref[c, at] for c in range(3, 6)]
-        lorentz = [a + b for a, b in zip(cross(current, magnetic), cross(velocity, vorticity))]
-        for c, value in enumerate(lorentz):
-            product_ref[c, at] = value.astype(jnp.bfloat16)
+    for group in range(groups):
+        lanes = slice(group * width, (group + 1) * width)
+        for i in range(THETA // CHUNK):
+            at = slice(i * CHUNK, (i + 1) * CHUNK)
+            velocity = [first_refs[group][c, at] for c in range(3)]
+            magnetic = [first_refs[group][c, at] for c in range(3, 6)]
+            current = [physical_ref[c, at, lanes] for c in range(3)]
+            vorticity = [physical_ref[c, at, lanes] for c in range(3, 6)]
+            lorentz = [a + b for a, b in zip(cross(current, magnetic), cross(velocity, vorticity))]
+            for c, value in enumerate(lorentz):
+                product_ref[c, at, lanes] = value.astype(jnp.bfloat16)
     to_modes(count, forward_ref, table_ref, product_ref, out_refs)
 
 
-def physics(kernel, received, extra, inverse, forward, outputs, keep):
-    components, tiles, rows, _ = received[0].shape[-4:]
-    count = 2 * M // rows
-    group = 2 if tiles % 2 == 0 else 1
-    steps = tiles // group
-    width = group * LANES
-    share = tiles * LANES
-    if keep:
-        in_block = pl.BlockSpec((components, group, rows, LANES), lambda i: (0, i, 0, 0))
-    else:
-        in_block = pl.BlockSpec((count, components, group, rows, LANES), lambda i: (0, 0, i, 0, 0))
-    out_block = pl.BlockSpec((outputs, group, rows, LANES), lambda i: (0, i, 0, 0))
-    whole = pl.BlockSpec((THETA, 2 * M), lambda i: (0, 0))
-    turned = pl.BlockSpec((2 * M, THETA), lambda i: (0, 0))
-    kept = pl.BlockSpec((6, THETA, width), lambda i: (0, 0, i))
-    kept_shape = jax.ShapeDtypeStruct((6, THETA, share), jnp.float32)
-    scratch = [
-        pltpu.VMEM((components, 2 * M, width), jnp.bfloat16),
-        pltpu.VMEM((outputs, THETA, width), jnp.bfloat16),
-        pltpu.VMEM((2 * M, THETA), jnp.bfloat16),
-    ]
-    if not keep:
-        scratch = [pltpu.VMEM((components, THETA, width), jnp.float32)] + scratch
-    out_shape = [jax.ShapeDtypeStruct((outputs, tiles, rows, LANES), jnp.bfloat16)] * count
-    return pl.pallas_call(
-        functools.partial(kernel, count),
-        grid=(steps,),
-        in_specs=[in_block] * len(received) + [kept] * len(extra) + [whole, turned],
-        out_specs=[out_block] * count + ([kept] if keep else []),
-        out_shape=out_shape + ([kept_shape] if keep else []),
-        scratch_shapes=scratch,
-        compiler_params=params(),
-        cost_estimate=cost(),
-    )(*received, *extra, inverse, forward)
-
-
-def interface_kernel(count, *refs):
-    in_refs, (nodes_ref,), (prev_ref, next_ref) = refs[:count], refs[count : count + 1], refs[count + 1 :]
+def second_physics(shares, physical, inverse, forward):
+    count, components, tiles, rows, _ = shares.shape
+    groups = len(physical)
+    width = tiles * LANES
+    return pl.pallas_call(
+        functools.partial(second_kernel, count, groups),
+        in_specs=[vmem()] * (groups + 3),
+        out_specs=[vmem()] * count,
+        out_shape=[jax.ShapeDtypeStruct((3, tiles, rows, LANES), jnp.bfloat16)] * count,
+        scratch_shapes=[
+            pltpu.VMEM((components, THETA, width), jnp.float32),
+            pltpu.VMEM((components, 2 * M, width), jnp.bfloat16),
+            pltpu.VMEM((3, THETA, width), jnp.bfloat16),
+            pltpu.VMEM((2 * M, THETA), jnp.bfloat16),
+        ],
+        compiler_params=params(),
+        cost_estimate=cost(),
+    )(shares, *physical, inverse, forward)
+
+
+def tiles_of(in_refs, count):
     me = lax.axis_index("mode")
-    components, tiles, rows, _ = in_refs[0].shape
+    components, held, rows, _ = in_refs[0].shape
+    groups = len(in_refs) // count
+    for group in range(groups):
+        for step in range(count):
+            share = source_of(me, step, count)
+            for t in range(held):
+                at = share * (groups * held) + group * held + t
+                yield at, in_refs[group * count + step][:, t].reshape(components * rows, LANES)
+
+
+def interface_kernel(count, arrived, *refs):
+    in_refs, (nodes_ref, prev_ref, next_ref) = refs[:arrived], refs[arrived:]
+    components, _, rows, _ = in_refs[0].shape
     halo = nodes_ref.shape[1]
     totals = [jnp.zeros((components * rows, halo), jnp.float32) for _ in range(2)]
     inner = lax.broadcasted_iota(jnp.int32, (LANES, halo), 0)
-    for step in range(count):
-        share = source_of(me, step, count)
-        for t in range(tiles):
-            ids = inner + (share * tiles + t) * LANES
-            values = in_refs[step][:, t].reshape(components * rows, LANES)
-            for way in range(2):
-                chosen = jnp.where(ids == nodes_ref[way : way + 1, :], 1.0, 0.0).astype(jnp.bfloat16)
-                totals[way] += jnp.dot(values, chosen, preferred_element_type=jnp.float32)
+    for at, values in tiles_of(in_refs, count):
+        ids = inner + at * LANES
+        for way in range(2):
+            chosen = jnp.where(ids == nodes_ref[way : way + 1, :], 1.0, 0.0).astype(jnp.bfloat16)
+            totals[way] += jnp.dot(values, chosen, preferred_element_type=jnp.float32)
     for out_ref, total in zip((prev_ref, next_ref), totals):
         picked = total.astype(jnp.bfloat16)
         for c in range(components):
@@ -267,15 +297,13 @@
                 out_ref[c, t] = picked[c * rows : (c + 1) * rows, t * LANES : (t + 1) * LANES]
 
 
-def interface(received, interface_nodes):
-    count = len(received)
-    components, tiles, rows, _ = received[0].shape
+def interface(received, interface_nodes, count):
+    components, _, rows, _ = received[0].shape
     halo = interface_nodes.shape[1]
     shape = jax.ShapeDtypeStruct((components, halo // LANES, rows, LANES), jnp.bfloat16)
-    width = count * tiles * LANES
-    return pl.pallas_call(
-        functools.partial(interface_kernel, count),
-        in_specs=[vmem()] * (count + 1),
+    return pl.pallas_call(
+        functools.partial(interface_kernel, count, len(received)),
+        in_specs=[vmem()] * (len(received) + 1),
         out_specs=[vmem()] * 2,
         out_shape=[shape] * 2,
         compiler_params=params(),
@@ -283,24 +311,22 @@
     )(*received, interface_nodes)
 
 
-def derive_kernel(count, *refs):
-    in_refs = refs[:count]
-    prev_ref, next_ref, radial_ref, axial_ref, radius_ref, columns_ref = refs[count : count + 6]
-    induction_ref, momentum_ref, extended_ref = refs[count + 6 :]
+def derive_kernel(count, arrived, *refs):
+    in_refs = refs[:arrived]
+    prev_ref, next_ref, radial_ref, axial_ref, radius_ref, columns_ref = refs[arrived : arrived + 6]
+    induction_ref, momentum_ref, extended_ref = refs[arrived + 6 :]
     me = lax.axis_index("mode")
-    components, tiles, rows, _ = in_refs[0].shape
+    components, held, rows, _ = in_refs[0].shape
     mode_count = rows // 2
-    node_tiles = count * tiles
+    node_tiles = arrived * held
     halo_tiles = prev_ref.shape[1]
 
     def extend(at, tile):
         extended_ref[0, at] = tile
         extended_ref[1, at] = jnp.concatenate([tile[:, BLK:], tile[:, :BLK]], axis=1)
 
-    for step in range(count):
-        share = source_of(me, step, count)
-        for t in range(tiles):
-            extend(share * tiles + t, in_refs[step][:, t].reshape(components * rows, LANES))
+    for at, tile in tiles_of(in_refs, count):
+        extend(at, tile)
     for t in range(halo_tiles):
         extend(node_tiles + t, prev_ref[:, t].reshape(components * rows, LANES))
         extend(node_tiles + halo_tiles + t, next_ref[:, t].reshape(components * rows, LANES))
@@ -351,15 +377,14 @@
     lax.fori_loop(0, node_tiles, pair, 0, unroll=2)
 
 
-def derive(received, from_prev, from_next, radial_blocks, axial_blocks, radius, columns):
-    count = len(received)
-    components, tiles, rows, _ = received[0].shape
-    node_tiles = count * tiles
+def derive(received, from_prev, from_next, radial_blocks, axial_blocks, radius, columns, count):
+    components, held, rows, _ = received[0].shape
+    node_tiles = len(received) * held
     halo_tiles = from_prev.shape[1]
     out_rows = 3 * rows * node_tiles
     return pl.pallas_call(
-        functools.partial(derive_kernel, count),
-        in_specs=[vmem()] * (count + 5) + [pl.BlockSpec(memory_space=pltpu.SMEM)],
+        functools.partial(derive_kernel, count, len(received)),
+        in_specs=[vmem()] * (len(received) + 5) + [pl.BlockSpec(memory_space=pltpu.SMEM)],
         out_specs=[vmem()] * 2,
         out_shape=[
             jax.ShapeDtypeStruct((out_rows, LANES), jnp.float32),
@@ -426,21 +451,28 @@
     def joined(pieces):
         return [piece.reshape(piece.shape[:-3] + (rows, LANES)) for piece in pieces]
 
-    fields = mode_fields[:6]
-    arrived = exchange([pack_step(fields, step, count) for step in range(1, count)])
-    own, shares, inverse, forward = pack_rest(fields, mode_fields, count, [inverse, forward])
-    arrived, shares = lax.optimization_barrier((arrived, shares))
-    flow = joined([own] + arrived)
-    sources = joined([lax.all_to_all(shares, "mode", 0, 0, tiled=True)])
-    *terms, physical = physics(first_kernel, flow, [], inverse, forward, 4, True)
-    local = terms[:1] + exchange(terms[1:])
-    toward_prev, toward_next = interface(local, interface_nodes)
+    groups = groups_of(width // count // LANES)
+    arrived = []
+    for group in range(groups):
+        arrived.append(exchange([pack(mode_fields, 0, 6, step, group, groups) for step in range(1, count)]))
+    *own, shares, inverse, forward = pack_rest(mode_fields, 6, groups, [inverse, forward])
+    local, physical = [], []
+    for group in range(groups):
+        *terms, velocity_magnetic = first_physics(joined([own[group]] + arrived[group]), inverse, forward)
+        back = exchange(terms[1:])
+        if group == 0:
+            back, shares = lax.optimization_barrier((back, shares))
+            shares = lax.all_to_all(shares, "mode", 0, 0, tiled=True)
+        local += terms[:1] + back
+        physical.append(velocity_magnetic)
+    toward_prev, toward_next = interface(local, interface_nodes, count)
     from_prev = from_behind(toward_next, "mer", 1)
     from_next = from_behind(toward_prev, "mer", -1)
     induction, gradient = derive(
-        local, from_prev, from_next, radial_blocks, axial_blocks, radius.reshape(1, width), block_columns.T
+        local, from_prev, from_next, radial_blocks, axial_blocks, radius.reshape(1, width), block_columns.T, count
     )
-    lorentz = list(physics(second_kernel, sources, [physical], inverse, forward, 3, False))
+    shares, gradient = lax.optimization_barrier((shares, gradient))
+    lorentz = list(second_physics(joined([shares])[0], physical, inverse, forward))
     lorentz = lorentz[:1] + exchange(lorentz[1:])
     momentum = momentum_of(lorentz, gradient)
     return (whole_output(induction, mode_count, width), whole_output(momentum, mode_count, width))

time: 83.1 us -> 101 us (1.22)
  waiting for transfers between devices: 29.3 us -> 43.9 us
  starting transfers between devices: 24.2 us -> 28.7 us
  Pallas kernels: 20.2 us -> 18.9 us
    ppermute x9 -> x15, waiting for transfers between devices: 14 us -> 39.6 us  [exchange(): received.append(lax.ppermute(pieces[step - 1], 'mode', pairs))]
    all_to_all x1, waiting for transfers between devices: 11 us -> 0.01 us  [body(): shares = lax.all_to_all(shares, 'mode', 0, 0, tiled=True)]
    ppermute x9 -> x15, starting transfers between devices: 9.1 us -> 15.2 us  [exchange(): received.append(lax.ppermute(pieces[step - 1], 'mode', pairs))]
    slice x1 -> x0, local copies, waits for them, and re-layouts: 2.9 us -> none  [body(): fields = mode_fields[:6]]
    ppermute x2, starting transfers between devices: 11.5 us -> 8.84 us  [from_behind(): lax.ppermute(value, axis, [(source, source + steps) for source in range(i...]
    unnamed x24 -> x44, local copies, waits for them, and re-layouts: 5.29 us -> 7.4 us
    pallas_call x8 -> x12, Pallas kernels: 18 us -> 16.8 us  [the longest x1 6.59 us: derive(): pl.pallas_call(functools.partial(derive_kernel, count, len(received)), in...]
    all_to_all x1, starting transfers between devices: 3.56 us -> 4.61 us  [body(): shares = lax.all_to_all(shares, 'mode', 0, 0, tiled=True)]
  transfers between devices with their start and end apart: 12 -> 18, of which waited for: 7 -> 12; matrix products, arithmetic and copies ran while one was open for 0% -> 0% of each run, Pallas kernels for 21% -> 13%
where the time goes in v4:
time: 101 us; the launch traced here: 99.9 us
  waiting for transfers between devices  43.9 us (43%)
  starting transfers between devices  28.7 us (28%)
  Pallas kernels  18.9 us (19%)
  local copies, waits for them, and re-layouts  7.4 us (7%)
    ppermute x15, waiting for transfers between devices, exchange(): received.append(lax.ppermute(pieces[step - 1], 'mode', pairs))  39.6 us
    ppermute x15, starting transfers between devices, exchange(): received.append(lax.ppermute(pieces[step - 1], 'mode', pairs))  15.2 us
    ppermute x2, starting transfers between devices, from_behind(): lax.ppermute(value, axis, [(source, source + steps) for source in range(i...  8.84 us
    unnamed x44, local copies, waits for them, and re-layouts  7.4 us
    pallas_call x1, Pallas kernels, derive(): pl.pallas_call(functools.partial(derive_kernel, count, len(received)), in...  6.59 us
    all_to_all x1, starting transfers between devices, body(): shares = lax.all_to_all(shares, 'mode', 0, 0, tiled=True)  4.61 us
    ppermute x2, waiting for transfers between devices, from_behind(): lax.ppermute(value, axis, [(source, source + steps) for source in range(i...  4.35 us
    pallas_call x1, Pallas kernels, second_physics(): pl.pallas_call(functools.partial(second_kernel, count, groups), in_specs=...  3.02 us
  transfers between devices with their start and end apart: 18, of which 12 were waited for; matrix products, arithmetic and copies ran while one was open for 0% of the time, Pallas kernels for 13%

profile of v4, /device:TPU:1, one launch (start us, length us, event | category | flops | bytes accessed | tf_op | source)
XLA Modules:
  0.0 99.9 jit_solution(2094252927806273136)
XLA Ops:
  0.6 1.9 %copy-done = bf16[12,32,2,2048]{3,2,1,0:T(2,128)(2,1)S(1)} copy-done((bf16[12,32,2,2048]{3,2,1,0:T(2,128)(2,1)S(1)}, bf16[12,32,2,2048]{3,2,1,0:T(2,128)(2,1)}, u32[]{:S(2)}) %copy-start) | copy-done | bytes 3145752
  2.5 0.3 shard_map.96
  2.8 2.1 %collective-permute-start = (bf16[6,2,32,2,128]{4,3,2,1,0:T(2,128)(2,1)S(1)}, bf16[6,2,32,2,128]{4,3,2,1,0:T(2,128)(2,1)S(1)}, u32[]{:S(2)}, u32[]{:S(2)}) collective-permute-start(bf16[6,2,32,2,128]{4,3,2,1,0:T(2,128)(2,1)S(1)} %shard_map.96), channel_id=1, source_target_pairs={{0,8},{8,0},{16,24},{24,16},{1,9},{9,1},{17,25},{25,17},{2,10},{10... | collective-permute-start | bytes 589832 | tf_op jit(solution)/shard_map/ppermute | solution.py:51
  4.9 0.3 shard_map.97
  5.2 1.3 %collective-permute-start.1 = (bf16[6,2,32,2,128]{4,3,2,1,0:T(2,128)(2,1)S(1)}, bf16[6,2,32,2,128]{4,3,2,1,0:T(2,128)(2,1)S(1)}, u32[]{:S(2)}, u32[]{:S(2)}) collective-permute-start(bf16[6,2,32,2,128]{4,3,2,1,0:T(2,128)(2,1)S(1)} %shard_map.97), channel_id=1, source_target_pairs={{0,16},{8,24},{16,0},{24,8},{1,17},{9,25},{17,1},{25,9},{2,18},{10... | collective-permute-start | bytes 589832 | tf_op jit(solution)/shard_map/ppermute | solution.py:51
  6.5 0.3 shard_map.98
  6.9 2.7 %shard_map.95 = (bf16[6,2,32,2,128]{4,3,2,1,0:T(2,128)(2,1)S(1)}, bf16[6,2,32,2,128]{4,3,2,1,0:T(2,128)(2,1)S(1)}, bf16[4,6,4,32,2,128]{5,4,3,2,1,0:T(2,128)(2,1...) custom-call(bf16[12,32,2,2048]{3,2,1,0:T(2,128)(2,1)S(1)} %copy-done, bf16[256,256]{1,0:T(8,128)(2,1)S(1)} %copy-done.18, ...), custom_call_target="tpu_custom_call" | custom-call | flops 1024 | bytes 1024 | tf_op jit(solution)/shard_map/pallas_call | solution.py:142
  9.6 1.1 %copy-done.4 = bf16[4,6,4,32,2,128]{5,4,3,2,1,0:T(2,128)(2,1)} copy-done((bf16[4,6,4,32,2,128]{5,4,3,2,1,0:T(2,128)(2,1)}, bf16[4,6,4,32,2,128]{5,4,3,2,1,0:T(2,128)(2,1)S(1)}, u32[]{:S(2)}) %copy-start.4) | copy-done | bytes 1572888
  10.7 0.2 collective-permute-done.1
  10.9 3.9 %collective-permute-done.2 = bf16[6,2,32,2,128]{4,3,2,1,0:T(2,128)(2,1)S(1)} collective-permute-done((bf16[6,2,32,2,128]{4,3,2,1,0:T(2,128)(2,1)S(1)}, bf16[6,2,32,2,128]{4,3,2,1,0:T(2,128)(2,1)S(1)}, u32[]{:S(2)}, u32[]{:S(2)}) %collective-permute-start.2) | collective-permute-done | bytes 196640 | tf_op jit(solution)/shard_map/ppermute | solution.py:51
  14.8 0.8 shard_map.99
  15.6 1.2 %copy-done.2 = f32[6,256,256]{2,1,0:T(8,128)} copy-done((f32[6,256,256]{2,1,0:T(8,128)}, f32[6,256,256]{2,1,0:T(8,128)S(1)}, u32[]{:S(2)}) %copy-start.2) | copy-done | bytes 1572888
  16.8 1.1 %collective-permute-start.3 = (bf16[4,2,64,128]{3,2,1,0:T(8,128)(2,1)S(1)}, bf16[4,2,64,128]{3,2,1,0:T(8,128)(2,1)S(1)}, u32[]{:S(2)}, u32[]{:S(2)}) collective-permute-start(bf16[4,2,64,128]{3,2,1,0:T(8,128)(2,1)S(1)} %get-tuple-element.35), channel_id=1, source_target_pairs={{0,8},{8,0},{16,24},{24,16},{1,9},{9,1},{17,25},{25,17},{2,10},{10... | collective-permute-start | bytes 393224 | tf_op jit(solution)/shard_map/ppermute | solution.py:51
  17.8 0.3 collective-permute-start.4
  18.2 1.2 %collective-permute-start.5 = (bf16[4,2,64,128]{3,2,1,0:T(8,128)(2,1)S(1)}, bf16[4,2,64,128]{3,2,1,0:T(8,128)(2,1)S(1)}, u32[]{:S(2)}, u32[]{:S(2)}) collective-permute-start(bf16[4,2,64,128]{3,2,1,0:T(8,128)(2,1)S(1)} %get-tuple-element.37), channel_id=1, source_target_pairs={{0,24},{8,16},{16,8},{24,0},{1,25},{9,17},{17,9},{25,1},{2,26},{10... | collective-permute-start | bytes 393224 | tf_op jit(solution)/shard_map/ppermute | solution.py:51
  19.4 1.2 %collective-permute-done.3.refs_1_ = bf16[4,2,64,128]{3,2,1,0:T(8,128)(2,1)S(1)} collective-permute-done((bf16[4,2,64,128]{3,2,1,0:T(8,128)(2,1)S(1)}, bf16[4,2,64,128]{3,2,1,0:T(8,128)(2,1)S(1)}, u32[]{:S(2)}, u32[]{:S(2)}) %collective-permute-start.3) | collective-permute-done | bytes 131104 | tf_op jit(solution)/shard_map/ppermute | solution.py:51
  20.6 0.6 copy-done.9
  21.2 0.4 collective-permute-done.4.refs_2_
  21.7 0.7 copy-done.11
  22.3 1.2 %collective-permute-done.5.refs_3_ = bf16[4,2,64,128]{3,2,1,0:T(8,128)(2,1)S(1)} collective-permute-done((bf16[4,2,64,128]{3,2,1,0:T(8,128)(2,1)S(1)}, bf16[4,2,64,128]{3,2,1,0:T(8,128)(2,1)S(1)}, u32[]{:S(2)}, u32[]{:S(2)}) %collective-permute-start.5) | collective-permute-done | bytes 131104 | tf_op jit(solution)/shard_map/ppermute | solution.py:51
  23.5 0.6 copy-done.13
  24.2 4.6 %all-to-all-start = ((bf16[4,6,4,32,2,128]{5,4,3,2,1,0:T(2,128)(2,1)}), bf16[4,6,4,32,2,128]{5,4,3,2,1,0:T(2,128)(2,1)}, u32[]{:S(2)}, u32[]{:S(2)}) async-start(bf16[4,6,4,32,2,128]{5,4,3,2,1,0:T(2,128)(2,1)} %copy-done.4), calls=%async_computation | async-start | bytes 3145728 | tf_op jit(solution)/shard_map/all_to_all | solution.py:465
  28.8 0.3 shard_map.101
  29.1 1.7 %collective-permute-start.7 = (bf16[6,2,32,2,128]{4,3,2,1,0:T(2,128)(2,1)S(1)}, bf16[6,2,32,2,128]{4,3,2,1,0:T(2,128)(2,1)S(1)}, u32[]{:S(2)}, u32[]{:S(2)}) collective-permute-start(bf16[6,2,32,2,128]{4,3,2,1,0:T(2,128)(2,1)S(1)} %shard_map.101), channel_id=1, source_target_pairs={{0,16},{8,24},{16,0},{24,8},{1,17},{9,25},{17,1},{25,9},{2,18},{10... | collective-permute-start | bytes 589832 | tf_op jit(solution)/shard_map/ppermute | solution.py:51
  30.8 0.3 shard_map.102
  31.1 1.9 %collective-permute-start.8 = (bf16[6,2,32,2,128]{4,3,2,1,0:T(2,128)(2,1)S(1)}, bf16[6,2,32,2,128]{4,3,2,1,0:T(2,128)(2,1)S(1)}, u32[]{:S(2)}, u32[]{:S(2)}) collective-permute-start(bf16[6,2,32,2,128]{4,3,2,1,0:T(2,128)(2,1)S(1)} %shard_map.102), channel_id=1, source_target_pairs={{0,24},{8,16},{16,8},{24,0},{1,25},{9,17},{17,9},{25,1},{2,26},{10... | collective-permute-start | bytes 589832 | tf_op jit(solution)/shard_map/ppermute | solution.py:51
  33.0 0.3 shard_map.100
  33.3 0.1 collective-permute-start.6
  33.4 22.9 %collective-permute-done.7 = bf16[6,2,32,2,128]{4,3,2,1,0:T(2,128)(2,1)S(1)} collective-permute-done((bf16[6,2,32,2,128]{4,3,2,1,0:T(2,128)(2,1)S(1)}, bf16[6,2,32,2,128]{4,3,2,1,0:T(2,128)(2,1)S(1)}, u32[]{:S(2)}, u32[]{:S(2)}) %collective-permute-start.7) | collective-permute-done | bytes 196640 | tf_op jit(solution)/shard_map/ppermute | solution.py:51
  56.3 0.8 shard_map.103
  57.2 0.1 collective-permute-start.9
  57.3 2.6 %collective-permute-start.11 = (bf16[4,2,64,128]{3,2,1,0:T(8,128)(2,1)S(1)}, bf16[4,2,64,128]{3,2,1,0:T(8,128)(2,1)S(1)}, u32[]{:S(2)}, u32[]{:S(2)}) collective-permute-start(bf16[4,2,64,128]{3,2,1,0:T(8,128)(2,1)S(1)} %get-tuple-element.46), channel_id=1, source_target_pairs={{0,24},{8,16},{16,8},{24,0},{1,25},{9,17},{17,9},{25,1},{2,26},{10... | collective-permute-start | bytes 393224 | tf_op jit(solution)/shard_map/ppermute | solution.py:51
  59.9 1.2 %collective-permute-done.9.refs_5_ = bf16[4,2,64,128]{3,2,1,0:T(8,128)(2,1)S(1)} collective-permute-done((bf16[4,2,64,128]{3,2,1,0:T(8,128)(2,1)S(1)}, bf16[4,2,64,128]{3,2,1,0:T(8,128)(2,1)S(1)}, u32[]{:S(2)}, u32[]{:S(2)}) %collective-permute-start.9) | collective-permute-done | bytes 131104 | tf_op jit(solution)/shard_map/ppermute | solution.py:51
  61.1 1.8 %collective-permute-done.10.refs_6_ = bf16[4,2,64,128]{3,2,1,0:T(8,128)(2,1)S(1)} collective-permute-done((bf16[4,2,64,128]{3,2,1,0:T(8,128)(2,1)S(1)}, bf16[4,2,64,128]{3,2,1,0:T(8,128)(2,1)S(1)}, u32[]{:S(2)}, u32[]{:S(2)}) %collective-permute-start.10) | collective-permute-done | bytes 131104 | tf_op jit(solution)/shard_map/ppermute | solution.py:51
  62.8 0.4 collective-permute-done.11.refs_7_
  63.2 1.2 %shard_map.104 = (bf16[4,2,64,128]{3,2,1,0:T(8,128)(2,1)S(1)}, bf16[4,2,64,128]{3,2,1,0:T(8,128)(2,1)S(1)}) custom-call(bf16[4,2,64,128]{3,2,1,0:T(8,128)(2,1)S(1)} %get-tuple-element.34.refs_0_, bf16[4,2,64,128]{3,2,1,0:T(8,128)(2,1)S(1)} %copy-done.10, bf16[4,2,64,128]{3,2,1,0:T(8,128)(2,1)S(1)} %copy-done.12, bf16[4,2,64,128]{3,2,1,0:T(8,128)(2,1)S(1)} %copy-done.14, ...), custom_call_target="tpu_custom_call" | custom-call | flops 1024 | bytes 1024 | tf_op jit(solution)/shard_map/pallas_call | solution.py:304
  64.4 6.9 %collective-permute-start.12 = (bf16[4,2,64,128]{3,2,1,0:T(8,128)(2,1)S(1)}, bf16[4,2,64,128]{3,2,1,0:T(8,128)(2,1)S(1)}, u32[]{:S(2)}, u32[]{:S(2)}) collective-permute-start(bf16[4,2,64,128]{3,2,1,0:T(8,128)(2,1)S(1)} %get-tuple-element.47), channel_id=1, source_target_pairs={{0,1},{1,2},{2,3},{3,4},{4,5},{5,6},{6,7},{8,9},{9,10},{10,11},{11... | collective-permute-start | bytes 393224 | tf_op jit(solution)/shard_map/ppermute | solution.py:58
  71.4 1.9 %collective-permute-start.13 = (bf16[4,2,64,128]{3,2,1,0:T(8,128)(2,1)S(1)}, bf16[4,2,64,128]{3,2,1,0:T(8,128)(2,1)S(1)}, u32[]{:S(2)}, u32[]{:S(2)}) collective-permute-start(bf16[4,2,64,128]{3,2,1,0:T(8,128)(2,1)S(1)} %get-tuple-element.48), channel_id=1, source_target_pairs={{1,0},{2,1},{3,2},{4,3},{5,4},{6,5},{7,6},{9,8},{10,9},{11,10},{12... | collective-permute-start | bytes 393224 | tf_op jit(solution)/shard_map/ppermute | solution.py:58
  73.3 4.3 %collective-permute-done.13.refs_9_ = bf16[4,2,64,128]{3,2,1,0:T(8,128)(2,1)S(1)} collective-permute-done((bf16[4,2,64,128]{3,2,1,0:T(8,128)(2,1)S(1)}, bf16[4,2,64,128]{3,2,1,0:T(8,128)(2,1)S(1)}, u32[]{:S(2)}, u32[]{:S(2)}) %collective-permute-start.13) | collective-permute-done | bytes 131104 | tf_op jit(solution)/shard_map/ppermute | solution.py:58
  77.7 6.6 %shard_map.105 = (f32[3072,128]{1,0:T(8,128)}, f32[3,16,64,128]{3,2,1,0:T(8,128)S(1)}) custom-call(bf16[4,2,64,128]{3,2,1,0:T(8,128)(2,1)S(1)} %get-tuple-element.34.refs_0_, bf16[4,2,64,128]{3,2,1,0:T(8,128)(2,1)S(1)} %copy-done.10, bf16[4,2,64,128]{3,2,1,0:T(8,128)(2,1)S(1)} %copy-done.12, bf16[4,2,64,128]{3,2,1,0:T(8,128)(2,1)S(1)} %copy-done.14, ...), custom_call_target="tpu_custom_call" | custom-call | flops 1024 | bytes 1024 | tf_op jit(solution)/shard_map/pallas_call | solution.py:385
  84.3 1.2 %copy-done.5 = f32[3,16,64,128]{3,2,1,0:T(8,128)} copy-done((f32[3,16,64,128]{3,2,1,0:T(8,128)}, f32[3,16,64,128]{3,2,1,0:T(8,128)S(1)}, u32[]{:S(2)}) %copy-start.5) | copy-done | bytes 1572888
  85.5 3.0 %shard_map.106 = (bf16[3,4,64,128]{3,2,1,0:T(8,128)(2,1)S(1)}, bf16[3,4,64,128]{3,2,1,0:T(8,128)(2,1)S(1)}, bf16[3,4,64,128]{3,2,1,0:T(8,128)(2,1)S(1)}, bf16[3,4,64,128]{3,2,1,0:T(8,128)(2,1)S(1)}) custom-call(bf16[4,6,4,64,128]{4,3,2,1,0:T(8,128)(2,1)} %bitcast.13.refs_0_, f32[6,256,256]{2,1,0:T(8,128)S(1)} %copy-done.3, ...), custom_call_target="tpu_custom_call" | custom-call | flops 1024 | bytes 1024 | tf_op jit(solution)/shard_map/pallas_call | solution.py:254
  88.5 0.5 collective-permute-start.14
  89.0 1.3 %collective-permute-start.15 = (bf16[3,4,64,128]{3,2,1,0:T(8,128)(2,1)S(1)}, bf16[3,4,64,128]{3,2,1,0:T(8,128)(2,1)S(1)}, u32[]{:S(2)}, u32[]{:S(2)}) collective-permute-start(bf16[3,4,64,128]{3,2,1,0:T(8,128)(2,1)S(1)} %get-tuple-element.57), channel_id=1, source_target_pairs={{0,16},{8,24},{16,0},{24,8},{1,17},{9,25},{17,1},{25,9},{2,18},{10... | collective-permute-start | bytes 589832 | tf_op jit(solution)/shard_map/ppermute | solution.py:51
  90.3 0.9 collective-permute-start.16
  91.2 3.9 %collective-permute-done.14.refs_1_ = bf16[3,4,64,128]{3,2,1,0:T(8,128)(2,1)S(1)} collective-permute-done((bf16[3,4,64,128]{3,2,1,0:T(8,128)(2,1)S(1)}, bf16[3,4,64,128]{3,2,1,0:T(8,128)(2,1)S(1)}, u32[]{:S(2)}, u32[]{:S(2)}) %collective-permute-start.14) | collective-permute-done | bytes 196640 | tf_op jit(solution)/shard_map/ppermute | solution.py:51
  95.1 2.6 %collective-permute-done.15.refs_2_ = bf16[3,4,64,128]{3,2,1,0:T(8,128)(2,1)S(1)} collective-permute-done((bf16[3,4,64,128]{3,2,1,0:T(8,128)(2,1)S(1)}, bf16[3,4,64,128]{3,2,1,0:T(8,128)(2,1)S(1)}, u32[]{:S(2)}, u32[]{:S(2)}) %collective-permute-start.15) | collective-permute-done | bytes 196640 | tf_op jit(solution)/shard_map/ppermute | solution.py:51
  97.7 2.2 %shard_map.107 = f32[3072,128]{1,0:T(8,128)} custom-call(bf16[3,4,64,128]{3,2,1,0:T(8,128)(2,1)S(1)} %get-tuple-element.55.refs_0_, bf16[3,4,64,128]{3,2,1,0:T(8,128)(2,1)S(1)} %collective-permute-done.14.refs_1_, bf16[3,4,64,128]{3,2,1,0:T(8,128)(2,1)S(1)} %collective-permute-done.15.refs_2_, bf16[3,4,64,128]{3,2,1,0:T(8,128)(2,1)S(1)} %collective-permute-done.16.refs_3_, ...), custom_call_target="tpu_custom_call" | custom-call | flops 1024 | bytes 1024 | tf_op jit(solution)/shard_map/pallas_call | solution.py:428
  (45 shorter events, 0.3 us)
Async XLA Ops:
  0.6 1.9 %copy-start = (bf16[12,32,2,2048]{3,2,1,0:T(2,128)(2,1)S(1)}, bf16[12,32,2,2048]{3,2,1,0:T(2,128)(2,1)}, u32[]{:S(2)}) copy-start(bf16[12,32,2,2048]{3,2,1,0:T(2,128)(2,1)} %fields_ref.13) | copy-start | bytes 9437188
  2.8 7.9 %collective-permute-start = (bf16[6,2,32,2,128]{4,3,2,1,0:T(2,128)(2,1)S(1)}, bf16[6,2,32,2,128]{4,3,2,1,0:T(2,128)(2,1)S(1)}, u32[]{:S(2)}, u32[]{:S(2)}) collective-permute-start(bf16[6,2,32,2,128]{4,3,2,1,0:T(2,128)(2,1)S(1)} %shard_map.96), channel_id=1, source_target_pairs={{0,8},{8,0},{16,24},{24,16},{1,9},{9,1},{17,25},{25,17},{2,10},{10... | collective-permute-start | bytes 589832 | tf_op jit(solution)/shard_map/ppermute | solution.py:51
  5.2 1.7 %copy-start.17 = (bf16[256,256]{1,0:T(8,128)(2,1)S(1)}, bf16[256,256]{1,0:T(8,128)(2,1)}, u32[]{:S(2)}) copy-start(bf16[256,256]{1,0:T(8,128)(2,1)} %constant.5.clone.refs_1_) | copy-start | bytes 393220
  5.2 1.7 %copy-start.18 = (bf16[256,256]{1,0:T(8,128)(2,1)S(1)}, bf16[256,256]{1,0:T(8,128)(2,1)}, u32[]{:S(2)}) copy-start(bf16[256,256]{1,0:T(8,128)(2,1)} %constant.4.clone.refs_0_) | copy-start | bytes 393220
  5.2 5.7 %collective-permute-start.1 = (bf16[6,2,32,2,128]{4,3,2,1,0:T(2,128)(2,1)S(1)}, bf16[6,2,32,2,128]{4,3,2,1,0:T(2,128)(2,1)S(1)}, u32[]{:S(2)}, u32[]{:S(2)}) collective-permute-start(bf16[6,2,32,2,128]{4,3,2,1,0:T(2,128)(2,1)S(1)} %shard_map.97), channel_id=1, source_target_pairs={{0,16},{8,24},{16,0},{24,8},{1,17},{9,25},{17,1},{25,9},{2,18},{10... | collective-permute-start | bytes 589832 | tf_op jit(solution)/shard_map/ppermute | solution.py:51
  6.8 8.0 %collective-permute-start.2 = (bf16[6,2,32,2,128]{4,3,2,1,0:T(2,128)(2,1)S(1)}, bf16[6,2,32,2,128]{4,3,2,1,0:T(2,128)(2,1)S(1)}, u32[]{:S(2)}, u32[]{:S(2)}) collective-permute-start(bf16[6,2,32,2,128]{4,3,2,1,0:T(2,128)(2,1)S(1)} %shard_map.98), channel_id=1, source_target_pairs={{0,24},{8,16},{16,8},{24,0},{1,25},{9,17},{17,9},{25,1},{2,26},{10... | collective-permute-start | bytes 589832 | tf_op jit(solution)/shard_map/ppermute | solution.py:51
  9.6 1.1 %copy-start.4 = (bf16[4,6,4,32,2,128]{5,4,3,2,1,0:T(2,128)(2,1)}, bf16[4,6,4,32,2,128]{5,4,3,2,1,0:T(2,128)(2,1)S(1)}, u32[]{:S(2)}) copy-start(bf16[4,6,4,32,2,128]{5,4,3,2,1,0:T(2,128)(2,1)S(1)} %get-tuple-element.50) | copy-start | bytes 4718596
  10.7 12.8 %copy-start.15 = (bf16[6,2,32,2,128]{4,3,2,1,0:T(2,128)(2,1)}, bf16[6,2,32,2,128]{4,3,2,1,0:T(2,128)(2,1)S(1)}, u32[]{:S(2)}) copy-start(bf16[6,2,32,2,128]{4,3,2,1,0:T(2,128)(2,1)S(1)} %get-tuple-element.42) | copy-start | bytes 589828
  15.6 1.2 %copy-start.2 = (f32[6,256,256]{2,1,0:T(8,128)}, f32[6,256,256]{2,1,0:T(8,128)S(1)}, u32[]{:S(2)}) copy-start(f32[6,256,256]{2,1,0:T(8,128)S(1)} %get-tuple-element.53.refs_1_) | copy-start | bytes 4718596
  16.8 3.8 %collective-permute-start.3 = (bf16[4,2,64,128]{3,2,1,0:T(8,128)(2,1)S(1)}, bf16[4,2,64,128]{3,2,1,0:T(8,128)(2,1)S(1)}, u32[]{:S(2)}, u32[]{:S(2)}) collective-permute-start(bf16[4,2,64,128]{3,2,1,0:T(8,128)(2,1)S(1)} %get-tuple-element.35), channel_id=1, source_target_pairs={{0,8},{8,0},{16,24},{24,16},{1,9},{9,1},{17,25},{25,17},{2,10},{10... | collective-permute-start | bytes 393224 | tf_op jit(solution)/shard_map/ppermute | solution.py:51
  17.8 3.8 %collective-permute-start.4 = (bf16[4,2,64,128]{3,2,1,0:T(8,128)(2,1)S(1)}, bf16[4,2,64,128]{3,2,1,0:T(8,128)(2,1)S(1)}, u32[]{:S(2)}, u32[]{:S(2)}) collective-permute-start(bf16[4,2,64,128]{3,2,1,0:T(8,128)(2,1)S(1)} %get-tuple-element.36), channel_id=1, source_target_pairs={{0,16},{8,24},{16,0},{24,8},{1,17},{9,25},{17,1},{25,9},{2,18},{10... | collective-permute-start | bytes 393224 | tf_op jit(solution)/shard_map/ppermute | solution.py:51
  18.2 5.3 %collective-permute-start.5 = (bf16[4,2,64,128]{3,2,1,0:T(8,128)(2,1)S(1)}, bf16[4,2,64,128]{3,2,1,0:T(8,128)(2,1)S(1)}, u32[]{:S(2)}, u32[]{:S(2)}) collective-permute-start(bf16[4,2,64,128]{3,2,1,0:T(8,128)(2,1)S(1)} %get-tuple-element.37), channel_id=1, source_target_pairs={{0,24},{8,16},{16,8},{24,0},{1,25},{9,17},{17,9},{25,1},{2,26},{10... | collective-permute-start | bytes 393224 | tf_op jit(solution)/shard_map/ppermute | solution.py:51
  20.6 0.6 copy-start.9
  21.7 0.7 copy-start.11
  23.5 0.6 copy-start.13
  24.2 4.6 %copy-start.1 = (bf16[12,32,2,2048]{3,2,1,0:T(2,128)(2,1)S(1)}, bf16[12,32,2,2048]{3,2,1,0:T(2,128)(2,1)}, u32[]{:S(2)}) copy-start(bf16[12,32,2,2048]{3,2,1,0:T(2,128)(2,1)} %fields_ref.13) | copy-start | bytes 9437188
  24.2 61.3 %all-to-all-start = ((bf16[4,6,4,32,2,128]{5,4,3,2,1,0:T(2,128)(2,1)}), bf16[4,6,4,32,2,128]{5,4,3,2,1,0:T(2,128)(2,1)}, u32[]{:S(2)}, u32[]{:S(2)}) async-start(bf16[4,6,4,32,2,128]{5,4,3,2,1,0:T(2,128)(2,1)} %copy-done.4), calls=%async_computation | async-start | bytes 3145728 | tf_op jit(solution)/shard_map/all_to_all | solution.py:465
  29.1 27.2 %collective-permute-start.7 = (bf16[6,2,32,2,128]{4,3,2,1,0:T(2,128)(2,1)S(1)}, bf16[6,2,32,2,128]{4,3,2,1,0:T(2,128)(2,1)S(1)}, u32[]{:S(2)}, u32[]{:S(2)}) collective-permute-start(bf16[6,2,32,2,128]{4,3,2,1,0:T(2,128)(2,1)S(1)} %shard_map.101), channel_id=1, source_target_pairs={{0,16},{8,24},{16,0},{24,8},{1,17},{9,25},{17,1},{25,9},{2,18},{10... | collective-permute-start | bytes 589832 | tf_op jit(solution)/shard_map/ppermute | solution.py:51
  31.1 25.3 %copy-start.16 = (bf16[6,2,32,2,128]{4,3,2,1,0:T(2,128)(2,1)S(1)}, bf16[6,2,32,2,128]{4,3,2,1,0:T(2,128)(2,1)}, u32[]{:S(2)}) copy-start(bf16[6,2,32,2,128]{4,3,2,1,0:T(2,128)(2,1)} %copy-done.15) | copy-start | bytes 589828
  31.1 32.1 %copy-start.10 = (bf16[4,2,64,128]{3,2,1,0:T(8,128)(2,1)S(1)}, bf16[4,2,64,128]{3,2,1,0:T(8,128)(2,1)}, u32[]{:S(2)}) copy-start(bf16[4,2,64,128]{3,2,1,0:T(8,128)(2,1)} %copy-done.9) | copy-start | bytes 393220
  31.1 32.1 %copy-start.12 = (bf16[4,2,64,128]{3,2,1,0:T(8,128)(2,1)S(1)}, bf16[4,2,64,128]{3,2,1,0:T(8,128)(2,1)}, u32[]{:S(2)}) copy-start(bf16[4,2,64,128]{3,2,1,0:T(8,128)(2,1)} %copy-done.11) | copy-start | bytes 393220
  31.1 32.1 %copy-start.14 = (bf16[4,2,64,128]{3,2,1,0:T(8,128)(2,1)S(1)}, bf16[4,2,64,128]{3,2,1,0:T(8,128)(2,1)}, u32[]{:S(2)}) copy-start(bf16[4,2,64,128]{3,2,1,0:T(8,128)(2,1)} %copy-done.13) | copy-start | bytes 393220
  31.1 32.1 %copy-start.21 = (s32[2,256]{1,0:T(2,128)S(1)}, s32[2,256]{1,0:T(2,128)}, u32[]{:S(2)}) copy-start(s32[2,256]{1,0:T(2,128)} %refs_8_.1) | copy-start | bytes 6148
  31.1 25.2 %collective-permute-start.8 = (bf16[6,2,32,2,128]{4,3,2,1,0:T(2,128)(2,1)S(1)}, bf16[6,2,32,2,128]{4,3,2,1,0:T(2,128)(2,1)S(1)}, u32[]{:S(2)}, u32[]{:S(2)}) collective-permute-start(bf16[6,2,32,2,128]{4,3,2,1,0:T(2,128)(2,1)S(1)} %shard_map.102), channel_id=1, source_target_pairs={{0,24},{8,16},{16,8},{24,0},{1,25},{9,17},{17,9},{25,1},{2,26},{10... | collective-permute-start | bytes 589832 | tf_op jit(solution)/shard_map/ppermute | solution.py:51
  33.0 44.6 %copy-start.8 = (bf16[5,64,2048]{2,1,0:T(8,128)(2,1)S(1)}, bf16[5,64,2048]{2,1,0:T(8,128)(2,1)}, u32[]{:S(2)}) copy-start(bf16[5,64,2048]{2,1,0:T(8,128)(2,1)} %refs_11_.1) | copy-start | bytes 3932164
  33.3 44.4 %copy-start.7 = (bf16[5,64,2048]{2,1,0:T(8,128)(2,1)S(1)}, bf16[5,64,2048]{2,1,0:T(8,128)(2,1)}, u32[]{:S(2)}) copy-start(bf16[5,64,2048]{2,1,0:T(8,128)(2,1)} %refs_10_.1) | copy-start | bytes 3932164
  33.3 44.4 %copy-start.19 = (f32[2048]{0:T(1024)S(1)}, f32[2048]{0:T(1024)}, u32[]{:S(2)}) copy-start(f32[2048]{0:T(1024)} %param.9) | copy-start | bytes 24580
  33.3 44.3 %copy-start.20 = (s32[32,5]{0,1:T(8,128)S(1)}, s32[32,5]{0,1:T(8,128)}, u32[]{:S(2)}) copy-start(s32[32,5]{0,1:T(8,128)} %param.12) | copy-start | bytes 1924
  33.3 23.0 %collective-permute-start.6 = (bf16[6,2,32,2,128]{4,3,2,1,0:T(2,128)(2,1)S(1)}, bf16[6,2,32,2,128]{4,3,2,1,0:T(2,128)(2,1)S(1)}, u32[]{:S(2)}, u32[]{:S(2)}) collective-permute-start(bf16[6,2,32,2,128]{4,3,2,1,0:T(2,128)(2,1)S(1)} %shard_map.100), channel_id=1, source_target_pairs={{0,8},{8,0},{16,24},{24,16},{1,9},{9,1},{17,25},{25,17},{2,10},{10... | collective-permute-start | bytes 589832 | tf_op jit(solution)/shard_map/ppermute | solution.py:51
  57.2 3.9 %collective-permute-start.9 = (bf16[4,2,64,128]{3,2,1,0:T(8,128)(2,1)S(1)}, bf16[4,2,64,128]{3,2,1,0:T(8,128)(2,1)S(1)}, u32[]{:S(2)}, u32[]{:S(2)}) collective-permute-start(bf16[4,2,64,128]{3,2,1,0:T(8,128)(2,1)S(1)} %get-tuple-element.44), channel_id=1, source_target_pairs={{0,8},{8,0},{16,24},{24,16},{1,9},{9,1},{17,25},{25,17},{2,10},{10... | collective-permute-start | bytes 393224 | tf_op jit(solution)/shard_map/ppermute | solution.py:51
  57.3 5.6 %collective-permute-start.10 = (bf16[4,2,64,128]{3,2,1,0:T(8,128)(2,1)S(1)}, bf16[4,2,64,128]{3,2,1,0:T(8,128)(2,1)S(1)}, u32[]{:S(2)}, u32[]{:S(2)}) collective-permute-start(bf16[4,2,64,128]{3,2,1,0:T(8,128)(2,1)S(1)} %get-tuple-element.45), channel_id=1, source_target_pairs={{0,16},{8,24},{16,0},{24,8},{1,17},{9,25},{17,1},{25,9},{2,18},{10... | collective-permute-start | bytes 393224 | tf_op jit(solution)/shard_map/ppermute | solution.py:51
  57.3 5.9 %collective-permute-start.11 = (bf16[4,2,64,128]{3,2,1,0:T(8,128)(2,1)S(1)}, bf16[4,2,64,128]{3,2,1,0:T(8,128)(2,1)S(1)}, u32[]{:S(2)}, u32[]{:S(2)}) collective-permute-start(bf16[4,2,64,128]{3,2,1,0:T(8,128)(2,1)S(1)} %get-tuple-element.46), channel_id=1, source_target_pairs={{0,24},{8,16},{16,8},{24,0},{1,25},{9,17},{17,9},{25,1},{2,26},{10... | collective-permute-start | bytes 393224 | tf_op jit(solution)/shard_map/ppermute | solution.py:51
  64.4 8.9 %collective-permute-start.12 = (bf16[4,2,64,128]{3,2,1,0:T(8,128)(2,1)S(1)}, bf16[4,2,64,128]{3,2,1,0:T(8,128)(2,1)S(1)}, u32[]{:S(2)}, u32[]{:S(2)}) collective-permute-start(bf16[4,2,64,128]{3,2,1,0:T(8,128)(2,1)S(1)} %get-tuple-element.47), channel_id=1, source_target_pairs={{0,1},{1,2},{2,3},{3,4},{4,5},{5,6},{6,7},{8,9},{9,10},{10,11},{11... | collective-permute-start | bytes 393224 | tf_op jit(solution)/shard_map/ppermute | solution.py:58
  71.4 6.3 %collective-permute-start.13 = (bf16[4,2,64,128]{3,2,1,0:T(8,128)(2,1)S(1)}, bf16[4,2,64,128]{3,2,1,0:T(8,128)(2,1)S(1)}, u32[]{:S(2)}, u32[]{:S(2)}) collective-permute-start(bf16[4,2,64,128]{3,2,1,0:T(8,128)(2,1)S(1)} %get-tuple-element.48), channel_id=1, source_target_pairs={{1,0},{2,1},{3,2},{4,3},{5,4},{6,5},{7,6},{9,8},{10,9},{11,10},{12... | collective-permute-start | bytes 393224 | tf_op jit(solution)/shard_map/ppermute | solution.py:58
  77.7 7.8 %copy-start.3 = (f32[6,256,256]{2,1,0:T(8,128)S(1)}, f32[6,256,256]{2,1,0:T(8,128)}, u32[]{:S(2)}) copy-start(f32[6,256,256]{2,1,0:T(8,128)} %copy-done.2) | copy-start | bytes 4718596
  84.3 1.2 %copy-start.5 = (f32[3,16,64,128]{3,2,1,0:T(8,128)}, f32[3,16,64,128]{3,2,1,0:T(8,128)S(1)}, u32[]{:S(2)}) copy-start(f32[3,16,64,128]{3,2,1,0:T(8,128)S(1)} %get-tuple-element.59.refs_4_) | copy-start | bytes 4718596
  85.4 12.3 %copy-start.6 = (f32[3,16,64,128]{3,2,1,0:T(8,128)S(1)}, f32[3,16,64,128]{3,2,1,0:T(8,128)}, u32[]{:S(2)}) copy-start(f32[3,16,64,128]{3,2,1,0:T(8,128)} %copy-done.5) | copy-start | bytes 4718596
  88.5 6.6 %collective-permute-start.14 = (bf16[3,4,64,128]{3,2,1,0:T(8,128)(2,1)S(1)}, bf16[3,4,64,128]{3,2,1,0:T(8,128)(2,1)S(1)}, u32[]{:S(2)}, u32[]{:S(2)}) collective-permute-start(bf16[3,4,64,128]{3,2,1,0:T(8,128)(2,1)S(1)} %get-tuple-element.56), channel_id=1, source_target_pairs={{0,8},{8,0},{16,24},{24,16},{1,9},{9,1},{17,25},{25,17},{2,10},{10... | collective-permute-start | bytes 589832 | tf_op jit(solution)/shard_map/ppermute | solution.py:51
  89.0 8.7 %collective-permute-start.15 = (bf16[3,4,64,128]{3,2,1,0:T(8,128)(2,1)S(1)}, bf16[3,4,64,128]{3,2,1,0:T(8,128)(2,1)S(1)}, u32[]{:S(2)}, u32[]{:S(2)}) collective-permute-start(bf16[3,4,64,128]{3,2,1,0:T(8,128)(2,1)S(1)} %get-tuple-element.57), channel_id=1, source_target_pairs={{0,16},{8,24},{16,0},{24,8},{1,17},{9,25},{17,1},{25,9},{2,18},{10... | collective-permute-start | bytes 589832 | tf_op jit(solution)/shard_map/ppermute | solution.py:51
  90.3 7.4 %collective-permute-start.16 = (bf16[3,4,64,128]{3,2,1,0:T(8,128)(2,1)S(1)}, bf16[3,4,64,128]{3,2,1,0:T(8,128)(2,1)S(1)}, u32[]{:S(2)}, u32[]{:S(2)}) collective-permute-start(bf16[3,4,64,128]{3,2,1,0:T(8,128)(2,1)S(1)} %get-tuple-element.58), channel_id=1, source_target_pairs={{0,24},{8,16},{16,8},{24,0},{1,25},{9,17},{17,9},{25,1},{2,26},{10... | collective-permute-start | bytes 589832 | tf_op jit(solution)/shard_map/ppermute | solution.py:51

commit v5 on v4

--- a/solution.py
+++ b/solution.py
@@ -74,7 +74,7 @@
 
 
 def groups_of(tiles):
-    return 2 if tiles % 2 == 0 else 1
+    return 1
 
 
 def pieces_of(fields_ref, first, share, group, out_ref):
@@ -130,21 +130,21 @@
 
     def kernel(fields_ref, *refs):
         inputs, refs = refs[: len(carried)], refs[len(carried) :]
-        own_refs, all_ref, outputs = refs[:groups], refs[groups], refs[groups + 1 : -1]
+        own_refs, share_refs, outputs = refs[:groups], refs[groups : groups + count], refs[groups + count : -1]
         me = lax.axis_index("mode")
         pairs = []
         for group in range(groups):
             pairs += pieces_of(fields_ref, 0, me, group, own_refs[group])
-        for share in range(count):
-            pairs += pieces_of(fields_ref, middle, share, 0, all_ref.at[share])
+        for step in range(count):
+            pairs += pieces_of(fields_ref, middle, dest_of(me, step, count), 0, share_refs[step])
         run_copies(pairs, refs[-1], zip(inputs, outputs))
 
     return pl.pallas_call(
         kernel,
         in_specs=[pl.BlockSpec(memory_space=pl.ANY)] + [vmem()] * len(carried),
-        out_specs=[vmem()] * (groups + 1 + len(carried)),
+        out_specs=[vmem()] * (groups + count + len(carried)),
         out_shape=[jax.ShapeDtypeStruct(shape, jnp.bfloat16)] * groups
-        + [jax.ShapeDtypeStruct((count,) + full, jnp.bfloat16)]
+        + [jax.ShapeDtypeStruct(full, jnp.bfloat16)] * count
         + [jax.ShapeDtypeStruct(value.shape, value.dtype) for value in carried],
         scratch_shapes=[pltpu.SemaphoreType.DMA((groups * shape[0] * shape[1] + count * full[0] * full[1],))],
         compiler_params=params(),
@@ -225,14 +225,17 @@
 
 
 def second_kernel(count, groups, *refs):
-    in_ref, first_refs, (inverse_ref, forward_ref) = refs[0], refs[1 : groups + 1], refs[groups + 1 : groups + 3]
-    out_refs, (physical_ref, x_ref, product_ref, table_ref) = refs[groups + 3 : groups + 3 + count], refs[groups + 3 + count :]
+    in_refs, refs = refs[:count], refs[count:]
+    first_refs, (inverse_ref, forward_ref) = refs[:groups], refs[groups : groups + 2]
+    out_refs, (physical_ref, x_ref, product_ref, table_ref) = refs[groups + 2 : groups + 2 + count], refs[groups + 2 + count :]
     width = first_refs[0].shape[2]
 
     def store(c, value):
         physical_ref[c] = value
 
-    to_physical(range(count), [in_ref.at[source] for source in range(count)], inverse_ref[...], x_ref, store)
+    me = lax.axis_index("mode")
+    sources = [source_of(me, step, count) for step in range(count)]
+    to_physical(sources, in_refs, inverse_ref[...], x_ref, store)
     for group in range(groups):
         lanes = slice(group * width, (group + 1) * width)
         for i in range(THETA // CHUNK):
@@ -247,13 +250,14 @@
     to_modes(count, forward_ref, table_ref, product_ref, out_refs)
 
 
-def second_physics(shares, physical, inverse, forward):
-    count, components, tiles, rows, _ = shares.shape
+def second_physics(received, physical, inverse, forward):
+    count = len(received)
+    components, tiles, rows, _ = received[0].shape
     groups = len(physical)
     width = tiles * LANES
     return pl.pallas_call(
         functools.partial(second_kernel, count, groups),
-        in_specs=[vmem()] * (groups + 3),
+        in_specs=[vmem()] * (count + groups + 2),
         out_specs=[vmem()] * count,
         out_shape=[jax.ShapeDtypeStruct((3, tiles, rows, LANES), jnp.bfloat16)] * count,
         scratch_shapes=[
@@ -264,7 +268,7 @@
         ],
         compiler_params=params(),
         cost_estimate=cost(),
-    )(shares, *physical, inverse, forward)
+    )(*received, *physical, inverse, forward)
 
 
 def tiles_of(in_refs, count):
@@ -455,14 +459,15 @@
     arrived = []
     for group in range(groups):
         arrived.append(exchange([pack(mode_fields, 0, 6, step, group, groups) for step in range(1, count)]))
-    *own, shares, inverse, forward = pack_rest(mode_fields, 6, groups, [inverse, forward])
+    *packed, inverse, forward = pack_rest(mode_fields, 6, groups, [inverse, forward])
+    own, shares = packed[:groups], packed[groups:]
     local, physical = [], []
     for group in range(groups):
         *terms, velocity_magnetic = first_physics(joined([own[group]] + arrived[group]), inverse, forward)
         back = exchange(terms[1:])
         if group == 0:
-            back, shares = lax.optimization_barrier((back, shares))
-            shares = lax.all_to_all(shares, "mode", 0, 0, tiled=True)
+            back[0], shares = lax.optimization_barrier((back[0], shares))
+            shares = shares[:1] + exchange(shares[1:])
         local += terms[:1] + back
         physical.append(velocity_magnetic)
     toward_prev, toward_next = interface(local, interface_nodes, count)
@@ -472,7 +477,7 @@
         local, from_prev, from_next, radial_blocks, axial_blocks, radius.reshape(1, width), block_columns.T, count
     )
     shares, gradient = lax.optimization_barrier((shares, gradient))
-    lorentz = list(second_physics(joined([shares])[0], physical, inverse, forward))
+    lorentz = list(second_physics(joined(shares), physical, inverse, forward))
     lorentz = lorentz[:1] + exchange(lorentz[1:])
     momentum = momentum_of(lorentz, gradient)
     return (whole_output(induction, mode_count, width), whole_output(momentum, mode_count, width))

time: 101 us -> 75 us (0.74)
  waiting for transfers between devices: 43.9 us -> 32.6 us
  starting transfers between devices: 28.7 us -> 21.7 us
  local copies, waits for them, and re-layouts: 7.4 us -> 1.93 us
  Pallas kernels: 18.9 us -> 17.3 us
    ppermute x15 -> x12, waiting for transfers between devices: 39.6 us -> 28 us  [exchange(): received.append(lax.ppermute(pieces[step - 1], 'mode', pairs))]
    unnamed x44 -> x16, local copies, waits for them, and re-layouts: 7.4 us -> 1.93 us
    all_to_all x1 -> x0, starting transfers between devices: 4.61 us -> none  [body(): shares = lax.all_to_all(shares, 'mode', 0, 0, tiled=True)]
    ppermute x15 -> x12, starting transfers between devices: 15.2 us -> 11.6 us  [exchange(): received.append(lax.ppermute(pieces[step - 1], 'mode', pairs))]
    pallas_call x1, Pallas kernels: 3.02 us -> 1.58 us  [second_physics(): pl.pallas_call(functools.partial(second_kernel, count, groups), in_specs=...]
    ppermute x2, starting transfers between devices: 8.84 us -> 10.1 us  [from_behind(): lax.ppermute(value, axis, [(source, source + steps) for source in range(i...]
  transfers between devices with their start and end apart: 18 -> 14, of which waited for: 12 -> 7; matrix products, arithmetic and copies ran while one was open for 0% -> 0% of each run, Pallas kernels for 13% -> 16%
where the time goes in v5:
time: 75 us; the launch traced here: 74.3 us
  waiting for transfers between devices  32.6 us (43%)
  starting transfers between devices  21.7 us (29%)
  Pallas kernels  17.3 us (23%)
  local copies, waits for them, and re-layouts  1.93 us (3%)
  between operations  0.79 us (1%)
    ppermute x12, waiting for transfers between devices, exchange(): received.append(lax.ppermute(pieces[step - 1], 'mode', pairs))  28 us
    ppermute x12, starting transfers between devices, exchange(): received.append(lax.ppermute(pieces[step - 1], 'mode', pairs))  11.6 us
    ppermute x2, starting transfers between devices, from_behind(): lax.ppermute(value, axis, [(source, source + steps) for source in range(i...  10.1 us
    pallas_call x1, Pallas kernels, derive(): pl.pallas_call(functools.partial(derive_kernel, count, len(received)), in...  6.59 us
    ppermute x2, waiting for transfers between devices, from_behind(): lax.ppermute(value, axis, [(source, source + steps) for source in range(i...  4.65 us
    pallas_call x1, Pallas kernels, pack_rest(): pl.pallas_call(kernel, in_specs=[pl.BlockSpec(memory_space=pl.ANY)] + [vm...  2.69 us
    pallas_call x1, Pallas kernels, momentum_of(): pl.pallas_call(functools.partial(momentum_kernel, count), in_specs=[vmem(...  2.16 us
    unnamed x16, local copies, waits for them, and re-layouts  1.93 us
  transfers between devices with their start and end apart: 14, of which 7 were waited for; matrix products, arithmetic and copies ran while one was open for 0% of the time, Pallas kernels for 16%

profile of v5, /device:TPU:1, one launch (start us, length us, event | category | flops | bytes accessed | tf_op | source)
XLA Modules:
  0.0 74.3 jit_solution(11208373177653852419)
XLA Ops:
  0.6 0.0 copy-start
  0.6 1.9 %copy-done = bf16[12,32,2,2048]{3,2,1,0:T(2,128)(2,1)S(1)} copy-done((bf16[12,32,2,2048]{3,2,1,0:T(2,128)(2,1)S(1)}, bf16[12,32,2,2048]{3,2,1,0:T(2,128)(2,1)}, u32[]{:S(2)}) %copy-start) | copy-done | bytes 3145752
  2.5 0.5 shard_map.97
  3.1 2.1 %collective-permute-start.1 = (bf16[6,4,32,2,128]{4,3,2,1,0:T(2,128)(2,1)S(1)}, bf16[6,4,32,2,128]{4,3,2,1,0:T(2,128)(2,1)S(1)}, u32[]{:S(2)}, u32[]{:S(2)}) collective-permute-start(bf16[6,4,32,2,128]{4,3,2,1,0:T(2,128)(2,1)S(1)} %shard_map.97), channel_id=1, source_target_pairs={{0,16},{8,24},{16,0},{24,8},{1,17},{9,25},{17,1},{25,9},{2,18},{10... | collective-permute-start | bytes 1179656 | tf_op jit(solution)/shard_map/ppermute | solution.py:51
  5.2 0.5 shard_map.98
  5.7 0.0 copy-start.3
  5.7 0.0 copy-start.4
  5.8 1.2 %collective-permute-start.2 = (bf16[6,4,32,2,128]{4,3,2,1,0:T(2,128)(2,1)S(1)}, bf16[6,4,32,2,128]{4,3,2,1,0:T(2,128)(2,1)S(1)}, u32[]{:S(2)}, u32[]{:S(2)}) collective-permute-start(bf16[6,4,32,2,128]{4,3,2,1,0:T(2,128)(2,1)S(1)} %shard_map.98), channel_id=1, source_target_pairs={{0,24},{8,16},{16,8},{24,0},{1,25},{9,17},{17,9},{25,1},{2,26},{10... | collective-permute-start | bytes 1179656 | tf_op jit(solution)/shard_map/ppermute | solution.py:51
  7.0 0.5 shard_map.96
  7.5 0.2 collective-permute-start
  7.7 0.0 copy-done.3
  7.7 0.0 copy-done.4
  7.7 2.7 %shard_map.95 = (bf16[6,4,32,2,128]{4,3,2,1,0:T(2,128)(2,1)S(1)}, bf16[6,4,32,2,128]{4,3,2,1,0:T(2,128)(2,1)S(1)}, bf16[6,4,32,2,128]{4,3,2,1,0:T(2,128)(2,1)S(1...) custom-call(bf16[12,32,2,2048]{3,2,1,0:T(2,128)(2,1)S(1)} %copy-done, ...), custom_call_target="tpu_custom_call" | custom-call | flops 1024 | bytes 1024 | tf_op jit(solution)/shard_map/pallas_call | solution.py:142
  10.4 0.0 copy-start.1
  10.4 0.0 copy-start.2
  10.4 0.0 copy-start.5
  10.4 0.0 copy-start.6
  10.4 12.0 %collective-permute-done.1 = bf16[6,4,32,2,128]{4,3,2,1,0:T(2,128)(2,1)S(1)} collective-permute-done((bf16[6,4,32,2,128]{4,3,2,1,0:T(2,128)(2,1)S(1)}, bf16[6,4,32,2,128]{4,3,2,1,0:T(2,128)(2,1)S(1)}, u32[]{:S(2)}, u32[]{:S(2)}) %collective-permute-start.1) | collective-permute-done | bytes 393248 | tf_op jit(solution)/shard_map/ppermute | solution.py:51
  22.5 0.0 collective-permute-done.2
  22.5 1.6 %collective-permute-done = bf16[6,4,32,2,128]{4,3,2,1,0:T(2,128)(2,1)S(1)} collective-permute-done((bf16[6,4,32,2,128]{4,3,2,1,0:T(2,128)(2,1)S(1)}, bf16[6,4,32,2,128]{4,3,2,1,0:T(2,128)(2,1)S(1)}, u32[]{:S(2)}, u32[]{:S(2)}) %collective-permute-start) | collective-permute-done | bytes 393248 | tf_op jit(solution)/shard_map/ppermute | solution.py:51
  24.1 1.4 %shard_map.99 = (bf16[4,4,64,128]{3,2,1,0:T(8,128)(2,1)S(1)}, bf16[4,4,64,128]{3,2,1,0:T(8,128)(2,1)S(1)}, bf16[4,4,64,128]{3,2,1,0:T(8,128)(2,1)S(1)}, bf16[4,4...) custom-call(bf16[6,4,64,128]{3,2,1,0:T(8,128)(2,1)S(1)} %bitcast.27, bf16[6,4,64,128]{3,2,1,0:T(8,128)(2,1)S(1)} %bitcast.26, ...), custom_call_target="tpu_custom_call" | custom-call | flops 1024 | bytes 1024 | tf_op jit(solution)/shard_map/pallas_call | solution.py:211
  25.5 1.1 %collective-permute-start.3 = (bf16[4,4,64,128]{3,2,1,0:T(8,128)(2,1)S(1)}, bf16[4,4,64,128]{3,2,1,0:T(8,128)(2,1)S(1)}, u32[]{:S(2)}, u32[]{:S(2)}) collective-permute-start(bf16[4,4,64,128]{3,2,1,0:T(8,128)(2,1)S(1)} %get-tuple-element.36), channel_id=1, source_target_pairs={{0,8},{8,0},{16,24},{24,16},{1,9},{9,1},{17,25},{25,17},{2,10},{10... | collective-permute-start | bytes 786440 | tf_op jit(solution)/shard_map/ppermute | solution.py:51
  26.7 1.2 %collective-permute-start.4 = (bf16[4,4,64,128]{3,2,1,0:T(8,128)(2,1)S(1)}, bf16[4,4,64,128]{3,2,1,0:T(8,128)(2,1)S(1)}, u32[]{:S(2)}, u32[]{:S(2)}) collective-permute-start(bf16[4,4,64,128]{3,2,1,0:T(8,128)(2,1)S(1)} %get-tuple-element.42), channel_id=1, source_target_pairs={{0,16},{8,24},{16,0},{24,8},{1,17},{9,25},{17,1},{25,9},{2,18},{10... | collective-permute-start | bytes 786440 | tf_op jit(solution)/shard_map/ppermute | solution.py:51
  27.9 0.3 collective-permute-start.5
  28.2 3.7 %collective-permute-done.3.refs_1_ = bf16[4,4,64,128]{3,2,1,0:T(8,128)(2,1)S(1)} collective-permute-done((bf16[4,4,64,128]{3,2,1,0:T(8,128)(2,1)S(1)}, bf16[4,4,64,128]{3,2,1,0:T(8,128)(2,1)S(1)}, u32[]{:S(2)}, u32[]{:S(2)}) %collective-permute-start.3) | collective-permute-done | bytes 262176 | tf_op jit(solution)/shard_map/ppermute | solution.py:51
  31.9 0.8 %collective-permute-start.8 = (bf16[6,4,32,2,128]{4,3,2,1,0:T(2,128)(2,1)S(1)}, bf16[6,4,32,2,128]{4,3,2,1,0:T(2,128)(2,1)S(1)}, u32[]{:S(2)}, u32[]{:S(2)}) collective-permute-start(bf16[6,4,32,2,128]{4,3,2,1,0:T(2,128)(2,1)S(1)} %get-tuple-element.48), channel_id=1, source_target_pairs={{0,8},{8,0},{16,24},{24,16},{1,9},{9,1},{17,25},{25,17},{2,10},{10... | collective-permute-start | bytes 1179656 | tf_op jit(solution)/shard_map/ppermute | solution.py:51
  32.6 1.2 %collective-permute-start.9 = (bf16[6,4,32,2,128]{4,3,2,1,0:T(2,128)(2,1)S(1)}, bf16[6,4,32,2,128]{4,3,2,1,0:T(2,128)(2,1)S(1)}, u32[]{:S(2)}, u32[]{:S(2)}) collective-permute-start(bf16[6,4,32,2,128]{4,3,2,1,0:T(2,128)(2,1)S(1)} %get-tuple-element.49), channel_id=1, source_target_pairs={{0,16},{8,24},{16,0},{24,8},{1,17},{9,25},{17,1},{25,9},{2,18},{10... | collective-permute-start | bytes 1179656 | tf_op jit(solution)/shard_map/ppermute | solution.py:51
  33.8 0.7 collective-permute-start.10
  34.5 0.0 collective-permute-done.4.refs_2_
  34.5 3.5 %collective-permute-done.5.refs_3_ = bf16[4,4,64,128]{3,2,1,0:T(8,128)(2,1)S(1)} collective-permute-done((bf16[4,4,64,128]{3,2,1,0:T(8,128)(2,1)S(1)}, bf16[4,4,64,128]{3,2,1,0:T(8,128)(2,1)S(1)}, u32[]{:S(2)}, u32[]{:S(2)}) %collective-permute-start.5) | collective-permute-done | bytes 262176 | tf_op jit(solution)/shard_map/ppermute | solution.py:51
  38.0 1.2 %shard_map.100 = (bf16[4,2,64,128]{3,2,1,0:T(8,128)(2,1)S(1)}, bf16[4,2,64,128]{3,2,1,0:T(8,128)(2,1)S(1)}) custom-call(bf16[4,4,64,128]{3,2,1,0:T(8,128)(2,1)S(1)} %get-tuple-element.35.refs_0_, bf16[4,4,64,128]{3,2,1,0:T(8,128)(2,1)S(1)} %collective-permute-done.3.refs_1_, bf16[4,4,64,128]{3,2,1,0:T(8,128)(2,1)S(1)} %collective-permute-done.4.refs_2_, ...), custom_call_target="tpu_custom_call" | custom-call | flops 1024 | bytes 1024 | tf_op jit(solution)/shard_map/pallas_call | solution.py:308
  39.3 8.2 %collective-permute-start.6 = (bf16[4,2,64,128]{3,2,1,0:T(8,128)(2,1)S(1)}, bf16[4,2,64,128]{3,2,1,0:T(8,128)(2,1)S(1)}, u32[]{:S(2)}, u32[]{:S(2)}) collective-permute-start(bf16[4,2,64,128]{3,2,1,0:T(8,128)(2,1)S(1)} %get-tuple-element.44), channel_id=1, source_target_pairs={{0,1},{1,2},{2,3},{3,4},{4,5},{5,6},{6,7},{8,9},{9,10},{10,11},{11... | collective-permute-start | bytes 393224 | tf_op jit(solution)/shard_map/ppermute | solution.py:58
  47.4 1.9 %collective-permute-start.7 = (bf16[4,2,64,128]{3,2,1,0:T(8,128)(2,1)S(1)}, bf16[4,2,64,128]{3,2,1,0:T(8,128)(2,1)S(1)}, u32[]{:S(2)}, u32[]{:S(2)}) collective-permute-start(bf16[4,2,64,128]{3,2,1,0:T(8,128)(2,1)S(1)} %get-tuple-element.45), channel_id=1, source_target_pairs={{1,0},{2,1},{3,2},{4,3},{5,4},{6,5},{7,6},{9,8},{10,9},{11,10},{12... | collective-permute-start | bytes 393224 | tf_op jit(solution)/shard_map/ppermute | solution.py:58
  49.4 0.0 collective-permute-done.6.refs_4_
  49.4 4.6 %collective-permute-done.7.refs_5_ = bf16[4,2,64,128]{3,2,1,0:T(8,128)(2,1)S(1)} collective-permute-done((bf16[4,2,64,128]{3,2,1,0:T(8,128)(2,1)S(1)}, bf16[4,2,64,128]{3,2,1,0:T(8,128)(2,1)S(1)}, u32[]{:S(2)}, u32[]{:S(2)}) %collective-permute-start.7) | collective-permute-done | bytes 131104 | tf_op jit(solution)/shard_map/ppermute | solution.py:58
  54.0 0.0 copy-done.6
  54.0 6.6 %shard_map.101 = (f32[3072,128]{1,0:T(8,128)}, f32[3,16,64,128]{3,2,1,0:T(8,128)S(1)}) custom-call(bf16[4,4,64,128]{3,2,1,0:T(8,128)(2,1)S(1)} %get-tuple-element.35.refs_0_, bf16[4,4,64,128]{3,2,1,0:T(8,128)(2,1)S(1)} %collective-permute-done.3.refs_1_, bf16[4,4,64,128]{3,2,1,0:T(8,128)(2,1)S(1)} %collective-permute-done.4.refs_2_, ...), custom_call_target="tpu_custom_call" | custom-call | flops 1024 | bytes 1024 | tf_op jit(solution)/shard_map/pallas_call | solution.py:389
  60.6 0.0 collective-permute-done.8
  60.6 0.0 collective-permute-done.9
  60.6 0.0 collective-permute-done.10
  60.6 1.6 %shard_map.102 = (bf16[3,4,64,128]{3,2,1,0:T(8,128)(2,1)S(1)}, bf16[3,4,64,128]{3,2,1,0:T(8,128)(2,1)S(1)}, bf16[3,4,64,128]{3,2,1,0:T(8,128)(2,1)S(1)}, bf16[3,4,64,128]{3,2,1,0:T(8,128)(2,1)S(1)}) custom-call(bf16[6,4,64,128]{3,2,1,0:T(8,128)(2,1)S(1)} %bitcast.20, bf16[6,4,64,128]{3,2,1,0:T(8,128)(2,1)S(1)} %bitcast.21, ...), custom_call_target="tpu_custom_call" | custom-call | flops 1024 | bytes 1024 | tf_op jit(solution)/shard_map/pallas_call | solution.py:258
  62.2 1.3 %collective-permute-start.11 = (bf16[3,4,64,128]{3,2,1,0:T(8,128)(2,1)S(1)}, bf16[3,4,64,128]{3,2,1,0:T(8,128)(2,1)S(1)}, u32[]{:S(2)}, u32[]{:S(2)}) collective-permute-start(bf16[3,4,64,128]{3,2,1,0:T(8,128)(2,1)S(1)} %get-tuple-element.58), channel_id=1, source_target_pairs={{0,8},{8,0},{16,24},{24,16},{1,9},{9,1},{17,25},{25,17},{2,10},{10... | collective-permute-start | bytes 589832 | tf_op jit(solution)/shard_map/ppermute | solution.py:51
  63.5 0.2 collective-permute-start.12
  63.7 1.2 %collective-permute-start.13 = (bf16[3,4,64,128]{3,2,1,0:T(8,128)(2,1)S(1)}, bf16[3,4,64,128]{3,2,1,0:T(8,128)(2,1)S(1)}, u32[]{:S(2)}, u32[]{:S(2)}) collective-permute-start(bf16[3,4,64,128]{3,2,1,0:T(8,128)(2,1)S(1)} %get-tuple-element.60), channel_id=1, source_target_pairs={{0,24},{8,16},{16,8},{24,0},{1,25},{9,17},{17,9},{25,1},{2,26},{10... | collective-permute-start | bytes 589832 | tf_op jit(solution)/shard_map/ppermute | solution.py:51
  64.9 4.0 %collective-permute-done.11.refs_1_ = bf16[3,4,64,128]{3,2,1,0:T(8,128)(2,1)S(1)} collective-permute-done((bf16[3,4,64,128]{3,2,1,0:T(8,128)(2,1)S(1)}, bf16[3,4,64,128]{3,2,1,0:T(8,128)(2,1)S(1)}, u32[]{:S(2)}, u32[]{:S(2)}) %collective-permute-start.11) | collective-permute-done | bytes 196640 | tf_op jit(solution)/shard_map/ppermute | solution.py:51
  68.9 3.2 %collective-permute-done.12.refs_2_ = bf16[3,4,64,128]{3,2,1,0:T(8,128)(2,1)S(1)} collective-permute-done((bf16[3,4,64,128]{3,2,1,0:T(8,128)(2,1)S(1)}, bf16[3,4,64,128]{3,2,1,0:T(8,128)(2,1)S(1)}, u32[]{:S(2)}, u32[]{:S(2)}) %collective-permute-start.12) | collective-permute-done | bytes 196640 | tf_op jit(solution)/shard_map/ppermute | solution.py:51
  72.1 0.0 collective-permute-done.13.refs_3_
  72.1 2.2 %shard_map.103 = f32[3072,128]{1,0:T(8,128)} custom-call(bf16[3,4,64,128]{3,2,1,0:T(8,128)(2,1)S(1)} %get-tuple-element.57.refs_0_, bf16[3,4,64,128]{3,2,1,0:T(8,128)(2,1)S(1)} %collective-permute-done.11.refs_1_, bf16[3,4,64,128]{3,2,1,0:T(8,128)(2,1)S(1)} %collective-permute-done.12.refs_2_, bf16[3,4,64,128]{3,2,1,0:T(8,128)(2,1)S(1)} %collective-permute-done.13.refs_3_, ...), custom_call_target="tpu_custom_call" | custom-call | flops 1024 | bytes 1024 | tf_op jit(solution)/shard_map/pallas_call | solution.py:432
  (5 shorter events, 0.0 us)
Async XLA Ops:
  0.6 1.9 %copy-start = (bf16[12,32,2,2048]{3,2,1,0:T(2,128)(2,1)S(1)}, bf16[12,32,2,2048]{3,2,1,0:T(2,128)(2,1)}, u32[]{:S(2)}) copy-start(bf16[12,32,2,2048]{3,2,1,0:T(2,128)(2,1)} %fields_ref.7) | copy-start | bytes 9437188
  3.1 19.4 %collective-permute-start.1 = (bf16[6,4,32,2,128]{4,3,2,1,0:T(2,128)(2,1)S(1)}, bf16[6,4,32,2,128]{4,3,2,1,0:T(2,128)(2,1)S(1)}, u32[]{:S(2)}, u32[]{:S(2)}) collective-permute-start(bf16[6,4,32,2,128]{4,3,2,1,0:T(2,128)(2,1)S(1)} %shard_map.97), channel_id=1, source_target_pairs={{0,16},{8,24},{16,0},{24,8},{1,17},{9,25},{17,1},{25,9},{2,18},{10... | collective-permute-start | bytes 1179656 | tf_op jit(solution)/shard_map/ppermute | solution.py:51
  5.7 1.9 %copy-start.3 = (bf16[256,256]{1,0:T(8,128)(2,1)S(1)}, bf16[256,256]{1,0:T(8,128)(2,1)}, u32[]{:S(2)}) copy-start(bf16[256,256]{1,0:T(8,128)(2,1)} %constant.5.clone.refs_1_) | copy-start | bytes 393220
  5.7 1.9 %copy-start.4 = (bf16[256,256]{1,0:T(8,128)(2,1)S(1)}, bf16[256,256]{1,0:T(8,128)(2,1)}, u32[]{:S(2)}) copy-start(bf16[256,256]{1,0:T(8,128)(2,1)} %constant.4.clone.refs_0_) | copy-start | bytes 393220
  5.8 16.7 %collective-permute-start.2 = (bf16[6,4,32,2,128]{4,3,2,1,0:T(2,128)(2,1)S(1)}, bf16[6,4,32,2,128]{4,3,2,1,0:T(2,128)(2,1)S(1)}, u32[]{:S(2)}, u32[]{:S(2)}) collective-permute-start(bf16[6,4,32,2,128]{4,3,2,1,0:T(2,128)(2,1)S(1)} %shard_map.98), channel_id=1, source_target_pairs={{0,24},{8,16},{16,8},{24,0},{1,25},{9,17},{17,9},{25,1},{2,26},{10... | collective-permute-start | bytes 1179656 | tf_op jit(solution)/shard_map/ppermute | solution.py:51
  7.5 16.6 %collective-permute-start = (bf16[6,4,32,2,128]{4,3,2,1,0:T(2,128)(2,1)S(1)}, bf16[6,4,32,2,128]{4,3,2,1,0:T(2,128)(2,1)S(1)}, u32[]{:S(2)}, u32[]{:S(2)}) collective-permute-start(bf16[6,4,32,2,128]{4,3,2,1,0:T(2,128)(2,1)S(1)} %shard_map.96), channel_id=1, source_target_pairs={{0,8},{8,0},{16,24},{24,16},{1,9},{9,1},{17,25},{25,17},{2,10},{10... | collective-permute-start | bytes 1179656 | tf_op jit(solution)/shard_map/ppermute | solution.py:51
  7.7 30.3 %copy-start.7 = (s32[2,256]{1,0:T(2,128)S(1)}, s32[2,256]{1,0:T(2,128)}, u32[]{:S(2)}) copy-start(s32[2,256]{1,0:T(2,128)} %refs_4_.1) | copy-start | bytes 6148
  10.4 43.6 %copy-start.1 = (bf16[5,64,2048]{2,1,0:T(8,128)(2,1)S(1)}, bf16[5,64,2048]{2,1,0:T(8,128)(2,1)}, u32[]{:S(2)}) copy-start(bf16[5,64,2048]{2,1,0:T(8,128)(2,1)} %refs_6_.1) | copy-start | bytes 3932164
  10.4 43.6 %copy-start.2 = (bf16[5,64,2048]{2,1,0:T(8,128)(2,1)S(1)}, bf16[5,64,2048]{2,1,0:T(8,128)(2,1)}, u32[]{:S(2)}) copy-start(bf16[5,64,2048]{2,1,0:T(8,128)(2,1)} %refs_7_.1) | copy-start | bytes 3932164
  10.4 43.6 %copy-start.5 = (f32[2048]{0:T(1024)S(1)}, f32[2048]{0:T(1024)}, u32[]{:S(2)}) copy-start(f32[2048]{0:T(1024)} %param.9) | copy-start | bytes 24580
  10.4 43.6 %copy-start.6 = (s32[32,5]{0,1:T(8,128)S(1)}, s32[32,5]{0,1:T(8,128)}, u32[]{:S(2)}) copy-start(s32[32,5]{0,1:T(8,128)} %param.12) | copy-start | bytes 1924
  25.5 6.4 %collective-permute-start.3 = (bf16[4,4,64,128]{3,2,1,0:T(8,128)(2,1)S(1)}, bf16[4,4,64,128]{3,2,1,0:T(8,128)(2,1)S(1)}, u32[]{:S(2)}, u32[]{:S(2)}) collective-permute-start(bf16[4,4,64,128]{3,2,1,0:T(8,128)(2,1)S(1)} %get-tuple-element.36), channel_id=1, source_target_pairs={{0,8},{8,0},{16,24},{24,16},{1,9},{9,1},{17,25},{25,17},{2,10},{10... | collective-permute-start | bytes 786440 | tf_op jit(solution)/shard_map/ppermute | solution.py:51
  26.7 7.9 %collective-permute-start.4 = (bf16[4,4,64,128]{3,2,1,0:T(8,128)(2,1)S(1)}, bf16[4,4,64,128]{3,2,1,0:T(8,128)(2,1)S(1)}, u32[]{:S(2)}, u32[]{:S(2)}) collective-permute-start(bf16[4,4,64,128]{3,2,1,0:T(8,128)(2,1)S(1)} %get-tuple-element.42), channel_id=1, source_target_pairs={{0,16},{8,24},{16,0},{24,8},{1,17},{9,25},{17,1},{25,9},{2,18},{10... | collective-permute-start | bytes 786440 | tf_op jit(solution)/shard_map/ppermute | solution.py:51
  27.9 10.1 %collective-permute-start.5 = (bf16[4,4,64,128]{3,2,1,0:T(8,128)(2,1)S(1)}, bf16[4,4,64,128]{3,2,1,0:T(8,128)(2,1)S(1)}, u32[]{:S(2)}, u32[]{:S(2)}) collective-permute-start(bf16[4,4,64,128]{3,2,1,0:T(8,128)(2,1)S(1)} %get-tuple-element.43), channel_id=1, source_target_pairs={{0,24},{8,16},{16,8},{24,0},{1,25},{9,17},{17,9},{25,1},{2,26},{10... | collective-permute-start | bytes 786440 | tf_op jit(solution)/shard_map/ppermute | solution.py:51
  31.9 28.7 %collective-permute-start.8 = (bf16[6,4,32,2,128]{4,3,2,1,0:T(2,128)(2,1)S(1)}, bf16[6,4,32,2,128]{4,3,2,1,0:T(2,128)(2,1)S(1)}, u32[]{:S(2)}, u32[]{:S(2)}) collective-permute-start(bf16[6,4,32,2,128]{4,3,2,1,0:T(2,128)(2,1)S(1)} %get-tuple-element.48), channel_id=1, source_target_pairs={{0,8},{8,0},{16,24},{24,16},{1,9},{9,1},{17,25},{25,17},{2,10},{10... | collective-permute-start | bytes 1179656 | tf_op jit(solution)/shard_map/ppermute | solution.py:51
  32.6 28.0 %collective-permute-start.9 = (bf16[6,4,32,2,128]{4,3,2,1,0:T(2,128)(2,1)S(1)}, bf16[6,4,32,2,128]{4,3,2,1,0:T(2,128)(2,1)S(1)}, u32[]{:S(2)}, u32[]{:S(2)}) collective-permute-start(bf16[6,4,32,2,128]{4,3,2,1,0:T(2,128)(2,1)S(1)} %get-tuple-element.49), channel_id=1, source_target_pairs={{0,16},{8,24},{16,0},{24,8},{1,17},{9,25},{17,1},{25,9},{2,18},{10... | collective-permute-start | bytes 1179656 | tf_op jit(solution)/shard_map/ppermute | solution.py:51
  33.8 26.8 %collective-permute-start.10 = (bf16[6,4,32,2,128]{4,3,2,1,0:T(2,128)(2,1)S(1)}, bf16[6,4,32,2,128]{4,3,2,1,0:T(2,128)(2,1)S(1)}, u32[]{:S(2)}, u32[]{:S(2)}) collective-permute-start(bf16[6,4,32,2,128]{4,3,2,1,0:T(2,128)(2,1)S(1)} %get-tuple-element.50), channel_id=1, source_target_pairs={{0,24},{8,16},{16,8},{24,0},{1,25},{9,17},{17,9},{25,1},{2,26},{10... | collective-permute-start | bytes 1179656 | tf_op jit(solution)/shard_map/ppermute | solution.py:51
  39.3 10.1 %collective-permute-start.6 = (bf16[4,2,64,128]{3,2,1,0:T(8,128)(2,1)S(1)}, bf16[4,2,64,128]{3,2,1,0:T(8,128)(2,1)S(1)}, u32[]{:S(2)}, u32[]{:S(2)}) collective-permute-start(bf16[4,2,64,128]{3,2,1,0:T(8,128)(2,1)S(1)} %get-tuple-element.44), channel_id=1, source_target_pairs={{0,1},{1,2},{2,3},{3,4},{4,5},{5,6},{6,7},{8,9},{9,10},{10,11},{11... | collective-permute-start | bytes 393224 | tf_op jit(solution)/shard_map/ppermute | solution.py:58
  47.4 6.6 %collective-permute-start.7 = (bf16[4,2,64,128]{3,2,1,0:T(8,128)(2,1)S(1)}, bf16[4,2,64,128]{3,2,1,0:T(8,128)(2,1)S(1)}, u32[]{:S(2)}, u32[]{:S(2)}) collective-permute-start(bf16[4,2,64,128]{3,2,1,0:T(8,128)(2,1)S(1)} %get-tuple-element.45), channel_id=1, source_target_pairs={{1,0},{2,1},{3,2},{4,3},{5,4},{6,5},{7,6},{9,8},{10,9},{11,10},{12... | collective-permute-start | bytes 393224 | tf_op jit(solution)/shard_map/ppermute | solution.py:58
  62.2 6.7 %collective-permute-start.11 = (bf16[3,4,64,128]{3,2,1,0:T(8,128)(2,1)S(1)}, bf16[3,4,64,128]{3,2,1,0:T(8,128)(2,1)S(1)}, u32[]{:S(2)}, u32[]{:S(2)}) collective-permute-start(bf16[3,4,64,128]{3,2,1,0:T(8,128)(2,1)S(1)} %get-tuple-element.58), channel_id=1, source_target_pairs={{0,8},{8,0},{16,24},{24,16},{1,9},{9,1},{17,25},{25,17},{2,10},{10... | collective-permute-start | bytes 589832 | tf_op jit(solution)/shard_map/ppermute | solution.py:51
  63.5 8.6 %collective-permute-start.12 = (bf16[3,4,64,128]{3,2,1,0:T(8,128)(2,1)S(1)}, bf16[3,4,64,128]{3,2,1,0:T(8,128)(2,1)S(1)}, u32[]{:S(2)}, u32[]{:S(2)}) collective-permute-start(bf16[3,4,64,128]{3,2,1,0:T(8,128)(2,1)S(1)} %get-tuple-element.59), channel_id=1, source_target_pairs={{0,16},{8,24},{16,0},{24,8},{1,17},{9,25},{17,1},{25,9},{2,18},{10... | collective-permute-start | bytes 589832 | tf_op jit(solution)/shard_map/ppermute | solution.py:51
  63.7 8.4 %collective-permute-start.13 = (bf16[3,4,64,128]{3,2,1,0:T(8,128)(2,1)S(1)}, bf16[3,4,64,128]{3,2,1,0:T(8,128)(2,1)S(1)}, u32[]{:S(2)}, u32[]{:S(2)}) collective-permute-start(bf16[3,4,64,128]{3,2,1,0:T(8,128)(2,1)S(1)} %get-tuple-element.60), channel_id=1, source_target_pairs={{0,24},{8,16},{16,8},{24,0},{1,25},{9,17},{17,9},{25,1},{2,26},{10... | collective-permute-start | bytes 589832 | tf_op jit(solution)/shard_map/ppermute | solution.py:51

commit v6 on v5

--- a/solution.py
+++ b/solution.py
@@ -42,14 +42,15 @@
     return lax.rem(me + count - step, count)
 
 
+def send(piece, step):
+    count = lax.axis_size("mode")
+    power = count & (count - 1) == 0
+    pairs = [(i, i ^ step if power else (i + step) % count) for i in range(count)]
+    return lax.ppermute(piece, "mode", pairs)
+
+
 def exchange(pieces):
-    count = len(pieces) + 1
-    power = count & (count - 1) == 0
-    received = []
-    for step in range(1, count):
-        pairs = [(i, i ^ step if power else (i + step) % count) for i in range(count)]
-        received.append(lax.ppermute(pieces[step - 1], "mode", pairs))
-    return received
+    return [send(piece, step) for step, piece in enumerate(pieces, 1)]
 
 
 def from_behind(value, axis, steps):
@@ -74,7 +75,7 @@
 
 
 def groups_of(tiles):
-    return 1
+    return 2 if tiles % 2 == 0 else 1
 
 
 def pieces_of(fields_ref, first, share, group, out_ref):
@@ -123,30 +124,26 @@
     )(fields)
 
 
-def pack_rest(fields, middle, groups, carried):
+def pack_rest(fields, parcels, carried):
     count = lax.axis_size("mode")
-    shape = packed_shape(fields, 0, middle, groups)
-    full = packed_shape(fields, middle, fields.shape[0], 1)
+    shapes = [packed_shape(fields, first, last, groups) for first, last, _, _, groups in parcels]
 
     def kernel(fields_ref, *refs):
         inputs, refs = refs[: len(carried)], refs[len(carried) :]
-        own_refs, share_refs, outputs = refs[:groups], refs[groups : groups + count], refs[groups + count : -1]
+        parcel_refs, outputs = refs[: len(parcels)], refs[len(parcels) : -1]
         me = lax.axis_index("mode")
         pairs = []
-        for group in range(groups):
-            pairs += pieces_of(fields_ref, 0, me, group, own_refs[group])
-        for step in range(count):
-            pairs += pieces_of(fields_ref, middle, dest_of(me, step, count), 0, share_refs[step])
+        for (first, _, step, group, _), parcel_ref in zip(parcels, parcel_refs):
+            pairs += pieces_of(fields_ref, first, dest_of(me, step, count), group, parcel_ref)
         run_copies(pairs, refs[-1], zip(inputs, outputs))
 
     return pl.pallas_call(
         kernel,
         in_specs=[pl.BlockSpec(memory_space=pl.ANY)] + [vmem()] * len(carried),
-        out_specs=[vmem()] * (groups + count + len(carried)),
-        out_shape=[jax.ShapeDtypeStruct(shape, jnp.bfloat16)] * groups
-        + [jax.ShapeDtypeStruct(full, jnp.bfloat16)] * count
+        out_specs=[vmem()] * (len(parcels) + len(carried)),
+        out_shape=[jax.ShapeDtypeStruct(shape, jnp.bfloat16) for shape in shapes]
         + [jax.ShapeDtypeStruct(value.shape, value.dtype) for value in carried],
-        scratch_shapes=[pltpu.SemaphoreType.DMA((groups * shape[0] * shape[1] + count * full[0] * full[1],))],
+        scratch_shapes=[pltpu.SemaphoreType.DMA((sum(shape[0] * shape[1] for shape in shapes),))],
         compiler_params=params(),
         cost_estimate=cost(),
     )(fields, *carried)
@@ -156,10 +153,11 @@
     return [a[1] * b[2] - a[2] * b[1], a[2] * b[0] - a[0] * b[2], a[0] * b[1] - a[1] * b[0]]
 
 
-def to_physical(sources, in_refs, inverse, x_ref, store):
+def to_physical(count, in_refs, inverse, x_ref, store):
+    me = lax.axis_index("mode")
     components, tiles, rows, _ = in_refs[0].shape
-    for step, source in enumerate(sources):
-        at = pl.multiple_of(source * rows, rows)
+    for step in range(count):
+        at = pl.multiple_of(source_of(me, step, count) * rows, rows)
         for c in range(components):
             for t in range(tiles):
                 x_ref[c, pl.ds(at, rows), t * LANES : (t + 1) * LANES] = in_refs[step][c, t]
@@ -191,9 +189,7 @@
     def store(c, value):
         physical_ref[c] = value
 
-    me = lax.axis_index("mode")
-    sources = [source_of(me, step, count) for step in range(count)]
-    to_physical(sources, in_refs, inverse_ref[...], x_ref, store)
+    to_physical(count, in_refs, inverse_ref[...], x_ref, store)
     for i in range(THETA // CHUNK):
         at = slice(i * CHUNK, (i + 1) * CHUNK)
         velocity = [physical_ref[c, at] for c in range(3)]
@@ -233,9 +229,7 @@
     def store(c, value):
         physical_ref[c] = value
 
-    me = lax.axis_index("mode")
-    sources = [source_of(me, step, count) for step in range(count)]
-    to_physical(sources, in_refs, inverse_ref[...], x_ref, store)
+    to_physical(count, in_refs, inverse_ref[...], x_ref, store)
     for group in range(groups):
         lanes = slice(group * width, (group + 1) * width)
         for i in range(THETA // CHUNK):
@@ -251,9 +245,8 @@
 
 
 def second_physics(received, physical, inverse, forward):
-    count = len(received)
+    count, groups = len(received), len(physical)
     components, tiles, rows, _ = received[0].shape
-    groups = len(physical)
     width = tiles * LANES
     return pl.pallas_call(
         functools.partial(second_kernel, count, groups),
@@ -400,24 +393,50 @@
     )(*received, from_prev, from_next, radial_blocks, axial_blocks, radius, columns)
 
 
-def momentum_kernel(count, *refs):
-    in_refs, (gradient_ref, out_ref, total_ref, sems) = refs[:count], refs[count:]
+SUBLANES = 8
+
+
+def interleaved(parts):
+    parts = list(parts)
+    row = lax.broadcasted_iota(jnp.int32, parts[0].shape, 1)
+    for distance in (1, 2, 4):
+        upper = jnp.bitwise_and(row, distance) != 0
+        for k in range(SUBLANES):
+            if k & distance == 0:
+                first, second = parts[k], parts[k + distance]
+                parts[k] = jnp.where(upper, pltpu.roll(second, distance, 1), first)
+                parts[k + distance] = jnp.where(upper, second, pltpu.roll(first, SUBLANES - distance, 1))
+    return parts
+
+
+def momentum_kernel(count, arrived, *refs):
+    in_refs, (gradient_ref, out_ref, total_ref, sems) = refs[:arrived], refs[arrived:]
     me = lax.axis_index("mode")
-    components, tiles, rows, _ = in_refs[0].shape
+    components, held, rows, _ = in_refs[0].shape
     mode_count = rows // 2
+    tiles = arrived // count * held
     stride = 2 * count * tiles
     out_rows = mode_count * stride
     copies = []
     for c in range(components):
         for step in range(count):
             share = source_of(me, step, count)
-            for t in range(tiles):
-                at = share * tiles + t
-                value = in_refs[step][c, t].astype(jnp.float32) - gradient_ref[c, at]
-                for p in range(2):
-                    total_ref[pl.ds(c * out_rows + 2 * at + p, mode_count, stride=stride), :] = value[
-                        p * mode_count : (p + 1) * mode_count
-                    ]
+            for start in range(0, tiles, SUBLANES // 2):
+                parts = []
+                for t in range(start, min(tiles, start + SUBLANES // 2)):
+                    at = share * tiles + t
+                    piece_ref = in_refs[t // held * count + step]
+                    value = piece_ref[c, t % held].astype(jnp.float32) - gradient_ref[c, at]
+                    parts += [value[:mode_count], value[mode_count:]]
+                first = c * out_rows + 2 * (share * tiles + start)
+                if len(parts) == SUBLANES:
+                    whole = interleaved([part.reshape(mode_count // SUBLANES, SUBLANES, LANES) for part in parts])
+                    for mode in range(mode_count):
+                        here = pl.ds(pl.multiple_of(first + mode * stride, SUBLANES), SUBLANES)
+                        total_ref[here, :] = whole[mode % SUBLANES][mode // SUBLANES]
+                else:
+                    for i, part in enumerate(parts):
+                        total_ref[pl.ds(first + i, mode_count, stride=stride), :] = part
         done = pl.ds(c * out_rows, out_rows)
         copies.append(pltpu.make_async_copy(total_ref.at[done], out_ref.at[done], sems.at[c]))
         copies[c].start()
@@ -425,13 +444,12 @@
         copy.wait()
 
 
-def momentum_of(received, gradient):
-    count = len(received)
-    components, tiles, rows, _ = received[0].shape
-    shape = (components * rows * count * tiles, LANES)
-    return pl.pallas_call(
-        functools.partial(momentum_kernel, count),
-        in_specs=[vmem()] * (count + 1),
+def momentum_of(received, gradient, count):
+    components, held, rows, _ = received[0].shape
+    shape = (components * rows * len(received) * held, LANES)
+    return pl.pallas_call(
+        functools.partial(momentum_kernel, count, len(received)),
+        in_specs=[vmem()] * (len(received) + 1),
         out_specs=pl.BlockSpec(memory_space=pl.ANY),
         out_shape=jax.ShapeDtypeStruct(shape, jnp.float32),
         scratch_shapes=[pltpu.VMEM(shape, jnp.float32), pltpu.SemaphoreType.DMA((components,))],
@@ -459,27 +477,27 @@
     arrived = []
     for group in range(groups):
         arrived.append(exchange([pack(mode_fields, 0, 6, step, group, groups) for step in range(1, count)]))
-    *packed, inverse, forward = pack_rest(mode_fields, 6, groups, [inverse, forward])
+    parcels = [(0, 6, 0, group, groups) for group in range(groups)]
+    parcels += [(6, 12, step, 0, 1) for step in range(count)]
+    *packed, inverse, forward = pack_rest(mode_fields, parcels, [inverse, forward])
     own, shares = packed[:groups], packed[groups:]
     local, physical = [], []
     for group in range(groups):
         *terms, velocity_magnetic = first_physics(joined([own[group]] + arrived[group]), inverse, forward)
-        back = exchange(terms[1:])
-        if group == 0:
-            back[0], shares = lax.optimization_barrier((back[0], shares))
-            shares = shares[:1] + exchange(shares[1:])
-        local += terms[:1] + back
+        local += terms[:1] + exchange(terms[1:])
         physical.append(velocity_magnetic)
+    local, shares = lax.optimization_barrier((local, shares))
+    sources = shares[:1] + exchange(shares[1:])
     toward_prev, toward_next = interface(local, interface_nodes, count)
     from_prev = from_behind(toward_next, "mer", 1)
     from_next = from_behind(toward_prev, "mer", -1)
     induction, gradient = derive(
         local, from_prev, from_next, radial_blocks, axial_blocks, radius.reshape(1, width), block_columns.T, count
     )
-    shares, gradient = lax.optimization_barrier((shares, gradient))
-    lorentz = list(second_physics(joined(shares), physical, inverse, forward))
+    sources, gradient = lax.optimization_barrier((sources, gradient))
+    lorentz = list(second_physics(joined(sources), physical, inverse, forward))
     lorentz = lorentz[:1] + exchange(lorentz[1:])
-    momentum = momentum_of(lorentz, gradient)
+    momentum = momentum_of(lorentz, gradient, count)
     return (whole_output(induction, mode_count, width), whole_output(momentum, mode_count, width))
 
 

time: 75 us -> 72 us (0.960)
  waiting for transfers between devices: 32.6 us -> 23.4 us
  starting transfers between devices: 21.7 us -> 28.5 us
    ppermute x12 -> x18, waiting for transfers between devices: 28 us -> 18.8 us  [send(): return lax.ppermute(piece, 'mode', pairs)]
    ppermute x12 -> x18, starting transfers between devices: 11.6 us -> 20.4 us  [send(): return lax.ppermute(piece, 'mode', pairs)]
    ppermute x2, starting transfers between devices: 10.1 us -> 8.14 us  [from_behind(): lax.ppermute(value, axis, [(source, source + steps) for source in range(i...]
    pallas_call x1, Pallas kernels: 2.16 us -> 1.31 us  [momentum_of(): pl.pallas_call(functools.partial(momentum_kernel, count, len(received)),...]
    pallas_call x1 -> x2, Pallas kernels: 1.42 us -> 1.63 us  [first_physics(): pl.pallas_call(functools.partial(first_kernel, count), in_specs=[vmem()]...]
    pallas_call x3 -> x6, Pallas kernels: 1.6 us -> 1.6 us  [pack(): pl.pallas_call(kernel, in_specs=[pl.BlockSpec(memory_space=pl.ANY)], out_...]
  transfers between devices with their start and end apart: 14 -> 20, of which waited for: 7 -> 9; matrix products, arithmetic and copies ran while one was open for 0% -> 0% of each run, Pallas kernels for 16% -> 19%
where the time goes in v6:
time: 72 us; the launch traced here: 71.3 us
  starting transfers between devices  28.5 us (40%)
  waiting for transfers between devices  23.4 us (32%)
  Pallas kernels  16.6 us (23%)
  local copies, waits for them, and re-layouts  1.93 us (3%)
  between operations  0.85 us (1%)
    ppermute x18, starting transfers between devices, send(): return lax.ppermute(piece, 'mode', pairs)  20.4 us
    ppermute x18, waiting for transfers between devices, send(): return lax.ppermute(piece, 'mode', pairs)  18.8 us
    ppermute x2, starting transfers between devices, from_behind(): lax.ppermute(value, axis, [(source, source + steps) for source in range(i...  8.14 us
    pallas_call x1, Pallas kernels, derive(): pl.pallas_call(functools.partial(derive_kernel, count, len(received)), in...  6.57 us
    ppermute x2, waiting for transfers between devices, from_behind(): lax.ppermute(value, axis, [(source, source + steps) for source in range(i...  4.65 us
    pallas_call x1, Pallas kernels, pack_rest(): pl.pallas_call(kernel, in_specs=[pl.BlockSpec(memory_space=pl.ANY)] + [vm...  2.69 us
    unnamed x16, local copies, waits for them, and re-layouts  1.93 us
    pallas_call x2, Pallas kernels, first_physics(): pl.pallas_call(functools.partial(first_kernel, count), in_specs=[vmem()]...  1.63 us
  transfers between devices with their start and end apart: 20, of which 9 were waited for; matrix products, arithmetic and copies ran while one was open for 0% of the time, Pallas kernels for 19%

profile of v6, /device:TPU:1, one launch (start us, length us, event | category | flops | bytes accessed | tf_op | source)
XLA Modules:
  0.0 71.3 jit_solution(12156219026946113815)
XLA Ops:
  0.6 1.9 %copy-done = bf16[12,32,2,2048]{3,2,1,0:T(2,128)(2,1)S(1)} copy-done((bf16[12,32,2,2048]{3,2,1,0:T(2,128)(2,1)S(1)}, bf16[12,32,2,2048]{3,2,1,0:T(2,128)(2,1)}, u32[]{:S(2)}) %copy-start) | copy-done | bytes 3145752
  2.5 0.3 shard_map.101
  2.8 2.1 %collective-permute-start.7 = (bf16[6,2,32,2,128]{4,3,2,1,0:T(2,128)(2,1)S(1)}, bf16[6,2,32,2,128]{4,3,2,1,0:T(2,128)(2,1)S(1)}, u32[]{:S(2)}, u32[]{:S(2)}) collective-permute-start(bf16[6,2,32,2,128]{4,3,2,1,0:T(2,128)(2,1)S(1)} %shard_map.101), channel_id=1, source_target_pairs={{0,16},{8,24},{16,0},{24,8},{1,17},{9,25},{17,1},{25,9},{2,18},{10... | collective-permute-start | bytes 589832 | tf_op jit(solution)/shard_map/ppermute | solution.py:49
  4.9 0.3 shard_map.102
  5.2 1.2 %collective-permute-start.8 = (bf16[6,2,32,2,128]{4,3,2,1,0:T(2,128)(2,1)S(1)}, bf16[6,2,32,2,128]{4,3,2,1,0:T(2,128)(2,1)S(1)}, u32[]{:S(2)}, u32[]{:S(2)}) collective-permute-start(bf16[6,2,32,2,128]{4,3,2,1,0:T(2,128)(2,1)S(1)} %shard_map.102), channel_id=1, source_target_pairs={{0,24},{8,16},{16,8},{24,0},{1,25},{9,17},{17,9},{25,1},{2,26},{10... | collective-permute-start | bytes 589832 | tf_op jit(solution)/shard_map/ppermute | solution.py:49
  6.4 0.3 shard_map.100
  6.7 0.1 collective-permute-start.6
  6.8 0.3 shard_map.96
  7.1 1.4 %collective-permute-start = (bf16[6,2,32,2,128]{4,3,2,1,0:T(2,128)(2,1)S(1)}, bf16[6,2,32,2,128]{4,3,2,1,0:T(2,128)(2,1)S(1)}, u32[]{:S(2)}, u32[]{:S(2)}) collective-permute-start(bf16[6,2,32,2,128]{4,3,2,1,0:T(2,128)(2,1)S(1)} %shard_map.96), channel_id=1, source_target_pairs={{0,8},{8,0},{16,24},{24,16},{1,9},{9,1},{17,25},{25,17},{2,10},{10... | collective-permute-start | bytes 589832 | tf_op jit(solution)/shard_map/ppermute | solution.py:49
  8.6 0.3 shard_map.97
  8.8 0.0 copy-start.3
  8.9 0.0 copy-start.4
  8.9 1.3 %collective-permute-start.1 = (bf16[6,2,32,2,128]{4,3,2,1,0:T(2,128)(2,1)S(1)}, bf16[6,2,32,2,128]{4,3,2,1,0:T(2,128)(2,1)S(1)}, u32[]{:S(2)}, u32[]{:S(2)}) collective-permute-start(bf16[6,2,32,2,128]{4,3,2,1,0:T(2,128)(2,1)S(1)} %shard_map.97), channel_id=1, source_target_pairs={{0,16},{8,24},{16,0},{24,8},{1,17},{9,25},{17,1},{25,9},{2,18},{10... | collective-permute-start | bytes 589832 | tf_op jit(solution)/shard_map/ppermute | solution.py:49
  10.2 0.3 shard_map.98
  10.4 2.5 %collective-permute-done.7 = bf16[6,2,32,2,128]{4,3,2,1,0:T(2,128)(2,1)S(1)} collective-permute-done((bf16[6,2,32,2,128]{4,3,2,1,0:T(2,128)(2,1)S(1)}, bf16[6,2,32,2,128]{4,3,2,1,0:T(2,128)(2,1)S(1)}, u32[]{:S(2)}, u32[]{:S(2)}) %collective-permute-start.7) | collective-permute-done | bytes 196640 | tf_op jit(solution)/shard_map/ppermute | solution.py:49
  13.0 2.9 %collective-permute-start.2 = (bf16[6,2,32,2,128]{4,3,2,1,0:T(2,128)(2,1)S(1)}, bf16[6,2,32,2,128]{4,3,2,1,0:T(2,128)(2,1)S(1)}, u32[]{:S(2)}, u32[]{:S(2)}) collective-permute-start(bf16[6,2,32,2,128]{4,3,2,1,0:T(2,128)(2,1)S(1)} %shard_map.98), channel_id=1, source_target_pairs={{0,24},{8,16},{16,8},{24,0},{1,25},{9,17},{17,9},{25,1},{2,26},{10... | collective-permute-start | bytes 589832 | tf_op jit(solution)/shard_map/ppermute | solution.py:49
  15.8 2.7 %shard_map.95 = (bf16[6,2,32,2,128]{4,3,2,1,0:T(2,128)(2,1)S(1)}, bf16[6,2,32,2,128]{4,3,2,1,0:T(2,128)(2,1)S(1)}, bf16[6,4,32,2,128]{4,3,2,1,0:T(2,128)(2,1)S(1...) custom-call(bf16[12,32,2,2048]{3,2,1,0:T(2,128)(2,1)S(1)} %copy-done, ...), custom_call_target="tpu_custom_call" | custom-call | flops 1024 | bytes 1024 | tf_op jit(solution)/shard_map/pallas_call | solution.py:140
  18.5 0.0 copy-start.7
  18.6 0.0 copy-start.2
  18.6 0.0 copy-start.5
  18.6 0.8 %shard_map.103 = (bf16[4,2,64,128]{3,2,1,0:T(8,128)(2,1)S(1)}, bf16[4,2,64,128]{3,2,1,0:T(8,128)(2,1)S(1)}, bf16[4,2,64,128]{3,2,1,0:T(8,128)(2,1)S(1)}, bf16[4,...) custom-call(bf16[6,2,64,128]{3,2,1,0:T(8,128)(2,1)S(1)} %bitcast.35, bf16[6,2,64,128]{3,2,1,0:T(8,128)(2,1)S(1)} %bitcast.34, ...), custom_call_target="tpu_custom_call" | custom-call | flops 1024 | bytes 1024 | tf_op jit(solution)/shard_map/pallas_call | solution.py:207
  19.4 0.3 collective-permute-start.9
  19.8 0.1 collective-permute-start.10
  19.8 2.3 %collective-permute-start.11 = (bf16[4,2,64,128]{3,2,1,0:T(8,128)(2,1)S(1)}, bf16[4,2,64,128]{3,2,1,0:T(8,128)(2,1)S(1)}, u32[]{:S(2)}, u32[]{:S(2)}) collective-permute-start(bf16[4,2,64,128]{3,2,1,0:T(8,128)(2,1)S(1)} %get-tuple-element.56), channel_id=1, source_target_pairs={{0,24},{8,16},{16,8},{24,0},{1,25},{9,17},{17,9},{25,1},{2,26},{10... | collective-permute-start | bytes 393224 | tf_op jit(solution)/shard_map/ppermute | solution.py:49
  22.2 2.2 %collective-permute-done.2 = bf16[6,2,32,2,128]{4,3,2,1,0:T(2,128)(2,1)S(1)} collective-permute-done((bf16[6,2,32,2,128]{4,3,2,1,0:T(2,128)(2,1)S(1)}, bf16[6,2,32,2,128]{4,3,2,1,0:T(2,128)(2,1)S(1)}, u32[]{:S(2)}, u32[]{:S(2)}) %collective-permute-start.2) | collective-permute-done | bytes 196640 | tf_op jit(solution)/shard_map/ppermute | solution.py:49
  24.4 0.8 %shard_map.99 = (bf16[4,2,64,128]{3,2,1,0:T(8,128)(2,1)S(1)}, bf16[4,2,64,128]{3,2,1,0:T(8,128)(2,1)S(1)}, bf16[4,2,64,128]{3,2,1,0:T(8,128)(2,1)S(1)}, bf16[4,2...) custom-call(bf16[6,2,64,128]{3,2,1,0:T(8,128)(2,1)S(1)} %bitcast.31, bf16[6,2,64,128]{3,2,1,0:T(8,128)(2,1)S(1)} %bitcast.28, ...), custom_call_target="tpu_custom_call" | custom-call | flops 1024 | bytes 1024 | tf_op jit(solution)/shard_map/pallas_call | solution.py:207
  25.2 1.3 %collective-permute-start.3 = (bf16[4,2,64,128]{3,2,1,0:T(8,128)(2,1)S(1)}, bf16[4,2,64,128]{3,2,1,0:T(8,128)(2,1)S(1)}, u32[]{:S(2)}, u32[]{:S(2)}) collective-permute-start(bf16[4,2,64,128]{3,2,1,0:T(8,128)(2,1)S(1)} %get-tuple-element.49), channel_id=1, source_target_pairs={{0,8},{8,0},{16,24},{24,16},{1,9},{9,1},{17,25},{25,17},{2,10},{10... | collective-permute-start | bytes 393224 | tf_op jit(solution)/shard_map/ppermute | solution.py:49
  26.5 0.2 collective-permute-start.4
  26.7 1.7 %collective-permute-start.5 = (bf16[4,2,64,128]{3,2,1,0:T(8,128)(2,1)S(1)}, bf16[4,2,64,128]{3,2,1,0:T(8,128)(2,1)S(1)}, u32[]{:S(2)}, u32[]{:S(2)}) collective-permute-start(bf16[4,2,64,128]{3,2,1,0:T(8,128)(2,1)S(1)} %get-tuple-element.51), channel_id=1, source_target_pairs={{0,24},{8,16},{16,8},{24,0},{1,25},{9,17},{17,9},{25,1},{2,26},{10... | collective-permute-start | bytes 393224 | tf_op jit(solution)/shard_map/ppermute | solution.py:49
  28.4 1.3 %collective-permute-done.11.refs_7_ = bf16[4,2,64,128]{3,2,1,0:T(8,128)(2,1)S(1)} collective-permute-done((bf16[4,2,64,128]{3,2,1,0:T(8,128)(2,1)S(1)}, bf16[4,2,64,128]{3,2,1,0:T(8,128)(2,1)S(1)}, u32[]{:S(2)}, u32[]{:S(2)}) %collective-permute-start.11) | collective-permute-done | bytes 131104 | tf_op jit(solution)/shard_map/ppermute | solution.py:49
  29.7 2.0 %collective-permute-done.3.refs_1_ = bf16[4,2,64,128]{3,2,1,0:T(8,128)(2,1)S(1)} collective-permute-done((bf16[4,2,64,128]{3,2,1,0:T(8,128)(2,1)S(1)}, bf16[4,2,64,128]{3,2,1,0:T(8,128)(2,1)S(1)}, u32[]{:S(2)}, u32[]{:S(2)}) %collective-permute-start.3) | collective-permute-done | bytes 131104 | tf_op jit(solution)/shard_map/ppermute | solution.py:49
  31.7 0.5 collective-permute-done.4.refs_2_
  32.2 3.1 %collective-permute-done.5.refs_3_ = bf16[4,2,64,128]{3,2,1,0:T(8,128)(2,1)S(1)} collective-permute-done((bf16[4,2,64,128]{3,2,1,0:T(8,128)(2,1)S(1)}, bf16[4,2,64,128]{3,2,1,0:T(8,128)(2,1)S(1)}, u32[]{:S(2)}, u32[]{:S(2)}) %collective-permute-start.5) | collective-permute-done | bytes 131104 | tf_op jit(solution)/shard_map/ppermute | solution.py:49
  35.3 1.2 %collective-permute-start.14 = (bf16[6,4,32,2,128]{4,3,2,1,0:T(2,128)(2,1)S(1)}, bf16[6,4,32,2,128]{4,3,2,1,0:T(2,128)(2,1)S(1)}, u32[]{:S(2)}, u32[]{:S(2)}) collective-permute-start(bf16[6,4,32,2,128]{4,3,2,1,0:T(2,128)(2,1)S(1)} %get-tuple-element.73), channel_id=1, source_target_pairs={{0,8},{8,0},{16,24},{24,16},{1,9},{9,1},{17,25},{25,17},{2,10},{10... | collective-permute-start | bytes 1179656 | tf_op jit(solution)/shard_map/ppermute | solution.py:49
  36.5 0.2 collective-permute-start.15
  36.8 1.2 %collective-permute-start.16 = (bf16[6,4,32,2,128]{4,3,2,1,0:T(2,128)(2,1)S(1)}, bf16[6,4,32,2,128]{4,3,2,1,0:T(2,128)(2,1)S(1)}, u32[]{:S(2)}, u32[]{:S(2)}) collective-permute-start(bf16[6,4,32,2,128]{4,3,2,1,0:T(2,128)(2,1)S(1)} %get-tuple-element.75), channel_id=1, source_target_pairs={{0,24},{8,16},{16,8},{24,0},{1,25},{9,17},{17,9},{25,1},{2,26},{10... | collective-permute-start | bytes 1179656 | tf_op jit(solution)/shard_map/ppermute | solution.py:49
  38.0 1.2 %shard_map.104 = (bf16[4,2,64,128]{3,2,1,0:T(8,128)(2,1)S(1)}, bf16[4,2,64,128]{3,2,1,0:T(8,128)(2,1)S(1)}) custom-call(bf16[4,2,64,128]{3,2,1,0:T(8,128)(2,1)S(1)} %get-tuple-element.61.refs_0_, bf16[4,2,64,128]{3,2,1,0:T(8,128)(2,1)S(1)} %collective-permute-done.3.refs_1_, bf16[4,2,64,128]{3,2,1,0:T(8,128)(2,1)S(1)} %collective-permute-done.4.refs_2_, ...), custom_call_target="tpu_custom_call" | custom-call | flops 1024 | bytes 1024 | tf_op jit(solution)/shard_map/pallas_call | solution.py:301
  39.2 6.2 %collective-permute-start.12 = (bf16[4,2,64,128]{3,2,1,0:T(8,128)(2,1)S(1)}, bf16[4,2,64,128]{3,2,1,0:T(8,128)(2,1)S(1)}, u32[]{:S(2)}, u32[]{:S(2)}) collective-permute-start(bf16[4,2,64,128]{3,2,1,0:T(8,128)(2,1)S(1)} %get-tuple-element.69), channel_id=1, source_target_pairs={{0,1},{1,2},{2,3},{3,4},{4,5},{5,6},{6,7},{8,9},{9,10},{10,11},{11... | collective-permute-start | bytes 393224 | tf_op jit(solution)/shard_map/ppermute | solution.py:59
  45.4 1.9 %collective-permute-start.13 = (bf16[4,2,64,128]{3,2,1,0:T(8,128)(2,1)S(1)}, bf16[4,2,64,128]{3,2,1,0:T(8,128)(2,1)S(1)}, u32[]{:S(2)}, u32[]{:S(2)}) collective-permute-start(bf16[4,2,64,128]{3,2,1,0:T(8,128)(2,1)S(1)} %get-tuple-element.70), channel_id=1, source_target_pairs={{1,0},{2,1},{3,2},{4,3},{5,4},{6,5},{7,6},{9,8},{10,9},{11,10},{12... | collective-permute-start | bytes 393224 | tf_op jit(solution)/shard_map/ppermute | solution.py:59
  47.4 4.6 %collective-permute-done.13.refs_9_ = bf16[4,2,64,128]{3,2,1,0:T(8,128)(2,1)S(1)} collective-permute-done((bf16[4,2,64,128]{3,2,1,0:T(8,128)(2,1)S(1)}, bf16[4,2,64,128]{3,2,1,0:T(8,128)(2,1)S(1)}, u32[]{:S(2)}, u32[]{:S(2)}) %collective-permute-start.13) | collective-permute-done | bytes 131104 | tf_op jit(solution)/shard_map/ppermute | solution.py:59
  52.0 6.6 %shard_map.105 = (f32[3072,128]{1,0:T(8,128)}, f32[3,16,64,128]{3,2,1,0:T(8,128)S(1)}) custom-call(bf16[4,2,64,128]{3,2,1,0:T(8,128)(2,1)S(1)} %get-tuple-element.61.refs_0_, bf16[4,2,64,128]{3,2,1,0:T(8,128)(2,1)S(1)} %collective-permute-done.3.refs_1_, bf16[4,2,64,128]{3,2,1,0:T(8,128)(2,1)S(1)} %collective-permute-done.4.refs_2_, ...), custom_call_target="tpu_custom_call" | custom-call | flops 1024 | bytes 1024 | tf_op jit(solution)/shard_map/pallas_call | solution.py:382
  58.6 1.6 %shard_map.106 = (bf16[3,4,64,128]{3,2,1,0:T(8,128)(2,1)S(1)}, bf16[3,4,64,128]{3,2,1,0:T(8,128)(2,1)S(1)}, bf16[3,4,64,128]{3,2,1,0:T(8,128)(2,1)S(1)}, bf16[3,4,64,128]{3,2,1,0:T(8,128)(2,1)S(1)}) custom-call(bf16[6,4,64,128]{3,2,1,0:T(8,128)(2,1)S(1)} %bitcast.24, bf16[6,4,64,128]{3,2,1,0:T(8,128)(2,1)S(1)} %bitcast.25, ...), custom_call_target="tpu_custom_call" | custom-call | flops 1024 | bytes 1024 | tf_op jit(solution)/shard_map/pallas_call | solution.py:251
  60.2 1.1 %collective-permute-start.17 = (bf16[3,4,64,128]{3,2,1,0:T(8,128)(2,1)S(1)}, bf16[3,4,64,128]{3,2,1,0:T(8,128)(2,1)S(1)}, u32[]{:S(2)}, u32[]{:S(2)}) collective-permute-start(bf16[3,4,64,128]{3,2,1,0:T(8,128)(2,1)S(1)} %get-tuple-element.84), channel_id=1, source_target_pairs={{0,8},{8,0},{16,24},{24,16},{1,9},{9,1},{17,25},{25,17},{2,10},{10... | collective-permute-start | bytes 589832 | tf_op jit(solution)/shard_map/ppermute | solution.py:49
  61.3 0.2 collective-permute-start.18
  61.6 1.4 %collective-permute-start.19 = (bf16[3,4,64,128]{3,2,1,0:T(8,128)(2,1)S(1)}, bf16[3,4,64,128]{3,2,1,0:T(8,128)(2,1)S(1)}, u32[]{:S(2)}, u32[]{:S(2)}) collective-permute-start(bf16[3,4,64,128]{3,2,1,0:T(8,128)(2,1)S(1)} %get-tuple-element.86), channel_id=1, source_target_pairs={{0,24},{8,16},{16,8},{24,0},{1,25},{9,17},{17,9},{25,1},{2,26},{10... | collective-permute-start | bytes 589832 | tf_op jit(solution)/shard_map/ppermute | solution.py:49
  62.9 4.3 %collective-permute-done.17.refs_1_ = bf16[3,4,64,128]{3,2,1,0:T(8,128)(2,1)S(1)} collective-permute-done((bf16[3,4,64,128]{3,2,1,0:T(8,128)(2,1)S(1)}, bf16[3,4,64,128]{3,2,1,0:T(8,128)(2,1)S(1)}, u32[]{:S(2)}, u32[]{:S(2)}) %collective-permute-start.17) | collective-permute-done | bytes 196640 | tf_op jit(solution)/shard_map/ppermute | solution.py:49
  67.3 2.8 %collective-permute-done.18.refs_2_ = bf16[3,4,64,128]{3,2,1,0:T(8,128)(2,1)S(1)} collective-permute-done((bf16[3,4,64,128]{3,2,1,0:T(8,128)(2,1)S(1)}, bf16[3,4,64,128]{3,2,1,0:T(8,128)(2,1)S(1)}, u32[]{:S(2)}, u32[]{:S(2)}) %collective-permute-start.18) | collective-permute-done | bytes 196640 | tf_op jit(solution)/shard_map/ppermute | solution.py:49
  70.0 1.3 %shard_map.107 = f32[3072,128]{1,0:T(8,128)} custom-call(bf16[3,4,64,128]{3,2,1,0:T(8,128)(2,1)S(1)} %get-tuple-element.83.refs_0_, bf16[3,4,64,128]{3,2,1,0:T(8,128)(2,1)S(1)} %collective-permute-done.17.refs_1_, bf16[3,4,64,128]{3,2,1,0:T(8,128)(2,1)S(1)} %collective-permute-done.18.refs_2_, bf16[3,4,64,128]{3,2,1,0:T(8,128)(2,1)S(1)} %collective-permute-done.19.refs_3_, ...), custom_call_target="tpu_custom_call" | custom-call | flops 1024 | bytes 1024 | tf_op jit(solution)/shard_map/pallas_call | solution.py:450
  (21 shorter events, 0.1 us)
Async XLA Ops:
  0.6 1.9 %copy-start = (bf16[12,32,2,2048]{3,2,1,0:T(2,128)(2,1)S(1)}, bf16[12,32,2,2048]{3,2,1,0:T(2,128)(2,1)}, u32[]{:S(2)}) copy-start(bf16[12,32,2,2048]{3,2,1,0:T(2,128)(2,1)} %fields_ref.13) | copy-start | bytes 9437188
  2.8 10.2 %collective-permute-start.7 = (bf16[6,2,32,2,128]{4,3,2,1,0:T(2,128)(2,1)S(1)}, bf16[6,2,32,2,128]{4,3,2,1,0:T(2,128)(2,1)S(1)}, u32[]{:S(2)}, u32[]{:S(2)}) collective-permute-start(bf16[6,2,32,2,128]{4,3,2,1,0:T(2,128)(2,1)S(1)} %shard_map.101), channel_id=1, source_target_pairs={{0,16},{8,24},{16,0},{24,8},{1,17},{9,25},{17,1},{25,9},{2,18},{10... | collective-permute-start | bytes 589832 | tf_op jit(solution)/shard_map/ppermute | solution.py:49
  5.2 13.4 %collective-permute-start.8 = (bf16[6,2,32,2,128]{4,3,2,1,0:T(2,128)(2,1)S(1)}, bf16[6,2,32,2,128]{4,3,2,1,0:T(2,128)(2,1)S(1)}, u32[]{:S(2)}, u32[]{:S(2)}) collective-permute-start(bf16[6,2,32,2,128]{4,3,2,1,0:T(2,128)(2,1)S(1)} %shard_map.102), channel_id=1, source_target_pairs={{0,24},{8,16},{16,8},{24,0},{1,25},{9,17},{17,9},{25,1},{2,26},{10... | collective-permute-start | bytes 589832 | tf_op jit(solution)/shard_map/ppermute | solution.py:49
  6.7 11.9 %collective-permute-start.6 = (bf16[6,2,32,2,128]{4,3,2,1,0:T(2,128)(2,1)S(1)}, bf16[6,2,32,2,128]{4,3,2,1,0:T(2,128)(2,1)S(1)}, u32[]{:S(2)}, u32[]{:S(2)}) collective-permute-start(bf16[6,2,32,2,128]{4,3,2,1,0:T(2,128)(2,1)S(1)} %shard_map.100), channel_id=1, source_target_pairs={{0,8},{8,0},{16,24},{24,16},{1,9},{9,1},{17,25},{25,17},{2,10},{10... | collective-permute-start | bytes 589832 | tf_op jit(solution)/shard_map/ppermute | solution.py:49
  7.1 12.7 %collective-permute-start = (bf16[6,2,32,2,128]{4,3,2,1,0:T(2,128)(2,1)S(1)}, bf16[6,2,32,2,128]{4,3,2,1,0:T(2,128)(2,1)S(1)}, u32[]{:S(2)}, u32[]{:S(2)}) collective-permute-start(bf16[6,2,32,2,128]{4,3,2,1,0:T(2,128)(2,1)S(1)} %shard_map.96), channel_id=1, source_target_pairs={{0,8},{8,0},{16,24},{24,16},{1,9},{9,1},{17,25},{25,17},{2,10},{10... | collective-permute-start | bytes 589832 | tf_op jit(solution)/shard_map/ppermute | solution.py:49
  8.8 7.0 %copy-start.3 = (bf16[256,256]{1,0:T(8,128)(2,1)S(1)}, bf16[256,256]{1,0:T(8,128)(2,1)}, u32[]{:S(2)}) copy-start(bf16[256,256]{1,0:T(8,128)(2,1)} %constant.5.clone.refs_1_) | copy-start | bytes 393220
  8.9 7.0 %copy-start.4 = (bf16[256,256]{1,0:T(8,128)(2,1)S(1)}, bf16[256,256]{1,0:T(8,128)(2,1)}, u32[]{:S(2)}) copy-start(bf16[256,256]{1,0:T(8,128)(2,1)} %constant.4.clone.refs_0_) | copy-start | bytes 393220
  8.9 13.3 %collective-permute-start.1 = (bf16[6,2,32,2,128]{4,3,2,1,0:T(2,128)(2,1)S(1)}, bf16[6,2,32,2,128]{4,3,2,1,0:T(2,128)(2,1)S(1)}, u32[]{:S(2)}, u32[]{:S(2)}) collective-permute-start(bf16[6,2,32,2,128]{4,3,2,1,0:T(2,128)(2,1)S(1)} %shard_map.97), channel_id=1, source_target_pairs={{0,16},{8,24},{16,0},{24,8},{1,17},{9,25},{17,1},{25,9},{2,18},{10... | collective-permute-start | bytes 589832 | tf_op jit(solution)/shard_map/ppermute | solution.py:49
  13.0 11.4 %collective-permute-start.2 = (bf16[6,2,32,2,128]{4,3,2,1,0:T(2,128)(2,1)S(1)}, bf16[6,2,32,2,128]{4,3,2,1,0:T(2,128)(2,1)S(1)}, u32[]{:S(2)}, u32[]{:S(2)}) collective-permute-start(bf16[6,2,32,2,128]{4,3,2,1,0:T(2,128)(2,1)S(1)} %shard_map.98), channel_id=1, source_target_pairs={{0,24},{8,16},{16,8},{24,0},{1,25},{9,17},{17,9},{25,1},{2,26},{10... | collective-permute-start | bytes 589832 | tf_op jit(solution)/shard_map/ppermute | solution.py:49
  18.5 19.4 %copy-start.7 = (s32[2,256]{1,0:T(2,128)S(1)}, s32[2,256]{1,0:T(2,128)}, u32[]{:S(2)}) copy-start(s32[2,256]{1,0:T(2,128)} %refs_8_.1) | copy-start | bytes 6148
  18.6 33.5 %copy-start.1 = (bf16[5,64,2048]{2,1,0:T(8,128)(2,1)S(1)}, bf16[5,64,2048]{2,1,0:T(8,128)(2,1)}, u32[]{:S(2)}) copy-start(bf16[5,64,2048]{2,1,0:T(8,128)(2,1)} %refs_10_.1) | copy-start | bytes 3932164
  18.6 33.4 %copy-start.2 = (bf16[5,64,2048]{2,1,0:T(8,128)(2,1)S(1)}, bf16[5,64,2048]{2,1,0:T(8,128)(2,1)}, u32[]{:S(2)}) copy-start(bf16[5,64,2048]{2,1,0:T(8,128)(2,1)} %refs_11_.1) | copy-start | bytes 3932164
  18.6 33.4 %copy-start.5 = (f32[2048]{0:T(1024)S(1)}, f32[2048]{0:T(1024)}, u32[]{:S(2)}) copy-start(f32[2048]{0:T(1024)} %param.9) | copy-start | bytes 24580
  18.6 33.4 %copy-start.6 = (s32[32,5]{0,1:T(8,128)S(1)}, s32[32,5]{0,1:T(8,128)}, u32[]{:S(2)}) copy-start(s32[32,5]{0,1:T(8,128)} %param.12) | copy-start | bytes 1924
  19.4 7.3 %collective-permute-start.9 = (bf16[4,2,64,128]{3,2,1,0:T(8,128)(2,1)S(1)}, bf16[4,2,64,128]{3,2,1,0:T(8,128)(2,1)S(1)}, u32[]{:S(2)}, u32[]{:S(2)}) collective-permute-start(bf16[4,2,64,128]{3,2,1,0:T(8,128)(2,1)S(1)} %get-tuple-element.54), channel_id=1, source_target_pairs={{0,8},{8,0},{16,24},{24,16},{1,9},{9,1},{17,25},{25,17},{2,10},{10... | collective-permute-start | bytes 393224 | tf_op jit(solution)/shard_map/ppermute | solution.py:49
  19.8 8.6 %collective-permute-start.10 = (bf16[4,2,64,128]{3,2,1,0:T(8,128)(2,1)S(1)}, bf16[4,2,64,128]{3,2,1,0:T(8,128)(2,1)S(1)}, u32[]{:S(2)}, u32[]{:S(2)}) collective-permute-start(bf16[4,2,64,128]{3,2,1,0:T(8,128)(2,1)S(1)} %get-tuple-element.55), channel_id=1, source_target_pairs={{0,16},{8,24},{16,0},{24,8},{1,17},{9,25},{17,1},{25,9},{2,18},{10... | collective-permute-start | bytes 393224 | tf_op jit(solution)/shard_map/ppermute | solution.py:49
  19.8 9.9 %collective-permute-start.11 = (bf16[4,2,64,128]{3,2,1,0:T(8,128)(2,1)S(1)}, bf16[4,2,64,128]{3,2,1,0:T(8,128)(2,1)S(1)}, u32[]{:S(2)}, u32[]{:S(2)}) collective-permute-start(bf16[4,2,64,128]{3,2,1,0:T(8,128)(2,1)S(1)} %get-tuple-element.56), channel_id=1, source_target_pairs={{0,24},{8,16},{16,8},{24,0},{1,25},{9,17},{17,9},{25,1},{2,26},{10... | collective-permute-start | bytes 393224 | tf_op jit(solution)/shard_map/ppermute | solution.py:49
  25.2 6.5 %collective-permute-start.3 = (bf16[4,2,64,128]{3,2,1,0:T(8,128)(2,1)S(1)}, bf16[4,2,64,128]{3,2,1,0:T(8,128)(2,1)S(1)}, u32[]{:S(2)}, u32[]{:S(2)}) collective-permute-start(bf16[4,2,64,128]{3,2,1,0:T(8,128)(2,1)S(1)} %get-tuple-element.49), channel_id=1, source_target_pairs={{0,8},{8,0},{16,24},{24,16},{1,9},{9,1},{17,25},{25,17},{2,10},{10... | collective-permute-start | bytes 393224 | tf_op jit(solution)/shard_map/ppermute | solution.py:49
  26.5 5.7 %collective-permute-start.4 = (bf16[4,2,64,128]{3,2,1,0:T(8,128)(2,1)S(1)}, bf16[4,2,64,128]{3,2,1,0:T(8,128)(2,1)S(1)}, u32[]{:S(2)}, u32[]{:S(2)}) collective-permute-start(bf16[4,2,64,128]{3,2,1,0:T(8,128)(2,1)S(1)} %get-tuple-element.50), channel_id=1, source_target_pairs={{0,16},{8,24},{16,0},{24,8},{1,17},{9,25},{17,1},{25,9},{2,18},{10... | collective-permute-start | bytes 393224 | tf_op jit(solution)/shard_map/ppermute | solution.py:49
  26.7 8.6 %collective-permute-start.5 = (bf16[4,2,64,128]{3,2,1,0:T(8,128)(2,1)S(1)}, bf16[4,2,64,128]{3,2,1,0:T(8,128)(2,1)S(1)}, u32[]{:S(2)}, u32[]{:S(2)}) collective-permute-start(bf16[4,2,64,128]{3,2,1,0:T(8,128)(2,1)S(1)} %get-tuple-element.51), channel_id=1, source_target_pairs={{0,24},{8,16},{16,8},{24,0},{1,25},{9,17},{17,9},{25,1},{2,26},{10... | collective-permute-start | bytes 393224 | tf_op jit(solution)/shard_map/ppermute | solution.py:49
  35.3 23.3 %collective-permute-start.14 = (bf16[6,4,32,2,128]{4,3,2,1,0:T(2,128)(2,1)S(1)}, bf16[6,4,32,2,128]{4,3,2,1,0:T(2,128)(2,1)S(1)}, u32[]{:S(2)}, u32[]{:S(2)}) collective-permute-start(bf16[6,4,32,2,128]{4,3,2,1,0:T(2,128)(2,1)S(1)} %get-tuple-element.73), channel_id=1, source_target_pairs={{0,8},{8,0},{16,24},{24,16},{1,9},{9,1},{17,25},{25,17},{2,10},{10... | collective-permute-start | bytes 1179656 | tf_op jit(solution)/shard_map/ppermute | solution.py:49
  36.5 22.1 %collective-permute-start.15 = (bf16[6,4,32,2,128]{4,3,2,1,0:T(2,128)(2,1)S(1)}, bf16[6,4,32,2,128]{4,3,2,1,0:T(2,128)(2,1)S(1)}, u32[]{:S(2)}, u32[]{:S(2)}) collective-permute-start(bf16[6,4,32,2,128]{4,3,2,1,0:T(2,128)(2,1)S(1)} %get-tuple-element.74), channel_id=1, source_target_pairs={{0,16},{8,24},{16,0},{24,8},{1,17},{9,25},{17,1},{25,9},{2,18},{10... | collective-permute-start | bytes 1179656 | tf_op jit(solution)/shard_map/ppermute | solution.py:49
  36.8 21.9 %collective-permute-start.16 = (bf16[6,4,32,2,128]{4,3,2,1,0:T(2,128)(2,1)S(1)}, bf16[6,4,32,2,128]{4,3,2,1,0:T(2,128)(2,1)S(1)}, u32[]{:S(2)}, u32[]{:S(2)}) collective-permute-start(bf16[6,4,32,2,128]{4,3,2,1,0:T(2,128)(2,1)S(1)} %get-tuple-element.75), channel_id=1, source_target_pairs={{0,24},{8,16},{16,8},{24,0},{1,25},{9,17},{17,9},{25,1},{2,26},{10... | collective-permute-start | bytes 1179656 | tf_op jit(solution)/shard_map/ppermute | solution.py:49
  39.2 8.2 %collective-permute-start.12 = (bf16[4,2,64,128]{3,2,1,0:T(8,128)(2,1)S(1)}, bf16[4,2,64,128]{3,2,1,0:T(8,128)(2,1)S(1)}, u32[]{:S(2)}, u32[]{:S(2)}) collective-permute-start(bf16[4,2,64,128]{3,2,1,0:T(8,128)(2,1)S(1)} %get-tuple-element.69), channel_id=1, source_target_pairs={{0,1},{1,2},{2,3},{3,4},{4,5},{5,6},{6,7},{8,9},{9,10},{10,11},{11... | collective-permute-start | bytes 393224 | tf_op jit(solution)/shard_map/ppermute | solution.py:59
  45.4 6.6 %collective-permute-start.13 = (bf16[4,2,64,128]{3,2,1,0:T(8,128)(2,1)S(1)}, bf16[4,2,64,128]{3,2,1,0:T(8,128)(2,1)S(1)}, u32[]{:S(2)}, u32[]{:S(2)}) collective-permute-start(bf16[4,2,64,128]{3,2,1,0:T(8,128)(2,1)S(1)} %get-tuple-element.70), channel_id=1, source_target_pairs={{1,0},{2,1},{3,2},{4,3},{5,4},{6,5},{7,6},{9,8},{10,9},{11,10},{12... | collective-permute-start | bytes 393224 | tf_op jit(solution)/shard_map/ppermute | solution.py:59
  60.2 7.1 %collective-permute-start.17 = (bf16[3,4,64,128]{3,2,1,0:T(8,128)(2,1)S(1)}, bf16[3,4,64,128]{3,2,1,0:T(8,128)(2,1)S(1)}, u32[]{:S(2)}, u32[]{:S(2)}) collective-permute-start(bf16[3,4,64,128]{3,2,1,0:T(8,128)(2,1)S(1)} %get-tuple-element.84), channel_id=1, source_target_pairs={{0,8},{8,0},{16,24},{24,16},{1,9},{9,1},{17,25},{25,17},{2,10},{10... | collective-permute-start | bytes 589832 | tf_op jit(solution)/shard_map/ppermute | solution.py:49
  61.3 8.7 %collective-permute-start.18 = (bf16[3,4,64,128]{3,2,1,0:T(8,128)(2,1)S(1)}, bf16[3,4,64,128]{3,2,1,0:T(8,128)(2,1)S(1)}, u32[]{:S(2)}, u32[]{:S(2)}) collective-permute-start(bf16[3,4,64,128]{3,2,1,0:T(8,128)(2,1)S(1)} %get-tuple-element.85), channel_id=1, source_target_pairs={{0,16},{8,24},{16,0},{24,8},{1,17},{9,25},{17,1},{25,9},{2,18},{10... | collective-permute-start | bytes 589832 | tf_op jit(solution)/shard_map/ppermute | solution.py:49
  61.6 8.5 %collective-permute-start.19 = (bf16[3,4,64,128]{3,2,1,0:T(8,128)(2,1)S(1)}, bf16[3,4,64,128]{3,2,1,0:T(8,128)(2,1)S(1)}, u32[]{:S(2)}, u32[]{:S(2)}) collective-permute-start(bf16[3,4,64,128]{3,2,1,0:T(8,128)(2,1)S(1)} %get-tuple-element.86), channel_id=1, source_target_pairs={{0,24},{8,16},{16,8},{24,0},{1,25},{9,17},{17,9},{25,1},{2,26},{10... | collective-permute-start | bytes 589832 | tf_op jit(solution)/shard_map/ppermute | solution.py:49

commit v7 on v6

--- a/solution.py
+++ b/solution.py
@@ -85,8 +85,7 @@
     pairs = []
     for t in range(held):
         start = pl.multiple_of((share * tiles + group * held + t) * LANES, LANES)
-        for c in range(components):
-            pairs.append((fields_ref.at[first + c, :, :, pl.ds(start, LANES)], out_ref.at[c, t]))
+        pairs.append((fields_ref.at[pl.ds(first, components), :, :, pl.ds(start, LANES)], out_ref.at[:, t]))
     return pairs
 
 
@@ -118,7 +117,7 @@
         in_specs=[pl.BlockSpec(memory_space=pl.ANY)],
         out_specs=vmem(),
         out_shape=jax.ShapeDtypeStruct(shape, jnp.bfloat16),
-        scratch_shapes=[pltpu.SemaphoreType.DMA((shape[0] * shape[1],))],
+        scratch_shapes=[pltpu.SemaphoreType.DMA((shape[1],))],
         compiler_params=params(),
         cost_estimate=cost(),
     )(fields)
@@ -143,7 +142,7 @@
         out_specs=[vmem()] * (len(parcels) + len(carried)),
         out_shape=[jax.ShapeDtypeStruct(shape, jnp.bfloat16) for shape in shapes]
         + [jax.ShapeDtypeStruct(value.shape, value.dtype) for value in carried],
-        scratch_shapes=[pltpu.SemaphoreType.DMA((sum(shape[0] * shape[1] for shape in shapes),))],
+        scratch_shapes=[pltpu.SemaphoreType.DMA((sum(shape[1] for shape in shapes),))],
         compiler_params=params(),
         cost_estimate=cost(),
     )(fields, *carried)
@@ -478,25 +477,30 @@
     for group in range(groups):
         arrived.append(exchange([pack(mode_fields, 0, 6, step, group, groups) for step in range(1, count)]))
     parcels = [(0, 6, 0, group, groups) for group in range(groups)]
-    parcels += [(6, 12, step, 0, 1) for step in range(count)]
-    *packed, inverse, forward = pack_rest(mode_fields, parcels, [inverse, forward])
-    own, shares = packed[:groups], packed[groups:]
+    *own, inverse, forward = pack_rest(mode_fields, parcels, [inverse, forward])
+    arrived[0][1:2], carried = lax.optimization_barrier((arrived[0][1:2], [inverse, forward]))
+    parcels = [(6, 12, step, 0, 1) for step in range(count)]
+    *shares, later_inverse, later_forward = pack_rest(mode_fields, parcels, carried)
     local, physical = [], []
     for group in range(groups):
-        *terms, velocity_magnetic = first_physics(joined([own[group]] + arrived[group]), inverse, forward)
+        if group == 0:
+            tables_here = (later_inverse, later_forward)
+        else:
+            tables_here = (inverse, forward)
+        *terms, velocity_magnetic = first_physics(joined([own[group]] + arrived[group]), *tables_here)
         local += terms[:1] + exchange(terms[1:])
         physical.append(velocity_magnetic)
     local, shares = lax.optimization_barrier((local, shares))
     sources = shares[:1] + exchange(shares[1:])
     toward_prev, toward_next = interface(local, interface_nodes, count)
-    from_prev = from_behind(toward_next, "mer", 1)
-    from_next = from_behind(toward_prev, "mer", -1)
+    halos = (from_behind(toward_next, "mer", 1), from_behind(toward_prev, "mer", -1))
+    sources, halos = lax.optimization_barrier((sources, halos))
+    lorentz = list(second_physics(joined(sources), physical, later_inverse, later_forward))
+    lorentz, radius = lax.optimization_barrier((lorentz, radius))
+    lorentz = lorentz[:1] + exchange(lorentz[1:])
     induction, gradient = derive(
-        local, from_prev, from_next, radial_blocks, axial_blocks, radius.reshape(1, width), block_columns.T, count
+        local, *halos, radial_blocks, axial_blocks, radius.reshape(1, width), block_columns.T, count
     )
-    sources, gradient = lax.optimization_barrier((sources, gradient))
-    lorentz = list(second_physics(joined(sources), physical, inverse, forward))
-    lorentz = lorentz[:1] + exchange(lorentz[1:])
     momentum = momentum_of(lorentz, gradient, count)
     return (whole_output(induction, mode_count, width), whole_output(momentum, mode_count, width))
 

time: 72 us -> 69.5 us (0.965)
  the two profiles are of different devices: /device:TPU:1 before, /device:TPU:0 now
where the time goes in v7:
time: 69.5 us; the launch traced here: 69.3 us
  starting transfers between devices  28 us (40%)
  waiting for transfers between devices  23.6 us (34%)
  Pallas kernels  14.9 us (21%)
  local copies, waits for them, and re-layouts  1.93 us (3%)
  between operations  0.85 us (1%)
    ppermute x18, starting transfers between devices, send(): return lax.ppermute(piece, 'mode', pairs)  25.4 us
    ppermute x18, waiting for transfers between devices, send(): return lax.ppermute(piece, 'mode', pairs)  19.9 us
    pallas_call x1, Pallas kernels, derive(): pl.pallas_call(functools.partial(derive_kernel, count, len(received)), in...  6.58 us
    ppermute x2, waiting for transfers between devices, from_behind(): lax.ppermute(value, axis, [(source, source + steps) for source in range(i...  3.74 us
    ppermute x2, starting transfers between devices, from_behind(): lax.ppermute(value, axis, [(source, source + steps) for source in range(i...  2.59 us
    unnamed x18, local copies, waits for them, and re-layouts  1.93 us
    pallas_call x2, Pallas kernels, first_physics(): pl.pallas_call(functools.partial(first_kernel, count), in_specs=[vmem()]...  1.64 us
    pallas_call x2, Pallas kernels, pack_rest(): pl.pallas_call(kernel, in_specs=[pl.BlockSpec(memory_space=pl.ANY)] + [vm...  1.62 us
  transfers between devices with their start and end apart: 20, of which 8 were waited for; matrix products, arithmetic and copies ran while one was open for 0% of the time, Pallas kernels for 17%

profile of v7, /device:TPU:0, one launch (start us, length us, event | category | flops | bytes accessed | tf_op | source)
XLA Modules:
  0.0 69.3 jit_solution(18229370281919413817)
XLA Ops:
  0.6 0.0 copy-start
  0.6 1.9 %copy-done = bf16[12,32,2,2048]{3,2,1,0:T(2,128)(2,1)S(1)} copy-done((bf16[12,32,2,2048]{3,2,1,0:T(2,128)(2,1)S(1)}, bf16[12,32,2,2048]{3,2,1,0:T(2,128)(2,1)}, u32[]{:S(2)}) %copy-start) | copy-done | bytes 3145752
  2.5 0.2 shard_map.102
  2.7 3.0 %collective-permute-start.7 = (bf16[6,2,32,2,128]{4,3,2,1,0:T(2,128)(2,1)S(1)}, bf16[6,2,32,2,128]{4,3,2,1,0:T(2,128)(2,1)S(1)}, u32[]{:S(2)}, u32[]{:S(2)}) collective-permute-start(bf16[6,2,32,2,128]{4,3,2,1,0:T(2,128)(2,1)S(1)} %shard_map.102), channel_id=1, source_target_pairs={{0,16},{8,24},{16,0},{24,8},{1,17},{9,25},{17,1},{25,9},{2,18},{10... | collective-permute-start | bytes 589832 | tf_op jit(solution)/shard_map/ppermute | solution.py:49
  5.7 0.2 shard_map.103
  5.9 1.5 %collective-permute-start.8 = (bf16[6,2,32,2,128]{4,3,2,1,0:T(2,128)(2,1)S(1)}, bf16[6,2,32,2,128]{4,3,2,1,0:T(2,128)(2,1)S(1)}, u32[]{:S(2)}, u32[]{:S(2)}) collective-permute-start(bf16[6,2,32,2,128]{4,3,2,1,0:T(2,128)(2,1)S(1)} %shard_map.103), channel_id=1, source_target_pairs={{0,24},{8,16},{16,8},{24,0},{1,25},{9,17},{17,9},{25,1},{2,26},{10... | collective-permute-start | bytes 589832 | tf_op jit(solution)/shard_map/ppermute | solution.py:49
  7.4 0.2 shard_map.101
  7.6 0.1 collective-permute-start.6
  7.7 0.2 shard_map.97
  7.9 2.0 %collective-permute-start.1 = (bf16[6,2,32,2,128]{4,3,2,1,0:T(2,128)(2,1)S(1)}, bf16[6,2,32,2,128]{4,3,2,1,0:T(2,128)(2,1)S(1)}, u32[]{:S(2)}, u32[]{:S(2)}) collective-permute-start(bf16[6,2,32,2,128]{4,3,2,1,0:T(2,128)(2,1)S(1)} %shard_map.97), channel_id=1, source_target_pairs={{0,16},{8,24},{16,0},{24,8},{1,17},{9,25},{17,1},{25,9},{2,18},{10... | collective-permute-start | bytes 589832 | tf_op jit(solution)/shard_map/ppermute | solution.py:49
  9.9 0.2 shard_map.96
  10.1 0.0 copy-start.4
  10.1 0.0 copy-start.5
  10.1 1.6 %collective-permute-start = (bf16[6,2,32,2,128]{4,3,2,1,0:T(2,128)(2,1)S(1)}, bf16[6,2,32,2,128]{4,3,2,1,0:T(2,128)(2,1)S(1)}, u32[]{:S(2)}, u32[]{:S(2)}) collective-permute-start(bf16[6,2,32,2,128]{4,3,2,1,0:T(2,128)(2,1)S(1)} %shard_map.96), channel_id=1, source_target_pairs={{0,8},{8,0},{16,24},{24,16},{1,9},{9,1},{17,25},{25,17},{2,10},{10... | collective-permute-start | bytes 589832 | tf_op jit(solution)/shard_map/ppermute | solution.py:49
  11.7 0.2 shard_map.98
  11.8 0.0 copy-start.1
  11.8 3.8 %collective-permute-done.7 = bf16[6,2,32,2,128]{4,3,2,1,0:T(2,128)(2,1)S(1)} collective-permute-done((bf16[6,2,32,2,128]{4,3,2,1,0:T(2,128)(2,1)S(1)}, bf16[6,2,32,2,128]{4,3,2,1,0:T(2,128)(2,1)S(1)}, u32[]{:S(2)}, u32[]{:S(2)}) %collective-permute-start.7) | collective-permute-done | bytes 196640 | tf_op jit(solution)/shard_map/ppermute | solution.py:49
  15.7 3.0 %collective-permute-start.2 = (bf16[6,2,32,2,128]{4,3,2,1,0:T(2,128)(2,1)S(1)}, bf16[6,2,32,2,128]{4,3,2,1,0:T(2,128)(2,1)S(1)}, u32[]{:S(2)}, u32[]{:S(2)}) collective-permute-start(bf16[6,2,32,2,128]{4,3,2,1,0:T(2,128)(2,1)S(1)} %shard_map.98), channel_id=1, source_target_pairs={{0,24},{8,16},{16,8},{24,0},{1,25},{9,17},{17,9},{25,1},{2,26},{10... | collective-permute-start | bytes 589832 | tf_op jit(solution)/shard_map/ppermute | solution.py:49
  18.7 0.3 shard_map.95
  19.0 0.8 %shard_map.104 = (bf16[4,2,64,128]{3,2,1,0:T(8,128)(2,1)S(1)}, bf16[4,2,64,128]{3,2,1,0:T(8,128)(2,1)S(1)}, bf16[4,2,64,128]{3,2,1,0:T(8,128)(2,1)S(1)}, bf16[4,...) custom-call(bf16[6,2,64,128]{3,2,1,0:T(8,128)(2,1)S(1)} %bitcast.35, bf16[6,2,64,128]{3,2,1,0:T(8,128)(2,1)S(1)} %bitcast.34, ...), custom_call_target="tpu_custom_call" | custom-call | flops 1024 | bytes 1024 | tf_op jit(solution)/shard_map/pallas_call | solution.py:206
  19.8 0.6 collective-permute-start.9
  20.4 1.4 %collective-permute-start.10 = (bf16[4,2,64,128]{3,2,1,0:T(8,128)(2,1)S(1)}, bf16[4,2,64,128]{3,2,1,0:T(8,128)(2,1)S(1)}, u32[]{:S(2)}, u32[]{:S(2)}) collective-permute-start(bf16[4,2,64,128]{3,2,1,0:T(8,128)(2,1)S(1)} %get-tuple-element.71), channel_id=1, source_target_pairs={{0,16},{8,24},{16,0},{24,8},{1,17},{9,25},{17,1},{25,9},{2,18},{10... | collective-permute-start | bytes 393224 | tf_op jit(solution)/shard_map/ppermute | solution.py:49
  21.8 1.6 %collective-permute-start.11 = (bf16[4,2,64,128]{3,2,1,0:T(8,128)(2,1)S(1)}, bf16[4,2,64,128]{3,2,1,0:T(8,128)(2,1)S(1)}, u32[]{:S(2)}, u32[]{:S(2)}) collective-permute-start(bf16[4,2,64,128]{3,2,1,0:T(8,128)(2,1)S(1)} %get-tuple-element.72), channel_id=1, source_target_pairs={{0,24},{8,16},{16,8},{24,0},{1,25},{9,17},{17,9},{25,1},{2,26},{10... | collective-permute-start | bytes 393224 | tf_op jit(solution)/shard_map/ppermute | solution.py:49
  23.4 1.3 %shard_map.99 = (bf16[6,4,32,2,128]{4,3,2,1,0:T(2,128)(2,1)S(1)}, bf16[6,4,32,2,128]{4,3,2,1,0:T(2,128)(2,1)S(1)}, bf16[6,4,32,2,128]{4,3,2,1,0:T(2,128)(2,1)S(1...) custom-call(bf16[12,32,2,2048]{3,2,1,0:T(2,128)(2,1)S(1)} %copy-done.1, ...), custom_call_target="tpu_custom_call" | custom-call | flops 1024 | bytes 1024 | tf_op jit(solution)/shard_map/pallas_call | solution.py:139
  24.7 2.7 %collective-permute-done.2 = bf16[6,2,32,2,128]{4,3,2,1,0:T(2,128)(2,1)S(1)} collective-permute-done((bf16[6,2,32,2,128]{4,3,2,1,0:T(2,128)(2,1)S(1)}, bf16[6,2,32,2,128]{4,3,2,1,0:T(2,128)(2,1)S(1)}, u32[]{:S(2)}, u32[]{:S(2)}) %collective-permute-start.2) | collective-permute-done | bytes 196640 | tf_op jit(solution)/shard_map/ppermute | solution.py:49
  27.4 0.8 %shard_map.100 = (bf16[4,2,64,128]{3,2,1,0:T(8,128)(2,1)S(1)}, bf16[4,2,64,128]{3,2,1,0:T(8,128)(2,1)S(1)}, bf16[4,2,64,128]{3,2,1,0:T(8,128)(2,1)S(1)}, bf16[4,...) custom-call(bf16[6,2,64,128]{3,2,1,0:T(8,128)(2,1)S(1)} %bitcast.31, bf16[6,2,64,128]{3,2,1,0:T(8,128)(2,1)S(1)} %bitcast.29, ...), custom_call_target="tpu_custom_call" | custom-call | flops 1024 | bytes 1024 | tf_op jit(solution)/shard_map/pallas_call | solution.py:206
  28.2 1.6 %collective-permute-start.3 = (bf16[4,2,64,128]{3,2,1,0:T(8,128)(2,1)S(1)}, bf16[4,2,64,128]{3,2,1,0:T(8,128)(2,1)S(1)}, u32[]{:S(2)}, u32[]{:S(2)}) collective-permute-start(bf16[4,2,64,128]{3,2,1,0:T(8,128)(2,1)S(1)} %get-tuple-element.65), channel_id=1, source_target_pairs={{0,8},{8,0},{16,24},{24,16},{1,9},{9,1},{17,25},{25,17},{2,10},{10... | collective-permute-start | bytes 393224 | tf_op jit(solution)/shard_map/ppermute | solution.py:49
  29.8 0.5 collective-permute-start.4
  30.3 1.5 %collective-permute-start.5 = (bf16[4,2,64,128]{3,2,1,0:T(8,128)(2,1)S(1)}, bf16[4,2,64,128]{3,2,1,0:T(8,128)(2,1)S(1)}, u32[]{:S(2)}, u32[]{:S(2)}) collective-permute-start(bf16[4,2,64,128]{3,2,1,0:T(8,128)(2,1)S(1)} %get-tuple-element.67), channel_id=1, source_target_pairs={{0,24},{8,16},{16,8},{24,0},{1,25},{9,17},{17,9},{25,1},{2,26},{10... | collective-permute-start | bytes 393224 | tf_op jit(solution)/shard_map/ppermute | solution.py:49
  31.8 1.2 %collective-permute-done.11.refs_7_ = bf16[4,2,64,128]{3,2,1,0:T(8,128)(2,1)S(1)} collective-permute-done((bf16[4,2,64,128]{3,2,1,0:T(8,128)(2,1)S(1)}, bf16[4,2,64,128]{3,2,1,0:T(8,128)(2,1)S(1)}, u32[]{:S(2)}, u32[]{:S(2)}) %collective-permute-start.11) | collective-permute-done | bytes 131104 | tf_op jit(solution)/shard_map/ppermute | solution.py:49
  33.0 1.6 %collective-permute-done.3.refs_1_ = bf16[4,2,64,128]{3,2,1,0:T(8,128)(2,1)S(1)} collective-permute-done((bf16[4,2,64,128]{3,2,1,0:T(8,128)(2,1)S(1)}, bf16[4,2,64,128]{3,2,1,0:T(8,128)(2,1)S(1)}, u32[]{:S(2)}, u32[]{:S(2)}) %collective-permute-start.3) | collective-permute-done | bytes 131104 | tf_op jit(solution)/shard_map/ppermute | solution.py:49
  34.6 2.7 %collective-permute-done.4.refs_2_ = bf16[4,2,64,128]{3,2,1,0:T(8,128)(2,1)S(1)} collective-permute-done((bf16[4,2,64,128]{3,2,1,0:T(8,128)(2,1)S(1)}, bf16[4,2,64,128]{3,2,1,0:T(8,128)(2,1)S(1)}, u32[]{:S(2)}, u32[]{:S(2)}) %collective-permute-start.4) | collective-permute-done | bytes 131104 | tf_op jit(solution)/shard_map/ppermute | solution.py:49
  37.4 1.3 %collective-permute-start.12 = (bf16[6,4,32,2,128]{4,3,2,1,0:T(2,128)(2,1)S(1)}, bf16[6,4,32,2,128]{4,3,2,1,0:T(2,128)(2,1)S(1)}, u32[]{:S(2)}, u32[]{:S(2)}) collective-permute-start(bf16[6,4,32,2,128]{4,3,2,1,0:T(2,128)(2,1)S(1)} %get-tuple-element.86), channel_id=1, source_target_pairs={{0,8},{8,0},{16,24},{24,16},{1,9},{9,1},{17,25},{25,17},{2,10},{10... | collective-permute-start | bytes 1179656 | tf_op jit(solution)/shard_map/ppermute | solution.py:49
  38.7 0.5 collective-permute-start.13
  39.2 1.7 %collective-permute-start.14 = (bf16[6,4,32,2,128]{4,3,2,1,0:T(2,128)(2,1)S(1)}, bf16[6,4,32,2,128]{4,3,2,1,0:T(2,128)(2,1)S(1)}, u32[]{:S(2)}, u32[]{:S(2)}) collective-permute-start(bf16[6,4,32,2,128]{4,3,2,1,0:T(2,128)(2,1)S(1)} %get-tuple-element.88), channel_id=1, source_target_pairs={{0,24},{8,16},{16,8},{24,0},{1,25},{9,17},{17,9},{25,1},{2,26},{10... | collective-permute-start | bytes 1179656 | tf_op jit(solution)/shard_map/ppermute | solution.py:49
  40.8 1.2 %shard_map.105 = (bf16[4,2,64,128]{3,2,1,0:T(8,128)(2,1)S(1)}, bf16[4,2,64,128]{3,2,1,0:T(8,128)(2,1)S(1)}) custom-call(bf16[4,2,64,128]{3,2,1,0:T(8,128)(2,1)S(1)} %get-tuple-element.77.refs_0_, bf16[4,2,64,128]{3,2,1,0:T(8,128)(2,1)S(1)} %collective-permute-done.3.refs_1_, bf16[4,2,64,128]{3,2,1,0:T(8,128)(2,1)S(1)} %collective-permute-done.4.refs_2_, ...), custom_call_target="tpu_custom_call" | custom-call | flops 1024 | bytes 1024 | tf_op jit(solution)/shard_map/pallas_call | solution.py:300
  42.1 1.3 %collective-permute-start.15 = (bf16[4,2,64,128]{3,2,1,0:T(8,128)(2,1)S(1)}, bf16[4,2,64,128]{3,2,1,0:T(8,128)(2,1)S(1)}, u32[]{:S(2)}, u32[]{:S(2)}) collective-permute-start(bf16[4,2,64,128]{3,2,1,0:T(8,128)(2,1)S(1)} %get-tuple-element.89), channel_id=1, source_target_pairs={{0,1},{1,2},{2,3},{3,4},{4,5},{5,6},{6,7},{8,9},{9,10},{10,11},{11... | collective-permute-start | bytes 393224 | tf_op jit(solution)/shard_map/ppermute | solution.py:59
  43.4 1.3 %collective-permute-start.16 = (bf16[4,2,64,128]{3,2,1,0:T(8,128)(2,1)S(1)}, bf16[4,2,64,128]{3,2,1,0:T(8,128)(2,1)S(1)}, u32[]{:S(2)}, u32[]{:S(2)}) collective-permute-start(bf16[4,2,64,128]{3,2,1,0:T(8,128)(2,1)S(1)} %get-tuple-element.90), channel_id=1, source_target_pairs={{1,0},{2,1},{3,2},{4,3},{5,4},{6,5},{7,6},{9,8},{10,9},{11,10},{12... | collective-permute-start | bytes 393224 | tf_op jit(solution)/shard_map/ppermute | solution.py:59
  44.7 3.7 %collective-permute-done.16.refs_9_ = bf16[4,2,64,128]{3,2,1,0:T(8,128)(2,1)S(1)} collective-permute-done((bf16[4,2,64,128]{3,2,1,0:T(8,128)(2,1)S(1)}, bf16[4,2,64,128]{3,2,1,0:T(8,128)(2,1)S(1)}, u32[]{:S(2)}, u32[]{:S(2)}) %collective-permute-start.16) | collective-permute-done | bytes 131104 | tf_op jit(solution)/shard_map/ppermute | solution.py:59
  48.4 1.0 %collective-permute-done.12 = bf16[6,4,32,2,128]{4,3,2,1,0:T(2,128)(2,1)S(1)} collective-permute-done((bf16[6,4,32,2,128]{4,3,2,1,0:T(2,128)(2,1)S(1)}, bf16[6,4,32,2,128]{4,3,2,1,0:T(2,128)(2,1)S(1)}, u32[]{:S(2)}, u32[]{:S(2)}) %collective-permute-start.12) | collective-permute-done | bytes 393248 | tf_op jit(solution)/shard_map/ppermute | solution.py:49
  49.4 6.8 %collective-permute-done.13 = bf16[6,4,32,2,128]{4,3,2,1,0:T(2,128)(2,1)S(1)} collective-permute-done((bf16[6,4,32,2,128]{4,3,2,1,0:T(2,128)(2,1)S(1)}, bf16[6,4,32,2,128]{4,3,2,1,0:T(2,128)(2,1)S(1)}, u32[]{:S(2)}, u32[]{:S(2)}) %collective-permute-start.13) | collective-permute-done | bytes 393248 | tf_op jit(solution)/shard_map/ppermute | solution.py:49
  56.3 0.0 copy-start.7
  56.3 1.6 %shard_map.106 = (bf16[3,4,64,128]{3,2,1,0:T(8,128)(2,1)S(1)}, bf16[3,4,64,128]{3,2,1,0:T(8,128)(2,1)S(1)}, bf16[3,4,64,128]{3,2,1,0:T(8,128)(2,1)S(1)}, bf16[3,4,64,128]{3,2,1,0:T(8,128)(2,1)S(1)}) custom-call(bf16[6,4,64,128]{3,2,1,0:T(8,128)(2,1)S(1)} %bitcast.24, bf16[6,4,64,128]{3,2,1,0:T(8,128)(2,1)S(1)} %bitcast.25, ...), custom_call_target="tpu_custom_call" | custom-call | flops 1024 | bytes 1024 | tf_op jit(solution)/shard_map/pallas_call | solution.py:250
  57.9 0.6 collective-permute-start.17
  58.5 1.2 %collective-permute-start.18 = (bf16[3,4,64,128]{3,2,1,0:T(8,128)(2,1)S(1)}, bf16[3,4,64,128]{3,2,1,0:T(8,128)(2,1)S(1)}, u32[]{:S(2)}, u32[]{:S(2)}) collective-permute-start(bf16[3,4,64,128]{3,2,1,0:T(8,128)(2,1)S(1)} %get-tuple-element.107), channel_id=1, source_target_pairs={{0,16},{8,24},{16,0},{24,8},{1,17},{9,25},{17,1},{25,9},{2,18},{10... | collective-permute-start | bytes 589832 | tf_op jit(solution)/shard_map/ppermute | solution.py:49
  59.7 1.8 %collective-permute-start.19 = (bf16[3,4,64,128]{3,2,1,0:T(8,128)(2,1)S(1)}, bf16[3,4,64,128]{3,2,1,0:T(8,128)(2,1)S(1)}, u32[]{:S(2)}, u32[]{:S(2)}) collective-permute-start(bf16[3,4,64,128]{3,2,1,0:T(8,128)(2,1)S(1)} %get-tuple-element.108), channel_id=1, source_target_pairs={{0,24},{8,16},{16,8},{24,0},{1,25},{9,17},{17,9},{25,1},{2,26},{10... | collective-permute-start | bytes 589832 | tf_op jit(solution)/shard_map/ppermute | solution.py:49
  61.4 6.6 %shard_map.107 = (f32[3072,128]{1,0:T(8,128)}, f32[3,16,64,128]{3,2,1,0:T(8,128)S(1)}) custom-call(bf16[4,2,64,128]{3,2,1,0:T(8,128)(2,1)S(1)} %get-tuple-element.77.refs_0_, bf16[4,2,64,128]{3,2,1,0:T(8,128)(2,1)S(1)} %collective-permute-done.3.refs_1_, bf16[4,2,64,128]{3,2,1,0:T(8,128)(2,1)S(1)} %collective-permute-done.4.refs_2_, ...), custom_call_target="tpu_custom_call" | custom-call | flops 1024 | bytes 1024 | tf_op jit(solution)/shard_map/pallas_call | solution.py:381
  68.0 1.3 %shard_map.108 = f32[3072,128]{1,0:T(8,128)} custom-call(bf16[3,4,64,128]{3,2,1,0:T(8,128)(2,1)S(1)} %get-tuple-element.105.refs_0_, bf16[3,4,64,128]{3,2,1,0:T(8,128)(2,1)S(1)} %collective-permute-done.17.refs_1_, bf16[3,4,64,128]{3,2,1,0:T(8,128)(2,1)S(1)} %collective-permute-done.18.refs_2_, bf16[3,4,64,128]{3,2,1,0:T(8,128)(2,1)S(1)} %collective-permute-done.19.refs_3_, ...), custom_call_target="tpu_custom_call" | custom-call | flops 1024 | bytes 1024 | tf_op jit(solution)/shard_map/pallas_call | solution.py:449
  (24 shorter events, 0.1 us)
Async XLA Ops:
  0.6 1.9 %copy-start = (bf16[12,32,2,2048]{3,2,1,0:T(2,128)(2,1)S(1)}, bf16[12,32,2,2048]{3,2,1,0:T(2,128)(2,1)}, u32[]{:S(2)}) copy-start(bf16[12,32,2,2048]{3,2,1,0:T(2,128)(2,1)} %fields_ref.15) | copy-start | bytes 9437188
  2.7 13.0 %collective-permute-start.7 = (bf16[6,2,32,2,128]{4,3,2,1,0:T(2,128)(2,1)S(1)}, bf16[6,2,32,2,128]{4,3,2,1,0:T(2,128)(2,1)S(1)}, u32[]{:S(2)}, u32[]{:S(2)}) collective-permute-start(bf16[6,2,32,2,128]{4,3,2,1,0:T(2,128)(2,1)S(1)} %shard_map.102), channel_id=1, source_target_pairs={{0,16},{8,24},{16,0},{24,8},{1,17},{9,25},{17,1},{25,9},{2,18},{10... | collective-permute-start | bytes 589832 | tf_op jit(solution)/shard_map/ppermute | solution.py:49
  5.9 13.1 %collective-permute-start.8 = (bf16[6,2,32,2,128]{4,3,2,1,0:T(2,128)(2,1)S(1)}, bf16[6,2,32,2,128]{4,3,2,1,0:T(2,128)(2,1)S(1)}, u32[]{:S(2)}, u32[]{:S(2)}) collective-permute-start(bf16[6,2,32,2,128]{4,3,2,1,0:T(2,128)(2,1)S(1)} %shard_map.103), channel_id=1, source_target_pairs={{0,24},{8,16},{16,8},{24,0},{1,25},{9,17},{17,9},{25,1},{2,26},{10... | collective-permute-start | bytes 589832 | tf_op jit(solution)/shard_map/ppermute | solution.py:49
  7.6 11.5 %collective-permute-start.6 = (bf16[6,2,32,2,128]{4,3,2,1,0:T(2,128)(2,1)S(1)}, bf16[6,2,32,2,128]{4,3,2,1,0:T(2,128)(2,1)S(1)}, u32[]{:S(2)}, u32[]{:S(2)}) collective-permute-start(bf16[6,2,32,2,128]{4,3,2,1,0:T(2,128)(2,1)S(1)} %shard_map.101), channel_id=1, source_target_pairs={{0,8},{8,0},{16,24},{24,16},{1,9},{9,1},{17,25},{25,17},{2,10},{10... | collective-permute-start | bytes 589832 | tf_op jit(solution)/shard_map/ppermute | solution.py:49
  7.9 12.6 %collective-permute-start.1 = (bf16[6,2,32,2,128]{4,3,2,1,0:T(2,128)(2,1)S(1)}, bf16[6,2,32,2,128]{4,3,2,1,0:T(2,128)(2,1)S(1)}, u32[]{:S(2)}, u32[]{:S(2)}) collective-permute-start(bf16[6,2,32,2,128]{4,3,2,1,0:T(2,128)(2,1)S(1)} %shard_map.97), channel_id=1, source_target_pairs={{0,16},{8,24},{16,0},{24,8},{1,17},{9,25},{17,1},{25,9},{2,18},{10... | collective-permute-start | bytes 589832 | tf_op jit(solution)/shard_map/ppermute | solution.py:49
  10.1 8.6 %copy-start.4 = (bf16[256,256]{1,0:T(8,128)(2,1)S(1)}, bf16[256,256]{1,0:T(8,128)(2,1)}, u32[]{:S(2)}) copy-start(bf16[256,256]{1,0:T(8,128)(2,1)} %constant.5.clone.refs_1_) | copy-start | bytes 393220
  10.1 8.6 %copy-start.5 = (bf16[256,256]{1,0:T(8,128)(2,1)S(1)}, bf16[256,256]{1,0:T(8,128)(2,1)}, u32[]{:S(2)}) copy-start(bf16[256,256]{1,0:T(8,128)(2,1)} %constant.4.clone.refs_0_) | copy-start | bytes 393220
  10.1 14.6 %collective-permute-start = (bf16[6,2,32,2,128]{4,3,2,1,0:T(2,128)(2,1)S(1)}, bf16[6,2,32,2,128]{4,3,2,1,0:T(2,128)(2,1)S(1)}, u32[]{:S(2)}, u32[]{:S(2)}) collective-permute-start(bf16[6,2,32,2,128]{4,3,2,1,0:T(2,128)(2,1)S(1)} %shard_map.96), channel_id=1, source_target_pairs={{0,8},{8,0},{16,24},{24,16},{1,9},{9,1},{17,25},{25,17},{2,10},{10... | collective-permute-start | bytes 589832 | tf_op jit(solution)/shard_map/ppermute | solution.py:49
  11.8 11.6 %copy-start.1 = (bf16[12,32,2,2048]{3,2,1,0:T(2,128)(2,1)S(1)}, bf16[12,32,2,2048]{3,2,1,0:T(2,128)(2,1)}, u32[]{:S(2)}) copy-start(bf16[12,32,2,2048]{3,2,1,0:T(2,128)(2,1)} %fields_ref.15) | copy-start | bytes 9437188
  15.7 11.7 %collective-permute-start.2 = (bf16[6,2,32,2,128]{4,3,2,1,0:T(2,128)(2,1)S(1)}, bf16[6,2,32,2,128]{4,3,2,1,0:T(2,128)(2,1)S(1)}, u32[]{:S(2)}, u32[]{:S(2)}) collective-permute-start(bf16[6,2,32,2,128]{4,3,2,1,0:T(2,128)(2,1)S(1)} %shard_map.98), channel_id=1, source_target_pairs={{0,24},{8,16},{16,8},{24,0},{1,25},{9,17},{17,9},{25,1},{2,26},{10... | collective-permute-start | bytes 589832 | tf_op jit(solution)/shard_map/ppermute | solution.py:49
  19.8 10.4 %collective-permute-start.9 = (bf16[4,2,64,128]{3,2,1,0:T(8,128)(2,1)S(1)}, bf16[4,2,64,128]{3,2,1,0:T(8,128)(2,1)S(1)}, u32[]{:S(2)}, u32[]{:S(2)}) collective-permute-start(bf16[4,2,64,128]{3,2,1,0:T(8,128)(2,1)S(1)} %get-tuple-element.70), channel_id=1, source_target_pairs={{0,8},{8,0},{16,24},{24,16},{1,9},{9,1},{17,25},{25,17},{2,10},{10... | collective-permute-start | bytes 393224 | tf_op jit(solution)/shard_map/ppermute | solution.py:49
  20.4 11.3 %collective-permute-start.10 = (bf16[4,2,64,128]{3,2,1,0:T(8,128)(2,1)S(1)}, bf16[4,2,64,128]{3,2,1,0:T(8,128)(2,1)S(1)}, u32[]{:S(2)}, u32[]{:S(2)}) collective-permute-start(bf16[4,2,64,128]{3,2,1,0:T(8,128)(2,1)S(1)} %get-tuple-element.71), channel_id=1, source_target_pairs={{0,16},{8,24},{16,0},{24,8},{1,17},{9,25},{17,1},{25,9},{2,18},{10... | collective-permute-start | bytes 393224 | tf_op jit(solution)/shard_map/ppermute | solution.py:49
  21.8 19.0 %copy-start.8 = (s32[2,256]{1,0:T(2,128)S(1)}, s32[2,256]{1,0:T(2,128)}, u32[]{:S(2)}) copy-start(s32[2,256]{1,0:T(2,128)} %refs_8_.1) | copy-start | bytes 6148
  21.8 11.1 %collective-permute-start.11 = (bf16[4,2,64,128]{3,2,1,0:T(8,128)(2,1)S(1)}, bf16[4,2,64,128]{3,2,1,0:T(8,128)(2,1)S(1)}, u32[]{:S(2)}, u32[]{:S(2)}) collective-permute-start(bf16[4,2,64,128]{3,2,1,0:T(8,128)(2,1)S(1)} %get-tuple-element.72), channel_id=1, source_target_pairs={{0,24},{8,16},{16,8},{24,0},{1,25},{9,17},{17,9},{25,1},{2,26},{10... | collective-permute-start | bytes 393224 | tf_op jit(solution)/shard_map/ppermute | solution.py:49
  28.2 6.4 %collective-permute-start.3 = (bf16[4,2,64,128]{3,2,1,0:T(8,128)(2,1)S(1)}, bf16[4,2,64,128]{3,2,1,0:T(8,128)(2,1)S(1)}, u32[]{:S(2)}, u32[]{:S(2)}) collective-permute-start(bf16[4,2,64,128]{3,2,1,0:T(8,128)(2,1)S(1)} %get-tuple-element.65), channel_id=1, source_target_pairs={{0,8},{8,0},{16,24},{24,16},{1,9},{9,1},{17,25},{25,17},{2,10},{10... | collective-permute-start | bytes 393224 | tf_op jit(solution)/shard_map/ppermute | solution.py:49
  29.8 7.6 %collective-permute-start.4 = (bf16[4,2,64,128]{3,2,1,0:T(8,128)(2,1)S(1)}, bf16[4,2,64,128]{3,2,1,0:T(8,128)(2,1)S(1)}, u32[]{:S(2)}, u32[]{:S(2)}) collective-permute-start(bf16[4,2,64,128]{3,2,1,0:T(8,128)(2,1)S(1)} %get-tuple-element.66), channel_id=1, source_target_pairs={{0,16},{8,24},{16,0},{24,8},{1,17},{9,25},{17,1},{25,9},{2,18},{10... | collective-permute-start | bytes 393224 | tf_op jit(solution)/shard_map/ppermute | solution.py:49
  30.3 7.1 %collective-permute-start.5 = (bf16[4,2,64,128]{3,2,1,0:T(8,128)(2,1)S(1)}, bf16[4,2,64,128]{3,2,1,0:T(8,128)(2,1)S(1)}, u32[]{:S(2)}, u32[]{:S(2)}) collective-permute-start(bf16[4,2,64,128]{3,2,1,0:T(8,128)(2,1)S(1)} %get-tuple-element.67), channel_id=1, source_target_pairs={{0,24},{8,16},{16,8},{24,0},{1,25},{9,17},{17,9},{25,1},{2,26},{10... | collective-permute-start | bytes 393224 | tf_op jit(solution)/shard_map/ppermute | solution.py:49
  37.4 12.1 %collective-permute-start.12 = (bf16[6,4,32,2,128]{4,3,2,1,0:T(2,128)(2,1)S(1)}, bf16[6,4,32,2,128]{4,3,2,1,0:T(2,128)(2,1)S(1)}, u32[]{:S(2)}, u32[]{:S(2)}) collective-permute-start(bf16[6,4,32,2,128]{4,3,2,1,0:T(2,128)(2,1)S(1)} %get-tuple-element.86), channel_id=1, source_target_pairs={{0,8},{8,0},{16,24},{24,16},{1,9},{9,1},{17,25},{25,17},{2,10},{10... | collective-permute-start | bytes 1179656 | tf_op jit(solution)/shard_map/ppermute | solution.py:49
  38.7 17.6 %collective-permute-start.13 = (bf16[6,4,32,2,128]{4,3,2,1,0:T(2,128)(2,1)S(1)}, bf16[6,4,32,2,128]{4,3,2,1,0:T(2,128)(2,1)S(1)}, u32[]{:S(2)}, u32[]{:S(2)}) collective-permute-start(bf16[6,4,32,2,128]{4,3,2,1,0:T(2,128)(2,1)S(1)} %get-tuple-element.87), channel_id=1, source_target_pairs={{0,16},{8,24},{16,0},{24,8},{1,17},{9,25},{17,1},{25,9},{2,18},{10... | collective-permute-start | bytes 1179656 | tf_op jit(solution)/shard_map/ppermute | solution.py:49
  39.2 17.1 %collective-permute-start.14 = (bf16[6,4,32,2,128]{4,3,2,1,0:T(2,128)(2,1)S(1)}, bf16[6,4,32,2,128]{4,3,2,1,0:T(2,128)(2,1)S(1)}, u32[]{:S(2)}, u32[]{:S(2)}) collective-permute-start(bf16[6,4,32,2,128]{4,3,2,1,0:T(2,128)(2,1)S(1)} %get-tuple-element.88), channel_id=1, source_target_pairs={{0,24},{8,16},{16,8},{24,0},{1,25},{9,17},{17,9},{25,1},{2,26},{10... | collective-permute-start | bytes 1179656 | tf_op jit(solution)/shard_map/ppermute | solution.py:49
  42.1 2.6 %collective-permute-start.15 = (bf16[4,2,64,128]{3,2,1,0:T(8,128)(2,1)S(1)}, bf16[4,2,64,128]{3,2,1,0:T(8,128)(2,1)S(1)}, u32[]{:S(2)}, u32[]{:S(2)}) collective-permute-start(bf16[4,2,64,128]{3,2,1,0:T(8,128)(2,1)S(1)} %get-tuple-element.89), channel_id=1, source_target_pairs={{0,1},{1,2},{2,3},{3,4},{4,5},{5,6},{6,7},{8,9},{9,10},{10,11},{11... | collective-permute-start | bytes 393224 | tf_op jit(solution)/shard_map/ppermute | solution.py:59
  43.4 5.0 %collective-permute-start.16 = (bf16[4,2,64,128]{3,2,1,0:T(8,128)(2,1)S(1)}, bf16[4,2,64,128]{3,2,1,0:T(8,128)(2,1)S(1)}, u32[]{:S(2)}, u32[]{:S(2)}) collective-permute-start(bf16[4,2,64,128]{3,2,1,0:T(8,128)(2,1)S(1)} %get-tuple-element.90), channel_id=1, source_target_pairs={{1,0},{2,1},{3,2},{4,3},{5,4},{6,5},{7,6},{9,8},{10,9},{11,10},{12... | collective-permute-start | bytes 393224 | tf_op jit(solution)/shard_map/ppermute | solution.py:59
  56.2 5.2 %copy-start.2 = (bf16[5,64,2048]{2,1,0:T(8,128)(2,1)S(1)}, bf16[5,64,2048]{2,1,0:T(8,128)(2,1)}, u32[]{:S(2)}) copy-start(bf16[5,64,2048]{2,1,0:T(8,128)(2,1)} %refs_10_.1) | copy-start | bytes 3932164
  56.2 5.2 %copy-start.3 = (bf16[5,64,2048]{2,1,0:T(8,128)(2,1)S(1)}, bf16[5,64,2048]{2,1,0:T(8,128)(2,1)}, u32[]{:S(2)}) copy-start(bf16[5,64,2048]{2,1,0:T(8,128)(2,1)} %refs_11_.1) | copy-start | bytes 3932164
  56.2 5.2 %copy-start.6 = (f32[2048]{0:T(1024)S(1)}, f32[2048]{0:T(1024)}, u32[]{:S(2)}) copy-start(f32[2048]{0:T(1024)} %param.9) | copy-start | bytes 24580
  56.3 5.2 %copy-start.7 = (s32[32,5]{0,1:T(8,128)S(1)}, s32[32,5]{0,1:T(8,128)}, u32[]{:S(2)}) copy-start(s32[32,5]{0,1:T(8,128)} %param.12) | copy-start | bytes 1924
  57.9 10.2 %collective-permute-start.17 = (bf16[3,4,64,128]{3,2,1,0:T(8,128)(2,1)S(1)}, bf16[3,4,64,128]{3,2,1,0:T(8,128)(2,1)S(1)}, u32[]{:S(2)}, u32[]{:S(2)}) collective-permute-start(bf16[3,4,64,128]{3,2,1,0:T(8,128)(2,1)S(1)} %get-tuple-element.106), channel_id=1, source_target_pairs={{0,8},{8,0},{16,24},{24,16},{1,9},{9,1},{17,25},{25,17},{2,10},{10... | collective-permute-start | bytes 589832 | tf_op jit(solution)/shard_map/ppermute | solution.py:49
  58.5 9.6 %collective-permute-start.18 = (bf16[3,4,64,128]{3,2,1,0:T(8,128)(2,1)S(1)}, bf16[3,4,64,128]{3,2,1,0:T(8,128)(2,1)S(1)}, u32[]{:S(2)}, u32[]{:S(2)}) collective-permute-start(bf16[3,4,64,128]{3,2,1,0:T(8,128)(2,1)S(1)} %get-tuple-element.107), channel_id=1, source_target_pairs={{0,16},{8,24},{16,0},{24,8},{1,17},{9,25},{17,1},{25,9},{2,18},{10... | collective-permute-start | bytes 589832 | tf_op jit(solution)/shard_map/ppermute | solution.py:49
  59.7 8.4 %collective-permute-start.19 = (bf16[3,4,64,128]{3,2,1,0:T(8,128)(2,1)S(1)}, bf16[3,4,64,128]{3,2,1,0:T(8,128)(2,1)S(1)}, u32[]{:S(2)}, u32[]{:S(2)}) collective-permute-start(bf16[3,4,64,128]{3,2,1,0:T(8,128)(2,1)S(1)} %get-tuple-element.108), channel_id=1, source_target_pairs={{0,24},{8,16},{16,8},{24,0},{1,25},{9,17},{17,9},{25,1},{2,26},{10... | collective-permute-start | bytes 589832 | tf_op jit(solution)/shard_map/ppermute | solution.py:49

commit v8 on v7

--- a/solution.py
+++ b/solution.py
@@ -51,6 +51,13 @@
 
 def exchange(pieces):
     return [send(piece, step) for step, piece in enumerate(pieces, 1)]
+
+
+def swap(piece, step):
+    count = lax.axis_size("mode")
+    pairs = [[i, i ^ step] for i in range(count) if i < i ^ step]
+    both = lax.all_gather(piece.reshape(-1, LANES), "mode", axis_index_groups=pairs)
+    return both.reshape((2,) + piece.shape)
 
 
 def from_behind(value, axis, steps):
@@ -220,7 +227,10 @@
 
 
 def second_kernel(count, groups, *refs):
-    in_refs, refs = refs[:count], refs[count:]
+    me = lax.axis_index("mode")
+    in_refs, refs = list(refs[:count]), refs[count:]
+    for step in range(1, count):
+        in_refs[step] = in_refs[step].at[(jnp.bitwise_xor(me, step) > me).astype(jnp.int32)]
     first_refs, (inverse_ref, forward_ref) = refs[:groups], refs[groups : groups + 2]
     out_refs, (physical_ref, x_ref, product_ref, table_ref) = refs[groups + 2 : groups + 2 + count], refs[groups + 2 + count :]
     width = first_refs[0].shape[2]
@@ -491,7 +501,7 @@
         local += terms[:1] + exchange(terms[1:])
         physical.append(velocity_magnetic)
     local, shares = lax.optimization_barrier((local, shares))
-    sources = shares[:1] + exchange(shares[1:])
+    sources = shares[:1] + [swap(share, step) for step, share in enumerate(shares[1:], 1)]
     toward_prev, toward_next = interface(local, interface_nodes, count)
     halos = (from_behind(toward_next, "mer", 1), from_behind(toward_prev, "mer", -1))
     sources, halos = lax.optimization_barrier((sources, halos))

time: 69.5 us -> 87.9 us (1.26)
  the two profiles are of different devices: /device:TPU:0 before, /device:TPU:1 now
where the time goes in v8:
time: 87.9 us; the launch traced here: 86.6 us
  blocking collectives  27.3 us (31%)
  starting transfers between devices  26.7 us (30%)
  Pallas kernels  15 us (17%)
  waiting for transfers between devices  14.8 us (17%)
  local copies, waits for them, and re-layouts  1.92 us (2%)
    all_gather x3, blocking collectives, swap(): lax.all_gather(piece.reshape(-1, LANES), 'mode', axis_index_groups=pairs)  27.3 us
    ppermute x15, starting transfers between devices, send(): return lax.ppermute(piece, 'mode', pairs)  17.4 us
    ppermute x15, waiting for transfers between devices, send(): return lax.ppermute(piece, 'mode', pairs)  14.8 us
    ppermute x2, starting transfers between devices, from_behind(): lax.ppermute(value, axis, [(source, source + steps) for source in range(i...  9.33 us
    pallas_call x1, Pallas kernels, derive(): pl.pallas_call(functools.partial(derive_kernel, count, len(received)), in...  6.59 us
    unnamed x16, local copies, waits for them, and re-layouts  1.92 us
  transfers between devices with their start and end apart: 17, of which 7 were waited for; matrix products, arithmetic and copies ran while one was open for 0% of the time, Pallas kernels for 12%

profile of v8, /device:TPU:1, one launch (start us, length us, event | category | flops | bytes accessed | tf_op | source)
XLA Modules:
  0.0 86.6 jit_solution(4461239703254081426)
XLA Ops:
  0.6 1.9 %copy-done = bf16[12,32,2,2048]{3,2,1,0:T(2,128)(2,1)S(1)} copy-done((bf16[12,32,2,2048]{3,2,1,0:T(2,128)(2,1)S(1)}, bf16[12,32,2,2048]{3,2,1,0:T(2,128)(2,1)}, u32[]{:S(2)}) %copy-start) | copy-done | bytes 3145752
  2.5 0.2 shard_map.97
  2.7 2.1 %collective-permute-start.1 = (bf16[6,2,32,2,128]{4,3,2,1,0:T(2,128)(2,1)S(1)}, bf16[6,2,32,2,128]{4,3,2,1,0:T(2,128)(2,1)S(1)}, u32[]{:S(2)}, u32[]{:S(2)}) collective-permute-start(bf16[6,2,32,2,128]{4,3,2,1,0:T(2,128)(2,1)S(1)} %shard_map.97), channel_id=1, source_target_pairs={{0,16},{8,24},{16,0},{24,8},{1,17},{9,25},{17,1},{25,9},{2,18},{10... | collective-permute-start | bytes 589832 | tf_op jit(solution)/shard_map/ppermute | solution.py:49
  4.8 0.2 shard_map.96
  5.0 1.3 %collective-permute-start = (bf16[6,2,32,2,128]{4,3,2,1,0:T(2,128)(2,1)S(1)}, bf16[6,2,32,2,128]{4,3,2,1,0:T(2,128)(2,1)S(1)}, u32[]{:S(2)}, u32[]{:S(2)}) collective-permute-start(bf16[6,2,32,2,128]{4,3,2,1,0:T(2,128)(2,1)S(1)} %shard_map.96), channel_id=1, source_target_pairs={{0,8},{8,0},{16,24},{24,16},{1,9},{9,1},{17,25},{25,17},{2,10},{10... | collective-permute-start | bytes 589832 | tf_op jit(solution)/shard_map/ppermute | solution.py:49
  6.3 0.2 shard_map.98
  6.4 0.1 collective-permute-start.2
  6.5 0.2 shard_map.101
  6.7 1.4 %collective-permute-start.6 = (bf16[6,2,32,2,128]{4,3,2,1,0:T(2,128)(2,1)S(1)}, bf16[6,2,32,2,128]{4,3,2,1,0:T(2,128)(2,1)S(1)}, u32[]{:S(2)}, u32[]{:S(2)}) collective-permute-start(bf16[6,2,32,2,128]{4,3,2,1,0:T(2,128)(2,1)S(1)} %shard_map.101), channel_id=1, source_target_pairs={{0,8},{8,0},{16,24},{24,16},{1,9},{9,1},{17,25},{25,17},{2,10},{10... | collective-permute-start | bytes 589832 | tf_op jit(solution)/shard_map/ppermute | solution.py:49
  8.1 0.2 shard_map.102
  8.3 0.0 copy-start.3
  8.3 0.0 copy-start.4
  8.3 1.3 %collective-permute-start.7 = (bf16[6,2,32,2,128]{4,3,2,1,0:T(2,128)(2,1)S(1)}, bf16[6,2,32,2,128]{4,3,2,1,0:T(2,128)(2,1)S(1)}, u32[]{:S(2)}, u32[]{:S(2)}) collective-permute-start(bf16[6,2,32,2,128]{4,3,2,1,0:T(2,128)(2,1)S(1)} %shard_map.102), channel_id=1, source_target_pairs={{0,16},{8,24},{16,0},{24,8},{1,17},{9,25},{17,1},{25,9},{2,18},{10... | collective-permute-start | bytes 589832 | tf_op jit(solution)/shard_map/ppermute | solution.py:49
  9.6 0.2 shard_map.103
  9.8 1.7 %collective-permute-start.8 = (bf16[6,2,32,2,128]{4,3,2,1,0:T(2,128)(2,1)S(1)}, bf16[6,2,32,2,128]{4,3,2,1,0:T(2,128)(2,1)S(1)}, u32[]{:S(2)}, u32[]{:S(2)}) collective-permute-start(bf16[6,2,32,2,128]{4,3,2,1,0:T(2,128)(2,1)S(1)} %shard_map.103), channel_id=1, source_target_pairs={{0,24},{8,16},{16,8},{24,0},{1,25},{9,17},{17,9},{25,1},{2,26},{10... | collective-permute-start | bytes 589832 | tf_op jit(solution)/shard_map/ppermute | solution.py:49
  11.5 0.3 shard_map.95
  11.9 1.3 %shard_map.99 = (bf16[6,4,32,2,128]{4,3,2,1,0:T(2,128)(2,1)S(1)}, bf16[6,4,32,2,128]{4,3,2,1,0:T(2,128)(2,1)S(1)}, bf16[6,4,32,2,128]{4,3,2,1,0:T(2,128)(2,1)S(1...) custom-call(bf16[12,32,2,2048]{3,2,1,0:T(2,128)(2,1)S(1)} %copy-done, ...), custom_call_target="tpu_custom_call" | custom-call | flops 1024 | bytes 1024 | tf_op jit(solution)/shard_map/pallas_call | solution.py:146
  13.2 0.0 collective-permute-done
  13.2 1.6 %collective-permute-done.2 = bf16[6,2,32,2,128]{4,3,2,1,0:T(2,128)(2,1)S(1)} collective-permute-done((bf16[6,2,32,2,128]{4,3,2,1,0:T(2,128)(2,1)S(1)}, bf16[6,2,32,2,128]{4,3,2,1,0:T(2,128)(2,1)S(1)}, u32[]{:S(2)}, u32[]{:S(2)}) %collective-permute-start.2) | collective-permute-done | bytes 196640 | tf_op jit(solution)/shard_map/ppermute | solution.py:49
  14.8 0.8 shard_map.100
  15.7 1.2 %collective-permute-start.3 = (bf16[4,2,64,128]{3,2,1,0:T(8,128)(2,1)S(1)}, bf16[4,2,64,128]{3,2,1,0:T(8,128)(2,1)S(1)}, u32[]{:S(2)}, u32[]{:S(2)}) collective-permute-start(bf16[4,2,64,128]{3,2,1,0:T(8,128)(2,1)S(1)} %get-tuple-element.65), channel_id=1, source_target_pairs={{0,8},{8,0},{16,24},{24,16},{1,9},{9,1},{17,25},{25,17},{2,10},{10... | collective-permute-start | bytes 393224 | tf_op jit(solution)/shard_map/ppermute | solution.py:49
  16.8 1.2 %collective-permute-start.4 = (bf16[4,2,64,128]{3,2,1,0:T(8,128)(2,1)S(1)}, bf16[4,2,64,128]{3,2,1,0:T(8,128)(2,1)S(1)}, u32[]{:S(2)}, u32[]{:S(2)}) collective-permute-start(bf16[4,2,64,128]{3,2,1,0:T(8,128)(2,1)S(1)} %get-tuple-element.66), channel_id=1, source_target_pairs={{0,16},{8,24},{16,0},{24,8},{1,17},{9,25},{17,1},{25,9},{2,18},{10... | collective-permute-start | bytes 393224 | tf_op jit(solution)/shard_map/ppermute | solution.py:49
  18.0 0.9 %collective-permute-done.6 = bf16[6,2,32,2,128]{4,3,2,1,0:T(2,128)(2,1)S(1)} collective-permute-done((bf16[6,2,32,2,128]{4,3,2,1,0:T(2,128)(2,1)S(1)}, bf16[6,2,32,2,128]{4,3,2,1,0:T(2,128)(2,1)S(1)}, u32[]{:S(2)}, u32[]{:S(2)}) %collective-permute-start.6) | collective-permute-done | bytes 196640 | tf_op jit(solution)/shard_map/ppermute | solution.py:49
  19.0 1.2 %collective-permute-start.5 = (bf16[4,2,64,128]{3,2,1,0:T(8,128)(2,1)S(1)}, bf16[4,2,64,128]{3,2,1,0:T(8,128)(2,1)S(1)}, u32[]{:S(2)}, u32[]{:S(2)}) collective-permute-start(bf16[4,2,64,128]{3,2,1,0:T(8,128)(2,1)S(1)} %get-tuple-element.67), channel_id=1, source_target_pairs={{0,24},{8,16},{16,8},{24,0},{1,25},{9,17},{17,9},{25,1},{2,26},{10... | collective-permute-start | bytes 393224 | tf_op jit(solution)/shard_map/ppermute | solution.py:49
  20.1 3.2 %collective-permute-done.8 = bf16[6,2,32,2,128]{4,3,2,1,0:T(2,128)(2,1)S(1)} collective-permute-done((bf16[6,2,32,2,128]{4,3,2,1,0:T(2,128)(2,1)S(1)}, bf16[6,2,32,2,128]{4,3,2,1,0:T(2,128)(2,1)S(1)}, u32[]{:S(2)}, u32[]{:S(2)}) %collective-permute-start.8) | collective-permute-done | bytes 196640 | tf_op jit(solution)/shard_map/ppermute | solution.py:49
  23.3 0.8 shard_map.104
  24.1 1.1 %collective-permute-start.9 = (bf16[4,2,64,128]{3,2,1,0:T(8,128)(2,1)S(1)}, bf16[4,2,64,128]{3,2,1,0:T(8,128)(2,1)S(1)}, u32[]{:S(2)}, u32[]{:S(2)}) collective-permute-start(bf16[4,2,64,128]{3,2,1,0:T(8,128)(2,1)S(1)} %get-tuple-element.70), channel_id=1, source_target_pairs={{0,8},{8,0},{16,24},{24,16},{1,9},{9,1},{17,25},{25,17},{2,10},{10... | collective-permute-start | bytes 393224 | tf_op jit(solution)/shard_map/ppermute | solution.py:49
  25.2 1.2 %collective-permute-start.10 = (bf16[4,2,64,128]{3,2,1,0:T(8,128)(2,1)S(1)}, bf16[4,2,64,128]{3,2,1,0:T(8,128)(2,1)S(1)}, u32[]{:S(2)}, u32[]{:S(2)}) collective-permute-start(bf16[4,2,64,128]{3,2,1,0:T(8,128)(2,1)S(1)} %get-tuple-element.71), channel_id=1, source_target_pairs={{0,16},{8,24},{16,0},{24,8},{1,17},{9,25},{17,1},{25,9},{2,18},{10... | collective-permute-start | bytes 393224 | tf_op jit(solution)/shard_map/ppermute | solution.py:49
  26.5 0.7 collective-permute-start.11
  27.2 1.8 %collective-permute-done.5.refs_3_ = bf16[4,2,64,128]{3,2,1,0:T(8,128)(2,1)S(1)} collective-permute-done((bf16[4,2,64,128]{3,2,1,0:T(8,128)(2,1)S(1)}, bf16[4,2,64,128]{3,2,1,0:T(8,128)(2,1)S(1)}, u32[]{:S(2)}, u32[]{:S(2)}) %collective-permute-start.5) | collective-permute-done | bytes 131104 | tf_op jit(solution)/shard_map/ppermute | solution.py:49
  28.9 2.5 %collective-permute-done.9.refs_5_ = bf16[4,2,64,128]{3,2,1,0:T(8,128)(2,1)S(1)} collective-permute-done((bf16[4,2,64,128]{3,2,1,0:T(8,128)(2,1)S(1)}, bf16[4,2,64,128]{3,2,1,0:T(8,128)(2,1)S(1)}, u32[]{:S(2)}, u32[]{:S(2)}) %collective-permute-start.9) | collective-permute-done | bytes 131104 | tf_op jit(solution)/shard_map/ppermute | solution.py:49
  31.4 2.5 %collective-permute-done.11.refs_7_ = bf16[4,2,64,128]{3,2,1,0:T(8,128)(2,1)S(1)} collective-permute-done((bf16[4,2,64,128]{3,2,1,0:T(8,128)(2,1)S(1)}, bf16[4,2,64,128]{3,2,1,0:T(8,128)(2,1)S(1)}, u32[]{:S(2)}, u32[]{:S(2)}) %collective-permute-start.11) | collective-permute-done | bytes 131104 | tf_op jit(solution)/shard_map/ppermute | solution.py:49
  33.8 8.8 %all_gather.9 = bf16[2,1536,128]{2,1,0:T(8,128)(2,1)S(1)} all-gather(bf16[1,1536,128]{2,1,0:T(8,128)(2,1)S(1)} %bitcast.36), channel_id=1, replica_groups={{0,8},{16,24},{1,9},{17,25},{2,10},{18,26},{3,11},{19,27},{4,12},{20,28..., dimensions={0}, use_global_device_ids=true | all-gather | bytes 1179648 | tf_op jit(solution)/shard_map/all_gather | solution.py:59
  42.7 8.3 %all_gather.10 = bf16[2,1536,128]{2,1,0:T(8,128)(2,1)S(1)} all-gather(bf16[1,1536,128]{2,1,0:T(8,128)(2,1)S(1)} %bitcast.35), channel_id=1, replica_groups={{0,16},{8,24},{1,17},{9,25},{2,18},{10,26},{3,19},{11,27},{4,20},{12,28..., dimensions={0}, use_global_device_ids=true | all-gather | bytes 1179648 | tf_op jit(solution)/shard_map/all_gather | solution.py:59
  51.0 1.2 %shard_map.105 = (bf16[4,2,64,128]{3,2,1,0:T(8,128)(2,1)S(1)}, bf16[4,2,64,128]{3,2,1,0:T(8,128)(2,1)S(1)}) custom-call(bf16[4,2,64,128]{3,2,1,0:T(8,128)(2,1)S(1)} %get-tuple-element.77.refs_0_, bf16[4,2,64,128]{3,2,1,0:T(8,128)(2,1)S(1)} %collective-permute-done.3.refs_1_, bf16[4,2,64,128]{3,2,1,0:T(8,128)(2,1)S(1)} %collective-permute-done.4.refs_2_, ...), custom_call_target="tpu_custom_call" | custom-call | flops 1024 | bytes 1024 | tf_op jit(solution)/shard_map/pallas_call | solution.py:310
  52.2 7.4 %collective-permute-start.12 = (bf16[4,2,64,128]{3,2,1,0:T(8,128)(2,1)S(1)}, bf16[4,2,64,128]{3,2,1,0:T(8,128)(2,1)S(1)}, u32[]{:S(2)}, u32[]{:S(2)}) collective-permute-start(bf16[4,2,64,128]{3,2,1,0:T(8,128)(2,1)S(1)} %get-tuple-element.89), channel_id=1, source_target_pairs={{0,1},{1,2},{2,3},{3,4},{4,5},{5,6},{6,7},{8,9},{9,10},{10,11},{11... | collective-permute-start | bytes 393224 | tf_op jit(solution)/shard_map/ppermute | solution.py:66
  59.6 1.9 %collective-permute-start.13 = (bf16[4,2,64,128]{3,2,1,0:T(8,128)(2,1)S(1)}, bf16[4,2,64,128]{3,2,1,0:T(8,128)(2,1)S(1)}, u32[]{:S(2)}, u32[]{:S(2)}) collective-permute-start(bf16[4,2,64,128]{3,2,1,0:T(8,128)(2,1)S(1)} %get-tuple-element.90), channel_id=1, source_target_pairs={{1,0},{2,1},{3,2},{4,3},{5,4},{6,5},{7,6},{9,8},{10,9},{11,10},{12... | collective-permute-start | bytes 393224 | tf_op jit(solution)/shard_map/ppermute | solution.py:66
  61.5 10.2 %all_gather.11 = bf16[2,1536,128]{2,1,0:T(8,128)(2,1)S(1)} all-gather(bf16[1,1536,128]{2,1,0:T(8,128)(2,1)S(1)} %bitcast.34), channel_id=1, replica_groups={{0,24},{8,16},{1,25},{9,17},{2,26},{10,18},{3,27},{11,19},{4,28},{12,20..., dimensions={0}, use_global_device_ids=true | all-gather | bytes 1179648 | tf_op jit(solution)/shard_map/all_gather | solution.py:59
  71.8 0.0 copy-start.2
  71.8 0.0 copy-start.5
  71.8 0.0 copy-start.6
  71.8 1.6 %shard_map.106 = (bf16[3,4,64,128]{3,2,1,0:T(8,128)(2,1)S(1)}, bf16[3,4,64,128]{3,2,1,0:T(8,128)(2,1)S(1)}, bf16[3,4,64,128]{3,2,1,0:T(8,128)(2,1)S(1)}, bf16[3,4,64,128]{3,2,1,0:T(8,128)(2,1)S(1)}) custom-call(bf16[6,4,64,128]{3,2,1,0:T(8,128)(2,1)S(1)} %bitcast.33, bf16[2,6,4,64,128]{4,3,2,1,0:T(8,128)(2,1)S(1)} %bitcast.30, ...), custom_call_target="tpu_custom_call" | custom-call | flops 1024 | bytes 1024 | tf_op jit(solution)/shard_map/pallas_call | solution.py:260
  73.4 1.6 %collective-permute-start.14 = (bf16[3,4,64,128]{3,2,1,0:T(8,128)(2,1)S(1)}, bf16[3,4,64,128]{3,2,1,0:T(8,128)(2,1)S(1)}, u32[]{:S(2)}, u32[]{:S(2)}) collective-permute-start(bf16[3,4,64,128]{3,2,1,0:T(8,128)(2,1)S(1)} %get-tuple-element.106), channel_id=1, source_target_pairs={{0,8},{8,0},{16,24},{24,16},{1,9},{9,1},{17,25},{25,17},{2,10},{10... | collective-permute-start | bytes 589832 | tf_op jit(solution)/shard_map/ppermute | solution.py:49
  75.0 1.2 %collective-permute-start.15 = (bf16[3,4,64,128]{3,2,1,0:T(8,128)(2,1)S(1)}, bf16[3,4,64,128]{3,2,1,0:T(8,128)(2,1)S(1)}, u32[]{:S(2)}, u32[]{:S(2)}) collective-permute-start(bf16[3,4,64,128]{3,2,1,0:T(8,128)(2,1)S(1)} %get-tuple-element.107), channel_id=1, source_target_pairs={{0,16},{8,24},{16,0},{24,8},{1,17},{9,25},{17,1},{25,9},{2,18},{10... | collective-permute-start | bytes 589832 | tf_op jit(solution)/shard_map/ppermute | solution.py:49
  76.3 0.0 collective-permute-start.16
  76.3 6.6 %shard_map.107 = (f32[3072,128]{1,0:T(8,128)}, f32[3,16,64,128]{3,2,1,0:T(8,128)S(1)}) custom-call(bf16[4,2,64,128]{3,2,1,0:T(8,128)(2,1)S(1)} %get-tuple-element.77.refs_0_, bf16[4,2,64,128]{3,2,1,0:T(8,128)(2,1)S(1)} %collective-permute-done.3.refs_1_, bf16[4,2,64,128]{3,2,1,0:T(8,128)(2,1)S(1)} %collective-permute-done.4.refs_2_, ...), custom_call_target="tpu_custom_call" | custom-call | flops 1024 | bytes 1024 | tf_op jit(solution)/shard_map/pallas_call | solution.py:391
  82.9 2.4 %collective-permute-done.15.refs_2_ = bf16[3,4,64,128]{3,2,1,0:T(8,128)(2,1)S(1)} collective-permute-done((bf16[3,4,64,128]{3,2,1,0:T(8,128)(2,1)S(1)}, bf16[3,4,64,128]{3,2,1,0:T(8,128)(2,1)S(1)}, u32[]{:S(2)}, u32[]{:S(2)}) %collective-permute-start.15) | collective-permute-done | bytes 196640 | tf_op jit(solution)/shard_map/ppermute | solution.py:49
  85.3 1.3 %shard_map.108 = f32[3072,128]{1,0:T(8,128)} custom-call(bf16[3,4,64,128]{3,2,1,0:T(8,128)(2,1)S(1)} %get-tuple-element.105.refs_0_, bf16[3,4,64,128]{3,2,1,0:T(8,128)(2,1)S(1)} %collective-permute-done.14.refs_1_, bf16[3,4,64,128]{3,2,1,0:T(8,128)(2,1)S(1)} %collective-permute-done.15.refs_2_, bf16[3,4,64,128]{3,2,1,0:T(8,128)(2,1)S(1)} %collective-permute-done.16.refs_3_, ...), custom_call_target="tpu_custom_call" | custom-call | flops 1024 | bytes 1024 | tf_op jit(solution)/shard_map/pallas_call | solution.py:459
  (19 shorter events, 0.0 us)
Async XLA Ops:
  0.6 1.9 %copy-start = (bf16[12,32,2,2048]{3,2,1,0:T(2,128)(2,1)S(1)}, bf16[12,32,2,2048]{3,2,1,0:T(2,128)(2,1)}, u32[]{:S(2)}) copy-start(bf16[12,32,2,2048]{3,2,1,0:T(2,128)(2,1)} %fields_ref.15) | copy-start | bytes 9437188
  2.7 7.1 %collective-permute-start.1 = (bf16[6,2,32,2,128]{4,3,2,1,0:T(2,128)(2,1)S(1)}, bf16[6,2,32,2,128]{4,3,2,1,0:T(2,128)(2,1)S(1)}, u32[]{:S(2)}, u32[]{:S(2)}) collective-permute-start(bf16[6,2,32,2,128]{4,3,2,1,0:T(2,128)(2,1)S(1)} %shard_map.97), channel_id=1, source_target_pairs={{0,16},{8,24},{16,0},{24,8},{1,17},{9,25},{17,1},{25,9},{2,18},{10... | collective-permute-start | bytes 589832 | tf_op jit(solution)/shard_map/ppermute | solution.py:49
  5.0 8.2 %collective-permute-start = (bf16[6,2,32,2,128]{4,3,2,1,0:T(2,128)(2,1)S(1)}, bf16[6,2,32,2,128]{4,3,2,1,0:T(2,128)(2,1)S(1)}, u32[]{:S(2)}, u32[]{:S(2)}) collective-permute-start(bf16[6,2,32,2,128]{4,3,2,1,0:T(2,128)(2,1)S(1)} %shard_map.96), channel_id=1, source_target_pairs={{0,8},{8,0},{16,24},{24,16},{1,9},{9,1},{17,25},{25,17},{2,10},{10... | collective-permute-start | bytes 589832 | tf_op jit(solution)/shard_map/ppermute | solution.py:49
  6.4 8.4 %collective-permute-start.2 = (bf16[6,2,32,2,128]{4,3,2,1,0:T(2,128)(2,1)S(1)}, bf16[6,2,32,2,128]{4,3,2,1,0:T(2,128)(2,1)S(1)}, u32[]{:S(2)}, u32[]{:S(2)}) collective-permute-start(bf16[6,2,32,2,128]{4,3,2,1,0:T(2,128)(2,1)S(1)} %shard_map.98), channel_id=1, source_target_pairs={{0,24},{8,16},{16,8},{24,0},{1,25},{9,17},{17,9},{25,1},{2,26},{10... | collective-permute-start | bytes 589832 | tf_op jit(solution)/shard_map/ppermute | solution.py:49
  6.7 12.3 %collective-permute-start.6 = (bf16[6,2,32,2,128]{4,3,2,1,0:T(2,128)(2,1)S(1)}, bf16[6,2,32,2,128]{4,3,2,1,0:T(2,128)(2,1)S(1)}, u32[]{:S(2)}, u32[]{:S(2)}) collective-permute-start(bf16[6,2,32,2,128]{4,3,2,1,0:T(2,128)(2,1)S(1)} %shard_map.101), channel_id=1, source_target_pairs={{0,8},{8,0},{16,24},{24,16},{1,9},{9,1},{17,25},{25,17},{2,10},{10... | collective-permute-start | bytes 589832 | tf_op jit(solution)/shard_map/ppermute | solution.py:49
  8.3 3.2 %copy-start.3 = (bf16[256,256]{1,0:T(8,128)(2,1)S(1)}, bf16[256,256]{1,0:T(8,128)(2,1)}, u32[]{:S(2)}) copy-start(bf16[256,256]{1,0:T(8,128)(2,1)} %constant.4.clone.refs_0_) | copy-start | bytes 393220
  8.3 3.2 %copy-start.4 = (bf16[256,256]{1,0:T(8,128)(2,1)S(1)}, bf16[256,256]{1,0:T(8,128)(2,1)}, u32[]{:S(2)}) copy-start(bf16[256,256]{1,0:T(8,128)(2,1)} %constant.5.clone.refs_1_) | copy-start | bytes 393220
  8.3 11.8 %collective-permute-start.7 = (bf16[6,2,32,2,128]{4,3,2,1,0:T(2,128)(2,1)S(1)}, bf16[6,2,32,2,128]{4,3,2,1,0:T(2,128)(2,1)S(1)}, u32[]{:S(2)}, u32[]{:S(2)}) collective-permute-start(bf16[6,2,32,2,128]{4,3,2,1,0:T(2,128)(2,1)S(1)} %shard_map.102), channel_id=1, source_target_pairs={{0,16},{8,24},{16,0},{24,8},{1,17},{9,25},{17,1},{25,9},{2,18},{10... | collective-permute-start | bytes 589832 | tf_op jit(solution)/shard_map/ppermute | solution.py:49
  9.8 13.5 %collective-permute-start.8 = (bf16[6,2,32,2,128]{4,3,2,1,0:T(2,128)(2,1)S(1)}, bf16[6,2,32,2,128]{4,3,2,1,0:T(2,128)(2,1)S(1)}, u32[]{:S(2)}, u32[]{:S(2)}) collective-permute-start(bf16[6,2,32,2,128]{4,3,2,1,0:T(2,128)(2,1)S(1)} %shard_map.103), channel_id=1, source_target_pairs={{0,24},{8,16},{16,8},{24,0},{1,25},{9,17},{17,9},{25,1},{2,26},{10... | collective-permute-start | bytes 589832 | tf_op jit(solution)/shard_map/ppermute | solution.py:49
  15.7 10.8 %collective-permute-start.3 = (bf16[4,2,64,128]{3,2,1,0:T(8,128)(2,1)S(1)}, bf16[4,2,64,128]{3,2,1,0:T(8,128)(2,1)S(1)}, u32[]{:S(2)}, u32[]{:S(2)}) collective-permute-start(bf16[4,2,64,128]{3,2,1,0:T(8,128)(2,1)S(1)} %get-tuple-element.65), channel_id=1, source_target_pairs={{0,8},{8,0},{16,24},{24,16},{1,9},{9,1},{17,25},{25,17},{2,10},{10... | collective-permute-start | bytes 393224 | tf_op jit(solution)/shard_map/ppermute | solution.py:49
  16.8 10.3 %collective-permute-start.4 = (bf16[4,2,64,128]{3,2,1,0:T(8,128)(2,1)S(1)}, bf16[4,2,64,128]{3,2,1,0:T(8,128)(2,1)S(1)}, u32[]{:S(2)}, u32[]{:S(2)}) collective-permute-start(bf16[4,2,64,128]{3,2,1,0:T(8,128)(2,1)S(1)} %get-tuple-element.66), channel_id=1, source_target_pairs={{0,16},{8,24},{16,0},{24,8},{1,17},{9,25},{17,1},{25,9},{2,18},{10... | collective-permute-start | bytes 393224 | tf_op jit(solution)/shard_map/ppermute | solution.py:49
  19.0 9.9 %collective-permute-start.5 = (bf16[4,2,64,128]{3,2,1,0:T(8,128)(2,1)S(1)}, bf16[4,2,64,128]{3,2,1,0:T(8,128)(2,1)S(1)}, u32[]{:S(2)}, u32[]{:S(2)}) collective-permute-start(bf16[4,2,64,128]{3,2,1,0:T(8,128)(2,1)S(1)} %get-tuple-element.67), channel_id=1, source_target_pairs={{0,24},{8,16},{16,8},{24,0},{1,25},{9,17},{17,9},{25,1},{2,26},{10... | collective-permute-start | bytes 393224 | tf_op jit(solution)/shard_map/ppermute | solution.py:49
  23.3 27.7 %copy-start.7 = (s32[2,256]{1,0:T(2,128)S(1)}, s32[2,256]{1,0:T(2,128)}, u32[]{:S(2)}) copy-start(s32[2,256]{1,0:T(2,128)} %refs_8_.1) | copy-start | bytes 6148
  24.1 7.2 %collective-permute-start.9 = (bf16[4,2,64,128]{3,2,1,0:T(8,128)(2,1)S(1)}, bf16[4,2,64,128]{3,2,1,0:T(8,128)(2,1)S(1)}, u32[]{:S(2)}, u32[]{:S(2)}) collective-permute-start(bf16[4,2,64,128]{3,2,1,0:T(8,128)(2,1)S(1)} %get-tuple-element.70), channel_id=1, source_target_pairs={{0,8},{8,0},{16,24},{24,16},{1,9},{9,1},{17,25},{25,17},{2,10},{10... | collective-permute-start | bytes 393224 | tf_op jit(solution)/shard_map/ppermute | solution.py:49
  25.2 6.1 %collective-permute-start.10 = (bf16[4,2,64,128]{3,2,1,0:T(8,128)(2,1)S(1)}, bf16[4,2,64,128]{3,2,1,0:T(8,128)(2,1)S(1)}, u32[]{:S(2)}, u32[]{:S(2)}) collective-permute-start(bf16[4,2,64,128]{3,2,1,0:T(8,128)(2,1)S(1)} %get-tuple-element.71), channel_id=1, source_target_pairs={{0,16},{8,24},{16,0},{24,8},{1,17},{9,25},{17,1},{25,9},{2,18},{10... | collective-permute-start | bytes 393224 | tf_op jit(solution)/shard_map/ppermute | solution.py:49
  26.5 7.4 %collective-permute-start.11 = (bf16[4,2,64,128]{3,2,1,0:T(8,128)(2,1)S(1)}, bf16[4,2,64,128]{3,2,1,0:T(8,128)(2,1)S(1)}, u32[]{:S(2)}, u32[]{:S(2)}) collective-permute-start(bf16[4,2,64,128]{3,2,1,0:T(8,128)(2,1)S(1)} %get-tuple-element.72), channel_id=1, source_target_pairs={{0,24},{8,16},{16,8},{24,0},{1,25},{9,17},{17,9},{25,1},{2,26},{10... | collective-permute-start | bytes 393224 | tf_op jit(solution)/shard_map/ppermute | solution.py:49
  52.2 19.6 %collective-permute-start.12 = (bf16[4,2,64,128]{3,2,1,0:T(8,128)(2,1)S(1)}, bf16[4,2,64,128]{3,2,1,0:T(8,128)(2,1)S(1)}, u32[]{:S(2)}, u32[]{:S(2)}) collective-permute-start(bf16[4,2,64,128]{3,2,1,0:T(8,128)(2,1)S(1)} %get-tuple-element.89), channel_id=1, source_target_pairs={{0,1},{1,2},{2,3},{3,4},{4,5},{5,6},{6,7},{8,9},{9,10},{10,11},{11... | collective-permute-start | bytes 393224 | tf_op jit(solution)/shard_map/ppermute | solution.py:66
  59.6 12.2 %collective-permute-start.13 = (bf16[4,2,64,128]{3,2,1,0:T(8,128)(2,1)S(1)}, bf16[4,2,64,128]{3,2,1,0:T(8,128)(2,1)S(1)}, u32[]{:S(2)}, u32[]{:S(2)}) collective-permute-start(bf16[4,2,64,128]{3,2,1,0:T(8,128)(2,1)S(1)} %get-tuple-element.90), channel_id=1, source_target_pairs={{1,0},{2,1},{3,2},{4,3},{5,4},{6,5},{7,6},{9,8},{10,9},{11,10},{12... | collective-permute-start | bytes 393224 | tf_op jit(solution)/shard_map/ppermute | solution.py:66
  71.8 4.5 %copy-start.1 = (bf16[5,64,2048]{2,1,0:T(8,128)(2,1)S(1)}, bf16[5,64,2048]{2,1,0:T(8,128)(2,1)}, u32[]{:S(2)}) copy-start(bf16[5,64,2048]{2,1,0:T(8,128)(2,1)} %refs_10_.1) | copy-start | bytes 3932164
  71.8 4.5 %copy-start.2 = (bf16[5,64,2048]{2,1,0:T(8,128)(2,1)S(1)}, bf16[5,64,2048]{2,1,0:T(8,128)(2,1)}, u32[]{:S(2)}) copy-start(bf16[5,64,2048]{2,1,0:T(8,128)(2,1)} %refs_11_.1) | copy-start | bytes 3932164
  71.8 4.5 %copy-start.5 = (f32[2048]{0:T(1024)S(1)}, f32[2048]{0:T(1024)}, u32[]{:S(2)}) copy-start(f32[2048]{0:T(1024)} %param.9) | copy-start | bytes 24580
  71.8 4.5 %copy-start.6 = (s32[32,5]{0,1:T(8,128)S(1)}, s32[32,5]{0,1:T(8,128)}, u32[]{:S(2)}) copy-start(s32[32,5]{0,1:T(8,128)} %param.12) | copy-start | bytes 1924
  73.4 9.5 %collective-permute-start.14 = (bf16[3,4,64,128]{3,2,1,0:T(8,128)(2,1)S(1)}, bf16[3,4,64,128]{3,2,1,0:T(8,128)(2,1)S(1)}, u32[]{:S(2)}, u32[]{:S(2)}) collective-permute-start(bf16[3,4,64,128]{3,2,1,0:T(8,128)(2,1)S(1)} %get-tuple-element.106), channel_id=1, source_target_pairs={{0,8},{8,0},{16,24},{24,16},{1,9},{9,1},{17,25},{25,17},{2,10},{10... | collective-permute-start | bytes 589832 | tf_op jit(solution)/shard_map/ppermute | solution.py:49
  75.0 10.2 %collective-permute-start.15 = (bf16[3,4,64,128]{3,2,1,0:T(8,128)(2,1)S(1)}, bf16[3,4,64,128]{3,2,1,0:T(8,128)(2,1)S(1)}, u32[]{:S(2)}, u32[]{:S(2)}) collective-permute-start(bf16[3,4,64,128]{3,2,1,0:T(8,128)(2,1)S(1)} %get-tuple-element.107), channel_id=1, source_target_pairs={{0,16},{8,24},{16,0},{24,8},{1,17},{9,25},{17,1},{25,9},{2,18},{10... | collective-permute-start | bytes 589832 | tf_op jit(solution)/shard_map/ppermute | solution.py:49
  76.3 9.0 %collective-permute-start.16 = (bf16[3,4,64,128]{3,2,1,0:T(8,128)(2,1)S(1)}, bf16[3,4,64,128]{3,2,1,0:T(8,128)(2,1)S(1)}, u32[]{:S(2)}, u32[]{:S(2)}) collective-permute-start(bf16[3,4,64,128]{3,2,1,0:T(8,128)(2,1)S(1)} %get-tuple-element.108), channel_id=1, source_target_pairs={{0,24},{8,16},{16,8},{24,0},{1,25},{9,17},{17,9},{25,1},{2,26},{10... | collective-permute-start | bytes 589832 | tf_op jit(solution)/shard_map/ppermute | solution.py:49

commit v9 on v7

--- a/solution.py
+++ b/solution.py
@@ -30,27 +30,35 @@
     return pl.CostEstimate(flops=1024, bytes_accessed=1024, transcendentals=0)
 
 
-def dest_of(me, step, count):
+def offsets(count, place):
+    order = list(range(count - 1))
+    order.insert(place, count - 1)
+    return order if place < count else list(range(count))
+
+
+def dest_of(me, offset, count):
     if count & (count - 1) == 0:
-        return jnp.bitwise_xor(me, step)
-    return lax.rem(me + step, count)
-
-
-def source_of(me, step, count):
+        return jnp.bitwise_xor(me, offset)
+    return lax.rem(me + offset, count)
+
+
+def source_of(me, offset, count):
     if count & (count - 1) == 0:
-        return jnp.bitwise_xor(me, step)
-    return lax.rem(me + count - step, count)
-
-
-def send(piece, step):
+        return jnp.bitwise_xor(me, offset)
+    return lax.rem(me + count - offset, count)
+
+
+def exchange(pieces, order):
     count = lax.axis_size("mode")
     power = count & (count - 1) == 0
-    pairs = [(i, i ^ step if power else (i + step) % count) for i in range(count)]
-    return lax.ppermute(piece, "mode", pairs)
-
-
-def exchange(pieces):
-    return [send(piece, step) for step, piece in enumerate(pieces, 1)]
+    received = []
+    for piece, offset in zip(pieces, order):
+        if offset == 0:
+            received.append(piece)
+            continue
+        pairs = [(i, i ^ offset if power else (i + offset) % count) for i in range(count)]
+        received.append(lax.ppermute(piece, "mode", pairs))
+    return received
 
 
 def from_behind(value, axis, steps):
@@ -104,12 +112,12 @@
     return (last - first, width // lax.axis_size("mode") // LANES // groups, mode_count, 2, LANES)
 
 
-def pack(fields, first, last, step, group, groups):
+def pack(fields, first, last, offset, group, groups):
     count = lax.axis_size("mode")
     shape = packed_shape(fields, first, last, groups)
 
     def kernel(fields_ref, out_ref, sems):
-        share = dest_of(lax.axis_index("mode"), step, count)
+        share = dest_of(lax.axis_index("mode"), offset, count)
         run_copies(pieces_of(fields_ref, first, share, group, out_ref), sems)
 
     return pl.pallas_call(
@@ -132,8 +140,8 @@
         parcel_refs, outputs = refs[: len(parcels)], refs[len(parcels) : -1]
         me = lax.axis_index("mode")
         pairs = []
-        for (first, _, step, group, _), parcel_ref in zip(parcels, parcel_refs):
-            pairs += pieces_of(fields_ref, first, dest_of(me, step, count), group, parcel_ref)
+        for (first, _, offset, group, _), parcel_ref in zip(parcels, parcel_refs):
+            pairs += pieces_of(fields_ref, first, dest_of(me, offset, count), group, parcel_ref)
         run_copies(pairs, refs[-1], zip(inputs, outputs))
 
     return pl.pallas_call(
@@ -152,23 +160,24 @@
     return [a[1] * b[2] - a[2] * b[1], a[2] * b[0] - a[0] * b[2], a[0] * b[1] - a[1] * b[0]]
 
 
-def to_physical(count, in_refs, inverse, x_ref, store):
+def to_physical(order, in_refs, inverse, x_ref, store):
     me = lax.axis_index("mode")
     components, tiles, rows, _ = in_refs[0].shape
-    for step in range(count):
-        at = pl.multiple_of(source_of(me, step, count) * rows, rows)
+    for in_ref, offset in zip(in_refs, order):
+        at = pl.multiple_of(source_of(me, offset, len(order)) * rows, rows)
         for c in range(components):
             for t in range(tiles):
-                x_ref[c, pl.ds(at, rows), t * LANES : (t + 1) * LANES] = in_refs[step][c, t]
+                x_ref[c, pl.ds(at, rows), t * LANES : (t + 1) * LANES] = in_ref[c, t]
     for c in range(components):
         store(c, jnp.dot(inverse, x_ref[c], preferred_element_type=jnp.float32))
 
 
-def to_modes(count, forward_ref, table_ref, product_ref, out_refs):
+def to_modes(order, forward_ref, table_ref, product_ref, out_refs):
+    count = len(order)
     me = lax.axis_index("mode")
     components, tiles, rows, _ = out_refs[0].shape
-    for step in range(count):
-        at = pl.multiple_of(dest_of(me, step, count) * rows, rows)
+    for step, offset in enumerate(order):
+        at = pl.multiple_of(dest_of(me, offset, count) * rows, rows)
         table_ref[step * rows : (step + 1) * rows] = forward_ref[pl.ds(at, rows)]
     for c in range(components):
         terms = jnp.dot(table_ref[...], product_ref[c], preferred_element_type=jnp.float32)
@@ -188,7 +197,7 @@
     def store(c, value):
         physical_ref[c] = value
 
-    to_physical(count, in_refs, inverse_ref[...], x_ref, store)
+    to_physical(offsets(count, 2), in_refs, inverse_ref[...], x_ref, store)
     for i in range(THETA // CHUNK):
         at = slice(i * CHUNK, (i + 1) * CHUNK)
         velocity = [physical_ref[c, at] for c in range(3)]
@@ -196,7 +205,7 @@
         energy = 0.5 * (velocity[0] * velocity[0] + velocity[1] * velocity[1] + velocity[2] * velocity[2])
         for c, value in enumerate(cross(velocity, magnetic) + [energy]):
             product_ref[c, at] = value.astype(jnp.bfloat16)
-    to_modes(count, forward_ref, table_ref, product_ref, out_refs)
+    to_modes(offsets(count, 1), forward_ref, table_ref, product_ref, out_refs)
 
 
 def first_physics(received, inverse, forward):
@@ -228,7 +237,7 @@
     def store(c, value):
         physical_ref[c] = value
 
-    to_physical(count, in_refs, inverse_ref[...], x_ref, store)
+    to_physical(offsets(count, 1), in_refs, inverse_ref[...], x_ref, store)
     for group in range(groups):
         lanes = slice(group * width, (group + 1) * width)
         for i in range(THETA // CHUNK):
@@ -240,7 +249,7 @@
             lorentz = [a + b for a, b in zip(cross(current, magnetic), cross(velocity, vorticity))]
             for c, value in enumerate(lorentz):
                 product_ref[c, at, lanes] = value.astype(jnp.bfloat16)
-    to_modes(count, forward_ref, table_ref, product_ref, out_refs)
+    to_modes(offsets(count, 1), forward_ref, table_ref, product_ref, out_refs)
 
 
 def second_physics(received, physical, inverse, forward):
@@ -268,8 +277,8 @@
     components, held, rows, _ = in_refs[0].shape
     groups = len(in_refs) // count
     for group in range(groups):
-        for step in range(count):
-            share = source_of(me, step, count)
+        for step, offset in enumerate(offsets(count, 1)):
+            share = source_of(me, offset, count)
             for t in range(held):
                 at = share * (groups * held) + group * held + t
                 yield at, in_refs[group * count + step][:, t].reshape(components * rows, LANES)
@@ -307,6 +316,35 @@
     )(*received, interface_nodes)
 
 
+SUBLANES = 8
+
+
+def interleaved(parts):
+    parts = list(parts)
+    row = lax.broadcasted_iota(jnp.int32, parts[0].shape, 1)
+    for distance in (1, 2, 4):
+        upper = jnp.bitwise_and(row, distance) != 0
+        for k in range(SUBLANES):
+            if k & distance == 0:
+                first, second = parts[k], parts[k + distance]
+                parts[k] = jnp.where(upper, pltpu.roll(second, distance, 1), first)
+                parts[k + distance] = jnp.where(upper, second, pltpu.roll(first, SUBLANES - distance, 1))
+    return parts
+
+
+def put_rows(out_ref, first, stride, tiles):
+    modes = tiles[0].shape[0] // 2
+    parts = [part for tile in tiles for part in (tile[:modes], tile[modes:])]
+    if len(parts) == SUBLANES:
+        whole = interleaved([part.reshape(modes // SUBLANES, SUBLANES, LANES) for part in parts])
+        for mode in range(modes):
+            here = pl.ds(pl.multiple_of(first + mode * stride, SUBLANES), SUBLANES)
+            out_ref[here, :] = whole[mode % SUBLANES][mode // SUBLANES]
+    else:
+        for i, part in enumerate(parts):
+            out_ref[pl.ds(first + i, modes, stride=stride), :] = part
+
+
 def derive_kernel(count, arrived, *refs):
     in_refs = refs[:arrived]
     prev_ref, next_ref, radial_ref, axial_ref, radius_ref, columns_ref = refs[arrived : arrived + 6]
@@ -335,7 +373,7 @@
     def rotated(values):
         return jnp.concatenate([-modes * values[mode_count:], modes * values[:mode_count]], axis=0)
 
-    def pair(b, carry):
+    def tile_of(b):
         here = pl.ds(pl.multiple_of(b * LANES, LANES), LANES)
         left, right = [], []
         for k in range(NNZB):
@@ -354,23 +392,25 @@
         along_z = [total[c * rows : (c + 1) * rows, LANES:] for c in range(components)]
         values = [extended_ref[0, b, c * rows : (c + 1) * rows].astype(jnp.float32) for c in range(components)]
         inv_radius = 1.0 / radius_ref[:, here]
-        induction = [
+        momentum_ref[0, b] = along_r[3]
+        momentum_ref[1, b] = rotated(values[3]) * inv_radius
+        momentum_ref[2, b] = along_z[3]
+        return [
             rotated(values[2]) * inv_radius - along_z[1],
             along_z[0] - along_r[2],
             along_r[1] + values[1] * inv_radius - rotated(values[0]) * inv_radius,
         ]
-        stride = 2 * node_tiles
-        for i, value in enumerate(induction):
-            for p in range(2):
-                induction_ref[pl.ds(i * mode_count * stride + 2 * b + p, mode_count, stride=stride), :] = value[
-                    p * mode_count : (p + 1) * mode_count
-                ]
-        momentum_ref[0, b] = along_r[3]
-        momentum_ref[1, b] = rotated(values[3]) * inv_radius
-        momentum_ref[2, b] = along_z[3]
+
+    stride = 2 * node_tiles
+    together = SUBLANES // 2 if node_tiles % (SUBLANES // 2) == 0 else 1
+
+    def tiles_at(q, carry):
+        induction = [tile_of(q * together + i) for i in range(together)]
+        for i in range(3):
+            put_rows(induction_ref, i * mode_count * stride + 2 * q * together, stride, [tile[i] for tile in induction])
         return carry
 
-    lax.fori_loop(0, node_tiles, pair, 0, unroll=2)
+    lax.fori_loop(0, node_tiles // together, tiles_at, 0)
 
 
 def derive(received, from_prev, from_next, radial_blocks, axial_blocks, radius, columns, count):
@@ -390,22 +430,6 @@
         compiler_params=params(),
         cost_estimate=cost(),
     )(*received, from_prev, from_next, radial_blocks, axial_blocks, radius, columns)
-
-
-SUBLANES = 8
-
-
-def interleaved(parts):
-    parts = list(parts)
-    row = lax.broadcasted_iota(jnp.int32, parts[0].shape, 1)
-    for distance in (1, 2, 4):
-        upper = jnp.bitwise_and(row, distance) != 0
-        for k in range(SUBLANES):
-            if k & distance == 0:
-                first, second = parts[k], parts[k + distance]
-                parts[k] = jnp.where(upper, pltpu.roll(second, distance, 1), first)
-                parts[k + distance] = jnp.where(upper, second, pltpu.roll(first, SUBLANES - distance, 1))
-    return parts
 
 
 def momentum_kernel(count, arrived, *refs):
@@ -418,24 +442,14 @@
     out_rows = mode_count * stride
     copies = []
     for c in range(components):
-        for step in range(count):
-            share = source_of(me, step, count)
+        for step, offset in enumerate(offsets(count, 1)):
+            share = source_of(me, offset, count)
             for start in range(0, tiles, SUBLANES // 2):
-                parts = []
+                values = []
                 for t in range(start, min(tiles, start + SUBLANES // 2)):
-                    at = share * tiles + t
-                    piece_ref = in_refs[t // held * count + step]
-                    value = piece_ref[c, t % held].astype(jnp.float32) - gradient_ref[c, at]
-                    parts += [value[:mode_count], value[mode_count:]]
-                first = c * out_rows + 2 * (share * tiles + start)
-                if len(parts) == SUBLANES:
-                    whole = interleaved([part.reshape(mode_count // SUBLANES, SUBLANES, LANES) for part in parts])
-                    for mode in range(mode_count):
-                        here = pl.ds(pl.multiple_of(first + mode * stride, SUBLANES), SUBLANES)
-                        total_ref[here, :] = whole[mode % SUBLANES][mode // SUBLANES]
-                else:
-                    for i, part in enumerate(parts):
-                        total_ref[pl.ds(first + i, mode_count, stride=stride), :] = part
+                    piece = in_refs[t // held * count + step][c, t % held].astype(jnp.float32)
+                    values.append(piece - gradient_ref[c, share * tiles + t])
+                put_rows(total_ref, c * out_rows + 2 * (share * tiles + start), stride, values)
         done = pl.ds(c * out_rows, out_rows)
         copies.append(pltpu.make_async_copy(total_ref.at[done], out_ref.at[done], sems.at[c]))
         copies[c].start()
@@ -475,11 +489,13 @@
     groups = groups_of(width // count // LANES)
     arrived = []
     for group in range(groups):
-        arrived.append(exchange([pack(mode_fields, 0, 6, step, group, groups) for step in range(1, count)]))
+        order = offsets(count, 2)
+        arrived.append(exchange([pack(mode_fields, 0, 6, offset, group, groups) for offset in order[1:]], order[1:]))
     parcels = [(0, 6, 0, group, groups) for group in range(groups)]
     *own, inverse, forward = pack_rest(mode_fields, parcels, [inverse, forward])
     arrived[0][1:2], carried = lax.optimization_barrier((arrived[0][1:2], [inverse, forward]))
-    parcels = [(6, 12, step, 0, 1) for step in range(count)]
+    order = offsets(count, 1)
+    parcels = [(6, 12, offset, 0, 1) for offset in order]
     *shares, later_inverse, later_forward = pack_rest(mode_fields, parcels, carried)
     local, physical = [], []
     for group in range(groups):
@@ -488,16 +504,16 @@
         else:
             tables_here = (inverse, forward)
         *terms, velocity_magnetic = first_physics(joined([own[group]] + arrived[group]), *tables_here)
-        local += terms[:1] + exchange(terms[1:])
+        local += exchange(terms, order)
         physical.append(velocity_magnetic)
     local, shares = lax.optimization_barrier((local, shares))
-    sources = shares[:1] + exchange(shares[1:])
+    sources = exchange(shares, order)
     toward_prev, toward_next = interface(local, interface_nodes, count)
     halos = (from_behind(toward_next, "mer", 1), from_behind(toward_prev, "mer", -1))
     sources, halos = lax.optimization_barrier((sources, halos))
     lorentz = list(second_physics(joined(sources), physical, later_inverse, later_forward))
     lorentz, radius = lax.optimization_barrier((lorentz, radius))
-    lorentz = lorentz[:1] + exchange(lorentz[1:])
+    lorentz = exchange(lorentz, order)
     induction, gradient = derive(
         local, *halos, radial_blocks, axial_blocks, radius.reshape(1, width), block_columns.T, count
     )

time: 69.5 us -> 71.1 us (1.023)
  waiting for transfers between devices: 23.6 us -> 25.3 us
  Pallas kernels: 14.9 us -> 13.4 us
  starting transfers between devices: 28 us -> 29.5 us
    ppermute x18, waiting for transfers between devices: 19.9 us -> 21.6 us  [exchange(): received.append(lax.ppermute(piece, 'mode', pairs))]
    pallas_call x1, Pallas kernels: 6.58 us -> 5.02 us  [derive(): pl.pallas_call(functools.partial(derive_kernel, count, len(received)), in...]
    ppermute x18, starting transfers between devices: 25.4 us -> 26.9 us  [exchange(): received.append(lax.ppermute(piece, 'mode', pairs))]
  transfers between devices with their start and end apart: 20 -> 20, of which waited for: 8 -> 12; matrix products, arithmetic and copies ran while one was open for 0% -> 0% of each run, Pallas kernels for 17% -> 15%
where the time goes in v9:
time: 71.1 us; the launch traced here: 70.9 us
  starting transfers between devices  29.5 us (41%)
  waiting for transfers between devices  25.3 us (36%)
  Pallas kernels  13.4 us (19%)
  local copies, waits for them, and re-layouts  1.93 us (3%)
  between operations  0.84 us (1%)
    ppermute x18, starting transfers between devices, exchange(): received.append(lax.ppermute(piece, 'mode', pairs))  26.9 us
    ppermute x18, waiting for transfers between devices, exchange(): received.append(lax.ppermute(piece, 'mode', pairs))  21.6 us
    pallas_call x1, Pallas kernels, derive(): pl.pallas_call(functools.partial(derive_kernel, count, len(received)), in...  5.02 us
    ppermute x2, waiting for transfers between devices, from_behind(): lax.ppermute(value, axis, [(source, source + steps) for source in range(i...  3.74 us
    ppermute x2, starting transfers between devices, from_behind(): lax.ppermute(value, axis, [(source, source + steps) for source in range(i...  2.59 us
    unnamed x18, local copies, waits for them, and re-layouts  1.93 us
    pallas_call x2, Pallas kernels, first_physics(): pl.pallas_call(functools.partial(first_kernel, count), in_specs=[vmem()]...  1.64 us
    pallas_call x2, Pallas kernels, pack_rest(): pl.pallas_call(kernel, in_specs=[pl.BlockSpec(memory_space=pl.ANY)] + [vm...  1.62 us
  transfers between devices with their start and end apart: 20, of which 12 were waited for; matrix products, arithmetic and copies ran while one was open for 0% of the time, Pallas kernels for 15%

profile of v9, /device:TPU:0, one launch (start us, length us, event | category | flops | bytes accessed | tf_op | source)
XLA Modules:
  0.0 70.9 jit_solution(14574435281362555763)
XLA Ops:
  0.6 1.9 %copy-done = bf16[12,32,2,2048]{3,2,1,0:T(2,128)(2,1)S(1)} copy-done((bf16[12,32,2,2048]{3,2,1,0:T(2,128)(2,1)S(1)}, bf16[12,32,2,2048]{3,2,1,0:T(2,128)(2,1)}, u32[]{:S(2)}) %copy-start) | copy-done | bytes 3145752
  2.5 0.2 shard_map.102
  2.7 4.0 %collective-permute-start.7 = (bf16[6,2,32,2,128]{4,3,2,1,0:T(2,128)(2,1)S(1)}, bf16[6,2,32,2,128]{4,3,2,1,0:T(2,128)(2,1)S(1)}, u32[]{:S(2)}, u32[]{:S(2)}) collective-permute-start(bf16[6,2,32,2,128]{4,3,2,1,0:T(2,128)(2,1)S(1)} %shard_map.102), channel_id=1, source_target_pairs={{0,24},{8,16},{16,8},{24,0},{1,25},{9,17},{17,9},{25,1},{2,26},{10... | collective-permute-start | bytes 589832 | tf_op jit(solution)/shard_map/ppermute | solution.py:60
  6.6 0.2 shard_map.103
  6.8 0.6 collective-permute-start.8
  7.4 0.2 shard_map.101
  7.6 0.1 collective-permute-start.6
  7.7 0.2 shard_map.97
  7.9 3.0 %collective-permute-start.1 = (bf16[6,2,32,2,128]{4,3,2,1,0:T(2,128)(2,1)S(1)}, bf16[6,2,32,2,128]{4,3,2,1,0:T(2,128)(2,1)S(1)}, u32[]{:S(2)}, u32[]{:S(2)}) collective-permute-start(bf16[6,2,32,2,128]{4,3,2,1,0:T(2,128)(2,1)S(1)} %shard_map.97), channel_id=1, source_target_pairs={{0,24},{8,16},{16,8},{24,0},{1,25},{9,17},{17,9},{25,1},{2,26},{10... | collective-permute-start | bytes 589832 | tf_op jit(solution)/shard_map/ppermute | solution.py:60
  10.8 0.2 shard_map.96
  11.0 0.0 copy-start.4
  11.0 0.6 collective-permute-start
  11.6 0.2 shard_map.98
  11.8 0.6 collective-permute-done.7
  12.4 2.1 %collective-permute-start.2 = (bf16[6,2,32,2,128]{4,3,2,1,0:T(2,128)(2,1)S(1)}, bf16[6,2,32,2,128]{4,3,2,1,0:T(2,128)(2,1)S(1)}, u32[]{:S(2)}, u32[]{:S(2)}) collective-permute-start(bf16[6,2,32,2,128]{4,3,2,1,0:T(2,128)(2,1)S(1)} %shard_map.98), channel_id=1, source_target_pairs={{0,16},{8,24},{16,0},{24,8},{1,17},{9,25},{17,1},{25,9},{2,18},{10... | collective-permute-start | bytes 589832 | tf_op jit(solution)/shard_map/ppermute | solution.py:60
  14.5 0.3 shard_map.95
  14.8 1.9 %collective-permute-done.8 = bf16[6,2,32,2,128]{4,3,2,1,0:T(2,128)(2,1)S(1)} collective-permute-done((bf16[6,2,32,2,128]{4,3,2,1,0:T(2,128)(2,1)S(1)}, bf16[6,2,32,2,128]{4,3,2,1,0:T(2,128)(2,1)S(1)}, u32[]{:S(2)}, u32[]{:S(2)}) %collective-permute-start.8) | collective-permute-done | bytes 196640 | tf_op jit(solution)/shard_map/ppermute | solution.py:60
  16.7 0.5 collective-permute-done.6
  17.2 0.8 %shard_map.104 = (bf16[4,2,64,128]{3,2,1,0:T(8,128)(2,1)S(1)}, bf16[4,2,64,128]{3,2,1,0:T(8,128)(2,1)S(1)}, bf16[4,2,64,128]{3,2,1,0:T(8,128)(2,1)S(1)}, bf16[4,...) custom-call(bf16[6,2,64,128]{3,2,1,0:T(8,128)(2,1)S(1)} %bitcast.35, bf16[6,2,64,128]{3,2,1,0:T(8,128)(2,1)S(1)} %bitcast.34, ...), custom_call_target="tpu_custom_call" | custom-call | flops 1024 | bytes 1024 | tf_op jit(solution)/shard_map/pallas_call | solution.py:215
  18.0 2.5 %collective-permute-start.9 = (bf16[4,2,64,128]{3,2,1,0:T(8,128)(2,1)S(1)}, bf16[4,2,64,128]{3,2,1,0:T(8,128)(2,1)S(1)}, u32[]{:S(2)}, u32[]{:S(2)}) collective-permute-start(bf16[4,2,64,128]{3,2,1,0:T(8,128)(2,1)S(1)} %get-tuple-element.70), channel_id=1, source_target_pairs={{0,24},{8,16},{16,8},{24,0},{1,25},{9,17},{17,9},{25,1},{2,26},{10... | collective-permute-start | bytes 393224 | tf_op jit(solution)/shard_map/ppermute | solution.py:60
  20.5 0.4 collective-permute-done.1
  20.9 2.0 %collective-permute-start.10 = (bf16[4,2,64,128]{3,2,1,0:T(8,128)(2,1)S(1)}, bf16[4,2,64,128]{3,2,1,0:T(8,128)(2,1)S(1)}, u32[]{:S(2)}, u32[]{:S(2)}) collective-permute-start(bf16[4,2,64,128]{3,2,1,0:T(8,128)(2,1)S(1)} %get-tuple-element.71), channel_id=1, source_target_pairs={{0,8},{8,0},{16,24},{24,16},{1,9},{9,1},{17,25},{25,17},{2,10},{10... | collective-permute-start | bytes 393224 | tf_op jit(solution)/shard_map/ppermute | solution.py:60
  22.9 1.5 %collective-permute-start.11 = (bf16[4,2,64,128]{3,2,1,0:T(8,128)(2,1)S(1)}, bf16[4,2,64,128]{3,2,1,0:T(8,128)(2,1)S(1)}, u32[]{:S(2)}, u32[]{:S(2)}) collective-permute-start(bf16[4,2,64,128]{3,2,1,0:T(8,128)(2,1)S(1)} %get-tuple-element.72), channel_id=1, source_target_pairs={{0,16},{8,24},{16,0},{24,8},{1,17},{9,25},{17,1},{25,9},{2,18},{10... | collective-permute-start | bytes 393224 | tf_op jit(solution)/shard_map/ppermute | solution.py:60
  24.4 1.3 %shard_map.99 = (bf16[6,4,32,2,128]{4,3,2,1,0:T(2,128)(2,1)S(1)}, bf16[6,4,32,2,128]{4,3,2,1,0:T(2,128)(2,1)S(1)}, bf16[6,4,32,2,128]{4,3,2,1,0:T(2,128)(2,1)S(1...) custom-call(bf16[12,32,2,2048]{3,2,1,0:T(2,128)(2,1)S(1)} %copy-done.1, ...), custom_call_target="tpu_custom_call" | custom-call | flops 1024 | bytes 1024 | tf_op jit(solution)/shard_map/pallas_call | solution.py:147
  25.7 0.8 %shard_map.100 = (bf16[4,2,64,128]{3,2,1,0:T(8,128)(2,1)S(1)}, bf16[4,2,64,128]{3,2,1,0:T(8,128)(2,1)S(1)}, bf16[4,2,64,128]{3,2,1,0:T(8,128)(2,1)S(1)}, bf16[4,...) custom-call(bf16[6,2,64,128]{3,2,1,0:T(8,128)(2,1)S(1)} %bitcast.31, bf16[6,2,64,128]{3,2,1,0:T(8,128)(2,1)S(1)} %bitcast.29, ...), custom_call_target="tpu_custom_call" | custom-call | flops 1024 | bytes 1024 | tf_op jit(solution)/shard_map/pallas_call | solution.py:215
  26.5 2.4 %collective-permute-start.3 = (bf16[4,2,64,128]{3,2,1,0:T(8,128)(2,1)S(1)}, bf16[4,2,64,128]{3,2,1,0:T(8,128)(2,1)S(1)}, u32[]{:S(2)}, u32[]{:S(2)}) collective-permute-start(bf16[4,2,64,128]{3,2,1,0:T(8,128)(2,1)S(1)} %get-tuple-element.65), channel_id=1, source_target_pairs={{0,24},{8,16},{16,8},{24,0},{1,25},{9,17},{17,9},{25,1},{2,26},{10... | collective-permute-start | bytes 393224 | tf_op jit(solution)/shard_map/ppermute | solution.py:60
  28.9 0.6 collective-permute-start.4
  29.5 0.6 collective-permute-start.5
  30.1 0.3 collective-permute-done.10.refs_6_
  30.4 3.5 %collective-permute-done.3.refs_1_ = bf16[4,2,64,128]{3,2,1,0:T(8,128)(2,1)S(1)} collective-permute-done((bf16[4,2,64,128]{3,2,1,0:T(8,128)(2,1)S(1)}, bf16[4,2,64,128]{3,2,1,0:T(8,128)(2,1)S(1)}, u32[]{:S(2)}, u32[]{:S(2)}) %collective-permute-start.3) | collective-permute-done | bytes 131104 | tf_op jit(solution)/shard_map/ppermute | solution.py:60
  33.9 1.9 %collective-permute-done.4.refs_2_ = bf16[4,2,64,128]{3,2,1,0:T(8,128)(2,1)S(1)} collective-permute-done((bf16[4,2,64,128]{3,2,1,0:T(8,128)(2,1)S(1)}, bf16[4,2,64,128]{3,2,1,0:T(8,128)(2,1)S(1)}, u32[]{:S(2)}, u32[]{:S(2)}) %collective-permute-start.4) | collective-permute-done | bytes 131104 | tf_op jit(solution)/shard_map/ppermute | solution.py:60
  35.8 1.9 %collective-permute-start.12 = (bf16[6,4,32,2,128]{4,3,2,1,0:T(2,128)(2,1)S(1)}, bf16[6,4,32,2,128]{4,3,2,1,0:T(2,128)(2,1)S(1)}, u32[]{:S(2)}, u32[]{:S(2)}) collective-permute-start(bf16[6,4,32,2,128]{4,3,2,1,0:T(2,128)(2,1)S(1)} %get-tuple-element.86), channel_id=1, source_target_pairs={{0,24},{8,16},{16,8},{24,0},{1,25},{9,17},{17,9},{25,1},{2,26},{10... | collective-permute-start | bytes 1179656 | tf_op jit(solution)/shard_map/ppermute | solution.py:60
  37.7 0.9 %collective-permute-start.13 = (bf16[6,4,32,2,128]{4,3,2,1,0:T(2,128)(2,1)S(1)}, bf16[6,4,32,2,128]{4,3,2,1,0:T(2,128)(2,1)S(1)}, u32[]{:S(2)}, u32[]{:S(2)}) collective-permute-start(bf16[6,4,32,2,128]{4,3,2,1,0:T(2,128)(2,1)S(1)} %get-tuple-element.87), channel_id=1, source_target_pairs={{0,8},{8,0},{16,24},{24,16},{1,9},{9,1},{17,25},{25,17},{2,10},{10... | collective-permute-start | bytes 1179656 | tf_op jit(solution)/shard_map/ppermute | solution.py:60
  38.6 0.7 collective-permute-start.14
  39.3 1.2 %shard_map.105 = (bf16[4,2,64,128]{3,2,1,0:T(8,128)(2,1)S(1)}, bf16[4,2,64,128]{3,2,1,0:T(8,128)(2,1)S(1)}) custom-call(bf16[4,2,64,128]{3,2,1,0:T(8,128)(2,1)S(1)} %get-tuple-element.77.refs_0_, bf16[4,2,64,128]{3,2,1,0:T(8,128)(2,1)S(1)} %collective-permute-done.3.refs_1_, bf16[4,2,64,128]{3,2,1,0:T(8,128)(2,1)S(1)} %collective-permute-done.4.refs_2_, ...), custom_call_target="tpu_custom_call" | custom-call | flops 1024 | bytes 1024 | tf_op jit(solution)/shard_map/pallas_call | solution.py:309
  40.5 1.3 %collective-permute-start.15 = (bf16[4,2,64,128]{3,2,1,0:T(8,128)(2,1)S(1)}, bf16[4,2,64,128]{3,2,1,0:T(8,128)(2,1)S(1)}, u32[]{:S(2)}, u32[]{:S(2)}) collective-permute-start(bf16[4,2,64,128]{3,2,1,0:T(8,128)(2,1)S(1)} %get-tuple-element.89), channel_id=1, source_target_pairs={{0,1},{1,2},{2,3},{3,4},{4,5},{5,6},{6,7},{8,9},{9,10},{10,11},{11... | collective-permute-start | bytes 393224 | tf_op jit(solution)/shard_map/ppermute | solution.py:67
  41.8 1.3 %collective-permute-start.16 = (bf16[4,2,64,128]{3,2,1,0:T(8,128)(2,1)S(1)}, bf16[4,2,64,128]{3,2,1,0:T(8,128)(2,1)S(1)}, u32[]{:S(2)}, u32[]{:S(2)}) collective-permute-start(bf16[4,2,64,128]{3,2,1,0:T(8,128)(2,1)S(1)} %get-tuple-element.90), channel_id=1, source_target_pairs={{1,0},{2,1},{3,2},{4,3},{5,4},{6,5},{7,6},{9,8},{10,9},{11,10},{12... | collective-permute-start | bytes 393224 | tf_op jit(solution)/shard_map/ppermute | solution.py:67
  43.2 3.7 %collective-permute-done.16.refs_9_ = bf16[4,2,64,128]{3,2,1,0:T(8,128)(2,1)S(1)} collective-permute-done((bf16[4,2,64,128]{3,2,1,0:T(8,128)(2,1)S(1)}, bf16[4,2,64,128]{3,2,1,0:T(8,128)(2,1)S(1)}, u32[]{:S(2)}, u32[]{:S(2)}) %collective-permute-start.16) | collective-permute-done | bytes 131104 | tf_op jit(solution)/shard_map/ppermute | solution.py:67
  46.9 1.9 %collective-permute-done.12 = bf16[6,4,32,2,128]{4,3,2,1,0:T(2,128)(2,1)S(1)} collective-permute-done((bf16[6,4,32,2,128]{4,3,2,1,0:T(2,128)(2,1)S(1)}, bf16[6,4,32,2,128]{4,3,2,1,0:T(2,128)(2,1)S(1)}, u32[]{:S(2)}, u32[]{:S(2)}) %collective-permute-start.12) | collective-permute-done | bytes 393248 | tf_op jit(solution)/shard_map/ppermute | solution.py:60
  48.8 7.2 %collective-permute-done.13 = bf16[6,4,32,2,128]{4,3,2,1,0:T(2,128)(2,1)S(1)} collective-permute-done((bf16[6,4,32,2,128]{4,3,2,1,0:T(2,128)(2,1)S(1)}, bf16[6,4,32,2,128]{4,3,2,1,0:T(2,128)(2,1)S(1)}, u32[]{:S(2)}, u32[]{:S(2)}) %collective-permute-start.13) | collective-permute-done | bytes 393248 | tf_op jit(solution)/shard_map/ppermute | solution.py:60
  56.0 1.6 %shard_map.106 = (bf16[3,4,64,128]{3,2,1,0:T(8,128)(2,1)S(1)}, bf16[3,4,64,128]{3,2,1,0:T(8,128)(2,1)S(1)}, bf16[3,4,64,128]{3,2,1,0:T(8,128)(2,1)S(1)}, bf16[3,4,64,128]{3,2,1,0:T(8,128)(2,1)S(1)}) custom-call(bf16[6,4,64,128]{3,2,1,0:T(8,128)(2,1)S(1)} %bitcast.24, bf16[6,4,64,128]{3,2,1,0:T(8,128)(2,1)S(1)} %bitcast.25, ...), custom_call_target="tpu_custom_call" | custom-call | flops 1024 | bytes 1024 | tf_op jit(solution)/shard_map/pallas_call | solution.py:259
  57.6 1.5 %collective-permute-start.17 = (bf16[3,4,64,128]{3,2,1,0:T(8,128)(2,1)S(1)}, bf16[3,4,64,128]{3,2,1,0:T(8,128)(2,1)S(1)}, u32[]{:S(2)}, u32[]{:S(2)}) collective-permute-start(bf16[3,4,64,128]{3,2,1,0:T(8,128)(2,1)S(1)} %get-tuple-element.106), channel_id=1, source_target_pairs={{0,24},{8,16},{16,8},{24,0},{1,25},{9,17},{17,9},{25,1},{2,26},{10... | collective-permute-start | bytes 589832 | tf_op jit(solution)/shard_map/ppermute | solution.py:60
  59.1 1.4 %collective-permute-start.18 = (bf16[3,4,64,128]{3,2,1,0:T(8,128)(2,1)S(1)}, bf16[3,4,64,128]{3,2,1,0:T(8,128)(2,1)S(1)}, u32[]{:S(2)}, u32[]{:S(2)}) collective-permute-start(bf16[3,4,64,128]{3,2,1,0:T(8,128)(2,1)S(1)} %get-tuple-element.107), channel_id=1, source_target_pairs={{0,8},{8,0},{16,24},{24,16},{1,9},{9,1},{17,25},{25,17},{2,10},{10... | collective-permute-start | bytes 589832 | tf_op jit(solution)/shard_map/ppermute | solution.py:60
  60.5 0.6 collective-permute-start.19
  61.2 5.0 %shard_map.107 = (f32[3072,128]{1,0:T(8,128)}, f32[3,16,64,128]{3,2,1,0:T(8,128)S(1)}) custom-call(bf16[4,2,64,128]{3,2,1,0:T(8,128)(2,1)S(1)} %get-tuple-element.77.refs_0_, bf16[4,2,64,128]{3,2,1,0:T(8,128)(2,1)S(1)} %collective-permute-done.3.refs_1_, bf16[4,2,64,128]{3,2,1,0:T(8,128)(2,1)S(1)} %collective-permute-done.4.refs_2_, ...), custom_call_target="tpu_custom_call" | custom-call | flops 1024 | bytes 1024 | tf_op jit(solution)/shard_map/pallas_call | solution.py:421
  66.2 0.2 collective-permute-done.17.refs_1_
  66.4 3.2 %collective-permute-done.18.refs_2_ = bf16[3,4,64,128]{3,2,1,0:T(8,128)(2,1)S(1)} collective-permute-done((bf16[3,4,64,128]{3,2,1,0:T(8,128)(2,1)S(1)}, bf16[3,4,64,128]{3,2,1,0:T(8,128)(2,1)S(1)}, u32[]{:S(2)}, u32[]{:S(2)}) %collective-permute-start.18) | collective-permute-done | bytes 196640 | tf_op jit(solution)/shard_map/ppermute | solution.py:60
  69.6 1.3 %shard_map.108 = f32[3072,128]{1,0:T(8,128)} custom-call(bf16[3,4,64,128]{3,2,1,0:T(8,128)(2,1)S(1)} %get-tuple-element.105.refs_0_, bf16[3,4,64,128]{3,2,1,0:T(8,128)(2,1)S(1)} %collective-permute-done.17.refs_1_, bf16[3,4,64,128]{3,2,1,0:T(8,128)(2,1)S(1)} %collective-permute-done.18.refs_2_, bf16[3,4,64,128]{3,2,1,0:T(8,128)(2,1)S(1)} %collective-permute-done.19.refs_3_, ...), custom_call_target="tpu_custom_call" | custom-call | flops 1024 | bytes 1024 | tf_op jit(solution)/shard_map/pallas_call | solution.py:463
  (24 shorter events, 0.1 us)
Async XLA Ops:
  0.6 1.9 %copy-start = (bf16[12,32,2,2048]{3,2,1,0:T(2,128)(2,1)S(1)}, bf16[12,32,2,2048]{3,2,1,0:T(2,128)(2,1)}, u32[]{:S(2)}) copy-start(bf16[12,32,2,2048]{3,2,1,0:T(2,128)(2,1)} %fields_ref.15) | copy-start | bytes 9437188
  2.7 9.7 %collective-permute-start.7 = (bf16[6,2,32,2,128]{4,3,2,1,0:T(2,128)(2,1)S(1)}, bf16[6,2,32,2,128]{4,3,2,1,0:T(2,128)(2,1)S(1)}, u32[]{:S(2)}, u32[]{:S(2)}) collective-permute-start(bf16[6,2,32,2,128]{4,3,2,1,0:T(2,128)(2,1)S(1)} %shard_map.102), channel_id=1, source_target_pairs={{0,24},{8,16},{16,8},{24,0},{1,25},{9,17},{17,9},{25,1},{2,26},{10... | collective-permute-start | bytes 589832 | tf_op jit(solution)/shard_map/ppermute | solution.py:60
  6.8 9.9 %collective-permute-start.8 = (bf16[6,2,32,2,128]{4,3,2,1,0:T(2,128)(2,1)S(1)}, bf16[6,2,32,2,128]{4,3,2,1,0:T(2,128)(2,1)S(1)}, u32[]{:S(2)}, u32[]{:S(2)}) collective-permute-start(bf16[6,2,32,2,128]{4,3,2,1,0:T(2,128)(2,1)S(1)} %shard_map.103), channel_id=1, source_target_pairs={{0,16},{8,24},{16,0},{24,8},{1,17},{9,25},{17,1},{25,9},{2,18},{10... | collective-permute-start | bytes 589832 | tf_op jit(solution)/shard_map/ppermute | solution.py:60
  7.6 9.6 %collective-permute-start.6 = (bf16[6,2,32,2,128]{4,3,2,1,0:T(2,128)(2,1)S(1)}, bf16[6,2,32,2,128]{4,3,2,1,0:T(2,128)(2,1)S(1)}, u32[]{:S(2)}, u32[]{:S(2)}) collective-permute-start(bf16[6,2,32,2,128]{4,3,2,1,0:T(2,128)(2,1)S(1)} %shard_map.101), channel_id=1, source_target_pairs={{0,8},{8,0},{16,24},{24,16},{1,9},{9,1},{17,25},{25,17},{2,10},{10... | collective-permute-start | bytes 589832 | tf_op jit(solution)/shard_map/ppermute | solution.py:60
  7.9 13.0 %collective-permute-start.1 = (bf16[6,2,32,2,128]{4,3,2,1,0:T(2,128)(2,1)S(1)}, bf16[6,2,32,2,128]{4,3,2,1,0:T(2,128)(2,1)S(1)}, u32[]{:S(2)}, u32[]{:S(2)}) collective-permute-start(bf16[6,2,32,2,128]{4,3,2,1,0:T(2,128)(2,1)S(1)} %shard_map.97), channel_id=1, source_target_pairs={{0,24},{8,16},{16,8},{24,0},{1,25},{9,17},{17,9},{25,1},{2,26},{10... | collective-permute-start | bytes 589832 | tf_op jit(solution)/shard_map/ppermute | solution.py:60
  11.0 3.5 %copy-start.4 = (bf16[256,256]{1,0:T(8,128)(2,1)S(1)}, bf16[256,256]{1,0:T(8,128)(2,1)}, u32[]{:S(2)}) copy-start(bf16[256,256]{1,0:T(8,128)(2,1)} %constant.5.clone.refs_1_) | copy-start | bytes 393220
  11.0 3.4 %copy-start.5 = (bf16[256,256]{1,0:T(8,128)(2,1)S(1)}, bf16[256,256]{1,0:T(8,128)(2,1)}, u32[]{:S(2)}) copy-start(bf16[256,256]{1,0:T(8,128)(2,1)} %constant.4.clone.refs_0_) | copy-start | bytes 393220
  11.0 14.7 %collective-permute-start = (bf16[6,2,32,2,128]{4,3,2,1,0:T(2,128)(2,1)S(1)}, bf16[6,2,32,2,128]{4,3,2,1,0:T(2,128)(2,1)S(1)}, u32[]{:S(2)}, u32[]{:S(2)}) collective-permute-start(bf16[6,2,32,2,128]{4,3,2,1,0:T(2,128)(2,1)S(1)} %shard_map.96), channel_id=1, source_target_pairs={{0,8},{8,0},{16,24},{24,16},{1,9},{9,1},{17,25},{25,17},{2,10},{10... | collective-permute-start | bytes 589832 | tf_op jit(solution)/shard_map/ppermute | solution.py:60
  11.8 12.6 %copy-start.1 = (bf16[12,32,2,2048]{3,2,1,0:T(2,128)(2,1)S(1)}, bf16[12,32,2,2048]{3,2,1,0:T(2,128)(2,1)}, u32[]{:S(2)}) copy-start(bf16[12,32,2,2048]{3,2,1,0:T(2,128)(2,1)} %fields_ref.15) | copy-start | bytes 9437188
  12.4 13.3 %collective-permute-start.2 = (bf16[6,2,32,2,128]{4,3,2,1,0:T(2,128)(2,1)S(1)}, bf16[6,2,32,2,128]{4,3,2,1,0:T(2,128)(2,1)S(1)}, u32[]{:S(2)}, u32[]{:S(2)}) collective-permute-start(bf16[6,2,32,2,128]{4,3,2,1,0:T(2,128)(2,1)S(1)} %shard_map.98), channel_id=1, source_target_pairs={{0,16},{8,24},{16,0},{24,8},{1,17},{9,25},{17,1},{25,9},{2,18},{10... | collective-permute-start | bytes 589832 | tf_op jit(solution)/shard_map/ppermute | solution.py:60
  18.0 11.5 %collective-permute-start.9 = (bf16[4,2,64,128]{3,2,1,0:T(8,128)(2,1)S(1)}, bf16[4,2,64,128]{3,2,1,0:T(8,128)(2,1)S(1)}, u32[]{:S(2)}, u32[]{:S(2)}) collective-permute-start(bf16[4,2,64,128]{3,2,1,0:T(8,128)(2,1)S(1)} %get-tuple-element.70), channel_id=1, source_target_pairs={{0,24},{8,16},{16,8},{24,0},{1,25},{9,17},{17,9},{25,1},{2,26},{10... | collective-permute-start | bytes 393224 | tf_op jit(solution)/shard_map/ppermute | solution.py:60
  20.9 9.6 %collective-permute-start.10 = (bf16[4,2,64,128]{3,2,1,0:T(8,128)(2,1)S(1)}, bf16[4,2,64,128]{3,2,1,0:T(8,128)(2,1)S(1)}, u32[]{:S(2)}, u32[]{:S(2)}) collective-permute-start(bf16[4,2,64,128]{3,2,1,0:T(8,128)(2,1)S(1)} %get-tuple-element.71), channel_id=1, source_target_pairs={{0,8},{8,0},{16,24},{24,16},{1,9},{9,1},{17,25},{25,17},{2,10},{10... | collective-permute-start | bytes 393224 | tf_op jit(solution)/shard_map/ppermute | solution.py:60
  22.9 16.4 %copy-start.8 = (s32[2,256]{1,0:T(2,128)S(1)}, s32[2,256]{1,0:T(2,128)}, u32[]{:S(2)}) copy-start(s32[2,256]{1,0:T(2,128)} %refs_8_.1) | copy-start | bytes 6148
  22.9 7.5 %collective-permute-start.11 = (bf16[4,2,64,128]{3,2,1,0:T(8,128)(2,1)S(1)}, bf16[4,2,64,128]{3,2,1,0:T(8,128)(2,1)S(1)}, u32[]{:S(2)}, u32[]{:S(2)}) collective-permute-start(bf16[4,2,64,128]{3,2,1,0:T(8,128)(2,1)S(1)} %get-tuple-element.72), channel_id=1, source_target_pairs={{0,16},{8,24},{16,0},{24,8},{1,17},{9,25},{17,1},{25,9},{2,18},{10... | collective-permute-start | bytes 393224 | tf_op jit(solution)/shard_map/ppermute | solution.py:60
  26.5 7.4 %collective-permute-start.3 = (bf16[4,2,64,128]{3,2,1,0:T(8,128)(2,1)S(1)}, bf16[4,2,64,128]{3,2,1,0:T(8,128)(2,1)S(1)}, u32[]{:S(2)}, u32[]{:S(2)}) collective-permute-start(bf16[4,2,64,128]{3,2,1,0:T(8,128)(2,1)S(1)} %get-tuple-element.65), channel_id=1, source_target_pairs={{0,24},{8,16},{16,8},{24,0},{1,25},{9,17},{17,9},{25,1},{2,26},{10... | collective-permute-start | bytes 393224 | tf_op jit(solution)/shard_map/ppermute | solution.py:60
  28.9 6.9 %collective-permute-start.4 = (bf16[4,2,64,128]{3,2,1,0:T(8,128)(2,1)S(1)}, bf16[4,2,64,128]{3,2,1,0:T(8,128)(2,1)S(1)}, u32[]{:S(2)}, u32[]{:S(2)}) collective-permute-start(bf16[4,2,64,128]{3,2,1,0:T(8,128)(2,1)S(1)} %get-tuple-element.66), channel_id=1, source_target_pairs={{0,8},{8,0},{16,24},{24,16},{1,9},{9,1},{17,25},{25,17},{2,10},{10... | collective-permute-start | bytes 393224 | tf_op jit(solution)/shard_map/ppermute | solution.py:60
  29.5 6.3 %collective-permute-start.5 = (bf16[4,2,64,128]{3,2,1,0:T(8,128)(2,1)S(1)}, bf16[4,2,64,128]{3,2,1,0:T(8,128)(2,1)S(1)}, u32[]{:S(2)}, u32[]{:S(2)}) collective-permute-start(bf16[4,2,64,128]{3,2,1,0:T(8,128)(2,1)S(1)} %get-tuple-element.67), channel_id=1, source_target_pairs={{0,16},{8,24},{16,0},{24,8},{1,17},{9,25},{17,1},{25,9},{2,18},{10... | collective-permute-start | bytes 393224 | tf_op jit(solution)/shard_map/ppermute | solution.py:60
  35.8 13.0 %collective-permute-start.12 = (bf16[6,4,32,2,128]{4,3,2,1,0:T(2,128)(2,1)S(1)}, bf16[6,4,32,2,128]{4,3,2,1,0:T(2,128)(2,1)S(1)}, u32[]{:S(2)}, u32[]{:S(2)}) collective-permute-start(bf16[6,4,32,2,128]{4,3,2,1,0:T(2,128)(2,1)S(1)} %get-tuple-element.86), channel_id=1, source_target_pairs={{0,24},{8,16},{16,8},{24,0},{1,25},{9,17},{17,9},{25,1},{2,26},{10... | collective-permute-start | bytes 1179656 | tf_op jit(solution)/shard_map/ppermute | solution.py:60
  37.7 18.3 %collective-permute-start.13 = (bf16[6,4,32,2,128]{4,3,2,1,0:T(2,128)(2,1)S(1)}, bf16[6,4,32,2,128]{4,3,2,1,0:T(2,128)(2,1)S(1)}, u32[]{:S(2)}, u32[]{:S(2)}) collective-permute-start(bf16[6,4,32,2,128]{4,3,2,1,0:T(2,128)(2,1)S(1)} %get-tuple-element.87), channel_id=1, source_target_pairs={{0,8},{8,0},{16,24},{24,16},{1,9},{9,1},{17,25},{25,17},{2,10},{10... | collective-permute-start | bytes 1179656 | tf_op jit(solution)/shard_map/ppermute | solution.py:60
  38.6 17.4 %collective-permute-start.14 = (bf16[6,4,32,2,128]{4,3,2,1,0:T(2,128)(2,1)S(1)}, bf16[6,4,32,2,128]{4,3,2,1,0:T(2,128)(2,1)S(1)}, u32[]{:S(2)}, u32[]{:S(2)}) collective-permute-start(bf16[6,4,32,2,128]{4,3,2,1,0:T(2,128)(2,1)S(1)} %get-tuple-element.88), channel_id=1, source_target_pairs={{0,16},{8,24},{16,0},{24,8},{1,17},{9,25},{17,1},{25,9},{2,18},{10... | collective-permute-start | bytes 1179656 | tf_op jit(solution)/shard_map/ppermute | solution.py:60
  40.5 2.6 %collective-permute-start.15 = (bf16[4,2,64,128]{3,2,1,0:T(8,128)(2,1)S(1)}, bf16[4,2,64,128]{3,2,1,0:T(8,128)(2,1)S(1)}, u32[]{:S(2)}, u32[]{:S(2)}) collective-permute-start(bf16[4,2,64,128]{3,2,1,0:T(8,128)(2,1)S(1)} %get-tuple-element.89), channel_id=1, source_target_pairs={{0,1},{1,2},{2,3},{3,4},{4,5},{5,6},{6,7},{8,9},{9,10},{10,11},{11... | collective-permute-start | bytes 393224 | tf_op jit(solution)/shard_map/ppermute | solution.py:67
  41.8 5.0 %collective-permute-start.16 = (bf16[4,2,64,128]{3,2,1,0:T(8,128)(2,1)S(1)}, bf16[4,2,64,128]{3,2,1,0:T(8,128)(2,1)S(1)}, u32[]{:S(2)}, u32[]{:S(2)}) collective-permute-start(bf16[4,2,64,128]{3,2,1,0:T(8,128)(2,1)S(1)} %get-tuple-element.90), channel_id=1, source_target_pairs={{1,0},{2,1},{3,2},{4,3},{5,4},{6,5},{7,6},{9,8},{10,9},{11,10},{12... | collective-permute-start | bytes 393224 | tf_op jit(solution)/shard_map/ppermute | solution.py:67
  56.0 5.2 %copy-start.2 = (bf16[5,64,2048]{2,1,0:T(8,128)(2,1)S(1)}, bf16[5,64,2048]{2,1,0:T(8,128)(2,1)}, u32[]{:S(2)}) copy-start(bf16[5,64,2048]{2,1,0:T(8,128)(2,1)} %refs_10_.1) | copy-start | bytes 3932164
  56.0 5.2 %copy-start.3 = (bf16[5,64,2048]{2,1,0:T(8,128)(2,1)S(1)}, bf16[5,64,2048]{2,1,0:T(8,128)(2,1)}, u32[]{:S(2)}) copy-start(bf16[5,64,2048]{2,1,0:T(8,128)(2,1)} %refs_11_.1) | copy-start | bytes 3932164
  56.0 5.2 %copy-start.6 = (f32[2048]{0:T(1024)S(1)}, f32[2048]{0:T(1024)}, u32[]{:S(2)}) copy-start(f32[2048]{0:T(1024)} %param.9) | copy-start | bytes 24580
  56.0 5.2 %copy-start.7 = (s32[32,5]{0,1:T(8,128)S(1)}, s32[32,5]{0,1:T(8,128)}, u32[]{:S(2)}) copy-start(s32[32,5]{0,1:T(8,128)} %param.12) | copy-start | bytes 1924
  57.6 8.8 %collective-permute-start.17 = (bf16[3,4,64,128]{3,2,1,0:T(8,128)(2,1)S(1)}, bf16[3,4,64,128]{3,2,1,0:T(8,128)(2,1)S(1)}, u32[]{:S(2)}, u32[]{:S(2)}) collective-permute-start(bf16[3,4,64,128]{3,2,1,0:T(8,128)(2,1)S(1)} %get-tuple-element.106), channel_id=1, source_target_pairs={{0,24},{8,16},{16,8},{24,0},{1,25},{9,17},{17,9},{25,1},{2,26},{10... | collective-permute-start | bytes 589832 | tf_op jit(solution)/shard_map/ppermute | solution.py:60
  59.1 10.4 %collective-permute-start.18 = (bf16[3,4,64,128]{3,2,1,0:T(8,128)(2,1)S(1)}, bf16[3,4,64,128]{3,2,1,0:T(8,128)(2,1)S(1)}, u32[]{:S(2)}, u32[]{:S(2)}) collective-permute-start(bf16[3,4,64,128]{3,2,1,0:T(8,128)(2,1)S(1)} %get-tuple-element.107), channel_id=1, source_target_pairs={{0,8},{8,0},{16,24},{24,16},{1,9},{9,1},{17,25},{25,17},{2,10},{10... | collective-permute-start | bytes 589832 | tf_op jit(solution)/shard_map/ppermute | solution.py:60
  60.5 9.1 %collective-permute-start.19 = (bf16[3,4,64,128]{3,2,1,0:T(8,128)(2,1)S(1)}, bf16[3,4,64,128]{3,2,1,0:T(8,128)(2,1)S(1)}, u32[]{:S(2)}, u32[]{:S(2)}) collective-permute-start(bf16[3,4,64,128]{3,2,1,0:T(8,128)(2,1)S(1)} %get-tuple-element.108), channel_id=1, source_target_pairs={{0,16},{8,24},{16,0},{24,8},{1,17},{9,25},{17,1},{25,9},{2,18},{10... | collective-permute-start | bytes 589832 | tf_op jit(solution)/shard_map/ppermute | solution.py:60

commit v10 on v9

--- a/solution.py
+++ b/solution.py
@@ -30,10 +30,13 @@
     return pl.CostEstimate(flops=1024, bytes_accessed=1024, transcendentals=0)
 
 
+FIRST_SEND, FIRST_RETURN, SECOND = 2, 1, None
+
+
 def offsets(count, place):
     order = list(range(count - 1))
-    order.insert(place, count - 1)
-    return order if place < count else list(range(count))
+    order.insert(count - 1 if place is None else min(place, count - 1), count - 1)
+    return order
 
 
 def dest_of(me, offset, count):
@@ -197,7 +200,7 @@
     def store(c, value):
         physical_ref[c] = value
 
-    to_physical(offsets(count, 2), in_refs, inverse_ref[...], x_ref, store)
+    to_physical(offsets(count, FIRST_SEND), in_refs, inverse_ref[...], x_ref, store)
     for i in range(THETA // CHUNK):
         at = slice(i * CHUNK, (i + 1) * CHUNK)
         velocity = [physical_ref[c, at] for c in range(3)]
@@ -205,7 +208,7 @@
         energy = 0.5 * (velocity[0] * velocity[0] + velocity[1] * velocity[1] + velocity[2] * velocity[2])
         for c, value in enumerate(cross(velocity, magnetic) + [energy]):
             product_ref[c, at] = value.astype(jnp.bfloat16)
-    to_modes(offsets(count, 1), forward_ref, table_ref, product_ref, out_refs)
+    to_modes(offsets(count, FIRST_RETURN), forward_ref, table_ref, product_ref, out_refs)
 
 
 def first_physics(received, inverse, forward):
@@ -237,7 +240,7 @@
     def store(c, value):
         physical_ref[c] = value
 
-    to_physical(offsets(count, 1), in_refs, inverse_ref[...], x_ref, store)
+    to_physical(offsets(count, SECOND), in_refs, inverse_ref[...], x_ref, store)
     for group in range(groups):
         lanes = slice(group * width, (group + 1) * width)
         for i in range(THETA // CHUNK):
@@ -249,7 +252,7 @@
             lorentz = [a + b for a, b in zip(cross(current, magnetic), cross(velocity, vorticity))]
             for c, value in enumerate(lorentz):
                 product_ref[c, at, lanes] = value.astype(jnp.bfloat16)
-    to_modes(offsets(count, 1), forward_ref, table_ref, product_ref, out_refs)
+    to_modes(offsets(count, SECOND), forward_ref, table_ref, product_ref, out_refs)
 
 
 def second_physics(received, physical, inverse, forward):
@@ -277,7 +280,7 @@
     components, held, rows, _ = in_refs[0].shape
     groups = len(in_refs) // count
     for group in range(groups):
-        for step, offset in enumerate(offsets(count, 1)):
+        for step, offset in enumerate(offsets(count, FIRST_RETURN)):
             share = source_of(me, offset, count)
             for t in range(held):
                 at = share * (groups * held) + group * held + t
@@ -442,7 +445,7 @@
     out_rows = mode_count * stride
     copies = []
     for c in range(components):
-        for step, offset in enumerate(offsets(count, 1)):
+        for step, offset in enumerate(offsets(count, SECOND)):
             share = source_of(me, offset, count)
             for start in range(0, tiles, SUBLANES // 2):
                 values = []
@@ -489,12 +492,12 @@
     groups = groups_of(width // count // LANES)
     arrived = []
     for group in range(groups):
-        order = offsets(count, 2)
+        order = offsets(count, FIRST_SEND)
         arrived.append(exchange([pack(mode_fields, 0, 6, offset, group, groups) for offset in order[1:]], order[1:]))
     parcels = [(0, 6, 0, group, groups) for group in range(groups)]
     *own, inverse, forward = pack_rest(mode_fields, parcels, [inverse, forward])
     arrived[0][1:2], carried = lax.optimization_barrier((arrived[0][1:2], [inverse, forward]))
-    order = offsets(count, 1)
+    order = offsets(count, SECOND)
     parcels = [(6, 12, offset, 0, 1) for offset in order]
     *shares, later_inverse, later_forward = pack_rest(mode_fields, parcels, carried)
     local, physical = [], []
@@ -504,7 +507,7 @@
         else:
             tables_here = (inverse, forward)
         *terms, velocity_magnetic = first_physics(joined([own[group]] + arrived[group]), *tables_here)
-        local += exchange(terms, order)
+        local += exchange(terms, offsets(count, FIRST_RETURN))
         physical.append(velocity_magnetic)
     local, shares = lax.optimization_barrier((local, shares))
     sources = exchange(shares, order)

time: 71.1 us -> 69.3 us (0.975)
  waiting for transfers between devices: 25.3 us -> 23.5 us
    ppermute x18, waiting for transfers between devices: 21.6 us -> 19.8 us  [exchange(): received.append(lax.ppermute(piece, 'mode', pairs))]
where the time goes in v10:
time: 69.3 us; the launch traced here: 69.1 us
  starting transfers between devices  29.5 us (43%)
  waiting for transfers between devices  23.5 us (34%)
  Pallas kernels  13.4 us (19%)
  local copies, waits for them, and re-layouts  1.92 us (3%)
  between operations  0.83 us (1%)
    ppermute x18, starting transfers between devices, exchange(): received.append(lax.ppermute(piece, 'mode', pairs))  26.9 us
    ppermute x18, waiting for transfers between devices, exchange(): received.append(lax.ppermute(piece, 'mode', pairs))  19.8 us
    pallas_call x1, Pallas kernels, derive(): pl.pallas_call(functools.partial(derive_kernel, count, len(received)), in...  5.02 us
    ppermute x2, waiting for transfers between devices, from_behind(): lax.ppermute(value, axis, [(source, source + steps) for source in range(i...  3.74 us
    ppermute x2, starting transfers between devices, from_behind(): lax.ppermute(value, axis, [(source, source + steps) for source in range(i...  2.59 us
    unnamed x18, local copies, waits for them, and re-layouts  1.92 us
    pallas_call x2, Pallas kernels, first_physics(): pl.pallas_call(functools.partial(first_kernel, count), in_specs=[vmem()]...  1.64 us
    pallas_call x2, Pallas kernels, pack_rest(): pl.pallas_call(kernel, in_specs=[pl.BlockSpec(memory_space=pl.ANY)] + [vm...  1.62 us
  transfers between devices with their start and end apart: 20, of which 12 were waited for; matrix products, arithmetic and copies ran while one was open for 0% of the time, Pallas kernels for 15%

profile of v10, /device:TPU:0, one launch (start us, length us, event | category | flops | bytes accessed | tf_op | source)
XLA Modules:
  0.0 69.1 jit_solution(10115025513481497374)
XLA Ops:
  0.6 1.9 %copy-done = bf16[12,32,2,2048]{3,2,1,0:T(2,128)(2,1)S(1)} copy-done((bf16[12,32,2,2048]{3,2,1,0:T(2,128)(2,1)S(1)}, bf16[12,32,2,2048]{3,2,1,0:T(2,128)(2,1)}, u32[]{:S(2)}) %copy-start) | copy-done | bytes 3145752
  2.5 0.2 shard_map.102
  2.7 4.0 %collective-permute-start.7 = (bf16[6,2,32,2,128]{4,3,2,1,0:T(2,128)(2,1)S(1)}, bf16[6,2,32,2,128]{4,3,2,1,0:T(2,128)(2,1)S(1)}, u32[]{:S(2)}, u32[]{:S(2)}) collective-permute-start(bf16[6,2,32,2,128]{4,3,2,1,0:T(2,128)(2,1)S(1)} %shard_map.102), channel_id=1, source_target_pairs={{0,24},{8,16},{16,8},{24,0},{1,25},{9,17},{17,9},{25,1},{2,26},{10... | collective-permute-start | bytes 589832 | tf_op jit(solution)/shard_map/ppermute | solution.py:63
  6.6 0.2 shard_map.103
  6.8 0.6 collective-permute-start.8
  7.4 0.2 shard_map.101
  7.6 0.1 collective-permute-start.6
  7.7 0.2 shard_map.97
  7.9 3.0 %collective-permute-start.1 = (bf16[6,2,32,2,128]{4,3,2,1,0:T(2,128)(2,1)S(1)}, bf16[6,2,32,2,128]{4,3,2,1,0:T(2,128)(2,1)S(1)}, u32[]{:S(2)}, u32[]{:S(2)}) collective-permute-start(bf16[6,2,32,2,128]{4,3,2,1,0:T(2,128)(2,1)S(1)} %shard_map.97), channel_id=1, source_target_pairs={{0,24},{8,16},{16,8},{24,0},{1,25},{9,17},{17,9},{25,1},{2,26},{10... | collective-permute-start | bytes 589832 | tf_op jit(solution)/shard_map/ppermute | solution.py:63
  10.8 0.2 shard_map.96
  11.0 0.0 copy-start.4
  11.0 0.6 collective-permute-start
  11.6 0.2 shard_map.98
  11.8 0.6 collective-permute-done.7
  12.4 2.1 %collective-permute-start.2 = (bf16[6,2,32,2,128]{4,3,2,1,0:T(2,128)(2,1)S(1)}, bf16[6,2,32,2,128]{4,3,2,1,0:T(2,128)(2,1)S(1)}, u32[]{:S(2)}, u32[]{:S(2)}) collective-permute-start(bf16[6,2,32,2,128]{4,3,2,1,0:T(2,128)(2,1)S(1)} %shard_map.98), channel_id=1, source_target_pairs={{0,16},{8,24},{16,0},{24,8},{1,17},{9,25},{17,1},{25,9},{2,18},{10... | collective-permute-start | bytes 589832 | tf_op jit(solution)/shard_map/ppermute | solution.py:63
  14.5 0.3 shard_map.95
  14.8 1.9 %collective-permute-done.8 = bf16[6,2,32,2,128]{4,3,2,1,0:T(2,128)(2,1)S(1)} collective-permute-done((bf16[6,2,32,2,128]{4,3,2,1,0:T(2,128)(2,1)S(1)}, bf16[6,2,32,2,128]{4,3,2,1,0:T(2,128)(2,1)S(1)}, u32[]{:S(2)}, u32[]{:S(2)}) %collective-permute-start.8) | collective-permute-done | bytes 196640 | tf_op jit(solution)/shard_map/ppermute | solution.py:63
  16.7 0.5 collective-permute-done.6
  17.2 0.8 %shard_map.104 = (bf16[4,2,64,128]{3,2,1,0:T(8,128)(2,1)S(1)}, bf16[4,2,64,128]{3,2,1,0:T(8,128)(2,1)S(1)}, bf16[4,2,64,128]{3,2,1,0:T(8,128)(2,1)S(1)}, bf16[4,...) custom-call(bf16[6,2,64,128]{3,2,1,0:T(8,128)(2,1)S(1)} %bitcast.35, bf16[6,2,64,128]{3,2,1,0:T(8,128)(2,1)S(1)} %bitcast.34, ...), custom_call_target="tpu_custom_call" | custom-call | flops 1024 | bytes 1024 | tf_op jit(solution)/shard_map/pallas_call | solution.py:218
  18.0 2.5 %collective-permute-start.9 = (bf16[4,2,64,128]{3,2,1,0:T(8,128)(2,1)S(1)}, bf16[4,2,64,128]{3,2,1,0:T(8,128)(2,1)S(1)}, u32[]{:S(2)}, u32[]{:S(2)}) collective-permute-start(bf16[4,2,64,128]{3,2,1,0:T(8,128)(2,1)S(1)} %get-tuple-element.70), channel_id=1, source_target_pairs={{0,24},{8,16},{16,8},{24,0},{1,25},{9,17},{17,9},{25,1},{2,26},{10... | collective-permute-start | bytes 393224 | tf_op jit(solution)/shard_map/ppermute | solution.py:63
  20.5 0.4 collective-permute-done.1
  20.9 2.0 %collective-permute-start.10 = (bf16[4,2,64,128]{3,2,1,0:T(8,128)(2,1)S(1)}, bf16[4,2,64,128]{3,2,1,0:T(8,128)(2,1)S(1)}, u32[]{:S(2)}, u32[]{:S(2)}) collective-permute-start(bf16[4,2,64,128]{3,2,1,0:T(8,128)(2,1)S(1)} %get-tuple-element.71), channel_id=1, source_target_pairs={{0,8},{8,0},{16,24},{24,16},{1,9},{9,1},{17,25},{25,17},{2,10},{10... | collective-permute-start | bytes 393224 | tf_op jit(solution)/shard_map/ppermute | solution.py:63
  22.9 1.5 %collective-permute-start.11 = (bf16[4,2,64,128]{3,2,1,0:T(8,128)(2,1)S(1)}, bf16[4,2,64,128]{3,2,1,0:T(8,128)(2,1)S(1)}, u32[]{:S(2)}, u32[]{:S(2)}) collective-permute-start(bf16[4,2,64,128]{3,2,1,0:T(8,128)(2,1)S(1)} %get-tuple-element.72), channel_id=1, source_target_pairs={{0,16},{8,24},{16,0},{24,8},{1,17},{9,25},{17,1},{25,9},{2,18},{10... | collective-permute-start | bytes 393224 | tf_op jit(solution)/shard_map/ppermute | solution.py:63
  24.4 1.3 %shard_map.99 = (bf16[6,4,32,2,128]{4,3,2,1,0:T(2,128)(2,1)S(1)}, bf16[6,4,32,2,128]{4,3,2,1,0:T(2,128)(2,1)S(1)}, bf16[6,4,32,2,128]{4,3,2,1,0:T(2,128)(2,1)S(1...) custom-call(bf16[12,32,2,2048]{3,2,1,0:T(2,128)(2,1)S(1)} %copy-done.1, ...), custom_call_target="tpu_custom_call" | custom-call | flops 1024 | bytes 1024 | tf_op jit(solution)/shard_map/pallas_call | solution.py:150
  25.7 0.8 %shard_map.100 = (bf16[4,2,64,128]{3,2,1,0:T(8,128)(2,1)S(1)}, bf16[4,2,64,128]{3,2,1,0:T(8,128)(2,1)S(1)}, bf16[4,2,64,128]{3,2,1,0:T(8,128)(2,1)S(1)}, bf16[4,...) custom-call(bf16[6,2,64,128]{3,2,1,0:T(8,128)(2,1)S(1)} %bitcast.31, bf16[6,2,64,128]{3,2,1,0:T(8,128)(2,1)S(1)} %bitcast.29, ...), custom_call_target="tpu_custom_call" | custom-call | flops 1024 | bytes 1024 | tf_op jit(solution)/shard_map/pallas_call | solution.py:218
  26.5 2.4 %collective-permute-start.3 = (bf16[4,2,64,128]{3,2,1,0:T(8,128)(2,1)S(1)}, bf16[4,2,64,128]{3,2,1,0:T(8,128)(2,1)S(1)}, u32[]{:S(2)}, u32[]{:S(2)}) collective-permute-start(bf16[4,2,64,128]{3,2,1,0:T(8,128)(2,1)S(1)} %get-tuple-element.65), channel_id=1, source_target_pairs={{0,24},{8,16},{16,8},{24,0},{1,25},{9,17},{17,9},{25,1},{2,26},{10... | collective-permute-start | bytes 393224 | tf_op jit(solution)/shard_map/ppermute | solution.py:63
  28.9 0.6 collective-permute-start.4
  29.5 0.6 collective-permute-start.5
  30.1 0.3 collective-permute-done.10.refs_6_
  30.4 3.5 %collective-permute-done.3.refs_1_ = bf16[4,2,64,128]{3,2,1,0:T(8,128)(2,1)S(1)} collective-permute-done((bf16[4,2,64,128]{3,2,1,0:T(8,128)(2,1)S(1)}, bf16[4,2,64,128]{3,2,1,0:T(8,128)(2,1)S(1)}, u32[]{:S(2)}, u32[]{:S(2)}) %collective-permute-start.3) | collective-permute-done | bytes 131104 | tf_op jit(solution)/shard_map/ppermute | solution.py:63
  33.9 1.9 %collective-permute-done.4.refs_2_ = bf16[4,2,64,128]{3,2,1,0:T(8,128)(2,1)S(1)} collective-permute-done((bf16[4,2,64,128]{3,2,1,0:T(8,128)(2,1)S(1)}, bf16[4,2,64,128]{3,2,1,0:T(8,128)(2,1)S(1)}, u32[]{:S(2)}, u32[]{:S(2)}) %collective-permute-start.4) | collective-permute-done | bytes 131104 | tf_op jit(solution)/shard_map/ppermute | solution.py:63
  35.8 1.4 %collective-permute-start.12 = (bf16[6,4,32,2,128]{4,3,2,1,0:T(2,128)(2,1)S(1)}, bf16[6,4,32,2,128]{4,3,2,1,0:T(2,128)(2,1)S(1)}, u32[]{:S(2)}, u32[]{:S(2)}) collective-permute-start(bf16[6,4,32,2,128]{4,3,2,1,0:T(2,128)(2,1)S(1)} %get-tuple-element.86), channel_id=1, source_target_pairs={{0,8},{8,0},{16,24},{24,16},{1,9},{9,1},{17,25},{25,17},{2,10},{10... | collective-permute-start | bytes 1179656 | tf_op jit(solution)/shard_map/ppermute | solution.py:63
  37.3 1.0 %collective-permute-start.13 = (bf16[6,4,32,2,128]{4,3,2,1,0:T(2,128)(2,1)S(1)}, bf16[6,4,32,2,128]{4,3,2,1,0:T(2,128)(2,1)S(1)}, u32[]{:S(2)}, u32[]{:S(2)}) collective-permute-start(bf16[6,4,32,2,128]{4,3,2,1,0:T(2,128)(2,1)S(1)} %get-tuple-element.87), channel_id=1, source_target_pairs={{0,16},{8,24},{16,0},{24,8},{1,17},{9,25},{17,1},{25,9},{2,18},{10... | collective-permute-start | bytes 1179656 | tf_op jit(solution)/shard_map/ppermute | solution.py:63
  38.2 1.1 %collective-permute-start.14 = (bf16[6,4,32,2,128]{4,3,2,1,0:T(2,128)(2,1)S(1)}, bf16[6,4,32,2,128]{4,3,2,1,0:T(2,128)(2,1)S(1)}, u32[]{:S(2)}, u32[]{:S(2)}) collective-permute-start(bf16[6,4,32,2,128]{4,3,2,1,0:T(2,128)(2,1)S(1)} %get-tuple-element.88), channel_id=1, source_target_pairs={{0,24},{8,16},{16,8},{24,0},{1,25},{9,17},{17,9},{25,1},{2,26},{10... | collective-permute-start | bytes 1179656 | tf_op jit(solution)/shard_map/ppermute | solution.py:63
  39.3 1.2 %shard_map.105 = (bf16[4,2,64,128]{3,2,1,0:T(8,128)(2,1)S(1)}, bf16[4,2,64,128]{3,2,1,0:T(8,128)(2,1)S(1)}) custom-call(bf16[4,2,64,128]{3,2,1,0:T(8,128)(2,1)S(1)} %get-tuple-element.77.refs_0_, bf16[4,2,64,128]{3,2,1,0:T(8,128)(2,1)S(1)} %collective-permute-done.3.refs_1_, bf16[4,2,64,128]{3,2,1,0:T(8,128)(2,1)S(1)} %collective-permute-done.4.refs_2_, ...), custom_call_target="tpu_custom_call" | custom-call | flops 1024 | bytes 1024 | tf_op jit(solution)/shard_map/pallas_call | solution.py:312
  40.5 1.3 %collective-permute-start.15 = (bf16[4,2,64,128]{3,2,1,0:T(8,128)(2,1)S(1)}, bf16[4,2,64,128]{3,2,1,0:T(8,128)(2,1)S(1)}, u32[]{:S(2)}, u32[]{:S(2)}) collective-permute-start(bf16[4,2,64,128]{3,2,1,0:T(8,128)(2,1)S(1)} %get-tuple-element.89), channel_id=1, source_target_pairs={{0,1},{1,2},{2,3},{3,4},{4,5},{5,6},{6,7},{8,9},{9,10},{10,11},{11... | collective-permute-start | bytes 393224 | tf_op jit(solution)/shard_map/ppermute | solution.py:70
  41.8 1.3 %collective-permute-start.16 = (bf16[4,2,64,128]{3,2,1,0:T(8,128)(2,1)S(1)}, bf16[4,2,64,128]{3,2,1,0:T(8,128)(2,1)S(1)}, u32[]{:S(2)}, u32[]{:S(2)}) collective-permute-start(bf16[4,2,64,128]{3,2,1,0:T(8,128)(2,1)S(1)} %get-tuple-element.90), channel_id=1, source_target_pairs={{1,0},{2,1},{3,2},{4,3},{5,4},{6,5},{7,6},{9,8},{10,9},{11,10},{12... | collective-permute-start | bytes 393224 | tf_op jit(solution)/shard_map/ppermute | solution.py:70
  43.2 3.7 %collective-permute-done.16.refs_9_ = bf16[4,2,64,128]{3,2,1,0:T(8,128)(2,1)S(1)} collective-permute-done((bf16[4,2,64,128]{3,2,1,0:T(8,128)(2,1)S(1)}, bf16[4,2,64,128]{3,2,1,0:T(8,128)(2,1)S(1)}, u32[]{:S(2)}, u32[]{:S(2)}) %collective-permute-start.16) | collective-permute-done | bytes 131104 | tf_op jit(solution)/shard_map/ppermute | solution.py:70
  46.9 1.0 %collective-permute-done.12 = bf16[6,4,32,2,128]{4,3,2,1,0:T(2,128)(2,1)S(1)} collective-permute-done((bf16[6,4,32,2,128]{4,3,2,1,0:T(2,128)(2,1)S(1)}, bf16[6,4,32,2,128]{4,3,2,1,0:T(2,128)(2,1)S(1)}, u32[]{:S(2)}, u32[]{:S(2)}) %collective-permute-start.12) | collective-permute-done | bytes 393248 | tf_op jit(solution)/shard_map/ppermute | solution.py:63
  47.9 6.5 %collective-permute-done.13 = bf16[6,4,32,2,128]{4,3,2,1,0:T(2,128)(2,1)S(1)} collective-permute-done((bf16[6,4,32,2,128]{4,3,2,1,0:T(2,128)(2,1)S(1)}, bf16[6,4,32,2,128]{4,3,2,1,0:T(2,128)(2,1)S(1)}, u32[]{:S(2)}, u32[]{:S(2)}) %collective-permute-start.13) | collective-permute-done | bytes 393248 | tf_op jit(solution)/shard_map/ppermute | solution.py:63
  54.4 1.6 %collective-permute-done.14 = bf16[6,4,32,2,128]{4,3,2,1,0:T(2,128)(2,1)S(1)} collective-permute-done((bf16[6,4,32,2,128]{4,3,2,1,0:T(2,128)(2,1)S(1)}, bf16[6,4,32,2,128]{4,3,2,1,0:T(2,128)(2,1)S(1)}, u32[]{:S(2)}, u32[]{:S(2)}) %collective-permute-start.14) | collective-permute-done | bytes 393248 | tf_op jit(solution)/shard_map/ppermute | solution.py:63
  55.9 1.6 %shard_map.106 = (bf16[3,4,64,128]{3,2,1,0:T(8,128)(2,1)S(1)}, bf16[3,4,64,128]{3,2,1,0:T(8,128)(2,1)S(1)}, bf16[3,4,64,128]{3,2,1,0:T(8,128)(2,1)S(1)}, bf16[3,4,64,128]{3,2,1,0:T(8,128)(2,1)S(1)}) custom-call(bf16[6,4,64,128]{3,2,1,0:T(8,128)(2,1)S(1)} %bitcast.24, bf16[6,4,64,128]{3,2,1,0:T(8,128)(2,1)S(1)} %bitcast.25, ...), custom_call_target="tpu_custom_call" | custom-call | flops 1024 | bytes 1024 | tf_op jit(solution)/shard_map/pallas_call | solution.py:262
  57.5 0.7 %collective-permute-start.17 = (bf16[3,4,64,128]{3,2,1,0:T(8,128)(2,1)S(1)}, bf16[3,4,64,128]{3,2,1,0:T(8,128)(2,1)S(1)}, u32[]{:S(2)}, u32[]{:S(2)}) collective-permute-start(bf16[3,4,64,128]{3,2,1,0:T(8,128)(2,1)S(1)} %get-tuple-element.106), channel_id=1, source_target_pairs={{0,8},{8,0},{16,24},{24,16},{1,9},{9,1},{17,25},{25,17},{2,10},{10... | collective-permute-start | bytes 589832 | tf_op jit(solution)/shard_map/ppermute | solution.py:63
  58.2 1.7 %collective-permute-start.18 = (bf16[3,4,64,128]{3,2,1,0:T(8,128)(2,1)S(1)}, bf16[3,4,64,128]{3,2,1,0:T(8,128)(2,1)S(1)}, u32[]{:S(2)}, u32[]{:S(2)}) collective-permute-start(bf16[3,4,64,128]{3,2,1,0:T(8,128)(2,1)S(1)} %get-tuple-element.107), channel_id=1, source_target_pairs={{0,16},{8,24},{16,0},{24,8},{1,17},{9,25},{17,1},{25,9},{2,18},{10... | collective-permute-start | bytes 589832 | tf_op jit(solution)/shard_map/ppermute | solution.py:63
  59.9 1.2 %collective-permute-start.19 = (bf16[3,4,64,128]{3,2,1,0:T(8,128)(2,1)S(1)}, bf16[3,4,64,128]{3,2,1,0:T(8,128)(2,1)S(1)}, u32[]{:S(2)}, u32[]{:S(2)}) collective-permute-start(bf16[3,4,64,128]{3,2,1,0:T(8,128)(2,1)S(1)} %get-tuple-element.108), channel_id=1, source_target_pairs={{0,24},{8,16},{16,8},{24,0},{1,25},{9,17},{17,9},{25,1},{2,26},{10... | collective-permute-start | bytes 589832 | tf_op jit(solution)/shard_map/ppermute | solution.py:63
  61.1 5.0 %shard_map.107 = (f32[3072,128]{1,0:T(8,128)}, f32[3,16,64,128]{3,2,1,0:T(8,128)S(1)}) custom-call(bf16[4,2,64,128]{3,2,1,0:T(8,128)(2,1)S(1)} %get-tuple-element.77.refs_0_, bf16[4,2,64,128]{3,2,1,0:T(8,128)(2,1)S(1)} %collective-permute-done.3.refs_1_, bf16[4,2,64,128]{3,2,1,0:T(8,128)(2,1)S(1)} %collective-permute-done.4.refs_2_, ...), custom_call_target="tpu_custom_call" | custom-call | flops 1024 | bytes 1024 | tf_op jit(solution)/shard_map/pallas_call | solution.py:424
  66.1 1.6 %collective-permute-done.18.refs_2_ = bf16[3,4,64,128]{3,2,1,0:T(8,128)(2,1)S(1)} collective-permute-done((bf16[3,4,64,128]{3,2,1,0:T(8,128)(2,1)S(1)}, bf16[3,4,64,128]{3,2,1,0:T(8,128)(2,1)S(1)}, u32[]{:S(2)}, u32[]{:S(2)}) %collective-permute-start.18) | collective-permute-done | bytes 196640 | tf_op jit(solution)/shard_map/ppermute | solution.py:63
  67.8 1.3 %shard_map.108 = f32[3072,128]{1,0:T(8,128)} custom-call(bf16[3,4,64,128]{3,2,1,0:T(8,128)(2,1)S(1)} %get-tuple-element.105.refs_0_, bf16[3,4,64,128]{3,2,1,0:T(8,128)(2,1)S(1)} %collective-permute-done.17.refs_1_, bf16[3,4,64,128]{3,2,1,0:T(8,128)(2,1)S(1)} %collective-permute-done.18.refs_2_, bf16[3,4,64,128]{3,2,1,0:T(8,128)(2,1)S(1)} %collective-permute-done.19.refs_3_, ...), custom_call_target="tpu_custom_call" | custom-call | flops 1024 | bytes 1024 | tf_op jit(solution)/shard_map/pallas_call | solution.py:466
  (24 shorter events, 0.1 us)
Async XLA Ops:
  0.6 1.9 %copy-start = (bf16[12,32,2,2048]{3,2,1,0:T(2,128)(2,1)S(1)}, bf16[12,32,2,2048]{3,2,1,0:T(2,128)(2,1)}, u32[]{:S(2)}) copy-start(bf16[12,32,2,2048]{3,2,1,0:T(2,128)(2,1)} %fields_ref.15) | copy-start | bytes 9437188
  2.7 9.7 %collective-permute-start.7 = (bf16[6,2,32,2,128]{4,3,2,1,0:T(2,128)(2,1)S(1)}, bf16[6,2,32,2,128]{4,3,2,1,0:T(2,128)(2,1)S(1)}, u32[]{:S(2)}, u32[]{:S(2)}) collective-permute-start(bf16[6,2,32,2,128]{4,3,2,1,0:T(2,128)(2,1)S(1)} %shard_map.102), channel_id=1, source_target_pairs={{0,24},{8,16},{16,8},{24,0},{1,25},{9,17},{17,9},{25,1},{2,26},{10... | collective-permute-start | bytes 589832 | tf_op jit(solution)/shard_map/ppermute | solution.py:63
  6.8 9.9 %collective-permute-start.8 = (bf16[6,2,32,2,128]{4,3,2,1,0:T(2,128)(2,1)S(1)}, bf16[6,2,32,2,128]{4,3,2,1,0:T(2,128)(2,1)S(1)}, u32[]{:S(2)}, u32[]{:S(2)}) collective-permute-start(bf16[6,2,32,2,128]{4,3,2,1,0:T(2,128)(2,1)S(1)} %shard_map.103), channel_id=1, source_target_pairs={{0,16},{8,24},{16,0},{24,8},{1,17},{9,25},{17,1},{25,9},{2,18},{10... | collective-permute-start | bytes 589832 | tf_op jit(solution)/shard_map/ppermute | solution.py:63
  7.6 9.6 %collective-permute-start.6 = (bf16[6,2,32,2,128]{4,3,2,1,0:T(2,128)(2,1)S(1)}, bf16[6,2,32,2,128]{4,3,2,1,0:T(2,128)(2,1)S(1)}, u32[]{:S(2)}, u32[]{:S(2)}) collective-permute-start(bf16[6,2,32,2,128]{4,3,2,1,0:T(2,128)(2,1)S(1)} %shard_map.101), channel_id=1, source_target_pairs={{0,8},{8,0},{16,24},{24,16},{1,9},{9,1},{17,25},{25,17},{2,10},{10... | collective-permute-start | bytes 589832 | tf_op jit(solution)/shard_map/ppermute | solution.py:63
  7.9 13.0 %collective-permute-start.1 = (bf16[6,2,32,2,128]{4,3,2,1,0:T(2,128)(2,1)S(1)}, bf16[6,2,32,2,128]{4,3,2,1,0:T(2,128)(2,1)S(1)}, u32[]{:S(2)}, u32[]{:S(2)}) collective-permute-start(bf16[6,2,32,2,128]{4,3,2,1,0:T(2,128)(2,1)S(1)} %shard_map.97), channel_id=1, source_target_pairs={{0,24},{8,16},{16,8},{24,0},{1,25},{9,17},{17,9},{25,1},{2,26},{10... | collective-permute-start | bytes 589832 | tf_op jit(solution)/shard_map/ppermute | solution.py:63
  11.0 3.5 %copy-start.4 = (bf16[256,256]{1,0:T(8,128)(2,1)S(1)}, bf16[256,256]{1,0:T(8,128)(2,1)}, u32[]{:S(2)}) copy-start(bf16[256,256]{1,0:T(8,128)(2,1)} %constant.5.clone.refs_1_) | copy-start | bytes 393220
  11.0 3.4 %copy-start.5 = (bf16[256,256]{1,0:T(8,128)(2,1)S(1)}, bf16[256,256]{1,0:T(8,128)(2,1)}, u32[]{:S(2)}) copy-start(bf16[256,256]{1,0:T(8,128)(2,1)} %constant.4.clone.refs_0_) | copy-start | bytes 393220
  11.0 14.7 %collective-permute-start = (bf16[6,2,32,2,128]{4,3,2,1,0:T(2,128)(2,1)S(1)}, bf16[6,2,32,2,128]{4,3,2,1,0:T(2,128)(2,1)S(1)}, u32[]{:S(2)}, u32[]{:S(2)}) collective-permute-start(bf16[6,2,32,2,128]{4,3,2,1,0:T(2,128)(2,1)S(1)} %shard_map.96), channel_id=1, source_target_pairs={{0,8},{8,0},{16,24},{24,16},{1,9},{9,1},{17,25},{25,17},{2,10},{10... | collective-permute-start | bytes 589832 | tf_op jit(solution)/shard_map/ppermute | solution.py:63
  11.8 12.6 %copy-start.1 = (bf16[12,32,2,2048]{3,2,1,0:T(2,128)(2,1)S(1)}, bf16[12,32,2,2048]{3,2,1,0:T(2,128)(2,1)}, u32[]{:S(2)}) copy-start(bf16[12,32,2,2048]{3,2,1,0:T(2,128)(2,1)} %fields_ref.15) | copy-start | bytes 9437188
  12.4 13.3 %collective-permute-start.2 = (bf16[6,2,32,2,128]{4,3,2,1,0:T(2,128)(2,1)S(1)}, bf16[6,2,32,2,128]{4,3,2,1,0:T(2,128)(2,1)S(1)}, u32[]{:S(2)}, u32[]{:S(2)}) collective-permute-start(bf16[6,2,32,2,128]{4,3,2,1,0:T(2,128)(2,1)S(1)} %shard_map.98), channel_id=1, source_target_pairs={{0,16},{8,24},{16,0},{24,8},{1,17},{9,25},{17,1},{25,9},{2,18},{10... | collective-permute-start | bytes 589832 | tf_op jit(solution)/shard_map/ppermute | solution.py:63
  18.0 11.5 %collective-permute-start.9 = (bf16[4,2,64,128]{3,2,1,0:T(8,128)(2,1)S(1)}, bf16[4,2,64,128]{3,2,1,0:T(8,128)(2,1)S(1)}, u32[]{:S(2)}, u32[]{:S(2)}) collective-permute-start(bf16[4,2,64,128]{3,2,1,0:T(8,128)(2,1)S(1)} %get-tuple-element.70), channel_id=1, source_target_pairs={{0,24},{8,16},{16,8},{24,0},{1,25},{9,17},{17,9},{25,1},{2,26},{10... | collective-permute-start | bytes 393224 | tf_op jit(solution)/shard_map/ppermute | solution.py:63
  20.9 9.6 %collective-permute-start.10 = (bf16[4,2,64,128]{3,2,1,0:T(8,128)(2,1)S(1)}, bf16[4,2,64,128]{3,2,1,0:T(8,128)(2,1)S(1)}, u32[]{:S(2)}, u32[]{:S(2)}) collective-permute-start(bf16[4,2,64,128]{3,2,1,0:T(8,128)(2,1)S(1)} %get-tuple-element.71), channel_id=1, source_target_pairs={{0,8},{8,0},{16,24},{24,16},{1,9},{9,1},{17,25},{25,17},{2,10},{10... | collective-permute-start | bytes 393224 | tf_op jit(solution)/shard_map/ppermute | solution.py:63
  22.9 16.4 %copy-start.8 = (s32[2,256]{1,0:T(2,128)S(1)}, s32[2,256]{1,0:T(2,128)}, u32[]{:S(2)}) copy-start(s32[2,256]{1,0:T(2,128)} %refs_8_.1) | copy-start | bytes 6148
  22.9 7.5 %collective-permute-start.11 = (bf16[4,2,64,128]{3,2,1,0:T(8,128)(2,1)S(1)}, bf16[4,2,64,128]{3,2,1,0:T(8,128)(2,1)S(1)}, u32[]{:S(2)}, u32[]{:S(2)}) collective-permute-start(bf16[4,2,64,128]{3,2,1,0:T(8,128)(2,1)S(1)} %get-tuple-element.72), channel_id=1, source_target_pairs={{0,16},{8,24},{16,0},{24,8},{1,17},{9,25},{17,1},{25,9},{2,18},{10... | collective-permute-start | bytes 393224 | tf_op jit(solution)/shard_map/ppermute | solution.py:63
  26.5 7.4 %collective-permute-start.3 = (bf16[4,2,64,128]{3,2,1,0:T(8,128)(2,1)S(1)}, bf16[4,2,64,128]{3,2,1,0:T(8,128)(2,1)S(1)}, u32[]{:S(2)}, u32[]{:S(2)}) collective-permute-start(bf16[4,2,64,128]{3,2,1,0:T(8,128)(2,1)S(1)} %get-tuple-element.65), channel_id=1, source_target_pairs={{0,24},{8,16},{16,8},{24,0},{1,25},{9,17},{17,9},{25,1},{2,26},{10... | collective-permute-start | bytes 393224 | tf_op jit(solution)/shard_map/ppermute | solution.py:63
  28.9 6.9 %collective-permute-start.4 = (bf16[4,2,64,128]{3,2,1,0:T(8,128)(2,1)S(1)}, bf16[4,2,64,128]{3,2,1,0:T(8,128)(2,1)S(1)}, u32[]{:S(2)}, u32[]{:S(2)}) collective-permute-start(bf16[4,2,64,128]{3,2,1,0:T(8,128)(2,1)S(1)} %get-tuple-element.66), channel_id=1, source_target_pairs={{0,8},{8,0},{16,24},{24,16},{1,9},{9,1},{17,25},{25,17},{2,10},{10... | collective-permute-start | bytes 393224 | tf_op jit(solution)/shard_map/ppermute | solution.py:63
  29.5 6.3 %collective-permute-start.5 = (bf16[4,2,64,128]{3,2,1,0:T(8,128)(2,1)S(1)}, bf16[4,2,64,128]{3,2,1,0:T(8,128)(2,1)S(1)}, u32[]{:S(2)}, u32[]{:S(2)}) collective-permute-start(bf16[4,2,64,128]{3,2,1,0:T(8,128)(2,1)S(1)} %get-tuple-element.67), channel_id=1, source_target_pairs={{0,16},{8,24},{16,0},{24,8},{1,17},{9,25},{17,1},{25,9},{2,18},{10... | collective-permute-start | bytes 393224 | tf_op jit(solution)/shard_map/ppermute | solution.py:63
  35.8 12.1 %collective-permute-start.12 = (bf16[6,4,32,2,128]{4,3,2,1,0:T(2,128)(2,1)S(1)}, bf16[6,4,32,2,128]{4,3,2,1,0:T(2,128)(2,1)S(1)}, u32[]{:S(2)}, u32[]{:S(2)}) collective-permute-start(bf16[6,4,32,2,128]{4,3,2,1,0:T(2,128)(2,1)S(1)} %get-tuple-element.86), channel_id=1, source_target_pairs={{0,8},{8,0},{16,24},{24,16},{1,9},{9,1},{17,25},{25,17},{2,10},{10... | collective-permute-start | bytes 1179656 | tf_op jit(solution)/shard_map/ppermute | solution.py:63
  37.3 17.1 %collective-permute-start.13 = (bf16[6,4,32,2,128]{4,3,2,1,0:T(2,128)(2,1)S(1)}, bf16[6,4,32,2,128]{4,3,2,1,0:T(2,128)(2,1)S(1)}, u32[]{:S(2)}, u32[]{:S(2)}) collective-permute-start(bf16[6,4,32,2,128]{4,3,2,1,0:T(2,128)(2,1)S(1)} %get-tuple-element.87), channel_id=1, source_target_pairs={{0,16},{8,24},{16,0},{24,8},{1,17},{9,25},{17,1},{25,9},{2,18},{10... | collective-permute-start | bytes 1179656 | tf_op jit(solution)/shard_map/ppermute | solution.py:63
  38.2 17.7 %collective-permute-start.14 = (bf16[6,4,32,2,128]{4,3,2,1,0:T(2,128)(2,1)S(1)}, bf16[6,4,32,2,128]{4,3,2,1,0:T(2,128)(2,1)S(1)}, u32[]{:S(2)}, u32[]{:S(2)}) collective-permute-start(bf16[6,4,32,2,128]{4,3,2,1,0:T(2,128)(2,1)S(1)} %get-tuple-element.88), channel_id=1, source_target_pairs={{0,24},{8,16},{16,8},{24,0},{1,25},{9,17},{17,9},{25,1},{2,26},{10... | collective-permute-start | bytes 1179656 | tf_op jit(solution)/shard_map/ppermute | solution.py:63
  40.5 2.6 %collective-permute-start.15 = (bf16[4,2,64,128]{3,2,1,0:T(8,128)(2,1)S(1)}, bf16[4,2,64,128]{3,2,1,0:T(8,128)(2,1)S(1)}, u32[]{:S(2)}, u32[]{:S(2)}) collective-permute-start(bf16[4,2,64,128]{3,2,1,0:T(8,128)(2,1)S(1)} %get-tuple-element.89), channel_id=1, source_target_pairs={{0,1},{1,2},{2,3},{3,4},{4,5},{5,6},{6,7},{8,9},{9,10},{10,11},{11... | collective-permute-start | bytes 393224 | tf_op jit(solution)/shard_map/ppermute | solution.py:70
  41.8 5.0 %collective-permute-start.16 = (bf16[4,2,64,128]{3,2,1,0:T(8,128)(2,1)S(1)}, bf16[4,2,64,128]{3,2,1,0:T(8,128)(2,1)S(1)}, u32[]{:S(2)}, u32[]{:S(2)}) collective-permute-start(bf16[4,2,64,128]{3,2,1,0:T(8,128)(2,1)S(1)} %get-tuple-element.90), channel_id=1, source_target_pairs={{1,0},{2,1},{3,2},{4,3},{5,4},{6,5},{7,6},{9,8},{10,9},{11,10},{12... | collective-permute-start | bytes 393224 | tf_op jit(solution)/shard_map/ppermute | solution.py:70
  55.9 5.2 %copy-start.2 = (bf16[5,64,2048]{2,1,0:T(8,128)(2,1)S(1)}, bf16[5,64,2048]{2,1,0:T(8,128)(2,1)}, u32[]{:S(2)}) copy-start(bf16[5,64,2048]{2,1,0:T(8,128)(2,1)} %refs_10_.1) | copy-start | bytes 3932164
  55.9 5.2 %copy-start.3 = (bf16[5,64,2048]{2,1,0:T(8,128)(2,1)S(1)}, bf16[5,64,2048]{2,1,0:T(8,128)(2,1)}, u32[]{:S(2)}) copy-start(bf16[5,64,2048]{2,1,0:T(8,128)(2,1)} %refs_11_.1) | copy-start | bytes 3932164
  55.9 5.2 %copy-start.6 = (f32[2048]{0:T(1024)S(1)}, f32[2048]{0:T(1024)}, u32[]{:S(2)}) copy-start(f32[2048]{0:T(1024)} %param.9) | copy-start | bytes 24580
  55.9 5.2 %copy-start.7 = (s32[32,5]{0,1:T(8,128)S(1)}, s32[32,5]{0,1:T(8,128)}, u32[]{:S(2)}) copy-start(s32[32,5]{0,1:T(8,128)} %param.12) | copy-start | bytes 1924
  57.5 8.6 %collective-permute-start.17 = (bf16[3,4,64,128]{3,2,1,0:T(8,128)(2,1)S(1)}, bf16[3,4,64,128]{3,2,1,0:T(8,128)(2,1)S(1)}, u32[]{:S(2)}, u32[]{:S(2)}) collective-permute-start(bf16[3,4,64,128]{3,2,1,0:T(8,128)(2,1)S(1)} %get-tuple-element.106), channel_id=1, source_target_pairs={{0,8},{8,0},{16,24},{24,16},{1,9},{9,1},{17,25},{25,17},{2,10},{10... | collective-permute-start | bytes 589832 | tf_op jit(solution)/shard_map/ppermute | solution.py:63
  58.2 9.5 %collective-permute-start.18 = (bf16[3,4,64,128]{3,2,1,0:T(8,128)(2,1)S(1)}, bf16[3,4,64,128]{3,2,1,0:T(8,128)(2,1)S(1)}, u32[]{:S(2)}, u32[]{:S(2)}) collective-permute-start(bf16[3,4,64,128]{3,2,1,0:T(8,128)(2,1)S(1)} %get-tuple-element.107), channel_id=1, source_target_pairs={{0,16},{8,24},{16,0},{24,8},{1,17},{9,25},{17,1},{25,9},{2,18},{10... | collective-permute-start | bytes 589832 | tf_op jit(solution)/shard_map/ppermute | solution.py:63
  59.9 7.8 %collective-permute-start.19 = (bf16[3,4,64,128]{3,2,1,0:T(8,128)(2,1)S(1)}, bf16[3,4,64,128]{3,2,1,0:T(8,128)(2,1)S(1)}, u32[]{:S(2)}, u32[]{:S(2)}) collective-permute-start(bf16[3,4,64,128]{3,2,1,0:T(8,128)(2,1)S(1)} %get-tuple-element.108), channel_id=1, source_target_pairs={{0,24},{8,16},{16,8},{24,0},{1,25},{9,17},{17,9},{25,1},{2,26},{10... | collective-permute-start | bytes 589832 | tf_op jit(solution)/shard_map/ppermute | solution.py:63

commit v11 on v10

--- a/solution.py
+++ b/solution.py
@@ -509,7 +509,9 @@
         *terms, velocity_magnetic = first_physics(joined([own[group]] + arrived[group]), *tables_here)
         local += exchange(terms, offsets(count, FIRST_RETURN))
         physical.append(velocity_magnetic)
-    local, shares = lax.optimization_barrier((local, shares))
+    for group in range(groups):
+        held, sent = slice(count if group == 0 else 0, None), slice(1, 2) if group == 0 else slice(2, None)
+        local[held], shares[sent] = lax.optimization_barrier((local[held], shares[sent]))
     sources = exchange(shares, order)
     toward_prev, toward_next = interface(local, interface_nodes, count)
     halos = (from_behind(toward_next, "mer", 1), from_behind(toward_prev, "mer", -1))

time: 69.3 us -> 69 us (level)
  waiting for transfers between devices: 23.5 us -> 21.3 us
  starting transfers between devices: 29.5 us -> 31.4 us
    ppermute x18, waiting for transfers between devices: 19.8 us -> 17.6 us  [exchange(): received.append(lax.ppermute(piece, 'mode', pairs))]
    ppermute x18, starting transfers between devices: 26.9 us -> 28.8 us  [exchange(): received.append(lax.ppermute(piece, 'mode', pairs))]
  transfers between devices with their start and end apart: 20 -> 20, of which waited for: 12 -> 11; matrix products, arithmetic and copies ran while one was open for 0% -> 0% of each run, Pallas kernels for 15% -> 15%
where the time goes in v11:
time: 69 us; the launch traced here: 68.8 us
  starting transfers between devices  31.4 us (46%)
  waiting for transfers between devices  21.3 us (31%)
  Pallas kernels  13.4 us (19%)
  local copies, waits for them, and re-layouts  1.93 us (3%)
  between operations  0.84 us (1%)
    ppermute x18, starting transfers between devices, exchange(): received.append(lax.ppermute(piece, 'mode', pairs))  28.8 us
    ppermute x18, waiting for transfers between devices, exchange(): received.append(lax.ppermute(piece, 'mode', pairs))  17.6 us
    pallas_call x1, Pallas kernels, derive(): pl.pallas_call(functools.partial(derive_kernel, count, len(received)), in...  5.02 us
    ppermute x2, waiting for transfers between devices, from_behind(): lax.ppermute(value, axis, [(source, source + steps) for source in range(i...  3.74 us
    ppermute x2, starting transfers between devices, from_behind(): lax.ppermute(value, axis, [(source, source + steps) for source in range(i...  2.59 us
    unnamed x18, local copies, waits for them, and re-layouts  1.93 us
    pallas_call x2, Pallas kernels, first_physics(): pl.pallas_call(functools.partial(first_kernel, count), in_specs=[vmem()]...  1.64 us
    pallas_call x2, Pallas kernels, pack_rest(): pl.pallas_call(kernel, in_specs=[pl.BlockSpec(memory_space=pl.ANY)] + [vm...  1.62 us
  transfers between devices with their start and end apart: 20, of which 11 were waited for; matrix products, arithmetic and copies ran while one was open for 0% of the time, Pallas kernels for 15%

profile of v11, /device:TPU:0, one launch (start us, length us, event | category | flops | bytes accessed | tf_op | source)
XLA Modules:
  0.0 68.8 jit_solution(15083799570917371430)
XLA Ops:
  0.6 1.9 %copy-done = bf16[12,32,2,2048]{3,2,1,0:T(2,128)(2,1)S(1)} copy-done((bf16[12,32,2,2048]{3,2,1,0:T(2,128)(2,1)S(1)}, bf16[12,32,2,2048]{3,2,1,0:T(2,128)(2,1)}, u32[]{:S(2)}) %copy-start) | copy-done | bytes 3145752
  2.5 0.2 shard_map.102
  2.7 4.0 %collective-permute-start.7 = (bf16[6,2,32,2,128]{4,3,2,1,0:T(2,128)(2,1)S(1)}, bf16[6,2,32,2,128]{4,3,2,1,0:T(2,128)(2,1)S(1)}, u32[]{:S(2)}, u32[]{:S(2)}) collective-permute-start(bf16[6,2,32,2,128]{4,3,2,1,0:T(2,128)(2,1)S(1)} %shard_map.102), channel_id=1, source_target_pairs={{0,24},{8,16},{16,8},{24,0},{1,25},{9,17},{17,9},{25,1},{2,26},{10... | collective-permute-start | bytes 589832 | tf_op jit(solution)/shard_map/ppermute | solution.py:63
  6.6 0.2 shard_map.103
  6.8 0.6 collective-permute-start.8
  7.4 0.2 shard_map.101
  7.6 0.1 collective-permute-start.6
  7.7 0.2 shard_map.97
  7.9 3.0 %collective-permute-start.1 = (bf16[6,2,32,2,128]{4,3,2,1,0:T(2,128)(2,1)S(1)}, bf16[6,2,32,2,128]{4,3,2,1,0:T(2,128)(2,1)S(1)}, u32[]{:S(2)}, u32[]{:S(2)}) collective-permute-start(bf16[6,2,32,2,128]{4,3,2,1,0:T(2,128)(2,1)S(1)} %shard_map.97), channel_id=1, source_target_pairs={{0,24},{8,16},{16,8},{24,0},{1,25},{9,17},{17,9},{25,1},{2,26},{10... | collective-permute-start | bytes 589832 | tf_op jit(solution)/shard_map/ppermute | solution.py:63
  10.8 0.2 shard_map.96
  11.0 0.0 copy-start.4
  11.0 0.0 copy-start.5
  11.0 0.6 collective-permute-start
  11.6 0.2 shard_map.98
  11.8 0.6 collective-permute-done.7
  12.4 2.1 %collective-permute-start.2 = (bf16[6,2,32,2,128]{4,3,2,1,0:T(2,128)(2,1)S(1)}, bf16[6,2,32,2,128]{4,3,2,1,0:T(2,128)(2,1)S(1)}, u32[]{:S(2)}, u32[]{:S(2)}) collective-permute-start(bf16[6,2,32,2,128]{4,3,2,1,0:T(2,128)(2,1)S(1)} %shard_map.98), channel_id=1, source_target_pairs={{0,16},{8,24},{16,0},{24,8},{1,17},{9,25},{17,1},{25,9},{2,18},{10... | collective-permute-start | bytes 589832 | tf_op jit(solution)/shard_map/ppermute | solution.py:63
  14.5 0.3 shard_map.95
  14.8 1.9 %collective-permute-done.8 = bf16[6,2,32,2,128]{4,3,2,1,0:T(2,128)(2,1)S(1)} collective-permute-done((bf16[6,2,32,2,128]{4,3,2,1,0:T(2,128)(2,1)S(1)}, bf16[6,2,32,2,128]{4,3,2,1,0:T(2,128)(2,1)S(1)}, u32[]{:S(2)}, u32[]{:S(2)}) %collective-permute-start.8) | collective-permute-done | bytes 196640 | tf_op jit(solution)/shard_map/ppermute | solution.py:63
  16.7 0.5 collective-permute-done.6
  17.2 0.8 %shard_map.104 = (bf16[4,2,64,128]{3,2,1,0:T(8,128)(2,1)S(1)}, bf16[4,2,64,128]{3,2,1,0:T(8,128)(2,1)S(1)}, bf16[4,2,64,128]{3,2,1,0:T(8,128)(2,1)S(1)}, bf16[4,...) custom-call(bf16[6,2,64,128]{3,2,1,0:T(8,128)(2,1)S(1)} %bitcast.35, bf16[6,2,64,128]{3,2,1,0:T(8,128)(2,1)S(1)} %bitcast.34, ...), custom_call_target="tpu_custom_call" | custom-call | flops 1024 | bytes 1024 | tf_op jit(solution)/shard_map/pallas_call | solution.py:218
  18.0 2.5 %collective-permute-start.9 = (bf16[4,2,64,128]{3,2,1,0:T(8,128)(2,1)S(1)}, bf16[4,2,64,128]{3,2,1,0:T(8,128)(2,1)S(1)}, u32[]{:S(2)}, u32[]{:S(2)}) collective-permute-start(bf16[4,2,64,128]{3,2,1,0:T(8,128)(2,1)S(1)} %get-tuple-element.73), channel_id=1, source_target_pairs={{0,24},{8,16},{16,8},{24,0},{1,25},{9,17},{17,9},{25,1},{2,26},{10... | collective-permute-start | bytes 393224 | tf_op jit(solution)/shard_map/ppermute | solution.py:63
  20.5 0.4 collective-permute-done.1
  20.9 2.0 %collective-permute-start.10 = (bf16[4,2,64,128]{3,2,1,0:T(8,128)(2,1)S(1)}, bf16[4,2,64,128]{3,2,1,0:T(8,128)(2,1)S(1)}, u32[]{:S(2)}, u32[]{:S(2)}) collective-permute-start(bf16[4,2,64,128]{3,2,1,0:T(8,128)(2,1)S(1)} %get-tuple-element.74), channel_id=1, source_target_pairs={{0,8},{8,0},{16,24},{24,16},{1,9},{9,1},{17,25},{25,17},{2,10},{10... | collective-permute-start | bytes 393224 | tf_op jit(solution)/shard_map/ppermute | solution.py:63
  22.9 1.5 %collective-permute-start.11 = (bf16[4,2,64,128]{3,2,1,0:T(8,128)(2,1)S(1)}, bf16[4,2,64,128]{3,2,1,0:T(8,128)(2,1)S(1)}, u32[]{:S(2)}, u32[]{:S(2)}) collective-permute-start(bf16[4,2,64,128]{3,2,1,0:T(8,128)(2,1)S(1)} %get-tuple-element.75), channel_id=1, source_target_pairs={{0,16},{8,24},{16,0},{24,8},{1,17},{9,25},{17,1},{25,9},{2,18},{10... | collective-permute-start | bytes 393224 | tf_op jit(solution)/shard_map/ppermute | solution.py:63
  24.4 1.3 %shard_map.99 = (bf16[6,4,32,2,128]{4,3,2,1,0:T(2,128)(2,1)S(1)}, bf16[6,4,32,2,128]{4,3,2,1,0:T(2,128)(2,1)S(1)}, bf16[6,4,32,2,128]{4,3,2,1,0:T(2,128)(2,1)S(1...) custom-call(bf16[12,32,2,2048]{3,2,1,0:T(2,128)(2,1)S(1)} %copy-done.1, ...), custom_call_target="tpu_custom_call" | custom-call | flops 1024 | bytes 1024 | tf_op jit(solution)/shard_map/pallas_call | solution.py:150
  25.7 0.8 %shard_map.100 = (bf16[4,2,64,128]{3,2,1,0:T(8,128)(2,1)S(1)}, bf16[4,2,64,128]{3,2,1,0:T(8,128)(2,1)S(1)}, bf16[4,2,64,128]{3,2,1,0:T(8,128)(2,1)S(1)}, bf16[4,...) custom-call(bf16[6,2,64,128]{3,2,1,0:T(8,128)(2,1)S(1)} %bitcast.31, bf16[6,2,64,128]{3,2,1,0:T(8,128)(2,1)S(1)} %bitcast.29, ...), custom_call_target="tpu_custom_call" | custom-call | flops 1024 | bytes 1024 | tf_op jit(solution)/shard_map/pallas_call | solution.py:218
  26.5 2.4 %collective-permute-start.3 = (bf16[4,2,64,128]{3,2,1,0:T(8,128)(2,1)S(1)}, bf16[4,2,64,128]{3,2,1,0:T(8,128)(2,1)S(1)}, u32[]{:S(2)}, u32[]{:S(2)}) collective-permute-start(bf16[4,2,64,128]{3,2,1,0:T(8,128)(2,1)S(1)} %get-tuple-element.68), channel_id=1, source_target_pairs={{0,24},{8,16},{16,8},{24,0},{1,25},{9,17},{17,9},{25,1},{2,26},{10... | collective-permute-start | bytes 393224 | tf_op jit(solution)/shard_map/ppermute | solution.py:63
  28.9 0.6 collective-permute-start.4
  29.5 0.6 collective-permute-start.5
  30.1 0.3 collective-permute-done.10.refs_6_
  30.4 2.3 %collective-permute-start.12 = (bf16[6,4,32,2,128]{4,3,2,1,0:T(2,128)(2,1)S(1)}, bf16[6,4,32,2,128]{4,3,2,1,0:T(2,128)(2,1)S(1)}, u32[]{:S(2)}, u32[]{:S(2)}) collective-permute-start(bf16[6,4,32,2,128]{4,3,2,1,0:T(2,128)(2,1)S(1)} %get-tuple-element.92), channel_id=1, source_target_pairs={{0,8},{8,0},{16,24},{24,16},{1,9},{9,1},{17,25},{25,17},{2,10},{10... | collective-permute-start | bytes 1179656 | tf_op jit(solution)/shard_map/ppermute | solution.py:63
  32.7 1.2 %collective-permute-done.3.refs_1_ = bf16[4,2,64,128]{3,2,1,0:T(8,128)(2,1)S(1)} collective-permute-done((bf16[4,2,64,128]{3,2,1,0:T(8,128)(2,1)S(1)}, bf16[4,2,64,128]{3,2,1,0:T(8,128)(2,1)S(1)}, u32[]{:S(2)}, u32[]{:S(2)}) %collective-permute-start.3) | collective-permute-done | bytes 131104 | tf_op jit(solution)/shard_map/ppermute | solution.py:63
  33.9 2.8 %collective-permute-done.4.refs_2_ = bf16[4,2,64,128]{3,2,1,0:T(8,128)(2,1)S(1)} collective-permute-done((bf16[4,2,64,128]{3,2,1,0:T(8,128)(2,1)S(1)}, bf16[4,2,64,128]{3,2,1,0:T(8,128)(2,1)S(1)}, u32[]{:S(2)}, u32[]{:S(2)}) %collective-permute-start.4) | collective-permute-done | bytes 131104 | tf_op jit(solution)/shard_map/ppermute | solution.py:63
  36.7 0.6 collective-permute-start.13
  37.3 2.5 %collective-permute-start.14 = (bf16[6,4,32,2,128]{4,3,2,1,0:T(2,128)(2,1)S(1)}, bf16[6,4,32,2,128]{4,3,2,1,0:T(2,128)(2,1)S(1)}, u32[]{:S(2)}, u32[]{:S(2)}) collective-permute-start(bf16[6,4,32,2,128]{4,3,2,1,0:T(2,128)(2,1)S(1)} %get-tuple-element.94), channel_id=1, source_target_pairs={{0,24},{8,16},{16,8},{24,0},{1,25},{9,17},{17,9},{25,1},{2,26},{10... | collective-permute-start | bytes 1179656 | tf_op jit(solution)/shard_map/ppermute | solution.py:63
  39.8 1.2 %shard_map.105 = (bf16[4,2,64,128]{3,2,1,0:T(8,128)(2,1)S(1)}, bf16[4,2,64,128]{3,2,1,0:T(8,128)(2,1)S(1)}) custom-call(bf16[4,2,64,128]{3,2,1,0:T(8,128)(2,1)S(1)} %get-tuple-element.83.refs_0_, bf16[4,2,64,128]{3,2,1,0:T(8,128)(2,1)S(1)} %collective-permute-done.3.refs_1_, bf16[4,2,64,128]{3,2,1,0:T(8,128)(2,1)S(1)} %collective-permute-done.4.refs_2_, ...), custom_call_target="tpu_custom_call" | custom-call | flops 1024 | bytes 1024 | tf_op jit(solution)/shard_map/pallas_call | solution.py:312
  41.1 1.3 %collective-permute-start.15 = (bf16[4,2,64,128]{3,2,1,0:T(8,128)(2,1)S(1)}, bf16[4,2,64,128]{3,2,1,0:T(8,128)(2,1)S(1)}, u32[]{:S(2)}, u32[]{:S(2)}) collective-permute-start(bf16[4,2,64,128]{3,2,1,0:T(8,128)(2,1)S(1)} %get-tuple-element.95), channel_id=1, source_target_pairs={{0,1},{1,2},{2,3},{3,4},{4,5},{5,6},{6,7},{8,9},{9,10},{10,11},{11... | collective-permute-start | bytes 393224 | tf_op jit(solution)/shard_map/ppermute | solution.py:70
  42.4 1.3 %collective-permute-start.16 = (bf16[4,2,64,128]{3,2,1,0:T(8,128)(2,1)S(1)}, bf16[4,2,64,128]{3,2,1,0:T(8,128)(2,1)S(1)}, u32[]{:S(2)}, u32[]{:S(2)}) collective-permute-start(bf16[4,2,64,128]{3,2,1,0:T(8,128)(2,1)S(1)} %get-tuple-element.96), channel_id=1, source_target_pairs={{1,0},{2,1},{3,2},{4,3},{5,4},{6,5},{7,6},{9,8},{10,9},{11,10},{12... | collective-permute-start | bytes 393224 | tf_op jit(solution)/shard_map/ppermute | solution.py:70
  43.7 3.7 %collective-permute-done.16.refs_9_ = bf16[4,2,64,128]{3,2,1,0:T(8,128)(2,1)S(1)} collective-permute-done((bf16[4,2,64,128]{3,2,1,0:T(8,128)(2,1)S(1)}, bf16[4,2,64,128]{3,2,1,0:T(8,128)(2,1)S(1)}, u32[]{:S(2)}, u32[]{:S(2)}) %collective-permute-start.16) | collective-permute-done | bytes 131104 | tf_op jit(solution)/shard_map/ppermute | solution.py:70
  47.4 7.3 %collective-permute-done.13 = bf16[6,4,32,2,128]{4,3,2,1,0:T(2,128)(2,1)S(1)} collective-permute-done((bf16[6,4,32,2,128]{4,3,2,1,0:T(2,128)(2,1)S(1)}, bf16[6,4,32,2,128]{4,3,2,1,0:T(2,128)(2,1)S(1)}, u32[]{:S(2)}, u32[]{:S(2)}) %collective-permute-start.13) | collective-permute-done | bytes 393248 | tf_op jit(solution)/shard_map/ppermute | solution.py:63
  54.8 1.6 %shard_map.106 = (bf16[3,4,64,128]{3,2,1,0:T(8,128)(2,1)S(1)}, bf16[3,4,64,128]{3,2,1,0:T(8,128)(2,1)S(1)}, bf16[3,4,64,128]{3,2,1,0:T(8,128)(2,1)S(1)}, bf16[3,4,64,128]{3,2,1,0:T(8,128)(2,1)S(1)}) custom-call(bf16[6,4,64,128]{3,2,1,0:T(8,128)(2,1)S(1)} %bitcast.24, bf16[6,4,64,128]{3,2,1,0:T(8,128)(2,1)S(1)} %bitcast.25, ...), custom_call_target="tpu_custom_call" | custom-call | flops 1024 | bytes 1024 | tf_op jit(solution)/shard_map/pallas_call | solution.py:262
  56.4 1.3 %collective-permute-start.17 = (bf16[3,4,64,128]{3,2,1,0:T(8,128)(2,1)S(1)}, bf16[3,4,64,128]{3,2,1,0:T(8,128)(2,1)S(1)}, u32[]{:S(2)}, u32[]{:S(2)}) collective-permute-start(bf16[3,4,64,128]{3,2,1,0:T(8,128)(2,1)S(1)} %get-tuple-element.112), channel_id=1, source_target_pairs={{0,8},{8,0},{16,24},{24,16},{1,9},{9,1},{17,25},{25,17},{2,10},{10... | collective-permute-start | bytes 589832 | tf_op jit(solution)/shard_map/ppermute | solution.py:63
  57.6 1.2 %collective-permute-start.18 = (bf16[3,4,64,128]{3,2,1,0:T(8,128)(2,1)S(1)}, bf16[3,4,64,128]{3,2,1,0:T(8,128)(2,1)S(1)}, u32[]{:S(2)}, u32[]{:S(2)}) collective-permute-start(bf16[3,4,64,128]{3,2,1,0:T(8,128)(2,1)S(1)} %get-tuple-element.113), channel_id=1, source_target_pairs={{0,16},{8,24},{16,0},{24,8},{1,17},{9,25},{17,1},{25,9},{2,18},{10... | collective-permute-start | bytes 589832 | tf_op jit(solution)/shard_map/ppermute | solution.py:63
  58.8 1.1 %collective-permute-start.19 = (bf16[3,4,64,128]{3,2,1,0:T(8,128)(2,1)S(1)}, bf16[3,4,64,128]{3,2,1,0:T(8,128)(2,1)S(1)}, u32[]{:S(2)}, u32[]{:S(2)}) collective-permute-start(bf16[3,4,64,128]{3,2,1,0:T(8,128)(2,1)S(1)} %get-tuple-element.114), channel_id=1, source_target_pairs={{0,24},{8,16},{16,8},{24,0},{1,25},{9,17},{17,9},{25,1},{2,26},{10... | collective-permute-start | bytes 589832 | tf_op jit(solution)/shard_map/ppermute | solution.py:63
  59.9 5.0 %shard_map.107 = (f32[3072,128]{1,0:T(8,128)}, f32[3,16,64,128]{3,2,1,0:T(8,128)S(1)}) custom-call(bf16[4,2,64,128]{3,2,1,0:T(8,128)(2,1)S(1)} %get-tuple-element.83.refs_0_, bf16[4,2,64,128]{3,2,1,0:T(8,128)(2,1)S(1)} %collective-permute-done.3.refs_1_, bf16[4,2,64,128]{3,2,1,0:T(8,128)(2,1)S(1)} %collective-permute-done.4.refs_2_, ...), custom_call_target="tpu_custom_call" | custom-call | flops 1024 | bytes 1024 | tf_op jit(solution)/shard_map/pallas_call | solution.py:424
  65.0 0.7 %collective-permute-done.18.refs_2_ = bf16[3,4,64,128]{3,2,1,0:T(8,128)(2,1)S(1)} collective-permute-done((bf16[3,4,64,128]{3,2,1,0:T(8,128)(2,1)S(1)}, bf16[3,4,64,128]{3,2,1,0:T(8,128)(2,1)S(1)}, u32[]{:S(2)}, u32[]{:S(2)}) %collective-permute-start.18) | collective-permute-done | bytes 196640 | tf_op jit(solution)/shard_map/ppermute | solution.py:63
  65.7 1.8 %collective-permute-done.19.refs_3_ = bf16[3,4,64,128]{3,2,1,0:T(8,128)(2,1)S(1)} collective-permute-done((bf16[3,4,64,128]{3,2,1,0:T(8,128)(2,1)S(1)}, bf16[3,4,64,128]{3,2,1,0:T(8,128)(2,1)S(1)}, u32[]{:S(2)}, u32[]{:S(2)}) %collective-permute-start.19) | collective-permute-done | bytes 196640 | tf_op jit(solution)/shard_map/ppermute | solution.py:63
  67.5 1.3 %shard_map.108 = f32[3072,128]{1,0:T(8,128)} custom-call(bf16[3,4,64,128]{3,2,1,0:T(8,128)(2,1)S(1)} %get-tuple-element.111.refs_0_, bf16[3,4,64,128]{3,2,1,0:T(8,128)(2,1)S(1)} %collective-permute-done.17.refs_1_, bf16[3,4,64,128]{3,2,1,0:T(8,128)(2,1)S(1)} %collective-permute-done.18.refs_2_, bf16[3,4,64,128]{3,2,1,0:T(8,128)(2,1)S(1)} %collective-permute-done.19.refs_3_, ...), custom_call_target="tpu_custom_call" | custom-call | flops 1024 | bytes 1024 | tf_op jit(solution)/shard_map/pallas_call | solution.py:466
  (24 shorter events, 0.1 us)
Async XLA Ops:
  0.6 1.9 %copy-start = (bf16[12,32,2,2048]{3,2,1,0:T(2,128)(2,1)S(1)}, bf16[12,32,2,2048]{3,2,1,0:T(2,128)(2,1)}, u32[]{:S(2)}) copy-start(bf16[12,32,2,2048]{3,2,1,0:T(2,128)(2,1)} %fields_ref.15) | copy-start | bytes 9437188
  2.7 9.7 %collective-permute-start.7 = (bf16[6,2,32,2,128]{4,3,2,1,0:T(2,128)(2,1)S(1)}, bf16[6,2,32,2,128]{4,3,2,1,0:T(2,128)(2,1)S(1)}, u32[]{:S(2)}, u32[]{:S(2)}) collective-permute-start(bf16[6,2,32,2,128]{4,3,2,1,0:T(2,128)(2,1)S(1)} %shard_map.102), channel_id=1, source_target_pairs={{0,24},{8,16},{16,8},{24,0},{1,25},{9,17},{17,9},{25,1},{2,26},{10... | collective-permute-start | bytes 589832 | tf_op jit(solution)/shard_map/ppermute | solution.py:63
  6.8 9.9 %collective-permute-start.8 = (bf16[6,2,32,2,128]{4,3,2,1,0:T(2,128)(2,1)S(1)}, bf16[6,2,32,2,128]{4,3,2,1,0:T(2,128)(2,1)S(1)}, u32[]{:S(2)}, u32[]{:S(2)}) collective-permute-start(bf16[6,2,32,2,128]{4,3,2,1,0:T(2,128)(2,1)S(1)} %shard_map.103), channel_id=1, source_target_pairs={{0,16},{8,24},{16,0},{24,8},{1,17},{9,25},{17,1},{25,9},{2,18},{10... | collective-permute-start | bytes 589832 | tf_op jit(solution)/shard_map/ppermute | solution.py:63
  7.6 9.6 %collective-permute-start.6 = (bf16[6,2,32,2,128]{4,3,2,1,0:T(2,128)(2,1)S(1)}, bf16[6,2,32,2,128]{4,3,2,1,0:T(2,128)(2,1)S(1)}, u32[]{:S(2)}, u32[]{:S(2)}) collective-permute-start(bf16[6,2,32,2,128]{4,3,2,1,0:T(2,128)(2,1)S(1)} %shard_map.101), channel_id=1, source_target_pairs={{0,8},{8,0},{16,24},{24,16},{1,9},{9,1},{17,25},{25,17},{2,10},{10... | collective-permute-start | bytes 589832 | tf_op jit(solution)/shard_map/ppermute | solution.py:63
  7.9 13.0 %collective-permute-start.1 = (bf16[6,2,32,2,128]{4,3,2,1,0:T(2,128)(2,1)S(1)}, bf16[6,2,32,2,128]{4,3,2,1,0:T(2,128)(2,1)S(1)}, u32[]{:S(2)}, u32[]{:S(2)}) collective-permute-start(bf16[6,2,32,2,128]{4,3,2,1,0:T(2,128)(2,1)S(1)} %shard_map.97), channel_id=1, source_target_pairs={{0,24},{8,16},{16,8},{24,0},{1,25},{9,17},{17,9},{25,1},{2,26},{10... | collective-permute-start | bytes 589832 | tf_op jit(solution)/shard_map/ppermute | solution.py:63
  11.0 3.5 %copy-start.4 = (bf16[256,256]{1,0:T(8,128)(2,1)S(1)}, bf16[256,256]{1,0:T(8,128)(2,1)}, u32[]{:S(2)}) copy-start(bf16[256,256]{1,0:T(8,128)(2,1)} %constant.5.clone.refs_1_) | copy-start | bytes 393220
  11.0 3.4 %copy-start.5 = (bf16[256,256]{1,0:T(8,128)(2,1)S(1)}, bf16[256,256]{1,0:T(8,128)(2,1)}, u32[]{:S(2)}) copy-start(bf16[256,256]{1,0:T(8,128)(2,1)} %constant.4.clone.refs_0_) | copy-start | bytes 393220
  11.0 14.7 %collective-permute-start = (bf16[6,2,32,2,128]{4,3,2,1,0:T(2,128)(2,1)S(1)}, bf16[6,2,32,2,128]{4,3,2,1,0:T(2,128)(2,1)S(1)}, u32[]{:S(2)}, u32[]{:S(2)}) collective-permute-start(bf16[6,2,32,2,128]{4,3,2,1,0:T(2,128)(2,1)S(1)} %shard_map.96), channel_id=1, source_target_pairs={{0,8},{8,0},{16,24},{24,16},{1,9},{9,1},{17,25},{25,17},{2,10},{10... | collective-permute-start | bytes 589832 | tf_op jit(solution)/shard_map/ppermute | solution.py:63
  11.8 12.6 %copy-start.1 = (bf16[12,32,2,2048]{3,2,1,0:T(2,128)(2,1)S(1)}, bf16[12,32,2,2048]{3,2,1,0:T(2,128)(2,1)}, u32[]{:S(2)}) copy-start(bf16[12,32,2,2048]{3,2,1,0:T(2,128)(2,1)} %fields_ref.15) | copy-start | bytes 9437188
  12.4 13.3 %collective-permute-start.2 = (bf16[6,2,32,2,128]{4,3,2,1,0:T(2,128)(2,1)S(1)}, bf16[6,2,32,2,128]{4,3,2,1,0:T(2,128)(2,1)S(1)}, u32[]{:S(2)}, u32[]{:S(2)}) collective-permute-start(bf16[6,2,32,2,128]{4,3,2,1,0:T(2,128)(2,1)S(1)} %shard_map.98), channel_id=1, source_target_pairs={{0,16},{8,24},{16,0},{24,8},{1,17},{9,25},{17,1},{25,9},{2,18},{10... | collective-permute-start | bytes 589832 | tf_op jit(solution)/shard_map/ppermute | solution.py:63
  18.0 11.5 %collective-permute-start.9 = (bf16[4,2,64,128]{3,2,1,0:T(8,128)(2,1)S(1)}, bf16[4,2,64,128]{3,2,1,0:T(8,128)(2,1)S(1)}, u32[]{:S(2)}, u32[]{:S(2)}) collective-permute-start(bf16[4,2,64,128]{3,2,1,0:T(8,128)(2,1)S(1)} %get-tuple-element.73), channel_id=1, source_target_pairs={{0,24},{8,16},{16,8},{24,0},{1,25},{9,17},{17,9},{25,1},{2,26},{10... | collective-permute-start | bytes 393224 | tf_op jit(solution)/shard_map/ppermute | solution.py:63
  20.9 9.6 %collective-permute-start.10 = (bf16[4,2,64,128]{3,2,1,0:T(8,128)(2,1)S(1)}, bf16[4,2,64,128]{3,2,1,0:T(8,128)(2,1)S(1)}, u32[]{:S(2)}, u32[]{:S(2)}) collective-permute-start(bf16[4,2,64,128]{3,2,1,0:T(8,128)(2,1)S(1)} %get-tuple-element.74), channel_id=1, source_target_pairs={{0,8},{8,0},{16,24},{24,16},{1,9},{9,1},{17,25},{25,17},{2,10},{10... | collective-permute-start | bytes 393224 | tf_op jit(solution)/shard_map/ppermute | solution.py:63
  22.9 16.9 %copy-start.8 = (s32[2,256]{1,0:T(2,128)S(1)}, s32[2,256]{1,0:T(2,128)}, u32[]{:S(2)}) copy-start(s32[2,256]{1,0:T(2,128)} %refs_8_.1) | copy-start | bytes 6148
  22.9 7.5 %collective-permute-start.11 = (bf16[4,2,64,128]{3,2,1,0:T(8,128)(2,1)S(1)}, bf16[4,2,64,128]{3,2,1,0:T(8,128)(2,1)S(1)}, u32[]{:S(2)}, u32[]{:S(2)}) collective-permute-start(bf16[4,2,64,128]{3,2,1,0:T(8,128)(2,1)S(1)} %get-tuple-element.75), channel_id=1, source_target_pairs={{0,16},{8,24},{16,0},{24,8},{1,17},{9,25},{17,1},{25,9},{2,18},{10... | collective-permute-start | bytes 393224 | tf_op jit(solution)/shard_map/ppermute | solution.py:63
  26.5 7.4 %collective-permute-start.3 = (bf16[4,2,64,128]{3,2,1,0:T(8,128)(2,1)S(1)}, bf16[4,2,64,128]{3,2,1,0:T(8,128)(2,1)S(1)}, u32[]{:S(2)}, u32[]{:S(2)}) collective-permute-start(bf16[4,2,64,128]{3,2,1,0:T(8,128)(2,1)S(1)} %get-tuple-element.68), channel_id=1, source_target_pairs={{0,24},{8,16},{16,8},{24,0},{1,25},{9,17},{17,9},{25,1},{2,26},{10... | collective-permute-start | bytes 393224 | tf_op jit(solution)/shard_map/ppermute | solution.py:63
  28.9 7.8 %collective-permute-start.4 = (bf16[4,2,64,128]{3,2,1,0:T(8,128)(2,1)S(1)}, bf16[4,2,64,128]{3,2,1,0:T(8,128)(2,1)S(1)}, u32[]{:S(2)}, u32[]{:S(2)}) collective-permute-start(bf16[4,2,64,128]{3,2,1,0:T(8,128)(2,1)S(1)} %get-tuple-element.69), channel_id=1, source_target_pairs={{0,8},{8,0},{16,24},{24,16},{1,9},{9,1},{17,25},{25,17},{2,10},{10... | collective-permute-start | bytes 393224 | tf_op jit(solution)/shard_map/ppermute | solution.py:63
  29.5 7.2 %collective-permute-start.5 = (bf16[4,2,64,128]{3,2,1,0:T(8,128)(2,1)S(1)}, bf16[4,2,64,128]{3,2,1,0:T(8,128)(2,1)S(1)}, u32[]{:S(2)}, u32[]{:S(2)}) collective-permute-start(bf16[4,2,64,128]{3,2,1,0:T(8,128)(2,1)S(1)} %get-tuple-element.70), channel_id=1, source_target_pairs={{0,16},{8,24},{16,0},{24,8},{1,17},{9,25},{17,1},{25,9},{2,18},{10... | collective-permute-start | bytes 393224 | tf_op jit(solution)/shard_map/ppermute | solution.py:63
  30.4 17.0 %collective-permute-start.12 = (bf16[6,4,32,2,128]{4,3,2,1,0:T(2,128)(2,1)S(1)}, bf16[6,4,32,2,128]{4,3,2,1,0:T(2,128)(2,1)S(1)}, u32[]{:S(2)}, u32[]{:S(2)}) collective-permute-start(bf16[6,4,32,2,128]{4,3,2,1,0:T(2,128)(2,1)S(1)} %get-tuple-element.92), channel_id=1, source_target_pairs={{0,8},{8,0},{16,24},{24,16},{1,9},{9,1},{17,25},{25,17},{2,10},{10... | collective-permute-start | bytes 1179656 | tf_op jit(solution)/shard_map/ppermute | solution.py:63
  36.7 18.0 %collective-permute-start.13 = (bf16[6,4,32,2,128]{4,3,2,1,0:T(2,128)(2,1)S(1)}, bf16[6,4,32,2,128]{4,3,2,1,0:T(2,128)(2,1)S(1)}, u32[]{:S(2)}, u32[]{:S(2)}) collective-permute-start(bf16[6,4,32,2,128]{4,3,2,1,0:T(2,128)(2,1)S(1)} %get-tuple-element.93), channel_id=1, source_target_pairs={{0,16},{8,24},{16,0},{24,8},{1,17},{9,25},{17,1},{25,9},{2,18},{10... | collective-permute-start | bytes 1179656 | tf_op jit(solution)/shard_map/ppermute | solution.py:63
  37.3 17.5 %collective-permute-start.14 = (bf16[6,4,32,2,128]{4,3,2,1,0:T(2,128)(2,1)S(1)}, bf16[6,4,32,2,128]{4,3,2,1,0:T(2,128)(2,1)S(1)}, u32[]{:S(2)}, u32[]{:S(2)}) collective-permute-start(bf16[6,4,32,2,128]{4,3,2,1,0:T(2,128)(2,1)S(1)} %get-tuple-element.94), channel_id=1, source_target_pairs={{0,24},{8,16},{16,8},{24,0},{1,25},{9,17},{17,9},{25,1},{2,26},{10... | collective-permute-start | bytes 1179656 | tf_op jit(solution)/shard_map/ppermute | solution.py:63
  41.1 2.6 %collective-permute-start.15 = (bf16[4,2,64,128]{3,2,1,0:T(8,128)(2,1)S(1)}, bf16[4,2,64,128]{3,2,1,0:T(8,128)(2,1)S(1)}, u32[]{:S(2)}, u32[]{:S(2)}) collective-permute-start(bf16[4,2,64,128]{3,2,1,0:T(8,128)(2,1)S(1)} %get-tuple-element.95), channel_id=1, source_target_pairs={{0,1},{1,2},{2,3},{3,4},{4,5},{5,6},{6,7},{8,9},{9,10},{10,11},{11... | collective-permute-start | bytes 393224 | tf_op jit(solution)/shard_map/ppermute | solution.py:70
  42.4 5.0 %collective-permute-start.16 = (bf16[4,2,64,128]{3,2,1,0:T(8,128)(2,1)S(1)}, bf16[4,2,64,128]{3,2,1,0:T(8,128)(2,1)S(1)}, u32[]{:S(2)}, u32[]{:S(2)}) collective-permute-start(bf16[4,2,64,128]{3,2,1,0:T(8,128)(2,1)S(1)} %get-tuple-element.96), channel_id=1, source_target_pairs={{1,0},{2,1},{3,2},{4,3},{5,4},{6,5},{7,6},{9,8},{10,9},{11,10},{12... | collective-permute-start | bytes 393224 | tf_op jit(solution)/shard_map/ppermute | solution.py:70
  54.8 5.2 %copy-start.2 = (bf16[5,64,2048]{2,1,0:T(8,128)(2,1)S(1)}, bf16[5,64,2048]{2,1,0:T(8,128)(2,1)}, u32[]{:S(2)}) copy-start(bf16[5,64,2048]{2,1,0:T(8,128)(2,1)} %refs_10_.1) | copy-start | bytes 3932164
  54.8 5.2 %copy-start.3 = (bf16[5,64,2048]{2,1,0:T(8,128)(2,1)S(1)}, bf16[5,64,2048]{2,1,0:T(8,128)(2,1)}, u32[]{:S(2)}) copy-start(bf16[5,64,2048]{2,1,0:T(8,128)(2,1)} %refs_11_.1) | copy-start | bytes 3932164
  54.8 5.2 %copy-start.6 = (f32[2048]{0:T(1024)S(1)}, f32[2048]{0:T(1024)}, u32[]{:S(2)}) copy-start(f32[2048]{0:T(1024)} %param.9) | copy-start | bytes 24580
  54.8 5.2 %copy-start.7 = (s32[32,5]{0,1:T(8,128)S(1)}, s32[32,5]{0,1:T(8,128)}, u32[]{:S(2)}) copy-start(s32[32,5]{0,1:T(8,128)} %param.12) | copy-start | bytes 1924
  56.4 8.6 %collective-permute-start.17 = (bf16[3,4,64,128]{3,2,1,0:T(8,128)(2,1)S(1)}, bf16[3,4,64,128]{3,2,1,0:T(8,128)(2,1)S(1)}, u32[]{:S(2)}, u32[]{:S(2)}) collective-permute-start(bf16[3,4,64,128]{3,2,1,0:T(8,128)(2,1)S(1)} %get-tuple-element.112), channel_id=1, source_target_pairs={{0,8},{8,0},{16,24},{24,16},{1,9},{9,1},{17,25},{25,17},{2,10},{10... | collective-permute-start | bytes 589832 | tf_op jit(solution)/shard_map/ppermute | solution.py:63
  57.6 8.0 %collective-permute-start.18 = (bf16[3,4,64,128]{3,2,1,0:T(8,128)(2,1)S(1)}, bf16[3,4,64,128]{3,2,1,0:T(8,128)(2,1)S(1)}, u32[]{:S(2)}, u32[]{:S(2)}) collective-permute-start(bf16[3,4,64,128]{3,2,1,0:T(8,128)(2,1)S(1)} %get-tuple-element.113), channel_id=1, source_target_pairs={{0,16},{8,24},{16,0},{24,8},{1,17},{9,25},{17,1},{25,9},{2,18},{10... | collective-permute-start | bytes 589832 | tf_op jit(solution)/shard_map/ppermute | solution.py:63
  58.8 8.7 %collective-permute-start.19 = (bf16[3,4,64,128]{3,2,1,0:T(8,128)(2,1)S(1)}, bf16[3,4,64,128]{3,2,1,0:T(8,128)(2,1)S(1)}, u32[]{:S(2)}, u32[]{:S(2)}) collective-permute-start(bf16[3,4,64,128]{3,2,1,0:T(8,128)(2,1)S(1)} %get-tuple-element.114), channel_id=1, source_target_pairs={{0,24},{8,16},{16,8},{24,0},{1,25},{9,17},{17,9},{25,1},{2,26},{10... | collective-permute-start | bytes 589832 | tf_op jit(solution)/shard_map/ppermute | solution.py:63

commit v12 on v10

--- a/solution.py
+++ b/solution.py
@@ -509,8 +509,12 @@
         *terms, velocity_magnetic = first_physics(joined([own[group]] + arrived[group]), *tables_here)
         local += exchange(terms, offsets(count, FIRST_RETURN))
         physical.append(velocity_magnetic)
-    local, shares = lax.optimization_barrier((local, shares))
-    sources = exchange(shares, order)
+    early = min(3, count)
+    arrived[0][0], shares[:early] = lax.optimization_barrier((arrived[0][0], shares[:early]))
+    sources = exchange(shares[:early], order[:early])
+    local, shares[early:] = lax.optimization_barrier((local, shares[early:]))
+    sources += exchange(shares[early:], order[early:])
+    local, sources[:early] = lax.optimization_barrier((local, sources[:early]))
     toward_prev, toward_next = interface(local, interface_nodes, count)
     halos = (from_behind(toward_next, "mer", 1), from_behind(toward_prev, "mer", -1))
     sources, halos = lax.optimization_barrier((sources, halos))

time: 69.3 us -> 72.1 us (1.040)
  the two profiles are of different devices: /device:TPU:0 before, /device:TPU:1 now
where the time goes in v12:
time: 72.1 us; the launch traced here: 71.3 us
  starting transfers between devices  27.9 us (39%)
  waiting for transfers between devices  27.2 us (38%)
  Pallas kernels  13.4 us (19%)
  local copies, waits for them, and re-layouts  1.93 us (3%)
  between operations  0.83 us (1%)
    ppermute x18, waiting for transfers between devices, exchange(): received.append(lax.ppermute(piece, 'mode', pairs))  22.9 us
    ppermute x18, starting transfers between devices, exchange(): received.append(lax.ppermute(piece, 'mode', pairs))  21.3 us
    ppermute x2, starting transfers between devices, from_behind(): lax.ppermute(value, axis, [(source, source + steps) for source in range(i...  6.61 us
    pallas_call x1, Pallas kernels, derive(): pl.pallas_call(functools.partial(derive_kernel, count, len(received)), in...  5.02 us
    ppermute x2, waiting for transfers between devices, from_behind(): lax.ppermute(value, axis, [(source, source + steps) for source in range(i...  4.35 us
    unnamed x18, local copies, waits for them, and re-layouts  1.93 us
    pallas_call x2, Pallas kernels, first_physics(): pl.pallas_call(functools.partial(first_kernel, count), in_specs=[vmem()]...  1.63 us
    pallas_call x2, Pallas kernels, pack_rest(): pl.pallas_call(kernel, in_specs=[pl.BlockSpec(memory_space=pl.ANY)] + [vm...  1.62 us
  transfers between devices with their start and end apart: 20, of which 10 were waited for; matrix products, arithmetic and copies ran while one was open for 0% of the time, Pallas kernels for 14%

profile of v12, /device:TPU:1, one launch (start us, length us, event | category | flops | bytes accessed | tf_op | source)
XLA Modules:
  0.0 71.3 jit_solution(3446465928807880422)
XLA Ops:
  0.6 0.0 copy-start
  0.6 1.9 %copy-done = bf16[12,32,2,2048]{3,2,1,0:T(2,128)(2,1)S(1)} copy-done((bf16[12,32,2,2048]{3,2,1,0:T(2,128)(2,1)S(1)}, bf16[12,32,2,2048]{3,2,1,0:T(2,128)(2,1)}, u32[]{:S(2)}) %copy-start) | copy-done | bytes 3145752
  2.5 0.2 shard_map.102
  2.7 3.1 %collective-permute-start.7 = (bf16[6,2,32,2,128]{4,3,2,1,0:T(2,128)(2,1)S(1)}, bf16[6,2,32,2,128]{4,3,2,1,0:T(2,128)(2,1)S(1)}, u32[]{:S(2)}, u32[]{:S(2)}) collective-permute-start(bf16[6,2,32,2,128]{4,3,2,1,0:T(2,128)(2,1)S(1)} %shard_map.102), channel_id=1, source_target_pairs={{0,24},{8,16},{16,8},{24,0},{1,25},{9,17},{17,9},{25,1},{2,26},{10... | collective-permute-start | bytes 589832 | tf_op jit(solution)/shard_map/ppermute | solution.py:63
  5.7 0.2 shard_map.103
  5.9 0.3 collective-permute-start.8
  6.2 0.2 shard_map.101
  6.4 0.1 collective-permute-start.6
  6.5 0.2 shard_map.97
  6.7 2.4 %collective-permute-start.1 = (bf16[6,2,32,2,128]{4,3,2,1,0:T(2,128)(2,1)S(1)}, bf16[6,2,32,2,128]{4,3,2,1,0:T(2,128)(2,1)S(1)}, u32[]{:S(2)}, u32[]{:S(2)}) collective-permute-start(bf16[6,2,32,2,128]{4,3,2,1,0:T(2,128)(2,1)S(1)} %shard_map.97), channel_id=1, source_target_pairs={{0,24},{8,16},{16,8},{24,0},{1,25},{9,17},{17,9},{25,1},{2,26},{10... | collective-permute-start | bytes 589832 | tf_op jit(solution)/shard_map/ppermute | solution.py:63
  9.1 0.2 shard_map.96
  9.3 0.0 copy-start.4
  9.3 0.0 copy-start.5
  9.3 0.3 collective-permute-start
  9.6 0.2 shard_map.98
  9.8 0.6 collective-permute-done.7
  10.4 1.1 %collective-permute-start.2 = (bf16[6,2,32,2,128]{4,3,2,1,0:T(2,128)(2,1)S(1)}, bf16[6,2,32,2,128]{4,3,2,1,0:T(2,128)(2,1)S(1)}, u32[]{:S(2)}, u32[]{:S(2)}) collective-permute-start(bf16[6,2,32,2,128]{4,3,2,1,0:T(2,128)(2,1)S(1)} %shard_map.98), channel_id=1, source_target_pairs={{0,16},{8,24},{16,0},{24,8},{1,17},{9,25},{17,1},{25,9},{2,18},{10... | collective-permute-start | bytes 589832 | tf_op jit(solution)/shard_map/ppermute | solution.py:63
  11.5 0.3 shard_map.95
  11.9 4.2 %collective-permute-done.8 = bf16[6,2,32,2,128]{4,3,2,1,0:T(2,128)(2,1)S(1)} collective-permute-done((bf16[6,2,32,2,128]{4,3,2,1,0:T(2,128)(2,1)S(1)}, bf16[6,2,32,2,128]{4,3,2,1,0:T(2,128)(2,1)S(1)}, u32[]{:S(2)}, u32[]{:S(2)}) %collective-permute-start.8) | collective-permute-done | bytes 196640 | tf_op jit(solution)/shard_map/ppermute | solution.py:63
  16.0 0.8 %shard_map.104 = (bf16[4,2,64,128]{3,2,1,0:T(8,128)(2,1)S(1)}, bf16[4,2,64,128]{3,2,1,0:T(8,128)(2,1)S(1)}, bf16[4,2,64,128]{3,2,1,0:T(8,128)(2,1)S(1)}, bf16[4,...) custom-call(bf16[6,2,64,128]{3,2,1,0:T(8,128)(2,1)S(1)} %bitcast.35, bf16[6,2,64,128]{3,2,1,0:T(8,128)(2,1)S(1)} %bitcast.34, ...), custom_call_target="tpu_custom_call" | custom-call | flops 1024 | bytes 1024 | tf_op jit(solution)/shard_map/pallas_call | solution.py:218
  16.9 0.4 collective-permute-start.9
  17.3 2.6 %collective-permute-start.10 = (bf16[4,2,64,128]{3,2,1,0:T(8,128)(2,1)S(1)}, bf16[4,2,64,128]{3,2,1,0:T(8,128)(2,1)S(1)}, u32[]{:S(2)}, u32[]{:S(2)}) collective-permute-start(bf16[4,2,64,128]{3,2,1,0:T(8,128)(2,1)S(1)} %get-tuple-element.82), channel_id=1, source_target_pairs={{0,8},{8,0},{16,24},{24,16},{1,9},{9,1},{17,25},{25,17},{2,10},{10... | collective-permute-start | bytes 393224 | tf_op jit(solution)/shard_map/ppermute | solution.py:63
  19.8 0.2 collective-permute-start.11
  20.0 1.3 %shard_map.99 = (bf16[6,4,32,2,128]{4,3,2,1,0:T(2,128)(2,1)S(1)}, bf16[6,4,32,2,128]{4,3,2,1,0:T(2,128)(2,1)S(1)}, bf16[6,4,32,2,128]{4,3,2,1,0:T(2,128)(2,1)S(1...) custom-call(bf16[12,32,2,2048]{3,2,1,0:T(2,128)(2,1)S(1)} %copy-done.1, ...), custom_call_target="tpu_custom_call" | custom-call | flops 1024 | bytes 1024 | tf_op jit(solution)/shard_map/pallas_call | solution.py:150
  21.3 1.7 %collective-permute-done = bf16[6,2,32,2,128]{4,3,2,1,0:T(2,128)(2,1)S(1)} collective-permute-done((bf16[6,2,32,2,128]{4,3,2,1,0:T(2,128)(2,1)S(1)}, bf16[6,2,32,2,128]{4,3,2,1,0:T(2,128)(2,1)S(1)}, u32[]{:S(2)}, u32[]{:S(2)}) %collective-permute-start) | collective-permute-done | bytes 196640 | tf_op jit(solution)/shard_map/ppermute | solution.py:63
  23.0 1.3 %collective-permute-start.12 = (bf16[6,4,32,2,128]{4,3,2,1,0:T(2,128)(2,1)S(1)}, bf16[6,4,32,2,128]{4,3,2,1,0:T(2,128)(2,1)S(1)}, u32[]{:S(2)}, u32[]{:S(2)}) collective-permute-start(bf16[6,4,32,2,128]{4,3,2,1,0:T(2,128)(2,1)S(1)} %get-tuple-element.97), channel_id=1, source_target_pairs={{0,8},{8,0},{16,24},{24,16},{1,9},{9,1},{17,25},{25,17},{2,10},{10... | collective-permute-start | bytes 1179656 | tf_op jit(solution)/shard_map/ppermute | solution.py:63
  24.3 0.1 collective-permute-done.2
  24.4 1.7 %collective-permute-start.13 = (bf16[6,4,32,2,128]{4,3,2,1,0:T(2,128)(2,1)S(1)}, bf16[6,4,32,2,128]{4,3,2,1,0:T(2,128)(2,1)S(1)}, u32[]{:S(2)}, u32[]{:S(2)}) collective-permute-start(bf16[6,4,32,2,128]{4,3,2,1,0:T(2,128)(2,1)S(1)} %get-tuple-element.98), channel_id=1, source_target_pairs={{0,16},{8,24},{16,0},{24,8},{1,17},{9,25},{17,1},{25,9},{2,18},{10... | collective-permute-start | bytes 1179656 | tf_op jit(solution)/shard_map/ppermute | solution.py:63
  26.1 0.8 %shard_map.100 = (bf16[4,2,64,128]{3,2,1,0:T(8,128)(2,1)S(1)}, bf16[4,2,64,128]{3,2,1,0:T(8,128)(2,1)S(1)}, bf16[4,2,64,128]{3,2,1,0:T(8,128)(2,1)S(1)}, bf16[4,...) custom-call(bf16[6,2,64,128]{3,2,1,0:T(8,128)(2,1)S(1)} %bitcast.31, bf16[6,2,64,128]{3,2,1,0:T(8,128)(2,1)S(1)} %bitcast.29, ...), custom_call_target="tpu_custom_call" | custom-call | flops 1024 | bytes 1024 | tf_op jit(solution)/shard_map/pallas_call | solution.py:218
  27.0 1.2 %collective-permute-start.3 = (bf16[4,2,64,128]{3,2,1,0:T(8,128)(2,1)S(1)}, bf16[4,2,64,128]{3,2,1,0:T(8,128)(2,1)S(1)}, u32[]{:S(2)}, u32[]{:S(2)}) collective-permute-start(bf16[4,2,64,128]{3,2,1,0:T(8,128)(2,1)S(1)} %get-tuple-element.76), channel_id=1, source_target_pairs={{0,24},{8,16},{16,8},{24,0},{1,25},{9,17},{17,9},{25,1},{2,26},{10... | collective-permute-start | bytes 393224 | tf_op jit(solution)/shard_map/ppermute | solution.py:63
  28.2 0.5 collective-permute-done.10.refs_6_
  28.7 1.3 %collective-permute-start.4 = (bf16[4,2,64,128]{3,2,1,0:T(8,128)(2,1)S(1)}, bf16[4,2,64,128]{3,2,1,0:T(8,128)(2,1)S(1)}, u32[]{:S(2)}, u32[]{:S(2)}) collective-permute-start(bf16[4,2,64,128]{3,2,1,0:T(8,128)(2,1)S(1)} %get-tuple-element.77), channel_id=1, source_target_pairs={{0,8},{8,0},{16,24},{24,16},{1,9},{9,1},{17,25},{25,17},{2,10},{10... | collective-permute-start | bytes 393224 | tf_op jit(solution)/shard_map/ppermute | solution.py:63
  29.9 0.9 %collective-permute-start.5 = (bf16[4,2,64,128]{3,2,1,0:T(8,128)(2,1)S(1)}, bf16[4,2,64,128]{3,2,1,0:T(8,128)(2,1)S(1)}, u32[]{:S(2)}, u32[]{:S(2)}) collective-permute-start(bf16[4,2,64,128]{3,2,1,0:T(8,128)(2,1)S(1)} %get-tuple-element.78), channel_id=1, source_target_pairs={{0,16},{8,24},{16,0},{24,8},{1,17},{9,25},{17,1},{25,9},{2,18},{10... | collective-permute-start | bytes 393224 | tf_op jit(solution)/shard_map/ppermute | solution.py:63
  30.8 9.2 %collective-permute-done.3.refs_1_ = bf16[4,2,64,128]{3,2,1,0:T(8,128)(2,1)S(1)} collective-permute-done((bf16[4,2,64,128]{3,2,1,0:T(8,128)(2,1)S(1)}, bf16[4,2,64,128]{3,2,1,0:T(8,128)(2,1)S(1)}, u32[]{:S(2)}, u32[]{:S(2)}) %collective-permute-start.3) | collective-permute-done | bytes 131104 | tf_op jit(solution)/shard_map/ppermute | solution.py:63
  40.0 2.7 %collective-permute-done.4.refs_2_ = bf16[4,2,64,128]{3,2,1,0:T(8,128)(2,1)S(1)} collective-permute-done((bf16[4,2,64,128]{3,2,1,0:T(8,128)(2,1)S(1)}, bf16[4,2,64,128]{3,2,1,0:T(8,128)(2,1)S(1)}, u32[]{:S(2)}, u32[]{:S(2)}) %collective-permute-start.4) | collective-permute-done | bytes 131104 | tf_op jit(solution)/shard_map/ppermute | solution.py:63
  42.7 1.8 %collective-permute-start.14 = (bf16[6,4,32,2,128]{4,3,2,1,0:T(2,128)(2,1)S(1)}, bf16[6,4,32,2,128]{4,3,2,1,0:T(2,128)(2,1)S(1)}, u32[]{:S(2)}, u32[]{:S(2)}) collective-permute-start(bf16[6,4,32,2,128]{4,3,2,1,0:T(2,128)(2,1)S(1)} %get-tuple-element.110), channel_id=1, source_target_pairs={{0,24},{8,16},{16,8},{24,0},{1,25},{9,17},{17,9},{25,1},{2,26},{10... | collective-permute-start | bytes 1179656 | tf_op jit(solution)/shard_map/ppermute | solution.py:63
  44.5 1.2 %shard_map.105 = (bf16[4,2,64,128]{3,2,1,0:T(8,128)(2,1)S(1)}, bf16[4,2,64,128]{3,2,1,0:T(8,128)(2,1)S(1)}) custom-call(bf16[4,2,64,128]{3,2,1,0:T(8,128)(2,1)S(1)} %get-tuple-element.99.refs_0_, bf16[4,2,64,128]{3,2,1,0:T(8,128)(2,1)S(1)} %collective-permute-done.3.refs_1_, bf16[4,2,64,128]{3,2,1,0:T(8,128)(2,1)S(1)} %collective-permute-done.4.refs_2_, ...), custom_call_target="tpu_custom_call" | custom-call | flops 1024 | bytes 1024 | tf_op jit(solution)/shard_map/pallas_call | solution.py:312
  45.7 4.7 %collective-permute-start.15 = (bf16[4,2,64,128]{3,2,1,0:T(8,128)(2,1)S(1)}, bf16[4,2,64,128]{3,2,1,0:T(8,128)(2,1)S(1)}, u32[]{:S(2)}, u32[]{:S(2)}) collective-permute-start(bf16[4,2,64,128]{3,2,1,0:T(8,128)(2,1)S(1)} %get-tuple-element.111), channel_id=1, source_target_pairs={{0,1},{1,2},{2,3},{3,4},{4,5},{5,6},{6,7},{8,9},{9,10},{10,11},{11... | collective-permute-start | bytes 393224 | tf_op jit(solution)/shard_map/ppermute | solution.py:70
  50.4 1.9 %collective-permute-start.16 = (bf16[4,2,64,128]{3,2,1,0:T(8,128)(2,1)S(1)}, bf16[4,2,64,128]{3,2,1,0:T(8,128)(2,1)S(1)}, u32[]{:S(2)}, u32[]{:S(2)}) collective-permute-start(bf16[4,2,64,128]{3,2,1,0:T(8,128)(2,1)S(1)} %get-tuple-element.112), channel_id=1, source_target_pairs={{1,0},{2,1},{3,2},{4,3},{5,4},{6,5},{7,6},{9,8},{10,9},{11,10},{12... | collective-permute-start | bytes 393224 | tf_op jit(solution)/shard_map/ppermute | solution.py:70
  52.4 4.3 %collective-permute-done.16.refs_9_ = bf16[4,2,64,128]{3,2,1,0:T(8,128)(2,1)S(1)} collective-permute-done((bf16[4,2,64,128]{3,2,1,0:T(8,128)(2,1)S(1)}, bf16[4,2,64,128]{3,2,1,0:T(8,128)(2,1)S(1)}, u32[]{:S(2)}, u32[]{:S(2)}) %collective-permute-start.16) | collective-permute-done | bytes 131104 | tf_op jit(solution)/shard_map/ppermute | solution.py:70
  56.7 1.6 %shard_map.106 = (bf16[3,4,64,128]{3,2,1,0:T(8,128)(2,1)S(1)}, bf16[3,4,64,128]{3,2,1,0:T(8,128)(2,1)S(1)}, bf16[3,4,64,128]{3,2,1,0:T(8,128)(2,1)S(1)}, bf16[3,4,64,128]{3,2,1,0:T(8,128)(2,1)S(1)}) custom-call(bf16[6,4,64,128]{3,2,1,0:T(8,128)(2,1)S(1)} %bitcast.24, bf16[6,4,64,128]{3,2,1,0:T(8,128)(2,1)S(1)} %bitcast.25, ...), custom_call_target="tpu_custom_call" | custom-call | flops 1024 | bytes 1024 | tf_op jit(solution)/shard_map/pallas_call | solution.py:262
  58.3 0.8 %collective-permute-start.17 = (bf16[3,4,64,128]{3,2,1,0:T(8,128)(2,1)S(1)}, bf16[3,4,64,128]{3,2,1,0:T(8,128)(2,1)S(1)}, u32[]{:S(2)}, u32[]{:S(2)}) collective-permute-start(bf16[3,4,64,128]{3,2,1,0:T(8,128)(2,1)S(1)} %get-tuple-element.128), channel_id=1, source_target_pairs={{0,8},{8,0},{16,24},{24,16},{1,9},{9,1},{17,25},{25,17},{2,10},{10... | collective-permute-start | bytes 589832 | tf_op jit(solution)/shard_map/ppermute | solution.py:63
  59.1 0.4 collective-permute-start.18
  59.5 1.5 %collective-permute-start.19 = (bf16[3,4,64,128]{3,2,1,0:T(8,128)(2,1)S(1)}, bf16[3,4,64,128]{3,2,1,0:T(8,128)(2,1)S(1)}, u32[]{:S(2)}, u32[]{:S(2)}) collective-permute-start(bf16[3,4,64,128]{3,2,1,0:T(8,128)(2,1)S(1)} %get-tuple-element.130), channel_id=1, source_target_pairs={{0,24},{8,16},{16,8},{24,0},{1,25},{9,17},{17,9},{25,1},{2,26},{10... | collective-permute-start | bytes 589832 | tf_op jit(solution)/shard_map/ppermute | solution.py:63
  61.1 5.0 %shard_map.107 = (f32[3072,128]{1,0:T(8,128)}, f32[3,16,64,128]{3,2,1,0:T(8,128)S(1)}) custom-call(bf16[4,2,64,128]{3,2,1,0:T(8,128)(2,1)S(1)} %get-tuple-element.99.refs_0_, bf16[4,2,64,128]{3,2,1,0:T(8,128)(2,1)S(1)} %collective-permute-done.3.refs_1_, bf16[4,2,64,128]{3,2,1,0:T(8,128)(2,1)S(1)} %collective-permute-done.4.refs_2_, ...), custom_call_target="tpu_custom_call" | custom-call | flops 1024 | bytes 1024 | tf_op jit(solution)/shard_map/pallas_call | solution.py:424
  66.1 2.1 %collective-permute-done.18.refs_2_ = bf16[3,4,64,128]{3,2,1,0:T(8,128)(2,1)S(1)} collective-permute-done((bf16[3,4,64,128]{3,2,1,0:T(8,128)(2,1)S(1)}, bf16[3,4,64,128]{3,2,1,0:T(8,128)(2,1)S(1)}, u32[]{:S(2)}, u32[]{:S(2)}) %collective-permute-start.18) | collective-permute-done | bytes 196640 | tf_op jit(solution)/shard_map/ppermute | solution.py:63
  68.2 1.8 %collective-permute-done.19.refs_3_ = bf16[3,4,64,128]{3,2,1,0:T(8,128)(2,1)S(1)} collective-permute-done((bf16[3,4,64,128]{3,2,1,0:T(8,128)(2,1)S(1)}, bf16[3,4,64,128]{3,2,1,0:T(8,128)(2,1)S(1)}, u32[]{:S(2)}, u32[]{:S(2)}) %collective-permute-start.19) | collective-permute-done | bytes 196640 | tf_op jit(solution)/shard_map/ppermute | solution.py:63
  70.0 1.3 %shard_map.108 = f32[3072,128]{1,0:T(8,128)} custom-call(bf16[3,4,64,128]{3,2,1,0:T(8,128)(2,1)S(1)} %get-tuple-element.127.refs_0_, bf16[3,4,64,128]{3,2,1,0:T(8,128)(2,1)S(1)} %collective-permute-done.17.refs_1_, bf16[3,4,64,128]{3,2,1,0:T(8,128)(2,1)S(1)} %collective-permute-done.18.refs_2_, bf16[3,4,64,128]{3,2,1,0:T(8,128)(2,1)S(1)} %collective-permute-done.19.refs_3_, ...), custom_call_target="tpu_custom_call" | custom-call | flops 1024 | bytes 1024 | tf_op jit(solution)/shard_map/pallas_call | solution.py:466
  (24 shorter events, 0.1 us)
Async XLA Ops:
  0.6 1.9 %copy-start = (bf16[12,32,2,2048]{3,2,1,0:T(2,128)(2,1)S(1)}, bf16[12,32,2,2048]{3,2,1,0:T(2,128)(2,1)}, u32[]{:S(2)}) copy-start(bf16[12,32,2,2048]{3,2,1,0:T(2,128)(2,1)} %fields_ref.15) | copy-start | bytes 9437188
  2.7 7.7 %collective-permute-start.7 = (bf16[6,2,32,2,128]{4,3,2,1,0:T(2,128)(2,1)S(1)}, bf16[6,2,32,2,128]{4,3,2,1,0:T(2,128)(2,1)S(1)}, u32[]{:S(2)}, u32[]{:S(2)}) collective-permute-start(bf16[6,2,32,2,128]{4,3,2,1,0:T(2,128)(2,1)S(1)} %shard_map.102), channel_id=1, source_target_pairs={{0,24},{8,16},{16,8},{24,0},{1,25},{9,17},{17,9},{25,1},{2,26},{10... | collective-permute-start | bytes 589832 | tf_op jit(solution)/shard_map/ppermute | solution.py:63
  5.9 10.1 %collective-permute-start.8 = (bf16[6,2,32,2,128]{4,3,2,1,0:T(2,128)(2,1)S(1)}, bf16[6,2,32,2,128]{4,3,2,1,0:T(2,128)(2,1)S(1)}, u32[]{:S(2)}, u32[]{:S(2)}) collective-permute-start(bf16[6,2,32,2,128]{4,3,2,1,0:T(2,128)(2,1)S(1)} %shard_map.103), channel_id=1, source_target_pairs={{0,16},{8,24},{16,0},{24,8},{1,17},{9,25},{17,1},{25,9},{2,18},{10... | collective-permute-start | bytes 589832 | tf_op jit(solution)/shard_map/ppermute | solution.py:63
  6.4 9.7 %collective-permute-start.6 = (bf16[6,2,32,2,128]{4,3,2,1,0:T(2,128)(2,1)S(1)}, bf16[6,2,32,2,128]{4,3,2,1,0:T(2,128)(2,1)S(1)}, u32[]{:S(2)}, u32[]{:S(2)}) collective-permute-start(bf16[6,2,32,2,128]{4,3,2,1,0:T(2,128)(2,1)S(1)} %shard_map.101), channel_id=1, source_target_pairs={{0,8},{8,0},{16,24},{24,16},{1,9},{9,1},{17,25},{25,17},{2,10},{10... | collective-permute-start | bytes 589832 | tf_op jit(solution)/shard_map/ppermute | solution.py:63
  6.7 13.2 %collective-permute-start.1 = (bf16[6,2,32,2,128]{4,3,2,1,0:T(2,128)(2,1)S(1)}, bf16[6,2,32,2,128]{4,3,2,1,0:T(2,128)(2,1)S(1)}, u32[]{:S(2)}, u32[]{:S(2)}) collective-permute-start(bf16[6,2,32,2,128]{4,3,2,1,0:T(2,128)(2,1)S(1)} %shard_map.97), channel_id=1, source_target_pairs={{0,24},{8,16},{16,8},{24,0},{1,25},{9,17},{17,9},{25,1},{2,26},{10... | collective-permute-start | bytes 589832 | tf_op jit(solution)/shard_map/ppermute | solution.py:63
  9.3 2.3 %copy-start.4 = (bf16[256,256]{1,0:T(8,128)(2,1)S(1)}, bf16[256,256]{1,0:T(8,128)(2,1)}, u32[]{:S(2)}) copy-start(bf16[256,256]{1,0:T(8,128)(2,1)} %constant.5.clone.refs_1_) | copy-start | bytes 393220
  9.3 2.3 %copy-start.5 = (bf16[256,256]{1,0:T(8,128)(2,1)S(1)}, bf16[256,256]{1,0:T(8,128)(2,1)}, u32[]{:S(2)}) copy-start(bf16[256,256]{1,0:T(8,128)(2,1)} %constant.4.clone.refs_0_) | copy-start | bytes 393220
  9.3 13.8 %collective-permute-start = (bf16[6,2,32,2,128]{4,3,2,1,0:T(2,128)(2,1)S(1)}, bf16[6,2,32,2,128]{4,3,2,1,0:T(2,128)(2,1)S(1)}, u32[]{:S(2)}, u32[]{:S(2)}) collective-permute-start(bf16[6,2,32,2,128]{4,3,2,1,0:T(2,128)(2,1)S(1)} %shard_map.96), channel_id=1, source_target_pairs={{0,8},{8,0},{16,24},{24,16},{1,9},{9,1},{17,25},{25,17},{2,10},{10... | collective-permute-start | bytes 589832 | tf_op jit(solution)/shard_map/ppermute | solution.py:63
  9.8 10.2 %copy-start.1 = (bf16[12,32,2,2048]{3,2,1,0:T(2,128)(2,1)S(1)}, bf16[12,32,2,2048]{3,2,1,0:T(2,128)(2,1)}, u32[]{:S(2)}) copy-start(bf16[12,32,2,2048]{3,2,1,0:T(2,128)(2,1)} %fields_ref.15) | copy-start | bytes 9437188
  10.4 14.0 %collective-permute-start.2 = (bf16[6,2,32,2,128]{4,3,2,1,0:T(2,128)(2,1)S(1)}, bf16[6,2,32,2,128]{4,3,2,1,0:T(2,128)(2,1)S(1)}, u32[]{:S(2)}, u32[]{:S(2)}) collective-permute-start(bf16[6,2,32,2,128]{4,3,2,1,0:T(2,128)(2,1)S(1)} %shard_map.98), channel_id=1, source_target_pairs={{0,16},{8,24},{16,0},{24,8},{1,17},{9,25},{17,1},{25,9},{2,18},{10... | collective-permute-start | bytes 589832 | tf_op jit(solution)/shard_map/ppermute | solution.py:63
  16.9 10.1 %collective-permute-start.9 = (bf16[4,2,64,128]{3,2,1,0:T(8,128)(2,1)S(1)}, bf16[4,2,64,128]{3,2,1,0:T(8,128)(2,1)S(1)}, u32[]{:S(2)}, u32[]{:S(2)}) collective-permute-start(bf16[4,2,64,128]{3,2,1,0:T(8,128)(2,1)S(1)} %get-tuple-element.81), channel_id=1, source_target_pairs={{0,24},{8,16},{16,8},{24,0},{1,25},{9,17},{17,9},{25,1},{2,26},{10... | collective-permute-start | bytes 393224 | tf_op jit(solution)/shard_map/ppermute | solution.py:63
  17.3 11.4 %collective-permute-start.10 = (bf16[4,2,64,128]{3,2,1,0:T(8,128)(2,1)S(1)}, bf16[4,2,64,128]{3,2,1,0:T(8,128)(2,1)S(1)}, u32[]{:S(2)}, u32[]{:S(2)}) collective-permute-start(bf16[4,2,64,128]{3,2,1,0:T(8,128)(2,1)S(1)} %get-tuple-element.82), channel_id=1, source_target_pairs={{0,8},{8,0},{16,24},{24,16},{1,9},{9,1},{17,25},{25,17},{2,10},{10... | collective-permute-start | bytes 393224 | tf_op jit(solution)/shard_map/ppermute | solution.py:63
  19.8 24.6 %copy-start.8 = (s32[2,256]{1,0:T(2,128)S(1)}, s32[2,256]{1,0:T(2,128)}, u32[]{:S(2)}) copy-start(s32[2,256]{1,0:T(2,128)} %refs_8_.1) | copy-start | bytes 6148
  19.8 10.1 %collective-permute-start.11 = (bf16[4,2,64,128]{3,2,1,0:T(8,128)(2,1)S(1)}, bf16[4,2,64,128]{3,2,1,0:T(8,128)(2,1)S(1)}, u32[]{:S(2)}, u32[]{:S(2)}) collective-permute-start(bf16[4,2,64,128]{3,2,1,0:T(8,128)(2,1)S(1)} %get-tuple-element.83), channel_id=1, source_target_pairs={{0,16},{8,24},{16,0},{24,8},{1,17},{9,25},{17,1},{25,9},{2,18},{10... | collective-permute-start | bytes 393224 | tf_op jit(solution)/shard_map/ppermute | solution.py:63
  23.0 21.4 %collective-permute-start.12 = (bf16[6,4,32,2,128]{4,3,2,1,0:T(2,128)(2,1)S(1)}, bf16[6,4,32,2,128]{4,3,2,1,0:T(2,128)(2,1)S(1)}, u32[]{:S(2)}, u32[]{:S(2)}) collective-permute-start(bf16[6,4,32,2,128]{4,3,2,1,0:T(2,128)(2,1)S(1)} %get-tuple-element.97), channel_id=1, source_target_pairs={{0,8},{8,0},{16,24},{24,16},{1,9},{9,1},{17,25},{25,17},{2,10},{10... | collective-permute-start | bytes 1179656 | tf_op jit(solution)/shard_map/ppermute | solution.py:63
  24.4 20.1 %collective-permute-start.13 = (bf16[6,4,32,2,128]{4,3,2,1,0:T(2,128)(2,1)S(1)}, bf16[6,4,32,2,128]{4,3,2,1,0:T(2,128)(2,1)S(1)}, u32[]{:S(2)}, u32[]{:S(2)}) collective-permute-start(bf16[6,4,32,2,128]{4,3,2,1,0:T(2,128)(2,1)S(1)} %get-tuple-element.98), channel_id=1, source_target_pairs={{0,16},{8,24},{16,0},{24,8},{1,17},{9,25},{17,1},{25,9},{2,18},{10... | collective-permute-start | bytes 1179656 | tf_op jit(solution)/shard_map/ppermute | solution.py:63
  27.0 13.0 %collective-permute-start.3 = (bf16[4,2,64,128]{3,2,1,0:T(8,128)(2,1)S(1)}, bf16[4,2,64,128]{3,2,1,0:T(8,128)(2,1)S(1)}, u32[]{:S(2)}, u32[]{:S(2)}) collective-permute-start(bf16[4,2,64,128]{3,2,1,0:T(8,128)(2,1)S(1)} %get-tuple-element.76), channel_id=1, source_target_pairs={{0,24},{8,16},{16,8},{24,0},{1,25},{9,17},{17,9},{25,1},{2,26},{10... | collective-permute-start | bytes 393224 | tf_op jit(solution)/shard_map/ppermute | solution.py:63
  28.7 14.0 %collective-permute-start.4 = (bf16[4,2,64,128]{3,2,1,0:T(8,128)(2,1)S(1)}, bf16[4,2,64,128]{3,2,1,0:T(8,128)(2,1)S(1)}, u32[]{:S(2)}, u32[]{:S(2)}) collective-permute-start(bf16[4,2,64,128]{3,2,1,0:T(8,128)(2,1)S(1)} %get-tuple-element.77), channel_id=1, source_target_pairs={{0,8},{8,0},{16,24},{24,16},{1,9},{9,1},{17,25},{25,17},{2,10},{10... | collective-permute-start | bytes 393224 | tf_op jit(solution)/shard_map/ppermute | solution.py:63
  29.9 12.8 %collective-permute-start.5 = (bf16[4,2,64,128]{3,2,1,0:T(8,128)(2,1)S(1)}, bf16[4,2,64,128]{3,2,1,0:T(8,128)(2,1)S(1)}, u32[]{:S(2)}, u32[]{:S(2)}) collective-permute-start(bf16[4,2,64,128]{3,2,1,0:T(8,128)(2,1)S(1)} %get-tuple-element.78), channel_id=1, source_target_pairs={{0,16},{8,24},{16,0},{24,8},{1,17},{9,25},{17,1},{25,9},{2,18},{10... | collective-permute-start | bytes 393224 | tf_op jit(solution)/shard_map/ppermute | solution.py:63
  42.7 14.0 %collective-permute-start.14 = (bf16[6,4,32,2,128]{4,3,2,1,0:T(2,128)(2,1)S(1)}, bf16[6,4,32,2,128]{4,3,2,1,0:T(2,128)(2,1)S(1)}, u32[]{:S(2)}, u32[]{:S(2)}) collective-permute-start(bf16[6,4,32,2,128]{4,3,2,1,0:T(2,128)(2,1)S(1)} %get-tuple-element.110), channel_id=1, source_target_pairs={{0,24},{8,16},{16,8},{24,0},{1,25},{9,17},{17,9},{25,1},{2,26},{10... | collective-permute-start | bytes 1179656 | tf_op jit(solution)/shard_map/ppermute | solution.py:63
  45.7 6.6 %collective-permute-start.15 = (bf16[4,2,64,128]{3,2,1,0:T(8,128)(2,1)S(1)}, bf16[4,2,64,128]{3,2,1,0:T(8,128)(2,1)S(1)}, u32[]{:S(2)}, u32[]{:S(2)}) collective-permute-start(bf16[4,2,64,128]{3,2,1,0:T(8,128)(2,1)S(1)} %get-tuple-element.111), channel_id=1, source_target_pairs={{0,1},{1,2},{2,3},{3,4},{4,5},{5,6},{6,7},{8,9},{9,10},{10,11},{11... | collective-permute-start | bytes 393224 | tf_op jit(solution)/shard_map/ppermute | solution.py:70
  50.4 6.3 %collective-permute-start.16 = (bf16[4,2,64,128]{3,2,1,0:T(8,128)(2,1)S(1)}, bf16[4,2,64,128]{3,2,1,0:T(8,128)(2,1)S(1)}, u32[]{:S(2)}, u32[]{:S(2)}) collective-permute-start(bf16[4,2,64,128]{3,2,1,0:T(8,128)(2,1)S(1)} %get-tuple-element.112), channel_id=1, source_target_pairs={{1,0},{2,1},{3,2},{4,3},{5,4},{6,5},{7,6},{9,8},{10,9},{11,10},{12... | collective-permute-start | bytes 393224 | tf_op jit(solution)/shard_map/ppermute | solution.py:70
  56.7 4.3 %copy-start.2 = (bf16[5,64,2048]{2,1,0:T(8,128)(2,1)S(1)}, bf16[5,64,2048]{2,1,0:T(8,128)(2,1)}, u32[]{:S(2)}) copy-start(bf16[5,64,2048]{2,1,0:T(8,128)(2,1)} %refs_10_.1) | copy-start | bytes 3932164
  56.7 4.3 %copy-start.3 = (bf16[5,64,2048]{2,1,0:T(8,128)(2,1)S(1)}, bf16[5,64,2048]{2,1,0:T(8,128)(2,1)}, u32[]{:S(2)}) copy-start(bf16[5,64,2048]{2,1,0:T(8,128)(2,1)} %refs_11_.1) | copy-start | bytes 3932164
  56.7 4.3 %copy-start.6 = (f32[2048]{0:T(1024)S(1)}, f32[2048]{0:T(1024)}, u32[]{:S(2)}) copy-start(f32[2048]{0:T(1024)} %param.9) | copy-start | bytes 24580
  56.7 4.3 %copy-start.7 = (s32[32,5]{0,1:T(8,128)S(1)}, s32[32,5]{0,1:T(8,128)}, u32[]{:S(2)}) copy-start(s32[32,5]{0,1:T(8,128)} %param.12) | copy-start | bytes 1924
  58.3 7.8 %collective-permute-start.17 = (bf16[3,4,64,128]{3,2,1,0:T(8,128)(2,1)S(1)}, bf16[3,4,64,128]{3,2,1,0:T(8,128)(2,1)S(1)}, u32[]{:S(2)}, u32[]{:S(2)}) collective-permute-start(bf16[3,4,64,128]{3,2,1,0:T(8,128)(2,1)S(1)} %get-tuple-element.128), channel_id=1, source_target_pairs={{0,8},{8,0},{16,24},{24,16},{1,9},{9,1},{17,25},{25,17},{2,10},{10... | collective-permute-start | bytes 589832 | tf_op jit(solution)/shard_map/ppermute | solution.py:63
  59.1 9.1 %collective-permute-start.18 = (bf16[3,4,64,128]{3,2,1,0:T(8,128)(2,1)S(1)}, bf16[3,4,64,128]{3,2,1,0:T(8,128)(2,1)S(1)}, u32[]{:S(2)}, u32[]{:S(2)}) collective-permute-start(bf16[3,4,64,128]{3,2,1,0:T(8,128)(2,1)S(1)} %get-tuple-element.129), channel_id=1, source_target_pairs={{0,16},{8,24},{16,0},{24,8},{1,17},{9,25},{17,1},{25,9},{2,18},{10... | collective-permute-start | bytes 589832 | tf_op jit(solution)/shard_map/ppermute | solution.py:63
  59.5 10.5 %collective-permute-start.19 = (bf16[3,4,64,128]{3,2,1,0:T(8,128)(2,1)S(1)}, bf16[3,4,64,128]{3,2,1,0:T(8,128)(2,1)S(1)}, u32[]{:S(2)}, u32[]{:S(2)}) collective-permute-start(bf16[3,4,64,128]{3,2,1,0:T(8,128)(2,1)S(1)} %get-tuple-element.130), channel_id=1, source_target_pairs={{0,24},{8,16},{16,8},{24,0},{1,25},{9,17},{17,9},{25,1},{2,26},{10... | collective-permute-start | bytes 589832 | tf_op jit(solution)/shard_map/ppermute | solution.py:63

commit v13 on v11

--- a/solution.py
+++ b/solution.py
@@ -30,7 +30,7 @@
     return pl.CostEstimate(flops=1024, bytes_accessed=1024, transcendentals=0)
 
 
-FIRST_SEND, FIRST_RETURN, SECOND = 2, 1, None
+FIRST_SEND, FIRST_RETURN, SECOND_SEND, SECOND_RETURN = 2, 1, None, 1
 
 
 def offsets(count, place):
@@ -240,7 +240,7 @@
     def store(c, value):
         physical_ref[c] = value
 
-    to_physical(offsets(count, SECOND), in_refs, inverse_ref[...], x_ref, store)
+    to_physical(offsets(count, SECOND_SEND), in_refs, inverse_ref[...], x_ref, store)
     for group in range(groups):
         lanes = slice(group * width, (group + 1) * width)
         for i in range(THETA // CHUNK):
@@ -252,7 +252,7 @@
             lorentz = [a + b for a, b in zip(cross(current, magnetic), cross(velocity, vorticity))]
             for c, value in enumerate(lorentz):
                 product_ref[c, at, lanes] = value.astype(jnp.bfloat16)
-    to_modes(offsets(count, SECOND), forward_ref, table_ref, product_ref, out_refs)
+    to_modes(offsets(count, SECOND_RETURN), forward_ref, table_ref, product_ref, out_refs)
 
 
 def second_physics(received, physical, inverse, forward):
@@ -435,43 +435,47 @@
     )(*received, from_prev, from_next, radial_blocks, axial_blocks, radius, columns)
 
 
-def momentum_kernel(count, arrived, *refs):
-    in_refs, (gradient_ref, out_ref, total_ref, sems) = refs[:arrived], refs[arrived:]
+def momentum_kernel(places, *refs):
+    count = lax.axis_size("mode")
+    in_refs, gradient_ref = refs[: len(places)], refs[len(places)]
+    out_ref, total_ref, sems = refs[-3:]
     me = lax.axis_index("mode")
-    components, held, rows, _ = in_refs[0].shape
+    components, tiles, rows, _ = in_refs[0].shape
     mode_count = rows // 2
-    tiles = arrived // count * held
-    stride = 2 * count * tiles
-    out_rows = mode_count * stride
     copies = []
-    for c in range(components):
-        for step, offset in enumerate(offsets(count, SECOND)):
-            share = source_of(me, offset, count)
+    for i, place in enumerate(places):
+        share = source_of(me, offsets(count, SECOND_RETURN)[place], count)
+        for c in range(components):
             for start in range(0, tiles, SUBLANES // 2):
                 values = []
                 for t in range(start, min(tiles, start + SUBLANES // 2)):
-                    piece = in_refs[t // held * count + step][c, t % held].astype(jnp.float32)
-                    values.append(piece - gradient_ref[c, share * tiles + t])
-                put_rows(total_ref, c * out_rows + 2 * (share * tiles + start), stride, values)
-        done = pl.ds(c * out_rows, out_rows)
-        copies.append(pltpu.make_async_copy(total_ref.at[done], out_ref.at[done], sems.at[c]))
-        copies[c].start()
+                    values.append(in_refs[i][c, t].astype(jnp.float32) - gradient_ref[c, share * tiles + t])
+                put_rows(total_ref.at[i], c * mode_count * 2 * tiles + 2 * start, 2 * tiles, values)
+        here = pl.ds(pl.multiple_of(share * 2 * tiles, 2 * tiles), 2 * tiles)
+        source = total_ref.at[i].reshape(components * mode_count, 2 * tiles, LANES)
+        copies.append(pltpu.make_async_copy(source, out_ref.at[:, here, :], sems.at[i]))
+        copies[i].start()
     for copy in copies:
         copy.wait()
 
 
-def momentum_of(received, gradient, count):
-    components, held, rows, _ = received[0].shape
-    shape = (components * rows * len(received) * held, LANES)
-    return pl.pallas_call(
-        functools.partial(momentum_kernel, count, len(received)),
-        in_specs=[vmem()] * (len(received) + 1),
-        out_specs=pl.BlockSpec(memory_space=pl.ANY),
+def momentum_of(received, gradient, places, before):
+    components, tiles, rows, _ = received[0].shape
+    shape = (components * rows // 2, 2 * gradient.shape[1], LANES)
+    anywhere = pl.BlockSpec(memory_space=pl.ANY)
+    return pl.pallas_call(
+        functools.partial(momentum_kernel, places),
+        in_specs=[vmem()] * (len(received) + 1) + [anywhere] * len(before),
+        out_specs=anywhere,
         out_shape=jax.ShapeDtypeStruct(shape, jnp.float32),
-        scratch_shapes=[pltpu.VMEM(shape, jnp.float32), pltpu.SemaphoreType.DMA((components,))],
-        compiler_params=params(),
-        cost_estimate=cost(),
-    )(*received, gradient)
+        scratch_shapes=[
+            pltpu.VMEM((len(places), components * rows * tiles, LANES), jnp.float32),
+            pltpu.SemaphoreType.DMA((len(places),)),
+        ],
+        input_output_aliases={len(received) + 1: 0} if before else {},
+        compiler_params=params(),
+        cost_estimate=cost(),
+    )(*received, gradient, *before)
 
 
 def whole_output(value, mode_count, width):
@@ -497,7 +501,7 @@
     parcels = [(0, 6, 0, group, groups) for group in range(groups)]
     *own, inverse, forward = pack_rest(mode_fields, parcels, [inverse, forward])
     arrived[0][1:2], carried = lax.optimization_barrier((arrived[0][1:2], [inverse, forward]))
-    order = offsets(count, SECOND)
+    order = offsets(count, SECOND_SEND)
     parcels = [(6, 12, offset, 0, 1) for offset in order]
     *shares, later_inverse, later_forward = pack_rest(mode_fields, parcels, carried)
     local, physical = [], []
@@ -518,11 +522,14 @@
     sources, halos = lax.optimization_barrier((sources, halos))
     lorentz = list(second_physics(joined(sources), physical, later_inverse, later_forward))
     lorentz, radius = lax.optimization_barrier((lorentz, radius))
-    lorentz = exchange(lorentz, order)
+    lorentz = exchange(lorentz, offsets(count, SECOND_RETURN))
     induction, gradient = derive(
         local, *halos, radial_blocks, axial_blocks, radius.reshape(1, width), block_columns.T, count
     )
-    momentum = momentum_of(lorentz, gradient, count)
+    late = count - 1
+    places = [place for place in range(count) if place != late]
+    momentum = momentum_of([lorentz[place] for place in places], gradient, places, [])
+    momentum = momentum_of([lorentz[late]], gradient, [late], [momentum])
     return (whole_output(induction, mode_count, width), whole_output(momentum, mode_count, width))
 
 

time: 69 us -> 69.8 us (1.012)
  Pallas kernels: 13.4 us -> 14.1 us
    pallas_call x1 -> x2, Pallas kernels: 1.32 us -> 2.02 us  [momentum_of(): pl.pallas_call(functools.partial(momentum_kernel, places), in_specs=[vmem...]
  transfers between devices with their start and end apart: 20 -> 20, of which waited for: 11 -> 10; matrix products, arithmetic and copies ran while one was open for 0% -> 0% of each run, Pallas kernels for 15% -> 16%
where the time goes in v13:
time: 69.8 us; the launch traced here: 69.6 us
  starting transfers between devices  31.4 us (45%)
  waiting for transfers between devices  21.4 us (31%)
  Pallas kernels  14.1 us (20%)
  local copies, waits for them, and re-layouts  1.93 us (3%)
  between operations  0.85 us (1%)
    ppermute x18, starting transfers between devices, exchange(): received.append(lax.ppermute(piece, 'mode', pairs))  28.8 us
    ppermute x18, waiting for transfers between devices, exchange(): received.append(lax.ppermute(piece, 'mode', pairs))  17.6 us
    pallas_call x1, Pallas kernels, derive(): pl.pallas_call(functools.partial(derive_kernel, count, len(received)), in...  5.02 us
    ppermute x2, waiting for transfers between devices, from_behind(): lax.ppermute(value, axis, [(source, source + steps) for source in range(i...  3.74 us
    ppermute x2, starting transfers between devices, from_behind(): lax.ppermute(value, axis, [(source, source + steps) for source in range(i...  2.59 us
    pallas_call x2, Pallas kernels, momentum_of(): pl.pallas_call(functools.partial(momentum_kernel, places), in_specs=[vmem...  2.02 us
    unnamed x18, local copies, waits for them, and re-layouts  1.93 us
    pallas_call x2, Pallas kernels, first_physics(): pl.pallas_call(functools.partial(first_kernel, count), in_specs=[vmem()]...  1.64 us
  transfers between devices with their start and end apart: 20, of which 10 were waited for; matrix products, arithmetic and copies ran while one was open for 0% of the time, Pallas kernels for 16%

profile of v13, /device:TPU:0, one launch (start us, length us, event | category | flops | bytes accessed | tf_op | source)
XLA Modules:
  0.0 69.6 jit_solution(15806410087557271774)
XLA Ops:
  0.6 1.9 %copy-done = bf16[12,32,2,2048]{3,2,1,0:T(2,128)(2,1)S(1)} copy-done((bf16[12,32,2,2048]{3,2,1,0:T(2,128)(2,1)S(1)}, bf16[12,32,2,2048]{3,2,1,0:T(2,128)(2,1)}, u32[]{:S(2)}) %copy-start) | copy-done | bytes 3145752
  2.5 0.2 shard_map.102
  2.7 4.0 %collective-permute-start.7 = (bf16[6,2,32,2,128]{4,3,2,1,0:T(2,128)(2,1)S(1)}, bf16[6,2,32,2,128]{4,3,2,1,0:T(2,128)(2,1)S(1)}, u32[]{:S(2)}, u32[]{:S(2)}) collective-permute-start(bf16[6,2,32,2,128]{4,3,2,1,0:T(2,128)(2,1)S(1)} %shard_map.102), channel_id=1, source_target_pairs={{0,24},{8,16},{16,8},{24,0},{1,25},{9,17},{17,9},{25,1},{2,26},{10... | collective-permute-start | bytes 589832 | tf_op jit(solution)/shard_map/ppermute | solution.py:63
  6.6 0.2 shard_map.103
  6.8 0.6 collective-permute-start.8
  7.4 0.2 shard_map.101
  7.6 0.1 collective-permute-start.6
  7.7 0.2 shard_map.97
  7.9 3.0 %collective-permute-start.1 = (bf16[6,2,32,2,128]{4,3,2,1,0:T(2,128)(2,1)S(1)}, bf16[6,2,32,2,128]{4,3,2,1,0:T(2,128)(2,1)S(1)}, u32[]{:S(2)}, u32[]{:S(2)}) collective-permute-start(bf16[6,2,32,2,128]{4,3,2,1,0:T(2,128)(2,1)S(1)} %shard_map.97), channel_id=1, source_target_pairs={{0,24},{8,16},{16,8},{24,0},{1,25},{9,17},{17,9},{25,1},{2,26},{10... | collective-permute-start | bytes 589832 | tf_op jit(solution)/shard_map/ppermute | solution.py:63
  10.8 0.2 shard_map.96
  11.0 0.0 copy-start.4
  11.0 0.0 copy-start.5
  11.0 0.6 collective-permute-start
  11.6 0.2 shard_map.98
  11.8 0.6 collective-permute-done.7
  12.4 2.1 %collective-permute-start.2 = (bf16[6,2,32,2,128]{4,3,2,1,0:T(2,128)(2,1)S(1)}, bf16[6,2,32,2,128]{4,3,2,1,0:T(2,128)(2,1)S(1)}, u32[]{:S(2)}, u32[]{:S(2)}) collective-permute-start(bf16[6,2,32,2,128]{4,3,2,1,0:T(2,128)(2,1)S(1)} %shard_map.98), channel_id=1, source_target_pairs={{0,16},{8,24},{16,0},{24,8},{1,17},{9,25},{17,1},{25,9},{2,18},{10... | collective-permute-start | bytes 589832 | tf_op jit(solution)/shard_map/ppermute | solution.py:63
  14.5 0.3 shard_map.95
  14.8 1.9 %collective-permute-done.8 = bf16[6,2,32,2,128]{4,3,2,1,0:T(2,128)(2,1)S(1)} collective-permute-done((bf16[6,2,32,2,128]{4,3,2,1,0:T(2,128)(2,1)S(1)}, bf16[6,2,32,2,128]{4,3,2,1,0:T(2,128)(2,1)S(1)}, u32[]{:S(2)}, u32[]{:S(2)}) %collective-permute-start.8) | collective-permute-done | bytes 196640 | tf_op jit(solution)/shard_map/ppermute | solution.py:63
  16.7 0.5 collective-permute-done.6
  17.2 0.8 %shard_map.104 = (bf16[4,2,64,128]{3,2,1,0:T(8,128)(2,1)S(1)}, bf16[4,2,64,128]{3,2,1,0:T(8,128)(2,1)S(1)}, bf16[4,2,64,128]{3,2,1,0:T(8,128)(2,1)S(1)}, bf16[4,...) custom-call(bf16[6,2,64,128]{3,2,1,0:T(8,128)(2,1)S(1)} %bitcast.35, bf16[6,2,64,128]{3,2,1,0:T(8,128)(2,1)S(1)} %bitcast.34, ...), custom_call_target="tpu_custom_call" | custom-call | flops 1024 | bytes 1024 | tf_op jit(solution)/shard_map/pallas_call | solution.py:218
  18.0 2.5 %collective-permute-start.9 = (bf16[4,2,64,128]{3,2,1,0:T(8,128)(2,1)S(1)}, bf16[4,2,64,128]{3,2,1,0:T(8,128)(2,1)S(1)}, u32[]{:S(2)}, u32[]{:S(2)}) collective-permute-start(bf16[4,2,64,128]{3,2,1,0:T(8,128)(2,1)S(1)} %get-tuple-element.73), channel_id=1, source_target_pairs={{0,24},{8,16},{16,8},{24,0},{1,25},{9,17},{17,9},{25,1},{2,26},{10... | collective-permute-start | bytes 393224 | tf_op jit(solution)/shard_map/ppermute | solution.py:63
  20.5 0.4 collective-permute-done.1
  20.9 2.0 %collective-permute-start.10 = (bf16[4,2,64,128]{3,2,1,0:T(8,128)(2,1)S(1)}, bf16[4,2,64,128]{3,2,1,0:T(8,128)(2,1)S(1)}, u32[]{:S(2)}, u32[]{:S(2)}) collective-permute-start(bf16[4,2,64,128]{3,2,1,0:T(8,128)(2,1)S(1)} %get-tuple-element.74), channel_id=1, source_target_pairs={{0,8},{8,0},{16,24},{24,16},{1,9},{9,1},{17,25},{25,17},{2,10},{10... | collective-permute-start | bytes 393224 | tf_op jit(solution)/shard_map/ppermute | solution.py:63
  22.9 1.5 %collective-permute-start.11 = (bf16[4,2,64,128]{3,2,1,0:T(8,128)(2,1)S(1)}, bf16[4,2,64,128]{3,2,1,0:T(8,128)(2,1)S(1)}, u32[]{:S(2)}, u32[]{:S(2)}) collective-permute-start(bf16[4,2,64,128]{3,2,1,0:T(8,128)(2,1)S(1)} %get-tuple-element.75), channel_id=1, source_target_pairs={{0,16},{8,24},{16,0},{24,8},{1,17},{9,25},{17,1},{25,9},{2,18},{10... | collective-permute-start | bytes 393224 | tf_op jit(solution)/shard_map/ppermute | solution.py:63
  24.4 1.3 %shard_map.99 = (bf16[6,4,32,2,128]{4,3,2,1,0:T(2,128)(2,1)S(1)}, bf16[6,4,32,2,128]{4,3,2,1,0:T(2,128)(2,1)S(1)}, bf16[6,4,32,2,128]{4,3,2,1,0:T(2,128)(2,1)S(1...) custom-call(bf16[12,32,2,2048]{3,2,1,0:T(2,128)(2,1)S(1)} %copy-done.1, ...), custom_call_target="tpu_custom_call" | custom-call | flops 1024 | bytes 1024 | tf_op jit(solution)/shard_map/pallas_call | solution.py:150
  25.7 0.8 %shard_map.100 = (bf16[4,2,64,128]{3,2,1,0:T(8,128)(2,1)S(1)}, bf16[4,2,64,128]{3,2,1,0:T(8,128)(2,1)S(1)}, bf16[4,2,64,128]{3,2,1,0:T(8,128)(2,1)S(1)}, bf16[4,...) custom-call(bf16[6,2,64,128]{3,2,1,0:T(8,128)(2,1)S(1)} %bitcast.31, bf16[6,2,64,128]{3,2,1,0:T(8,128)(2,1)S(1)} %bitcast.29, ...), custom_call_target="tpu_custom_call" | custom-call | flops 1024 | bytes 1024 | tf_op jit(solution)/shard_map/pallas_call | solution.py:218
  26.5 2.4 %collective-permute-start.3 = (bf16[4,2,64,128]{3,2,1,0:T(8,128)(2,1)S(1)}, bf16[4,2,64,128]{3,2,1,0:T(8,128)(2,1)S(1)}, u32[]{:S(2)}, u32[]{:S(2)}) collective-permute-start(bf16[4,2,64,128]{3,2,1,0:T(8,128)(2,1)S(1)} %get-tuple-element.68), channel_id=1, source_target_pairs={{0,24},{8,16},{16,8},{24,0},{1,25},{9,17},{17,9},{25,1},{2,26},{10... | collective-permute-start | bytes 393224 | tf_op jit(solution)/shard_map/ppermute | solution.py:63
  28.9 0.6 collective-permute-start.4
  29.5 0.6 collective-permute-start.5
  30.1 0.3 collective-permute-done.10.refs_6_
  30.4 2.3 %collective-permute-start.12 = (bf16[6,4,32,2,128]{4,3,2,1,0:T(2,128)(2,1)S(1)}, bf16[6,4,32,2,128]{4,3,2,1,0:T(2,128)(2,1)S(1)}, u32[]{:S(2)}, u32[]{:S(2)}) collective-permute-start(bf16[6,4,32,2,128]{4,3,2,1,0:T(2,128)(2,1)S(1)} %get-tuple-element.92), channel_id=1, source_target_pairs={{0,8},{8,0},{16,24},{24,16},{1,9},{9,1},{17,25},{25,17},{2,10},{10... | collective-permute-start | bytes 1179656 | tf_op jit(solution)/shard_map/ppermute | solution.py:63
  32.7 1.2 %collective-permute-done.3.refs_1_ = bf16[4,2,64,128]{3,2,1,0:T(8,128)(2,1)S(1)} collective-permute-done((bf16[4,2,64,128]{3,2,1,0:T(8,128)(2,1)S(1)}, bf16[4,2,64,128]{3,2,1,0:T(8,128)(2,1)S(1)}, u32[]{:S(2)}, u32[]{:S(2)}) %collective-permute-start.3) | collective-permute-done | bytes 131104 | tf_op jit(solution)/shard_map/ppermute | solution.py:63
  33.9 2.8 %collective-permute-done.4.refs_2_ = bf16[4,2,64,128]{3,2,1,0:T(8,128)(2,1)S(1)} collective-permute-done((bf16[4,2,64,128]{3,2,1,0:T(8,128)(2,1)S(1)}, bf16[4,2,64,128]{3,2,1,0:T(8,128)(2,1)S(1)}, u32[]{:S(2)}, u32[]{:S(2)}) %collective-permute-start.4) | collective-permute-done | bytes 131104 | tf_op jit(solution)/shard_map/ppermute | solution.py:63
  36.7 0.6 collective-permute-start.13
  37.3 2.5 %collective-permute-start.14 = (bf16[6,4,32,2,128]{4,3,2,1,0:T(2,128)(2,1)S(1)}, bf16[6,4,32,2,128]{4,3,2,1,0:T(2,128)(2,1)S(1)}, u32[]{:S(2)}, u32[]{:S(2)}) collective-permute-start(bf16[6,4,32,2,128]{4,3,2,1,0:T(2,128)(2,1)S(1)} %get-tuple-element.94), channel_id=1, source_target_pairs={{0,24},{8,16},{16,8},{24,0},{1,25},{9,17},{17,9},{25,1},{2,26},{10... | collective-permute-start | bytes 1179656 | tf_op jit(solution)/shard_map/ppermute | solution.py:63
  39.8 1.2 %shard_map.105 = (bf16[4,2,64,128]{3,2,1,0:T(8,128)(2,1)S(1)}, bf16[4,2,64,128]{3,2,1,0:T(8,128)(2,1)S(1)}) custom-call(bf16[4,2,64,128]{3,2,1,0:T(8,128)(2,1)S(1)} %get-tuple-element.83.refs_0_, bf16[4,2,64,128]{3,2,1,0:T(8,128)(2,1)S(1)} %collective-permute-done.3.refs_1_, bf16[4,2,64,128]{3,2,1,0:T(8,128)(2,1)S(1)} %collective-permute-done.4.refs_2_, ...), custom_call_target="tpu_custom_call" | custom-call | flops 1024 | bytes 1024 | tf_op jit(solution)/shard_map/pallas_call | solution.py:312
  41.1 1.3 %collective-permute-start.15 = (bf16[4,2,64,128]{3,2,1,0:T(8,128)(2,1)S(1)}, bf16[4,2,64,128]{3,2,1,0:T(8,128)(2,1)S(1)}, u32[]{:S(2)}, u32[]{:S(2)}) collective-permute-start(bf16[4,2,64,128]{3,2,1,0:T(8,128)(2,1)S(1)} %get-tuple-element.95), channel_id=1, source_target_pairs={{0,1},{1,2},{2,3},{3,4},{4,5},{5,6},{6,7},{8,9},{9,10},{10,11},{11... | collective-permute-start | bytes 393224 | tf_op jit(solution)/shard_map/ppermute | solution.py:70
  42.4 1.3 %collective-permute-start.16 = (bf16[4,2,64,128]{3,2,1,0:T(8,128)(2,1)S(1)}, bf16[4,2,64,128]{3,2,1,0:T(8,128)(2,1)S(1)}, u32[]{:S(2)}, u32[]{:S(2)}) collective-permute-start(bf16[4,2,64,128]{3,2,1,0:T(8,128)(2,1)S(1)} %get-tuple-element.96), channel_id=1, source_target_pairs={{1,0},{2,1},{3,2},{4,3},{5,4},{6,5},{7,6},{9,8},{10,9},{11,10},{12... | collective-permute-start | bytes 393224 | tf_op jit(solution)/shard_map/ppermute | solution.py:70
  43.7 3.7 %collective-permute-done.16.refs_9_ = bf16[4,2,64,128]{3,2,1,0:T(8,128)(2,1)S(1)} collective-permute-done((bf16[4,2,64,128]{3,2,1,0:T(8,128)(2,1)S(1)}, bf16[4,2,64,128]{3,2,1,0:T(8,128)(2,1)S(1)}, u32[]{:S(2)}, u32[]{:S(2)}) %collective-permute-start.16) | collective-permute-done | bytes 131104 | tf_op jit(solution)/shard_map/ppermute | solution.py:70
  47.4 7.3 %collective-permute-done.13 = bf16[6,4,32,2,128]{4,3,2,1,0:T(2,128)(2,1)S(1)} collective-permute-done((bf16[6,4,32,2,128]{4,3,2,1,0:T(2,128)(2,1)S(1)}, bf16[6,4,32,2,128]{4,3,2,1,0:T(2,128)(2,1)S(1)}, u32[]{:S(2)}, u32[]{:S(2)}) %collective-permute-start.13) | collective-permute-done | bytes 393248 | tf_op jit(solution)/shard_map/ppermute | solution.py:63
  54.8 1.6 %shard_map.106 = (bf16[3,4,64,128]{3,2,1,0:T(8,128)(2,1)S(1)}, bf16[3,4,64,128]{3,2,1,0:T(8,128)(2,1)S(1)}, bf16[3,4,64,128]{3,2,1,0:T(8,128)(2,1)S(1)}, bf16[3,4,64,128]{3,2,1,0:T(8,128)(2,1)S(1)}) custom-call(bf16[6,4,64,128]{3,2,1,0:T(8,128)(2,1)S(1)} %bitcast.24, bf16[6,4,64,128]{3,2,1,0:T(8,128)(2,1)S(1)} %bitcast.25, ...), custom_call_target="tpu_custom_call" | custom-call | flops 1024 | bytes 1024 | tf_op jit(solution)/shard_map/pallas_call | solution.py:262
  56.4 1.9 %collective-permute-start.18 = (bf16[3,4,64,128]{3,2,1,0:T(8,128)(2,1)S(1)}, bf16[3,4,64,128]{3,2,1,0:T(8,128)(2,1)S(1)}, u32[]{:S(2)}, u32[]{:S(2)}) collective-permute-start(bf16[3,4,64,128]{3,2,1,0:T(8,128)(2,1)S(1)} %get-tuple-element.114), channel_id=1, source_target_pairs={{0,24},{8,16},{16,8},{24,0},{1,25},{9,17},{17,9},{25,1},{2,26},{10... | collective-permute-start | bytes 589832 | tf_op jit(solution)/shard_map/ppermute | solution.py:63
  58.3 1.4 %collective-permute-start.19 = (bf16[3,4,64,128]{3,2,1,0:T(8,128)(2,1)S(1)}, bf16[3,4,64,128]{3,2,1,0:T(8,128)(2,1)S(1)}, u32[]{:S(2)}, u32[]{:S(2)}) collective-permute-start(bf16[3,4,64,128]{3,2,1,0:T(8,128)(2,1)S(1)} %get-tuple-element.115), channel_id=1, source_target_pairs={{0,8},{8,0},{16,24},{24,16},{1,9},{9,1},{17,25},{25,17},{2,10},{10... | collective-permute-start | bytes 589832 | tf_op jit(solution)/shard_map/ppermute | solution.py:63
  59.7 0.3 collective-permute-start.17
  59.9 5.0 %shard_map.107 = (f32[3072,128]{1,0:T(8,128)}, f32[3,16,64,128]{3,2,1,0:T(8,128)S(1)}) custom-call(bf16[4,2,64,128]{3,2,1,0:T(8,128)(2,1)S(1)} %get-tuple-element.83.refs_0_, bf16[4,2,64,128]{3,2,1,0:T(8,128)(2,1)S(1)} %collective-permute-done.3.refs_1_, bf16[4,2,64,128]{3,2,1,0:T(8,128)(2,1)S(1)} %collective-permute-done.4.refs_2_, ...), custom_call_target="tpu_custom_call" | custom-call | flops 1024 | bytes 1024 | tf_op jit(solution)/shard_map/pallas_call | solution.py:424
  65.0 2.6 %collective-permute-done.19.refs_2_ = bf16[3,4,64,128]{3,2,1,0:T(8,128)(2,1)S(1)} collective-permute-done((bf16[3,4,64,128]{3,2,1,0:T(8,128)(2,1)S(1)}, bf16[3,4,64,128]{3,2,1,0:T(8,128)(2,1)S(1)}, u32[]{:S(2)}, u32[]{:S(2)}) %collective-permute-start.19) | collective-permute-done | bytes 196640 | tf_op jit(solution)/shard_map/ppermute | solution.py:63
  67.6 1.1 %shard_map.108.refs_2_ = f32[96,32,128]{2,1,0:T(8,128)} custom-call(bf16[3,4,64,128]{3,2,1,0:T(8,128)(2,1)S(1)} %get-tuple-element.113.refs_0_, bf16[3,4,64,128]{3,2,1,0:T(8,128)(2,1)S(1)} %collective-permute-done.18.refs_1_, bf16[3,4,64,128]{3,2,1,0:T(8,128)(2,1)S(1)} %collective-permute-done.19.refs_2_, ...), custom_call_target="tpu_custom_call" | custom-call | flops 1024 | bytes 1024 | tf_op jit(solution)/shard_map/pallas_call | solution.py:466
  68.7 0.9 %shard_map.109 = f32[96,32,128]{2,1,0:T(8,128)} custom-call(bf16[3,4,64,128]{3,2,1,0:T(8,128)(2,1)S(1)} %collective-permute-done.17.refs_0_, f32[3,16,64,128]{3,2,1,0:T(8,128)S(1)} %get-tuple-element.112.refs_3_.refs_1_, f32[96,32,128]{2,1,0:T(8,128)} %shard_map.108.refs_2_), custom_call_target="tpu_custom_call", output_to_operand_aliasing={{}: (2, {})} | custom-call | flops 1024 | bytes 1024 | tf_op jit(solution)/shard_map/pallas_call | solution.py:466
  (25 shorter events, 0.1 us)
Async XLA Ops:
  0.6 1.9 %copy-start = (bf16[12,32,2,2048]{3,2,1,0:T(2,128)(2,1)S(1)}, bf16[12,32,2,2048]{3,2,1,0:T(2,128)(2,1)}, u32[]{:S(2)}) copy-start(bf16[12,32,2,2048]{3,2,1,0:T(2,128)(2,1)} %fields_ref.15) | copy-start | bytes 9437188
  2.7 9.7 %collective-permute-start.7 = (bf16[6,2,32,2,128]{4,3,2,1,0:T(2,128)(2,1)S(1)}, bf16[6,2,32,2,128]{4,3,2,1,0:T(2,128)(2,1)S(1)}, u32[]{:S(2)}, u32[]{:S(2)}) collective-permute-start(bf16[6,2,32,2,128]{4,3,2,1,0:T(2,128)(2,1)S(1)} %shard_map.102), channel_id=1, source_target_pairs={{0,24},{8,16},{16,8},{24,0},{1,25},{9,17},{17,9},{25,1},{2,26},{10... | collective-permute-start | bytes 589832 | tf_op jit(solution)/shard_map/ppermute | solution.py:63
  6.8 9.9 %collective-permute-start.8 = (bf16[6,2,32,2,128]{4,3,2,1,0:T(2,128)(2,1)S(1)}, bf16[6,2,32,2,128]{4,3,2,1,0:T(2,128)(2,1)S(1)}, u32[]{:S(2)}, u32[]{:S(2)}) collective-permute-start(bf16[6,2,32,2,128]{4,3,2,1,0:T(2,128)(2,1)S(1)} %shard_map.103), channel_id=1, source_target_pairs={{0,16},{8,24},{16,0},{24,8},{1,17},{9,25},{17,1},{25,9},{2,18},{10... | collective-permute-start | bytes 589832 | tf_op jit(solution)/shard_map/ppermute | solution.py:63
  7.6 9.6 %collective-permute-start.6 = (bf16[6,2,32,2,128]{4,3,2,1,0:T(2,128)(2,1)S(1)}, bf16[6,2,32,2,128]{4,3,2,1,0:T(2,128)(2,1)S(1)}, u32[]{:S(2)}, u32[]{:S(2)}) collective-permute-start(bf16[6,2,32,2,128]{4,3,2,1,0:T(2,128)(2,1)S(1)} %shard_map.101), channel_id=1, source_target_pairs={{0,8},{8,0},{16,24},{24,16},{1,9},{9,1},{17,25},{25,17},{2,10},{10... | collective-permute-start | bytes 589832 | tf_op jit(solution)/shard_map/ppermute | solution.py:63
  7.9 13.0 %collective-permute-start.1 = (bf16[6,2,32,2,128]{4,3,2,1,0:T(2,128)(2,1)S(1)}, bf16[6,2,32,2,128]{4,3,2,1,0:T(2,128)(2,1)S(1)}, u32[]{:S(2)}, u32[]{:S(2)}) collective-permute-start(bf16[6,2,32,2,128]{4,3,2,1,0:T(2,128)(2,1)S(1)} %shard_map.97), channel_id=1, source_target_pairs={{0,24},{8,16},{16,8},{24,0},{1,25},{9,17},{17,9},{25,1},{2,26},{10... | collective-permute-start | bytes 589832 | tf_op jit(solution)/shard_map/ppermute | solution.py:63
  11.0 3.5 %copy-start.4 = (bf16[256,256]{1,0:T(8,128)(2,1)S(1)}, bf16[256,256]{1,0:T(8,128)(2,1)}, u32[]{:S(2)}) copy-start(bf16[256,256]{1,0:T(8,128)(2,1)} %constant.5.clone.refs_1_) | copy-start | bytes 393220
  11.0 3.4 %copy-start.5 = (bf16[256,256]{1,0:T(8,128)(2,1)S(1)}, bf16[256,256]{1,0:T(8,128)(2,1)}, u32[]{:S(2)}) copy-start(bf16[256,256]{1,0:T(8,128)(2,1)} %constant.4.clone.refs_0_) | copy-start | bytes 393220
  11.0 14.7 %collective-permute-start = (bf16[6,2,32,2,128]{4,3,2,1,0:T(2,128)(2,1)S(1)}, bf16[6,2,32,2,128]{4,3,2,1,0:T(2,128)(2,1)S(1)}, u32[]{:S(2)}, u32[]{:S(2)}) collective-permute-start(bf16[6,2,32,2,128]{4,3,2,1,0:T(2,128)(2,1)S(1)} %shard_map.96), channel_id=1, source_target_pairs={{0,8},{8,0},{16,24},{24,16},{1,9},{9,1},{17,25},{25,17},{2,10},{10... | collective-permute-start | bytes 589832 | tf_op jit(solution)/shard_map/ppermute | solution.py:63
  11.8 12.6 %copy-start.1 = (bf16[12,32,2,2048]{3,2,1,0:T(2,128)(2,1)S(1)}, bf16[12,32,2,2048]{3,2,1,0:T(2,128)(2,1)}, u32[]{:S(2)}) copy-start(bf16[12,32,2,2048]{3,2,1,0:T(2,128)(2,1)} %fields_ref.15) | copy-start | bytes 9437188
  12.4 13.3 %collective-permute-start.2 = (bf16[6,2,32,2,128]{4,3,2,1,0:T(2,128)(2,1)S(1)}, bf16[6,2,32,2,128]{4,3,2,1,0:T(2,128)(2,1)S(1)}, u32[]{:S(2)}, u32[]{:S(2)}) collective-permute-start(bf16[6,2,32,2,128]{4,3,2,1,0:T(2,128)(2,1)S(1)} %shard_map.98), channel_id=1, source_target_pairs={{0,16},{8,24},{16,0},{24,8},{1,17},{9,25},{17,1},{25,9},{2,18},{10... | collective-permute-start | bytes 589832 | tf_op jit(solution)/shard_map/ppermute | solution.py:63
  18.0 11.5 %collective-permute-start.9 = (bf16[4,2,64,128]{3,2,1,0:T(8,128)(2,1)S(1)}, bf16[4,2,64,128]{3,2,1,0:T(8,128)(2,1)S(1)}, u32[]{:S(2)}, u32[]{:S(2)}) collective-permute-start(bf16[4,2,64,128]{3,2,1,0:T(8,128)(2,1)S(1)} %get-tuple-element.73), channel_id=1, source_target_pairs={{0,24},{8,16},{16,8},{24,0},{1,25},{9,17},{17,9},{25,1},{2,26},{10... | collective-permute-start | bytes 393224 | tf_op jit(solution)/shard_map/ppermute | solution.py:63
  20.9 9.6 %collective-permute-start.10 = (bf16[4,2,64,128]{3,2,1,0:T(8,128)(2,1)S(1)}, bf16[4,2,64,128]{3,2,1,0:T(8,128)(2,1)S(1)}, u32[]{:S(2)}, u32[]{:S(2)}) collective-permute-start(bf16[4,2,64,128]{3,2,1,0:T(8,128)(2,1)S(1)} %get-tuple-element.74), channel_id=1, source_target_pairs={{0,8},{8,0},{16,24},{24,16},{1,9},{9,1},{17,25},{25,17},{2,10},{10... | collective-permute-start | bytes 393224 | tf_op jit(solution)/shard_map/ppermute | solution.py:63
  22.9 16.9 %copy-start.8 = (s32[2,256]{1,0:T(2,128)S(1)}, s32[2,256]{1,0:T(2,128)}, u32[]{:S(2)}) copy-start(s32[2,256]{1,0:T(2,128)} %refs_8_.1) | copy-start | bytes 6148
  22.9 7.5 %collective-permute-start.11 = (bf16[4,2,64,128]{3,2,1,0:T(8,128)(2,1)S(1)}, bf16[4,2,64,128]{3,2,1,0:T(8,128)(2,1)S(1)}, u32[]{:S(2)}, u32[]{:S(2)}) collective-permute-start(bf16[4,2,64,128]{3,2,1,0:T(8,128)(2,1)S(1)} %get-tuple-element.75), channel_id=1, source_target_pairs={{0,16},{8,24},{16,0},{24,8},{1,17},{9,25},{17,1},{25,9},{2,18},{10... | collective-permute-start | bytes 393224 | tf_op jit(solution)/shard_map/ppermute | solution.py:63
  26.5 7.4 %collective-permute-start.3 = (bf16[4,2,64,128]{3,2,1,0:T(8,128)(2,1)S(1)}, bf16[4,2,64,128]{3,2,1,0:T(8,128)(2,1)S(1)}, u32[]{:S(2)}, u32[]{:S(2)}) collective-permute-start(bf16[4,2,64,128]{3,2,1,0:T(8,128)(2,1)S(1)} %get-tuple-element.68), channel_id=1, source_target_pairs={{0,24},{8,16},{16,8},{24,0},{1,25},{9,17},{17,9},{25,1},{2,26},{10... | collective-permute-start | bytes 393224 | tf_op jit(solution)/shard_map/ppermute | solution.py:63
  28.9 7.8 %collective-permute-start.4 = (bf16[4,2,64,128]{3,2,1,0:T(8,128)(2,1)S(1)}, bf16[4,2,64,128]{3,2,1,0:T(8,128)(2,1)S(1)}, u32[]{:S(2)}, u32[]{:S(2)}) collective-permute-start(bf16[4,2,64,128]{3,2,1,0:T(8,128)(2,1)S(1)} %get-tuple-element.69), channel_id=1, source_target_pairs={{0,8},{8,0},{16,24},{24,16},{1,9},{9,1},{17,25},{25,17},{2,10},{10... | collective-permute-start | bytes 393224 | tf_op jit(solution)/shard_map/ppermute | solution.py:63
  29.5 7.2 %collective-permute-start.5 = (bf16[4,2,64,128]{3,2,1,0:T(8,128)(2,1)S(1)}, bf16[4,2,64,128]{3,2,1,0:T(8,128)(2,1)S(1)}, u32[]{:S(2)}, u32[]{:S(2)}) collective-permute-start(bf16[4,2,64,128]{3,2,1,0:T(8,128)(2,1)S(1)} %get-tuple-element.70), channel_id=1, source_target_pairs={{0,16},{8,24},{16,0},{24,8},{1,17},{9,25},{17,1},{25,9},{2,18},{10... | collective-permute-start | bytes 393224 | tf_op jit(solution)/shard_map/ppermute | solution.py:63
  30.4 17.0 %collective-permute-start.12 = (bf16[6,4,32,2,128]{4,3,2,1,0:T(2,128)(2,1)S(1)}, bf16[6,4,32,2,128]{4,3,2,1,0:T(2,128)(2,1)S(1)}, u32[]{:S(2)}, u32[]{:S(2)}) collective-permute-start(bf16[6,4,32,2,128]{4,3,2,1,0:T(2,128)(2,1)S(1)} %get-tuple-element.92), channel_id=1, source_target_pairs={{0,8},{8,0},{16,24},{24,16},{1,9},{9,1},{17,25},{25,17},{2,10},{10... | collective-permute-start | bytes 1179656 | tf_op jit(solution)/shard_map/ppermute | solution.py:63
  36.7 18.0 %collective-permute-start.13 = (bf16[6,4,32,2,128]{4,3,2,1,0:T(2,128)(2,1)S(1)}, bf16[6,4,32,2,128]{4,3,2,1,0:T(2,128)(2,1)S(1)}, u32[]{:S(2)}, u32[]{:S(2)}) collective-permute-start(bf16[6,4,32,2,128]{4,3,2,1,0:T(2,128)(2,1)S(1)} %get-tuple-element.93), channel_id=1, source_target_pairs={{0,16},{8,24},{16,0},{24,8},{1,17},{9,25},{17,1},{25,9},{2,18},{10... | collective-permute-start | bytes 1179656 | tf_op jit(solution)/shard_map/ppermute | solution.py:63
  37.3 17.5 %collective-permute-start.14 = (bf16[6,4,32,2,128]{4,3,2,1,0:T(2,128)(2,1)S(1)}, bf16[6,4,32,2,128]{4,3,2,1,0:T(2,128)(2,1)S(1)}, u32[]{:S(2)}, u32[]{:S(2)}) collective-permute-start(bf16[6,4,32,2,128]{4,3,2,1,0:T(2,128)(2,1)S(1)} %get-tuple-element.94), channel_id=1, source_target_pairs={{0,24},{8,16},{16,8},{24,0},{1,25},{9,17},{17,9},{25,1},{2,26},{10... | collective-permute-start | bytes 1179656 | tf_op jit(solution)/shard_map/ppermute | solution.py:63
  41.1 2.6 %collective-permute-start.15 = (bf16[4,2,64,128]{3,2,1,0:T(8,128)(2,1)S(1)}, bf16[4,2,64,128]{3,2,1,0:T(8,128)(2,1)S(1)}, u32[]{:S(2)}, u32[]{:S(2)}) collective-permute-start(bf16[4,2,64,128]{3,2,1,0:T(8,128)(2,1)S(1)} %get-tuple-element.95), channel_id=1, source_target_pairs={{0,1},{1,2},{2,3},{3,4},{4,5},{5,6},{6,7},{8,9},{9,10},{10,11},{11... | collective-permute-start | bytes 393224 | tf_op jit(solution)/shard_map/ppermute | solution.py:70
  42.4 5.0 %collective-permute-start.16 = (bf16[4,2,64,128]{3,2,1,0:T(8,128)(2,1)S(1)}, bf16[4,2,64,128]{3,2,1,0:T(8,128)(2,1)S(1)}, u32[]{:S(2)}, u32[]{:S(2)}) collective-permute-start(bf16[4,2,64,128]{3,2,1,0:T(8,128)(2,1)S(1)} %get-tuple-element.96), channel_id=1, source_target_pairs={{1,0},{2,1},{3,2},{4,3},{5,4},{6,5},{7,6},{9,8},{10,9},{11,10},{12... | collective-permute-start | bytes 393224 | tf_op jit(solution)/shard_map/ppermute | solution.py:70
  54.8 5.2 %copy-start.2 = (bf16[5,64,2048]{2,1,0:T(8,128)(2,1)S(1)}, bf16[5,64,2048]{2,1,0:T(8,128)(2,1)}, u32[]{:S(2)}) copy-start(bf16[5,64,2048]{2,1,0:T(8,128)(2,1)} %refs_10_.1) | copy-start | bytes 3932164
  54.8 5.2 %copy-start.3 = (bf16[5,64,2048]{2,1,0:T(8,128)(2,1)S(1)}, bf16[5,64,2048]{2,1,0:T(8,128)(2,1)}, u32[]{:S(2)}) copy-start(bf16[5,64,2048]{2,1,0:T(8,128)(2,1)} %refs_11_.1) | copy-start | bytes 3932164
  54.8 5.2 %copy-start.6 = (f32[2048]{0:T(1024)S(1)}, f32[2048]{0:T(1024)}, u32[]{:S(2)}) copy-start(f32[2048]{0:T(1024)} %param.9) | copy-start | bytes 24580
  54.8 5.2 %copy-start.7 = (s32[32,5]{0,1:T(8,128)S(1)}, s32[32,5]{0,1:T(8,128)}, u32[]{:S(2)}) copy-start(s32[32,5]{0,1:T(8,128)} %param.12) | copy-start | bytes 1924
  56.4 8.6 %collective-permute-start.18 = (bf16[3,4,64,128]{3,2,1,0:T(8,128)(2,1)S(1)}, bf16[3,4,64,128]{3,2,1,0:T(8,128)(2,1)S(1)}, u32[]{:S(2)}, u32[]{:S(2)}) collective-permute-start(bf16[3,4,64,128]{3,2,1,0:T(8,128)(2,1)S(1)} %get-tuple-element.114), channel_id=1, source_target_pairs={{0,24},{8,16},{16,8},{24,0},{1,25},{9,17},{17,9},{25,1},{2,26},{10... | collective-permute-start | bytes 589832 | tf_op jit(solution)/shard_map/ppermute | solution.py:63
  58.3 9.3 %collective-permute-start.19 = (bf16[3,4,64,128]{3,2,1,0:T(8,128)(2,1)S(1)}, bf16[3,4,64,128]{3,2,1,0:T(8,128)(2,1)S(1)}, u32[]{:S(2)}, u32[]{:S(2)}) collective-permute-start(bf16[3,4,64,128]{3,2,1,0:T(8,128)(2,1)S(1)} %get-tuple-element.115), channel_id=1, source_target_pairs={{0,8},{8,0},{16,24},{24,16},{1,9},{9,1},{17,25},{25,17},{2,10},{10... | collective-permute-start | bytes 589832 | tf_op jit(solution)/shard_map/ppermute | solution.py:63
  59.7 9.1 %collective-permute-start.17 = (bf16[3,4,64,128]{3,2,1,0:T(8,128)(2,1)S(1)}, bf16[3,4,64,128]{3,2,1,0:T(8,128)(2,1)S(1)}, u32[]{:S(2)}, u32[]{:S(2)}) collective-permute-start(bf16[3,4,64,128]{3,2,1,0:T(8,128)(2,1)S(1)} %get-tuple-element.111), channel_id=1, source_target_pairs={{0,16},{8,24},{16,0},{24,8},{1,17},{9,25},{17,1},{25,9},{2,18},{10... | collective-permute-start | bytes 589832 | tf_op jit(solution)/shard_map/ppermute | solution.py:63

commit v14 on v11

--- a/solution.py
+++ b/solution.py
@@ -30,7 +30,7 @@
     return pl.CostEstimate(flops=1024, bytes_accessed=1024, transcendentals=0)
 
 
-FIRST_SEND, FIRST_RETURN, SECOND = 2, 1, None
+FIRST_SEND, FIRST_RETURN, SECOND = 1, 1, None
 
 
 def offsets(count, place):
@@ -108,6 +108,23 @@
         target[...] = source[...]
     for copy in copies:
         copy.wait()
+
+
+def load(fields, components):
+    shape = (components,) + fields.shape[1:]
+
+    def kernel(fields_ref, out_ref, sems):
+        run_copies([(fields_ref.at[c], out_ref.at[c]) for c in range(components)], sems)
+
+    return pl.pallas_call(
+        kernel,
+        in_specs=[pl.BlockSpec(memory_space=pltpu.HBM)],
+        out_specs=vmem(),
+        out_shape=jax.ShapeDtypeStruct(shape, fields.dtype),
+        scratch_shapes=[pltpu.SemaphoreType.DMA((components,))],
+        compiler_params=params(),
+        cost_estimate=cost(),
+    )(pltpu.with_memory_space_constraint(fields, pltpu.HBM))
 
 
 def packed_shape(fields, first, last, groups):
@@ -490,12 +507,13 @@
         return [piece.reshape(piece.shape[:-3] + (rows, LANES)) for piece in pieces]
 
     groups = groups_of(width // count // LANES)
+    flow = load(mode_fields, 6)
     arrived = []
     for group in range(groups):
         order = offsets(count, FIRST_SEND)
-        arrived.append(exchange([pack(mode_fields, 0, 6, offset, group, groups) for offset in order[1:]], order[1:]))
+        arrived.append(exchange([pack(flow, 0, 6, offset, group, groups) for offset in order[1:]], order[1:]))
     parcels = [(0, 6, 0, group, groups) for group in range(groups)]
-    *own, inverse, forward = pack_rest(mode_fields, parcels, [inverse, forward])
+    *own, inverse, forward = pack_rest(flow, parcels, [inverse, forward])
     arrived[0][1:2], carried = lax.optimization_barrier((arrived[0][1:2], [inverse, forward]))
     order = offsets(count, SECOND)
     parcels = [(6, 12, offset, 0, 1) for offset in order]

time: 69 us -> 68.7 us (level)
  waiting for transfers between devices: 21.3 us -> 25.4 us
  starting transfers between devices: 31.4 us -> 27.6 us
  local copies, waits for them, and re-layouts: 1.93 us -> 0.04 us
  Pallas kernels: 13.4 us -> 14.8 us
    ppermute x18, waiting for transfers between devices: 17.6 us -> 21.6 us  [exchange(): received.append(lax.ppermute(piece, 'mode', pairs))]
    ppermute x18, starting transfers between devices: 28.8 us -> 25 us  [exchange(): received.append(lax.ppermute(piece, 'mode', pairs))]
    unnamed x18 -> x16, local copies, waits for them, and re-layouts: 1.93 us -> 0.04 us
    pallas_call x0 -> x1, Pallas kernels: none -> 1.4 us  [load(): pl.pallas_call(kernel, in_specs=[pl.BlockSpec(memory_space=pltpu.HBM)], o...]
  transfers between devices with their start and end apart: 20 -> 20, of which waited for: 11 -> 12; matrix products, arithmetic and copies ran while one was open for 0% -> 0% of each run, Pallas kernels for 15% -> 15%
where the time goes in v14:
time: 68.7 us; the launch traced here: 68.6 us
  starting transfers between devices  27.6 us (40%)
  waiting for transfers between devices  25.4 us (37%)
  Pallas kernels  14.8 us (22%)
  between operations  0.81 us (1%)
    ppermute x18, starting transfers between devices, exchange(): received.append(lax.ppermute(piece, 'mode', pairs))  25 us
    ppermute x18, waiting for transfers between devices, exchange(): received.append(lax.ppermute(piece, 'mode', pairs))  21.6 us
    pallas_call x1, Pallas kernels, derive(): pl.pallas_call(functools.partial(derive_kernel, count, len(received)), in...  5.02 us
    ppermute x2, waiting for transfers between devices, from_behind(): lax.ppermute(value, axis, [(source, source + steps) for source in range(i...  3.74 us
    ppermute x2, starting transfers between devices, from_behind(): lax.ppermute(value, axis, [(source, source + steps) for source in range(i...  2.59 us
    pallas_call x2, Pallas kernels, first_physics(): pl.pallas_call(functools.partial(first_kernel, count), in_specs=[vmem()]...  1.64 us
    pallas_call x2, Pallas kernels, pack_rest(): pl.pallas_call(kernel, in_specs=[pl.BlockSpec(memory_space=pl.ANY)] + [vm...  1.62 us
    pallas_call x1, Pallas kernels, second_physics(): pl.pallas_call(functools.partial(second_kernel, count, groups), in_specs=...  1.59 us
  transfers between devices with their start and end apart: 20, of which 12 were waited for; matrix products, arithmetic and copies ran while one was open for 0% of the time, Pallas kernels for 15%

profile of v14, /device:TPU:0, one launch (start us, length us, event | category | flops | bytes accessed | tf_op | source)
XLA Modules:
  0.0 68.6 jit_solution(8502631388665685902)
XLA Ops:
  0.6 1.4 %shard_map.95.fields_ref = bf16[6,32,2,2048]{3,2,1,0:T(2,128)(2,1)S(1)} custom-call(bf16[12,32,2,2048]{3,2,1,0:T(2,128)(2,1)} %fields_ref.3), custom_call_target="tpu_custom_call" | custom-call | flops 1024 | bytes 1024 | tf_op jit(solution)/shard_map/pallas_call | solution.py:119
  2.0 0.2 shard_map.102
  2.2 4.0 %collective-permute-start.6 = (bf16[6,2,32,2,128]{4,3,2,1,0:T(2,128)(2,1)S(1)}, bf16[6,2,32,2,128]{4,3,2,1,0:T(2,128)(2,1)S(1)}, u32[]{:S(2)}, u32[]{:S(2)}) collective-permute-start(bf16[6,2,32,2,128]{4,3,2,1,0:T(2,128)(2,1)S(1)} %shard_map.102), channel_id=1, source_target_pairs={{0,24},{8,16},{16,8},{24,0},{1,25},{9,17},{17,9},{25,1},{2,26},{10... | collective-permute-start | bytes 589832 | tf_op jit(solution)/shard_map/ppermute | solution.py:63
  6.2 0.2 shard_map.103
  6.3 0.6 collective-permute-start.7
  6.9 0.2 shard_map.104
  7.1 0.1 collective-permute-start.8
  7.2 0.2 shard_map.98
  7.4 0.0 copy-start.3
  7.4 2.0 %collective-permute-start.1 = (bf16[6,2,32,2,128]{4,3,2,1,0:T(2,128)(2,1)S(1)}, bf16[6,2,32,2,128]{4,3,2,1,0:T(2,128)(2,1)S(1)}, u32[]{:S(2)}, u32[]{:S(2)}) collective-permute-start(bf16[6,2,32,2,128]{4,3,2,1,0:T(2,128)(2,1)S(1)} %shard_map.98), channel_id=1, source_target_pairs={{0,8},{8,0},{16,24},{24,16},{1,9},{9,1},{17,25},{25,17},{2,10},{10... | collective-permute-start | bytes 589832 | tf_op jit(solution)/shard_map/ppermute | solution.py:63
  9.4 0.2 shard_map.97
  9.6 1.6 %collective-permute-start = (bf16[6,2,32,2,128]{4,3,2,1,0:T(2,128)(2,1)S(1)}, bf16[6,2,32,2,128]{4,3,2,1,0:T(2,128)(2,1)S(1)}, u32[]{:S(2)}, u32[]{:S(2)}) collective-permute-start(bf16[6,2,32,2,128]{4,3,2,1,0:T(2,128)(2,1)S(1)} %shard_map.97), channel_id=1, source_target_pairs={{0,24},{8,16},{16,8},{24,0},{1,25},{9,17},{17,9},{25,1},{2,26},{10... | collective-permute-start | bytes 589832 | tf_op jit(solution)/shard_map/ppermute | solution.py:63
  11.2 0.2 shard_map.99
  11.3 0.6 collective-permute-done.6
  11.9 2.1 %collective-permute-start.2 = (bf16[6,2,32,2,128]{4,3,2,1,0:T(2,128)(2,1)S(1)}, bf16[6,2,32,2,128]{4,3,2,1,0:T(2,128)(2,1)S(1)}, u32[]{:S(2)}, u32[]{:S(2)}) collective-permute-start(bf16[6,2,32,2,128]{4,3,2,1,0:T(2,128)(2,1)S(1)} %shard_map.99), channel_id=1, source_target_pairs={{0,16},{8,24},{16,0},{24,8},{1,17},{9,25},{17,1},{25,9},{2,18},{10... | collective-permute-start | bytes 589832 | tf_op jit(solution)/shard_map/ppermute | solution.py:63
  14.0 0.3 shard_map.96
  14.3 2.4 %collective-permute-done.7 = bf16[6,2,32,2,128]{4,3,2,1,0:T(2,128)(2,1)S(1)} collective-permute-done((bf16[6,2,32,2,128]{4,3,2,1,0:T(2,128)(2,1)S(1)}, bf16[6,2,32,2,128]{4,3,2,1,0:T(2,128)(2,1)S(1)}, u32[]{:S(2)}, u32[]{:S(2)}) %collective-permute-start.7) | collective-permute-done | bytes 196640 | tf_op jit(solution)/shard_map/ppermute | solution.py:63
  16.7 0.8 %shard_map.105 = (bf16[4,2,64,128]{3,2,1,0:T(8,128)(2,1)S(1)}, bf16[4,2,64,128]{3,2,1,0:T(8,128)(2,1)S(1)}, bf16[4,2,64,128]{3,2,1,0:T(8,128)(2,1)S(1)}, bf16[4,...) custom-call(bf16[6,2,64,128]{3,2,1,0:T(8,128)(2,1)S(1)} %bitcast.35, bf16[6,2,64,128]{3,2,1,0:T(8,128)(2,1)S(1)} %bitcast.32, ...), custom_call_target="tpu_custom_call" | custom-call | flops 1024 | bytes 1024 | tf_op jit(solution)/shard_map/pallas_call | solution.py:235
  17.6 1.4 %collective-permute-start.9 = (bf16[4,2,64,128]{3,2,1,0:T(8,128)(2,1)S(1)}, bf16[4,2,64,128]{3,2,1,0:T(8,128)(2,1)S(1)}, u32[]{:S(2)}, u32[]{:S(2)}) collective-permute-start(bf16[4,2,64,128]{3,2,1,0:T(8,128)(2,1)S(1)} %get-tuple-element.73), channel_id=1, source_target_pairs={{0,24},{8,16},{16,8},{24,0},{1,25},{9,17},{17,9},{25,1},{2,26},{10... | collective-permute-start | bytes 393224 | tf_op jit(solution)/shard_map/ppermute | solution.py:63
  19.0 1.9 %collective-permute-done.1 = bf16[6,2,32,2,128]{4,3,2,1,0:T(2,128)(2,1)S(1)} collective-permute-done((bf16[6,2,32,2,128]{4,3,2,1,0:T(2,128)(2,1)S(1)}, bf16[6,2,32,2,128]{4,3,2,1,0:T(2,128)(2,1)S(1)}, u32[]{:S(2)}, u32[]{:S(2)}) %collective-permute-start.1) | collective-permute-done | bytes 196640 | tf_op jit(solution)/shard_map/ppermute | solution.py:63
  20.9 1.5 %collective-permute-start.10 = (bf16[4,2,64,128]{3,2,1,0:T(8,128)(2,1)S(1)}, bf16[4,2,64,128]{3,2,1,0:T(8,128)(2,1)S(1)}, u32[]{:S(2)}, u32[]{:S(2)}) collective-permute-start(bf16[4,2,64,128]{3,2,1,0:T(8,128)(2,1)S(1)} %get-tuple-element.74), channel_id=1, source_target_pairs={{0,8},{8,0},{16,24},{24,16},{1,9},{9,1},{17,25},{25,17},{2,10},{10... | collective-permute-start | bytes 393224 | tf_op jit(solution)/shard_map/ppermute | solution.py:63
  22.4 0.5 collective-permute-start.11
  22.9 1.3 %shard_map.100 = (bf16[6,4,32,2,128]{4,3,2,1,0:T(2,128)(2,1)S(1)}, bf16[6,4,32,2,128]{4,3,2,1,0:T(2,128)(2,1)S(1)}, bf16[6,4,32,2,128]{4,3,2,1,0:T(2,128)(2,1)S(...) custom-call(bf16[12,32,2,2048]{3,2,1,0:T(2,128)(2,1)S(1)} %copy-done, ...), custom_call_target="tpu_custom_call" | custom-call | flops 1024 | bytes 1024 | tf_op jit(solution)/shard_map/pallas_call | solution.py:167
  24.2 0.4 collective-permute-done
  24.6 0.8 %shard_map.101 = (bf16[4,2,64,128]{3,2,1,0:T(8,128)(2,1)S(1)}, bf16[4,2,64,128]{3,2,1,0:T(8,128)(2,1)S(1)}, bf16[4,2,64,128]{3,2,1,0:T(8,128)(2,1)S(1)}, bf16[4,...) custom-call(bf16[6,2,64,128]{3,2,1,0:T(8,128)(2,1)S(1)} %bitcast.31, bf16[6,2,64,128]{3,2,1,0:T(8,128)(2,1)S(1)} %bitcast.29, ...), custom_call_target="tpu_custom_call" | custom-call | flops 1024 | bytes 1024 | tf_op jit(solution)/shard_map/pallas_call | solution.py:235
  25.5 3.1 %collective-permute-start.3 = (bf16[4,2,64,128]{3,2,1,0:T(8,128)(2,1)S(1)}, bf16[4,2,64,128]{3,2,1,0:T(8,128)(2,1)S(1)}, u32[]{:S(2)}, u32[]{:S(2)}) collective-permute-start(bf16[4,2,64,128]{3,2,1,0:T(8,128)(2,1)S(1)} %get-tuple-element.68), channel_id=1, source_target_pairs={{0,24},{8,16},{16,8},{24,0},{1,25},{9,17},{17,9},{25,1},{2,26},{10... | collective-permute-start | bytes 393224 | tf_op jit(solution)/shard_map/ppermute | solution.py:63
  28.5 0.5 collective-permute-start.4
  29.1 0.4 collective-permute-start.5
  29.5 1.3 %collective-permute-done.10.refs_6_ = bf16[4,2,64,128]{3,2,1,0:T(8,128)(2,1)S(1)} collective-permute-done((bf16[4,2,64,128]{3,2,1,0:T(8,128)(2,1)S(1)}, bf16[4,2,64,128]{3,2,1,0:T(8,128)(2,1)S(1)}, u32[]{:S(2)}, u32[]{:S(2)}) %collective-permute-start.10) | collective-permute-done | bytes 131104 | tf_op jit(solution)/shard_map/ppermute | solution.py:63
  30.8 0.7 %collective-permute-done.11.refs_7_ = bf16[4,2,64,128]{3,2,1,0:T(8,128)(2,1)S(1)} collective-permute-done((bf16[4,2,64,128]{3,2,1,0:T(8,128)(2,1)S(1)}, bf16[4,2,64,128]{3,2,1,0:T(8,128)(2,1)S(1)}, u32[]{:S(2)}, u32[]{:S(2)}) %collective-permute-start.11) | collective-permute-done | bytes 131104 | tf_op jit(solution)/shard_map/ppermute | solution.py:63
  31.6 0.8 %collective-permute-start.12 = (bf16[6,4,32,2,128]{4,3,2,1,0:T(2,128)(2,1)S(1)}, bf16[6,4,32,2,128]{4,3,2,1,0:T(2,128)(2,1)S(1)}, u32[]{:S(2)}, u32[]{:S(2)}) collective-permute-start(bf16[6,4,32,2,128]{4,3,2,1,0:T(2,128)(2,1)S(1)} %get-tuple-element.92), channel_id=1, source_target_pairs={{0,8},{8,0},{16,24},{24,16},{1,9},{9,1},{17,25},{25,17},{2,10},{10... | collective-permute-start | bytes 1179656 | tf_op jit(solution)/shard_map/ppermute | solution.py:63
  32.3 0.7 %collective-permute-done.3.refs_1_ = bf16[4,2,64,128]{3,2,1,0:T(8,128)(2,1)S(1)} collective-permute-done((bf16[4,2,64,128]{3,2,1,0:T(8,128)(2,1)S(1)}, bf16[4,2,64,128]{3,2,1,0:T(8,128)(2,1)S(1)}, u32[]{:S(2)}, u32[]{:S(2)}) %collective-permute-start.3) | collective-permute-done | bytes 131104 | tf_op jit(solution)/shard_map/ppermute | solution.py:63
  33.1 3.4 %collective-permute-done.4.refs_2_ = bf16[4,2,64,128]{3,2,1,0:T(8,128)(2,1)S(1)} collective-permute-done((bf16[4,2,64,128]{3,2,1,0:T(8,128)(2,1)S(1)}, bf16[4,2,64,128]{3,2,1,0:T(8,128)(2,1)S(1)}, u32[]{:S(2)}, u32[]{:S(2)}) %collective-permute-start.4) | collective-permute-done | bytes 131104 | tf_op jit(solution)/shard_map/ppermute | solution.py:63
  36.4 0.3 collective-permute-start.13
  36.7 2.7 %collective-permute-start.14 = (bf16[6,4,32,2,128]{4,3,2,1,0:T(2,128)(2,1)S(1)}, bf16[6,4,32,2,128]{4,3,2,1,0:T(2,128)(2,1)S(1)}, u32[]{:S(2)}, u32[]{:S(2)}) collective-permute-start(bf16[6,4,32,2,128]{4,3,2,1,0:T(2,128)(2,1)S(1)} %get-tuple-element.94), channel_id=1, source_target_pairs={{0,24},{8,16},{16,8},{24,0},{1,25},{9,17},{17,9},{25,1},{2,26},{10... | collective-permute-start | bytes 1179656 | tf_op jit(solution)/shard_map/ppermute | solution.py:63
  39.4 1.2 %shard_map.106 = (bf16[4,2,64,128]{3,2,1,0:T(8,128)(2,1)S(1)}, bf16[4,2,64,128]{3,2,1,0:T(8,128)(2,1)S(1)}) custom-call(bf16[4,2,64,128]{3,2,1,0:T(8,128)(2,1)S(1)} %get-tuple-element.83.refs_0_, bf16[4,2,64,128]{3,2,1,0:T(8,128)(2,1)S(1)} %collective-permute-done.3.refs_1_, bf16[4,2,64,128]{3,2,1,0:T(8,128)(2,1)S(1)} %collective-permute-done.4.refs_2_, ...), custom_call_target="tpu_custom_call" | custom-call | flops 1024 | bytes 1024 | tf_op jit(solution)/shard_map/pallas_call | solution.py:329
  40.6 1.3 %collective-permute-start.15 = (bf16[4,2,64,128]{3,2,1,0:T(8,128)(2,1)S(1)}, bf16[4,2,64,128]{3,2,1,0:T(8,128)(2,1)S(1)}, u32[]{:S(2)}, u32[]{:S(2)}) collective-permute-start(bf16[4,2,64,128]{3,2,1,0:T(8,128)(2,1)S(1)} %get-tuple-element.95), channel_id=1, source_target_pairs={{0,1},{1,2},{2,3},{3,4},{4,5},{5,6},{6,7},{8,9},{9,10},{10,11},{11... | collective-permute-start | bytes 393224 | tf_op jit(solution)/shard_map/ppermute | solution.py:70
  41.9 1.3 %collective-permute-start.16 = (bf16[4,2,64,128]{3,2,1,0:T(8,128)(2,1)S(1)}, bf16[4,2,64,128]{3,2,1,0:T(8,128)(2,1)S(1)}, u32[]{:S(2)}, u32[]{:S(2)}) collective-permute-start(bf16[4,2,64,128]{3,2,1,0:T(8,128)(2,1)S(1)} %get-tuple-element.96), channel_id=1, source_target_pairs={{1,0},{2,1},{3,2},{4,3},{5,4},{6,5},{7,6},{9,8},{10,9},{11,10},{12... | collective-permute-start | bytes 393224 | tf_op jit(solution)/shard_map/ppermute | solution.py:70
  43.3 3.7 %collective-permute-done.16.refs_9_ = bf16[4,2,64,128]{3,2,1,0:T(8,128)(2,1)S(1)} collective-permute-done((bf16[4,2,64,128]{3,2,1,0:T(8,128)(2,1)S(1)}, bf16[4,2,64,128]{3,2,1,0:T(8,128)(2,1)S(1)}, u32[]{:S(2)}, u32[]{:S(2)}) %collective-permute-start.16) | collective-permute-done | bytes 131104 | tf_op jit(solution)/shard_map/ppermute | solution.py:70
  47.0 7.3 %collective-permute-done.13 = bf16[6,4,32,2,128]{4,3,2,1,0:T(2,128)(2,1)S(1)} collective-permute-done((bf16[6,4,32,2,128]{4,3,2,1,0:T(2,128)(2,1)S(1)}, bf16[6,4,32,2,128]{4,3,2,1,0:T(2,128)(2,1)S(1)}, u32[]{:S(2)}, u32[]{:S(2)}) %collective-permute-start.13) | collective-permute-done | bytes 393248 | tf_op jit(solution)/shard_map/ppermute | solution.py:63
  54.3 1.6 %shard_map.107 = (bf16[3,4,64,128]{3,2,1,0:T(8,128)(2,1)S(1)}, bf16[3,4,64,128]{3,2,1,0:T(8,128)(2,1)S(1)}, bf16[3,4,64,128]{3,2,1,0:T(8,128)(2,1)S(1)}, bf16[3,4,64,128]{3,2,1,0:T(8,128)(2,1)S(1)}) custom-call(bf16[6,4,64,128]{3,2,1,0:T(8,128)(2,1)S(1)} %bitcast.24, bf16[6,4,64,128]{3,2,1,0:T(8,128)(2,1)S(1)} %bitcast.25, ...), custom_call_target="tpu_custom_call" | custom-call | flops 1024 | bytes 1024 | tf_op jit(solution)/shard_map/pallas_call | solution.py:279
  55.9 1.4 %collective-permute-start.17 = (bf16[3,4,64,128]{3,2,1,0:T(8,128)(2,1)S(1)}, bf16[3,4,64,128]{3,2,1,0:T(8,128)(2,1)S(1)}, u32[]{:S(2)}, u32[]{:S(2)}) collective-permute-start(bf16[3,4,64,128]{3,2,1,0:T(8,128)(2,1)S(1)} %get-tuple-element.112), channel_id=1, source_target_pairs={{0,8},{8,0},{16,24},{24,16},{1,9},{9,1},{17,25},{25,17},{2,10},{10... | collective-permute-start | bytes 589832 | tf_op jit(solution)/shard_map/ppermute | solution.py:63
  57.4 1.7 %collective-permute-start.18 = (bf16[3,4,64,128]{3,2,1,0:T(8,128)(2,1)S(1)}, bf16[3,4,64,128]{3,2,1,0:T(8,128)(2,1)S(1)}, u32[]{:S(2)}, u32[]{:S(2)}) collective-permute-start(bf16[3,4,64,128]{3,2,1,0:T(8,128)(2,1)S(1)} %get-tuple-element.113), channel_id=1, source_target_pairs={{0,16},{8,24},{16,0},{24,8},{1,17},{9,25},{17,1},{25,9},{2,18},{10... | collective-permute-start | bytes 589832 | tf_op jit(solution)/shard_map/ppermute | solution.py:63
  59.1 0.4 collective-permute-start.19
  59.5 5.0 %shard_map.108 = (f32[3072,128]{1,0:T(8,128)}, f32[3,16,64,128]{3,2,1,0:T(8,128)S(1)}) custom-call(bf16[4,2,64,128]{3,2,1,0:T(8,128)(2,1)S(1)} %get-tuple-element.83.refs_0_, bf16[4,2,64,128]{3,2,1,0:T(8,128)(2,1)S(1)} %collective-permute-done.3.refs_1_, bf16[4,2,64,128]{3,2,1,0:T(8,128)(2,1)S(1)} %collective-permute-done.4.refs_2_, ...), custom_call_target="tpu_custom_call" | custom-call | flops 1024 | bytes 1024 | tf_op jit(solution)/shard_map/pallas_call | solution.py:441
  64.5 1.5 %collective-permute-done.18.refs_2_ = bf16[3,4,64,128]{3,2,1,0:T(8,128)(2,1)S(1)} collective-permute-done((bf16[3,4,64,128]{3,2,1,0:T(8,128)(2,1)S(1)}, bf16[3,4,64,128]{3,2,1,0:T(8,128)(2,1)S(1)}, u32[]{:S(2)}, u32[]{:S(2)}) %collective-permute-start.18) | collective-permute-done | bytes 196640 | tf_op jit(solution)/shard_map/ppermute | solution.py:63
  66.0 1.2 %collective-permute-done.19.refs_3_ = bf16[3,4,64,128]{3,2,1,0:T(8,128)(2,1)S(1)} collective-permute-done((bf16[3,4,64,128]{3,2,1,0:T(8,128)(2,1)S(1)}, bf16[3,4,64,128]{3,2,1,0:T(8,128)(2,1)S(1)}, u32[]{:S(2)}, u32[]{:S(2)}) %collective-permute-start.19) | collective-permute-done | bytes 196640 | tf_op jit(solution)/shard_map/ppermute | solution.py:63
  67.2 1.3 %shard_map.109 = f32[3072,128]{1,0:T(8,128)} custom-call(bf16[3,4,64,128]{3,2,1,0:T(8,128)(2,1)S(1)} %get-tuple-element.111.refs_0_, bf16[3,4,64,128]{3,2,1,0:T(8,128)(2,1)S(1)} %collective-permute-done.17.refs_1_, bf16[3,4,64,128]{3,2,1,0:T(8,128)(2,1)S(1)} %collective-permute-done.18.refs_2_, bf16[3,4,64,128]{3,2,1,0:T(8,128)(2,1)S(1)} %collective-permute-done.19.refs_3_, ...), custom_call_target="tpu_custom_call" | custom-call | flops 1024 | bytes 1024 | tf_op jit(solution)/shard_map/pallas_call | solution.py:483
  (23 shorter events, 0.1 us)
Async XLA Ops:
  2.2 9.7 %collective-permute-start.6 = (bf16[6,2,32,2,128]{4,3,2,1,0:T(2,128)(2,1)S(1)}, bf16[6,2,32,2,128]{4,3,2,1,0:T(2,128)(2,1)S(1)}, u32[]{:S(2)}, u32[]{:S(2)}) collective-permute-start(bf16[6,2,32,2,128]{4,3,2,1,0:T(2,128)(2,1)S(1)} %shard_map.102), channel_id=1, source_target_pairs={{0,24},{8,16},{16,8},{24,0},{1,25},{9,17},{17,9},{25,1},{2,26},{10... | collective-permute-start | bytes 589832 | tf_op jit(solution)/shard_map/ppermute | solution.py:63
  6.3 10.4 %collective-permute-start.7 = (bf16[6,2,32,2,128]{4,3,2,1,0:T(2,128)(2,1)S(1)}, bf16[6,2,32,2,128]{4,3,2,1,0:T(2,128)(2,1)S(1)}, u32[]{:S(2)}, u32[]{:S(2)}) collective-permute-start(bf16[6,2,32,2,128]{4,3,2,1,0:T(2,128)(2,1)S(1)} %shard_map.103), channel_id=1, source_target_pairs={{0,8},{8,0},{16,24},{24,16},{1,9},{9,1},{17,25},{25,17},{2,10},{10... | collective-permute-start | bytes 589832 | tf_op jit(solution)/shard_map/ppermute | solution.py:63
  7.1 9.6 %collective-permute-start.8 = (bf16[6,2,32,2,128]{4,3,2,1,0:T(2,128)(2,1)S(1)}, bf16[6,2,32,2,128]{4,3,2,1,0:T(2,128)(2,1)S(1)}, u32[]{:S(2)}, u32[]{:S(2)}) collective-permute-start(bf16[6,2,32,2,128]{4,3,2,1,0:T(2,128)(2,1)S(1)} %shard_map.104), channel_id=1, source_target_pairs={{0,16},{8,24},{16,0},{24,8},{1,17},{9,25},{17,1},{25,9},{2,18},{10... | collective-permute-start | bytes 589832 | tf_op jit(solution)/shard_map/ppermute | solution.py:63
  7.4 6.6 %copy-start.3 = (bf16[256,256]{1,0:T(8,128)(2,1)S(1)}, bf16[256,256]{1,0:T(8,128)(2,1)}, u32[]{:S(2)}) copy-start(bf16[256,256]{1,0:T(8,128)(2,1)} %constant.5.clone.refs_1_) | copy-start | bytes 393220
  7.4 6.6 %copy-start.4 = (bf16[256,256]{1,0:T(8,128)(2,1)S(1)}, bf16[256,256]{1,0:T(8,128)(2,1)}, u32[]{:S(2)}) copy-start(bf16[256,256]{1,0:T(8,128)(2,1)} %constant.4.clone.refs_0_) | copy-start | bytes 393220
  7.4 13.5 %collective-permute-start.1 = (bf16[6,2,32,2,128]{4,3,2,1,0:T(2,128)(2,1)S(1)}, bf16[6,2,32,2,128]{4,3,2,1,0:T(2,128)(2,1)S(1)}, u32[]{:S(2)}, u32[]{:S(2)}) collective-permute-start(bf16[6,2,32,2,128]{4,3,2,1,0:T(2,128)(2,1)S(1)} %shard_map.98), channel_id=1, source_target_pairs={{0,8},{8,0},{16,24},{24,16},{1,9},{9,1},{17,25},{25,17},{2,10},{10... | collective-permute-start | bytes 589832 | tf_op jit(solution)/shard_map/ppermute | solution.py:63
  9.6 15.1 %collective-permute-start = (bf16[6,2,32,2,128]{4,3,2,1,0:T(2,128)(2,1)S(1)}, bf16[6,2,32,2,128]{4,3,2,1,0:T(2,128)(2,1)S(1)}, u32[]{:S(2)}, u32[]{:S(2)}) collective-permute-start(bf16[6,2,32,2,128]{4,3,2,1,0:T(2,128)(2,1)S(1)} %shard_map.97), channel_id=1, source_target_pairs={{0,24},{8,16},{16,8},{24,0},{1,25},{9,17},{17,9},{25,1},{2,26},{10... | collective-permute-start | bytes 589832 | tf_op jit(solution)/shard_map/ppermute | solution.py:63
  11.2 11.8 %copy-start = (bf16[12,32,2,2048]{3,2,1,0:T(2,128)(2,1)S(1)}, bf16[12,32,2,2048]{3,2,1,0:T(2,128)(2,1)}, u32[]{:S(2)}) copy-start(bf16[12,32,2,2048]{3,2,1,0:T(2,128)(2,1)} %fields_ref.3) | copy-start | bytes 9437188
  11.9 12.7 %collective-permute-start.2 = (bf16[6,2,32,2,128]{4,3,2,1,0:T(2,128)(2,1)S(1)}, bf16[6,2,32,2,128]{4,3,2,1,0:T(2,128)(2,1)S(1)}, u32[]{:S(2)}, u32[]{:S(2)}) collective-permute-start(bf16[6,2,32,2,128]{4,3,2,1,0:T(2,128)(2,1)S(1)} %shard_map.99), channel_id=1, source_target_pairs={{0,16},{8,24},{16,0},{24,8},{1,17},{9,25},{17,1},{25,9},{2,18},{10... | collective-permute-start | bytes 589832 | tf_op jit(solution)/shard_map/ppermute | solution.py:63
  17.6 11.5 %collective-permute-start.9 = (bf16[4,2,64,128]{3,2,1,0:T(8,128)(2,1)S(1)}, bf16[4,2,64,128]{3,2,1,0:T(8,128)(2,1)S(1)}, u32[]{:S(2)}, u32[]{:S(2)}) collective-permute-start(bf16[4,2,64,128]{3,2,1,0:T(8,128)(2,1)S(1)} %get-tuple-element.73), channel_id=1, source_target_pairs={{0,24},{8,16},{16,8},{24,0},{1,25},{9,17},{17,9},{25,1},{2,26},{10... | collective-permute-start | bytes 393224 | tf_op jit(solution)/shard_map/ppermute | solution.py:63
  20.9 9.9 %collective-permute-start.10 = (bf16[4,2,64,128]{3,2,1,0:T(8,128)(2,1)S(1)}, bf16[4,2,64,128]{3,2,1,0:T(8,128)(2,1)S(1)}, u32[]{:S(2)}, u32[]{:S(2)}) collective-permute-start(bf16[4,2,64,128]{3,2,1,0:T(8,128)(2,1)S(1)} %get-tuple-element.74), channel_id=1, source_target_pairs={{0,8},{8,0},{16,24},{24,16},{1,9},{9,1},{17,25},{25,17},{2,10},{10... | collective-permute-start | bytes 393224 | tf_op jit(solution)/shard_map/ppermute | solution.py:63
  22.4 17.0 %copy-start.7 = (s32[2,256]{1,0:T(2,128)S(1)}, s32[2,256]{1,0:T(2,128)}, u32[]{:S(2)}) copy-start(s32[2,256]{1,0:T(2,128)} %refs_8_.1) | copy-start | bytes 6148
  22.4 9.1 %collective-permute-start.11 = (bf16[4,2,64,128]{3,2,1,0:T(8,128)(2,1)S(1)}, bf16[4,2,64,128]{3,2,1,0:T(8,128)(2,1)S(1)}, u32[]{:S(2)}, u32[]{:S(2)}) collective-permute-start(bf16[4,2,64,128]{3,2,1,0:T(8,128)(2,1)S(1)} %get-tuple-element.75), channel_id=1, source_target_pairs={{0,16},{8,24},{16,0},{24,8},{1,17},{9,25},{17,1},{25,9},{2,18},{10... | collective-permute-start | bytes 393224 | tf_op jit(solution)/shard_map/ppermute | solution.py:63
  25.5 7.6 %collective-permute-start.3 = (bf16[4,2,64,128]{3,2,1,0:T(8,128)(2,1)S(1)}, bf16[4,2,64,128]{3,2,1,0:T(8,128)(2,1)S(1)}, u32[]{:S(2)}, u32[]{:S(2)}) collective-permute-start(bf16[4,2,64,128]{3,2,1,0:T(8,128)(2,1)S(1)} %get-tuple-element.68), channel_id=1, source_target_pairs={{0,24},{8,16},{16,8},{24,0},{1,25},{9,17},{17,9},{25,1},{2,26},{10... | collective-permute-start | bytes 393224 | tf_op jit(solution)/shard_map/ppermute | solution.py:63
  28.5 7.9 %collective-permute-start.4 = (bf16[4,2,64,128]{3,2,1,0:T(8,128)(2,1)S(1)}, bf16[4,2,64,128]{3,2,1,0:T(8,128)(2,1)S(1)}, u32[]{:S(2)}, u32[]{:S(2)}) collective-permute-start(bf16[4,2,64,128]{3,2,1,0:T(8,128)(2,1)S(1)} %get-tuple-element.69), channel_id=1, source_target_pairs={{0,8},{8,0},{16,24},{24,16},{1,9},{9,1},{17,25},{25,17},{2,10},{10... | collective-permute-start | bytes 393224 | tf_op jit(solution)/shard_map/ppermute | solution.py:63
  29.1 7.4 %collective-permute-start.5 = (bf16[4,2,64,128]{3,2,1,0:T(8,128)(2,1)S(1)}, bf16[4,2,64,128]{3,2,1,0:T(8,128)(2,1)S(1)}, u32[]{:S(2)}, u32[]{:S(2)}) collective-permute-start(bf16[4,2,64,128]{3,2,1,0:T(8,128)(2,1)S(1)} %get-tuple-element.70), channel_id=1, source_target_pairs={{0,16},{8,24},{16,0},{24,8},{1,17},{9,25},{17,1},{25,9},{2,18},{10... | collective-permute-start | bytes 393224 | tf_op jit(solution)/shard_map/ppermute | solution.py:63
  31.6 15.4 %collective-permute-start.12 = (bf16[6,4,32,2,128]{4,3,2,1,0:T(2,128)(2,1)S(1)}, bf16[6,4,32,2,128]{4,3,2,1,0:T(2,128)(2,1)S(1)}, u32[]{:S(2)}, u32[]{:S(2)}) collective-permute-start(bf16[6,4,32,2,128]{4,3,2,1,0:T(2,128)(2,1)S(1)} %get-tuple-element.92), channel_id=1, source_target_pairs={{0,8},{8,0},{16,24},{24,16},{1,9},{9,1},{17,25},{25,17},{2,10},{10... | collective-permute-start | bytes 1179656 | tf_op jit(solution)/shard_map/ppermute | solution.py:63
  36.4 17.9 %collective-permute-start.13 = (bf16[6,4,32,2,128]{4,3,2,1,0:T(2,128)(2,1)S(1)}, bf16[6,4,32,2,128]{4,3,2,1,0:T(2,128)(2,1)S(1)}, u32[]{:S(2)}, u32[]{:S(2)}) collective-permute-start(bf16[6,4,32,2,128]{4,3,2,1,0:T(2,128)(2,1)S(1)} %get-tuple-element.93), channel_id=1, source_target_pairs={{0,16},{8,24},{16,0},{24,8},{1,17},{9,25},{17,1},{25,9},{2,18},{10... | collective-permute-start | bytes 1179656 | tf_op jit(solution)/shard_map/ppermute | solution.py:63
  36.7 17.6 %collective-permute-start.14 = (bf16[6,4,32,2,128]{4,3,2,1,0:T(2,128)(2,1)S(1)}, bf16[6,4,32,2,128]{4,3,2,1,0:T(2,128)(2,1)S(1)}, u32[]{:S(2)}, u32[]{:S(2)}) collective-permute-start(bf16[6,4,32,2,128]{4,3,2,1,0:T(2,128)(2,1)S(1)} %get-tuple-element.94), channel_id=1, source_target_pairs={{0,24},{8,16},{16,8},{24,0},{1,25},{9,17},{17,9},{25,1},{2,26},{10... | collective-permute-start | bytes 1179656 | tf_op jit(solution)/shard_map/ppermute | solution.py:63
  40.6 2.6 %collective-permute-start.15 = (bf16[4,2,64,128]{3,2,1,0:T(8,128)(2,1)S(1)}, bf16[4,2,64,128]{3,2,1,0:T(8,128)(2,1)S(1)}, u32[]{:S(2)}, u32[]{:S(2)}) collective-permute-start(bf16[4,2,64,128]{3,2,1,0:T(8,128)(2,1)S(1)} %get-tuple-element.95), channel_id=1, source_target_pairs={{0,1},{1,2},{2,3},{3,4},{4,5},{5,6},{6,7},{8,9},{9,10},{10,11},{11... | collective-permute-start | bytes 393224 | tf_op jit(solution)/shard_map/ppermute | solution.py:70
  41.9 5.0 %collective-permute-start.16 = (bf16[4,2,64,128]{3,2,1,0:T(8,128)(2,1)S(1)}, bf16[4,2,64,128]{3,2,1,0:T(8,128)(2,1)S(1)}, u32[]{:S(2)}, u32[]{:S(2)}) collective-permute-start(bf16[4,2,64,128]{3,2,1,0:T(8,128)(2,1)S(1)} %get-tuple-element.96), channel_id=1, source_target_pairs={{1,0},{2,1},{3,2},{4,3},{5,4},{6,5},{7,6},{9,8},{10,9},{11,10},{12... | collective-permute-start | bytes 393224 | tf_op jit(solution)/shard_map/ppermute | solution.py:70
  54.3 5.2 %copy-start.1 = (bf16[5,64,2048]{2,1,0:T(8,128)(2,1)S(1)}, bf16[5,64,2048]{2,1,0:T(8,128)(2,1)}, u32[]{:S(2)}) copy-start(bf16[5,64,2048]{2,1,0:T(8,128)(2,1)} %refs_10_.1) | copy-start | bytes 3932164
  54.3 5.2 %copy-start.2 = (bf16[5,64,2048]{2,1,0:T(8,128)(2,1)S(1)}, bf16[5,64,2048]{2,1,0:T(8,128)(2,1)}, u32[]{:S(2)}) copy-start(bf16[5,64,2048]{2,1,0:T(8,128)(2,1)} %refs_11_.1) | copy-start | bytes 3932164
  54.3 5.2 %copy-start.5 = (f32[2048]{0:T(1024)S(1)}, f32[2048]{0:T(1024)}, u32[]{:S(2)}) copy-start(f32[2048]{0:T(1024)} %param.9) | copy-start | bytes 24580
  54.3 5.2 %copy-start.6 = (s32[32,5]{0,1:T(8,128)S(1)}, s32[32,5]{0,1:T(8,128)}, u32[]{:S(2)}) copy-start(s32[32,5]{0,1:T(8,128)} %param.12) | copy-start | bytes 1924
  55.9 8.6 %collective-permute-start.17 = (bf16[3,4,64,128]{3,2,1,0:T(8,128)(2,1)S(1)}, bf16[3,4,64,128]{3,2,1,0:T(8,128)(2,1)S(1)}, u32[]{:S(2)}, u32[]{:S(2)}) collective-permute-start(bf16[3,4,64,128]{3,2,1,0:T(8,128)(2,1)S(1)} %get-tuple-element.112), channel_id=1, source_target_pairs={{0,8},{8,0},{16,24},{24,16},{1,9},{9,1},{17,25},{25,17},{2,10},{10... | collective-permute-start | bytes 589832 | tf_op jit(solution)/shard_map/ppermute | solution.py:63
  57.4 8.7 %collective-permute-start.18 = (bf16[3,4,64,128]{3,2,1,0:T(8,128)(2,1)S(1)}, bf16[3,4,64,128]{3,2,1,0:T(8,128)(2,1)S(1)}, u32[]{:S(2)}, u32[]{:S(2)}) collective-permute-start(bf16[3,4,64,128]{3,2,1,0:T(8,128)(2,1)S(1)} %get-tuple-element.113), channel_id=1, source_target_pairs={{0,16},{8,24},{16,0},{24,8},{1,17},{9,25},{17,1},{25,9},{2,18},{10... | collective-permute-start | bytes 589832 | tf_op jit(solution)/shard_map/ppermute | solution.py:63
  59.1 8.1 %collective-permute-start.19 = (bf16[3,4,64,128]{3,2,1,0:T(8,128)(2,1)S(1)}, bf16[3,4,64,128]{3,2,1,0:T(8,128)(2,1)S(1)}, u32[]{:S(2)}, u32[]{:S(2)}) collective-permute-start(bf16[3,4,64,128]{3,2,1,0:T(8,128)(2,1)S(1)} %get-tuple-element.114), channel_id=1, source_target_pairs={{0,24},{8,16},{16,8},{24,0},{1,25},{9,17},{17,9},{25,1},{2,26},{10... | collective-permute-start | bytes 589832 | tf_op jit(solution)/shard_map/ppermute | solution.py:63

commit v15 on v14

--- a/solution.py
+++ b/solution.py
@@ -30,7 +30,7 @@
     return pl.CostEstimate(flops=1024, bytes_accessed=1024, transcendentals=0)
 
 
-FIRST_SEND, FIRST_RETURN, SECOND = 1, 1, None
+FIRST_SEND, FIRST_RETURN, SECOND_SEND, SECOND_RETURN = 1, 1, 1, None
 
 
 def offsets(count, place):
@@ -257,7 +257,7 @@
     def store(c, value):
         physical_ref[c] = value
 
-    to_physical(offsets(count, SECOND), in_refs, inverse_ref[...], x_ref, store)
+    to_physical(offsets(count, SECOND_SEND), in_refs, inverse_ref[...], x_ref, store)
     for group in range(groups):
         lanes = slice(group * width, (group + 1) * width)
         for i in range(THETA // CHUNK):
@@ -269,7 +269,7 @@
             lorentz = [a + b for a, b in zip(cross(current, magnetic), cross(velocity, vorticity))]
             for c, value in enumerate(lorentz):
                 product_ref[c, at, lanes] = value.astype(jnp.bfloat16)
-    to_modes(offsets(count, SECOND), forward_ref, table_ref, product_ref, out_refs)
+    to_modes(offsets(count, SECOND_RETURN), forward_ref, table_ref, product_ref, out_refs)
 
 
 def second_physics(received, physical, inverse, forward):
@@ -462,7 +462,7 @@
     out_rows = mode_count * stride
     copies = []
     for c in range(components):
-        for step, offset in enumerate(offsets(count, SECOND)):
+        for step, offset in enumerate(offsets(count, SECOND_RETURN)):
             share = source_of(me, offset, count)
             for start in range(0, tiles, SUBLANES // 2):
                 values = []
@@ -515,7 +515,7 @@
     parcels = [(0, 6, 0, group, groups) for group in range(groups)]
     *own, inverse, forward = pack_rest(flow, parcels, [inverse, forward])
     arrived[0][1:2], carried = lax.optimization_barrier((arrived[0][1:2], [inverse, forward]))
-    order = offsets(count, SECOND)
+    order = offsets(count, SECOND_SEND)
     parcels = [(6, 12, offset, 0, 1) for offset in order]
     *shares, later_inverse, later_forward = pack_rest(mode_fields, parcels, carried)
     local, physical = [], []
@@ -536,7 +536,7 @@
     sources, halos = lax.optimization_barrier((sources, halos))
     lorentz = list(second_physics(joined(sources), physical, later_inverse, later_forward))
     lorentz, radius = lax.optimization_barrier((lorentz, radius))
-    lorentz = exchange(lorentz, order)
+    lorentz = exchange(lorentz, offsets(count, SECOND_RETURN))
     induction, gradient = derive(
         local, *halos, radial_blocks, axial_blocks, radius.reshape(1, width), block_columns.T, count
     )

time: 68.7 us -> 67.5 us (0.983)
  waiting for transfers between devices: 25.4 us -> 23.2 us
  starting transfers between devices: 27.6 us -> 28.4 us
    ppermute x18, waiting for transfers between devices: 21.6 us -> 19.5 us  [exchange(): received.append(lax.ppermute(piece, 'mode', pairs))]
    ppermute x18, starting transfers between devices: 25 us -> 25.8 us  [exchange(): received.append(lax.ppermute(piece, 'mode', pairs))]
  transfers between devices with their start and end apart: 20 -> 20, of which waited for: 12 -> 10; matrix products, arithmetic and copies ran while one was open for 0% -> 0% of each run, Pallas kernels for 15% -> 15%
where the time goes in v15:
time: 67.5 us; the launch traced here: 67.3 us
  starting transfers between devices  28.4 us (42%)
  waiting for transfers between devices  23.2 us (34%)
  Pallas kernels  14.8 us (22%)
  between operations  0.81 us (1%)
    ppermute x18, starting transfers between devices, exchange(): received.append(lax.ppermute(piece, 'mode', pairs))  25.8 us
    ppermute x18, waiting for transfers between devices, exchange(): received.append(lax.ppermute(piece, 'mode', pairs))  19.5 us
    pallas_call x1, Pallas kernels, derive(): pl.pallas_call(functools.partial(derive_kernel, count, len(received)), in...  5.02 us
    ppermute x2, waiting for transfers between devices, from_behind(): lax.ppermute(value, axis, [(source, source + steps) for source in range(i...  3.74 us
    ppermute x2, starting transfers between devices, from_behind(): lax.ppermute(value, axis, [(source, source + steps) for source in range(i...  2.59 us
    pallas_call x2, Pallas kernels, first_physics(): pl.pallas_call(functools.partial(first_kernel, count), in_specs=[vmem()]...  1.64 us
    pallas_call x2, Pallas kernels, pack_rest(): pl.pallas_call(kernel, in_specs=[pl.BlockSpec(memory_space=pl.ANY)] + [vm...  1.62 us
    pallas_call x1, Pallas kernels, second_physics(): pl.pallas_call(functools.partial(second_kernel, count, groups), in_specs=...  1.59 us
  transfers between devices with their start and end apart: 20, of which 10 were waited for; matrix products, arithmetic and copies ran while one was open for 0% of the time, Pallas kernels for 15%

profile of v15, /device:TPU:0, one launch (start us, length us, event | category | flops | bytes accessed | tf_op | source)
XLA Modules:
  0.0 67.3 jit_solution(2256838505856817507)
XLA Ops:
  0.6 1.4 %shard_map.95.fields_ref = bf16[6,32,2,2048]{3,2,1,0:T(2,128)(2,1)S(1)} custom-call(bf16[12,32,2,2048]{3,2,1,0:T(2,128)(2,1)} %fields_ref.3), custom_call_target="tpu_custom_call" | custom-call | flops 1024 | bytes 1024 | tf_op jit(solution)/shard_map/pallas_call | solution.py:119
  2.0 0.2 shard_map.102
  2.2 4.0 %collective-permute-start.6 = (bf16[6,2,32,2,128]{4,3,2,1,0:T(2,128)(2,1)S(1)}, bf16[6,2,32,2,128]{4,3,2,1,0:T(2,128)(2,1)S(1)}, u32[]{:S(2)}, u32[]{:S(2)}) collective-permute-start(bf16[6,2,32,2,128]{4,3,2,1,0:T(2,128)(2,1)S(1)} %shard_map.102), channel_id=1, source_target_pairs={{0,24},{8,16},{16,8},{24,0},{1,25},{9,17},{17,9},{25,1},{2,26},{10... | collective-permute-start | bytes 589832 | tf_op jit(solution)/shard_map/ppermute | solution.py:63
  6.2 0.2 shard_map.103
  6.3 0.6 collective-permute-start.7
  6.9 0.2 shard_map.104
  7.1 0.1 collective-permute-start.8
  7.2 0.2 shard_map.98
  7.4 0.0 copy-start.3
  7.4 0.0 copy-start.4
  7.4 2.0 %collective-permute-start.1 = (bf16[6,2,32,2,128]{4,3,2,1,0:T(2,128)(2,1)S(1)}, bf16[6,2,32,2,128]{4,3,2,1,0:T(2,128)(2,1)S(1)}, u32[]{:S(2)}, u32[]{:S(2)}) collective-permute-start(bf16[6,2,32,2,128]{4,3,2,1,0:T(2,128)(2,1)S(1)} %shard_map.98), channel_id=1, source_target_pairs={{0,8},{8,0},{16,24},{24,16},{1,9},{9,1},{17,25},{25,17},{2,10},{10... | collective-permute-start | bytes 589832 | tf_op jit(solution)/shard_map/ppermute | solution.py:63
  9.4 0.2 shard_map.97
  9.6 1.6 %collective-permute-start = (bf16[6,2,32,2,128]{4,3,2,1,0:T(2,128)(2,1)S(1)}, bf16[6,2,32,2,128]{4,3,2,1,0:T(2,128)(2,1)S(1)}, u32[]{:S(2)}, u32[]{:S(2)}) collective-permute-start(bf16[6,2,32,2,128]{4,3,2,1,0:T(2,128)(2,1)S(1)} %shard_map.97), channel_id=1, source_target_pairs={{0,24},{8,16},{16,8},{24,0},{1,25},{9,17},{17,9},{25,1},{2,26},{10... | collective-permute-start | bytes 589832 | tf_op jit(solution)/shard_map/ppermute | solution.py:63
  11.2 0.2 shard_map.99
  11.3 0.6 collective-permute-done.6
  11.9 2.1 %collective-permute-start.2 = (bf16[6,2,32,2,128]{4,3,2,1,0:T(2,128)(2,1)S(1)}, bf16[6,2,32,2,128]{4,3,2,1,0:T(2,128)(2,1)S(1)}, u32[]{:S(2)}, u32[]{:S(2)}) collective-permute-start(bf16[6,2,32,2,128]{4,3,2,1,0:T(2,128)(2,1)S(1)} %shard_map.99), channel_id=1, source_target_pairs={{0,16},{8,24},{16,0},{24,8},{1,17},{9,25},{17,1},{25,9},{2,18},{10... | collective-permute-start | bytes 589832 | tf_op jit(solution)/shard_map/ppermute | solution.py:63
  14.0 0.3 shard_map.96
  14.3 2.4 %collective-permute-done.7 = bf16[6,2,32,2,128]{4,3,2,1,0:T(2,128)(2,1)S(1)} collective-permute-done((bf16[6,2,32,2,128]{4,3,2,1,0:T(2,128)(2,1)S(1)}, bf16[6,2,32,2,128]{4,3,2,1,0:T(2,128)(2,1)S(1)}, u32[]{:S(2)}, u32[]{:S(2)}) %collective-permute-start.7) | collective-permute-done | bytes 196640 | tf_op jit(solution)/shard_map/ppermute | solution.py:63
  16.7 0.8 %shard_map.105 = (bf16[4,2,64,128]{3,2,1,0:T(8,128)(2,1)S(1)}, bf16[4,2,64,128]{3,2,1,0:T(8,128)(2,1)S(1)}, bf16[4,2,64,128]{3,2,1,0:T(8,128)(2,1)S(1)}, bf16[4,...) custom-call(bf16[6,2,64,128]{3,2,1,0:T(8,128)(2,1)S(1)} %bitcast.35, bf16[6,2,64,128]{3,2,1,0:T(8,128)(2,1)S(1)} %bitcast.32, ...), custom_call_target="tpu_custom_call" | custom-call | flops 1024 | bytes 1024 | tf_op jit(solution)/shard_map/pallas_call | solution.py:235
  17.6 1.4 %collective-permute-start.9 = (bf16[4,2,64,128]{3,2,1,0:T(8,128)(2,1)S(1)}, bf16[4,2,64,128]{3,2,1,0:T(8,128)(2,1)S(1)}, u32[]{:S(2)}, u32[]{:S(2)}) collective-permute-start(bf16[4,2,64,128]{3,2,1,0:T(8,128)(2,1)S(1)} %get-tuple-element.73), channel_id=1, source_target_pairs={{0,24},{8,16},{16,8},{24,0},{1,25},{9,17},{17,9},{25,1},{2,26},{10... | collective-permute-start | bytes 393224 | tf_op jit(solution)/shard_map/ppermute | solution.py:63
  19.0 1.9 %collective-permute-done.1 = bf16[6,2,32,2,128]{4,3,2,1,0:T(2,128)(2,1)S(1)} collective-permute-done((bf16[6,2,32,2,128]{4,3,2,1,0:T(2,128)(2,1)S(1)}, bf16[6,2,32,2,128]{4,3,2,1,0:T(2,128)(2,1)S(1)}, u32[]{:S(2)}, u32[]{:S(2)}) %collective-permute-start.1) | collective-permute-done | bytes 196640 | tf_op jit(solution)/shard_map/ppermute | solution.py:63
  20.9 1.5 %collective-permute-start.10 = (bf16[4,2,64,128]{3,2,1,0:T(8,128)(2,1)S(1)}, bf16[4,2,64,128]{3,2,1,0:T(8,128)(2,1)S(1)}, u32[]{:S(2)}, u32[]{:S(2)}) collective-permute-start(bf16[4,2,64,128]{3,2,1,0:T(8,128)(2,1)S(1)} %get-tuple-element.74), channel_id=1, source_target_pairs={{0,8},{8,0},{16,24},{24,16},{1,9},{9,1},{17,25},{25,17},{2,10},{10... | collective-permute-start | bytes 393224 | tf_op jit(solution)/shard_map/ppermute | solution.py:63
  22.4 0.5 collective-permute-start.11
  22.9 1.3 %shard_map.100 = (bf16[6,4,32,2,128]{4,3,2,1,0:T(2,128)(2,1)S(1)}, bf16[6,4,32,2,128]{4,3,2,1,0:T(2,128)(2,1)S(1)}, bf16[6,4,32,2,128]{4,3,2,1,0:T(2,128)(2,1)S(...) custom-call(bf16[12,32,2,2048]{3,2,1,0:T(2,128)(2,1)S(1)} %copy-done, ...), custom_call_target="tpu_custom_call" | custom-call | flops 1024 | bytes 1024 | tf_op jit(solution)/shard_map/pallas_call | solution.py:167
  24.2 0.4 collective-permute-done
  24.6 0.8 %shard_map.101 = (bf16[4,2,64,128]{3,2,1,0:T(8,128)(2,1)S(1)}, bf16[4,2,64,128]{3,2,1,0:T(8,128)(2,1)S(1)}, bf16[4,2,64,128]{3,2,1,0:T(8,128)(2,1)S(1)}, bf16[4,...) custom-call(bf16[6,2,64,128]{3,2,1,0:T(8,128)(2,1)S(1)} %bitcast.31, bf16[6,2,64,128]{3,2,1,0:T(8,128)(2,1)S(1)} %bitcast.29, ...), custom_call_target="tpu_custom_call" | custom-call | flops 1024 | bytes 1024 | tf_op jit(solution)/shard_map/pallas_call | solution.py:235
  25.5 3.1 %collective-permute-start.3 = (bf16[4,2,64,128]{3,2,1,0:T(8,128)(2,1)S(1)}, bf16[4,2,64,128]{3,2,1,0:T(8,128)(2,1)S(1)}, u32[]{:S(2)}, u32[]{:S(2)}) collective-permute-start(bf16[4,2,64,128]{3,2,1,0:T(8,128)(2,1)S(1)} %get-tuple-element.68), channel_id=1, source_target_pairs={{0,24},{8,16},{16,8},{24,0},{1,25},{9,17},{17,9},{25,1},{2,26},{10... | collective-permute-start | bytes 393224 | tf_op jit(solution)/shard_map/ppermute | solution.py:63
  28.5 0.5 collective-permute-start.4
  29.1 0.4 collective-permute-start.5
  29.5 1.3 %collective-permute-done.10.refs_6_ = bf16[4,2,64,128]{3,2,1,0:T(8,128)(2,1)S(1)} collective-permute-done((bf16[4,2,64,128]{3,2,1,0:T(8,128)(2,1)S(1)}, bf16[4,2,64,128]{3,2,1,0:T(8,128)(2,1)S(1)}, u32[]{:S(2)}, u32[]{:S(2)}) %collective-permute-start.10) | collective-permute-done | bytes 131104 | tf_op jit(solution)/shard_map/ppermute | solution.py:63
  30.8 0.7 %collective-permute-done.11.refs_7_ = bf16[4,2,64,128]{3,2,1,0:T(8,128)(2,1)S(1)} collective-permute-done((bf16[4,2,64,128]{3,2,1,0:T(8,128)(2,1)S(1)}, bf16[4,2,64,128]{3,2,1,0:T(8,128)(2,1)S(1)}, u32[]{:S(2)}, u32[]{:S(2)}) %collective-permute-start.11) | collective-permute-done | bytes 131104 | tf_op jit(solution)/shard_map/ppermute | solution.py:63
  31.6 1.7 %collective-permute-start.12 = (bf16[6,4,32,2,128]{4,3,2,1,0:T(2,128)(2,1)S(1)}, bf16[6,4,32,2,128]{4,3,2,1,0:T(2,128)(2,1)S(1)}, u32[]{:S(2)}, u32[]{:S(2)}) collective-permute-start(bf16[6,4,32,2,128]{4,3,2,1,0:T(2,128)(2,1)S(1)} %get-tuple-element.92), channel_id=1, source_target_pairs={{0,24},{8,16},{16,8},{24,0},{1,25},{9,17},{17,9},{25,1},{2,26},{10... | collective-permute-start | bytes 1179656 | tf_op jit(solution)/shard_map/ppermute | solution.py:63
  33.3 3.1 %collective-permute-done.4.refs_2_ = bf16[4,2,64,128]{3,2,1,0:T(8,128)(2,1)S(1)} collective-permute-done((bf16[4,2,64,128]{3,2,1,0:T(8,128)(2,1)S(1)}, bf16[4,2,64,128]{3,2,1,0:T(8,128)(2,1)S(1)}, u32[]{:S(2)}, u32[]{:S(2)}) %collective-permute-start.4) | collective-permute-done | bytes 131104 | tf_op jit(solution)/shard_map/ppermute | solution.py:63
  36.4 1.6 %collective-permute-start.13 = (bf16[6,4,32,2,128]{4,3,2,1,0:T(2,128)(2,1)S(1)}, bf16[6,4,32,2,128]{4,3,2,1,0:T(2,128)(2,1)S(1)}, u32[]{:S(2)}, u32[]{:S(2)}) collective-permute-start(bf16[6,4,32,2,128]{4,3,2,1,0:T(2,128)(2,1)S(1)} %get-tuple-element.93), channel_id=1, source_target_pairs={{0,8},{8,0},{16,24},{24,16},{1,9},{9,1},{17,25},{25,17},{2,10},{10... | collective-permute-start | bytes 1179656 | tf_op jit(solution)/shard_map/ppermute | solution.py:63
  37.9 1.3 %collective-permute-start.14 = (bf16[6,4,32,2,128]{4,3,2,1,0:T(2,128)(2,1)S(1)}, bf16[6,4,32,2,128]{4,3,2,1,0:T(2,128)(2,1)S(1)}, u32[]{:S(2)}, u32[]{:S(2)}) collective-permute-start(bf16[6,4,32,2,128]{4,3,2,1,0:T(2,128)(2,1)S(1)} %get-tuple-element.94), channel_id=1, source_target_pairs={{0,16},{8,24},{16,0},{24,8},{1,17},{9,25},{17,1},{25,9},{2,18},{10... | collective-permute-start | bytes 1179656 | tf_op jit(solution)/shard_map/ppermute | solution.py:63
  39.2 1.2 %shard_map.106 = (bf16[4,2,64,128]{3,2,1,0:T(8,128)(2,1)S(1)}, bf16[4,2,64,128]{3,2,1,0:T(8,128)(2,1)S(1)}) custom-call(bf16[4,2,64,128]{3,2,1,0:T(8,128)(2,1)S(1)} %get-tuple-element.83.refs_0_, bf16[4,2,64,128]{3,2,1,0:T(8,128)(2,1)S(1)} %collective-permute-done.3.refs_1_, bf16[4,2,64,128]{3,2,1,0:T(8,128)(2,1)S(1)} %collective-permute-done.4.refs_2_, ...), custom_call_target="tpu_custom_call" | custom-call | flops 1024 | bytes 1024 | tf_op jit(solution)/shard_map/pallas_call | solution.py:329
  40.5 1.3 %collective-permute-start.15 = (bf16[4,2,64,128]{3,2,1,0:T(8,128)(2,1)S(1)}, bf16[4,2,64,128]{3,2,1,0:T(8,128)(2,1)S(1)}, u32[]{:S(2)}, u32[]{:S(2)}) collective-permute-start(bf16[4,2,64,128]{3,2,1,0:T(8,128)(2,1)S(1)} %get-tuple-element.95), channel_id=1, source_target_pairs={{0,1},{1,2},{2,3},{3,4},{4,5},{5,6},{6,7},{8,9},{9,10},{10,11},{11... | collective-permute-start | bytes 393224 | tf_op jit(solution)/shard_map/ppermute | solution.py:70
  41.8 1.3 %collective-permute-start.16 = (bf16[4,2,64,128]{3,2,1,0:T(8,128)(2,1)S(1)}, bf16[4,2,64,128]{3,2,1,0:T(8,128)(2,1)S(1)}, u32[]{:S(2)}, u32[]{:S(2)}) collective-permute-start(bf16[4,2,64,128]{3,2,1,0:T(8,128)(2,1)S(1)} %get-tuple-element.96), channel_id=1, source_target_pairs={{1,0},{2,1},{3,2},{4,3},{5,4},{6,5},{7,6},{9,8},{10,9},{11,10},{12... | collective-permute-start | bytes 393224 | tf_op jit(solution)/shard_map/ppermute | solution.py:70
  43.1 3.7 %collective-permute-done.16.refs_9_ = bf16[4,2,64,128]{3,2,1,0:T(8,128)(2,1)S(1)} collective-permute-done((bf16[4,2,64,128]{3,2,1,0:T(8,128)(2,1)S(1)}, bf16[4,2,64,128]{3,2,1,0:T(8,128)(2,1)S(1)}, u32[]{:S(2)}, u32[]{:S(2)}) %collective-permute-start.16) | collective-permute-done | bytes 131104 | tf_op jit(solution)/shard_map/ppermute | solution.py:70
  46.8 5.4 %collective-permute-done.13 = bf16[6,4,32,2,128]{4,3,2,1,0:T(2,128)(2,1)S(1)} collective-permute-done((bf16[6,4,32,2,128]{4,3,2,1,0:T(2,128)(2,1)S(1)}, bf16[6,4,32,2,128]{4,3,2,1,0:T(2,128)(2,1)S(1)}, u32[]{:S(2)}, u32[]{:S(2)}) %collective-permute-start.13) | collective-permute-done | bytes 393248 | tf_op jit(solution)/shard_map/ppermute | solution.py:63
  52.2 0.0 copy-start.6
  52.2 1.6 %shard_map.107 = (bf16[3,4,64,128]{3,2,1,0:T(8,128)(2,1)S(1)}, bf16[3,4,64,128]{3,2,1,0:T(8,128)(2,1)S(1)}, bf16[3,4,64,128]{3,2,1,0:T(8,128)(2,1)S(1)}, bf16[3,4,64,128]{3,2,1,0:T(8,128)(2,1)S(1)}) custom-call(bf16[6,4,64,128]{3,2,1,0:T(8,128)(2,1)S(1)} %bitcast.24, bf16[6,4,64,128]{3,2,1,0:T(8,128)(2,1)S(1)} %bitcast.25, ...), custom_call_target="tpu_custom_call" | custom-call | flops 1024 | bytes 1024 | tf_op jit(solution)/shard_map/pallas_call | solution.py:279
  53.8 1.6 %collective-permute-start.17 = (bf16[3,4,64,128]{3,2,1,0:T(8,128)(2,1)S(1)}, bf16[3,4,64,128]{3,2,1,0:T(8,128)(2,1)S(1)}, u32[]{:S(2)}, u32[]{:S(2)}) collective-permute-start(bf16[3,4,64,128]{3,2,1,0:T(8,128)(2,1)S(1)} %get-tuple-element.112), channel_id=1, source_target_pairs={{0,8},{8,0},{16,24},{24,16},{1,9},{9,1},{17,25},{25,17},{2,10},{10... | collective-permute-start | bytes 589832 | tf_op jit(solution)/shard_map/ppermute | solution.py:63
  55.4 1.4 %collective-permute-start.18 = (bf16[3,4,64,128]{3,2,1,0:T(8,128)(2,1)S(1)}, bf16[3,4,64,128]{3,2,1,0:T(8,128)(2,1)S(1)}, u32[]{:S(2)}, u32[]{:S(2)}) collective-permute-start(bf16[3,4,64,128]{3,2,1,0:T(8,128)(2,1)S(1)} %get-tuple-element.113), channel_id=1, source_target_pairs={{0,16},{8,24},{16,0},{24,8},{1,17},{9,25},{17,1},{25,9},{2,18},{10... | collective-permute-start | bytes 589832 | tf_op jit(solution)/shard_map/ppermute | solution.py:63
  56.8 0.6 collective-permute-start.19
  57.4 5.0 %shard_map.108 = (f32[3072,128]{1,0:T(8,128)}, f32[3,16,64,128]{3,2,1,0:T(8,128)S(1)}) custom-call(bf16[4,2,64,128]{3,2,1,0:T(8,128)(2,1)S(1)} %get-tuple-element.83.refs_0_, bf16[4,2,64,128]{3,2,1,0:T(8,128)(2,1)S(1)} %collective-permute-done.3.refs_1_, bf16[4,2,64,128]{3,2,1,0:T(8,128)(2,1)S(1)} %collective-permute-done.4.refs_2_, ...), custom_call_target="tpu_custom_call" | custom-call | flops 1024 | bytes 1024 | tf_op jit(solution)/shard_map/pallas_call | solution.py:441
  62.4 3.6 %collective-permute-done.18.refs_2_ = bf16[3,4,64,128]{3,2,1,0:T(8,128)(2,1)S(1)} collective-permute-done((bf16[3,4,64,128]{3,2,1,0:T(8,128)(2,1)S(1)}, bf16[3,4,64,128]{3,2,1,0:T(8,128)(2,1)S(1)}, u32[]{:S(2)}, u32[]{:S(2)}) %collective-permute-start.18) | collective-permute-done | bytes 196640 | tf_op jit(solution)/shard_map/ppermute | solution.py:63
  66.0 1.3 %shard_map.109 = f32[3072,128]{1,0:T(8,128)} custom-call(bf16[3,4,64,128]{3,2,1,0:T(8,128)(2,1)S(1)} %get-tuple-element.111.refs_0_, bf16[3,4,64,128]{3,2,1,0:T(8,128)(2,1)S(1)} %collective-permute-done.17.refs_1_, bf16[3,4,64,128]{3,2,1,0:T(8,128)(2,1)S(1)} %collective-permute-done.18.refs_2_, bf16[3,4,64,128]{3,2,1,0:T(8,128)(2,1)S(1)} %collective-permute-done.19.refs_3_, ...), custom_call_target="tpu_custom_call" | custom-call | flops 1024 | bytes 1024 | tf_op jit(solution)/shard_map/pallas_call | solution.py:483
  (23 shorter events, 0.1 us)
Async XLA Ops:
  2.2 9.7 %collective-permute-start.6 = (bf16[6,2,32,2,128]{4,3,2,1,0:T(2,128)(2,1)S(1)}, bf16[6,2,32,2,128]{4,3,2,1,0:T(2,128)(2,1)S(1)}, u32[]{:S(2)}, u32[]{:S(2)}) collective-permute-start(bf16[6,2,32,2,128]{4,3,2,1,0:T(2,128)(2,1)S(1)} %shard_map.102), channel_id=1, source_target_pairs={{0,24},{8,16},{16,8},{24,0},{1,25},{9,17},{17,9},{25,1},{2,26},{10... | collective-permute-start | bytes 589832 | tf_op jit(solution)/shard_map/ppermute | solution.py:63
  6.3 10.4 %collective-permute-start.7 = (bf16[6,2,32,2,128]{4,3,2,1,0:T(2,128)(2,1)S(1)}, bf16[6,2,32,2,128]{4,3,2,1,0:T(2,128)(2,1)S(1)}, u32[]{:S(2)}, u32[]{:S(2)}) collective-permute-start(bf16[6,2,32,2,128]{4,3,2,1,0:T(2,128)(2,1)S(1)} %shard_map.103), channel_id=1, source_target_pairs={{0,8},{8,0},{16,24},{24,16},{1,9},{9,1},{17,25},{25,17},{2,10},{10... | collective-permute-start | bytes 589832 | tf_op jit(solution)/shard_map/ppermute | solution.py:63
  7.1 9.6 %collective-permute-start.8 = (bf16[6,2,32,2,128]{4,3,2,1,0:T(2,128)(2,1)S(1)}, bf16[6,2,32,2,128]{4,3,2,1,0:T(2,128)(2,1)S(1)}, u32[]{:S(2)}, u32[]{:S(2)}) collective-permute-start(bf16[6,2,32,2,128]{4,3,2,1,0:T(2,128)(2,1)S(1)} %shard_map.104), channel_id=1, source_target_pairs={{0,16},{8,24},{16,0},{24,8},{1,17},{9,25},{17,1},{25,9},{2,18},{10... | collective-permute-start | bytes 589832 | tf_op jit(solution)/shard_map/ppermute | solution.py:63
  7.4 6.6 %copy-start.3 = (bf16[256,256]{1,0:T(8,128)(2,1)S(1)}, bf16[256,256]{1,0:T(8,128)(2,1)}, u32[]{:S(2)}) copy-start(bf16[256,256]{1,0:T(8,128)(2,1)} %constant.5.clone.refs_1_) | copy-start | bytes 393220
  7.4 6.6 %copy-start.4 = (bf16[256,256]{1,0:T(8,128)(2,1)S(1)}, bf16[256,256]{1,0:T(8,128)(2,1)}, u32[]{:S(2)}) copy-start(bf16[256,256]{1,0:T(8,128)(2,1)} %constant.4.clone.refs_0_) | copy-start | bytes 393220
  7.4 13.5 %collective-permute-start.1 = (bf16[6,2,32,2,128]{4,3,2,1,0:T(2,128)(2,1)S(1)}, bf16[6,2,32,2,128]{4,3,2,1,0:T(2,128)(2,1)S(1)}, u32[]{:S(2)}, u32[]{:S(2)}) collective-permute-start(bf16[6,2,32,2,128]{4,3,2,1,0:T(2,128)(2,1)S(1)} %shard_map.98), channel_id=1, source_target_pairs={{0,8},{8,0},{16,24},{24,16},{1,9},{9,1},{17,25},{25,17},{2,10},{10... | collective-permute-start | bytes 589832 | tf_op jit(solution)/shard_map/ppermute | solution.py:63
  9.6 15.1 %collective-permute-start = (bf16[6,2,32,2,128]{4,3,2,1,0:T(2,128)(2,1)S(1)}, bf16[6,2,32,2,128]{4,3,2,1,0:T(2,128)(2,1)S(1)}, u32[]{:S(2)}, u32[]{:S(2)}) collective-permute-start(bf16[6,2,32,2,128]{4,3,2,1,0:T(2,128)(2,1)S(1)} %shard_map.97), channel_id=1, source_target_pairs={{0,24},{8,16},{16,8},{24,0},{1,25},{9,17},{17,9},{25,1},{2,26},{10... | collective-permute-start | bytes 589832 | tf_op jit(solution)/shard_map/ppermute | solution.py:63
  11.2 11.8 %copy-start = (bf16[12,32,2,2048]{3,2,1,0:T(2,128)(2,1)S(1)}, bf16[12,32,2,2048]{3,2,1,0:T(2,128)(2,1)}, u32[]{:S(2)}) copy-start(bf16[12,32,2,2048]{3,2,1,0:T(2,128)(2,1)} %fields_ref.3) | copy-start | bytes 9437188
  11.9 12.7 %collective-permute-start.2 = (bf16[6,2,32,2,128]{4,3,2,1,0:T(2,128)(2,1)S(1)}, bf16[6,2,32,2,128]{4,3,2,1,0:T(2,128)(2,1)S(1)}, u32[]{:S(2)}, u32[]{:S(2)}) collective-permute-start(bf16[6,2,32,2,128]{4,3,2,1,0:T(2,128)(2,1)S(1)} %shard_map.99), channel_id=1, source_target_pairs={{0,16},{8,24},{16,0},{24,8},{1,17},{9,25},{17,1},{25,9},{2,18},{10... | collective-permute-start | bytes 589832 | tf_op jit(solution)/shard_map/ppermute | solution.py:63
  17.6 11.5 %collective-permute-start.9 = (bf16[4,2,64,128]{3,2,1,0:T(8,128)(2,1)S(1)}, bf16[4,2,64,128]{3,2,1,0:T(8,128)(2,1)S(1)}, u32[]{:S(2)}, u32[]{:S(2)}) collective-permute-start(bf16[4,2,64,128]{3,2,1,0:T(8,128)(2,1)S(1)} %get-tuple-element.73), channel_id=1, source_target_pairs={{0,24},{8,16},{16,8},{24,0},{1,25},{9,17},{17,9},{25,1},{2,26},{10... | collective-permute-start | bytes 393224 | tf_op jit(solution)/shard_map/ppermute | solution.py:63
  20.9 9.9 %collective-permute-start.10 = (bf16[4,2,64,128]{3,2,1,0:T(8,128)(2,1)S(1)}, bf16[4,2,64,128]{3,2,1,0:T(8,128)(2,1)S(1)}, u32[]{:S(2)}, u32[]{:S(2)}) collective-permute-start(bf16[4,2,64,128]{3,2,1,0:T(8,128)(2,1)S(1)} %get-tuple-element.74), channel_id=1, source_target_pairs={{0,8},{8,0},{16,24},{24,16},{1,9},{9,1},{17,25},{25,17},{2,10},{10... | collective-permute-start | bytes 393224 | tf_op jit(solution)/shard_map/ppermute | solution.py:63
  22.4 16.8 %copy-start.7 = (s32[2,256]{1,0:T(2,128)S(1)}, s32[2,256]{1,0:T(2,128)}, u32[]{:S(2)}) copy-start(s32[2,256]{1,0:T(2,128)} %refs_8_.1) | copy-start | bytes 6148
  22.4 9.1 %collective-permute-start.11 = (bf16[4,2,64,128]{3,2,1,0:T(8,128)(2,1)S(1)}, bf16[4,2,64,128]{3,2,1,0:T(8,128)(2,1)S(1)}, u32[]{:S(2)}, u32[]{:S(2)}) collective-permute-start(bf16[4,2,64,128]{3,2,1,0:T(8,128)(2,1)S(1)} %get-tuple-element.75), channel_id=1, source_target_pairs={{0,16},{8,24},{16,0},{24,8},{1,17},{9,25},{17,1},{25,9},{2,18},{10... | collective-permute-start | bytes 393224 | tf_op jit(solution)/shard_map/ppermute | solution.py:63
  25.5 7.8 %collective-permute-start.3 = (bf16[4,2,64,128]{3,2,1,0:T(8,128)(2,1)S(1)}, bf16[4,2,64,128]{3,2,1,0:T(8,128)(2,1)S(1)}, u32[]{:S(2)}, u32[]{:S(2)}) collective-permute-start(bf16[4,2,64,128]{3,2,1,0:T(8,128)(2,1)S(1)} %get-tuple-element.68), channel_id=1, source_target_pairs={{0,24},{8,16},{16,8},{24,0},{1,25},{9,17},{17,9},{25,1},{2,26},{10... | collective-permute-start | bytes 393224 | tf_op jit(solution)/shard_map/ppermute | solution.py:63
  28.5 7.8 %collective-permute-start.4 = (bf16[4,2,64,128]{3,2,1,0:T(8,128)(2,1)S(1)}, bf16[4,2,64,128]{3,2,1,0:T(8,128)(2,1)S(1)}, u32[]{:S(2)}, u32[]{:S(2)}) collective-permute-start(bf16[4,2,64,128]{3,2,1,0:T(8,128)(2,1)S(1)} %get-tuple-element.69), channel_id=1, source_target_pairs={{0,8},{8,0},{16,24},{24,16},{1,9},{9,1},{17,25},{25,17},{2,10},{10... | collective-permute-start | bytes 393224 | tf_op jit(solution)/shard_map/ppermute | solution.py:63
  29.1 7.3 %collective-permute-start.5 = (bf16[4,2,64,128]{3,2,1,0:T(8,128)(2,1)S(1)}, bf16[4,2,64,128]{3,2,1,0:T(8,128)(2,1)S(1)}, u32[]{:S(2)}, u32[]{:S(2)}) collective-permute-start(bf16[4,2,64,128]{3,2,1,0:T(8,128)(2,1)S(1)} %get-tuple-element.70), channel_id=1, source_target_pairs={{0,16},{8,24},{16,0},{24,8},{1,17},{9,25},{17,1},{25,9},{2,18},{10... | collective-permute-start | bytes 393224 | tf_op jit(solution)/shard_map/ppermute | solution.py:63
  31.6 15.2 %collective-permute-start.12 = (bf16[6,4,32,2,128]{4,3,2,1,0:T(2,128)(2,1)S(1)}, bf16[6,4,32,2,128]{4,3,2,1,0:T(2,128)(2,1)S(1)}, u32[]{:S(2)}, u32[]{:S(2)}) collective-permute-start(bf16[6,4,32,2,128]{4,3,2,1,0:T(2,128)(2,1)S(1)} %get-tuple-element.92), channel_id=1, source_target_pairs={{0,24},{8,16},{16,8},{24,0},{1,25},{9,17},{17,9},{25,1},{2,26},{10... | collective-permute-start | bytes 1179656 | tf_op jit(solution)/shard_map/ppermute | solution.py:63
  36.4 15.8 %collective-permute-start.13 = (bf16[6,4,32,2,128]{4,3,2,1,0:T(2,128)(2,1)S(1)}, bf16[6,4,32,2,128]{4,3,2,1,0:T(2,128)(2,1)S(1)}, u32[]{:S(2)}, u32[]{:S(2)}) collective-permute-start(bf16[6,4,32,2,128]{4,3,2,1,0:T(2,128)(2,1)S(1)} %get-tuple-element.93), channel_id=1, source_target_pairs={{0,8},{8,0},{16,24},{24,16},{1,9},{9,1},{17,25},{25,17},{2,10},{10... | collective-permute-start | bytes 1179656 | tf_op jit(solution)/shard_map/ppermute | solution.py:63
  37.9 14.3 %collective-permute-start.14 = (bf16[6,4,32,2,128]{4,3,2,1,0:T(2,128)(2,1)S(1)}, bf16[6,4,32,2,128]{4,3,2,1,0:T(2,128)(2,1)S(1)}, u32[]{:S(2)}, u32[]{:S(2)}) collective-permute-start(bf16[6,4,32,2,128]{4,3,2,1,0:T(2,128)(2,1)S(1)} %get-tuple-element.94), channel_id=1, source_target_pairs={{0,16},{8,24},{16,0},{24,8},{1,17},{9,25},{17,1},{25,9},{2,18},{10... | collective-permute-start | bytes 1179656 | tf_op jit(solution)/shard_map/ppermute | solution.py:63
  40.5 2.6 %collective-permute-start.15 = (bf16[4,2,64,128]{3,2,1,0:T(8,128)(2,1)S(1)}, bf16[4,2,64,128]{3,2,1,0:T(8,128)(2,1)S(1)}, u32[]{:S(2)}, u32[]{:S(2)}) collective-permute-start(bf16[4,2,64,128]{3,2,1,0:T(8,128)(2,1)S(1)} %get-tuple-element.95), channel_id=1, source_target_pairs={{0,1},{1,2},{2,3},{3,4},{4,5},{5,6},{6,7},{8,9},{9,10},{10,11},{11... | collective-permute-start | bytes 393224 | tf_op jit(solution)/shard_map/ppermute | solution.py:70
  41.8 5.0 %collective-permute-start.16 = (bf16[4,2,64,128]{3,2,1,0:T(8,128)(2,1)S(1)}, bf16[4,2,64,128]{3,2,1,0:T(8,128)(2,1)S(1)}, u32[]{:S(2)}, u32[]{:S(2)}) collective-permute-start(bf16[4,2,64,128]{3,2,1,0:T(8,128)(2,1)S(1)} %get-tuple-element.96), channel_id=1, source_target_pairs={{1,0},{2,1},{3,2},{4,3},{5,4},{6,5},{7,6},{9,8},{10,9},{11,10},{12... | collective-permute-start | bytes 393224 | tf_op jit(solution)/shard_map/ppermute | solution.py:70
  52.2 5.2 %copy-start.1 = (bf16[5,64,2048]{2,1,0:T(8,128)(2,1)S(1)}, bf16[5,64,2048]{2,1,0:T(8,128)(2,1)}, u32[]{:S(2)}) copy-start(bf16[5,64,2048]{2,1,0:T(8,128)(2,1)} %refs_10_.1) | copy-start | bytes 3932164
  52.2 5.2 %copy-start.2 = (bf16[5,64,2048]{2,1,0:T(8,128)(2,1)S(1)}, bf16[5,64,2048]{2,1,0:T(8,128)(2,1)}, u32[]{:S(2)}) copy-start(bf16[5,64,2048]{2,1,0:T(8,128)(2,1)} %refs_11_.1) | copy-start | bytes 3932164
  52.2 5.2 %copy-start.5 = (f32[2048]{0:T(1024)S(1)}, f32[2048]{0:T(1024)}, u32[]{:S(2)}) copy-start(f32[2048]{0:T(1024)} %param.9) | copy-start | bytes 24580
  52.2 5.2 %copy-start.6 = (s32[32,5]{0,1:T(8,128)S(1)}, s32[32,5]{0,1:T(8,128)}, u32[]{:S(2)}) copy-start(s32[32,5]{0,1:T(8,128)} %param.12) | copy-start | bytes 1924
  53.8 8.6 %collective-permute-start.17 = (bf16[3,4,64,128]{3,2,1,0:T(8,128)(2,1)S(1)}, bf16[3,4,64,128]{3,2,1,0:T(8,128)(2,1)S(1)}, u32[]{:S(2)}, u32[]{:S(2)}) collective-permute-start(bf16[3,4,64,128]{3,2,1,0:T(8,128)(2,1)S(1)} %get-tuple-element.112), channel_id=1, source_target_pairs={{0,8},{8,0},{16,24},{24,16},{1,9},{9,1},{17,25},{25,17},{2,10},{10... | collective-permute-start | bytes 589832 | tf_op jit(solution)/shard_map/ppermute | solution.py:63
  55.4 10.6 %collective-permute-start.18 = (bf16[3,4,64,128]{3,2,1,0:T(8,128)(2,1)S(1)}, bf16[3,4,64,128]{3,2,1,0:T(8,128)(2,1)S(1)}, u32[]{:S(2)}, u32[]{:S(2)}) collective-permute-start(bf16[3,4,64,128]{3,2,1,0:T(8,128)(2,1)S(1)} %get-tuple-element.113), channel_id=1, source_target_pairs={{0,16},{8,24},{16,0},{24,8},{1,17},{9,25},{17,1},{25,9},{2,18},{10... | collective-permute-start | bytes 589832 | tf_op jit(solution)/shard_map/ppermute | solution.py:63
  56.8 9.2 %collective-permute-start.19 = (bf16[3,4,64,128]{3,2,1,0:T(8,128)(2,1)S(1)}, bf16[3,4,64,128]{3,2,1,0:T(8,128)(2,1)S(1)}, u32[]{:S(2)}, u32[]{:S(2)}) collective-permute-start(bf16[3,4,64,128]{3,2,1,0:T(8,128)(2,1)S(1)} %get-tuple-element.114), channel_id=1, source_target_pairs={{0,24},{8,16},{16,8},{24,0},{1,25},{9,17},{17,9},{25,1},{2,26},{10... | collective-permute-start | bytes 589832 | tf_op jit(solution)/shard_map/ppermute | solution.py:63

commit v16 on v15

--- a/solution.py
+++ b/solution.py
@@ -89,13 +89,17 @@
     return 2 if tiles % 2 == 0 else 1
 
 
-def pieces_of(fields_ref, first, share, group, out_ref):
+def spans_of(tiles):
+    return [(0, tiles - 1), (tiles - 1, 1)] if tiles > 2 else [(0, tiles)]
+
+
+def pieces_of(fields_ref, first, share, begin, out_ref):
     count = lax.axis_size("mode")
     tiles = fields_ref.shape[3] // count // LANES
     components, held = out_ref.shape[:2]
     pairs = []
     for t in range(held):
-        start = pl.multiple_of((share * tiles + group * held + t) * LANES, LANES)
+        start = pl.multiple_of((share * tiles + begin + t) * LANES, LANES)
         pairs.append((fields_ref.at[pl.ds(first, components), :, :, pl.ds(start, LANES)], out_ref.at[:, t]))
     return pairs
 
@@ -127,18 +131,17 @@
     )(pltpu.with_memory_space_constraint(fields, pltpu.HBM))
 
 
-def packed_shape(fields, first, last, groups):
-    _, mode_count, _, width = fields.shape
-    return (last - first, width // lax.axis_size("mode") // LANES // groups, mode_count, 2, LANES)
-
-
-def pack(fields, first, last, offset, group, groups):
+def packed_shape(fields, first, last, held):
+    return (last - first, held, fields.shape[1], 2, LANES)
+
+
+def pack(fields, first, last, offset, begin, held):
     count = lax.axis_size("mode")
-    shape = packed_shape(fields, first, last, groups)
+    shape = packed_shape(fields, first, last, held)
 
     def kernel(fields_ref, out_ref, sems):
         share = dest_of(lax.axis_index("mode"), offset, count)
-        run_copies(pieces_of(fields_ref, first, share, group, out_ref), sems)
+        run_copies(pieces_of(fields_ref, first, share, begin, out_ref), sems)
 
     return pl.pallas_call(
         kernel,
@@ -153,15 +156,15 @@
 
 def pack_rest(fields, parcels, carried):
     count = lax.axis_size("mode")
-    shapes = [packed_shape(fields, first, last, groups) for first, last, _, _, groups in parcels]
+    shapes = [packed_shape(fields, first, last, held) for first, last, _, _, held in parcels]
 
     def kernel(fields_ref, *refs):
         inputs, refs = refs[: len(carried)], refs[len(carried) :]
         parcel_refs, outputs = refs[: len(parcels)], refs[len(parcels) : -1]
         me = lax.axis_index("mode")
         pairs = []
-        for (first, _, offset, group, _), parcel_ref in zip(parcels, parcel_refs):
-            pairs += pieces_of(fields_ref, first, dest_of(me, offset, count), group, parcel_ref)
+        for (first, _, offset, begin, _), parcel_ref in zip(parcels, parcel_refs):
+            pairs += pieces_of(fields_ref, first, dest_of(me, offset, count), begin, parcel_ref)
         run_copies(pairs, refs[-1], zip(inputs, outputs))
 
     return pl.pallas_call(
@@ -248,22 +251,24 @@
     )(*received, inverse, forward)
 
 
-def second_kernel(count, groups, *refs):
+def second_kernel(count, groups, begin, *refs):
     in_refs, refs = refs[:count], refs[count:]
     first_refs, (inverse_ref, forward_ref) = refs[:groups], refs[groups : groups + 2]
     out_refs, (physical_ref, x_ref, product_ref, table_ref) = refs[groups + 2 : groups + 2 + count], refs[groups + 2 + count :]
-    width = first_refs[0].shape[2]
+    in_group = first_refs[0].shape[2] // LANES
 
     def store(c, value):
         physical_ref[c] = value
 
     to_physical(offsets(count, SECOND_SEND), in_refs, inverse_ref[...], x_ref, store)
-    for group in range(groups):
-        lanes = slice(group * width, (group + 1) * width)
+    for t in range(in_refs[0].shape[1]):
+        lanes = slice(t * LANES, (t + 1) * LANES)
+        first_ref, place = first_refs[(begin + t) // in_group], (begin + t) % in_group
+        first_lanes = slice(place * LANES, (place + 1) * LANES)
         for i in range(THETA // CHUNK):
             at = slice(i * CHUNK, (i + 1) * CHUNK)
-            velocity = [first_refs[group][c, at] for c in range(3)]
-            magnetic = [first_refs[group][c, at] for c in range(3, 6)]
+            velocity = [first_ref[c, at, first_lanes] for c in range(3)]
+            magnetic = [first_ref[c, at, first_lanes] for c in range(3, 6)]
             current = [physical_ref[c, at, lanes] for c in range(3)]
             vorticity = [physical_ref[c, at, lanes] for c in range(3, 6)]
             lorentz = [a + b for a, b in zip(cross(current, magnetic), cross(velocity, vorticity))]
@@ -272,12 +277,12 @@
     to_modes(offsets(count, SECOND_RETURN), forward_ref, table_ref, product_ref, out_refs)
 
 
-def second_physics(received, physical, inverse, forward):
+def second_physics(received, physical, begin, inverse, forward):
     count, groups = len(received), len(physical)
     components, tiles, rows, _ = received[0].shape
     width = tiles * LANES
     return pl.pallas_call(
-        functools.partial(second_kernel, count, groups),
+        functools.partial(second_kernel, count, groups, begin),
         in_specs=[vmem()] * (count + groups + 2),
         out_specs=[vmem()] * count,
         out_shape=[jax.ShapeDtypeStruct((3, tiles, rows, LANES), jnp.bfloat16)] * count,
@@ -455,9 +460,10 @@
 def momentum_kernel(count, arrived, *refs):
     in_refs, (gradient_ref, out_ref, total_ref, sems) = refs[:arrived], refs[arrived:]
     me = lax.axis_index("mode")
-    components, held, rows, _ = in_refs[0].shape
+    components, _, rows, _ = in_refs[0].shape
+    tiles = gradient_ref.shape[1] // count
+    holders = [(part, t) for part in range(arrived // count) for t in range(in_refs[part * count].shape[1])]
     mode_count = rows // 2
-    tiles = arrived // count * held
     stride = 2 * count * tiles
     out_rows = mode_count * stride
     copies = []
@@ -467,7 +473,8 @@
             for start in range(0, tiles, SUBLANES // 2):
                 values = []
                 for t in range(start, min(tiles, start + SUBLANES // 2)):
-                    piece = in_refs[t // held * count + step][c, t % held].astype(jnp.float32)
+                    part, at = holders[t]
+                    piece = in_refs[part * count + step][c, at].astype(jnp.float32)
                     values.append(piece - gradient_ref[c, share * tiles + t])
                 put_rows(total_ref, c * out_rows + 2 * (share * tiles + start), stride, values)
         done = pl.ds(c * out_rows, out_rows)
@@ -478,8 +485,8 @@
 
 
 def momentum_of(received, gradient, count):
-    components, held, rows, _ = received[0].shape
-    shape = (components * rows * len(received) * held, LANES)
+    components, _, rows, _ = received[0].shape
+    shape = (components * rows * gradient.shape[1], LANES)
     return pl.pallas_call(
         functools.partial(momentum_kernel, count, len(received)),
         in_specs=[vmem()] * (len(received) + 1),
@@ -506,17 +513,20 @@
     def joined(pieces):
         return [piece.reshape(piece.shape[:-3] + (rows, LANES)) for piece in pieces]
 
-    groups = groups_of(width // count // LANES)
+    tiles = width // count // LANES
+    groups, spans = groups_of(tiles), spans_of(tiles)
+    held = tiles // groups
     flow = load(mode_fields, 6)
     arrived = []
     for group in range(groups):
         order = offsets(count, FIRST_SEND)
-        arrived.append(exchange([pack(flow, 0, 6, offset, group, groups) for offset in order[1:]], order[1:]))
-    parcels = [(0, 6, 0, group, groups) for group in range(groups)]
+        parcels = [pack(flow, 0, 6, offset, group * held, held) for offset in order[1:]]
+        arrived.append(exchange(parcels, order[1:]))
+    parcels = [(0, 6, 0, group * held, held) for group in range(groups)]
     *own, inverse, forward = pack_rest(flow, parcels, [inverse, forward])
     arrived[0][1:2], carried = lax.optimization_barrier((arrived[0][1:2], [inverse, forward]))
     order = offsets(count, SECOND_SEND)
-    parcels = [(6, 12, offset, 0, 1) for offset in order]
+    parcels = [(6, 12, offset) + span for span in spans for offset in order]
     *shares, later_inverse, later_forward = pack_rest(mode_fields, parcels, carried)
     local, physical = [], []
     for group in range(groups):
@@ -528,15 +538,18 @@
         local += exchange(terms, offsets(count, FIRST_RETURN))
         physical.append(velocity_magnetic)
     for group in range(groups):
-        held, sent = slice(count if group == 0 else 0, None), slice(1, 2) if group == 0 else slice(2, None)
-        local[held], shares[sent] = lax.optimization_barrier((local[held], shares[sent]))
-    sources = exchange(shares, order)
+        back, sent = slice(count if group == 0 else 0, None), slice(1, 2) if group == 0 else slice(2, count)
+        local[back], shares[sent] = lax.optimization_barrier((local[back], shares[sent]))
     toward_prev, toward_next = interface(local, interface_nodes, count)
     halos = (from_behind(toward_next, "mer", 1), from_behind(toward_prev, "mer", -1))
-    sources, halos = lax.optimization_barrier((sources, halos))
-    lorentz = list(second_physics(joined(sources), physical, later_inverse, later_forward))
-    lorentz, radius = lax.optimization_barrier((lorentz, radius))
-    lorentz = exchange(lorentz, offsets(count, SECOND_RETURN))
+    halos, shares[count:] = lax.optimization_barrier((halos, shares[count:]))
+    lorentz = []
+    for part, (begin, _) in enumerate(spans):
+        sources = exchange(shares[part * count : (part + 1) * count], order)
+        terms = list(second_physics(joined(sources), physical, begin, later_inverse, later_forward))
+        if part == len(spans) - 1:
+            terms, radius = lax.optimization_barrier((terms, radius))
+        lorentz += exchange(terms, offsets(count, SECOND_RETURN))
     induction, gradient = derive(
         local, *halos, radial_blocks, axial_blocks, radius.reshape(1, width), block_columns.T, count
     )

time: 67.5 us -> 70.7 us (1.047)
  the two profiles are of different devices: /device:TPU:0 before, /device:TPU:1 now
where the time goes in v16:
time: 70.7 us; the launch traced here: 70.3 us
  starting transfers between devices  33.9 us (48%)
  waiting for transfers between devices  20 us (28%)
  Pallas kernels  15.5 us (22%)
  between operations  0.85 us (1%)
    ppermute x24, starting transfers between devices, exchange(): received.append(lax.ppermute(piece, 'mode', pairs))  26.6 us
    ppermute x24, waiting for transfers between devices, exchange(): received.append(lax.ppermute(piece, 'mode', pairs))  15.7 us
    ppermute x2, starting transfers between devices, from_behind(): lax.ppermute(value, axis, [(source, source + steps) for source in range(i...  7.29 us
    pallas_call x1, Pallas kernels, derive(): pl.pallas_call(functools.partial(derive_kernel, count, len(received)), in...  5 us
    ppermute x2, waiting for transfers between devices, from_behind(): lax.ppermute(value, axis, [(source, source + steps) for source in range(i...  4.35 us
    pallas_call x2, Pallas kernels, second_physics(): pl.pallas_call(functools.partial(second_kernel, count, groups, begin), in...  2.05 us
    pallas_call x2, Pallas kernels, first_physics(): pl.pallas_call(functools.partial(first_kernel, count), in_specs=[vmem()]...  1.63 us
    pallas_call x2, Pallas kernels, pack_rest(): pl.pallas_call(kernel, in_specs=[pl.BlockSpec(memory_space=pl.ANY)] + [vm...  1.62 us
  transfers between devices with their start and end apart: 26, of which 9 were waited for; matrix products, arithmetic and copies ran while one was open for 0% of the time, Pallas kernels for 18%

profile of v16, /device:TPU:1, one launch (start us, length us, event | category | flops | bytes accessed | tf_op | source)
XLA Modules:
  0.0 70.3 jit_solution(15087999231345566149)
XLA Ops:
  0.6 1.4 %shard_map.95.fields_ref = bf16[6,32,2,2048]{3,2,1,0:T(2,128)(2,1)S(1)} custom-call(bf16[12,32,2,2048]{3,2,1,0:T(2,128)(2,1)} %fields_ref.3), custom_call_target="tpu_custom_call" | custom-call | flops 1024 | bytes 1024 | tf_op jit(solution)/shard_map/pallas_call | solution.py:123
  2.0 0.2 shard_map.102
  2.2 3.1 %collective-permute-start.6 = (bf16[6,2,32,2,128]{4,3,2,1,0:T(2,128)(2,1)S(1)}, bf16[6,2,32,2,128]{4,3,2,1,0:T(2,128)(2,1)S(1)}, u32[]{:S(2)}, u32[]{:S(2)}) collective-permute-start(bf16[6,2,32,2,128]{4,3,2,1,0:T(2,128)(2,1)S(1)} %shard_map.102), channel_id=1, source_target_pairs={{0,24},{8,16},{16,8},{24,0},{1,25},{9,17},{17,9},{25,1},{2,26},{10... | collective-permute-start | bytes 589832 | tf_op jit(solution)/shard_map/ppermute | solution.py:63
  5.3 0.2 shard_map.103
  5.4 0.3 collective-permute-start.7
  5.8 0.2 shard_map.104
  6.1 0.2 shard_map.98
  6.2 1.4 %collective-permute-start.1 = (bf16[6,2,32,2,128]{4,3,2,1,0:T(2,128)(2,1)S(1)}, bf16[6,2,32,2,128]{4,3,2,1,0:T(2,128)(2,1)S(1)}, u32[]{:S(2)}, u32[]{:S(2)}) collective-permute-start(bf16[6,2,32,2,128]{4,3,2,1,0:T(2,128)(2,1)S(1)} %shard_map.98), channel_id=1, source_target_pairs={{0,8},{8,0},{16,24},{24,16},{1,9},{9,1},{17,25},{25,17},{2,10},{10... | collective-permute-start | bytes 589832 | tf_op jit(solution)/shard_map/ppermute | solution.py:63
  7.9 1.3 %collective-permute-start = (bf16[6,2,32,2,128]{4,3,2,1,0:T(2,128)(2,1)S(1)}, bf16[6,2,32,2,128]{4,3,2,1,0:T(2,128)(2,1)S(1)}, u32[]{:S(2)}, u32[]{:S(2)}) collective-permute-start(bf16[6,2,32,2,128]{4,3,2,1,0:T(2,128)(2,1)S(1)} %shard_map.97), channel_id=1, source_target_pairs={{0,24},{8,16},{16,8},{24,0},{1,25},{9,17},{17,9},{25,1},{2,26},{10... | collective-permute-start | bytes 589832 | tf_op jit(solution)/shard_map/ppermute | solution.py:63
  9.3 0.6 collective-permute-done.6
  9.9 1.2 %collective-permute-start.2 = (bf16[6,2,32,2,128]{4,3,2,1,0:T(2,128)(2,1)S(1)}, bf16[6,2,32,2,128]{4,3,2,1,0:T(2,128)(2,1)S(1)}, u32[]{:S(2)}, u32[]{:S(2)}) collective-permute-start(bf16[6,2,32,2,128]{4,3,2,1,0:T(2,128)(2,1)S(1)} %shard_map.99), channel_id=1, source_target_pairs={{0,16},{8,24},{16,0},{24,8},{1,17},{9,25},{17,1},{25,9},{2,18},{10... | collective-permute-start | bytes 589832 | tf_op jit(solution)/shard_map/ppermute | solution.py:63
  11.1 0.3 shard_map.96
  11.4 2.7 %collective-permute-done.7 = bf16[6,2,32,2,128]{4,3,2,1,0:T(2,128)(2,1)S(1)} collective-permute-done((bf16[6,2,32,2,128]{4,3,2,1,0:T(2,128)(2,1)S(1)}, bf16[6,2,32,2,128]{4,3,2,1,0:T(2,128)(2,1)S(1)}, u32[]{:S(2)}, u32[]{:S(2)}) %collective-permute-start.7) | collective-permute-done | bytes 196640 | tf_op jit(solution)/shard_map/ppermute | solution.py:63
  14.1 0.6 collective-permute-done.8
  14.7 0.8 %shard_map.105 = (bf16[4,2,64,128]{3,2,1,0:T(8,128)(2,1)S(1)}, bf16[4,2,64,128]{3,2,1,0:T(8,128)(2,1)S(1)}, bf16[4,2,64,128]{3,2,1,0:T(8,128)(2,1)S(1)}, bf16[4,...) custom-call(bf16[6,2,64,128]{3,2,1,0:T(8,128)(2,1)S(1)} %bitcast.39, bf16[6,2,64,128]{3,2,1,0:T(8,128)(2,1)S(1)} %bitcast.36, ...), custom_call_target="tpu_custom_call" | custom-call | flops 1024 | bytes 1024 | tf_op jit(solution)/shard_map/pallas_call | solution.py:238
  15.5 2.6 %collective-permute-start.9 = (bf16[4,2,64,128]{3,2,1,0:T(8,128)(2,1)S(1)}, bf16[4,2,64,128]{3,2,1,0:T(8,128)(2,1)S(1)}, u32[]{:S(2)}, u32[]{:S(2)}) collective-permute-start(bf16[4,2,64,128]{3,2,1,0:T(8,128)(2,1)S(1)} %get-tuple-element.81), channel_id=1, source_target_pairs={{0,24},{8,16},{16,8},{24,0},{1,25},{9,17},{17,9},{25,1},{2,26},{10... | collective-permute-start | bytes 393224 | tf_op jit(solution)/shard_map/ppermute | solution.py:63
  18.1 0.2 collective-permute-start.10
  18.4 0.3 collective-permute-start.11
  18.6 1.3 %shard_map.100 = (bf16[6,3,32,2,128]{4,3,2,1,0:T(2,128)(2,1)S(1)}, bf16[6,3,32,2,128]{4,3,2,1,0:T(2,128)(2,1)S(1)}, bf16[6,3,32,2,128]{4,3,2,1,0:T(2,128)(2,1)S(...) custom-call(bf16[12,32,2,2048]{3,2,1,0:T(2,128)(2,1)S(1)} %copy-done, ...), custom_call_target="tpu_custom_call" | custom-call | flops 1024 | bytes 1024 | tf_op jit(solution)/shard_map/pallas_call | solution.py:170
  19.9 2.6 %collective-permute-done = bf16[6,2,32,2,128]{4,3,2,1,0:T(2,128)(2,1)S(1)} collective-permute-done((bf16[6,2,32,2,128]{4,3,2,1,0:T(2,128)(2,1)S(1)}, bf16[6,2,32,2,128]{4,3,2,1,0:T(2,128)(2,1)S(1)}, u32[]{:S(2)}, u32[]{:S(2)}) %collective-permute-start) | collective-permute-done | bytes 196640 | tf_op jit(solution)/shard_map/ppermute | solution.py:63
  22.5 0.8 %shard_map.101 = (bf16[4,2,64,128]{3,2,1,0:T(8,128)(2,1)S(1)}, bf16[4,2,64,128]{3,2,1,0:T(8,128)(2,1)S(1)}, bf16[4,2,64,128]{3,2,1,0:T(8,128)(2,1)S(1)}, bf16[4,...) custom-call(bf16[6,2,64,128]{3,2,1,0:T(8,128)(2,1)S(1)} %bitcast.35, bf16[6,2,64,128]{3,2,1,0:T(8,128)(2,1)S(1)} %bitcast.33, ...), custom_call_target="tpu_custom_call" | custom-call | flops 1024 | bytes 1024 | tf_op jit(solution)/shard_map/pallas_call | solution.py:238
  23.4 2.2 %collective-permute-start.3 = (bf16[4,2,64,128]{3,2,1,0:T(8,128)(2,1)S(1)}, bf16[4,2,64,128]{3,2,1,0:T(8,128)(2,1)S(1)}, u32[]{:S(2)}, u32[]{:S(2)}) collective-permute-start(bf16[4,2,64,128]{3,2,1,0:T(8,128)(2,1)S(1)} %get-tuple-element.76), channel_id=1, source_target_pairs={{0,24},{8,16},{16,8},{24,0},{1,25},{9,17},{17,9},{25,1},{2,26},{10... | collective-permute-start | bytes 393224 | tf_op jit(solution)/shard_map/ppermute | solution.py:63
  25.6 0.3 collective-permute-start.4
  25.8 0.7 %collective-permute-start.5 = (bf16[4,2,64,128]{3,2,1,0:T(8,128)(2,1)S(1)}, bf16[4,2,64,128]{3,2,1,0:T(8,128)(2,1)S(1)}, u32[]{:S(2)}, u32[]{:S(2)}) collective-permute-start(bf16[4,2,64,128]{3,2,1,0:T(8,128)(2,1)S(1)} %get-tuple-element.78), channel_id=1, source_target_pairs={{0,16},{8,24},{16,0},{24,8},{1,17},{9,25},{17,1},{25,9},{2,18},{10... | collective-permute-start | bytes 393224 | tf_op jit(solution)/shard_map/ppermute | solution.py:63
  26.6 1.6 %collective-permute-done.10.refs_6_ = bf16[4,2,64,128]{3,2,1,0:T(8,128)(2,1)S(1)} collective-permute-done((bf16[4,2,64,128]{3,2,1,0:T(8,128)(2,1)S(1)}, bf16[4,2,64,128]{3,2,1,0:T(8,128)(2,1)S(1)}, u32[]{:S(2)}, u32[]{:S(2)}) %collective-permute-start.10) | collective-permute-done | bytes 131104 | tf_op jit(solution)/shard_map/ppermute | solution.py:63
  28.2 1.4 %collective-permute-done.11.refs_7_ = bf16[4,2,64,128]{3,2,1,0:T(8,128)(2,1)S(1)} collective-permute-done((bf16[4,2,64,128]{3,2,1,0:T(8,128)(2,1)S(1)}, bf16[4,2,64,128]{3,2,1,0:T(8,128)(2,1)S(1)}, u32[]{:S(2)}, u32[]{:S(2)}) %collective-permute-start.11) | collective-permute-done | bytes 131104 | tf_op jit(solution)/shard_map/ppermute | solution.py:63
  29.6 2.4 %collective-permute-start.17 = (bf16[6,3,32,2,128]{4,3,2,1,0:T(2,128)(2,1)S(1)}, bf16[6,3,32,2,128]{4,3,2,1,0:T(2,128)(2,1)S(1)}, u32[]{:S(2)}, u32[]{:S(2)}) collective-permute-start(bf16[6,3,32,2,128]{4,3,2,1,0:T(2,128)(2,1)S(1)} %get-tuple-element.120), channel_id=1, source_target_pairs={{0,24},{8,16},{16,8},{24,0},{1,25},{9,17},{17,9},{25,1},{2,26},{10... | collective-permute-start | bytes 884744 | tf_op jit(solution)/shard_map/ppermute | solution.py:63
  32.0 1.8 %collective-permute-done.4.refs_2_ = bf16[4,2,64,128]{3,2,1,0:T(8,128)(2,1)S(1)} collective-permute-done((bf16[4,2,64,128]{3,2,1,0:T(8,128)(2,1)S(1)}, bf16[4,2,64,128]{3,2,1,0:T(8,128)(2,1)S(1)}, u32[]{:S(2)}, u32[]{:S(2)}) %collective-permute-start.4) | collective-permute-done | bytes 131104 | tf_op jit(solution)/shard_map/ppermute | solution.py:63
  33.8 1.1 %collective-permute-start.18 = (bf16[6,3,32,2,128]{4,3,2,1,0:T(2,128)(2,1)S(1)}, bf16[6,3,32,2,128]{4,3,2,1,0:T(2,128)(2,1)S(1)}, u32[]{:S(2)}, u32[]{:S(2)}) collective-permute-start(bf16[6,3,32,2,128]{4,3,2,1,0:T(2,128)(2,1)S(1)} %get-tuple-element.121), channel_id=1, source_target_pairs={{0,8},{8,0},{16,24},{24,16},{1,9},{9,1},{17,25},{25,17},{2,10},{10... | collective-permute-start | bytes 884744 | tf_op jit(solution)/shard_map/ppermute | solution.py:63
  34.9 2.3 %collective-permute-start.19 = (bf16[6,3,32,2,128]{4,3,2,1,0:T(2,128)(2,1)S(1)}, bf16[6,3,32,2,128]{4,3,2,1,0:T(2,128)(2,1)S(1)}, u32[]{:S(2)}, u32[]{:S(2)}) collective-permute-start(bf16[6,3,32,2,128]{4,3,2,1,0:T(2,128)(2,1)S(1)} %get-tuple-element.122), channel_id=1, source_target_pairs={{0,16},{8,24},{16,0},{24,8},{1,17},{9,25},{17,1},{25,9},{2,18},{10... | collective-permute-start | bytes 884744 | tf_op jit(solution)/shard_map/ppermute | solution.py:63
  37.2 1.2 %shard_map.106 = (bf16[4,2,64,128]{3,2,1,0:T(8,128)(2,1)S(1)}, bf16[4,2,64,128]{3,2,1,0:T(8,128)(2,1)S(1)}) custom-call(bf16[4,2,64,128]{3,2,1,0:T(8,128)(2,1)S(1)} %get-tuple-element.91.refs_0_, bf16[4,2,64,128]{3,2,1,0:T(8,128)(2,1)S(1)} %collective-permute-done.3.refs_1_, bf16[4,2,64,128]{3,2,1,0:T(8,128)(2,1)S(1)} %collective-permute-done.4.refs_2_, ...), custom_call_target="tpu_custom_call" | custom-call | flops 1024 | bytes 1024 | tf_op jit(solution)/shard_map/pallas_call | solution.py:334
  38.4 5.4 %collective-permute-start.12 = (bf16[4,2,64,128]{3,2,1,0:T(8,128)(2,1)S(1)}, bf16[4,2,64,128]{3,2,1,0:T(8,128)(2,1)S(1)}, u32[]{:S(2)}, u32[]{:S(2)}) collective-permute-start(bf16[4,2,64,128]{3,2,1,0:T(8,128)(2,1)S(1)} %get-tuple-element.99), channel_id=1, source_target_pairs={{0,1},{1,2},{2,3},{3,4},{4,5},{5,6},{6,7},{8,9},{9,10},{10,11},{11... | collective-permute-start | bytes 393224 | tf_op jit(solution)/shard_map/ppermute | solution.py:70
  43.8 1.9 %collective-permute-start.13 = (bf16[4,2,64,128]{3,2,1,0:T(8,128)(2,1)S(1)}, bf16[4,2,64,128]{3,2,1,0:T(8,128)(2,1)S(1)}, u32[]{:S(2)}, u32[]{:S(2)}) collective-permute-start(bf16[4,2,64,128]{3,2,1,0:T(8,128)(2,1)S(1)} %get-tuple-element.100), channel_id=1, source_target_pairs={{1,0},{2,1},{3,2},{4,3},{5,4},{6,5},{7,6},{9,8},{10,9},{11,10},{12... | collective-permute-start | bytes 393224 | tf_op jit(solution)/shard_map/ppermute | solution.py:70
  45.8 4.3 %collective-permute-done.13.refs_9_ = bf16[4,2,64,128]{3,2,1,0:T(8,128)(2,1)S(1)} collective-permute-done((bf16[4,2,64,128]{3,2,1,0:T(8,128)(2,1)S(1)}, bf16[4,2,64,128]{3,2,1,0:T(8,128)(2,1)S(1)}, u32[]{:S(2)}, u32[]{:S(2)}) %collective-permute-start.13) | collective-permute-done | bytes 131104 | tf_op jit(solution)/shard_map/ppermute | solution.py:70
  50.1 0.4 collective-permute-start.14
  50.5 1.2 %collective-permute-start.15 = (bf16[6,1,32,2,128]{4,3,2,1,0:T(2,128)(2,1)S(1)}, bf16[6,1,32,2,128]{4,3,2,1,0:T(2,128)(2,1)S(1)}, u32[]{:S(2)}, u32[]{:S(2)}) collective-permute-start(bf16[6,1,32,2,128]{4,3,2,1,0:T(2,128)(2,1)S(1)} %get-tuple-element.109), channel_id=1, source_target_pairs={{0,8},{8,0},{16,24},{24,16},{1,9},{9,1},{17,25},{25,17},{2,10},{10... | collective-permute-start | bytes 294920 | tf_op jit(solution)/shard_map/ppermute | solution.py:63
  51.8 1.0 %collective-permute-start.16 = (bf16[6,1,32,2,128]{4,3,2,1,0:T(2,128)(2,1)S(1)}, bf16[6,1,32,2,128]{4,3,2,1,0:T(2,128)(2,1)S(1)}, u32[]{:S(2)}, u32[]{:S(2)}) collective-permute-start(bf16[6,1,32,2,128]{4,3,2,1,0:T(2,128)(2,1)S(1)} %get-tuple-element.110), channel_id=1, source_target_pairs={{0,16},{8,24},{16,0},{24,8},{1,17},{9,25},{17,1},{25,9},{2,18},{10... | collective-permute-start | bytes 294920 | tf_op jit(solution)/shard_map/ppermute | solution.py:63
  52.8 1.3 %shard_map.109 = (bf16[3,3,64,128]{3,2,1,0:T(8,128)(2,1)S(1)}, bf16[3,3,64,128]{3,2,1,0:T(8,128)(2,1)S(1)}, bf16[3,3,64,128]{3,2,1,0:T(8,128)(2,1)S(1)}, bf16[3,3,64,128]{3,2,1,0:T(8,128)(2,1)S(1)}) custom-call(bf16[6,3,64,128]{3,2,1,0:T(8,128)(2,1)S(1)} %bitcast.28, bf16[6,3,64,128]{3,2,1,0:T(8,128)(2,1)S(1)} %bitcast.29, ...), custom_call_target="tpu_custom_call" | custom-call | flops 1024 | bytes 1024 | tf_op jit(solution)/shard_map/pallas_call | solution.py:284
  54.1 0.3 collective-permute-start.20
  54.4 0.5 collective-permute-start.21
  54.9 1.9 %collective-permute-start.22 = (bf16[3,3,64,128]{3,2,1,0:T(8,128)(2,1)S(1)}, bf16[3,3,64,128]{3,2,1,0:T(8,128)(2,1)S(1)}, u32[]{:S(2)}, u32[]{:S(2)}) collective-permute-start(bf16[3,3,64,128]{3,2,1,0:T(8,128)(2,1)S(1)} %get-tuple-element.126), channel_id=1, source_target_pairs={{0,24},{8,16},{16,8},{24,0},{1,25},{9,17},{17,9},{25,1},{2,26},{10... | collective-permute-start | bytes 442376 | tf_op jit(solution)/shard_map/ppermute | solution.py:63
  56.9 0.7 %shard_map.107 = (bf16[3,1,64,128]{3,2,1,0:T(8,128)(2,1)S(1)}, bf16[3,1,64,128]{3,2,1,0:T(8,128)(2,1)S(1)}, bf16[3,1,64,128]{3,2,1,0:T(8,128)(2,1)S(1)}, bf16[3,1,64,128]{3,2,1,0:T(8,128)(2,1)S(1)}) custom-call(bf16[6,1,64,128]{3,2,1,0:T(8,128)(2,1)S(1)} %bitcast.40, bf16[6,1,64,128]{3,2,1,0:T(8,128)(2,1)S(1)} %bitcast.41, ...), custom_call_target="tpu_custom_call" | custom-call | flops 1024 | bytes 1024 | tf_op jit(solution)/shard_map/pallas_call | solution.py:284
  57.6 0.3 collective-permute-start.23
  57.9 0.5 collective-permute-start.24
  58.4 4.3 %collective-permute-done.23.refs_5_ = bf16[3,1,64,128]{3,2,1,0:T(8,128)(2,1)S(1)} collective-permute-done((bf16[3,1,64,128]{3,2,1,0:T(8,128)(2,1)S(1)}, bf16[3,1,64,128]{3,2,1,0:T(8,128)(2,1)S(1)}, u32[]{:S(2)}, u32[]{:S(2)}) %collective-permute-start.23) | collective-permute-done | bytes 49184 | tf_op jit(solution)/shard_map/ppermute | solution.py:63
  62.7 1.0 %collective-permute-start.25 = (bf16[3,1,64,128]{3,2,1,0:T(8,128)(2,1)S(1)}, bf16[3,1,64,128]{3,2,1,0:T(8,128)(2,1)S(1)}, u32[]{:S(2)}, u32[]{:S(2)}) collective-permute-start(bf16[3,1,64,128]{3,2,1,0:T(8,128)(2,1)S(1)} %get-tuple-element.130), channel_id=1, source_target_pairs={{0,24},{8,16},{16,8},{24,0},{1,25},{9,17},{17,9},{25,1},{2,26},{10... | collective-permute-start | bytes 147464 | tf_op jit(solution)/shard_map/ppermute | solution.py:63
  63.7 5.0 %shard_map.108 = (f32[3072,128]{1,0:T(8,128)}, f32[3,16,64,128]{3,2,1,0:T(8,128)S(1)}) custom-call(bf16[4,2,64,128]{3,2,1,0:T(8,128)(2,1)S(1)} %get-tuple-element.91.refs_0_, bf16[4,2,64,128]{3,2,1,0:T(8,128)(2,1)S(1)} %collective-permute-done.3.refs_1_, bf16[4,2,64,128]{3,2,1,0:T(8,128)(2,1)S(1)} %collective-permute-done.4.refs_2_, ...), custom_call_target="tpu_custom_call" | custom-call | flops 1024 | bytes 1024 | tf_op jit(solution)/shard_map/pallas_call | solution.py:446
  68.7 1.6 %shard_map.110 = f32[3072,128]{1,0:T(8,128)} custom-call(bf16[3,3,64,128]{3,2,1,0:T(8,128)(2,1)S(1)} %get-tuple-element.123.refs_0_, bf16[3,3,64,128]{3,2,1,0:T(8,128)(2,1)S(1)} %collective-permute-done.20.refs_1_, bf16[3,3,64,128]{3,2,1,0:T(8,128)(2,1)S(1)} %collective-permute-done.21.refs_2_, bf16[3,3,64,128]{3,2,1,0:T(8,128)(2,1)S(1)} %collective-permute-done.22.refs_3_, ...), custom_call_target="tpu_custom_call" | custom-call | flops 1024 | bytes 1024 | tf_op jit(solution)/shard_map/pallas_call | solution.py:490
  (36 shorter events, 0.5 us)
Async XLA Ops:
  2.2 7.7 %collective-permute-start.6 = (bf16[6,2,32,2,128]{4,3,2,1,0:T(2,128)(2,1)S(1)}, bf16[6,2,32,2,128]{4,3,2,1,0:T(2,128)(2,1)S(1)}, u32[]{:S(2)}, u32[]{:S(2)}) collective-permute-start(bf16[6,2,32,2,128]{4,3,2,1,0:T(2,128)(2,1)S(1)} %shard_map.102), channel_id=1, source_target_pairs={{0,24},{8,16},{16,8},{24,0},{1,25},{9,17},{17,9},{25,1},{2,26},{10... | collective-permute-start | bytes 589832 | tf_op jit(solution)/shard_map/ppermute | solution.py:63
  5.4 8.6 %collective-permute-start.7 = (bf16[6,2,32,2,128]{4,3,2,1,0:T(2,128)(2,1)S(1)}, bf16[6,2,32,2,128]{4,3,2,1,0:T(2,128)(2,1)S(1)}, u32[]{:S(2)}, u32[]{:S(2)}) collective-permute-start(bf16[6,2,32,2,128]{4,3,2,1,0:T(2,128)(2,1)S(1)} %shard_map.103), channel_id=1, source_target_pairs={{0,8},{8,0},{16,24},{24,16},{1,9},{9,1},{17,25},{25,17},{2,10},{10... | collective-permute-start | bytes 589832 | tf_op jit(solution)/shard_map/ppermute | solution.py:63
  5.9 8.8 %collective-permute-start.8 = (bf16[6,2,32,2,128]{4,3,2,1,0:T(2,128)(2,1)S(1)}, bf16[6,2,32,2,128]{4,3,2,1,0:T(2,128)(2,1)S(1)}, u32[]{:S(2)}, u32[]{:S(2)}) collective-permute-start(bf16[6,2,32,2,128]{4,3,2,1,0:T(2,128)(2,1)S(1)} %shard_map.104), channel_id=1, source_target_pairs={{0,16},{8,24},{16,0},{24,8},{1,17},{9,25},{17,1},{25,9},{2,18},{10... | collective-permute-start | bytes 589832 | tf_op jit(solution)/shard_map/ppermute | solution.py:63
  6.2 4.8 %copy-start.3 = (bf16[256,256]{1,0:T(8,128)(2,1)S(1)}, bf16[256,256]{1,0:T(8,128)(2,1)}, u32[]{:S(2)}) copy-start(bf16[256,256]{1,0:T(8,128)(2,1)} %constant.5.clone.refs_1_) | copy-start | bytes 393220
  6.2 4.8 %copy-start.4 = (bf16[256,256]{1,0:T(8,128)(2,1)S(1)}, bf16[256,256]{1,0:T(8,128)(2,1)}, u32[]{:S(2)}) copy-start(bf16[256,256]{1,0:T(8,128)(2,1)} %constant.4.clone.refs_0_) | copy-start | bytes 393220
  6.2 12.1 %collective-permute-start.1 = (bf16[6,2,32,2,128]{4,3,2,1,0:T(2,128)(2,1)S(1)}, bf16[6,2,32,2,128]{4,3,2,1,0:T(2,128)(2,1)S(1)}, u32[]{:S(2)}, u32[]{:S(2)}) collective-permute-start(bf16[6,2,32,2,128]{4,3,2,1,0:T(2,128)(2,1)S(1)} %shard_map.98), channel_id=1, source_target_pairs={{0,8},{8,0},{16,24},{24,16},{1,9},{9,1},{17,25},{25,17},{2,10},{10... | collective-permute-start | bytes 589832 | tf_op jit(solution)/shard_map/ppermute | solution.py:63
  7.9 14.7 %collective-permute-start = (bf16[6,2,32,2,128]{4,3,2,1,0:T(2,128)(2,1)S(1)}, bf16[6,2,32,2,128]{4,3,2,1,0:T(2,128)(2,1)S(1)}, u32[]{:S(2)}, u32[]{:S(2)}) collective-permute-start(bf16[6,2,32,2,128]{4,3,2,1,0:T(2,128)(2,1)S(1)} %shard_map.97), channel_id=1, source_target_pairs={{0,24},{8,16},{16,8},{24,0},{1,25},{9,17},{17,9},{25,1},{2,26},{10... | collective-permute-start | bytes 589832 | tf_op jit(solution)/shard_map/ppermute | solution.py:63
  9.1 9.5 %copy-start = (bf16[12,32,2,2048]{3,2,1,0:T(2,128)(2,1)S(1)}, bf16[12,32,2,2048]{3,2,1,0:T(2,128)(2,1)}, u32[]{:S(2)}) copy-start(bf16[12,32,2,2048]{3,2,1,0:T(2,128)(2,1)} %fields_ref.3) | copy-start | bytes 9437188
  9.9 12.6 %collective-permute-start.2 = (bf16[6,2,32,2,128]{4,3,2,1,0:T(2,128)(2,1)S(1)}, bf16[6,2,32,2,128]{4,3,2,1,0:T(2,128)(2,1)S(1)}, u32[]{:S(2)}, u32[]{:S(2)}) collective-permute-start(bf16[6,2,32,2,128]{4,3,2,1,0:T(2,128)(2,1)S(1)} %shard_map.99), channel_id=1, source_target_pairs={{0,16},{8,24},{16,0},{24,8},{1,17},{9,25},{17,1},{25,9},{2,18},{10... | collective-permute-start | bytes 589832 | tf_op jit(solution)/shard_map/ppermute | solution.py:63
  15.5 10.3 %collective-permute-start.9 = (bf16[4,2,64,128]{3,2,1,0:T(8,128)(2,1)S(1)}, bf16[4,2,64,128]{3,2,1,0:T(8,128)(2,1)S(1)}, u32[]{:S(2)}, u32[]{:S(2)}) collective-permute-start(bf16[4,2,64,128]{3,2,1,0:T(8,128)(2,1)S(1)} %get-tuple-element.81), channel_id=1, source_target_pairs={{0,24},{8,16},{16,8},{24,0},{1,25},{9,17},{17,9},{25,1},{2,26},{10... | collective-permute-start | bytes 393224 | tf_op jit(solution)/shard_map/ppermute | solution.py:63
  18.1 10.1 %collective-permute-start.10 = (bf16[4,2,64,128]{3,2,1,0:T(8,128)(2,1)S(1)}, bf16[4,2,64,128]{3,2,1,0:T(8,128)(2,1)S(1)}, u32[]{:S(2)}, u32[]{:S(2)}) collective-permute-start(bf16[4,2,64,128]{3,2,1,0:T(8,128)(2,1)S(1)} %get-tuple-element.82), channel_id=1, source_target_pairs={{0,8},{8,0},{16,24},{24,16},{1,9},{9,1},{17,25},{25,17},{2,10},{10... | collective-permute-start | bytes 393224 | tf_op jit(solution)/shard_map/ppermute | solution.py:63
  18.4 18.8 %copy-start.7 = (s32[2,256]{1,0:T(2,128)S(1)}, s32[2,256]{1,0:T(2,128)}, u32[]{:S(2)}) copy-start(s32[2,256]{1,0:T(2,128)} %refs_8_.1) | copy-start | bytes 6148
  18.4 11.2 %collective-permute-start.11 = (bf16[4,2,64,128]{3,2,1,0:T(8,128)(2,1)S(1)}, bf16[4,2,64,128]{3,2,1,0:T(8,128)(2,1)S(1)}, u32[]{:S(2)}, u32[]{:S(2)}) collective-permute-start(bf16[4,2,64,128]{3,2,1,0:T(8,128)(2,1)S(1)} %get-tuple-element.83), channel_id=1, source_target_pairs={{0,16},{8,24},{16,0},{24,8},{1,17},{9,25},{17,1},{25,9},{2,18},{10... | collective-permute-start | bytes 393224 | tf_op jit(solution)/shard_map/ppermute | solution.py:63
  23.4 8.7 %collective-permute-start.3 = (bf16[4,2,64,128]{3,2,1,0:T(8,128)(2,1)S(1)}, bf16[4,2,64,128]{3,2,1,0:T(8,128)(2,1)S(1)}, u32[]{:S(2)}, u32[]{:S(2)}) collective-permute-start(bf16[4,2,64,128]{3,2,1,0:T(8,128)(2,1)S(1)} %get-tuple-element.76), channel_id=1, source_target_pairs={{0,24},{8,16},{16,8},{24,0},{1,25},{9,17},{17,9},{25,1},{2,26},{10... | collective-permute-start | bytes 393224 | tf_op jit(solution)/shard_map/ppermute | solution.py:63
  25.6 8.2 %collective-permute-start.4 = (bf16[4,2,64,128]{3,2,1,0:T(8,128)(2,1)S(1)}, bf16[4,2,64,128]{3,2,1,0:T(8,128)(2,1)S(1)}, u32[]{:S(2)}, u32[]{:S(2)}) collective-permute-start(bf16[4,2,64,128]{3,2,1,0:T(8,128)(2,1)S(1)} %get-tuple-element.77), channel_id=1, source_target_pairs={{0,8},{8,0},{16,24},{24,16},{1,9},{9,1},{17,25},{25,17},{2,10},{10... | collective-permute-start | bytes 393224 | tf_op jit(solution)/shard_map/ppermute | solution.py:63
  25.8 8.0 %collective-permute-start.5 = (bf16[4,2,64,128]{3,2,1,0:T(8,128)(2,1)S(1)}, bf16[4,2,64,128]{3,2,1,0:T(8,128)(2,1)S(1)}, u32[]{:S(2)}, u32[]{:S(2)}) collective-permute-start(bf16[4,2,64,128]{3,2,1,0:T(8,128)(2,1)S(1)} %get-tuple-element.78), channel_id=1, source_target_pairs={{0,16},{8,24},{16,0},{24,8},{1,17},{9,25},{17,1},{25,9},{2,18},{10... | collective-permute-start | bytes 393224 | tf_op jit(solution)/shard_map/ppermute | solution.py:63
  29.6 22.2 %collective-permute-start.17 = (bf16[6,3,32,2,128]{4,3,2,1,0:T(2,128)(2,1)S(1)}, bf16[6,3,32,2,128]{4,3,2,1,0:T(2,128)(2,1)S(1)}, u32[]{:S(2)}, u32[]{:S(2)}) collective-permute-start(bf16[6,3,32,2,128]{4,3,2,1,0:T(2,128)(2,1)S(1)} %get-tuple-element.120), channel_id=1, source_target_pairs={{0,24},{8,16},{16,8},{24,0},{1,25},{9,17},{17,9},{25,1},{2,26},{10... | collective-permute-start | bytes 884744 | tf_op jit(solution)/shard_map/ppermute | solution.py:63
  33.8 19.0 %collective-permute-start.18 = (bf16[6,3,32,2,128]{4,3,2,1,0:T(2,128)(2,1)S(1)}, bf16[6,3,32,2,128]{4,3,2,1,0:T(2,128)(2,1)S(1)}, u32[]{:S(2)}, u32[]{:S(2)}) collective-permute-start(bf16[6,3,32,2,128]{4,3,2,1,0:T(2,128)(2,1)S(1)} %get-tuple-element.121), channel_id=1, source_target_pairs={{0,8},{8,0},{16,24},{24,16},{1,9},{9,1},{17,25},{25,17},{2,10},{10... | collective-permute-start | bytes 884744 | tf_op jit(solution)/shard_map/ppermute | solution.py:63
  34.9 17.9 %collective-permute-start.19 = (bf16[6,3,32,2,128]{4,3,2,1,0:T(2,128)(2,1)S(1)}, bf16[6,3,32,2,128]{4,3,2,1,0:T(2,128)(2,1)S(1)}, u32[]{:S(2)}, u32[]{:S(2)}) collective-permute-start(bf16[6,3,32,2,128]{4,3,2,1,0:T(2,128)(2,1)S(1)} %get-tuple-element.122), channel_id=1, source_target_pairs={{0,16},{8,24},{16,0},{24,8},{1,17},{9,25},{17,1},{25,9},{2,18},{10... | collective-permute-start | bytes 884744 | tf_op jit(solution)/shard_map/ppermute | solution.py:63
  38.4 7.3 %collective-permute-start.12 = (bf16[4,2,64,128]{3,2,1,0:T(8,128)(2,1)S(1)}, bf16[4,2,64,128]{3,2,1,0:T(8,128)(2,1)S(1)}, u32[]{:S(2)}, u32[]{:S(2)}) collective-permute-start(bf16[4,2,64,128]{3,2,1,0:T(8,128)(2,1)S(1)} %get-tuple-element.99), channel_id=1, source_target_pairs={{0,1},{1,2},{2,3},{3,4},{4,5},{5,6},{6,7},{8,9},{9,10},{10,11},{11... | collective-permute-start | bytes 393224 | tf_op jit(solution)/shard_map/ppermute | solution.py:70
  43.8 6.3 %collective-permute-start.13 = (bf16[4,2,64,128]{3,2,1,0:T(8,128)(2,1)S(1)}, bf16[4,2,64,128]{3,2,1,0:T(8,128)(2,1)S(1)}, u32[]{:S(2)}, u32[]{:S(2)}) collective-permute-start(bf16[4,2,64,128]{3,2,1,0:T(8,128)(2,1)S(1)} %get-tuple-element.100), channel_id=1, source_target_pairs={{1,0},{2,1},{3,2},{4,3},{5,4},{6,5},{7,6},{9,8},{10,9},{11,10},{12... | collective-permute-start | bytes 393224 | tf_op jit(solution)/shard_map/ppermute | solution.py:70
  50.1 4.8 %collective-permute-start.14 = (bf16[6,1,32,2,128]{4,3,2,1,0:T(2,128)(2,1)S(1)}, bf16[6,1,32,2,128]{4,3,2,1,0:T(2,128)(2,1)S(1)}, u32[]{:S(2)}, u32[]{:S(2)}) collective-permute-start(bf16[6,1,32,2,128]{4,3,2,1,0:T(2,128)(2,1)S(1)} %get-tuple-element.108), channel_id=1, source_target_pairs={{0,24},{8,16},{16,8},{24,0},{1,25},{9,17},{17,9},{25,1},{2,26},{10... | collective-permute-start | bytes 294920 | tf_op jit(solution)/shard_map/ppermute | solution.py:63
  50.5 6.3 %collective-permute-start.15 = (bf16[6,1,32,2,128]{4,3,2,1,0:T(2,128)(2,1)S(1)}, bf16[6,1,32,2,128]{4,3,2,1,0:T(2,128)(2,1)S(1)}, u32[]{:S(2)}, u32[]{:S(2)}) collective-permute-start(bf16[6,1,32,2,128]{4,3,2,1,0:T(2,128)(2,1)S(1)} %get-tuple-element.109), channel_id=1, source_target_pairs={{0,8},{8,0},{16,24},{24,16},{1,9},{9,1},{17,25},{25,17},{2,10},{10... | collective-permute-start | bytes 294920 | tf_op jit(solution)/shard_map/ppermute | solution.py:63
  51.8 5.1 %collective-permute-start.16 = (bf16[6,1,32,2,128]{4,3,2,1,0:T(2,128)(2,1)S(1)}, bf16[6,1,32,2,128]{4,3,2,1,0:T(2,128)(2,1)S(1)}, u32[]{:S(2)}, u32[]{:S(2)}) collective-permute-start(bf16[6,1,32,2,128]{4,3,2,1,0:T(2,128)(2,1)S(1)} %get-tuple-element.110), channel_id=1, source_target_pairs={{0,16},{8,24},{16,0},{24,8},{1,17},{9,25},{17,1},{25,9},{2,18},{10... | collective-permute-start | bytes 294920 | tf_op jit(solution)/shard_map/ppermute | solution.py:63
  54.1 14.6 %collective-permute-start.20 = (bf16[3,3,64,128]{3,2,1,0:T(8,128)(2,1)S(1)}, bf16[3,3,64,128]{3,2,1,0:T(8,128)(2,1)S(1)}, u32[]{:S(2)}, u32[]{:S(2)}) collective-permute-start(bf16[3,3,64,128]{3,2,1,0:T(8,128)(2,1)S(1)} %get-tuple-element.124), channel_id=1, source_target_pairs={{0,8},{8,0},{16,24},{24,16},{1,9},{9,1},{17,25},{25,17},{2,10},{10... | collective-permute-start | bytes 442376 | tf_op jit(solution)/shard_map/ppermute | solution.py:63
  54.4 14.3 %collective-permute-start.21 = (bf16[3,3,64,128]{3,2,1,0:T(8,128)(2,1)S(1)}, bf16[3,3,64,128]{3,2,1,0:T(8,128)(2,1)S(1)}, u32[]{:S(2)}, u32[]{:S(2)}) collective-permute-start(bf16[3,3,64,128]{3,2,1,0:T(8,128)(2,1)S(1)} %get-tuple-element.125), channel_id=1, source_target_pairs={{0,16},{8,24},{16,0},{24,8},{1,17},{9,25},{17,1},{25,9},{2,18},{10... | collective-permute-start | bytes 442376 | tf_op jit(solution)/shard_map/ppermute | solution.py:63
  54.9 13.8 %collective-permute-start.22 = (bf16[3,3,64,128]{3,2,1,0:T(8,128)(2,1)S(1)}, bf16[3,3,64,128]{3,2,1,0:T(8,128)(2,1)S(1)}, u32[]{:S(2)}, u32[]{:S(2)}) collective-permute-start(bf16[3,3,64,128]{3,2,1,0:T(8,128)(2,1)S(1)} %get-tuple-element.126), channel_id=1, source_target_pairs={{0,24},{8,16},{16,8},{24,0},{1,25},{9,17},{17,9},{25,1},{2,26},{10... | collective-permute-start | bytes 442376 | tf_op jit(solution)/shard_map/ppermute | solution.py:63
  56.8 6.8 %copy-start.1 = (bf16[5,64,2048]{2,1,0:T(8,128)(2,1)S(1)}, bf16[5,64,2048]{2,1,0:T(8,128)(2,1)}, u32[]{:S(2)}) copy-start(bf16[5,64,2048]{2,1,0:T(8,128)(2,1)} %refs_10_.1) | copy-start | bytes 3932164
  56.8 6.8 %copy-start.2 = (bf16[5,64,2048]{2,1,0:T(8,128)(2,1)S(1)}, bf16[5,64,2048]{2,1,0:T(8,128)(2,1)}, u32[]{:S(2)}) copy-start(bf16[5,64,2048]{2,1,0:T(8,128)(2,1)} %refs_11_.1) | copy-start | bytes 3932164
  56.8 6.8 %copy-start.5 = (f32[2048]{0:T(1024)S(1)}, f32[2048]{0:T(1024)}, u32[]{:S(2)}) copy-start(f32[2048]{0:T(1024)} %param.9) | copy-start | bytes 24580
  56.9 6.8 %copy-start.6 = (s32[32,5]{0,1:T(8,128)S(1)}, s32[32,5]{0,1:T(8,128)}, u32[]{:S(2)}) copy-start(s32[32,5]{0,1:T(8,128)} %param.12) | copy-start | bytes 1924
  57.6 5.1 %collective-permute-start.23 = (bf16[3,1,64,128]{3,2,1,0:T(8,128)(2,1)S(1)}, bf16[3,1,64,128]{3,2,1,0:T(8,128)(2,1)S(1)}, u32[]{:S(2)}, u32[]{:S(2)}) collective-permute-start(bf16[3,1,64,128]{3,2,1,0:T(8,128)(2,1)S(1)} %get-tuple-element.128), channel_id=1, source_target_pairs={{0,8},{8,0},{16,24},{24,16},{1,9},{9,1},{17,25},{25,17},{2,10},{10... | collective-permute-start | bytes 147464 | tf_op jit(solution)/shard_map/ppermute | solution.py:63
  57.9 10.8 %collective-permute-start.24 = (bf16[3,1,64,128]{3,2,1,0:T(8,128)(2,1)S(1)}, bf16[3,1,64,128]{3,2,1,0:T(8,128)(2,1)S(1)}, u32[]{:S(2)}, u32[]{:S(2)}) collective-permute-start(bf16[3,1,64,128]{3,2,1,0:T(8,128)(2,1)S(1)} %get-tuple-element.129), channel_id=1, source_target_pairs={{0,16},{8,24},{16,0},{24,8},{1,17},{9,25},{17,1},{25,9},{2,18},{10... | collective-permute-start | bytes 147464 | tf_op jit(solution)/shard_map/ppermute | solution.py:63
  62.7 6.0 %collective-permute-start.25 = (bf16[3,1,64,128]{3,2,1,0:T(8,128)(2,1)S(1)}, bf16[3,1,64,128]{3,2,1,0:T(8,128)(2,1)S(1)}, u32[]{:S(2)}, u32[]{:S(2)}) collective-permute-start(bf16[3,1,64,128]{3,2,1,0:T(8,128)(2,1)S(1)} %get-tuple-element.130), channel_id=1, source_target_pairs={{0,24},{8,16},{16,8},{24,0},{1,25},{9,17},{17,9},{25,1},{2,26},{10... | collective-permute-start | bytes 147464 | tf_op jit(solution)/shard_map/ppermute | solution.py:63

commit v17 on v15

--- a/solution.py
+++ b/solution.py
@@ -527,10 +527,11 @@
         *terms, velocity_magnetic = first_physics(joined([own[group]] + arrived[group]), *tables_here)
         local += exchange(terms, offsets(count, FIRST_RETURN))
         physical.append(velocity_magnetic)
-    for group in range(groups):
-        held, sent = slice(count if group == 0 else 0, None), slice(1, 2) if group == 0 else slice(2, None)
-        local[held], shares[sent] = lax.optimization_barrier((local[held], shares[sent]))
-    sources = exchange(shares, order)
+    arrived[0][0], shares[1] = lax.optimization_barrier((arrived[0][0], shares[1]))
+    sources = exchange(shares[:2], order[:2])
+    local, shares[2:] = lax.optimization_barrier((local, shares[2:]))
+    sources += exchange(shares[2:], order[2:])
+    local, sources[1] = lax.optimization_barrier((local, sources[1]))
     toward_prev, toward_next = interface(local, interface_nodes, count)
     halos = (from_behind(toward_next, "mer", 1), from_behind(toward_prev, "mer", -1))
     sources, halos = lax.optimization_barrier((sources, halos))

time: 67.5 us -> 71.5 us (1.059)
  the two profiles are of different devices: /device:TPU:0 before, /device:TPU:1 now
where the time goes in v17:
time: 71.5 us; the launch traced here: 71 us
  waiting for transfers between devices  29.7 us (42%)
  starting transfers between devices  25.7 us (36%)
  Pallas kernels  14.8 us (21%)
  between operations  0.82 us (1%)
    ppermute x18, waiting for transfers between devices, exchange(): received.append(lax.ppermute(piece, 'mode', pairs))  25.3 us
    ppermute x18, starting transfers between devices, exchange(): received.append(lax.ppermute(piece, 'mode', pairs))  19.5 us
    ppermute x2, starting transfers between devices, from_behind(): lax.ppermute(value, axis, [(source, source + steps) for source in range(i...  6.22 us
    pallas_call x1, Pallas kernels, derive(): pl.pallas_call(functools.partial(derive_kernel, count, len(received)), in...  5.02 us
    ppermute x2, waiting for transfers between devices, from_behind(): lax.ppermute(value, axis, [(source, source + steps) for source in range(i...  4.35 us
    pallas_call x2, Pallas kernels, first_physics(): pl.pallas_call(functools.partial(first_kernel, count), in_specs=[vmem()]...  1.63 us
    pallas_call x2, Pallas kernels, pack_rest(): pl.pallas_call(kernel, in_specs=[pl.BlockSpec(memory_space=pl.ANY)] + [vm...  1.62 us
    pallas_call x1, Pallas kernels, second_physics(): pl.pallas_call(functools.partial(second_kernel, count, groups), in_specs=...  1.58 us
  transfers between devices with their start and end apart: 20, of which 12 were waited for; matrix products, arithmetic and copies ran while one was open for 0% of the time, Pallas kernels for 15%

profile of v17, /device:TPU:1, one launch (start us, length us, event | category | flops | bytes accessed | tf_op | source)
XLA Modules:
  0.0 71.0 jit_solution(8495354752446095373)
XLA Ops:
  0.6 1.4 %shard_map.95.fields_ref = bf16[6,32,2,2048]{3,2,1,0:T(2,128)(2,1)S(1)} custom-call(bf16[12,32,2,2048]{3,2,1,0:T(2,128)(2,1)} %fields_ref.3), custom_call_target="tpu_custom_call" | custom-call | flops 1024 | bytes 1024 | tf_op jit(solution)/shard_map/pallas_call | solution.py:119
  2.0 0.2 shard_map.102
  2.2 3.1 %collective-permute-start.6 = (bf16[6,2,32,2,128]{4,3,2,1,0:T(2,128)(2,1)S(1)}, bf16[6,2,32,2,128]{4,3,2,1,0:T(2,128)(2,1)S(1)}, u32[]{:S(2)}, u32[]{:S(2)}) collective-permute-start(bf16[6,2,32,2,128]{4,3,2,1,0:T(2,128)(2,1)S(1)} %shard_map.102), channel_id=1, source_target_pairs={{0,24},{8,16},{16,8},{24,0},{1,25},{9,17},{17,9},{25,1},{2,26},{10... | collective-permute-start | bytes 589832 | tf_op jit(solution)/shard_map/ppermute | solution.py:63
  5.3 0.2 shard_map.103
  5.4 0.3 collective-permute-start.7
  5.8 0.2 shard_map.104
  5.9 0.1 collective-permute-start.8
  6.1 0.2 shard_map.98
  6.2 0.0 copy-start.3
  6.2 1.4 %collective-permute-start.1 = (bf16[6,2,32,2,128]{4,3,2,1,0:T(2,128)(2,1)S(1)}, bf16[6,2,32,2,128]{4,3,2,1,0:T(2,128)(2,1)S(1)}, u32[]{:S(2)}, u32[]{:S(2)}) collective-permute-start(bf16[6,2,32,2,128]{4,3,2,1,0:T(2,128)(2,1)S(1)} %shard_map.98), channel_id=1, source_target_pairs={{0,8},{8,0},{16,24},{24,16},{1,9},{9,1},{17,25},{25,17},{2,10},{10... | collective-permute-start | bytes 589832 | tf_op jit(solution)/shard_map/ppermute | solution.py:63
  7.7 0.2 shard_map.97
  7.9 1.3 %collective-permute-start = (bf16[6,2,32,2,128]{4,3,2,1,0:T(2,128)(2,1)S(1)}, bf16[6,2,32,2,128]{4,3,2,1,0:T(2,128)(2,1)S(1)}, u32[]{:S(2)}, u32[]{:S(2)}) collective-permute-start(bf16[6,2,32,2,128]{4,3,2,1,0:T(2,128)(2,1)S(1)} %shard_map.97), channel_id=1, source_target_pairs={{0,24},{8,16},{16,8},{24,0},{1,25},{9,17},{17,9},{25,1},{2,26},{10... | collective-permute-start | bytes 589832 | tf_op jit(solution)/shard_map/ppermute | solution.py:63
  9.1 0.2 shard_map.99
  9.3 0.6 collective-permute-done.6
  9.9 1.2 %collective-permute-start.2 = (bf16[6,2,32,2,128]{4,3,2,1,0:T(2,128)(2,1)S(1)}, bf16[6,2,32,2,128]{4,3,2,1,0:T(2,128)(2,1)S(1)}, u32[]{:S(2)}, u32[]{:S(2)}) collective-permute-start(bf16[6,2,32,2,128]{4,3,2,1,0:T(2,128)(2,1)S(1)} %shard_map.99), channel_id=1, source_target_pairs={{0,16},{8,24},{16,0},{24,8},{1,17},{9,25},{17,1},{25,9},{2,18},{10... | collective-permute-start | bytes 589832 | tf_op jit(solution)/shard_map/ppermute | solution.py:63
  11.1 0.3 shard_map.96
  11.4 2.7 %collective-permute-done.7 = bf16[6,2,32,2,128]{4,3,2,1,0:T(2,128)(2,1)S(1)} collective-permute-done((bf16[6,2,32,2,128]{4,3,2,1,0:T(2,128)(2,1)S(1)}, bf16[6,2,32,2,128]{4,3,2,1,0:T(2,128)(2,1)S(1)}, u32[]{:S(2)}, u32[]{:S(2)}) %collective-permute-start.7) | collective-permute-done | bytes 196640 | tf_op jit(solution)/shard_map/ppermute | solution.py:63
  14.1 0.6 collective-permute-done.8
  14.7 0.8 %shard_map.105 = (bf16[4,2,64,128]{3,2,1,0:T(8,128)(2,1)S(1)}, bf16[4,2,64,128]{3,2,1,0:T(8,128)(2,1)S(1)}, bf16[4,2,64,128]{3,2,1,0:T(8,128)(2,1)S(1)}, bf16[4,...) custom-call(bf16[6,2,64,128]{3,2,1,0:T(8,128)(2,1)S(1)} %bitcast.35, bf16[6,2,64,128]{3,2,1,0:T(8,128)(2,1)S(1)} %bitcast.32, ...), custom_call_target="tpu_custom_call" | custom-call | flops 1024 | bytes 1024 | tf_op jit(solution)/shard_map/pallas_call | solution.py:235
  15.5 2.6 %collective-permute-start.9 = (bf16[4,2,64,128]{3,2,1,0:T(8,128)(2,1)S(1)}, bf16[4,2,64,128]{3,2,1,0:T(8,128)(2,1)S(1)}, u32[]{:S(2)}, u32[]{:S(2)}) collective-permute-start(bf16[4,2,64,128]{3,2,1,0:T(8,128)(2,1)S(1)} %get-tuple-element.78), channel_id=1, source_target_pairs={{0,24},{8,16},{16,8},{24,0},{1,25},{9,17},{17,9},{25,1},{2,26},{10... | collective-permute-start | bytes 393224 | tf_op jit(solution)/shard_map/ppermute | solution.py:63
  18.1 0.2 collective-permute-start.10
  18.4 0.3 collective-permute-start.11
  18.6 1.3 %shard_map.100 = (bf16[6,4,32,2,128]{4,3,2,1,0:T(2,128)(2,1)S(1)}, bf16[6,4,32,2,128]{4,3,2,1,0:T(2,128)(2,1)S(1)}, bf16[6,4,32,2,128]{4,3,2,1,0:T(2,128)(2,1)S(...) custom-call(bf16[12,32,2,2048]{3,2,1,0:T(2,128)(2,1)S(1)} %copy-done, ...), custom_call_target="tpu_custom_call" | custom-call | flops 1024 | bytes 1024 | tf_op jit(solution)/shard_map/pallas_call | solution.py:167
  19.9 2.6 %collective-permute-done = bf16[6,2,32,2,128]{4,3,2,1,0:T(2,128)(2,1)S(1)} collective-permute-done((bf16[6,2,32,2,128]{4,3,2,1,0:T(2,128)(2,1)S(1)}, bf16[6,2,32,2,128]{4,3,2,1,0:T(2,128)(2,1)S(1)}, u32[]{:S(2)}, u32[]{:S(2)}) %collective-permute-start) | collective-permute-done | bytes 196640 | tf_op jit(solution)/shard_map/ppermute | solution.py:63
  22.5 2.1 %collective-permute-start.12 = (bf16[6,4,32,2,128]{4,3,2,1,0:T(2,128)(2,1)S(1)}, bf16[6,4,32,2,128]{4,3,2,1,0:T(2,128)(2,1)S(1)}, u32[]{:S(2)}, u32[]{:S(2)}) collective-permute-start(bf16[6,4,32,2,128]{4,3,2,1,0:T(2,128)(2,1)S(1)} %get-tuple-element.92), channel_id=1, source_target_pairs={{0,24},{8,16},{16,8},{24,0},{1,25},{9,17},{17,9},{25,1},{2,26},{10... | collective-permute-start | bytes 1179656 | tf_op jit(solution)/shard_map/ppermute | solution.py:63
  24.7 0.8 %shard_map.101 = (bf16[4,2,64,128]{3,2,1,0:T(8,128)(2,1)S(1)}, bf16[4,2,64,128]{3,2,1,0:T(8,128)(2,1)S(1)}, bf16[4,2,64,128]{3,2,1,0:T(8,128)(2,1)S(1)}, bf16[4,...) custom-call(bf16[6,2,64,128]{3,2,1,0:T(8,128)(2,1)S(1)} %bitcast.31, bf16[6,2,64,128]{3,2,1,0:T(8,128)(2,1)S(1)} %bitcast.29, ...), custom_call_target="tpu_custom_call" | custom-call | flops 1024 | bytes 1024 | tf_op jit(solution)/shard_map/pallas_call | solution.py:235
  25.5 0.3 collective-permute-start.3
  25.8 1.1 %collective-permute-start.4 = (bf16[4,2,64,128]{3,2,1,0:T(8,128)(2,1)S(1)}, bf16[4,2,64,128]{3,2,1,0:T(8,128)(2,1)S(1)}, u32[]{:S(2)}, u32[]{:S(2)}) collective-permute-start(bf16[4,2,64,128]{3,2,1,0:T(8,128)(2,1)S(1)} %get-tuple-element.74), channel_id=1, source_target_pairs={{0,8},{8,0},{16,24},{24,16},{1,9},{9,1},{17,25},{25,17},{2,10},{10... | collective-permute-start | bytes 393224 | tf_op jit(solution)/shard_map/ppermute | solution.py:63
  26.9 1.3 %collective-permute-done.10.refs_6_ = bf16[4,2,64,128]{3,2,1,0:T(8,128)(2,1)S(1)} collective-permute-done((bf16[4,2,64,128]{3,2,1,0:T(8,128)(2,1)S(1)}, bf16[4,2,64,128]{3,2,1,0:T(8,128)(2,1)S(1)}, u32[]{:S(2)}, u32[]{:S(2)}) %collective-permute-start.10) | collective-permute-done | bytes 131104 | tf_op jit(solution)/shard_map/ppermute | solution.py:63
  28.2 0.3 collective-permute-start.5
  28.5 1.1 %collective-permute-done.11.refs_7_ = bf16[4,2,64,128]{3,2,1,0:T(8,128)(2,1)S(1)} collective-permute-done((bf16[4,2,64,128]{3,2,1,0:T(8,128)(2,1)S(1)}, bf16[4,2,64,128]{3,2,1,0:T(8,128)(2,1)S(1)}, u32[]{:S(2)}, u32[]{:S(2)}) %collective-permute-start.11) | collective-permute-done | bytes 131104 | tf_op jit(solution)/shard_map/ppermute | solution.py:63
  29.6 9.9 %collective-permute-done.3.refs_1_ = bf16[4,2,64,128]{3,2,1,0:T(8,128)(2,1)S(1)} collective-permute-done((bf16[4,2,64,128]{3,2,1,0:T(8,128)(2,1)S(1)}, bf16[4,2,64,128]{3,2,1,0:T(8,128)(2,1)S(1)}, u32[]{:S(2)}, u32[]{:S(2)}) %collective-permute-start.3) | collective-permute-done | bytes 131104 | tf_op jit(solution)/shard_map/ppermute | solution.py:63
  39.5 2.8 %collective-permute-done.4.refs_2_ = bf16[4,2,64,128]{3,2,1,0:T(8,128)(2,1)S(1)} collective-permute-done((bf16[4,2,64,128]{3,2,1,0:T(8,128)(2,1)S(1)}, bf16[4,2,64,128]{3,2,1,0:T(8,128)(2,1)S(1)}, u32[]{:S(2)}, u32[]{:S(2)}) %collective-permute-start.4) | collective-permute-done | bytes 131104 | tf_op jit(solution)/shard_map/ppermute | solution.py:63
  42.3 0.7 %collective-permute-done.5.refs_3_ = bf16[4,2,64,128]{3,2,1,0:T(8,128)(2,1)S(1)} collective-permute-done((bf16[4,2,64,128]{3,2,1,0:T(8,128)(2,1)S(1)}, bf16[4,2,64,128]{3,2,1,0:T(8,128)(2,1)S(1)}, u32[]{:S(2)}, u32[]{:S(2)}) %collective-permute-start.5) | collective-permute-done | bytes 131104 | tf_op jit(solution)/shard_map/ppermute | solution.py:63
  43.0 1.4 %collective-permute-start.13 = (bf16[6,4,32,2,128]{4,3,2,1,0:T(2,128)(2,1)S(1)}, bf16[6,4,32,2,128]{4,3,2,1,0:T(2,128)(2,1)S(1)}, u32[]{:S(2)}, u32[]{:S(2)}) collective-permute-start(bf16[6,4,32,2,128]{4,3,2,1,0:T(2,128)(2,1)S(1)} %get-tuple-element.103), channel_id=1, source_target_pairs={{0,8},{8,0},{16,24},{24,16},{1,9},{9,1},{17,25},{25,17},{2,10},{10... | collective-permute-start | bytes 1179656 | tf_op jit(solution)/shard_map/ppermute | solution.py:63
  44.4 1.0 %collective-permute-start.14 = (bf16[6,4,32,2,128]{4,3,2,1,0:T(2,128)(2,1)S(1)}, bf16[6,4,32,2,128]{4,3,2,1,0:T(2,128)(2,1)S(1)}, u32[]{:S(2)}, u32[]{:S(2)}) collective-permute-start(bf16[6,4,32,2,128]{4,3,2,1,0:T(2,128)(2,1)S(1)} %get-tuple-element.104), channel_id=1, source_target_pairs={{0,16},{8,24},{16,0},{24,8},{1,17},{9,25},{17,1},{25,9},{2,18},{10... | collective-permute-start | bytes 1179656 | tf_op jit(solution)/shard_map/ppermute | solution.py:63
  45.4 1.2 %shard_map.106 = (bf16[4,2,64,128]{3,2,1,0:T(8,128)(2,1)S(1)}, bf16[4,2,64,128]{3,2,1,0:T(8,128)(2,1)S(1)}) custom-call(bf16[4,2,64,128]{3,2,1,0:T(8,128)(2,1)S(1)} %get-tuple-element.93.refs_0_, bf16[4,2,64,128]{3,2,1,0:T(8,128)(2,1)S(1)} %collective-permute-done.3.refs_1_, bf16[4,2,64,128]{3,2,1,0:T(8,128)(2,1)S(1)} %collective-permute-done.4.refs_2_, ...), custom_call_target="tpu_custom_call" | custom-call | flops 1024 | bytes 1024 | tf_op jit(solution)/shard_map/pallas_call | solution.py:329
  46.7 4.3 %collective-permute-start.15 = (bf16[4,2,64,128]{3,2,1,0:T(8,128)(2,1)S(1)}, bf16[4,2,64,128]{3,2,1,0:T(8,128)(2,1)S(1)}, u32[]{:S(2)}, u32[]{:S(2)}) collective-permute-start(bf16[4,2,64,128]{3,2,1,0:T(8,128)(2,1)S(1)} %get-tuple-element.105), channel_id=1, source_target_pairs={{0,1},{1,2},{2,3},{3,4},{4,5},{5,6},{6,7},{8,9},{9,10},{10,11},{11... | collective-permute-start | bytes 393224 | tf_op jit(solution)/shard_map/ppermute | solution.py:70
  51.0 1.9 %collective-permute-start.16 = (bf16[4,2,64,128]{3,2,1,0:T(8,128)(2,1)S(1)}, bf16[4,2,64,128]{3,2,1,0:T(8,128)(2,1)S(1)}, u32[]{:S(2)}, u32[]{:S(2)}) collective-permute-start(bf16[4,2,64,128]{3,2,1,0:T(8,128)(2,1)S(1)} %get-tuple-element.106), channel_id=1, source_target_pairs={{1,0},{2,1},{3,2},{4,3},{5,4},{6,5},{7,6},{9,8},{10,9},{11,10},{12... | collective-permute-start | bytes 393224 | tf_op jit(solution)/shard_map/ppermute | solution.py:70
  52.9 4.3 %collective-permute-done.16.refs_9_ = bf16[4,2,64,128]{3,2,1,0:T(8,128)(2,1)S(1)} collective-permute-done((bf16[4,2,64,128]{3,2,1,0:T(8,128)(2,1)S(1)}, bf16[4,2,64,128]{3,2,1,0:T(8,128)(2,1)S(1)}, u32[]{:S(2)}, u32[]{:S(2)}) %collective-permute-start.16) | collective-permute-done | bytes 131104 | tf_op jit(solution)/shard_map/ppermute | solution.py:70
  57.3 1.6 %shard_map.107 = (bf16[3,4,64,128]{3,2,1,0:T(8,128)(2,1)S(1)}, bf16[3,4,64,128]{3,2,1,0:T(8,128)(2,1)S(1)}, bf16[3,4,64,128]{3,2,1,0:T(8,128)(2,1)S(1)}, bf16[3,4,64,128]{3,2,1,0:T(8,128)(2,1)S(1)}) custom-call(bf16[6,4,64,128]{3,2,1,0:T(8,128)(2,1)S(1)} %bitcast.24, bf16[6,4,64,128]{3,2,1,0:T(8,128)(2,1)S(1)} %bitcast.25, ...), custom_call_target="tpu_custom_call" | custom-call | flops 1024 | bytes 1024 | tf_op jit(solution)/shard_map/pallas_call | solution.py:279
  58.9 0.3 collective-permute-start.17
  59.2 0.4 collective-permute-start.18
  59.7 2.0 %collective-permute-start.19 = (bf16[3,4,64,128]{3,2,1,0:T(8,128)(2,1)S(1)}, bf16[3,4,64,128]{3,2,1,0:T(8,128)(2,1)S(1)}, u32[]{:S(2)}, u32[]{:S(2)}) collective-permute-start(bf16[3,4,64,128]{3,2,1,0:T(8,128)(2,1)S(1)} %get-tuple-element.124), channel_id=1, source_target_pairs={{0,24},{8,16},{16,8},{24,0},{1,25},{9,17},{17,9},{25,1},{2,26},{10... | collective-permute-start | bytes 589832 | tf_op jit(solution)/shard_map/ppermute | solution.py:63
  61.6 5.0 %shard_map.108 = (f32[3072,128]{1,0:T(8,128)}, f32[3,16,64,128]{3,2,1,0:T(8,128)S(1)}) custom-call(bf16[4,2,64,128]{3,2,1,0:T(8,128)(2,1)S(1)} %get-tuple-element.93.refs_0_, bf16[4,2,64,128]{3,2,1,0:T(8,128)(2,1)S(1)} %collective-permute-done.3.refs_1_, bf16[4,2,64,128]{3,2,1,0:T(8,128)(2,1)S(1)} %collective-permute-done.4.refs_2_, ...), custom_call_target="tpu_custom_call" | custom-call | flops 1024 | bytes 1024 | tf_op jit(solution)/shard_map/pallas_call | solution.py:441
  66.7 1.9 %collective-permute-done.18.refs_2_ = bf16[3,4,64,128]{3,2,1,0:T(8,128)(2,1)S(1)} collective-permute-done((bf16[3,4,64,128]{3,2,1,0:T(8,128)(2,1)S(1)}, bf16[3,4,64,128]{3,2,1,0:T(8,128)(2,1)S(1)}, u32[]{:S(2)}, u32[]{:S(2)}) %collective-permute-start.18) | collective-permute-done | bytes 196640 | tf_op jit(solution)/shard_map/ppermute | solution.py:63
  68.6 1.1 %collective-permute-done.19.refs_3_ = bf16[3,4,64,128]{3,2,1,0:T(8,128)(2,1)S(1)} collective-permute-done((bf16[3,4,64,128]{3,2,1,0:T(8,128)(2,1)S(1)}, bf16[3,4,64,128]{3,2,1,0:T(8,128)(2,1)S(1)}, u32[]{:S(2)}, u32[]{:S(2)}) %collective-permute-start.19) | collective-permute-done | bytes 196640 | tf_op jit(solution)/shard_map/ppermute | solution.py:63
  69.6 1.3 %shard_map.109 = f32[3072,128]{1,0:T(8,128)} custom-call(bf16[3,4,64,128]{3,2,1,0:T(8,128)(2,1)S(1)} %get-tuple-element.121.refs_0_, bf16[3,4,64,128]{3,2,1,0:T(8,128)(2,1)S(1)} %collective-permute-done.17.refs_1_, bf16[3,4,64,128]{3,2,1,0:T(8,128)(2,1)S(1)} %collective-permute-done.18.refs_2_, bf16[3,4,64,128]{3,2,1,0:T(8,128)(2,1)S(1)} %collective-permute-done.19.refs_3_, ...), custom_call_target="tpu_custom_call" | custom-call | flops 1024 | bytes 1024 | tf_op jit(solution)/shard_map/pallas_call | solution.py:483
  (23 shorter events, 0.1 us)
Async XLA Ops:
  2.2 7.7 %collective-permute-start.6 = (bf16[6,2,32,2,128]{4,3,2,1,0:T(2,128)(2,1)S(1)}, bf16[6,2,32,2,128]{4,3,2,1,0:T(2,128)(2,1)S(1)}, u32[]{:S(2)}, u32[]{:S(2)}) collective-permute-start(bf16[6,2,32,2,128]{4,3,2,1,0:T(2,128)(2,1)S(1)} %shard_map.102), channel_id=1, source_target_pairs={{0,24},{8,16},{16,8},{24,0},{1,25},{9,17},{17,9},{25,1},{2,26},{10... | collective-permute-start | bytes 589832 | tf_op jit(solution)/shard_map/ppermute | solution.py:63
  5.4 8.6 %collective-permute-start.7 = (bf16[6,2,32,2,128]{4,3,2,1,0:T(2,128)(2,1)S(1)}, bf16[6,2,32,2,128]{4,3,2,1,0:T(2,128)(2,1)S(1)}, u32[]{:S(2)}, u32[]{:S(2)}) collective-permute-start(bf16[6,2,32,2,128]{4,3,2,1,0:T(2,128)(2,1)S(1)} %shard_map.103), channel_id=1, source_target_pairs={{0,8},{8,0},{16,24},{24,16},{1,9},{9,1},{17,25},{25,17},{2,10},{10... | collective-permute-start | bytes 589832 | tf_op jit(solution)/shard_map/ppermute | solution.py:63
  5.9 8.8 %collective-permute-start.8 = (bf16[6,2,32,2,128]{4,3,2,1,0:T(2,128)(2,1)S(1)}, bf16[6,2,32,2,128]{4,3,2,1,0:T(2,128)(2,1)S(1)}, u32[]{:S(2)}, u32[]{:S(2)}) collective-permute-start(bf16[6,2,32,2,128]{4,3,2,1,0:T(2,128)(2,1)S(1)} %shard_map.104), channel_id=1, source_target_pairs={{0,16},{8,24},{16,0},{24,8},{1,17},{9,25},{17,1},{25,9},{2,18},{10... | collective-permute-start | bytes 589832 | tf_op jit(solution)/shard_map/ppermute | solution.py:63
  6.2 4.8 %copy-start.3 = (bf16[256,256]{1,0:T(8,128)(2,1)S(1)}, bf16[256,256]{1,0:T(8,128)(2,1)}, u32[]{:S(2)}) copy-start(bf16[256,256]{1,0:T(8,128)(2,1)} %constant.5.clone.refs_1_) | copy-start | bytes 393220
  6.2 4.8 %copy-start.4 = (bf16[256,256]{1,0:T(8,128)(2,1)S(1)}, bf16[256,256]{1,0:T(8,128)(2,1)}, u32[]{:S(2)}) copy-start(bf16[256,256]{1,0:T(8,128)(2,1)} %constant.4.clone.refs_0_) | copy-start | bytes 393220
  6.2 12.1 %collective-permute-start.1 = (bf16[6,2,32,2,128]{4,3,2,1,0:T(2,128)(2,1)S(1)}, bf16[6,2,32,2,128]{4,3,2,1,0:T(2,128)(2,1)S(1)}, u32[]{:S(2)}, u32[]{:S(2)}) collective-permute-start(bf16[6,2,32,2,128]{4,3,2,1,0:T(2,128)(2,1)S(1)} %shard_map.98), channel_id=1, source_target_pairs={{0,8},{8,0},{16,24},{24,16},{1,9},{9,1},{17,25},{25,17},{2,10},{10... | collective-permute-start | bytes 589832 | tf_op jit(solution)/shard_map/ppermute | solution.py:63
  7.9 14.7 %collective-permute-start = (bf16[6,2,32,2,128]{4,3,2,1,0:T(2,128)(2,1)S(1)}, bf16[6,2,32,2,128]{4,3,2,1,0:T(2,128)(2,1)S(1)}, u32[]{:S(2)}, u32[]{:S(2)}) collective-permute-start(bf16[6,2,32,2,128]{4,3,2,1,0:T(2,128)(2,1)S(1)} %shard_map.97), channel_id=1, source_target_pairs={{0,24},{8,16},{16,8},{24,0},{1,25},{9,17},{17,9},{25,1},{2,26},{10... | collective-permute-start | bytes 589832 | tf_op jit(solution)/shard_map/ppermute | solution.py:63
  9.1 9.5 %copy-start = (bf16[12,32,2,2048]{3,2,1,0:T(2,128)(2,1)S(1)}, bf16[12,32,2,2048]{3,2,1,0:T(2,128)(2,1)}, u32[]{:S(2)}) copy-start(bf16[12,32,2,2048]{3,2,1,0:T(2,128)(2,1)} %fields_ref.3) | copy-start | bytes 9437188
  9.9 14.8 %collective-permute-start.2 = (bf16[6,2,32,2,128]{4,3,2,1,0:T(2,128)(2,1)S(1)}, bf16[6,2,32,2,128]{4,3,2,1,0:T(2,128)(2,1)S(1)}, u32[]{:S(2)}, u32[]{:S(2)}) collective-permute-start(bf16[6,2,32,2,128]{4,3,2,1,0:T(2,128)(2,1)S(1)} %shard_map.99), channel_id=1, source_target_pairs={{0,16},{8,24},{16,0},{24,8},{1,17},{9,25},{17,1},{25,9},{2,18},{10... | collective-permute-start | bytes 589832 | tf_op jit(solution)/shard_map/ppermute | solution.py:63
  15.5 10.3 %collective-permute-start.9 = (bf16[4,2,64,128]{3,2,1,0:T(8,128)(2,1)S(1)}, bf16[4,2,64,128]{3,2,1,0:T(8,128)(2,1)S(1)}, u32[]{:S(2)}, u32[]{:S(2)}) collective-permute-start(bf16[4,2,64,128]{3,2,1,0:T(8,128)(2,1)S(1)} %get-tuple-element.78), channel_id=1, source_target_pairs={{0,24},{8,16},{16,8},{24,0},{1,25},{9,17},{17,9},{25,1},{2,26},{10... | collective-permute-start | bytes 393224 | tf_op jit(solution)/shard_map/ppermute | solution.py:63
  18.1 10.1 %collective-permute-start.10 = (bf16[4,2,64,128]{3,2,1,0:T(8,128)(2,1)S(1)}, bf16[4,2,64,128]{3,2,1,0:T(8,128)(2,1)S(1)}, u32[]{:S(2)}, u32[]{:S(2)}) collective-permute-start(bf16[4,2,64,128]{3,2,1,0:T(8,128)(2,1)S(1)} %get-tuple-element.79), channel_id=1, source_target_pairs={{0,8},{8,0},{16,24},{24,16},{1,9},{9,1},{17,25},{25,17},{2,10},{10... | collective-permute-start | bytes 393224 | tf_op jit(solution)/shard_map/ppermute | solution.py:63
  18.4 27.1 %copy-start.7 = (s32[2,256]{1,0:T(2,128)S(1)}, s32[2,256]{1,0:T(2,128)}, u32[]{:S(2)}) copy-start(s32[2,256]{1,0:T(2,128)} %refs_8_.1) | copy-start | bytes 6148
  18.4 11.2 %collective-permute-start.11 = (bf16[4,2,64,128]{3,2,1,0:T(8,128)(2,1)S(1)}, bf16[4,2,64,128]{3,2,1,0:T(8,128)(2,1)S(1)}, u32[]{:S(2)}, u32[]{:S(2)}) collective-permute-start(bf16[4,2,64,128]{3,2,1,0:T(8,128)(2,1)S(1)} %get-tuple-element.80), channel_id=1, source_target_pairs={{0,16},{8,24},{16,0},{24,8},{1,17},{9,25},{17,1},{25,9},{2,18},{10... | collective-permute-start | bytes 393224 | tf_op jit(solution)/shard_map/ppermute | solution.py:63
  22.5 22.9 %collective-permute-start.12 = (bf16[6,4,32,2,128]{4,3,2,1,0:T(2,128)(2,1)S(1)}, bf16[6,4,32,2,128]{4,3,2,1,0:T(2,128)(2,1)S(1)}, u32[]{:S(2)}, u32[]{:S(2)}) collective-permute-start(bf16[6,4,32,2,128]{4,3,2,1,0:T(2,128)(2,1)S(1)} %get-tuple-element.92), channel_id=1, source_target_pairs={{0,24},{8,16},{16,8},{24,0},{1,25},{9,17},{17,9},{25,1},{2,26},{10... | collective-permute-start | bytes 1179656 | tf_op jit(solution)/shard_map/ppermute | solution.py:63
  25.5 14.0 %collective-permute-start.3 = (bf16[4,2,64,128]{3,2,1,0:T(8,128)(2,1)S(1)}, bf16[4,2,64,128]{3,2,1,0:T(8,128)(2,1)S(1)}, u32[]{:S(2)}, u32[]{:S(2)}) collective-permute-start(bf16[4,2,64,128]{3,2,1,0:T(8,128)(2,1)S(1)} %get-tuple-element.73), channel_id=1, source_target_pairs={{0,24},{8,16},{16,8},{24,0},{1,25},{9,17},{17,9},{25,1},{2,26},{10... | collective-permute-start | bytes 393224 | tf_op jit(solution)/shard_map/ppermute | solution.py:63
  25.8 16.5 %collective-permute-start.4 = (bf16[4,2,64,128]{3,2,1,0:T(8,128)(2,1)S(1)}, bf16[4,2,64,128]{3,2,1,0:T(8,128)(2,1)S(1)}, u32[]{:S(2)}, u32[]{:S(2)}) collective-permute-start(bf16[4,2,64,128]{3,2,1,0:T(8,128)(2,1)S(1)} %get-tuple-element.74), channel_id=1, source_target_pairs={{0,8},{8,0},{16,24},{24,16},{1,9},{9,1},{17,25},{25,17},{2,10},{10... | collective-permute-start | bytes 393224 | tf_op jit(solution)/shard_map/ppermute | solution.py:63
  28.2 14.8 %collective-permute-start.5 = (bf16[4,2,64,128]{3,2,1,0:T(8,128)(2,1)S(1)}, bf16[4,2,64,128]{3,2,1,0:T(8,128)(2,1)S(1)}, u32[]{:S(2)}, u32[]{:S(2)}) collective-permute-start(bf16[4,2,64,128]{3,2,1,0:T(8,128)(2,1)S(1)} %get-tuple-element.75), channel_id=1, source_target_pairs={{0,16},{8,24},{16,0},{24,8},{1,17},{9,25},{17,1},{25,9},{2,18},{10... | collective-permute-start | bytes 393224 | tf_op jit(solution)/shard_map/ppermute | solution.py:63
  43.0 14.3 %collective-permute-start.13 = (bf16[6,4,32,2,128]{4,3,2,1,0:T(2,128)(2,1)S(1)}, bf16[6,4,32,2,128]{4,3,2,1,0:T(2,128)(2,1)S(1)}, u32[]{:S(2)}, u32[]{:S(2)}) collective-permute-start(bf16[6,4,32,2,128]{4,3,2,1,0:T(2,128)(2,1)S(1)} %get-tuple-element.103), channel_id=1, source_target_pairs={{0,8},{8,0},{16,24},{24,16},{1,9},{9,1},{17,25},{25,17},{2,10},{10... | collective-permute-start | bytes 1179656 | tf_op jit(solution)/shard_map/ppermute | solution.py:63
  44.4 12.9 %collective-permute-start.14 = (bf16[6,4,32,2,128]{4,3,2,1,0:T(2,128)(2,1)S(1)}, bf16[6,4,32,2,128]{4,3,2,1,0:T(2,128)(2,1)S(1)}, u32[]{:S(2)}, u32[]{:S(2)}) collective-permute-start(bf16[6,4,32,2,128]{4,3,2,1,0:T(2,128)(2,1)S(1)} %get-tuple-element.104), channel_id=1, source_target_pairs={{0,16},{8,24},{16,0},{24,8},{1,17},{9,25},{17,1},{25,9},{2,18},{10... | collective-permute-start | bytes 1179656 | tf_op jit(solution)/shard_map/ppermute | solution.py:63
  46.7 6.2 %collective-permute-start.15 = (bf16[4,2,64,128]{3,2,1,0:T(8,128)(2,1)S(1)}, bf16[4,2,64,128]{3,2,1,0:T(8,128)(2,1)S(1)}, u32[]{:S(2)}, u32[]{:S(2)}) collective-permute-start(bf16[4,2,64,128]{3,2,1,0:T(8,128)(2,1)S(1)} %get-tuple-element.105), channel_id=1, source_target_pairs={{0,1},{1,2},{2,3},{3,4},{4,5},{5,6},{6,7},{8,9},{9,10},{10,11},{11... | collective-permute-start | bytes 393224 | tf_op jit(solution)/shard_map/ppermute | solution.py:70
  51.0 6.3 %collective-permute-start.16 = (bf16[4,2,64,128]{3,2,1,0:T(8,128)(2,1)S(1)}, bf16[4,2,64,128]{3,2,1,0:T(8,128)(2,1)S(1)}, u32[]{:S(2)}, u32[]{:S(2)}) collective-permute-start(bf16[4,2,64,128]{3,2,1,0:T(8,128)(2,1)S(1)} %get-tuple-element.106), channel_id=1, source_target_pairs={{1,0},{2,1},{3,2},{4,3},{5,4},{6,5},{7,6},{9,8},{10,9},{11,10},{12... | collective-permute-start | bytes 393224 | tf_op jit(solution)/shard_map/ppermute | solution.py:70
  57.3 4.3 %copy-start.1 = (bf16[5,64,2048]{2,1,0:T(8,128)(2,1)S(1)}, bf16[5,64,2048]{2,1,0:T(8,128)(2,1)}, u32[]{:S(2)}) copy-start(bf16[5,64,2048]{2,1,0:T(8,128)(2,1)} %refs_10_.1) | copy-start | bytes 3932164
  57.3 4.3 %copy-start.2 = (bf16[5,64,2048]{2,1,0:T(8,128)(2,1)S(1)}, bf16[5,64,2048]{2,1,0:T(8,128)(2,1)}, u32[]{:S(2)}) copy-start(bf16[5,64,2048]{2,1,0:T(8,128)(2,1)} %refs_11_.1) | copy-start | bytes 3932164
  57.3 4.3 %copy-start.5 = (f32[2048]{0:T(1024)S(1)}, f32[2048]{0:T(1024)}, u32[]{:S(2)}) copy-start(f32[2048]{0:T(1024)} %param.9) | copy-start | bytes 24580
  57.3 4.3 %copy-start.6 = (s32[32,5]{0,1:T(8,128)S(1)}, s32[32,5]{0,1:T(8,128)}, u32[]{:S(2)}) copy-start(s32[32,5]{0,1:T(8,128)} %param.12) | copy-start | bytes 1924
  58.9 7.8 %collective-permute-start.17 = (bf16[3,4,64,128]{3,2,1,0:T(8,128)(2,1)S(1)}, bf16[3,4,64,128]{3,2,1,0:T(8,128)(2,1)S(1)}, u32[]{:S(2)}, u32[]{:S(2)}) collective-permute-start(bf16[3,4,64,128]{3,2,1,0:T(8,128)(2,1)S(1)} %get-tuple-element.122), channel_id=1, source_target_pairs={{0,8},{8,0},{16,24},{24,16},{1,9},{9,1},{17,25},{25,17},{2,10},{10... | collective-permute-start | bytes 589832 | tf_op jit(solution)/shard_map/ppermute | solution.py:63
  59.2 9.4 %collective-permute-start.18 = (bf16[3,4,64,128]{3,2,1,0:T(8,128)(2,1)S(1)}, bf16[3,4,64,128]{3,2,1,0:T(8,128)(2,1)S(1)}, u32[]{:S(2)}, u32[]{:S(2)}) collective-permute-start(bf16[3,4,64,128]{3,2,1,0:T(8,128)(2,1)S(1)} %get-tuple-element.123), channel_id=1, source_target_pairs={{0,16},{8,24},{16,0},{24,8},{1,17},{9,25},{17,1},{25,9},{2,18},{10... | collective-permute-start | bytes 589832 | tf_op jit(solution)/shard_map/ppermute | solution.py:63
  59.7 10.0 %collective-permute-start.19 = (bf16[3,4,64,128]{3,2,1,0:T(8,128)(2,1)S(1)}, bf16[3,4,64,128]{3,2,1,0:T(8,128)(2,1)S(1)}, u32[]{:S(2)}, u32[]{:S(2)}) collective-permute-start(bf16[3,4,64,128]{3,2,1,0:T(8,128)(2,1)S(1)} %get-tuple-element.124), channel_id=1, source_target_pairs={{0,24},{8,16},{16,8},{24,0},{1,25},{9,17},{17,9},{25,1},{2,26},{10... | collective-permute-start | bytes 589832 | tf_op jit(solution)/shard_map/ppermute | solution.py:63

commit v18 on v15

--- a/solution.py
+++ b/solution.py
@@ -30,7 +30,7 @@
     return pl.CostEstimate(flops=1024, bytes_accessed=1024, transcendentals=0)
 
 
-FIRST_SEND, FIRST_RETURN, SECOND_SEND, SECOND_RETURN = 1, 1, 1, None
+FIRST_SEND, FIRST_RETURN, SECOND_SEND, SECOND_RETURN = 1, 1, 1, 1
 
 
 def offsets(count, place):

time: 67.5 us -> 67.3 us (level)
  the two profiles are of different devices: /device:TPU:0 before, /device:TPU:1 now
where the time goes in v18:
time: 67.3 us; the launch traced here: 66.3 us
  starting transfers between devices  30.3 us (45%)
  waiting for transfers between devices  20.4 us (30%)
  Pallas kernels  14.8 us (22%)
  between operations  0.8 us (1%)
    ppermute x18, starting transfers between devices, exchange(): received.append(lax.ppermute(piece, 'mode', pairs))  23.7 us
    ppermute x18, waiting for transfers between devices, exchange(): received.append(lax.ppermute(piece, 'mode', pairs))  15.8 us
    ppermute x2, starting transfers between devices, from_behind(): lax.ppermute(value, axis, [(source, source + steps) for source in range(i...  6.58 us
    pallas_call x1, Pallas kernels, derive(): pl.pallas_call(functools.partial(derive_kernel, count, len(received)), in...  5.02 us
    ppermute x2, waiting for transfers between devices, from_behind(): lax.ppermute(value, axis, [(source, source + steps) for source in range(i...  4.65 us
    pallas_call x2, Pallas kernels, first_physics(): pl.pallas_call(functools.partial(first_kernel, count), in_specs=[vmem()]...  1.63 us
    pallas_call x2, Pallas kernels, pack_rest(): pl.pallas_call(kernel, in_specs=[pl.BlockSpec(memory_space=pl.ANY)] + [vm...  1.62 us
    pallas_call x1, Pallas kernels, second_physics(): pl.pallas_call(functools.partial(second_kernel, count, groups), in_specs=...  1.59 us
  transfers between devices with their start and end apart: 20, of which 14 were waited for; matrix products, arithmetic and copies ran while one was open for 0% of the time, Pallas kernels for 16%

profile of v18, /device:TPU:1, one launch (start us, length us, event | category | flops | bytes accessed | tf_op | source)
XLA Modules:
  0.0 66.3 jit_solution(1882203401532213813)
XLA Ops:
  0.6 1.4 %shard_map.95.fields_ref = bf16[6,32,2,2048]{3,2,1,0:T(2,128)(2,1)S(1)} custom-call(bf16[12,32,2,2048]{3,2,1,0:T(2,128)(2,1)} %fields_ref.3), custom_call_target="tpu_custom_call" | custom-call | flops 1024 | bytes 1024 | tf_op jit(solution)/shard_map/pallas_call | solution.py:119
  2.0 0.2 shard_map.102
  2.2 3.1 %collective-permute-start.6 = (bf16[6,2,32,2,128]{4,3,2,1,0:T(2,128)(2,1)S(1)}, bf16[6,2,32,2,128]{4,3,2,1,0:T(2,128)(2,1)S(1)}, u32[]{:S(2)}, u32[]{:S(2)}) collective-permute-start(bf16[6,2,32,2,128]{4,3,2,1,0:T(2,128)(2,1)S(1)} %shard_map.102), channel_id=1, source_target_pairs={{0,24},{8,16},{16,8},{24,0},{1,25},{9,17},{17,9},{25,1},{2,26},{10... | collective-permute-start | bytes 589832 | tf_op jit(solution)/shard_map/ppermute | solution.py:63
  5.3 0.2 shard_map.103
  5.4 0.3 collective-permute-start.7
  5.8 0.2 shard_map.104
  5.9 0.1 collective-permute-start.8
  6.1 0.2 shard_map.98
  6.2 1.4 %collective-permute-start.1 = (bf16[6,2,32,2,128]{4,3,2,1,0:T(2,128)(2,1)S(1)}, bf16[6,2,32,2,128]{4,3,2,1,0:T(2,128)(2,1)S(1)}, u32[]{:S(2)}, u32[]{:S(2)}) collective-permute-start(bf16[6,2,32,2,128]{4,3,2,1,0:T(2,128)(2,1)S(1)} %shard_map.98), channel_id=1, source_target_pairs={{0,8},{8,0},{16,24},{24,16},{1,9},{9,1},{17,25},{25,17},{2,10},{10... | collective-permute-start | bytes 589832 | tf_op jit(solution)/shard_map/ppermute | solution.py:63
  7.7 0.2 shard_map.97
  7.9 1.3 %collective-permute-start = (bf16[6,2,32,2,128]{4,3,2,1,0:T(2,128)(2,1)S(1)}, bf16[6,2,32,2,128]{4,3,2,1,0:T(2,128)(2,1)S(1)}, u32[]{:S(2)}, u32[]{:S(2)}) collective-permute-start(bf16[6,2,32,2,128]{4,3,2,1,0:T(2,128)(2,1)S(1)} %shard_map.97), channel_id=1, source_target_pairs={{0,24},{8,16},{16,8},{24,0},{1,25},{9,17},{17,9},{25,1},{2,26},{10... | collective-permute-start | bytes 589832 | tf_op jit(solution)/shard_map/ppermute | solution.py:63
  9.1 0.2 shard_map.99
  9.3 0.6 collective-permute-done.6
  9.9 1.2 %collective-permute-start.2 = (bf16[6,2,32,2,128]{4,3,2,1,0:T(2,128)(2,1)S(1)}, bf16[6,2,32,2,128]{4,3,2,1,0:T(2,128)(2,1)S(1)}, u32[]{:S(2)}, u32[]{:S(2)}) collective-permute-start(bf16[6,2,32,2,128]{4,3,2,1,0:T(2,128)(2,1)S(1)} %shard_map.99), channel_id=1, source_target_pairs={{0,16},{8,24},{16,0},{24,8},{1,17},{9,25},{17,1},{25,9},{2,18},{10... | collective-permute-start | bytes 589832 | tf_op jit(solution)/shard_map/ppermute | solution.py:63
  11.1 0.3 shard_map.96
  11.4 2.7 %collective-permute-done.7 = bf16[6,2,32,2,128]{4,3,2,1,0:T(2,128)(2,1)S(1)} collective-permute-done((bf16[6,2,32,2,128]{4,3,2,1,0:T(2,128)(2,1)S(1)}, bf16[6,2,32,2,128]{4,3,2,1,0:T(2,128)(2,1)S(1)}, u32[]{:S(2)}, u32[]{:S(2)}) %collective-permute-start.7) | collective-permute-done | bytes 196640 | tf_op jit(solution)/shard_map/ppermute | solution.py:63
  14.1 0.6 collective-permute-done.8
  14.7 0.8 %shard_map.105 = (bf16[4,2,64,128]{3,2,1,0:T(8,128)(2,1)S(1)}, bf16[4,2,64,128]{3,2,1,0:T(8,128)(2,1)S(1)}, bf16[4,2,64,128]{3,2,1,0:T(8,128)(2,1)S(1)}, bf16[4,...) custom-call(bf16[6,2,64,128]{3,2,1,0:T(8,128)(2,1)S(1)} %bitcast.35, bf16[6,2,64,128]{3,2,1,0:T(8,128)(2,1)S(1)} %bitcast.32, ...), custom_call_target="tpu_custom_call" | custom-call | flops 1024 | bytes 1024 | tf_op jit(solution)/shard_map/pallas_call | solution.py:235
  15.5 2.6 %collective-permute-start.9 = (bf16[4,2,64,128]{3,2,1,0:T(8,128)(2,1)S(1)}, bf16[4,2,64,128]{3,2,1,0:T(8,128)(2,1)S(1)}, u32[]{:S(2)}, u32[]{:S(2)}) collective-permute-start(bf16[4,2,64,128]{3,2,1,0:T(8,128)(2,1)S(1)} %get-tuple-element.73), channel_id=1, source_target_pairs={{0,24},{8,16},{16,8},{24,0},{1,25},{9,17},{17,9},{25,1},{2,26},{10... | collective-permute-start | bytes 393224 | tf_op jit(solution)/shard_map/ppermute | solution.py:63
  18.1 0.2 collective-permute-done.1
  18.3 1.2 %collective-permute-start.10 = (bf16[4,2,64,128]{3,2,1,0:T(8,128)(2,1)S(1)}, bf16[4,2,64,128]{3,2,1,0:T(8,128)(2,1)S(1)}, u32[]{:S(2)}, u32[]{:S(2)}) collective-permute-start(bf16[4,2,64,128]{3,2,1,0:T(8,128)(2,1)S(1)} %get-tuple-element.74), channel_id=1, source_target_pairs={{0,8},{8,0},{16,24},{24,16},{1,9},{9,1},{17,25},{25,17},{2,10},{10... | collective-permute-start | bytes 393224 | tf_op jit(solution)/shard_map/ppermute | solution.py:63
  19.5 0.2 collective-permute-start.11
  19.7 1.3 %shard_map.100 = (bf16[6,4,32,2,128]{4,3,2,1,0:T(2,128)(2,1)S(1)}, bf16[6,4,32,2,128]{4,3,2,1,0:T(2,128)(2,1)S(1)}, bf16[6,4,32,2,128]{4,3,2,1,0:T(2,128)(2,1)S(...) custom-call(bf16[12,32,2,2048]{3,2,1,0:T(2,128)(2,1)S(1)} %copy-done, ...), custom_call_target="tpu_custom_call" | custom-call | flops 1024 | bytes 1024 | tf_op jit(solution)/shard_map/pallas_call | solution.py:167
  21.0 1.5 %collective-permute-done = bf16[6,2,32,2,128]{4,3,2,1,0:T(2,128)(2,1)S(1)} collective-permute-done((bf16[6,2,32,2,128]{4,3,2,1,0:T(2,128)(2,1)S(1)}, bf16[6,2,32,2,128]{4,3,2,1,0:T(2,128)(2,1)S(1)}, u32[]{:S(2)}, u32[]{:S(2)}) %collective-permute-start) | collective-permute-done | bytes 196640 | tf_op jit(solution)/shard_map/ppermute | solution.py:63
  22.5 0.8 %shard_map.101 = (bf16[4,2,64,128]{3,2,1,0:T(8,128)(2,1)S(1)}, bf16[4,2,64,128]{3,2,1,0:T(8,128)(2,1)S(1)}, bf16[4,2,64,128]{3,2,1,0:T(8,128)(2,1)S(1)}, bf16[4,...) custom-call(bf16[6,2,64,128]{3,2,1,0:T(8,128)(2,1)S(1)} %bitcast.31, bf16[6,2,64,128]{3,2,1,0:T(8,128)(2,1)S(1)} %bitcast.29, ...), custom_call_target="tpu_custom_call" | custom-call | flops 1024 | bytes 1024 | tf_op jit(solution)/shard_map/pallas_call | solution.py:235
  23.4 2.2 %collective-permute-start.3 = (bf16[4,2,64,128]{3,2,1,0:T(8,128)(2,1)S(1)}, bf16[4,2,64,128]{3,2,1,0:T(8,128)(2,1)S(1)}, u32[]{:S(2)}, u32[]{:S(2)}) collective-permute-start(bf16[4,2,64,128]{3,2,1,0:T(8,128)(2,1)S(1)} %get-tuple-element.68), channel_id=1, source_target_pairs={{0,24},{8,16},{16,8},{24,0},{1,25},{9,17},{17,9},{25,1},{2,26},{10... | collective-permute-start | bytes 393224 | tf_op jit(solution)/shard_map/ppermute | solution.py:63
  25.6 0.2 collective-permute-start.4
  25.8 0.8 %collective-permute-start.5 = (bf16[4,2,64,128]{3,2,1,0:T(8,128)(2,1)S(1)}, bf16[4,2,64,128]{3,2,1,0:T(8,128)(2,1)S(1)}, u32[]{:S(2)}, u32[]{:S(2)}) collective-permute-start(bf16[4,2,64,128]{3,2,1,0:T(8,128)(2,1)S(1)} %get-tuple-element.70), channel_id=1, source_target_pairs={{0,16},{8,24},{16,0},{24,8},{1,17},{9,25},{17,1},{25,9},{2,18},{10... | collective-permute-start | bytes 393224 | tf_op jit(solution)/shard_map/ppermute | solution.py:63
  26.6 1.6 %collective-permute-done.10.refs_6_ = bf16[4,2,64,128]{3,2,1,0:T(8,128)(2,1)S(1)} collective-permute-done((bf16[4,2,64,128]{3,2,1,0:T(8,128)(2,1)S(1)}, bf16[4,2,64,128]{3,2,1,0:T(8,128)(2,1)S(1)}, u32[]{:S(2)}, u32[]{:S(2)}) %collective-permute-start.10) | collective-permute-done | bytes 131104 | tf_op jit(solution)/shard_map/ppermute | solution.py:63
  28.2 1.2 %collective-permute-done.11.refs_7_ = bf16[4,2,64,128]{3,2,1,0:T(8,128)(2,1)S(1)} collective-permute-done((bf16[4,2,64,128]{3,2,1,0:T(8,128)(2,1)S(1)}, bf16[4,2,64,128]{3,2,1,0:T(8,128)(2,1)S(1)}, u32[]{:S(2)}, u32[]{:S(2)}) %collective-permute-start.11) | collective-permute-done | bytes 131104 | tf_op jit(solution)/shard_map/ppermute | solution.py:63
  29.4 2.7 %collective-permute-start.12 = (bf16[6,4,32,2,128]{4,3,2,1,0:T(2,128)(2,1)S(1)}, bf16[6,4,32,2,128]{4,3,2,1,0:T(2,128)(2,1)S(1)}, u32[]{:S(2)}, u32[]{:S(2)}) collective-permute-start(bf16[6,4,32,2,128]{4,3,2,1,0:T(2,128)(2,1)S(1)} %get-tuple-element.92), channel_id=1, source_target_pairs={{0,24},{8,16},{16,8},{24,0},{1,25},{9,17},{17,9},{25,1},{2,26},{10... | collective-permute-start | bytes 1179656 | tf_op jit(solution)/shard_map/ppermute | solution.py:63
  32.1 1.7 %collective-permute-done.4.refs_2_ = bf16[4,2,64,128]{3,2,1,0:T(8,128)(2,1)S(1)} collective-permute-done((bf16[4,2,64,128]{3,2,1,0:T(8,128)(2,1)S(1)}, bf16[4,2,64,128]{3,2,1,0:T(8,128)(2,1)S(1)}, u32[]{:S(2)}, u32[]{:S(2)}) %collective-permute-start.4) | collective-permute-done | bytes 131104 | tf_op jit(solution)/shard_map/ppermute | solution.py:63
  33.8 0.2 collective-permute-done.5.refs_3_
  34.0 1.4 %collective-permute-start.13 = (bf16[6,4,32,2,128]{4,3,2,1,0:T(2,128)(2,1)S(1)}, bf16[6,4,32,2,128]{4,3,2,1,0:T(2,128)(2,1)S(1)}, u32[]{:S(2)}, u32[]{:S(2)}) collective-permute-start(bf16[6,4,32,2,128]{4,3,2,1,0:T(2,128)(2,1)S(1)} %get-tuple-element.93), channel_id=1, source_target_pairs={{0,8},{8,0},{16,24},{24,16},{1,9},{9,1},{17,25},{25,17},{2,10},{10... | collective-permute-start | bytes 1179656 | tf_op jit(solution)/shard_map/ppermute | solution.py:63
  35.4 2.3 %collective-permute-start.14 = (bf16[6,4,32,2,128]{4,3,2,1,0:T(2,128)(2,1)S(1)}, bf16[6,4,32,2,128]{4,3,2,1,0:T(2,128)(2,1)S(1)}, u32[]{:S(2)}, u32[]{:S(2)}) collective-permute-start(bf16[6,4,32,2,128]{4,3,2,1,0:T(2,128)(2,1)S(1)} %get-tuple-element.94), channel_id=1, source_target_pairs={{0,16},{8,24},{16,0},{24,8},{1,17},{9,25},{17,1},{25,9},{2,18},{10... | collective-permute-start | bytes 1179656 | tf_op jit(solution)/shard_map/ppermute | solution.py:63
  37.7 1.2 %shard_map.106 = (bf16[4,2,64,128]{3,2,1,0:T(8,128)(2,1)S(1)}, bf16[4,2,64,128]{3,2,1,0:T(8,128)(2,1)S(1)}) custom-call(bf16[4,2,64,128]{3,2,1,0:T(8,128)(2,1)S(1)} %get-tuple-element.83.refs_0_, bf16[4,2,64,128]{3,2,1,0:T(8,128)(2,1)S(1)} %collective-permute-done.3.refs_1_, bf16[4,2,64,128]{3,2,1,0:T(8,128)(2,1)S(1)} %collective-permute-done.4.refs_2_, ...), custom_call_target="tpu_custom_call" | custom-call | flops 1024 | bytes 1024 | tf_op jit(solution)/shard_map/pallas_call | solution.py:329
  38.9 4.7 %collective-permute-start.15 = (bf16[4,2,64,128]{3,2,1,0:T(8,128)(2,1)S(1)}, bf16[4,2,64,128]{3,2,1,0:T(8,128)(2,1)S(1)}, u32[]{:S(2)}, u32[]{:S(2)}) collective-permute-start(bf16[4,2,64,128]{3,2,1,0:T(8,128)(2,1)S(1)} %get-tuple-element.95), channel_id=1, source_target_pairs={{0,1},{1,2},{2,3},{3,4},{4,5},{5,6},{6,7},{8,9},{9,10},{10,11},{11... | collective-permute-start | bytes 393224 | tf_op jit(solution)/shard_map/ppermute | solution.py:70
  43.6 1.9 %collective-permute-start.16 = (bf16[4,2,64,128]{3,2,1,0:T(8,128)(2,1)S(1)}, bf16[4,2,64,128]{3,2,1,0:T(8,128)(2,1)S(1)}, u32[]{:S(2)}, u32[]{:S(2)}) collective-permute-start(bf16[4,2,64,128]{3,2,1,0:T(8,128)(2,1)S(1)} %get-tuple-element.96), channel_id=1, source_target_pairs={{1,0},{2,1},{3,2},{4,3},{5,4},{6,5},{7,6},{9,8},{10,9},{11,10},{12... | collective-permute-start | bytes 393224 | tf_op jit(solution)/shard_map/ppermute | solution.py:70
  45.5 4.6 %collective-permute-done.16.refs_9_ = bf16[4,2,64,128]{3,2,1,0:T(8,128)(2,1)S(1)} collective-permute-done((bf16[4,2,64,128]{3,2,1,0:T(8,128)(2,1)S(1)}, bf16[4,2,64,128]{3,2,1,0:T(8,128)(2,1)S(1)}, u32[]{:S(2)}, u32[]{:S(2)}) %collective-permute-start.16) | collective-permute-done | bytes 131104 | tf_op jit(solution)/shard_map/ppermute | solution.py:70
  50.2 0.6 collective-permute-done.13
  50.8 0.7 %collective-permute-done.14 = bf16[6,4,32,2,128]{4,3,2,1,0:T(2,128)(2,1)S(1)} collective-permute-done((bf16[6,4,32,2,128]{4,3,2,1,0:T(2,128)(2,1)S(1)}, bf16[6,4,32,2,128]{4,3,2,1,0:T(2,128)(2,1)S(1)}, u32[]{:S(2)}, u32[]{:S(2)}) %collective-permute-start.14) | collective-permute-done | bytes 393248 | tf_op jit(solution)/shard_map/ppermute | solution.py:63
  51.5 1.6 %shard_map.107 = (bf16[3,4,64,128]{3,2,1,0:T(8,128)(2,1)S(1)}, bf16[3,4,64,128]{3,2,1,0:T(8,128)(2,1)S(1)}, bf16[3,4,64,128]{3,2,1,0:T(8,128)(2,1)S(1)}, bf16[3,4,64,128]{3,2,1,0:T(8,128)(2,1)S(1)}) custom-call(bf16[6,4,64,128]{3,2,1,0:T(8,128)(2,1)S(1)} %bitcast.24, bf16[6,4,64,128]{3,2,1,0:T(8,128)(2,1)S(1)} %bitcast.25, ...), custom_call_target="tpu_custom_call" | custom-call | flops 1024 | bytes 1024 | tf_op jit(solution)/shard_map/pallas_call | solution.py:279
  53.1 2.4 %collective-permute-start.17 = (bf16[3,4,64,128]{3,2,1,0:T(8,128)(2,1)S(1)}, bf16[3,4,64,128]{3,2,1,0:T(8,128)(2,1)S(1)}, u32[]{:S(2)}, u32[]{:S(2)}) collective-permute-start(bf16[3,4,64,128]{3,2,1,0:T(8,128)(2,1)S(1)} %get-tuple-element.112), channel_id=1, source_target_pairs={{0,24},{8,16},{16,8},{24,0},{1,25},{9,17},{17,9},{25,1},{2,26},{10... | collective-permute-start | bytes 589832 | tf_op jit(solution)/shard_map/ppermute | solution.py:63
  55.5 0.2 collective-permute-start.18
  55.9 5.0 %shard_map.108 = (f32[3072,128]{1,0:T(8,128)}, f32[3,16,64,128]{3,2,1,0:T(8,128)S(1)}) custom-call(bf16[4,2,64,128]{3,2,1,0:T(8,128)(2,1)S(1)} %get-tuple-element.83.refs_0_, bf16[4,2,64,128]{3,2,1,0:T(8,128)(2,1)S(1)} %collective-permute-done.3.refs_1_, bf16[4,2,64,128]{3,2,1,0:T(8,128)(2,1)S(1)} %collective-permute-done.4.refs_2_, ...), custom_call_target="tpu_custom_call" | custom-call | flops 1024 | bytes 1024 | tf_op jit(solution)/shard_map/pallas_call | solution.py:441
  60.9 3.6 %collective-permute-done.18.refs_2_ = bf16[3,4,64,128]{3,2,1,0:T(8,128)(2,1)S(1)} collective-permute-done((bf16[3,4,64,128]{3,2,1,0:T(8,128)(2,1)S(1)}, bf16[3,4,64,128]{3,2,1,0:T(8,128)(2,1)S(1)}, u32[]{:S(2)}, u32[]{:S(2)}) %collective-permute-start.18) | collective-permute-done | bytes 196640 | tf_op jit(solution)/shard_map/ppermute | solution.py:63
  64.5 0.5 collective-permute-done.19.refs_3_
  65.0 1.3 %shard_map.109 = f32[3072,128]{1,0:T(8,128)} custom-call(bf16[3,4,64,128]{3,2,1,0:T(8,128)(2,1)S(1)} %get-tuple-element.111.refs_0_, bf16[3,4,64,128]{3,2,1,0:T(8,128)(2,1)S(1)} %collective-permute-done.17.refs_1_, bf16[3,4,64,128]{3,2,1,0:T(8,128)(2,1)S(1)} %collective-permute-done.18.refs_2_, bf16[3,4,64,128]{3,2,1,0:T(8,128)(2,1)S(1)} %collective-permute-done.19.refs_3_, ...), custom_call_target="tpu_custom_call" | custom-call | flops 1024 | bytes 1024 | tf_op jit(solution)/shard_map/pallas_call | solution.py:483
  (23 shorter events, 0.2 us)
Async XLA Ops:
  2.2 7.7 %collective-permute-start.6 = (bf16[6,2,32,2,128]{4,3,2,1,0:T(2,128)(2,1)S(1)}, bf16[6,2,32,2,128]{4,3,2,1,0:T(2,128)(2,1)S(1)}, u32[]{:S(2)}, u32[]{:S(2)}) collective-permute-start(bf16[6,2,32,2,128]{4,3,2,1,0:T(2,128)(2,1)S(1)} %shard_map.102), channel_id=1, source_target_pairs={{0,24},{8,16},{16,8},{24,0},{1,25},{9,17},{17,9},{25,1},{2,26},{10... | collective-permute-start | bytes 589832 | tf_op jit(solution)/shard_map/ppermute | solution.py:63
  5.4 8.6 %collective-permute-start.7 = (bf16[6,2,32,2,128]{4,3,2,1,0:T(2,128)(2,1)S(1)}, bf16[6,2,32,2,128]{4,3,2,1,0:T(2,128)(2,1)S(1)}, u32[]{:S(2)}, u32[]{:S(2)}) collective-permute-start(bf16[6,2,32,2,128]{4,3,2,1,0:T(2,128)(2,1)S(1)} %shard_map.103), channel_id=1, source_target_pairs={{0,8},{8,0},{16,24},{24,16},{1,9},{9,1},{17,25},{25,17},{2,10},{10... | collective-permute-start | bytes 589832 | tf_op jit(solution)/shard_map/ppermute | solution.py:63
  5.9 8.8 %collective-permute-start.8 = (bf16[6,2,32,2,128]{4,3,2,1,0:T(2,128)(2,1)S(1)}, bf16[6,2,32,2,128]{4,3,2,1,0:T(2,128)(2,1)S(1)}, u32[]{:S(2)}, u32[]{:S(2)}) collective-permute-start(bf16[6,2,32,2,128]{4,3,2,1,0:T(2,128)(2,1)S(1)} %shard_map.104), channel_id=1, source_target_pairs={{0,16},{8,24},{16,0},{24,8},{1,17},{9,25},{17,1},{25,9},{2,18},{10... | collective-permute-start | bytes 589832 | tf_op jit(solution)/shard_map/ppermute | solution.py:63
  6.2 4.8 %copy-start.3 = (bf16[256,256]{1,0:T(8,128)(2,1)S(1)}, bf16[256,256]{1,0:T(8,128)(2,1)}, u32[]{:S(2)}) copy-start(bf16[256,256]{1,0:T(8,128)(2,1)} %constant.5.clone.refs_1_) | copy-start | bytes 393220
  6.2 4.8 %copy-start.4 = (bf16[256,256]{1,0:T(8,128)(2,1)S(1)}, bf16[256,256]{1,0:T(8,128)(2,1)}, u32[]{:S(2)}) copy-start(bf16[256,256]{1,0:T(8,128)(2,1)} %constant.4.clone.refs_0_) | copy-start | bytes 393220
  6.2 12.1 %collective-permute-start.1 = (bf16[6,2,32,2,128]{4,3,2,1,0:T(2,128)(2,1)S(1)}, bf16[6,2,32,2,128]{4,3,2,1,0:T(2,128)(2,1)S(1)}, u32[]{:S(2)}, u32[]{:S(2)}) collective-permute-start(bf16[6,2,32,2,128]{4,3,2,1,0:T(2,128)(2,1)S(1)} %shard_map.98), channel_id=1, source_target_pairs={{0,8},{8,0},{16,24},{24,16},{1,9},{9,1},{17,25},{25,17},{2,10},{10... | collective-permute-start | bytes 589832 | tf_op jit(solution)/shard_map/ppermute | solution.py:63
  7.9 14.7 %collective-permute-start = (bf16[6,2,32,2,128]{4,3,2,1,0:T(2,128)(2,1)S(1)}, bf16[6,2,32,2,128]{4,3,2,1,0:T(2,128)(2,1)S(1)}, u32[]{:S(2)}, u32[]{:S(2)}) collective-permute-start(bf16[6,2,32,2,128]{4,3,2,1,0:T(2,128)(2,1)S(1)} %shard_map.97), channel_id=1, source_target_pairs={{0,24},{8,16},{16,8},{24,0},{1,25},{9,17},{17,9},{25,1},{2,26},{10... | collective-permute-start | bytes 589832 | tf_op jit(solution)/shard_map/ppermute | solution.py:63
  9.1 10.6 %copy-start = (bf16[12,32,2,2048]{3,2,1,0:T(2,128)(2,1)S(1)}, bf16[12,32,2,2048]{3,2,1,0:T(2,128)(2,1)}, u32[]{:S(2)}) copy-start(bf16[12,32,2,2048]{3,2,1,0:T(2,128)(2,1)} %fields_ref.3) | copy-start | bytes 9437188
  9.9 12.6 %collective-permute-start.2 = (bf16[6,2,32,2,128]{4,3,2,1,0:T(2,128)(2,1)S(1)}, bf16[6,2,32,2,128]{4,3,2,1,0:T(2,128)(2,1)S(1)}, u32[]{:S(2)}, u32[]{:S(2)}) collective-permute-start(bf16[6,2,32,2,128]{4,3,2,1,0:T(2,128)(2,1)S(1)} %shard_map.99), channel_id=1, source_target_pairs={{0,16},{8,24},{16,0},{24,8},{1,17},{9,25},{17,1},{25,9},{2,18},{10... | collective-permute-start | bytes 589832 | tf_op jit(solution)/shard_map/ppermute | solution.py:63
  15.5 10.3 %collective-permute-start.9 = (bf16[4,2,64,128]{3,2,1,0:T(8,128)(2,1)S(1)}, bf16[4,2,64,128]{3,2,1,0:T(8,128)(2,1)S(1)}, u32[]{:S(2)}, u32[]{:S(2)}) collective-permute-start(bf16[4,2,64,128]{3,2,1,0:T(8,128)(2,1)S(1)} %get-tuple-element.73), channel_id=1, source_target_pairs={{0,24},{8,16},{16,8},{24,0},{1,25},{9,17},{17,9},{25,1},{2,26},{10... | collective-permute-start | bytes 393224 | tf_op jit(solution)/shard_map/ppermute | solution.py:63
  18.3 9.9 %collective-permute-start.10 = (bf16[4,2,64,128]{3,2,1,0:T(8,128)(2,1)S(1)}, bf16[4,2,64,128]{3,2,1,0:T(8,128)(2,1)S(1)}, u32[]{:S(2)}, u32[]{:S(2)}) collective-permute-start(bf16[4,2,64,128]{3,2,1,0:T(8,128)(2,1)S(1)} %get-tuple-element.74), channel_id=1, source_target_pairs={{0,8},{8,0},{16,24},{24,16},{1,9},{9,1},{17,25},{25,17},{2,10},{10... | collective-permute-start | bytes 393224 | tf_op jit(solution)/shard_map/ppermute | solution.py:63
  19.5 18.2 %copy-start.7 = (s32[2,256]{1,0:T(2,128)S(1)}, s32[2,256]{1,0:T(2,128)}, u32[]{:S(2)}) copy-start(s32[2,256]{1,0:T(2,128)} %refs_8_.1) | copy-start | bytes 6148
  19.5 9.9 %collective-permute-start.11 = (bf16[4,2,64,128]{3,2,1,0:T(8,128)(2,1)S(1)}, bf16[4,2,64,128]{3,2,1,0:T(8,128)(2,1)S(1)}, u32[]{:S(2)}, u32[]{:S(2)}) collective-permute-start(bf16[4,2,64,128]{3,2,1,0:T(8,128)(2,1)S(1)} %get-tuple-element.75), channel_id=1, source_target_pairs={{0,16},{8,24},{16,0},{24,8},{1,17},{9,25},{17,1},{25,9},{2,18},{10... | collective-permute-start | bytes 393224 | tf_op jit(solution)/shard_map/ppermute | solution.py:63
  23.4 8.8 %collective-permute-start.3 = (bf16[4,2,64,128]{3,2,1,0:T(8,128)(2,1)S(1)}, bf16[4,2,64,128]{3,2,1,0:T(8,128)(2,1)S(1)}, u32[]{:S(2)}, u32[]{:S(2)}) collective-permute-start(bf16[4,2,64,128]{3,2,1,0:T(8,128)(2,1)S(1)} %get-tuple-element.68), channel_id=1, source_target_pairs={{0,24},{8,16},{16,8},{24,0},{1,25},{9,17},{17,9},{25,1},{2,26},{10... | collective-permute-start | bytes 393224 | tf_op jit(solution)/shard_map/ppermute | solution.py:63
  25.6 8.2 %collective-permute-start.4 = (bf16[4,2,64,128]{3,2,1,0:T(8,128)(2,1)S(1)}, bf16[4,2,64,128]{3,2,1,0:T(8,128)(2,1)S(1)}, u32[]{:S(2)}, u32[]{:S(2)}) collective-permute-start(bf16[4,2,64,128]{3,2,1,0:T(8,128)(2,1)S(1)} %get-tuple-element.69), channel_id=1, source_target_pairs={{0,8},{8,0},{16,24},{24,16},{1,9},{9,1},{17,25},{25,17},{2,10},{10... | collective-permute-start | bytes 393224 | tf_op jit(solution)/shard_map/ppermute | solution.py:63
  25.8 8.2 %collective-permute-start.5 = (bf16[4,2,64,128]{3,2,1,0:T(8,128)(2,1)S(1)}, bf16[4,2,64,128]{3,2,1,0:T(8,128)(2,1)S(1)}, u32[]{:S(2)}, u32[]{:S(2)}) collective-permute-start(bf16[4,2,64,128]{3,2,1,0:T(8,128)(2,1)S(1)} %get-tuple-element.70), channel_id=1, source_target_pairs={{0,16},{8,24},{16,0},{24,8},{1,17},{9,25},{17,1},{25,9},{2,18},{10... | collective-permute-start | bytes 393224 | tf_op jit(solution)/shard_map/ppermute | solution.py:63
  29.4 20.8 %collective-permute-start.12 = (bf16[6,4,32,2,128]{4,3,2,1,0:T(2,128)(2,1)S(1)}, bf16[6,4,32,2,128]{4,3,2,1,0:T(2,128)(2,1)S(1)}, u32[]{:S(2)}, u32[]{:S(2)}) collective-permute-start(bf16[6,4,32,2,128]{4,3,2,1,0:T(2,128)(2,1)S(1)} %get-tuple-element.92), channel_id=1, source_target_pairs={{0,24},{8,16},{16,8},{24,0},{1,25},{9,17},{17,9},{25,1},{2,26},{10... | collective-permute-start | bytes 1179656 | tf_op jit(solution)/shard_map/ppermute | solution.py:63
  34.0 16.8 %collective-permute-start.13 = (bf16[6,4,32,2,128]{4,3,2,1,0:T(2,128)(2,1)S(1)}, bf16[6,4,32,2,128]{4,3,2,1,0:T(2,128)(2,1)S(1)}, u32[]{:S(2)}, u32[]{:S(2)}) collective-permute-start(bf16[6,4,32,2,128]{4,3,2,1,0:T(2,128)(2,1)S(1)} %get-tuple-element.93), channel_id=1, source_target_pairs={{0,8},{8,0},{16,24},{24,16},{1,9},{9,1},{17,25},{25,17},{2,10},{10... | collective-permute-start | bytes 1179656 | tf_op jit(solution)/shard_map/ppermute | solution.py:63
  35.4 16.0 %collective-permute-start.14 = (bf16[6,4,32,2,128]{4,3,2,1,0:T(2,128)(2,1)S(1)}, bf16[6,4,32,2,128]{4,3,2,1,0:T(2,128)(2,1)S(1)}, u32[]{:S(2)}, u32[]{:S(2)}) collective-permute-start(bf16[6,4,32,2,128]{4,3,2,1,0:T(2,128)(2,1)S(1)} %get-tuple-element.94), channel_id=1, source_target_pairs={{0,16},{8,24},{16,0},{24,8},{1,17},{9,25},{17,1},{25,9},{2,18},{10... | collective-permute-start | bytes 1179656 | tf_op jit(solution)/shard_map/ppermute | solution.py:63
  38.9 6.6 %collective-permute-start.15 = (bf16[4,2,64,128]{3,2,1,0:T(8,128)(2,1)S(1)}, bf16[4,2,64,128]{3,2,1,0:T(8,128)(2,1)S(1)}, u32[]{:S(2)}, u32[]{:S(2)}) collective-permute-start(bf16[4,2,64,128]{3,2,1,0:T(8,128)(2,1)S(1)} %get-tuple-element.95), channel_id=1, source_target_pairs={{0,1},{1,2},{2,3},{3,4},{4,5},{5,6},{6,7},{8,9},{9,10},{10,11},{11... | collective-permute-start | bytes 393224 | tf_op jit(solution)/shard_map/ppermute | solution.py:70
  43.6 6.6 %collective-permute-start.16 = (bf16[4,2,64,128]{3,2,1,0:T(8,128)(2,1)S(1)}, bf16[4,2,64,128]{3,2,1,0:T(8,128)(2,1)S(1)}, u32[]{:S(2)}, u32[]{:S(2)}) collective-permute-start(bf16[4,2,64,128]{3,2,1,0:T(8,128)(2,1)S(1)} %get-tuple-element.96), channel_id=1, source_target_pairs={{1,0},{2,1},{3,2},{4,3},{5,4},{6,5},{7,6},{9,8},{10,9},{11,10},{12... | collective-permute-start | bytes 393224 | tf_op jit(solution)/shard_map/ppermute | solution.py:70
  51.5 4.4 %copy-start.1 = (bf16[5,64,2048]{2,1,0:T(8,128)(2,1)S(1)}, bf16[5,64,2048]{2,1,0:T(8,128)(2,1)}, u32[]{:S(2)}) copy-start(bf16[5,64,2048]{2,1,0:T(8,128)(2,1)} %refs_10_.1) | copy-start | bytes 3932164
  51.5 4.4 %copy-start.2 = (bf16[5,64,2048]{2,1,0:T(8,128)(2,1)S(1)}, bf16[5,64,2048]{2,1,0:T(8,128)(2,1)}, u32[]{:S(2)}) copy-start(bf16[5,64,2048]{2,1,0:T(8,128)(2,1)} %refs_11_.1) | copy-start | bytes 3932164
  51.5 4.4 %copy-start.5 = (f32[2048]{0:T(1024)S(1)}, f32[2048]{0:T(1024)}, u32[]{:S(2)}) copy-start(f32[2048]{0:T(1024)} %param.9) | copy-start | bytes 24580
  51.5 4.4 %copy-start.6 = (s32[32,5]{0,1:T(8,128)S(1)}, s32[32,5]{0,1:T(8,128)}, u32[]{:S(2)}) copy-start(s32[32,5]{0,1:T(8,128)} %param.12) | copy-start | bytes 1924
  53.1 7.8 %collective-permute-start.17 = (bf16[3,4,64,128]{3,2,1,0:T(8,128)(2,1)S(1)}, bf16[3,4,64,128]{3,2,1,0:T(8,128)(2,1)S(1)}, u32[]{:S(2)}, u32[]{:S(2)}) collective-permute-start(bf16[3,4,64,128]{3,2,1,0:T(8,128)(2,1)S(1)} %get-tuple-element.112), channel_id=1, source_target_pairs={{0,24},{8,16},{16,8},{24,0},{1,25},{9,17},{17,9},{25,1},{2,26},{10... | collective-permute-start | bytes 589832 | tf_op jit(solution)/shard_map/ppermute | solution.py:63
  55.5 9.0 %collective-permute-start.18 = (bf16[3,4,64,128]{3,2,1,0:T(8,128)(2,1)S(1)}, bf16[3,4,64,128]{3,2,1,0:T(8,128)(2,1)S(1)}, u32[]{:S(2)}, u32[]{:S(2)}) collective-permute-start(bf16[3,4,64,128]{3,2,1,0:T(8,128)(2,1)S(1)} %get-tuple-element.113), channel_id=1, source_target_pairs={{0,8},{8,0},{16,24},{24,16},{1,9},{9,1},{17,25},{25,17},{2,10},{10... | collective-permute-start | bytes 589832 | tf_op jit(solution)/shard_map/ppermute | solution.py:63
  55.7 9.3 %collective-permute-start.19 = (bf16[3,4,64,128]{3,2,1,0:T(8,128)(2,1)S(1)}, bf16[3,4,64,128]{3,2,1,0:T(8,128)(2,1)S(1)}, u32[]{:S(2)}, u32[]{:S(2)}) collective-permute-start(bf16[3,4,64,128]{3,2,1,0:T(8,128)(2,1)S(1)} %get-tuple-element.114), channel_id=1, source_target_pairs={{0,16},{8,24},{16,0},{24,8},{1,17},{9,25},{17,1},{25,9},{2,18},{10... | collective-permute-start | bytes 589832 | tf_op jit(solution)/shard_map/ppermute | solution.py:63

commit v19 on v16

--- a/solution.py
+++ b/solution.py
@@ -30,7 +30,7 @@
     return pl.CostEstimate(flops=1024, bytes_accessed=1024, transcendentals=0)
 
 
-FIRST_SEND, FIRST_RETURN, SECOND_SEND, SECOND_RETURN = 1, 1, 1, None
+FIRST_SEND, FIRST_RETURN, SECOND_SEND, SECOND_RETURN = 1, 1, 1, 1
 
 
 def offsets(count, place):
@@ -90,7 +90,7 @@
 
 
 def spans_of(tiles):
-    return [(0, tiles - 1), (tiles - 1, 1)] if tiles > 2 else [(0, tiles)]
+    return [(0, tiles // 2), (tiles // 2, tiles - tiles // 2)] if tiles > 1 else [(0, tiles)]
 
 
 def pieces_of(fields_ref, first, share, begin, out_ref):
@@ -542,10 +542,12 @@
         local[back], shares[sent] = lax.optimization_barrier((local[back], shares[sent]))
     toward_prev, toward_next = interface(local, interface_nodes, count)
     halos = (from_behind(toward_next, "mer", 1), from_behind(toward_prev, "mer", -1))
-    halos, shares[count:] = lax.optimization_barrier((halos, shares[count:]))
+    local, shares[count:] = lax.optimization_barrier((local, shares[count:]))
     lorentz = []
     for part, (begin, _) in enumerate(spans):
         sources = exchange(shares[part * count : (part + 1) * count], order)
+        if part == len(spans) - 1:
+            sources, halos = lax.optimization_barrier((sources, halos))
         terms = list(second_physics(joined(sources), physical, begin, later_inverse, later_forward))
         if part == len(spans) - 1:
             terms, radius = lax.optimization_barrier((terms, radius))

time: 70.7 us -> 67 us (0.948); the launches traced: 70.3 us -> 65.8 us
  waiting for transfers between devices: 20 us -> 15.6 us
    ppermute x24, waiting for transfers between devices: 15.7 us -> 12.3 us  [exchange(): received.append(lax.ppermute(piece, 'mode', pairs))]
    ppermute x2, waiting for transfers between devices: 4.35 us -> 3.29 us  [from_behind(): lax.ppermute(value, axis, [(source, source + steps) for source in range(i...]
    ppermute x24, starting transfers between devices: 26.6 us -> 27.5 us  [exchange(): received.append(lax.ppermute(piece, 'mode', pairs))]
    ppermute x2, starting transfers between devices: 7.29 us -> 6.57 us  [from_behind(): lax.ppermute(value, axis, [(source, source + steps) for source in range(i...]
  transfers between devices with their start and end apart: 26 -> 26, of which waited for: 9 -> 12; matrix products, arithmetic and copies ran while one was open for 0% -> 0% of each run, Pallas kernels for 18% -> 18%
where the time goes in v19:
time: 67 us; the launch traced here: 65.8 us
  starting transfers between devices  34 us (51%)
  waiting for transfers between devices  15.6 us (23%)
  Pallas kernels  15.3 us (23%)
  between operations  0.83 us (1%)
    ppermute x24, starting transfers between devices, exchange(): received.append(lax.ppermute(piece, 'mode', pairs))  27.5 us
    ppermute x24, waiting for transfers between devices, exchange(): received.append(lax.ppermute(piece, 'mode', pairs))  12.3 us
    ppermute x2, starting transfers between devices, from_behind(): lax.ppermute(value, axis, [(source, source + steps) for source in range(i...  6.57 us
    pallas_call x1, Pallas kernels, derive(): pl.pallas_call(functools.partial(derive_kernel, count, len(received)), in...  5 us
    ppermute x2, waiting for transfers between devices, from_behind(): lax.ppermute(value, axis, [(source, source + steps) for source in range(i...  3.29 us
    pallas_call x2, Pallas kernels, second_physics(): pl.pallas_call(functools.partial(second_kernel, count, groups, begin), in...  1.84 us
    pallas_call x2, Pallas kernels, first_physics(): pl.pallas_call(functools.partial(first_kernel, count), in_specs=[vmem()]...  1.63 us
    pallas_call x2, Pallas kernels, pack_rest(): pl.pallas_call(kernel, in_specs=[pl.BlockSpec(memory_space=pl.ANY)] + [vm...  1.62 us
  transfers between devices with their start and end apart: 26, of which 12 were waited for; matrix products, arithmetic and copies ran while one was open for 0% of the time, Pallas kernels for 18%

profile of v19, /device:TPU:1, one launch (start us, length us, event | category | flops | bytes accessed | tf_op | source)
XLA Modules:
  0.0 65.8 jit_solution(1927406981574281563)
XLA Ops:
  0.6 1.4 %shard_map.95.fields_ref = bf16[6,32,2,2048]{3,2,1,0:T(2,128)(2,1)S(1)} custom-call(bf16[12,32,2,2048]{3,2,1,0:T(2,128)(2,1)} %fields_ref.3), custom_call_target="tpu_custom_call" | custom-call | flops 1024 | bytes 1024 | tf_op jit(solution)/shard_map/pallas_call | solution.py:123
  2.0 0.2 shard_map.102
  2.2 3.1 %collective-permute-start.6 = (bf16[6,2,32,2,128]{4,3,2,1,0:T(2,128)(2,1)S(1)}, bf16[6,2,32,2,128]{4,3,2,1,0:T(2,128)(2,1)S(1)}, u32[]{:S(2)}, u32[]{:S(2)}) collective-permute-start(bf16[6,2,32,2,128]{4,3,2,1,0:T(2,128)(2,1)S(1)} %shard_map.102), channel_id=1, source_target_pairs={{0,24},{8,16},{16,8},{24,0},{1,25},{9,17},{17,9},{25,1},{2,26},{10... | collective-permute-start | bytes 589832 | tf_op jit(solution)/shard_map/ppermute | solution.py:63
  5.4 0.3 collective-permute-start.7
  6.2 1.4 %collective-permute-start.1 = (bf16[6,2,32,2,128]{4,3,2,1,0:T(2,128)(2,1)S(1)}, bf16[6,2,32,2,128]{4,3,2,1,0:T(2,128)(2,1)S(1)}, u32[]{:S(2)}, u32[]{:S(2)}) collective-permute-start(bf16[6,2,32,2,128]{4,3,2,1,0:T(2,128)(2,1)S(1)} %shard_map.98), channel_id=1, source_target_pairs={{0,8},{8,0},{16,24},{24,16},{1,9},{9,1},{17,25},{25,17},{2,10},{10... | collective-permute-start | bytes 589832 | tf_op jit(solution)/shard_map/ppermute | solution.py:63
  7.9 1.3 %collective-permute-start = (bf16[6,2,32,2,128]{4,3,2,1,0:T(2,128)(2,1)S(1)}, bf16[6,2,32,2,128]{4,3,2,1,0:T(2,128)(2,1)S(1)}, u32[]{:S(2)}, u32[]{:S(2)}) collective-permute-start(bf16[6,2,32,2,128]{4,3,2,1,0:T(2,128)(2,1)S(1)} %shard_map.97), channel_id=1, source_target_pairs={{0,24},{8,16},{16,8},{24,0},{1,25},{9,17},{17,9},{25,1},{2,26},{10... | collective-permute-start | bytes 589832 | tf_op jit(solution)/shard_map/ppermute | solution.py:63
  9.3 0.6 collective-permute-done.6
  9.9 1.2 %collective-permute-start.2 = (bf16[6,2,32,2,128]{4,3,2,1,0:T(2,128)(2,1)S(1)}, bf16[6,2,32,2,128]{4,3,2,1,0:T(2,128)(2,1)S(1)}, u32[]{:S(2)}, u32[]{:S(2)}) collective-permute-start(bf16[6,2,32,2,128]{4,3,2,1,0:T(2,128)(2,1)S(1)} %shard_map.99), channel_id=1, source_target_pairs={{0,16},{8,24},{16,0},{24,8},{1,17},{9,25},{17,1},{25,9},{2,18},{10... | collective-permute-start | bytes 589832 | tf_op jit(solution)/shard_map/ppermute | solution.py:63
  11.1 0.3 shard_map.96
  11.4 2.7 %collective-permute-done.7 = bf16[6,2,32,2,128]{4,3,2,1,0:T(2,128)(2,1)S(1)} collective-permute-done((bf16[6,2,32,2,128]{4,3,2,1,0:T(2,128)(2,1)S(1)}, bf16[6,2,32,2,128]{4,3,2,1,0:T(2,128)(2,1)S(1)}, u32[]{:S(2)}, u32[]{:S(2)}) %collective-permute-start.7) | collective-permute-done | bytes 196640 | tf_op jit(solution)/shard_map/ppermute | solution.py:63
  14.1 0.6 collective-permute-done.8
  14.7 0.8 %shard_map.105 = (bf16[4,2,64,128]{3,2,1,0:T(8,128)(2,1)S(1)}, bf16[4,2,64,128]{3,2,1,0:T(8,128)(2,1)S(1)}, bf16[4,2,64,128]{3,2,1,0:T(8,128)(2,1)S(1)}, bf16[4,...) custom-call(bf16[6,2,64,128]{3,2,1,0:T(8,128)(2,1)S(1)} %bitcast.43, bf16[6,2,64,128]{3,2,1,0:T(8,128)(2,1)S(1)} %bitcast.40, ...), custom_call_target="tpu_custom_call" | custom-call | flops 1024 | bytes 1024 | tf_op jit(solution)/shard_map/pallas_call | solution.py:238
  15.5 2.6 %collective-permute-start.9 = (bf16[4,2,64,128]{3,2,1,0:T(8,128)(2,1)S(1)}, bf16[4,2,64,128]{3,2,1,0:T(8,128)(2,1)S(1)}, u32[]{:S(2)}, u32[]{:S(2)}) collective-permute-start(bf16[4,2,64,128]{3,2,1,0:T(8,128)(2,1)S(1)} %get-tuple-element.93), channel_id=1, source_target_pairs={{0,24},{8,16},{16,8},{24,0},{1,25},{9,17},{17,9},{25,1},{2,26},{10... | collective-permute-start | bytes 393224 | tf_op jit(solution)/shard_map/ppermute | solution.py:63
  18.1 0.2 collective-permute-done.1
  18.3 1.2 %collective-permute-start.10 = (bf16[4,2,64,128]{3,2,1,0:T(8,128)(2,1)S(1)}, bf16[4,2,64,128]{3,2,1,0:T(8,128)(2,1)S(1)}, u32[]{:S(2)}, u32[]{:S(2)}) collective-permute-start(bf16[4,2,64,128]{3,2,1,0:T(8,128)(2,1)S(1)} %get-tuple-element.94), channel_id=1, source_target_pairs={{0,8},{8,0},{16,24},{24,16},{1,9},{9,1},{17,25},{25,17},{2,10},{10... | collective-permute-start | bytes 393224 | tf_op jit(solution)/shard_map/ppermute | solution.py:63
  19.5 0.2 collective-permute-start.11
  19.7 1.3 %shard_map.100 = (bf16[6,2,32,2,128]{4,3,2,1,0:T(2,128)(2,1)S(1)}, bf16[6,2,32,2,128]{4,3,2,1,0:T(2,128)(2,1)S(1)}, bf16[6,2,32,2,128]{4,3,2,1,0:T(2,128)(2,1)S(...) custom-call(bf16[12,32,2,2048]{3,2,1,0:T(2,128)(2,1)S(1)} %copy-done, ...), custom_call_target="tpu_custom_call" | custom-call | flops 1024 | bytes 1024 | tf_op jit(solution)/shard_map/pallas_call | solution.py:170
  21.0 1.5 %collective-permute-done = bf16[6,2,32,2,128]{4,3,2,1,0:T(2,128)(2,1)S(1)} collective-permute-done((bf16[6,2,32,2,128]{4,3,2,1,0:T(2,128)(2,1)S(1)}, bf16[6,2,32,2,128]{4,3,2,1,0:T(2,128)(2,1)S(1)}, u32[]{:S(2)}, u32[]{:S(2)}) %collective-permute-start) | collective-permute-done | bytes 196640 | tf_op jit(solution)/shard_map/ppermute | solution.py:63
  22.5 0.8 %shard_map.101 = (bf16[4,2,64,128]{3,2,1,0:T(8,128)(2,1)S(1)}, bf16[4,2,64,128]{3,2,1,0:T(8,128)(2,1)S(1)}, bf16[4,2,64,128]{3,2,1,0:T(8,128)(2,1)S(1)}, bf16[4,...) custom-call(bf16[6,2,64,128]{3,2,1,0:T(8,128)(2,1)S(1)} %bitcast.39, bf16[6,2,64,128]{3,2,1,0:T(8,128)(2,1)S(1)} %bitcast.37, ...), custom_call_target="tpu_custom_call" | custom-call | flops 1024 | bytes 1024 | tf_op jit(solution)/shard_map/pallas_call | solution.py:238
  23.4 2.2 %collective-permute-start.3 = (bf16[4,2,64,128]{3,2,1,0:T(8,128)(2,1)S(1)}, bf16[4,2,64,128]{3,2,1,0:T(8,128)(2,1)S(1)}, u32[]{:S(2)}, u32[]{:S(2)}) collective-permute-start(bf16[4,2,64,128]{3,2,1,0:T(8,128)(2,1)S(1)} %get-tuple-element.88), channel_id=1, source_target_pairs={{0,24},{8,16},{16,8},{24,0},{1,25},{9,17},{17,9},{25,1},{2,26},{10... | collective-permute-start | bytes 393224 | tf_op jit(solution)/shard_map/ppermute | solution.py:63
  25.6 0.2 collective-permute-start.4
  25.8 0.8 %collective-permute-start.5 = (bf16[4,2,64,128]{3,2,1,0:T(8,128)(2,1)S(1)}, bf16[4,2,64,128]{3,2,1,0:T(8,128)(2,1)S(1)}, u32[]{:S(2)}, u32[]{:S(2)}) collective-permute-start(bf16[4,2,64,128]{3,2,1,0:T(8,128)(2,1)S(1)} %get-tuple-element.90), channel_id=1, source_target_pairs={{0,16},{8,24},{16,0},{24,8},{1,17},{9,25},{17,1},{25,9},{2,18},{10... | collective-permute-start | bytes 393224 | tf_op jit(solution)/shard_map/ppermute | solution.py:63
  26.6 1.6 %collective-permute-done.10.refs_6_ = bf16[4,2,64,128]{3,2,1,0:T(8,128)(2,1)S(1)} collective-permute-done((bf16[4,2,64,128]{3,2,1,0:T(8,128)(2,1)S(1)}, bf16[4,2,64,128]{3,2,1,0:T(8,128)(2,1)S(1)}, u32[]{:S(2)}, u32[]{:S(2)}) %collective-permute-start.10) | collective-permute-done | bytes 131104 | tf_op jit(solution)/shard_map/ppermute | solution.py:63
  28.2 1.2 %collective-permute-done.11.refs_7_ = bf16[4,2,64,128]{3,2,1,0:T(8,128)(2,1)S(1)} collective-permute-done((bf16[4,2,64,128]{3,2,1,0:T(8,128)(2,1)S(1)}, bf16[4,2,64,128]{3,2,1,0:T(8,128)(2,1)S(1)}, u32[]{:S(2)}, u32[]{:S(2)}) %collective-permute-start.11) | collective-permute-done | bytes 131104 | tf_op jit(solution)/shard_map/ppermute | solution.py:63
  29.4 2.7 %collective-permute-start.17 = (bf16[6,2,32,2,128]{4,3,2,1,0:T(2,128)(2,1)S(1)}, bf16[6,2,32,2,128]{4,3,2,1,0:T(2,128)(2,1)S(1)}, u32[]{:S(2)}, u32[]{:S(2)}) collective-permute-start(bf16[6,2,32,2,128]{4,3,2,1,0:T(2,128)(2,1)S(1)} %get-tuple-element.144), channel_id=1, source_target_pairs={{0,24},{8,16},{16,8},{24,0},{1,25},{9,17},{17,9},{25,1},{2,26},{10... | collective-permute-start | bytes 589832 | tf_op jit(solution)/shard_map/ppermute | solution.py:63
  32.1 1.7 %collective-permute-done.4.refs_2_ = bf16[4,2,64,128]{3,2,1,0:T(8,128)(2,1)S(1)} collective-permute-done((bf16[4,2,64,128]{3,2,1,0:T(8,128)(2,1)S(1)}, bf16[4,2,64,128]{3,2,1,0:T(8,128)(2,1)S(1)}, u32[]{:S(2)}, u32[]{:S(2)}) %collective-permute-start.4) | collective-permute-done | bytes 131104 | tf_op jit(solution)/shard_map/ppermute | solution.py:63
  33.8 0.2 collective-permute-done.5.refs_3_
  34.0 1.4 %collective-permute-start.18 = (bf16[6,2,32,2,128]{4,3,2,1,0:T(2,128)(2,1)S(1)}, bf16[6,2,32,2,128]{4,3,2,1,0:T(2,128)(2,1)S(1)}, u32[]{:S(2)}, u32[]{:S(2)}) collective-permute-start(bf16[6,2,32,2,128]{4,3,2,1,0:T(2,128)(2,1)S(1)} %get-tuple-element.145), channel_id=1, source_target_pairs={{0,8},{8,0},{16,24},{24,16},{1,9},{9,1},{17,25},{25,17},{2,10},{10... | collective-permute-start | bytes 589832 | tf_op jit(solution)/shard_map/ppermute | solution.py:63
  35.4 2.3 %collective-permute-start.19 = (bf16[6,2,32,2,128]{4,3,2,1,0:T(2,128)(2,1)S(1)}, bf16[6,2,32,2,128]{4,3,2,1,0:T(2,128)(2,1)S(1)}, u32[]{:S(2)}, u32[]{:S(2)}) collective-permute-start(bf16[6,2,32,2,128]{4,3,2,1,0:T(2,128)(2,1)S(1)} %get-tuple-element.146), channel_id=1, source_target_pairs={{0,16},{8,24},{16,0},{24,8},{1,17},{9,25},{17,1},{25,9},{2,18},{10... | collective-permute-start | bytes 589832 | tf_op jit(solution)/shard_map/ppermute | solution.py:63
  37.7 1.2 %shard_map.106 = (bf16[4,2,64,128]{3,2,1,0:T(8,128)(2,1)S(1)}, bf16[4,2,64,128]{3,2,1,0:T(8,128)(2,1)S(1)}) custom-call(bf16[4,2,64,128]{3,2,1,0:T(8,128)(2,1)S(1)} %get-tuple-element.115.refs_0_, bf16[4,2,64,128]{3,2,1,0:T(8,128)(2,1)S(1)} %collective-permute-done.3.refs_1_, bf16[4,2,64,128]{3,2,1,0:T(8,128)(2,1)S(1)} %collective-permute-done.4.refs_2_, ...), custom_call_target="tpu_custom_call" | custom-call | flops 1024 | bytes 1024 | tf_op jit(solution)/shard_map/pallas_call | solution.py:334
  38.9 4.7 %collective-permute-start.15 = (bf16[4,2,64,128]{3,2,1,0:T(8,128)(2,1)S(1)}, bf16[4,2,64,128]{3,2,1,0:T(8,128)(2,1)S(1)}, u32[]{:S(2)}, u32[]{:S(2)}) collective-permute-start(bf16[4,2,64,128]{3,2,1,0:T(8,128)(2,1)S(1)} %get-tuple-element.127), channel_id=1, source_target_pairs={{0,1},{1,2},{2,3},{3,4},{4,5},{5,6},{6,7},{8,9},{9,10},{10,11},{11... | collective-permute-start | bytes 393224 | tf_op jit(solution)/shard_map/ppermute | solution.py:70
  43.6 0.4 collective-permute-start.12
  44.0 1.3 %collective-permute-start.13 = (bf16[6,2,32,2,128]{4,3,2,1,0:T(2,128)(2,1)S(1)}, bf16[6,2,32,2,128]{4,3,2,1,0:T(2,128)(2,1)S(1)}, u32[]{:S(2)}, u32[]{:S(2)}) collective-permute-start(bf16[6,2,32,2,128]{4,3,2,1,0:T(2,128)(2,1)S(1)} %get-tuple-element.125), channel_id=1, source_target_pairs={{0,8},{8,0},{16,24},{24,16},{1,9},{9,1},{17,25},{25,17},{2,10},{10... | collective-permute-start | bytes 589832 | tf_op jit(solution)/shard_map/ppermute | solution.py:63
  45.3 1.0 %collective-permute-start.14 = (bf16[6,2,32,2,128]{4,3,2,1,0:T(2,128)(2,1)S(1)}, bf16[6,2,32,2,128]{4,3,2,1,0:T(2,128)(2,1)S(1)}, u32[]{:S(2)}, u32[]{:S(2)}) collective-permute-start(bf16[6,2,32,2,128]{4,3,2,1,0:T(2,128)(2,1)S(1)} %get-tuple-element.126), channel_id=1, source_target_pairs={{0,16},{8,24},{16,0},{24,8},{1,17},{9,25},{17,1},{25,9},{2,18},{10... | collective-permute-start | bytes 589832 | tf_op jit(solution)/shard_map/ppermute | solution.py:63
  46.3 1.9 %collective-permute-start.16 = (bf16[4,2,64,128]{3,2,1,0:T(8,128)(2,1)S(1)}, bf16[4,2,64,128]{3,2,1,0:T(8,128)(2,1)S(1)}, u32[]{:S(2)}, u32[]{:S(2)}) collective-permute-start(bf16[4,2,64,128]{3,2,1,0:T(8,128)(2,1)S(1)} %get-tuple-element.128), channel_id=1, source_target_pairs={{1,0},{2,1},{3,2},{4,3},{5,4},{6,5},{7,6},{9,8},{10,9},{11,10},{12... | collective-permute-start | bytes 393224 | tf_op jit(solution)/shard_map/ppermute | solution.py:70
  48.3 0.9 %shard_map.109 = (bf16[3,2,64,128]{3,2,1,0:T(8,128)(2,1)S(1)}, bf16[3,2,64,128]{3,2,1,0:T(8,128)(2,1)S(1)}, bf16[3,2,64,128]{3,2,1,0:T(8,128)(2,1)S(1)}, bf16[3,2,64,128]{3,2,1,0:T(8,128)(2,1)S(1)}) custom-call(bf16[6,2,64,128]{3,2,1,0:T(8,128)(2,1)S(1)} %bitcast.29, bf16[6,2,64,128]{3,2,1,0:T(8,128)(2,1)S(1)} %bitcast.32, ...), custom_call_target="tpu_custom_call" | custom-call | flops 1024 | bytes 1024 | tf_op jit(solution)/shard_map/pallas_call | solution.py:284
  49.2 0.4 collective-permute-start.20
  49.6 3.3 %collective-permute-done.16.refs_9_ = bf16[4,2,64,128]{3,2,1,0:T(8,128)(2,1)S(1)} collective-permute-done((bf16[4,2,64,128]{3,2,1,0:T(8,128)(2,1)S(1)}, bf16[4,2,64,128]{3,2,1,0:T(8,128)(2,1)S(1)}, u32[]{:S(2)}, u32[]{:S(2)}) %collective-permute-start.16) | collective-permute-done | bytes 131104 | tf_op jit(solution)/shard_map/ppermute | solution.py:70
  52.9 0.3 collective-permute-start.21
  53.2 0.4 collective-permute-start.22
  53.6 1.5 %collective-permute-done.13 = bf16[6,2,32,2,128]{4,3,2,1,0:T(2,128)(2,1)S(1)} collective-permute-done((bf16[6,2,32,2,128]{4,3,2,1,0:T(2,128)(2,1)S(1)}, bf16[6,2,32,2,128]{4,3,2,1,0:T(2,128)(2,1)S(1)}, u32[]{:S(2)}, u32[]{:S(2)}) %collective-permute-start.13) | collective-permute-done | bytes 196640 | tf_op jit(solution)/shard_map/ppermute | solution.py:63
  55.0 0.5 collective-permute-done.14
  55.5 0.9 %shard_map.107 = (bf16[3,2,64,128]{3,2,1,0:T(8,128)(2,1)S(1)}, bf16[3,2,64,128]{3,2,1,0:T(8,128)(2,1)S(1)}, bf16[3,2,64,128]{3,2,1,0:T(8,128)(2,1)S(1)}, bf16[3,2,64,128]{3,2,1,0:T(8,128)(2,1)S(1)}) custom-call(bf16[6,2,64,128]{3,2,1,0:T(8,128)(2,1)S(1)} %bitcast.28, bf16[6,2,64,128]{3,2,1,0:T(8,128)(2,1)S(1)} %bitcast.30, ...), custom_call_target="tpu_custom_call" | custom-call | flops 1024 | bytes 1024 | tf_op jit(solution)/shard_map/pallas_call | solution.py:284
  56.4 0.6 collective-permute-start.23
  57.0 1.2 %collective-permute-start.24 = (bf16[3,2,64,128]{3,2,1,0:T(8,128)(2,1)S(1)}, bf16[3,2,64,128]{3,2,1,0:T(8,128)(2,1)S(1)}, u32[]{:S(2)}, u32[]{:S(2)}) collective-permute-start(bf16[3,2,64,128]{3,2,1,0:T(8,128)(2,1)S(1)} %get-tuple-element.153), channel_id=1, source_target_pairs={{0,8},{8,0},{16,24},{24,16},{1,9},{9,1},{17,25},{25,17},{2,10},{10... | collective-permute-start | bytes 294920 | tf_op jit(solution)/shard_map/ppermute | solution.py:63
  58.2 0.9 %collective-permute-start.25 = (bf16[3,2,64,128]{3,2,1,0:T(8,128)(2,1)S(1)}, bf16[3,2,64,128]{3,2,1,0:T(8,128)(2,1)S(1)}, u32[]{:S(2)}, u32[]{:S(2)}) collective-permute-start(bf16[3,2,64,128]{3,2,1,0:T(8,128)(2,1)S(1)} %get-tuple-element.154), channel_id=1, source_target_pairs={{0,16},{8,24},{16,0},{24,8},{1,17},{9,25},{17,1},{25,9},{2,18},{10... | collective-permute-start | bytes 294920 | tf_op jit(solution)/shard_map/ppermute | solution.py:63
  59.2 5.0 %shard_map.108 = (f32[3072,128]{1,0:T(8,128)}, f32[3,16,64,128]{3,2,1,0:T(8,128)S(1)}) custom-call(bf16[4,2,64,128]{3,2,1,0:T(8,128)(2,1)S(1)} %get-tuple-element.115.refs_0_, bf16[4,2,64,128]{3,2,1,0:T(8,128)(2,1)S(1)} %collective-permute-done.3.refs_1_, bf16[4,2,64,128]{3,2,1,0:T(8,128)(2,1)S(1)} %collective-permute-done.4.refs_2_, ...), custom_call_target="tpu_custom_call" | custom-call | flops 1024 | bytes 1024 | tf_op jit(solution)/shard_map/pallas_call | solution.py:446
  64.2 1.6 %shard_map.110 = f32[3072,128]{1,0:T(8,128)} custom-call(bf16[3,2,64,128]{3,2,1,0:T(8,128)(2,1)S(1)} %get-tuple-element.147.refs_0_, bf16[3,2,64,128]{3,2,1,0:T(8,128)(2,1)S(1)} %collective-permute-done.20.refs_1_, bf16[3,2,64,128]{3,2,1,0:T(8,128)(2,1)S(1)} %collective-permute-done.21.refs_2_, bf16[3,2,64,128]{3,2,1,0:T(8,128)(2,1)S(1)} %collective-permute-done.22.refs_3_, ...), custom_call_target="tpu_custom_call" | custom-call | flops 1024 | bytes 1024 | tf_op jit(solution)/shard_map/pallas_call | solution.py:490
  (36 shorter events, 1.0 us)
Async XLA Ops:
  2.2 7.7 %collective-permute-start.6 = (bf16[6,2,32,2,128]{4,3,2,1,0:T(2,128)(2,1)S(1)}, bf16[6,2,32,2,128]{4,3,2,1,0:T(2,128)(2,1)S(1)}, u32[]{:S(2)}, u32[]{:S(2)}) collective-permute-start(bf16[6,2,32,2,128]{4,3,2,1,0:T(2,128)(2,1)S(1)} %shard_map.102), channel_id=1, source_target_pairs={{0,24},{8,16},{16,8},{24,0},{1,25},{9,17},{17,9},{25,1},{2,26},{10... | collective-permute-start | bytes 589832 | tf_op jit(solution)/shard_map/ppermute | solution.py:63
  5.4 8.6 %collective-permute-start.7 = (bf16[6,2,32,2,128]{4,3,2,1,0:T(2,128)(2,1)S(1)}, bf16[6,2,32,2,128]{4,3,2,1,0:T(2,128)(2,1)S(1)}, u32[]{:S(2)}, u32[]{:S(2)}) collective-permute-start(bf16[6,2,32,2,128]{4,3,2,1,0:T(2,128)(2,1)S(1)} %shard_map.103), channel_id=1, source_target_pairs={{0,8},{8,0},{16,24},{24,16},{1,9},{9,1},{17,25},{25,17},{2,10},{10... | collective-permute-start | bytes 589832 | tf_op jit(solution)/shard_map/ppermute | solution.py:63
  5.9 8.8 %collective-permute-start.8 = (bf16[6,2,32,2,128]{4,3,2,1,0:T(2,128)(2,1)S(1)}, bf16[6,2,32,2,128]{4,3,2,1,0:T(2,128)(2,1)S(1)}, u32[]{:S(2)}, u32[]{:S(2)}) collective-permute-start(bf16[6,2,32,2,128]{4,3,2,1,0:T(2,128)(2,1)S(1)} %shard_map.104), channel_id=1, source_target_pairs={{0,16},{8,24},{16,0},{24,8},{1,17},{9,25},{17,1},{25,9},{2,18},{10... | collective-permute-start | bytes 589832 | tf_op jit(solution)/shard_map/ppermute | solution.py:63
  6.2 4.8 %copy-start.3 = (bf16[256,256]{1,0:T(8,128)(2,1)S(1)}, bf16[256,256]{1,0:T(8,128)(2,1)}, u32[]{:S(2)}) copy-start(bf16[256,256]{1,0:T(8,128)(2,1)} %constant.5.clone.refs_1_) | copy-start | bytes 393220
  6.2 4.8 %copy-start.4 = (bf16[256,256]{1,0:T(8,128)(2,1)S(1)}, bf16[256,256]{1,0:T(8,128)(2,1)}, u32[]{:S(2)}) copy-start(bf16[256,256]{1,0:T(8,128)(2,1)} %constant.4.clone.refs_0_) | copy-start | bytes 393220
  6.2 12.1 %collective-permute-start.1 = (bf16[6,2,32,2,128]{4,3,2,1,0:T(2,128)(2,1)S(1)}, bf16[6,2,32,2,128]{4,3,2,1,0:T(2,128)(2,1)S(1)}, u32[]{:S(2)}, u32[]{:S(2)}) collective-permute-start(bf16[6,2,32,2,128]{4,3,2,1,0:T(2,128)(2,1)S(1)} %shard_map.98), channel_id=1, source_target_pairs={{0,8},{8,0},{16,24},{24,16},{1,9},{9,1},{17,25},{25,17},{2,10},{10... | collective-permute-start | bytes 589832 | tf_op jit(solution)/shard_map/ppermute | solution.py:63
  7.9 14.7 %collective-permute-start = (bf16[6,2,32,2,128]{4,3,2,1,0:T(2,128)(2,1)S(1)}, bf16[6,2,32,2,128]{4,3,2,1,0:T(2,128)(2,1)S(1)}, u32[]{:S(2)}, u32[]{:S(2)}) collective-permute-start(bf16[6,2,32,2,128]{4,3,2,1,0:T(2,128)(2,1)S(1)} %shard_map.97), channel_id=1, source_target_pairs={{0,24},{8,16},{16,8},{24,0},{1,25},{9,17},{17,9},{25,1},{2,26},{10... | collective-permute-start | bytes 589832 | tf_op jit(solution)/shard_map/ppermute | solution.py:63
  9.1 10.6 %copy-start = (bf16[12,32,2,2048]{3,2,1,0:T(2,128)(2,1)S(1)}, bf16[12,32,2,2048]{3,2,1,0:T(2,128)(2,1)}, u32[]{:S(2)}) copy-start(bf16[12,32,2,2048]{3,2,1,0:T(2,128)(2,1)} %fields_ref.3) | copy-start | bytes 9437188
  9.9 12.6 %collective-permute-start.2 = (bf16[6,2,32,2,128]{4,3,2,1,0:T(2,128)(2,1)S(1)}, bf16[6,2,32,2,128]{4,3,2,1,0:T(2,128)(2,1)S(1)}, u32[]{:S(2)}, u32[]{:S(2)}) collective-permute-start(bf16[6,2,32,2,128]{4,3,2,1,0:T(2,128)(2,1)S(1)} %shard_map.99), channel_id=1, source_target_pairs={{0,16},{8,24},{16,0},{24,8},{1,17},{9,25},{17,1},{25,9},{2,18},{10... | collective-permute-start | bytes 589832 | tf_op jit(solution)/shard_map/ppermute | solution.py:63
  15.5 10.3 %collective-permute-start.9 = (bf16[4,2,64,128]{3,2,1,0:T(8,128)(2,1)S(1)}, bf16[4,2,64,128]{3,2,1,0:T(8,128)(2,1)S(1)}, u32[]{:S(2)}, u32[]{:S(2)}) collective-permute-start(bf16[4,2,64,128]{3,2,1,0:T(8,128)(2,1)S(1)} %get-tuple-element.93), channel_id=1, source_target_pairs={{0,24},{8,16},{16,8},{24,0},{1,25},{9,17},{17,9},{25,1},{2,26},{10... | collective-permute-start | bytes 393224 | tf_op jit(solution)/shard_map/ppermute | solution.py:63
  18.3 9.9 %collective-permute-start.10 = (bf16[4,2,64,128]{3,2,1,0:T(8,128)(2,1)S(1)}, bf16[4,2,64,128]{3,2,1,0:T(8,128)(2,1)S(1)}, u32[]{:S(2)}, u32[]{:S(2)}) collective-permute-start(bf16[4,2,64,128]{3,2,1,0:T(8,128)(2,1)S(1)} %get-tuple-element.94), channel_id=1, source_target_pairs={{0,8},{8,0},{16,24},{24,16},{1,9},{9,1},{17,25},{25,17},{2,10},{10... | collective-permute-start | bytes 393224 | tf_op jit(solution)/shard_map/ppermute | solution.py:63
  19.5 18.2 %copy-start.7 = (s32[2,256]{1,0:T(2,128)S(1)}, s32[2,256]{1,0:T(2,128)}, u32[]{:S(2)}) copy-start(s32[2,256]{1,0:T(2,128)} %refs_8_.1) | copy-start | bytes 6148
  19.5 9.9 %collective-permute-start.11 = (bf16[4,2,64,128]{3,2,1,0:T(8,128)(2,1)S(1)}, bf16[4,2,64,128]{3,2,1,0:T(8,128)(2,1)S(1)}, u32[]{:S(2)}, u32[]{:S(2)}) collective-permute-start(bf16[4,2,64,128]{3,2,1,0:T(8,128)(2,1)S(1)} %get-tuple-element.95), channel_id=1, source_target_pairs={{0,16},{8,24},{16,0},{24,8},{1,17},{9,25},{17,1},{25,9},{2,18},{10... | collective-permute-start | bytes 393224 | tf_op jit(solution)/shard_map/ppermute | solution.py:63
  23.4 8.8 %collective-permute-start.3 = (bf16[4,2,64,128]{3,2,1,0:T(8,128)(2,1)S(1)}, bf16[4,2,64,128]{3,2,1,0:T(8,128)(2,1)S(1)}, u32[]{:S(2)}, u32[]{:S(2)}) collective-permute-start(bf16[4,2,64,128]{3,2,1,0:T(8,128)(2,1)S(1)} %get-tuple-element.88), channel_id=1, source_target_pairs={{0,24},{8,16},{16,8},{24,0},{1,25},{9,17},{17,9},{25,1},{2,26},{10... | collective-permute-start | bytes 393224 | tf_op jit(solution)/shard_map/ppermute | solution.py:63
  25.6 8.2 %collective-permute-start.4 = (bf16[4,2,64,128]{3,2,1,0:T(8,128)(2,1)S(1)}, bf16[4,2,64,128]{3,2,1,0:T(8,128)(2,1)S(1)}, u32[]{:S(2)}, u32[]{:S(2)}) collective-permute-start(bf16[4,2,64,128]{3,2,1,0:T(8,128)(2,1)S(1)} %get-tuple-element.89), channel_id=1, source_target_pairs={{0,8},{8,0},{16,24},{24,16},{1,9},{9,1},{17,25},{25,17},{2,10},{10... | collective-permute-start | bytes 393224 | tf_op jit(solution)/shard_map/ppermute | solution.py:63
  25.8 8.2 %collective-permute-start.5 = (bf16[4,2,64,128]{3,2,1,0:T(8,128)(2,1)S(1)}, bf16[4,2,64,128]{3,2,1,0:T(8,128)(2,1)S(1)}, u32[]{:S(2)}, u32[]{:S(2)}) collective-permute-start(bf16[4,2,64,128]{3,2,1,0:T(8,128)(2,1)S(1)} %get-tuple-element.90), channel_id=1, source_target_pairs={{0,16},{8,24},{16,0},{24,8},{1,17},{9,25},{17,1},{25,9},{2,18},{10... | collective-permute-start | bytes 393224 | tf_op jit(solution)/shard_map/ppermute | solution.py:63
  29.4 14.6 %collective-permute-start.17 = (bf16[6,2,32,2,128]{4,3,2,1,0:T(2,128)(2,1)S(1)}, bf16[6,2,32,2,128]{4,3,2,1,0:T(2,128)(2,1)S(1)}, u32[]{:S(2)}, u32[]{:S(2)}) collective-permute-start(bf16[6,2,32,2,128]{4,3,2,1,0:T(2,128)(2,1)S(1)} %get-tuple-element.144), channel_id=1, source_target_pairs={{0,24},{8,16},{16,8},{24,0},{1,25},{9,17},{17,9},{25,1},{2,26},{10... | collective-permute-start | bytes 589832 | tf_op jit(solution)/shard_map/ppermute | solution.py:63
  34.0 11.4 %collective-permute-start.18 = (bf16[6,2,32,2,128]{4,3,2,1,0:T(2,128)(2,1)S(1)}, bf16[6,2,32,2,128]{4,3,2,1,0:T(2,128)(2,1)S(1)}, u32[]{:S(2)}, u32[]{:S(2)}) collective-permute-start(bf16[6,2,32,2,128]{4,3,2,1,0:T(2,128)(2,1)S(1)} %get-tuple-element.145), channel_id=1, source_target_pairs={{0,8},{8,0},{16,24},{24,16},{1,9},{9,1},{17,25},{25,17},{2,10},{10... | collective-permute-start | bytes 589832 | tf_op jit(solution)/shard_map/ppermute | solution.py:63
  35.4 10.9 %collective-permute-start.19 = (bf16[6,2,32,2,128]{4,3,2,1,0:T(2,128)(2,1)S(1)}, bf16[6,2,32,2,128]{4,3,2,1,0:T(2,128)(2,1)S(1)}, u32[]{:S(2)}, u32[]{:S(2)}) collective-permute-start(bf16[6,2,32,2,128]{4,3,2,1,0:T(2,128)(2,1)S(1)} %get-tuple-element.146), channel_id=1, source_target_pairs={{0,16},{8,24},{16,0},{24,8},{1,17},{9,25},{17,1},{25,9},{2,18},{10... | collective-permute-start | bytes 589832 | tf_op jit(solution)/shard_map/ppermute | solution.py:63
  38.9 10.2 %collective-permute-start.15 = (bf16[4,2,64,128]{3,2,1,0:T(8,128)(2,1)S(1)}, bf16[4,2,64,128]{3,2,1,0:T(8,128)(2,1)S(1)}, u32[]{:S(2)}, u32[]{:S(2)}) collective-permute-start(bf16[4,2,64,128]{3,2,1,0:T(8,128)(2,1)S(1)} %get-tuple-element.127), channel_id=1, source_target_pairs={{0,1},{1,2},{2,3},{3,4},{4,5},{5,6},{6,7},{8,9},{9,10},{10,11},{11... | collective-permute-start | bytes 393224 | tf_op jit(solution)/shard_map/ppermute | solution.py:70
  43.6 9.6 %collective-permute-start.12 = (bf16[6,2,32,2,128]{4,3,2,1,0:T(2,128)(2,1)S(1)}, bf16[6,2,32,2,128]{4,3,2,1,0:T(2,128)(2,1)S(1)}, u32[]{:S(2)}, u32[]{:S(2)}) collective-permute-start(bf16[6,2,32,2,128]{4,3,2,1,0:T(2,128)(2,1)S(1)} %get-tuple-element.124), channel_id=1, source_target_pairs={{0,24},{8,16},{16,8},{24,0},{1,25},{9,17},{17,9},{25,1},{2,26},{10... | collective-permute-start | bytes 589832 | tf_op jit(solution)/shard_map/ppermute | solution.py:63
  44.0 11.0 %collective-permute-start.13 = (bf16[6,2,32,2,128]{4,3,2,1,0:T(2,128)(2,1)S(1)}, bf16[6,2,32,2,128]{4,3,2,1,0:T(2,128)(2,1)S(1)}, u32[]{:S(2)}, u32[]{:S(2)}) collective-permute-start(bf16[6,2,32,2,128]{4,3,2,1,0:T(2,128)(2,1)S(1)} %get-tuple-element.125), channel_id=1, source_target_pairs={{0,8},{8,0},{16,24},{24,16},{1,9},{9,1},{17,25},{25,17},{2,10},{10... | collective-permute-start | bytes 589832 | tf_op jit(solution)/shard_map/ppermute | solution.py:63
  45.3 10.2 %collective-permute-start.14 = (bf16[6,2,32,2,128]{4,3,2,1,0:T(2,128)(2,1)S(1)}, bf16[6,2,32,2,128]{4,3,2,1,0:T(2,128)(2,1)S(1)}, u32[]{:S(2)}, u32[]{:S(2)}) collective-permute-start(bf16[6,2,32,2,128]{4,3,2,1,0:T(2,128)(2,1)S(1)} %get-tuple-element.126), channel_id=1, source_target_pairs={{0,16},{8,24},{16,0},{24,8},{1,17},{9,25},{17,1},{25,9},{2,18},{10... | collective-permute-start | bytes 589832 | tf_op jit(solution)/shard_map/ppermute | solution.py:63
  46.3 6.6 %collective-permute-start.16 = (bf16[4,2,64,128]{3,2,1,0:T(8,128)(2,1)S(1)}, bf16[4,2,64,128]{3,2,1,0:T(8,128)(2,1)S(1)}, u32[]{:S(2)}, u32[]{:S(2)}) collective-permute-start(bf16[4,2,64,128]{3,2,1,0:T(8,128)(2,1)S(1)} %get-tuple-element.128), channel_id=1, source_target_pairs={{1,0},{2,1},{3,2},{4,3},{5,4},{6,5},{7,6},{9,8},{10,9},{11,10},{12... | collective-permute-start | bytes 393224 | tf_op jit(solution)/shard_map/ppermute | solution.py:70
  49.2 9.1 %collective-permute-start.20 = (bf16[3,2,64,128]{3,2,1,0:T(8,128)(2,1)S(1)}, bf16[3,2,64,128]{3,2,1,0:T(8,128)(2,1)S(1)}, u32[]{:S(2)}, u32[]{:S(2)}) collective-permute-start(bf16[3,2,64,128]{3,2,1,0:T(8,128)(2,1)S(1)} %get-tuple-element.148), channel_id=1, source_target_pairs={{0,24},{8,16},{16,8},{24,0},{1,25},{9,17},{17,9},{25,1},{2,26},{10... | collective-permute-start | bytes 294920 | tf_op jit(solution)/shard_map/ppermute | solution.py:63
  52.9 11.3 %collective-permute-start.21 = (bf16[3,2,64,128]{3,2,1,0:T(8,128)(2,1)S(1)}, bf16[3,2,64,128]{3,2,1,0:T(8,128)(2,1)S(1)}, u32[]{:S(2)}, u32[]{:S(2)}) collective-permute-start(bf16[3,2,64,128]{3,2,1,0:T(8,128)(2,1)S(1)} %get-tuple-element.149), channel_id=1, source_target_pairs={{0,8},{8,0},{16,24},{24,16},{1,9},{9,1},{17,25},{25,17},{2,10},{10... | collective-permute-start | bytes 294920 | tf_op jit(solution)/shard_map/ppermute | solution.py:63
  53.2 11.0 %collective-permute-start.22 = (bf16[3,2,64,128]{3,2,1,0:T(8,128)(2,1)S(1)}, bf16[3,2,64,128]{3,2,1,0:T(8,128)(2,1)S(1)}, u32[]{:S(2)}, u32[]{:S(2)}) collective-permute-start(bf16[3,2,64,128]{3,2,1,0:T(8,128)(2,1)S(1)} %get-tuple-element.150), channel_id=1, source_target_pairs={{0,16},{8,24},{16,0},{24,8},{1,17},{9,25},{17,1},{25,9},{2,18},{10... | collective-permute-start | bytes 294920 | tf_op jit(solution)/shard_map/ppermute | solution.py:63
  55.5 3.7 %copy-start.1 = (bf16[5,64,2048]{2,1,0:T(8,128)(2,1)S(1)}, bf16[5,64,2048]{2,1,0:T(8,128)(2,1)}, u32[]{:S(2)}) copy-start(bf16[5,64,2048]{2,1,0:T(8,128)(2,1)} %refs_10_.1) | copy-start | bytes 3932164
  55.5 3.7 %copy-start.2 = (bf16[5,64,2048]{2,1,0:T(8,128)(2,1)S(1)}, bf16[5,64,2048]{2,1,0:T(8,128)(2,1)}, u32[]{:S(2)}) copy-start(bf16[5,64,2048]{2,1,0:T(8,128)(2,1)} %refs_11_.1) | copy-start | bytes 3932164
  55.5 3.7 %copy-start.5 = (f32[2048]{0:T(1024)S(1)}, f32[2048]{0:T(1024)}, u32[]{:S(2)}) copy-start(f32[2048]{0:T(1024)} %param.9) | copy-start | bytes 24580
  55.5 3.7 %copy-start.6 = (s32[32,5]{0,1:T(8,128)S(1)}, s32[32,5]{0,1:T(8,128)}, u32[]{:S(2)}) copy-start(s32[32,5]{0,1:T(8,128)} %param.12) | copy-start | bytes 1924
  56.4 7.7 %collective-permute-start.23 = (bf16[3,2,64,128]{3,2,1,0:T(8,128)(2,1)S(1)}, bf16[3,2,64,128]{3,2,1,0:T(8,128)(2,1)S(1)}, u32[]{:S(2)}, u32[]{:S(2)}) collective-permute-start(bf16[3,2,64,128]{3,2,1,0:T(8,128)(2,1)S(1)} %get-tuple-element.152), channel_id=1, source_target_pairs={{0,24},{8,16},{16,8},{24,0},{1,25},{9,17},{17,9},{25,1},{2,26},{10... | collective-permute-start | bytes 294920 | tf_op jit(solution)/shard_map/ppermute | solution.py:63
  57.0 7.1 %collective-permute-start.24 = (bf16[3,2,64,128]{3,2,1,0:T(8,128)(2,1)S(1)}, bf16[3,2,64,128]{3,2,1,0:T(8,128)(2,1)S(1)}, u32[]{:S(2)}, u32[]{:S(2)}) collective-permute-start(bf16[3,2,64,128]{3,2,1,0:T(8,128)(2,1)S(1)} %get-tuple-element.153), channel_id=1, source_target_pairs={{0,8},{8,0},{16,24},{24,16},{1,9},{9,1},{17,25},{25,17},{2,10},{10... | collective-permute-start | bytes 294920 | tf_op jit(solution)/shard_map/ppermute | solution.py:63
  58.2 5.9 %collective-permute-start.25 = (bf16[3,2,64,128]{3,2,1,0:T(8,128)(2,1)S(1)}, bf16[3,2,64,128]{3,2,1,0:T(8,128)(2,1)S(1)}, u32[]{:S(2)}, u32[]{:S(2)}) collective-permute-start(bf16[3,2,64,128]{3,2,1,0:T(8,128)(2,1)S(1)} %get-tuple-element.154), channel_id=1, source_target_pairs={{0,16},{8,24},{16,0},{24,8},{1,17},{9,25},{17,1},{25,9},{2,18},{10... | collective-permute-start | bytes 294920 | tf_op jit(solution)/shard_map/ppermute | solution.py:63

commit v20 on v19

--- a/solution.py
+++ b/solution.py
@@ -543,18 +543,16 @@
     toward_prev, toward_next = interface(local, interface_nodes, count)
     halos = (from_behind(toward_next, "mer", 1), from_behind(toward_prev, "mer", -1))
     local, shares[count:] = lax.optimization_barrier((local, shares[count:]))
+    induction, gradient = derive(
+        local, *halos, radial_blocks, axial_blocks, radius.reshape(1, width), block_columns.T, count
+    )
     lorentz = []
     for part, (begin, _) in enumerate(spans):
         sources = exchange(shares[part * count : (part + 1) * count], order)
         if part == len(spans) - 1:
-            sources, halos = lax.optimization_barrier((sources, halos))
+            sources, gradient = lax.optimization_barrier((sources, gradient))
         terms = list(second_physics(joined(sources), physical, begin, later_inverse, later_forward))
-        if part == len(spans) - 1:
-            terms, radius = lax.optimization_barrier((terms, radius))
         lorentz += exchange(terms, offsets(count, SECOND_RETURN))
-    induction, gradient = derive(
-        local, *halos, radial_blocks, axial_blocks, radius.reshape(1, width), block_columns.T, count
-    )
     momentum = momentum_of(lorentz, gradient, count)
     return (whole_output(induction, mode_count, width), whole_output(momentum, mode_count, width))
 

time: 67 us -> 68.6 us (1.024)
  waiting for transfers between devices: 15.6 us -> 17.2 us
    ppermute x24, waiting for transfers between devices: 12.3 us -> 14 us  [exchange(): received.append(lax.ppermute(piece, 'mode', pairs))]
  transfers between devices with their start and end apart: 26 -> 26, of which waited for: 12 -> 15; matrix products, arithmetic and copies ran while one was open for 0% -> 0% of each run, Pallas kernels for 18% -> 18%
where the time goes in v20:
time: 68.6 us; the launch traced here: 67.5 us
  starting transfers between devices  34 us (50%)
  waiting for transfers between devices  17.2 us (25%)
  Pallas kernels  15.3 us (22%)
  between operations  0.85 us (1%)
    ppermute x24, starting transfers between devices, exchange(): received.append(lax.ppermute(piece, 'mode', pairs))  27.4 us
    ppermute x24, waiting for transfers between devices, exchange(): received.append(lax.ppermute(piece, 'mode', pairs))  14 us
    ppermute x2, starting transfers between devices, from_behind(): lax.ppermute(value, axis, [(source, source + steps) for source in range(i...  6.58 us
    pallas_call x1, Pallas kernels, derive(): pl.pallas_call(functools.partial(derive_kernel, count, len(received)), in...  5.02 us
    ppermute x2, waiting for transfers between devices, from_behind(): lax.ppermute(value, axis, [(source, source + steps) for source in range(i...  3.18 us
    pallas_call x2, Pallas kernels, second_physics(): pl.pallas_call(functools.partial(second_kernel, count, groups, begin), in...  1.89 us
    pallas_call x2, Pallas kernels, first_physics(): pl.pallas_call(functools.partial(first_kernel, count), in_specs=[vmem()]...  1.65 us
    pallas_call x2, Pallas kernels, pack_rest(): pl.pallas_call(kernel, in_specs=[pl.BlockSpec(memory_space=pl.ANY)] + [vm...  1.62 us
  transfers between devices with their start and end apart: 26, of which 15 were waited for; matrix products, arithmetic and copies ran while one was open for 0% of the time, Pallas kernels for 18%

profile of v20, /device:TPU:1, one launch (start us, length us, event | category | flops | bytes accessed | tf_op | source)
XLA Modules:
  0.0 67.5 jit_solution(8079734585066394986)
XLA Ops:
  0.6 1.4 %shard_map.95.fields_ref = bf16[6,32,2,2048]{3,2,1,0:T(2,128)(2,1)S(1)} custom-call(bf16[12,32,2,2048]{3,2,1,0:T(2,128)(2,1)} %fields_ref.3), custom_call_target="tpu_custom_call" | custom-call | flops 1024 | bytes 1024 | tf_op jit(solution)/shard_map/pallas_call | solution.py:123
  2.2 3.1 %collective-permute-start.6 = (bf16[6,2,32,2,128]{4,3,2,1,0:T(2,128)(2,1)S(1)}, bf16[6,2,32,2,128]{4,3,2,1,0:T(2,128)(2,1)S(1)}, u32[]{:S(2)}, u32[]{:S(2)}) collective-permute-start(bf16[6,2,32,2,128]{4,3,2,1,0:T(2,128)(2,1)S(1)} %shard_map.102), channel_id=1, source_target_pairs={{0,24},{8,16},{16,8},{24,0},{1,25},{9,17},{17,9},{25,1},{2,26},{10... | collective-permute-start | bytes 589832 | tf_op jit(solution)/shard_map/ppermute | solution.py:63
  5.4 0.3 collective-permute-start.7
  6.2 1.4 %collective-permute-start.1 = (bf16[6,2,32,2,128]{4,3,2,1,0:T(2,128)(2,1)S(1)}, bf16[6,2,32,2,128]{4,3,2,1,0:T(2,128)(2,1)S(1)}, u32[]{:S(2)}, u32[]{:S(2)}) collective-permute-start(bf16[6,2,32,2,128]{4,3,2,1,0:T(2,128)(2,1)S(1)} %shard_map.98), channel_id=1, source_target_pairs={{0,8},{8,0},{16,24},{24,16},{1,9},{9,1},{17,25},{25,17},{2,10},{10... | collective-permute-start | bytes 589832 | tf_op jit(solution)/shard_map/ppermute | solution.py:63
  7.9 1.3 %collective-permute-start = (bf16[6,2,32,2,128]{4,3,2,1,0:T(2,128)(2,1)S(1)}, bf16[6,2,32,2,128]{4,3,2,1,0:T(2,128)(2,1)S(1)}, u32[]{:S(2)}, u32[]{:S(2)}) collective-permute-start(bf16[6,2,32,2,128]{4,3,2,1,0:T(2,128)(2,1)S(1)} %shard_map.97), channel_id=1, source_target_pairs={{0,24},{8,16},{16,8},{24,0},{1,25},{9,17},{17,9},{25,1},{2,26},{10... | collective-permute-start | bytes 589832 | tf_op jit(solution)/shard_map/ppermute | solution.py:63
  9.3 0.6 collective-permute-done.6
  9.9 1.2 %collective-permute-start.2 = (bf16[6,2,32,2,128]{4,3,2,1,0:T(2,128)(2,1)S(1)}, bf16[6,2,32,2,128]{4,3,2,1,0:T(2,128)(2,1)S(1)}, u32[]{:S(2)}, u32[]{:S(2)}) collective-permute-start(bf16[6,2,32,2,128]{4,3,2,1,0:T(2,128)(2,1)S(1)} %shard_map.99), channel_id=1, source_target_pairs={{0,16},{8,24},{16,0},{24,8},{1,17},{9,25},{17,1},{25,9},{2,18},{10... | collective-permute-start | bytes 589832 | tf_op jit(solution)/shard_map/ppermute | solution.py:63
  11.1 0.3 shard_map.96
  11.4 2.7 %collective-permute-done.7 = bf16[6,2,32,2,128]{4,3,2,1,0:T(2,128)(2,1)S(1)} collective-permute-done((bf16[6,2,32,2,128]{4,3,2,1,0:T(2,128)(2,1)S(1)}, bf16[6,2,32,2,128]{4,3,2,1,0:T(2,128)(2,1)S(1)}, u32[]{:S(2)}, u32[]{:S(2)}) %collective-permute-start.7) | collective-permute-done | bytes 196640 | tf_op jit(solution)/shard_map/ppermute | solution.py:63
  14.1 0.6 collective-permute-done.8
  14.7 0.8 %shard_map.105 = (bf16[4,2,64,128]{3,2,1,0:T(8,128)(2,1)S(1)}, bf16[4,2,64,128]{3,2,1,0:T(8,128)(2,1)S(1)}, bf16[4,2,64,128]{3,2,1,0:T(8,128)(2,1)S(1)}, bf16[4,...) custom-call(bf16[6,2,64,128]{3,2,1,0:T(8,128)(2,1)S(1)} %bitcast.43, bf16[6,2,64,128]{3,2,1,0:T(8,128)(2,1)S(1)} %bitcast.40, ...), custom_call_target="tpu_custom_call" | custom-call | flops 1024 | bytes 1024 | tf_op jit(solution)/shard_map/pallas_call | solution.py:238
  15.5 2.6 %collective-permute-start.9 = (bf16[4,2,64,128]{3,2,1,0:T(8,128)(2,1)S(1)}, bf16[4,2,64,128]{3,2,1,0:T(8,128)(2,1)S(1)}, u32[]{:S(2)}, u32[]{:S(2)}) collective-permute-start(bf16[4,2,64,128]{3,2,1,0:T(8,128)(2,1)S(1)} %get-tuple-element.87), channel_id=1, source_target_pairs={{0,24},{8,16},{16,8},{24,0},{1,25},{9,17},{17,9},{25,1},{2,26},{10... | collective-permute-start | bytes 393224 | tf_op jit(solution)/shard_map/ppermute | solution.py:63
  18.1 0.2 collective-permute-done.1
  18.3 1.2 %collective-permute-start.10 = (bf16[4,2,64,128]{3,2,1,0:T(8,128)(2,1)S(1)}, bf16[4,2,64,128]{3,2,1,0:T(8,128)(2,1)S(1)}, u32[]{:S(2)}, u32[]{:S(2)}) collective-permute-start(bf16[4,2,64,128]{3,2,1,0:T(8,128)(2,1)S(1)} %get-tuple-element.88), channel_id=1, source_target_pairs={{0,8},{8,0},{16,24},{24,16},{1,9},{9,1},{17,25},{25,17},{2,10},{10... | collective-permute-start | bytes 393224 | tf_op jit(solution)/shard_map/ppermute | solution.py:63
  19.7 1.3 %shard_map.100 = (bf16[6,2,32,2,128]{4,3,2,1,0:T(2,128)(2,1)S(1)}, bf16[6,2,32,2,128]{4,3,2,1,0:T(2,128)(2,1)S(1)}, bf16[6,2,32,2,128]{4,3,2,1,0:T(2,128)(2,1)S(...) custom-call(bf16[12,32,2,2048]{3,2,1,0:T(2,128)(2,1)S(1)} %copy-done, ...), custom_call_target="tpu_custom_call" | custom-call | flops 1024 | bytes 1024 | tf_op jit(solution)/shard_map/pallas_call | solution.py:170
  21.0 1.5 %collective-permute-done = bf16[6,2,32,2,128]{4,3,2,1,0:T(2,128)(2,1)S(1)} collective-permute-done((bf16[6,2,32,2,128]{4,3,2,1,0:T(2,128)(2,1)S(1)}, bf16[6,2,32,2,128]{4,3,2,1,0:T(2,128)(2,1)S(1)}, u32[]{:S(2)}, u32[]{:S(2)}) %collective-permute-start) | collective-permute-done | bytes 196640 | tf_op jit(solution)/shard_map/ppermute | solution.py:63
  22.5 0.8 %shard_map.101 = (bf16[4,2,64,128]{3,2,1,0:T(8,128)(2,1)S(1)}, bf16[4,2,64,128]{3,2,1,0:T(8,128)(2,1)S(1)}, bf16[4,2,64,128]{3,2,1,0:T(8,128)(2,1)S(1)}, bf16[4,...) custom-call(bf16[6,2,64,128]{3,2,1,0:T(8,128)(2,1)S(1)} %bitcast.39, bf16[6,2,64,128]{3,2,1,0:T(8,128)(2,1)S(1)} %bitcast.37, ...), custom_call_target="tpu_custom_call" | custom-call | flops 1024 | bytes 1024 | tf_op jit(solution)/shard_map/pallas_call | solution.py:238
  23.4 2.2 %collective-permute-start.3 = (bf16[4,2,64,128]{3,2,1,0:T(8,128)(2,1)S(1)}, bf16[4,2,64,128]{3,2,1,0:T(8,128)(2,1)S(1)}, u32[]{:S(2)}, u32[]{:S(2)}) collective-permute-start(bf16[4,2,64,128]{3,2,1,0:T(8,128)(2,1)S(1)} %get-tuple-element.82), channel_id=1, source_target_pairs={{0,24},{8,16},{16,8},{24,0},{1,25},{9,17},{17,9},{25,1},{2,26},{10... | collective-permute-start | bytes 393224 | tf_op jit(solution)/shard_map/ppermute | solution.py:63
  25.6 0.2 collective-permute-start.4
  25.8 0.8 %collective-permute-start.5 = (bf16[4,2,64,128]{3,2,1,0:T(8,128)(2,1)S(1)}, bf16[4,2,64,128]{3,2,1,0:T(8,128)(2,1)S(1)}, u32[]{:S(2)}, u32[]{:S(2)}) collective-permute-start(bf16[4,2,64,128]{3,2,1,0:T(8,128)(2,1)S(1)} %get-tuple-element.84), channel_id=1, source_target_pairs={{0,16},{8,24},{16,0},{24,8},{1,17},{9,25},{17,1},{25,9},{2,18},{10... | collective-permute-start | bytes 393224 | tf_op jit(solution)/shard_map/ppermute | solution.py:63
  26.6 1.6 %collective-permute-done.10.refs_6_ = bf16[4,2,64,128]{3,2,1,0:T(8,128)(2,1)S(1)} collective-permute-done((bf16[4,2,64,128]{3,2,1,0:T(8,128)(2,1)S(1)}, bf16[4,2,64,128]{3,2,1,0:T(8,128)(2,1)S(1)}, u32[]{:S(2)}, u32[]{:S(2)}) %collective-permute-start.10) | collective-permute-done | bytes 131104 | tf_op jit(solution)/shard_map/ppermute | solution.py:63
  28.2 1.2 %collective-permute-done.11.refs_7_ = bf16[4,2,64,128]{3,2,1,0:T(8,128)(2,1)S(1)} collective-permute-done((bf16[4,2,64,128]{3,2,1,0:T(8,128)(2,1)S(1)}, bf16[4,2,64,128]{3,2,1,0:T(8,128)(2,1)S(1)}, u32[]{:S(2)}, u32[]{:S(2)}) %collective-permute-start.11) | collective-permute-done | bytes 131104 | tf_op jit(solution)/shard_map/ppermute | solution.py:63
  29.4 2.7 %collective-permute-start.14 = (bf16[6,2,32,2,128]{4,3,2,1,0:T(2,128)(2,1)S(1)}, bf16[6,2,32,2,128]{4,3,2,1,0:T(2,128)(2,1)S(1)}, u32[]{:S(2)}, u32[]{:S(2)}) collective-permute-start(bf16[6,2,32,2,128]{4,3,2,1,0:T(2,128)(2,1)S(1)} %get-tuple-element.121), channel_id=1, source_target_pairs={{0,24},{8,16},{16,8},{24,0},{1,25},{9,17},{17,9},{25,1},{2,26},{10... | collective-permute-start | bytes 589832 | tf_op jit(solution)/shard_map/ppermute | solution.py:63
  32.1 1.7 %collective-permute-done.4.refs_2_ = bf16[4,2,64,128]{3,2,1,0:T(8,128)(2,1)S(1)} collective-permute-done((bf16[4,2,64,128]{3,2,1,0:T(8,128)(2,1)S(1)}, bf16[4,2,64,128]{3,2,1,0:T(8,128)(2,1)S(1)}, u32[]{:S(2)}, u32[]{:S(2)}) %collective-permute-start.4) | collective-permute-done | bytes 131104 | tf_op jit(solution)/shard_map/ppermute | solution.py:63
  34.0 1.4 %collective-permute-start.15 = (bf16[6,2,32,2,128]{4,3,2,1,0:T(2,128)(2,1)S(1)}, bf16[6,2,32,2,128]{4,3,2,1,0:T(2,128)(2,1)S(1)}, u32[]{:S(2)}, u32[]{:S(2)}) collective-permute-start(bf16[6,2,32,2,128]{4,3,2,1,0:T(2,128)(2,1)S(1)} %get-tuple-element.122), channel_id=1, source_target_pairs={{0,8},{8,0},{16,24},{24,16},{1,9},{9,1},{17,25},{25,17},{2,10},{10... | collective-permute-start | bytes 589832 | tf_op jit(solution)/shard_map/ppermute | solution.py:63
  35.4 2.3 %collective-permute-start.16 = (bf16[6,2,32,2,128]{4,3,2,1,0:T(2,128)(2,1)S(1)}, bf16[6,2,32,2,128]{4,3,2,1,0:T(2,128)(2,1)S(1)}, u32[]{:S(2)}, u32[]{:S(2)}) collective-permute-start(bf16[6,2,32,2,128]{4,3,2,1,0:T(2,128)(2,1)S(1)} %get-tuple-element.123), channel_id=1, source_target_pairs={{0,16},{8,24},{16,0},{24,8},{1,17},{9,25},{17,1},{25,9},{2,18},{10... | collective-permute-start | bytes 589832 | tf_op jit(solution)/shard_map/ppermute | solution.py:63
  37.7 1.2 %shard_map.106 = (bf16[4,2,64,128]{3,2,1,0:T(8,128)(2,1)S(1)}, bf16[4,2,64,128]{3,2,1,0:T(8,128)(2,1)S(1)}) custom-call(bf16[4,2,64,128]{3,2,1,0:T(8,128)(2,1)S(1)} %get-tuple-element.109.refs_0_, bf16[4,2,64,128]{3,2,1,0:T(8,128)(2,1)S(1)} %collective-permute-done.3.refs_1_, bf16[4,2,64,128]{3,2,1,0:T(8,128)(2,1)S(1)} %collective-permute-done.4.refs_2_, ...), custom_call_target="tpu_custom_call" | custom-call | flops 1024 | bytes 1024 | tf_op jit(solution)/shard_map/pallas_call | solution.py:334
  38.9 4.7 %collective-permute-start.12 = (bf16[4,2,64,128]{3,2,1,0:T(8,128)(2,1)S(1)}, bf16[4,2,64,128]{3,2,1,0:T(8,128)(2,1)S(1)}, u32[]{:S(2)}, u32[]{:S(2)}) collective-permute-start(bf16[4,2,64,128]{3,2,1,0:T(8,128)(2,1)S(1)} %get-tuple-element.117), channel_id=1, source_target_pairs={{0,1},{1,2},{2,3},{3,4},{4,5},{5,6},{6,7},{8,9},{9,10},{10,11},{11... | collective-permute-start | bytes 393224 | tf_op jit(solution)/shard_map/ppermute | solution.py:70
  43.6 0.4 collective-permute-start.20
  44.0 1.3 %collective-permute-start.21 = (bf16[6,2,32,2,128]{4,3,2,1,0:T(2,128)(2,1)S(1)}, bf16[6,2,32,2,128]{4,3,2,1,0:T(2,128)(2,1)S(1)}, u32[]{:S(2)}, u32[]{:S(2)}) collective-permute-start(bf16[6,2,32,2,128]{4,3,2,1,0:T(2,128)(2,1)S(1)} %get-tuple-element.132), channel_id=1, source_target_pairs={{0,8},{8,0},{16,24},{24,16},{1,9},{9,1},{17,25},{25,17},{2,10},{10... | collective-permute-start | bytes 589832 | tf_op jit(solution)/shard_map/ppermute | solution.py:63
  45.3 1.0 %collective-permute-start.22 = (bf16[6,2,32,2,128]{4,3,2,1,0:T(2,128)(2,1)S(1)}, bf16[6,2,32,2,128]{4,3,2,1,0:T(2,128)(2,1)S(1)}, u32[]{:S(2)}, u32[]{:S(2)}) collective-permute-start(bf16[6,2,32,2,128]{4,3,2,1,0:T(2,128)(2,1)S(1)} %get-tuple-element.133), channel_id=1, source_target_pairs={{0,16},{8,24},{16,0},{24,8},{1,17},{9,25},{17,1},{25,9},{2,18},{10... | collective-permute-start | bytes 589832 | tf_op jit(solution)/shard_map/ppermute | solution.py:63
  46.3 1.9 %collective-permute-start.13 = (bf16[4,2,64,128]{3,2,1,0:T(8,128)(2,1)S(1)}, bf16[4,2,64,128]{3,2,1,0:T(8,128)(2,1)S(1)}, u32[]{:S(2)}, u32[]{:S(2)}) collective-permute-start(bf16[4,2,64,128]{3,2,1,0:T(8,128)(2,1)S(1)} %get-tuple-element.118), channel_id=1, source_target_pairs={{1,0},{2,1},{3,2},{4,3},{5,4},{6,5},{7,6},{9,8},{10,9},{11,10},{12... | collective-permute-start | bytes 393224 | tf_op jit(solution)/shard_map/ppermute | solution.py:70
  48.3 1.0 %shard_map.108 = (bf16[3,2,64,128]{3,2,1,0:T(8,128)(2,1)S(1)}, bf16[3,2,64,128]{3,2,1,0:T(8,128)(2,1)S(1)}, bf16[3,2,64,128]{3,2,1,0:T(8,128)(2,1)S(1)}, bf16[3,2,64,128]{3,2,1,0:T(8,128)(2,1)S(1)}) custom-call(bf16[6,2,64,128]{3,2,1,0:T(8,128)(2,1)S(1)} %bitcast.29, bf16[6,2,64,128]{3,2,1,0:T(8,128)(2,1)S(1)} %bitcast.33, ...), custom_call_target="tpu_custom_call" | custom-call | flops 1024 | bytes 1024 | tf_op jit(solution)/shard_map/pallas_call | solution.py:284
  49.3 0.4 collective-permute-start.17
  49.7 3.2 %collective-permute-done.13.refs_9_ = bf16[4,2,64,128]{3,2,1,0:T(8,128)(2,1)S(1)} collective-permute-done((bf16[4,2,64,128]{3,2,1,0:T(8,128)(2,1)S(1)}, bf16[4,2,64,128]{3,2,1,0:T(8,128)(2,1)S(1)}, u32[]{:S(2)}, u32[]{:S(2)}) %collective-permute-start.13) | collective-permute-done | bytes 131104 | tf_op jit(solution)/shard_map/ppermute | solution.py:70
  52.9 5.0 %shard_map.107 = (f32[3072,128]{1,0:T(8,128)}, f32[3,16,64,128]{3,2,1,0:T(8,128)S(1)}) custom-call(bf16[4,2,64,128]{3,2,1,0:T(8,128)(2,1)S(1)} %get-tuple-element.109.refs_0_, bf16[4,2,64,128]{3,2,1,0:T(8,128)(2,1)S(1)} %collective-permute-done.3.refs_1_, bf16[4,2,64,128]{3,2,1,0:T(8,128)(2,1)S(1)} %collective-permute-done.4.refs_2_, ...), custom_call_target="tpu_custom_call" | custom-call | flops 1024 | bytes 1024 | tf_op jit(solution)/shard_map/pallas_call | solution.py:446
  57.9 0.3 collective-permute-start.18
  58.2 0.4 collective-permute-start.19
  58.6 0.9 %shard_map.109 = (bf16[3,2,64,128]{3,2,1,0:T(8,128)(2,1)S(1)}, bf16[3,2,64,128]{3,2,1,0:T(8,128)(2,1)S(1)}, bf16[3,2,64,128]{3,2,1,0:T(8,128)(2,1)S(1)}, bf16[3,2,64,128]{3,2,1,0:T(8,128)(2,1)S(1)}) custom-call(bf16[6,2,64,128]{3,2,1,0:T(8,128)(2,1)S(1)} %bitcast.28, bf16[6,2,64,128]{3,2,1,0:T(8,128)(2,1)S(1)} %bitcast.30, ...), custom_call_target="tpu_custom_call" | custom-call | flops 1024 | bytes 1024 | tf_op jit(solution)/shard_map/pallas_call | solution.py:284
  59.5 2.1 %collective-permute-start.23 = (bf16[3,2,64,128]{3,2,1,0:T(8,128)(2,1)S(1)}, bf16[3,2,64,128]{3,2,1,0:T(8,128)(2,1)S(1)}, u32[]{:S(2)}, u32[]{:S(2)}) collective-permute-start(bf16[3,2,64,128]{3,2,1,0:T(8,128)(2,1)S(1)} %get-tuple-element.140), channel_id=1, source_target_pairs={{0,24},{8,16},{16,8},{24,0},{1,25},{9,17},{17,9},{25,1},{2,26},{10... | collective-permute-start | bytes 294920 | tf_op jit(solution)/shard_map/ppermute | solution.py:63
  61.6 0.3 collective-permute-start.24
  61.9 0.4 collective-permute-start.25
  62.3 0.4 collective-permute-done.18.refs_2_
  62.6 0.4 collective-permute-done.19.refs_3_
  63.1 1.7 %collective-permute-done.23.refs_5_ = bf16[3,2,64,128]{3,2,1,0:T(8,128)(2,1)S(1)} collective-permute-done((bf16[3,2,64,128]{3,2,1,0:T(8,128)(2,1)S(1)}, bf16[3,2,64,128]{3,2,1,0:T(8,128)(2,1)S(1)}, u32[]{:S(2)}, u32[]{:S(2)}) %collective-permute-start.23) | collective-permute-done | bytes 98336 | tf_op jit(solution)/shard_map/ppermute | solution.py:63
  64.8 0.8 %collective-permute-done.24.refs_6_ = bf16[3,2,64,128]{3,2,1,0:T(8,128)(2,1)S(1)} collective-permute-done((bf16[3,2,64,128]{3,2,1,0:T(8,128)(2,1)S(1)}, bf16[3,2,64,128]{3,2,1,0:T(8,128)(2,1)S(1)}, u32[]{:S(2)}, u32[]{:S(2)}) %collective-permute-start.24) | collective-permute-done | bytes 98336 | tf_op jit(solution)/shard_map/ppermute | solution.py:63
  65.6 0.3 collective-permute-done.25.refs_7_
  65.9 1.5 %shard_map.110 = f32[3072,128]{1,0:T(8,128)} custom-call(bf16[3,2,64,128]{3,2,1,0:T(8,128)(2,1)S(1)} %get-tuple-element.126.refs_0_, bf16[3,2,64,128]{3,2,1,0:T(8,128)(2,1)S(1)} %collective-permute-done.17.refs_1_, bf16[3,2,64,128]{3,2,1,0:T(8,128)(2,1)S(1)} %collective-permute-done.18.refs_2_, bf16[3,2,64,128]{3,2,1,0:T(8,128)(2,1)S(1)} %collective-permute-done.19.refs_3_, ...), custom_call_target="tpu_custom_call" | custom-call | flops 1024 | bytes 1024 | tf_op jit(solution)/shard_map/pallas_call | solution.py:490
  (36 shorter events, 1.5 us)
Async XLA Ops:
  2.2 7.7 %collective-permute-start.6 = (bf16[6,2,32,2,128]{4,3,2,1,0:T(2,128)(2,1)S(1)}, bf16[6,2,32,2,128]{4,3,2,1,0:T(2,128)(2,1)S(1)}, u32[]{:S(2)}, u32[]{:S(2)}) collective-permute-start(bf16[6,2,32,2,128]{4,3,2,1,0:T(2,128)(2,1)S(1)} %shard_map.102), channel_id=1, source_target_pairs={{0,24},{8,16},{16,8},{24,0},{1,25},{9,17},{17,9},{25,1},{2,26},{10... | collective-permute-start | bytes 589832 | tf_op jit(solution)/shard_map/ppermute | solution.py:63
  5.4 8.6 %collective-permute-start.7 = (bf16[6,2,32,2,128]{4,3,2,1,0:T(2,128)(2,1)S(1)}, bf16[6,2,32,2,128]{4,3,2,1,0:T(2,128)(2,1)S(1)}, u32[]{:S(2)}, u32[]{:S(2)}) collective-permute-start(bf16[6,2,32,2,128]{4,3,2,1,0:T(2,128)(2,1)S(1)} %shard_map.103), channel_id=1, source_target_pairs={{0,8},{8,0},{16,24},{24,16},{1,9},{9,1},{17,25},{25,17},{2,10},{10... | collective-permute-start | bytes 589832 | tf_op jit(solution)/shard_map/ppermute | solution.py:63
  5.9 8.8 %collective-permute-start.8 = (bf16[6,2,32,2,128]{4,3,2,1,0:T(2,128)(2,1)S(1)}, bf16[6,2,32,2,128]{4,3,2,1,0:T(2,128)(2,1)S(1)}, u32[]{:S(2)}, u32[]{:S(2)}) collective-permute-start(bf16[6,2,32,2,128]{4,3,2,1,0:T(2,128)(2,1)S(1)} %shard_map.104), channel_id=1, source_target_pairs={{0,16},{8,24},{16,0},{24,8},{1,17},{9,25},{17,1},{25,9},{2,18},{10... | collective-permute-start | bytes 589832 | tf_op jit(solution)/shard_map/ppermute | solution.py:63
  6.2 4.8 %copy-start.3 = (bf16[256,256]{1,0:T(8,128)(2,1)S(1)}, bf16[256,256]{1,0:T(8,128)(2,1)}, u32[]{:S(2)}) copy-start(bf16[256,256]{1,0:T(8,128)(2,1)} %constant.5.clone.refs_1_) | copy-start | bytes 393220
  6.2 4.8 %copy-start.4 = (bf16[256,256]{1,0:T(8,128)(2,1)S(1)}, bf16[256,256]{1,0:T(8,128)(2,1)}, u32[]{:S(2)}) copy-start(bf16[256,256]{1,0:T(8,128)(2,1)} %constant.4.clone.refs_0_) | copy-start | bytes 393220
  6.2 12.1 %collective-permute-start.1 = (bf16[6,2,32,2,128]{4,3,2,1,0:T(2,128)(2,1)S(1)}, bf16[6,2,32,2,128]{4,3,2,1,0:T(2,128)(2,1)S(1)}, u32[]{:S(2)}, u32[]{:S(2)}) collective-permute-start(bf16[6,2,32,2,128]{4,3,2,1,0:T(2,128)(2,1)S(1)} %shard_map.98), channel_id=1, source_target_pairs={{0,8},{8,0},{16,24},{24,16},{1,9},{9,1},{17,25},{25,17},{2,10},{10... | collective-permute-start | bytes 589832 | tf_op jit(solution)/shard_map/ppermute | solution.py:63
  7.9 14.7 %collective-permute-start = (bf16[6,2,32,2,128]{4,3,2,1,0:T(2,128)(2,1)S(1)}, bf16[6,2,32,2,128]{4,3,2,1,0:T(2,128)(2,1)S(1)}, u32[]{:S(2)}, u32[]{:S(2)}) collective-permute-start(bf16[6,2,32,2,128]{4,3,2,1,0:T(2,128)(2,1)S(1)} %shard_map.97), channel_id=1, source_target_pairs={{0,24},{8,16},{16,8},{24,0},{1,25},{9,17},{17,9},{25,1},{2,26},{10... | collective-permute-start | bytes 589832 | tf_op jit(solution)/shard_map/ppermute | solution.py:63
  9.1 10.6 %copy-start = (bf16[12,32,2,2048]{3,2,1,0:T(2,128)(2,1)S(1)}, bf16[12,32,2,2048]{3,2,1,0:T(2,128)(2,1)}, u32[]{:S(2)}) copy-start(bf16[12,32,2,2048]{3,2,1,0:T(2,128)(2,1)} %fields_ref.3) | copy-start | bytes 9437188
  9.9 12.6 %collective-permute-start.2 = (bf16[6,2,32,2,128]{4,3,2,1,0:T(2,128)(2,1)S(1)}, bf16[6,2,32,2,128]{4,3,2,1,0:T(2,128)(2,1)S(1)}, u32[]{:S(2)}, u32[]{:S(2)}) collective-permute-start(bf16[6,2,32,2,128]{4,3,2,1,0:T(2,128)(2,1)S(1)} %shard_map.99), channel_id=1, source_target_pairs={{0,16},{8,24},{16,0},{24,8},{1,17},{9,25},{17,1},{25,9},{2,18},{10... | collective-permute-start | bytes 589832 | tf_op jit(solution)/shard_map/ppermute | solution.py:63
  15.5 10.3 %collective-permute-start.9 = (bf16[4,2,64,128]{3,2,1,0:T(8,128)(2,1)S(1)}, bf16[4,2,64,128]{3,2,1,0:T(8,128)(2,1)S(1)}, u32[]{:S(2)}, u32[]{:S(2)}) collective-permute-start(bf16[4,2,64,128]{3,2,1,0:T(8,128)(2,1)S(1)} %get-tuple-element.87), channel_id=1, source_target_pairs={{0,24},{8,16},{16,8},{24,0},{1,25},{9,17},{17,9},{25,1},{2,26},{10... | collective-permute-start | bytes 393224 | tf_op jit(solution)/shard_map/ppermute | solution.py:63
  18.3 9.9 %collective-permute-start.10 = (bf16[4,2,64,128]{3,2,1,0:T(8,128)(2,1)S(1)}, bf16[4,2,64,128]{3,2,1,0:T(8,128)(2,1)S(1)}, u32[]{:S(2)}, u32[]{:S(2)}) collective-permute-start(bf16[4,2,64,128]{3,2,1,0:T(8,128)(2,1)S(1)} %get-tuple-element.88), channel_id=1, source_target_pairs={{0,8},{8,0},{16,24},{24,16},{1,9},{9,1},{17,25},{25,17},{2,10},{10... | collective-permute-start | bytes 393224 | tf_op jit(solution)/shard_map/ppermute | solution.py:63
  19.5 18.2 %copy-start.7 = (s32[2,256]{1,0:T(2,128)S(1)}, s32[2,256]{1,0:T(2,128)}, u32[]{:S(2)}) copy-start(s32[2,256]{1,0:T(2,128)} %refs_8_.1) | copy-start | bytes 6148
  19.5 9.9 %collective-permute-start.11 = (bf16[4,2,64,128]{3,2,1,0:T(8,128)(2,1)S(1)}, bf16[4,2,64,128]{3,2,1,0:T(8,128)(2,1)S(1)}, u32[]{:S(2)}, u32[]{:S(2)}) collective-permute-start(bf16[4,2,64,128]{3,2,1,0:T(8,128)(2,1)S(1)} %get-tuple-element.89), channel_id=1, source_target_pairs={{0,16},{8,24},{16,0},{24,8},{1,17},{9,25},{17,1},{25,9},{2,18},{10... | collective-permute-start | bytes 393224 | tf_op jit(solution)/shard_map/ppermute | solution.py:63
  23.4 8.7 %collective-permute-start.3 = (bf16[4,2,64,128]{3,2,1,0:T(8,128)(2,1)S(1)}, bf16[4,2,64,128]{3,2,1,0:T(8,128)(2,1)S(1)}, u32[]{:S(2)}, u32[]{:S(2)}) collective-permute-start(bf16[4,2,64,128]{3,2,1,0:T(8,128)(2,1)S(1)} %get-tuple-element.82), channel_id=1, source_target_pairs={{0,24},{8,16},{16,8},{24,0},{1,25},{9,17},{17,9},{25,1},{2,26},{10... | collective-permute-start | bytes 393224 | tf_op jit(solution)/shard_map/ppermute | solution.py:63
  25.6 8.2 %collective-permute-start.4 = (bf16[4,2,64,128]{3,2,1,0:T(8,128)(2,1)S(1)}, bf16[4,2,64,128]{3,2,1,0:T(8,128)(2,1)S(1)}, u32[]{:S(2)}, u32[]{:S(2)}) collective-permute-start(bf16[4,2,64,128]{3,2,1,0:T(8,128)(2,1)S(1)} %get-tuple-element.83), channel_id=1, source_target_pairs={{0,8},{8,0},{16,24},{24,16},{1,9},{9,1},{17,25},{25,17},{2,10},{10... | collective-permute-start | bytes 393224 | tf_op jit(solution)/shard_map/ppermute | solution.py:63
  25.8 8.2 %collective-permute-start.5 = (bf16[4,2,64,128]{3,2,1,0:T(8,128)(2,1)S(1)}, bf16[4,2,64,128]{3,2,1,0:T(8,128)(2,1)S(1)}, u32[]{:S(2)}, u32[]{:S(2)}) collective-permute-start(bf16[4,2,64,128]{3,2,1,0:T(8,128)(2,1)S(1)} %get-tuple-element.84), channel_id=1, source_target_pairs={{0,16},{8,24},{16,0},{24,8},{1,17},{9,25},{17,1},{25,9},{2,18},{10... | collective-permute-start | bytes 393224 | tf_op jit(solution)/shard_map/ppermute | solution.py:63
  29.4 14.6 %collective-permute-start.14 = (bf16[6,2,32,2,128]{4,3,2,1,0:T(2,128)(2,1)S(1)}, bf16[6,2,32,2,128]{4,3,2,1,0:T(2,128)(2,1)S(1)}, u32[]{:S(2)}, u32[]{:S(2)}) collective-permute-start(bf16[6,2,32,2,128]{4,3,2,1,0:T(2,128)(2,1)S(1)} %get-tuple-element.121), channel_id=1, source_target_pairs={{0,24},{8,16},{16,8},{24,0},{1,25},{9,17},{17,9},{25,1},{2,26},{10... | collective-permute-start | bytes 589832 | tf_op jit(solution)/shard_map/ppermute | solution.py:63
  34.0 11.4 %collective-permute-start.15 = (bf16[6,2,32,2,128]{4,3,2,1,0:T(2,128)(2,1)S(1)}, bf16[6,2,32,2,128]{4,3,2,1,0:T(2,128)(2,1)S(1)}, u32[]{:S(2)}, u32[]{:S(2)}) collective-permute-start(bf16[6,2,32,2,128]{4,3,2,1,0:T(2,128)(2,1)S(1)} %get-tuple-element.122), channel_id=1, source_target_pairs={{0,8},{8,0},{16,24},{24,16},{1,9},{9,1},{17,25},{25,17},{2,10},{10... | collective-permute-start | bytes 589832 | tf_op jit(solution)/shard_map/ppermute | solution.py:63
  35.4 10.9 %collective-permute-start.16 = (bf16[6,2,32,2,128]{4,3,2,1,0:T(2,128)(2,1)S(1)}, bf16[6,2,32,2,128]{4,3,2,1,0:T(2,128)(2,1)S(1)}, u32[]{:S(2)}, u32[]{:S(2)}) collective-permute-start(bf16[6,2,32,2,128]{4,3,2,1,0:T(2,128)(2,1)S(1)} %get-tuple-element.123), channel_id=1, source_target_pairs={{0,16},{8,24},{16,0},{24,8},{1,17},{9,25},{17,1},{25,9},{2,18},{10... | collective-permute-start | bytes 589832 | tf_op jit(solution)/shard_map/ppermute | solution.py:63
  38.9 10.4 %collective-permute-start.12 = (bf16[4,2,64,128]{3,2,1,0:T(8,128)(2,1)S(1)}, bf16[4,2,64,128]{3,2,1,0:T(8,128)(2,1)S(1)}, u32[]{:S(2)}, u32[]{:S(2)}) collective-permute-start(bf16[4,2,64,128]{3,2,1,0:T(8,128)(2,1)S(1)} %get-tuple-element.117), channel_id=1, source_target_pairs={{0,1},{1,2},{2,3},{3,4},{4,5},{5,6},{6,7},{8,9},{9,10},{10,11},{11... | collective-permute-start | bytes 393224 | tf_op jit(solution)/shard_map/ppermute | solution.py:70
  43.6 14.6 %collective-permute-start.20 = (bf16[6,2,32,2,128]{4,3,2,1,0:T(2,128)(2,1)S(1)}, bf16[6,2,32,2,128]{4,3,2,1,0:T(2,128)(2,1)S(1)}, u32[]{:S(2)}, u32[]{:S(2)}) collective-permute-start(bf16[6,2,32,2,128]{4,3,2,1,0:T(2,128)(2,1)S(1)} %get-tuple-element.131), channel_id=1, source_target_pairs={{0,24},{8,16},{16,8},{24,0},{1,25},{9,17},{17,9},{25,1},{2,26},{10... | collective-permute-start | bytes 589832 | tf_op jit(solution)/shard_map/ppermute | solution.py:63
  44.0 14.6 %collective-permute-start.21 = (bf16[6,2,32,2,128]{4,3,2,1,0:T(2,128)(2,1)S(1)}, bf16[6,2,32,2,128]{4,3,2,1,0:T(2,128)(2,1)S(1)}, u32[]{:S(2)}, u32[]{:S(2)}) collective-permute-start(bf16[6,2,32,2,128]{4,3,2,1,0:T(2,128)(2,1)S(1)} %get-tuple-element.132), channel_id=1, source_target_pairs={{0,8},{8,0},{16,24},{24,16},{1,9},{9,1},{17,25},{25,17},{2,10},{10... | collective-permute-start | bytes 589832 | tf_op jit(solution)/shard_map/ppermute | solution.py:63
  45.3 13.3 %collective-permute-start.22 = (bf16[6,2,32,2,128]{4,3,2,1,0:T(2,128)(2,1)S(1)}, bf16[6,2,32,2,128]{4,3,2,1,0:T(2,128)(2,1)S(1)}, u32[]{:S(2)}, u32[]{:S(2)}) collective-permute-start(bf16[6,2,32,2,128]{4,3,2,1,0:T(2,128)(2,1)S(1)} %get-tuple-element.133), channel_id=1, source_target_pairs={{0,16},{8,24},{16,0},{24,8},{1,17},{9,25},{17,1},{25,9},{2,18},{10... | collective-permute-start | bytes 589832 | tf_op jit(solution)/shard_map/ppermute | solution.py:63
  46.3 6.6 %collective-permute-start.13 = (bf16[4,2,64,128]{3,2,1,0:T(8,128)(2,1)S(1)}, bf16[4,2,64,128]{3,2,1,0:T(8,128)(2,1)S(1)}, u32[]{:S(2)}, u32[]{:S(2)}) collective-permute-start(bf16[4,2,64,128]{3,2,1,0:T(8,128)(2,1)S(1)} %get-tuple-element.118), channel_id=1, source_target_pairs={{1,0},{2,1},{3,2},{4,3},{5,4},{6,5},{7,6},{9,8},{10,9},{11,10},{12... | collective-permute-start | bytes 393224 | tf_op jit(solution)/shard_map/ppermute | solution.py:70
  48.3 4.7 %copy-start.1 = (bf16[5,64,2048]{2,1,0:T(8,128)(2,1)S(1)}, bf16[5,64,2048]{2,1,0:T(8,128)(2,1)}, u32[]{:S(2)}) copy-start(bf16[5,64,2048]{2,1,0:T(8,128)(2,1)} %refs_10_.1) | copy-start | bytes 3932164
  48.3 4.6 %copy-start.2 = (bf16[5,64,2048]{2,1,0:T(8,128)(2,1)S(1)}, bf16[5,64,2048]{2,1,0:T(8,128)(2,1)}, u32[]{:S(2)}) copy-start(bf16[5,64,2048]{2,1,0:T(8,128)(2,1)} %refs_11_.1) | copy-start | bytes 3932164
  48.3 4.6 %copy-start.5 = (f32[2048]{0:T(1024)S(1)}, f32[2048]{0:T(1024)}, u32[]{:S(2)}) copy-start(f32[2048]{0:T(1024)} %param.9) | copy-start | bytes 24580
  48.3 4.6 %copy-start.6 = (s32[32,5]{0,1:T(8,128)S(1)}, s32[32,5]{0,1:T(8,128)}, u32[]{:S(2)}) copy-start(s32[32,5]{0,1:T(8,128)} %param.12) | copy-start | bytes 1924
  49.3 12.6 %collective-permute-start.17 = (bf16[3,2,64,128]{3,2,1,0:T(8,128)(2,1)S(1)}, bf16[3,2,64,128]{3,2,1,0:T(8,128)(2,1)S(1)}, u32[]{:S(2)}, u32[]{:S(2)}) collective-permute-start(bf16[3,2,64,128]{3,2,1,0:T(8,128)(2,1)S(1)} %get-tuple-element.127), channel_id=1, source_target_pairs={{0,24},{8,16},{16,8},{24,0},{1,25},{9,17},{17,9},{25,1},{2,26},{10... | collective-permute-start | bytes 294920 | tf_op jit(solution)/shard_map/ppermute | solution.py:63
  57.9 4.7 %collective-permute-start.18 = (bf16[3,2,64,128]{3,2,1,0:T(8,128)(2,1)S(1)}, bf16[3,2,64,128]{3,2,1,0:T(8,128)(2,1)S(1)}, u32[]{:S(2)}, u32[]{:S(2)}) collective-permute-start(bf16[3,2,64,128]{3,2,1,0:T(8,128)(2,1)S(1)} %get-tuple-element.128), channel_id=1, source_target_pairs={{0,8},{8,0},{16,24},{24,16},{1,9},{9,1},{17,25},{25,17},{2,10},{10... | collective-permute-start | bytes 294920 | tf_op jit(solution)/shard_map/ppermute | solution.py:63
  58.2 4.8 %collective-permute-start.19 = (bf16[3,2,64,128]{3,2,1,0:T(8,128)(2,1)S(1)}, bf16[3,2,64,128]{3,2,1,0:T(8,128)(2,1)S(1)}, u32[]{:S(2)}, u32[]{:S(2)}) collective-permute-start(bf16[3,2,64,128]{3,2,1,0:T(8,128)(2,1)S(1)} %get-tuple-element.129), channel_id=1, source_target_pairs={{0,16},{8,24},{16,0},{24,8},{1,17},{9,25},{17,1},{25,9},{2,18},{10... | collective-permute-start | bytes 294920 | tf_op jit(solution)/shard_map/ppermute | solution.py:63
  59.5 5.3 %collective-permute-start.23 = (bf16[3,2,64,128]{3,2,1,0:T(8,128)(2,1)S(1)}, bf16[3,2,64,128]{3,2,1,0:T(8,128)(2,1)S(1)}, u32[]{:S(2)}, u32[]{:S(2)}) collective-permute-start(bf16[3,2,64,128]{3,2,1,0:T(8,128)(2,1)S(1)} %get-tuple-element.140), channel_id=1, source_target_pairs={{0,24},{8,16},{16,8},{24,0},{1,25},{9,17},{17,9},{25,1},{2,26},{10... | collective-permute-start | bytes 294920 | tf_op jit(solution)/shard_map/ppermute | solution.py:63
  61.6 4.0 %collective-permute-start.24 = (bf16[3,2,64,128]{3,2,1,0:T(8,128)(2,1)S(1)}, bf16[3,2,64,128]{3,2,1,0:T(8,128)(2,1)S(1)}, u32[]{:S(2)}, u32[]{:S(2)}) collective-permute-start(bf16[3,2,64,128]{3,2,1,0:T(8,128)(2,1)S(1)} %get-tuple-element.141), channel_id=1, source_target_pairs={{0,8},{8,0},{16,24},{24,16},{1,9},{9,1},{17,25},{25,17},{2,10},{10... | collective-permute-start | bytes 294920 | tf_op jit(solution)/shard_map/ppermute | solution.py:63
  61.9 4.0 %collective-permute-start.25 = (bf16[3,2,64,128]{3,2,1,0:T(8,128)(2,1)S(1)}, bf16[3,2,64,128]{3,2,1,0:T(8,128)(2,1)S(1)}, u32[]{:S(2)}, u32[]{:S(2)}) collective-permute-start(bf16[3,2,64,128]{3,2,1,0:T(8,128)(2,1)S(1)} %get-tuple-element.142), channel_id=1, source_target_pairs={{0,16},{8,24},{16,0},{24,8},{1,17},{9,25},{17,1},{25,9},{2,18},{10... | collective-permute-start | bytes 294920 | tf_op jit(solution)/shard_map/ppermute | solution.py:63

commit v21 on v20

--- a/solution.py
+++ b/solution.py
@@ -543,13 +543,14 @@
     toward_prev, toward_next = interface(local, interface_nodes, count)
     halos = (from_behind(toward_next, "mer", 1), from_behind(toward_prev, "mer", -1))
     local, shares[count:] = lax.optimization_barrier((local, shares[count:]))
-    induction, gradient = derive(
-        local, *halos, radial_blocks, axial_blocks, radius.reshape(1, width), block_columns.T, count
-    )
     lorentz = []
     for part, (begin, _) in enumerate(spans):
         sources = exchange(shares[part * count : (part + 1) * count], order)
         if part == len(spans) - 1:
+            halos, sources[1] = lax.optimization_barrier((halos, sources[1]))
+            induction, gradient = derive(
+                local, *halos, radial_blocks, axial_blocks, radius.reshape(1, width), block_columns.T, count
+            )
             sources, gradient = lax.optimization_barrier((sources, gradient))
         terms = list(second_physics(joined(sources), physical, begin, later_inverse, later_forward))
         lorentz += exchange(terms, offsets(count, SECOND_RETURN))

time: 68.6 us -> 68.6 us (level)
  transfers between devices with their start and end apart: 26 -> 26, of which waited for: 15 -> 13; matrix products, arithmetic and copies ran while one was open for 0% -> 0% of each run, Pallas kernels for 18% -> 18%
where the time goes in v21:
time: 68.6 us; the launch traced here: 67.2 us
  starting transfers between devices  34 us (50%)
  waiting for transfers between devices  17 us (25%)
  Pallas kernels  15.3 us (22%)
  between operations  0.84 us (1%)
    ppermute x24, starting transfers between devices, exchange(): received.append(lax.ppermute(piece, 'mode', pairs))  27.4 us
    ppermute x24, waiting for transfers between devices, exchange(): received.append(lax.ppermute(piece, 'mode', pairs))  13.8 us
    ppermute x2, starting transfers between devices, from_behind(): lax.ppermute(value, axis, [(source, source + steps) for source in range(i...  6.58 us
    pallas_call x1, Pallas kernels, derive(): pl.pallas_call(functools.partial(derive_kernel, count, len(received)), in...  5.02 us
    ppermute x2, waiting for transfers between devices, from_behind(): lax.ppermute(value, axis, [(source, source + steps) for source in range(i...  3.18 us
    pallas_call x2, Pallas kernels, second_physics(): pl.pallas_call(functools.partial(second_kernel, count, groups, begin), in...  1.89 us
    pallas_call x2, Pallas kernels, first_physics(): pl.pallas_call(functools.partial(first_kernel, count), in_specs=[vmem()]...  1.65 us
    pallas_call x2, Pallas kernels, pack_rest(): pl.pallas_call(kernel, in_specs=[pl.BlockSpec(memory_space=pl.ANY)] + [vm...  1.62 us
  transfers between devices with their start and end apart: 26, of which 13 were waited for; matrix products, arithmetic and copies ran while one was open for 0% of the time, Pallas kernels for 18%

profile of v21, /device:TPU:1, one launch (start us, length us, event | category | flops | bytes accessed | tf_op | source)
XLA Modules:
  0.0 67.2 jit_solution(4922229376311644726)
XLA Ops:
  0.6 1.4 %shard_map.95.fields_ref = bf16[6,32,2,2048]{3,2,1,0:T(2,128)(2,1)S(1)} custom-call(bf16[12,32,2,2048]{3,2,1,0:T(2,128)(2,1)} %fields_ref.3), custom_call_target="tpu_custom_call" | custom-call | flops 1024 | bytes 1024 | tf_op jit(solution)/shard_map/pallas_call | solution.py:123
  2.2 3.1 %collective-permute-start.6 = (bf16[6,2,32,2,128]{4,3,2,1,0:T(2,128)(2,1)S(1)}, bf16[6,2,32,2,128]{4,3,2,1,0:T(2,128)(2,1)S(1)}, u32[]{:S(2)}, u32[]{:S(2)}) collective-permute-start(bf16[6,2,32,2,128]{4,3,2,1,0:T(2,128)(2,1)S(1)} %shard_map.102), channel_id=1, source_target_pairs={{0,24},{8,16},{16,8},{24,0},{1,25},{9,17},{17,9},{25,1},{2,26},{10... | collective-permute-start | bytes 589832 | tf_op jit(solution)/shard_map/ppermute | solution.py:63
  5.4 0.3 collective-permute-start.7
  6.2 1.4 %collective-permute-start.1 = (bf16[6,2,32,2,128]{4,3,2,1,0:T(2,128)(2,1)S(1)}, bf16[6,2,32,2,128]{4,3,2,1,0:T(2,128)(2,1)S(1)}, u32[]{:S(2)}, u32[]{:S(2)}) collective-permute-start(bf16[6,2,32,2,128]{4,3,2,1,0:T(2,128)(2,1)S(1)} %shard_map.98), channel_id=1, source_target_pairs={{0,8},{8,0},{16,24},{24,16},{1,9},{9,1},{17,25},{25,17},{2,10},{10... | collective-permute-start | bytes 589832 | tf_op jit(solution)/shard_map/ppermute | solution.py:63
  7.9 1.3 %collective-permute-start = (bf16[6,2,32,2,128]{4,3,2,1,0:T(2,128)(2,1)S(1)}, bf16[6,2,32,2,128]{4,3,2,1,0:T(2,128)(2,1)S(1)}, u32[]{:S(2)}, u32[]{:S(2)}) collective-permute-start(bf16[6,2,32,2,128]{4,3,2,1,0:T(2,128)(2,1)S(1)} %shard_map.97), channel_id=1, source_target_pairs={{0,24},{8,16},{16,8},{24,0},{1,25},{9,17},{17,9},{25,1},{2,26},{10... | collective-permute-start | bytes 589832 | tf_op jit(solution)/shard_map/ppermute | solution.py:63
  9.3 0.6 collective-permute-done.6
  9.9 1.2 %collective-permute-start.2 = (bf16[6,2,32,2,128]{4,3,2,1,0:T(2,128)(2,1)S(1)}, bf16[6,2,32,2,128]{4,3,2,1,0:T(2,128)(2,1)S(1)}, u32[]{:S(2)}, u32[]{:S(2)}) collective-permute-start(bf16[6,2,32,2,128]{4,3,2,1,0:T(2,128)(2,1)S(1)} %shard_map.99), channel_id=1, source_target_pairs={{0,16},{8,24},{16,0},{24,8},{1,17},{9,25},{17,1},{25,9},{2,18},{10... | collective-permute-start | bytes 589832 | tf_op jit(solution)/shard_map/ppermute | solution.py:63
  11.1 0.3 shard_map.96
  11.4 2.7 %collective-permute-done.7 = bf16[6,2,32,2,128]{4,3,2,1,0:T(2,128)(2,1)S(1)} collective-permute-done((bf16[6,2,32,2,128]{4,3,2,1,0:T(2,128)(2,1)S(1)}, bf16[6,2,32,2,128]{4,3,2,1,0:T(2,128)(2,1)S(1)}, u32[]{:S(2)}, u32[]{:S(2)}) %collective-permute-start.7) | collective-permute-done | bytes 196640 | tf_op jit(solution)/shard_map/ppermute | solution.py:63
  14.1 0.6 collective-permute-done.8
  14.7 0.8 %shard_map.105 = (bf16[4,2,64,128]{3,2,1,0:T(8,128)(2,1)S(1)}, bf16[4,2,64,128]{3,2,1,0:T(8,128)(2,1)S(1)}, bf16[4,2,64,128]{3,2,1,0:T(8,128)(2,1)S(1)}, bf16[4,...) custom-call(bf16[6,2,64,128]{3,2,1,0:T(8,128)(2,1)S(1)} %bitcast.43, bf16[6,2,64,128]{3,2,1,0:T(8,128)(2,1)S(1)} %bitcast.40, ...), custom_call_target="tpu_custom_call" | custom-call | flops 1024 | bytes 1024 | tf_op jit(solution)/shard_map/pallas_call | solution.py:238
  15.5 2.6 %collective-permute-start.9 = (bf16[4,2,64,128]{3,2,1,0:T(8,128)(2,1)S(1)}, bf16[4,2,64,128]{3,2,1,0:T(8,128)(2,1)S(1)}, u32[]{:S(2)}, u32[]{:S(2)}) collective-permute-start(bf16[4,2,64,128]{3,2,1,0:T(8,128)(2,1)S(1)} %get-tuple-element.90), channel_id=1, source_target_pairs={{0,24},{8,16},{16,8},{24,0},{1,25},{9,17},{17,9},{25,1},{2,26},{10... | collective-permute-start | bytes 393224 | tf_op jit(solution)/shard_map/ppermute | solution.py:63
  18.1 0.2 collective-permute-done.1
  18.3 1.2 %collective-permute-start.10 = (bf16[4,2,64,128]{3,2,1,0:T(8,128)(2,1)S(1)}, bf16[4,2,64,128]{3,2,1,0:T(8,128)(2,1)S(1)}, u32[]{:S(2)}, u32[]{:S(2)}) collective-permute-start(bf16[4,2,64,128]{3,2,1,0:T(8,128)(2,1)S(1)} %get-tuple-element.91), channel_id=1, source_target_pairs={{0,8},{8,0},{16,24},{24,16},{1,9},{9,1},{17,25},{25,17},{2,10},{10... | collective-permute-start | bytes 393224 | tf_op jit(solution)/shard_map/ppermute | solution.py:63
  19.5 0.2 collective-permute-start.11
  19.7 1.3 %shard_map.100 = (bf16[6,2,32,2,128]{4,3,2,1,0:T(2,128)(2,1)S(1)}, bf16[6,2,32,2,128]{4,3,2,1,0:T(2,128)(2,1)S(1)}, bf16[6,2,32,2,128]{4,3,2,1,0:T(2,128)(2,1)S(...) custom-call(bf16[12,32,2,2048]{3,2,1,0:T(2,128)(2,1)S(1)} %copy-done, ...), custom_call_target="tpu_custom_call" | custom-call | flops 1024 | bytes 1024 | tf_op jit(solution)/shard_map/pallas_call | solution.py:170
  21.0 1.5 %collective-permute-done = bf16[6,2,32,2,128]{4,3,2,1,0:T(2,128)(2,1)S(1)} collective-permute-done((bf16[6,2,32,2,128]{4,3,2,1,0:T(2,128)(2,1)S(1)}, bf16[6,2,32,2,128]{4,3,2,1,0:T(2,128)(2,1)S(1)}, u32[]{:S(2)}, u32[]{:S(2)}) %collective-permute-start) | collective-permute-done | bytes 196640 | tf_op jit(solution)/shard_map/ppermute | solution.py:63
  22.5 0.8 %shard_map.101 = (bf16[4,2,64,128]{3,2,1,0:T(8,128)(2,1)S(1)}, bf16[4,2,64,128]{3,2,1,0:T(8,128)(2,1)S(1)}, bf16[4,2,64,128]{3,2,1,0:T(8,128)(2,1)S(1)}, bf16[4,...) custom-call(bf16[6,2,64,128]{3,2,1,0:T(8,128)(2,1)S(1)} %bitcast.39, bf16[6,2,64,128]{3,2,1,0:T(8,128)(2,1)S(1)} %bitcast.37, ...), custom_call_target="tpu_custom_call" | custom-call | flops 1024 | bytes 1024 | tf_op jit(solution)/shard_map/pallas_call | solution.py:238
  23.4 2.2 %collective-permute-start.3 = (bf16[4,2,64,128]{3,2,1,0:T(8,128)(2,1)S(1)}, bf16[4,2,64,128]{3,2,1,0:T(8,128)(2,1)S(1)}, u32[]{:S(2)}, u32[]{:S(2)}) collective-permute-start(bf16[4,2,64,128]{3,2,1,0:T(8,128)(2,1)S(1)} %get-tuple-element.85), channel_id=1, source_target_pairs={{0,24},{8,16},{16,8},{24,0},{1,25},{9,17},{17,9},{25,1},{2,26},{10... | collective-permute-start | bytes 393224 | tf_op jit(solution)/shard_map/ppermute | solution.py:63
  25.6 0.2 collective-permute-start.4
  25.8 0.8 %collective-permute-start.5 = (bf16[4,2,64,128]{3,2,1,0:T(8,128)(2,1)S(1)}, bf16[4,2,64,128]{3,2,1,0:T(8,128)(2,1)S(1)}, u32[]{:S(2)}, u32[]{:S(2)}) collective-permute-start(bf16[4,2,64,128]{3,2,1,0:T(8,128)(2,1)S(1)} %get-tuple-element.87), channel_id=1, source_target_pairs={{0,16},{8,24},{16,0},{24,8},{1,17},{9,25},{17,1},{25,9},{2,18},{10... | collective-permute-start | bytes 393224 | tf_op jit(solution)/shard_map/ppermute | solution.py:63
  26.6 1.6 %collective-permute-done.10.refs_6_ = bf16[4,2,64,128]{3,2,1,0:T(8,128)(2,1)S(1)} collective-permute-done((bf16[4,2,64,128]{3,2,1,0:T(8,128)(2,1)S(1)}, bf16[4,2,64,128]{3,2,1,0:T(8,128)(2,1)S(1)}, u32[]{:S(2)}, u32[]{:S(2)}) %collective-permute-start.10) | collective-permute-done | bytes 131104 | tf_op jit(solution)/shard_map/ppermute | solution.py:63
  28.2 1.2 %collective-permute-done.11.refs_7_ = bf16[4,2,64,128]{3,2,1,0:T(8,128)(2,1)S(1)} collective-permute-done((bf16[4,2,64,128]{3,2,1,0:T(8,128)(2,1)S(1)}, bf16[4,2,64,128]{3,2,1,0:T(8,128)(2,1)S(1)}, u32[]{:S(2)}, u32[]{:S(2)}) %collective-permute-start.11) | collective-permute-done | bytes 131104 | tf_op jit(solution)/shard_map/ppermute | solution.py:63
  29.4 2.7 %collective-permute-start.15 = (bf16[6,2,32,2,128]{4,3,2,1,0:T(2,128)(2,1)S(1)}, bf16[6,2,32,2,128]{4,3,2,1,0:T(2,128)(2,1)S(1)}, u32[]{:S(2)}, u32[]{:S(2)}) collective-permute-start(bf16[6,2,32,2,128]{4,3,2,1,0:T(2,128)(2,1)S(1)} %get-tuple-element.127), channel_id=1, source_target_pairs={{0,24},{8,16},{16,8},{24,0},{1,25},{9,17},{17,9},{25,1},{2,26},{10... | collective-permute-start | bytes 589832 | tf_op jit(solution)/shard_map/ppermute | solution.py:63
  32.1 1.7 %collective-permute-done.4.refs_2_ = bf16[4,2,64,128]{3,2,1,0:T(8,128)(2,1)S(1)} collective-permute-done((bf16[4,2,64,128]{3,2,1,0:T(8,128)(2,1)S(1)}, bf16[4,2,64,128]{3,2,1,0:T(8,128)(2,1)S(1)}, u32[]{:S(2)}, u32[]{:S(2)}) %collective-permute-start.4) | collective-permute-done | bytes 131104 | tf_op jit(solution)/shard_map/ppermute | solution.py:63
  33.8 0.2 collective-permute-done.5.refs_3_
  34.0 1.4 %collective-permute-start.16 = (bf16[6,2,32,2,128]{4,3,2,1,0:T(2,128)(2,1)S(1)}, bf16[6,2,32,2,128]{4,3,2,1,0:T(2,128)(2,1)S(1)}, u32[]{:S(2)}, u32[]{:S(2)}) collective-permute-start(bf16[6,2,32,2,128]{4,3,2,1,0:T(2,128)(2,1)S(1)} %get-tuple-element.128), channel_id=1, source_target_pairs={{0,8},{8,0},{16,24},{24,16},{1,9},{9,1},{17,25},{25,17},{2,10},{10... | collective-permute-start | bytes 589832 | tf_op jit(solution)/shard_map/ppermute | solution.py:63
  35.4 2.3 %collective-permute-start.17 = (bf16[6,2,32,2,128]{4,3,2,1,0:T(2,128)(2,1)S(1)}, bf16[6,2,32,2,128]{4,3,2,1,0:T(2,128)(2,1)S(1)}, u32[]{:S(2)}, u32[]{:S(2)}) collective-permute-start(bf16[6,2,32,2,128]{4,3,2,1,0:T(2,128)(2,1)S(1)} %get-tuple-element.129), channel_id=1, source_target_pairs={{0,16},{8,24},{16,0},{24,8},{1,17},{9,25},{17,1},{25,9},{2,18},{10... | collective-permute-start | bytes 589832 | tf_op jit(solution)/shard_map/ppermute | solution.py:63
  37.7 1.2 %shard_map.106 = (bf16[4,2,64,128]{3,2,1,0:T(8,128)(2,1)S(1)}, bf16[4,2,64,128]{3,2,1,0:T(8,128)(2,1)S(1)}) custom-call(bf16[4,2,64,128]{3,2,1,0:T(8,128)(2,1)S(1)} %get-tuple-element.112.refs_0_, bf16[4,2,64,128]{3,2,1,0:T(8,128)(2,1)S(1)} %collective-permute-done.3.refs_1_, bf16[4,2,64,128]{3,2,1,0:T(8,128)(2,1)S(1)} %collective-permute-done.4.refs_2_, ...), custom_call_target="tpu_custom_call" | custom-call | flops 1024 | bytes 1024 | tf_op jit(solution)/shard_map/pallas_call | solution.py:334
  38.9 4.7 %collective-permute-start.12 = (bf16[4,2,64,128]{3,2,1,0:T(8,128)(2,1)S(1)}, bf16[4,2,64,128]{3,2,1,0:T(8,128)(2,1)S(1)}, u32[]{:S(2)}, u32[]{:S(2)}) collective-permute-start(bf16[4,2,64,128]{3,2,1,0:T(8,128)(2,1)S(1)} %get-tuple-element.120), channel_id=1, source_target_pairs={{0,1},{1,2},{2,3},{3,4},{4,5},{5,6},{6,7},{8,9},{9,10},{10,11},{11... | collective-permute-start | bytes 393224 | tf_op jit(solution)/shard_map/ppermute | solution.py:70
  43.6 0.4 collective-permute-start.14
  44.0 1.3 %collective-permute-start.21 = (bf16[6,2,32,2,128]{4,3,2,1,0:T(2,128)(2,1)S(1)}, bf16[6,2,32,2,128]{4,3,2,1,0:T(2,128)(2,1)S(1)}, u32[]{:S(2)}, u32[]{:S(2)}) collective-permute-start(bf16[6,2,32,2,128]{4,3,2,1,0:T(2,128)(2,1)S(1)} %get-tuple-element.138), channel_id=1, source_target_pairs={{0,8},{8,0},{16,24},{24,16},{1,9},{9,1},{17,25},{25,17},{2,10},{10... | collective-permute-start | bytes 589832 | tf_op jit(solution)/shard_map/ppermute | solution.py:63
  45.3 1.0 %collective-permute-start.22 = (bf16[6,2,32,2,128]{4,3,2,1,0:T(2,128)(2,1)S(1)}, bf16[6,2,32,2,128]{4,3,2,1,0:T(2,128)(2,1)S(1)}, u32[]{:S(2)}, u32[]{:S(2)}) collective-permute-start(bf16[6,2,32,2,128]{4,3,2,1,0:T(2,128)(2,1)S(1)} %get-tuple-element.139), channel_id=1, source_target_pairs={{0,16},{8,24},{16,0},{24,8},{1,17},{9,25},{17,1},{25,9},{2,18},{10... | collective-permute-start | bytes 589832 | tf_op jit(solution)/shard_map/ppermute | solution.py:63
  46.3 1.9 %collective-permute-start.13 = (bf16[4,2,64,128]{3,2,1,0:T(8,128)(2,1)S(1)}, bf16[4,2,64,128]{3,2,1,0:T(8,128)(2,1)S(1)}, u32[]{:S(2)}, u32[]{:S(2)}) collective-permute-start(bf16[4,2,64,128]{3,2,1,0:T(8,128)(2,1)S(1)} %get-tuple-element.121), channel_id=1, source_target_pairs={{1,0},{2,1},{3,2},{4,3},{5,4},{6,5},{7,6},{9,8},{10,9},{11,10},{12... | collective-permute-start | bytes 393224 | tf_op jit(solution)/shard_map/ppermute | solution.py:70
  48.3 1.0 %shard_map.108 = (bf16[3,2,64,128]{3,2,1,0:T(8,128)(2,1)S(1)}, bf16[3,2,64,128]{3,2,1,0:T(8,128)(2,1)S(1)}, bf16[3,2,64,128]{3,2,1,0:T(8,128)(2,1)S(1)}, bf16[3,2,64,128]{3,2,1,0:T(8,128)(2,1)S(1)}) custom-call(bf16[6,2,64,128]{3,2,1,0:T(8,128)(2,1)S(1)} %bitcast.29, bf16[6,2,64,128]{3,2,1,0:T(8,128)(2,1)S(1)} %bitcast.33, ...), custom_call_target="tpu_custom_call" | custom-call | flops 1024 | bytes 1024 | tf_op jit(solution)/shard_map/pallas_call | solution.py:284
  49.3 0.4 collective-permute-start.18
  49.7 3.2 %collective-permute-done.13.refs_9_ = bf16[4,2,64,128]{3,2,1,0:T(8,128)(2,1)S(1)} collective-permute-done((bf16[4,2,64,128]{3,2,1,0:T(8,128)(2,1)S(1)}, bf16[4,2,64,128]{3,2,1,0:T(8,128)(2,1)S(1)}, u32[]{:S(2)}, u32[]{:S(2)}) %collective-permute-start.13) | collective-permute-done | bytes 131104 | tf_op jit(solution)/shard_map/ppermute | solution.py:70
  52.9 0.3 collective-permute-start.19
  53.2 0.4 collective-permute-start.20
  53.6 5.0 %shard_map.107 = (f32[3072,128]{1,0:T(8,128)}, f32[3,16,64,128]{3,2,1,0:T(8,128)S(1)}) custom-call(bf16[4,2,64,128]{3,2,1,0:T(8,128)(2,1)S(1)} %get-tuple-element.112.refs_0_, bf16[4,2,64,128]{3,2,1,0:T(8,128)(2,1)S(1)} %collective-permute-done.3.refs_1_, bf16[4,2,64,128]{3,2,1,0:T(8,128)(2,1)S(1)} %collective-permute-done.4.refs_2_, ...), custom_call_target="tpu_custom_call" | custom-call | flops 1024 | bytes 1024 | tf_op jit(solution)/shard_map/pallas_call | solution.py:446
  58.6 0.9 %shard_map.109 = (bf16[3,2,64,128]{3,2,1,0:T(8,128)(2,1)S(1)}, bf16[3,2,64,128]{3,2,1,0:T(8,128)(2,1)S(1)}, bf16[3,2,64,128]{3,2,1,0:T(8,128)(2,1)S(1)}, bf16[3,2,64,128]{3,2,1,0:T(8,128)(2,1)S(1)}) custom-call(bf16[6,2,64,128]{3,2,1,0:T(8,128)(2,1)S(1)} %bitcast.28, bf16[6,2,64,128]{3,2,1,0:T(8,128)(2,1)S(1)} %bitcast.30, ...), custom_call_target="tpu_custom_call" | custom-call | flops 1024 | bytes 1024 | tf_op jit(solution)/shard_map/pallas_call | solution.py:284
  59.5 2.1 %collective-permute-start.23 = (bf16[3,2,64,128]{3,2,1,0:T(8,128)(2,1)S(1)}, bf16[3,2,64,128]{3,2,1,0:T(8,128)(2,1)S(1)}, u32[]{:S(2)}, u32[]{:S(2)}) collective-permute-start(bf16[3,2,64,128]{3,2,1,0:T(8,128)(2,1)S(1)} %get-tuple-element.146), channel_id=1, source_target_pairs={{0,24},{8,16},{16,8},{24,0},{1,25},{9,17},{17,9},{25,1},{2,26},{10... | collective-permute-start | bytes 294920 | tf_op jit(solution)/shard_map/ppermute | solution.py:63
  61.6 0.3 collective-permute-start.24
  61.9 0.4 collective-permute-start.25
  62.2 2.1 %collective-permute-done.23.refs_5_ = bf16[3,2,64,128]{3,2,1,0:T(8,128)(2,1)S(1)} collective-permute-done((bf16[3,2,64,128]{3,2,1,0:T(8,128)(2,1)S(1)}, bf16[3,2,64,128]{3,2,1,0:T(8,128)(2,1)S(1)}, u32[]{:S(2)}, u32[]{:S(2)}) %collective-permute-start.23) | collective-permute-done | bytes 98336 | tf_op jit(solution)/shard_map/ppermute | solution.py:63
  64.3 0.9 %collective-permute-done.24.refs_6_ = bf16[3,2,64,128]{3,2,1,0:T(8,128)(2,1)S(1)} collective-permute-done((bf16[3,2,64,128]{3,2,1,0:T(8,128)(2,1)S(1)}, bf16[3,2,64,128]{3,2,1,0:T(8,128)(2,1)S(1)}, u32[]{:S(2)}, u32[]{:S(2)}) %collective-permute-start.24) | collective-permute-done | bytes 98336 | tf_op jit(solution)/shard_map/ppermute | solution.py:63
  65.2 0.5 collective-permute-done.25.refs_7_
  65.7 1.5 %shard_map.110 = f32[3072,128]{1,0:T(8,128)} custom-call(bf16[3,2,64,128]{3,2,1,0:T(8,128)(2,1)S(1)} %get-tuple-element.132.refs_0_, bf16[3,2,64,128]{3,2,1,0:T(8,128)(2,1)S(1)} %collective-permute-done.18.refs_1_, bf16[3,2,64,128]{3,2,1,0:T(8,128)(2,1)S(1)} %collective-permute-done.19.refs_2_, bf16[3,2,64,128]{3,2,1,0:T(8,128)(2,1)S(1)} %collective-permute-done.20.refs_3_, ...), custom_call_target="tpu_custom_call" | custom-call | flops 1024 | bytes 1024 | tf_op jit(solution)/shard_map/pallas_call | solution.py:490
  (36 shorter events, 1.2 us)
Async XLA Ops:
  2.2 7.7 %collective-permute-start.6 = (bf16[6,2,32,2,128]{4,3,2,1,0:T(2,128)(2,1)S(1)}, bf16[6,2,32,2,128]{4,3,2,1,0:T(2,128)(2,1)S(1)}, u32[]{:S(2)}, u32[]{:S(2)}) collective-permute-start(bf16[6,2,32,2,128]{4,3,2,1,0:T(2,128)(2,1)S(1)} %shard_map.102), channel_id=1, source_target_pairs={{0,24},{8,16},{16,8},{24,0},{1,25},{9,17},{17,9},{25,1},{2,26},{10... | collective-permute-start | bytes 589832 | tf_op jit(solution)/shard_map/ppermute | solution.py:63
  5.4 8.6 %collective-permute-start.7 = (bf16[6,2,32,2,128]{4,3,2,1,0:T(2,128)(2,1)S(1)}, bf16[6,2,32,2,128]{4,3,2,1,0:T(2,128)(2,1)S(1)}, u32[]{:S(2)}, u32[]{:S(2)}) collective-permute-start(bf16[6,2,32,2,128]{4,3,2,1,0:T(2,128)(2,1)S(1)} %shard_map.103), channel_id=1, source_target_pairs={{0,8},{8,0},{16,24},{24,16},{1,9},{9,1},{17,25},{25,17},{2,10},{10... | collective-permute-start | bytes 589832 | tf_op jit(solution)/shard_map/ppermute | solution.py:63
  5.9 8.8 %collective-permute-start.8 = (bf16[6,2,32,2,128]{4,3,2,1,0:T(2,128)(2,1)S(1)}, bf16[6,2,32,2,128]{4,3,2,1,0:T(2,128)(2,1)S(1)}, u32[]{:S(2)}, u32[]{:S(2)}) collective-permute-start(bf16[6,2,32,2,128]{4,3,2,1,0:T(2,128)(2,1)S(1)} %shard_map.104), channel_id=1, source_target_pairs={{0,16},{8,24},{16,0},{24,8},{1,17},{9,25},{17,1},{25,9},{2,18},{10... | collective-permute-start | bytes 589832 | tf_op jit(solution)/shard_map/ppermute | solution.py:63
  6.2 4.8 %copy-start.3 = (bf16[256,256]{1,0:T(8,128)(2,1)S(1)}, bf16[256,256]{1,0:T(8,128)(2,1)}, u32[]{:S(2)}) copy-start(bf16[256,256]{1,0:T(8,128)(2,1)} %constant.5.clone.refs_1_) | copy-start | bytes 393220
  6.2 4.8 %copy-start.4 = (bf16[256,256]{1,0:T(8,128)(2,1)S(1)}, bf16[256,256]{1,0:T(8,128)(2,1)}, u32[]{:S(2)}) copy-start(bf16[256,256]{1,0:T(8,128)(2,1)} %constant.4.clone.refs_0_) | copy-start | bytes 393220
  6.2 12.1 %collective-permute-start.1 = (bf16[6,2,32,2,128]{4,3,2,1,0:T(2,128)(2,1)S(1)}, bf16[6,2,32,2,128]{4,3,2,1,0:T(2,128)(2,1)S(1)}, u32[]{:S(2)}, u32[]{:S(2)}) collective-permute-start(bf16[6,2,32,2,128]{4,3,2,1,0:T(2,128)(2,1)S(1)} %shard_map.98), channel_id=1, source_target_pairs={{0,8},{8,0},{16,24},{24,16},{1,9},{9,1},{17,25},{25,17},{2,10},{10... | collective-permute-start | bytes 589832 | tf_op jit(solution)/shard_map/ppermute | solution.py:63
  7.9 14.7 %collective-permute-start = (bf16[6,2,32,2,128]{4,3,2,1,0:T(2,128)(2,1)S(1)}, bf16[6,2,32,2,128]{4,3,2,1,0:T(2,128)(2,1)S(1)}, u32[]{:S(2)}, u32[]{:S(2)}) collective-permute-start(bf16[6,2,32,2,128]{4,3,2,1,0:T(2,128)(2,1)S(1)} %shard_map.97), channel_id=1, source_target_pairs={{0,24},{8,16},{16,8},{24,0},{1,25},{9,17},{17,9},{25,1},{2,26},{10... | collective-permute-start | bytes 589832 | tf_op jit(solution)/shard_map/ppermute | solution.py:63
  9.1 10.6 %copy-start = (bf16[12,32,2,2048]{3,2,1,0:T(2,128)(2,1)S(1)}, bf16[12,32,2,2048]{3,2,1,0:T(2,128)(2,1)}, u32[]{:S(2)}) copy-start(bf16[12,32,2,2048]{3,2,1,0:T(2,128)(2,1)} %fields_ref.3) | copy-start | bytes 9437188
  9.9 12.6 %collective-permute-start.2 = (bf16[6,2,32,2,128]{4,3,2,1,0:T(2,128)(2,1)S(1)}, bf16[6,2,32,2,128]{4,3,2,1,0:T(2,128)(2,1)S(1)}, u32[]{:S(2)}, u32[]{:S(2)}) collective-permute-start(bf16[6,2,32,2,128]{4,3,2,1,0:T(2,128)(2,1)S(1)} %shard_map.99), channel_id=1, source_target_pairs={{0,16},{8,24},{16,0},{24,8},{1,17},{9,25},{17,1},{25,9},{2,18},{10... | collective-permute-start | bytes 589832 | tf_op jit(solution)/shard_map/ppermute | solution.py:63
  15.5 10.3 %collective-permute-start.9 = (bf16[4,2,64,128]{3,2,1,0:T(8,128)(2,1)S(1)}, bf16[4,2,64,128]{3,2,1,0:T(8,128)(2,1)S(1)}, u32[]{:S(2)}, u32[]{:S(2)}) collective-permute-start(bf16[4,2,64,128]{3,2,1,0:T(8,128)(2,1)S(1)} %get-tuple-element.90), channel_id=1, source_target_pairs={{0,24},{8,16},{16,8},{24,0},{1,25},{9,17},{17,9},{25,1},{2,26},{10... | collective-permute-start | bytes 393224 | tf_op jit(solution)/shard_map/ppermute | solution.py:63
  18.3 9.9 %collective-permute-start.10 = (bf16[4,2,64,128]{3,2,1,0:T(8,128)(2,1)S(1)}, bf16[4,2,64,128]{3,2,1,0:T(8,128)(2,1)S(1)}, u32[]{:S(2)}, u32[]{:S(2)}) collective-permute-start(bf16[4,2,64,128]{3,2,1,0:T(8,128)(2,1)S(1)} %get-tuple-element.91), channel_id=1, source_target_pairs={{0,8},{8,0},{16,24},{24,16},{1,9},{9,1},{17,25},{25,17},{2,10},{10... | collective-permute-start | bytes 393224 | tf_op jit(solution)/shard_map/ppermute | solution.py:63
  19.5 18.2 %copy-start.7 = (s32[2,256]{1,0:T(2,128)S(1)}, s32[2,256]{1,0:T(2,128)}, u32[]{:S(2)}) copy-start(s32[2,256]{1,0:T(2,128)} %refs_8_.1) | copy-start | bytes 6148
  19.5 9.9 %collective-permute-start.11 = (bf16[4,2,64,128]{3,2,1,0:T(8,128)(2,1)S(1)}, bf16[4,2,64,128]{3,2,1,0:T(8,128)(2,1)S(1)}, u32[]{:S(2)}, u32[]{:S(2)}) collective-permute-start(bf16[4,2,64,128]{3,2,1,0:T(8,128)(2,1)S(1)} %get-tuple-element.92), channel_id=1, source_target_pairs={{0,16},{8,24},{16,0},{24,8},{1,17},{9,25},{17,1},{25,9},{2,18},{10... | collective-permute-start | bytes 393224 | tf_op jit(solution)/shard_map/ppermute | solution.py:63
  23.4 8.7 %collective-permute-start.3 = (bf16[4,2,64,128]{3,2,1,0:T(8,128)(2,1)S(1)}, bf16[4,2,64,128]{3,2,1,0:T(8,128)(2,1)S(1)}, u32[]{:S(2)}, u32[]{:S(2)}) collective-permute-start(bf16[4,2,64,128]{3,2,1,0:T(8,128)(2,1)S(1)} %get-tuple-element.85), channel_id=1, source_target_pairs={{0,24},{8,16},{16,8},{24,0},{1,25},{9,17},{17,9},{25,1},{2,26},{10... | collective-permute-start | bytes 393224 | tf_op jit(solution)/shard_map/ppermute | solution.py:63
  25.6 8.2 %collective-permute-start.4 = (bf16[4,2,64,128]{3,2,1,0:T(8,128)(2,1)S(1)}, bf16[4,2,64,128]{3,2,1,0:T(8,128)(2,1)S(1)}, u32[]{:S(2)}, u32[]{:S(2)}) collective-permute-start(bf16[4,2,64,128]{3,2,1,0:T(8,128)(2,1)S(1)} %get-tuple-element.86), channel_id=1, source_target_pairs={{0,8},{8,0},{16,24},{24,16},{1,9},{9,1},{17,25},{25,17},{2,10},{10... | collective-permute-start | bytes 393224 | tf_op jit(solution)/shard_map/ppermute | solution.py:63
  25.8 8.2 %collective-permute-start.5 = (bf16[4,2,64,128]{3,2,1,0:T(8,128)(2,1)S(1)}, bf16[4,2,64,128]{3,2,1,0:T(8,128)(2,1)S(1)}, u32[]{:S(2)}, u32[]{:S(2)}) collective-permute-start(bf16[4,2,64,128]{3,2,1,0:T(8,128)(2,1)S(1)} %get-tuple-element.87), channel_id=1, source_target_pairs={{0,16},{8,24},{16,0},{24,8},{1,17},{9,25},{17,1},{25,9},{2,18},{10... | collective-permute-start | bytes 393224 | tf_op jit(solution)/shard_map/ppermute | solution.py:63
  29.4 14.6 %collective-permute-start.15 = (bf16[6,2,32,2,128]{4,3,2,1,0:T(2,128)(2,1)S(1)}, bf16[6,2,32,2,128]{4,3,2,1,0:T(2,128)(2,1)S(1)}, u32[]{:S(2)}, u32[]{:S(2)}) collective-permute-start(bf16[6,2,32,2,128]{4,3,2,1,0:T(2,128)(2,1)S(1)} %get-tuple-element.127), channel_id=1, source_target_pairs={{0,24},{8,16},{16,8},{24,0},{1,25},{9,17},{17,9},{25,1},{2,26},{10... | collective-permute-start | bytes 589832 | tf_op jit(solution)/shard_map/ppermute | solution.py:63
  34.0 11.4 %collective-permute-start.16 = (bf16[6,2,32,2,128]{4,3,2,1,0:T(2,128)(2,1)S(1)}, bf16[6,2,32,2,128]{4,3,2,1,0:T(2,128)(2,1)S(1)}, u32[]{:S(2)}, u32[]{:S(2)}) collective-permute-start(bf16[6,2,32,2,128]{4,3,2,1,0:T(2,128)(2,1)S(1)} %get-tuple-element.128), channel_id=1, source_target_pairs={{0,8},{8,0},{16,24},{24,16},{1,9},{9,1},{17,25},{25,17},{2,10},{10... | collective-permute-start | bytes 589832 | tf_op jit(solution)/shard_map/ppermute | solution.py:63
  35.4 10.9 %collective-permute-start.17 = (bf16[6,2,32,2,128]{4,3,2,1,0:T(2,128)(2,1)S(1)}, bf16[6,2,32,2,128]{4,3,2,1,0:T(2,128)(2,1)S(1)}, u32[]{:S(2)}, u32[]{:S(2)}) collective-permute-start(bf16[6,2,32,2,128]{4,3,2,1,0:T(2,128)(2,1)S(1)} %get-tuple-element.129), channel_id=1, source_target_pairs={{0,16},{8,24},{16,0},{24,8},{1,17},{9,25},{17,1},{25,9},{2,18},{10... | collective-permute-start | bytes 589832 | tf_op jit(solution)/shard_map/ppermute | solution.py:63
  38.9 10.4 %collective-permute-start.12 = (bf16[4,2,64,128]{3,2,1,0:T(8,128)(2,1)S(1)}, bf16[4,2,64,128]{3,2,1,0:T(8,128)(2,1)S(1)}, u32[]{:S(2)}, u32[]{:S(2)}) collective-permute-start(bf16[4,2,64,128]{3,2,1,0:T(8,128)(2,1)S(1)} %get-tuple-element.120), channel_id=1, source_target_pairs={{0,1},{1,2},{2,3},{3,4},{4,5},{5,6},{6,7},{8,9},{9,10},{10,11},{11... | collective-permute-start | bytes 393224 | tf_op jit(solution)/shard_map/ppermute | solution.py:70
  43.6 9.6 %collective-permute-start.14 = (bf16[6,2,32,2,128]{4,3,2,1,0:T(2,128)(2,1)S(1)}, bf16[6,2,32,2,128]{4,3,2,1,0:T(2,128)(2,1)S(1)}, u32[]{:S(2)}, u32[]{:S(2)}) collective-permute-start(bf16[6,2,32,2,128]{4,3,2,1,0:T(2,128)(2,1)S(1)} %get-tuple-element.122), channel_id=1, source_target_pairs={{0,24},{8,16},{16,8},{24,0},{1,25},{9,17},{17,9},{25,1},{2,26},{10... | collective-permute-start | bytes 589832 | tf_op jit(solution)/shard_map/ppermute | solution.py:63
  44.0 14.5 %collective-permute-start.21 = (bf16[6,2,32,2,128]{4,3,2,1,0:T(2,128)(2,1)S(1)}, bf16[6,2,32,2,128]{4,3,2,1,0:T(2,128)(2,1)S(1)}, u32[]{:S(2)}, u32[]{:S(2)}) collective-permute-start(bf16[6,2,32,2,128]{4,3,2,1,0:T(2,128)(2,1)S(1)} %get-tuple-element.138), channel_id=1, source_target_pairs={{0,8},{8,0},{16,24},{24,16},{1,9},{9,1},{17,25},{25,17},{2,10},{10... | collective-permute-start | bytes 589832 | tf_op jit(solution)/shard_map/ppermute | solution.py:63
  45.3 13.3 %collective-permute-start.22 = (bf16[6,2,32,2,128]{4,3,2,1,0:T(2,128)(2,1)S(1)}, bf16[6,2,32,2,128]{4,3,2,1,0:T(2,128)(2,1)S(1)}, u32[]{:S(2)}, u32[]{:S(2)}) collective-permute-start(bf16[6,2,32,2,128]{4,3,2,1,0:T(2,128)(2,1)S(1)} %get-tuple-element.139), channel_id=1, source_target_pairs={{0,16},{8,24},{16,0},{24,8},{1,17},{9,25},{17,1},{25,9},{2,18},{10... | collective-permute-start | bytes 589832 | tf_op jit(solution)/shard_map/ppermute | solution.py:63
  46.3 6.6 %collective-permute-start.13 = (bf16[4,2,64,128]{3,2,1,0:T(8,128)(2,1)S(1)}, bf16[4,2,64,128]{3,2,1,0:T(8,128)(2,1)S(1)}, u32[]{:S(2)}, u32[]{:S(2)}) collective-permute-start(bf16[4,2,64,128]{3,2,1,0:T(8,128)(2,1)S(1)} %get-tuple-element.121), channel_id=1, source_target_pairs={{1,0},{2,1},{3,2},{4,3},{5,4},{6,5},{7,6},{9,8},{10,9},{11,10},{12... | collective-permute-start | bytes 393224 | tf_op jit(solution)/shard_map/ppermute | solution.py:70
  48.3 5.3 %copy-start.1 = (bf16[5,64,2048]{2,1,0:T(8,128)(2,1)S(1)}, bf16[5,64,2048]{2,1,0:T(8,128)(2,1)}, u32[]{:S(2)}) copy-start(bf16[5,64,2048]{2,1,0:T(8,128)(2,1)} %refs_10_.1) | copy-start | bytes 3932164
  48.3 5.3 %copy-start.2 = (bf16[5,64,2048]{2,1,0:T(8,128)(2,1)S(1)}, bf16[5,64,2048]{2,1,0:T(8,128)(2,1)}, u32[]{:S(2)}) copy-start(bf16[5,64,2048]{2,1,0:T(8,128)(2,1)} %refs_11_.1) | copy-start | bytes 3932164
  48.3 5.3 %copy-start.5 = (f32[2048]{0:T(1024)S(1)}, f32[2048]{0:T(1024)}, u32[]{:S(2)}) copy-start(f32[2048]{0:T(1024)} %param.9) | copy-start | bytes 24580
  48.3 5.3 %copy-start.6 = (s32[32,5]{0,1:T(8,128)S(1)}, s32[32,5]{0,1:T(8,128)}, u32[]{:S(2)}) copy-start(s32[32,5]{0,1:T(8,128)} %param.12) | copy-start | bytes 1924
  49.3 12.6 %collective-permute-start.18 = (bf16[3,2,64,128]{3,2,1,0:T(8,128)(2,1)S(1)}, bf16[3,2,64,128]{3,2,1,0:T(8,128)(2,1)S(1)}, u32[]{:S(2)}, u32[]{:S(2)}) collective-permute-start(bf16[3,2,64,128]{3,2,1,0:T(8,128)(2,1)S(1)} %get-tuple-element.133), channel_id=1, source_target_pairs={{0,24},{8,16},{16,8},{24,0},{1,25},{9,17},{17,9},{25,1},{2,26},{10... | collective-permute-start | bytes 294920 | tf_op jit(solution)/shard_map/ppermute | solution.py:63
  52.9 9.3 %collective-permute-start.19 = (bf16[3,2,64,128]{3,2,1,0:T(8,128)(2,1)S(1)}, bf16[3,2,64,128]{3,2,1,0:T(8,128)(2,1)S(1)}, u32[]{:S(2)}, u32[]{:S(2)}) collective-permute-start(bf16[3,2,64,128]{3,2,1,0:T(8,128)(2,1)S(1)} %get-tuple-element.134), channel_id=1, source_target_pairs={{0,8},{8,0},{16,24},{24,16},{1,9},{9,1},{17,25},{25,17},{2,10},{10... | collective-permute-start | bytes 294920 | tf_op jit(solution)/shard_map/ppermute | solution.py:63
  53.2 9.1 %collective-permute-start.20 = (bf16[3,2,64,128]{3,2,1,0:T(8,128)(2,1)S(1)}, bf16[3,2,64,128]{3,2,1,0:T(8,128)(2,1)S(1)}, u32[]{:S(2)}, u32[]{:S(2)}) collective-permute-start(bf16[3,2,64,128]{3,2,1,0:T(8,128)(2,1)S(1)} %get-tuple-element.135), channel_id=1, source_target_pairs={{0,16},{8,24},{16,0},{24,8},{1,17},{9,25},{17,1},{25,9},{2,18},{10... | collective-permute-start | bytes 294920 | tf_op jit(solution)/shard_map/ppermute | solution.py:63
  59.5 4.8 %collective-permute-start.23 = (bf16[3,2,64,128]{3,2,1,0:T(8,128)(2,1)S(1)}, bf16[3,2,64,128]{3,2,1,0:T(8,128)(2,1)S(1)}, u32[]{:S(2)}, u32[]{:S(2)}) collective-permute-start(bf16[3,2,64,128]{3,2,1,0:T(8,128)(2,1)S(1)} %get-tuple-element.146), channel_id=1, source_target_pairs={{0,24},{8,16},{16,8},{24,0},{1,25},{9,17},{17,9},{25,1},{2,26},{10... | collective-permute-start | bytes 294920 | tf_op jit(solution)/shard_map/ppermute | solution.py:63
  61.6 3.6 %collective-permute-start.24 = (bf16[3,2,64,128]{3,2,1,0:T(8,128)(2,1)S(1)}, bf16[3,2,64,128]{3,2,1,0:T(8,128)(2,1)S(1)}, u32[]{:S(2)}, u32[]{:S(2)}) collective-permute-start(bf16[3,2,64,128]{3,2,1,0:T(8,128)(2,1)S(1)} %get-tuple-element.147), channel_id=1, source_target_pairs={{0,8},{8,0},{16,24},{24,16},{1,9},{9,1},{17,25},{25,17},{2,10},{10... | collective-permute-start | bytes 294920 | tf_op jit(solution)/shard_map/ppermute | solution.py:63
  61.9 3.8 %collective-permute-start.25 = (bf16[3,2,64,128]{3,2,1,0:T(8,128)(2,1)S(1)}, bf16[3,2,64,128]{3,2,1,0:T(8,128)(2,1)S(1)}, u32[]{:S(2)}, u32[]{:S(2)}) collective-permute-start(bf16[3,2,64,128]{3,2,1,0:T(8,128)(2,1)S(1)} %get-tuple-element.148), channel_id=1, source_target_pairs={{0,16},{8,24},{16,0},{24,8},{1,17},{9,25},{17,1},{25,9},{2,18},{10... | collective-permute-start | bytes 294920 | tf_op jit(solution)/shard_map/ppermute | solution.py:63

commit v22 on v19

--- a/solution.py
+++ b/solution.py
@@ -435,7 +435,7 @@
             put_rows(induction_ref, i * mode_count * stride + 2 * q * together, stride, [tile[i] for tile in induction])
         return carry
 
-    lax.fori_loop(0, node_tiles // together, tiles_at, 0)
+    lax.fori_loop(0, node_tiles // together, tiles_at, 0, unroll=True)
 
 
 def derive(received, from_prev, from_next, radial_blocks, axial_blocks, radius, columns, count):

time: 67 us -> 66.7 us (level)
  transfers between devices with their start and end apart: 26 -> 26, of which waited for: 12 -> 13; matrix products, arithmetic and copies ran while one was open for 0% -> 0% of each run, Pallas kernels for 18% -> 18%
where the time goes in v22:
time: 66.7 us; the launch traced here: 65.6 us
  starting transfers between devices  34 us (51%)
  waiting for transfers between devices  15.7 us (24%)
  Pallas kernels  14.9 us (22%)
  between operations  0.82 us (1%)
    ppermute x24, starting transfers between devices, exchange(): received.append(lax.ppermute(piece, 'mode', pairs))  27.5 us
    ppermute x24, waiting for transfers between devices, exchange(): received.append(lax.ppermute(piece, 'mode', pairs))  12.5 us
    ppermute x2, starting transfers between devices, from_behind(): lax.ppermute(value, axis, [(source, source + steps) for source in range(i...  6.57 us
    pallas_call x1, Pallas kernels, derive(): pl.pallas_call(functools.partial(derive_kernel, count, len(received)), in...  4.69 us
    ppermute x2, waiting for transfers between devices, from_behind(): lax.ppermute(value, axis, [(source, source + steps) for source in range(i...  3.29 us
    pallas_call x2, Pallas kernels, second_physics(): pl.pallas_call(functools.partial(second_kernel, count, groups, begin), in...  1.84 us
    pallas_call x2, Pallas kernels, first_physics(): pl.pallas_call(functools.partial(first_kernel, count), in_specs=[vmem()]...  1.63 us
    pallas_call x2, Pallas kernels, pack_rest(): pl.pallas_call(kernel, in_specs=[pl.BlockSpec(memory_space=pl.ANY)] + [vm...  1.62 us
  transfers between devices with their start and end apart: 26, of which 13 were waited for; matrix products, arithmetic and copies ran while one was open for 0% of the time, Pallas kernels for 18%

profile of v22, /device:TPU:1, one launch (start us, length us, event | category | flops | bytes accessed | tf_op | source)
XLA Modules:
  0.0 65.6 jit_solution(17318859601148700586)
XLA Ops:
  0.6 1.4 %shard_map.95.fields_ref = bf16[6,32,2,2048]{3,2,1,0:T(2,128)(2,1)S(1)} custom-call(bf16[12,32,2,2048]{3,2,1,0:T(2,128)(2,1)} %fields_ref.3), custom_call_target="tpu_custom_call" | custom-call | flops 1024 | bytes 1024 | tf_op jit(solution)/shard_map/pallas_call | solution.py:123
  2.0 0.2 shard_map.102
  2.2 3.1 %collective-permute-start.6 = (bf16[6,2,32,2,128]{4,3,2,1,0:T(2,128)(2,1)S(1)}, bf16[6,2,32,2,128]{4,3,2,1,0:T(2,128)(2,1)S(1)}, u32[]{:S(2)}, u32[]{:S(2)}) collective-permute-start(bf16[6,2,32,2,128]{4,3,2,1,0:T(2,128)(2,1)S(1)} %shard_map.102), channel_id=1, source_target_pairs={{0,24},{8,16},{16,8},{24,0},{1,25},{9,17},{17,9},{25,1},{2,26},{10... | collective-permute-start | bytes 589832 | tf_op jit(solution)/shard_map/ppermute | solution.py:63
  5.4 0.3 collective-permute-start.7
  6.2 1.4 %collective-permute-start.1 = (bf16[6,2,32,2,128]{4,3,2,1,0:T(2,128)(2,1)S(1)}, bf16[6,2,32,2,128]{4,3,2,1,0:T(2,128)(2,1)S(1)}, u32[]{:S(2)}, u32[]{:S(2)}) collective-permute-start(bf16[6,2,32,2,128]{4,3,2,1,0:T(2,128)(2,1)S(1)} %shard_map.98), channel_id=1, source_target_pairs={{0,8},{8,0},{16,24},{24,16},{1,9},{9,1},{17,25},{25,17},{2,10},{10... | collective-permute-start | bytes 589832 | tf_op jit(solution)/shard_map/ppermute | solution.py:63
  7.9 1.3 %collective-permute-start = (bf16[6,2,32,2,128]{4,3,2,1,0:T(2,128)(2,1)S(1)}, bf16[6,2,32,2,128]{4,3,2,1,0:T(2,128)(2,1)S(1)}, u32[]{:S(2)}, u32[]{:S(2)}) collective-permute-start(bf16[6,2,32,2,128]{4,3,2,1,0:T(2,128)(2,1)S(1)} %shard_map.97), channel_id=1, source_target_pairs={{0,24},{8,16},{16,8},{24,0},{1,25},{9,17},{17,9},{25,1},{2,26},{10... | collective-permute-start | bytes 589832 | tf_op jit(solution)/shard_map/ppermute | solution.py:63
  9.3 0.6 collective-permute-done.6
  9.9 1.2 %collective-permute-start.2 = (bf16[6,2,32,2,128]{4,3,2,1,0:T(2,128)(2,1)S(1)}, bf16[6,2,32,2,128]{4,3,2,1,0:T(2,128)(2,1)S(1)}, u32[]{:S(2)}, u32[]{:S(2)}) collective-permute-start(bf16[6,2,32,2,128]{4,3,2,1,0:T(2,128)(2,1)S(1)} %shard_map.99), channel_id=1, source_target_pairs={{0,16},{8,24},{16,0},{24,8},{1,17},{9,25},{17,1},{25,9},{2,18},{10... | collective-permute-start | bytes 589832 | tf_op jit(solution)/shard_map/ppermute | solution.py:63
  11.1 0.3 shard_map.96
  11.4 2.7 %collective-permute-done.7 = bf16[6,2,32,2,128]{4,3,2,1,0:T(2,128)(2,1)S(1)} collective-permute-done((bf16[6,2,32,2,128]{4,3,2,1,0:T(2,128)(2,1)S(1)}, bf16[6,2,32,2,128]{4,3,2,1,0:T(2,128)(2,1)S(1)}, u32[]{:S(2)}, u32[]{:S(2)}) %collective-permute-start.7) | collective-permute-done | bytes 196640 | tf_op jit(solution)/shard_map/ppermute | solution.py:63
  14.1 0.6 collective-permute-done.8
  14.7 0.8 %shard_map.105 = (bf16[4,2,64,128]{3,2,1,0:T(8,128)(2,1)S(1)}, bf16[4,2,64,128]{3,2,1,0:T(8,128)(2,1)S(1)}, bf16[4,2,64,128]{3,2,1,0:T(8,128)(2,1)S(1)}, bf16[4,...) custom-call(bf16[6,2,64,128]{3,2,1,0:T(8,128)(2,1)S(1)} %bitcast.43, bf16[6,2,64,128]{3,2,1,0:T(8,128)(2,1)S(1)} %bitcast.40, ...), custom_call_target="tpu_custom_call" | custom-call | flops 1024 | bytes 1024 | tf_op jit(solution)/shard_map/pallas_call | solution.py:238
  15.5 2.6 %collective-permute-start.9 = (bf16[4,2,64,128]{3,2,1,0:T(8,128)(2,1)S(1)}, bf16[4,2,64,128]{3,2,1,0:T(8,128)(2,1)S(1)}, u32[]{:S(2)}, u32[]{:S(2)}) collective-permute-start(bf16[4,2,64,128]{3,2,1,0:T(8,128)(2,1)S(1)} %get-tuple-element.93), channel_id=1, source_target_pairs={{0,24},{8,16},{16,8},{24,0},{1,25},{9,17},{17,9},{25,1},{2,26},{10... | collective-permute-start | bytes 393224 | tf_op jit(solution)/shard_map/ppermute | solution.py:63
  18.1 0.2 collective-permute-done.1
  18.3 1.2 %collective-permute-start.10 = (bf16[4,2,64,128]{3,2,1,0:T(8,128)(2,1)S(1)}, bf16[4,2,64,128]{3,2,1,0:T(8,128)(2,1)S(1)}, u32[]{:S(2)}, u32[]{:S(2)}) collective-permute-start(bf16[4,2,64,128]{3,2,1,0:T(8,128)(2,1)S(1)} %get-tuple-element.94), channel_id=1, source_target_pairs={{0,8},{8,0},{16,24},{24,16},{1,9},{9,1},{17,25},{25,17},{2,10},{10... | collective-permute-start | bytes 393224 | tf_op jit(solution)/shard_map/ppermute | solution.py:63
  19.5 0.2 collective-permute-start.11
  19.7 1.3 %shard_map.100 = (bf16[6,2,32,2,128]{4,3,2,1,0:T(2,128)(2,1)S(1)}, bf16[6,2,32,2,128]{4,3,2,1,0:T(2,128)(2,1)S(1)}, bf16[6,2,32,2,128]{4,3,2,1,0:T(2,128)(2,1)S(...) custom-call(bf16[12,32,2,2048]{3,2,1,0:T(2,128)(2,1)S(1)} %copy-done, ...), custom_call_target="tpu_custom_call" | custom-call | flops 1024 | bytes 1024 | tf_op jit(solution)/shard_map/pallas_call | solution.py:170
  21.0 1.5 %collective-permute-done = bf16[6,2,32,2,128]{4,3,2,1,0:T(2,128)(2,1)S(1)} collective-permute-done((bf16[6,2,32,2,128]{4,3,2,1,0:T(2,128)(2,1)S(1)}, bf16[6,2,32,2,128]{4,3,2,1,0:T(2,128)(2,1)S(1)}, u32[]{:S(2)}, u32[]{:S(2)}) %collective-permute-start) | collective-permute-done | bytes 196640 | tf_op jit(solution)/shard_map/ppermute | solution.py:63
  22.5 0.8 %shard_map.101 = (bf16[4,2,64,128]{3,2,1,0:T(8,128)(2,1)S(1)}, bf16[4,2,64,128]{3,2,1,0:T(8,128)(2,1)S(1)}, bf16[4,2,64,128]{3,2,1,0:T(8,128)(2,1)S(1)}, bf16[4,...) custom-call(bf16[6,2,64,128]{3,2,1,0:T(8,128)(2,1)S(1)} %bitcast.39, bf16[6,2,64,128]{3,2,1,0:T(8,128)(2,1)S(1)} %bitcast.37, ...), custom_call_target="tpu_custom_call" | custom-call | flops 1024 | bytes 1024 | tf_op jit(solution)/shard_map/pallas_call | solution.py:238
  23.4 2.2 %collective-permute-start.3 = (bf16[4,2,64,128]{3,2,1,0:T(8,128)(2,1)S(1)}, bf16[4,2,64,128]{3,2,1,0:T(8,128)(2,1)S(1)}, u32[]{:S(2)}, u32[]{:S(2)}) collective-permute-start(bf16[4,2,64,128]{3,2,1,0:T(8,128)(2,1)S(1)} %get-tuple-element.88), channel_id=1, source_target_pairs={{0,24},{8,16},{16,8},{24,0},{1,25},{9,17},{17,9},{25,1},{2,26},{10... | collective-permute-start | bytes 393224 | tf_op jit(solution)/shard_map/ppermute | solution.py:63
  25.6 0.2 collective-permute-start.4
  25.8 0.8 %collective-permute-start.5 = (bf16[4,2,64,128]{3,2,1,0:T(8,128)(2,1)S(1)}, bf16[4,2,64,128]{3,2,1,0:T(8,128)(2,1)S(1)}, u32[]{:S(2)}, u32[]{:S(2)}) collective-permute-start(bf16[4,2,64,128]{3,2,1,0:T(8,128)(2,1)S(1)} %get-tuple-element.90), channel_id=1, source_target_pairs={{0,16},{8,24},{16,0},{24,8},{1,17},{9,25},{17,1},{25,9},{2,18},{10... | collective-permute-start | bytes 393224 | tf_op jit(solution)/shard_map/ppermute | solution.py:63
  26.6 1.6 %collective-permute-done.10.refs_6_ = bf16[4,2,64,128]{3,2,1,0:T(8,128)(2,1)S(1)} collective-permute-done((bf16[4,2,64,128]{3,2,1,0:T(8,128)(2,1)S(1)}, bf16[4,2,64,128]{3,2,1,0:T(8,128)(2,1)S(1)}, u32[]{:S(2)}, u32[]{:S(2)}) %collective-permute-start.10) | collective-permute-done | bytes 131104 | tf_op jit(solution)/shard_map/ppermute | solution.py:63
  28.2 1.2 %collective-permute-done.11.refs_7_ = bf16[4,2,64,128]{3,2,1,0:T(8,128)(2,1)S(1)} collective-permute-done((bf16[4,2,64,128]{3,2,1,0:T(8,128)(2,1)S(1)}, bf16[4,2,64,128]{3,2,1,0:T(8,128)(2,1)S(1)}, u32[]{:S(2)}, u32[]{:S(2)}) %collective-permute-start.11) | collective-permute-done | bytes 131104 | tf_op jit(solution)/shard_map/ppermute | solution.py:63
  29.4 2.7 %collective-permute-start.17 = (bf16[6,2,32,2,128]{4,3,2,1,0:T(2,128)(2,1)S(1)}, bf16[6,2,32,2,128]{4,3,2,1,0:T(2,128)(2,1)S(1)}, u32[]{:S(2)}, u32[]{:S(2)}) collective-permute-start(bf16[6,2,32,2,128]{4,3,2,1,0:T(2,128)(2,1)S(1)} %get-tuple-element.144), channel_id=1, source_target_pairs={{0,24},{8,16},{16,8},{24,0},{1,25},{9,17},{17,9},{25,1},{2,26},{10... | collective-permute-start | bytes 589832 | tf_op jit(solution)/shard_map/ppermute | solution.py:63
  32.1 1.7 %collective-permute-done.4.refs_2_ = bf16[4,2,64,128]{3,2,1,0:T(8,128)(2,1)S(1)} collective-permute-done((bf16[4,2,64,128]{3,2,1,0:T(8,128)(2,1)S(1)}, bf16[4,2,64,128]{3,2,1,0:T(8,128)(2,1)S(1)}, u32[]{:S(2)}, u32[]{:S(2)}) %collective-permute-start.4) | collective-permute-done | bytes 131104 | tf_op jit(solution)/shard_map/ppermute | solution.py:63
  33.8 0.2 collective-permute-done.5.refs_3_
  34.0 1.4 %collective-permute-start.18 = (bf16[6,2,32,2,128]{4,3,2,1,0:T(2,128)(2,1)S(1)}, bf16[6,2,32,2,128]{4,3,2,1,0:T(2,128)(2,1)S(1)}, u32[]{:S(2)}, u32[]{:S(2)}) collective-permute-start(bf16[6,2,32,2,128]{4,3,2,1,0:T(2,128)(2,1)S(1)} %get-tuple-element.145), channel_id=1, source_target_pairs={{0,8},{8,0},{16,24},{24,16},{1,9},{9,1},{17,25},{25,17},{2,10},{10... | collective-permute-start | bytes 589832 | tf_op jit(solution)/shard_map/ppermute | solution.py:63
  35.4 2.3 %collective-permute-start.19 = (bf16[6,2,32,2,128]{4,3,2,1,0:T(2,128)(2,1)S(1)}, bf16[6,2,32,2,128]{4,3,2,1,0:T(2,128)(2,1)S(1)}, u32[]{:S(2)}, u32[]{:S(2)}) collective-permute-start(bf16[6,2,32,2,128]{4,3,2,1,0:T(2,128)(2,1)S(1)} %get-tuple-element.146), channel_id=1, source_target_pairs={{0,16},{8,24},{16,0},{24,8},{1,17},{9,25},{17,1},{25,9},{2,18},{10... | collective-permute-start | bytes 589832 | tf_op jit(solution)/shard_map/ppermute | solution.py:63
  37.7 1.2 %shard_map.106 = (bf16[4,2,64,128]{3,2,1,0:T(8,128)(2,1)S(1)}, bf16[4,2,64,128]{3,2,1,0:T(8,128)(2,1)S(1)}) custom-call(bf16[4,2,64,128]{3,2,1,0:T(8,128)(2,1)S(1)} %get-tuple-element.115.refs_0_, bf16[4,2,64,128]{3,2,1,0:T(8,128)(2,1)S(1)} %collective-permute-done.3.refs_1_, bf16[4,2,64,128]{3,2,1,0:T(8,128)(2,1)S(1)} %collective-permute-done.4.refs_2_, ...), custom_call_target="tpu_custom_call" | custom-call | flops 1024 | bytes 1024 | tf_op jit(solution)/shard_map/pallas_call | solution.py:334
  38.9 4.7 %collective-permute-start.15 = (bf16[4,2,64,128]{3,2,1,0:T(8,128)(2,1)S(1)}, bf16[4,2,64,128]{3,2,1,0:T(8,128)(2,1)S(1)}, u32[]{:S(2)}, u32[]{:S(2)}) collective-permute-start(bf16[4,2,64,128]{3,2,1,0:T(8,128)(2,1)S(1)} %get-tuple-element.127), channel_id=1, source_target_pairs={{0,1},{1,2},{2,3},{3,4},{4,5},{5,6},{6,7},{8,9},{9,10},{10,11},{11... | collective-permute-start | bytes 393224 | tf_op jit(solution)/shard_map/ppermute | solution.py:70
  43.6 0.4 collective-permute-start.12
  44.0 1.3 %collective-permute-start.13 = (bf16[6,2,32,2,128]{4,3,2,1,0:T(2,128)(2,1)S(1)}, bf16[6,2,32,2,128]{4,3,2,1,0:T(2,128)(2,1)S(1)}, u32[]{:S(2)}, u32[]{:S(2)}) collective-permute-start(bf16[6,2,32,2,128]{4,3,2,1,0:T(2,128)(2,1)S(1)} %get-tuple-element.125), channel_id=1, source_target_pairs={{0,8},{8,0},{16,24},{24,16},{1,9},{9,1},{17,25},{25,17},{2,10},{10... | collective-permute-start | bytes 589832 | tf_op jit(solution)/shard_map/ppermute | solution.py:63
  45.3 1.0 %collective-permute-start.14 = (bf16[6,2,32,2,128]{4,3,2,1,0:T(2,128)(2,1)S(1)}, bf16[6,2,32,2,128]{4,3,2,1,0:T(2,128)(2,1)S(1)}, u32[]{:S(2)}, u32[]{:S(2)}) collective-permute-start(bf16[6,2,32,2,128]{4,3,2,1,0:T(2,128)(2,1)S(1)} %get-tuple-element.126), channel_id=1, source_target_pairs={{0,16},{8,24},{16,0},{24,8},{1,17},{9,25},{17,1},{25,9},{2,18},{10... | collective-permute-start | bytes 589832 | tf_op jit(solution)/shard_map/ppermute | solution.py:63
  46.3 1.9 %collective-permute-start.16 = (bf16[4,2,64,128]{3,2,1,0:T(8,128)(2,1)S(1)}, bf16[4,2,64,128]{3,2,1,0:T(8,128)(2,1)S(1)}, u32[]{:S(2)}, u32[]{:S(2)}) collective-permute-start(bf16[4,2,64,128]{3,2,1,0:T(8,128)(2,1)S(1)} %get-tuple-element.128), channel_id=1, source_target_pairs={{1,0},{2,1},{3,2},{4,3},{5,4},{6,5},{7,6},{9,8},{10,9},{11,10},{12... | collective-permute-start | bytes 393224 | tf_op jit(solution)/shard_map/ppermute | solution.py:70
  48.3 0.9 %shard_map.109 = (bf16[3,2,64,128]{3,2,1,0:T(8,128)(2,1)S(1)}, bf16[3,2,64,128]{3,2,1,0:T(8,128)(2,1)S(1)}, bf16[3,2,64,128]{3,2,1,0:T(8,128)(2,1)S(1)}, bf16[3,2,64,128]{3,2,1,0:T(8,128)(2,1)S(1)}) custom-call(bf16[6,2,64,128]{3,2,1,0:T(8,128)(2,1)S(1)} %bitcast.29, bf16[6,2,64,128]{3,2,1,0:T(8,128)(2,1)S(1)} %bitcast.32, ...), custom_call_target="tpu_custom_call" | custom-call | flops 1024 | bytes 1024 | tf_op jit(solution)/shard_map/pallas_call | solution.py:284
  49.2 0.4 collective-permute-start.20
  49.6 3.3 %collective-permute-done.16.refs_9_ = bf16[4,2,64,128]{3,2,1,0:T(8,128)(2,1)S(1)} collective-permute-done((bf16[4,2,64,128]{3,2,1,0:T(8,128)(2,1)S(1)}, bf16[4,2,64,128]{3,2,1,0:T(8,128)(2,1)S(1)}, u32[]{:S(2)}, u32[]{:S(2)}) %collective-permute-start.16) | collective-permute-done | bytes 131104 | tf_op jit(solution)/shard_map/ppermute | solution.py:70
  52.9 0.3 collective-permute-start.21
  53.2 0.4 collective-permute-start.22
  53.6 1.5 %collective-permute-done.13 = bf16[6,2,32,2,128]{4,3,2,1,0:T(2,128)(2,1)S(1)} collective-permute-done((bf16[6,2,32,2,128]{4,3,2,1,0:T(2,128)(2,1)S(1)}, bf16[6,2,32,2,128]{4,3,2,1,0:T(2,128)(2,1)S(1)}, u32[]{:S(2)}, u32[]{:S(2)}) %collective-permute-start.13) | collective-permute-done | bytes 196640 | tf_op jit(solution)/shard_map/ppermute | solution.py:63
  55.0 0.5 collective-permute-done.14
  55.5 0.9 %shard_map.107 = (bf16[3,2,64,128]{3,2,1,0:T(8,128)(2,1)S(1)}, bf16[3,2,64,128]{3,2,1,0:T(8,128)(2,1)S(1)}, bf16[3,2,64,128]{3,2,1,0:T(8,128)(2,1)S(1)}, bf16[3,2,64,128]{3,2,1,0:T(8,128)(2,1)S(1)}) custom-call(bf16[6,2,64,128]{3,2,1,0:T(8,128)(2,1)S(1)} %bitcast.28, bf16[6,2,64,128]{3,2,1,0:T(8,128)(2,1)S(1)} %bitcast.30, ...), custom_call_target="tpu_custom_call" | custom-call | flops 1024 | bytes 1024 | tf_op jit(solution)/shard_map/pallas_call | solution.py:284
  56.4 0.6 collective-permute-start.23
  57.0 1.2 %collective-permute-start.24 = (bf16[3,2,64,128]{3,2,1,0:T(8,128)(2,1)S(1)}, bf16[3,2,64,128]{3,2,1,0:T(8,128)(2,1)S(1)}, u32[]{:S(2)}, u32[]{:S(2)}) collective-permute-start(bf16[3,2,64,128]{3,2,1,0:T(8,128)(2,1)S(1)} %get-tuple-element.153), channel_id=1, source_target_pairs={{0,8},{8,0},{16,24},{24,16},{1,9},{9,1},{17,25},{25,17},{2,10},{10... | collective-permute-start | bytes 294920 | tf_op jit(solution)/shard_map/ppermute | solution.py:63
  58.2 0.9 %collective-permute-start.25 = (bf16[3,2,64,128]{3,2,1,0:T(8,128)(2,1)S(1)}, bf16[3,2,64,128]{3,2,1,0:T(8,128)(2,1)S(1)}, u32[]{:S(2)}, u32[]{:S(2)}) collective-permute-start(bf16[3,2,64,128]{3,2,1,0:T(8,128)(2,1)S(1)} %get-tuple-element.154), channel_id=1, source_target_pairs={{0,16},{8,24},{16,0},{24,8},{1,17},{9,25},{17,1},{25,9},{2,18},{10... | collective-permute-start | bytes 294920 | tf_op jit(solution)/shard_map/ppermute | solution.py:63
  59.2 4.7 %shard_map.108 = (f32[3072,128]{1,0:T(8,128)}, f32[3,16,64,128]{3,2,1,0:T(8,128)S(1)}) custom-call(bf16[4,2,64,128]{3,2,1,0:T(8,128)(2,1)S(1)} %get-tuple-element.115.refs_0_, bf16[4,2,64,128]{3,2,1,0:T(8,128)(2,1)S(1)} %collective-permute-done.3.refs_1_, bf16[4,2,64,128]{3,2,1,0:T(8,128)(2,1)S(1)} %collective-permute-done.4.refs_2_, ...), custom_call_target="tpu_custom_call" | custom-call | flops 1024 | bytes 1024 | tf_op jit(solution)/shard_map/pallas_call | solution.py:446
  64.0 1.6 %shard_map.110 = f32[3072,128]{1,0:T(8,128)} custom-call(bf16[3,2,64,128]{3,2,1,0:T(8,128)(2,1)S(1)} %get-tuple-element.147.refs_0_, bf16[3,2,64,128]{3,2,1,0:T(8,128)(2,1)S(1)} %collective-permute-done.20.refs_1_, bf16[3,2,64,128]{3,2,1,0:T(8,128)(2,1)S(1)} %collective-permute-done.21.refs_2_, bf16[3,2,64,128]{3,2,1,0:T(8,128)(2,1)S(1)} %collective-permute-done.22.refs_3_, ...), custom_call_target="tpu_custom_call" | custom-call | flops 1024 | bytes 1024 | tf_op jit(solution)/shard_map/pallas_call | solution.py:490
  (36 shorter events, 1.1 us)
Async XLA Ops:
  2.2 7.7 %collective-permute-start.6 = (bf16[6,2,32,2,128]{4,3,2,1,0:T(2,128)(2,1)S(1)}, bf16[6,2,32,2,128]{4,3,2,1,0:T(2,128)(2,1)S(1)}, u32[]{:S(2)}, u32[]{:S(2)}) collective-permute-start(bf16[6,2,32,2,128]{4,3,2,1,0:T(2,128)(2,1)S(1)} %shard_map.102), channel_id=1, source_target_pairs={{0,24},{8,16},{16,8},{24,0},{1,25},{9,17},{17,9},{25,1},{2,26},{10... | collective-permute-start | bytes 589832 | tf_op jit(solution)/shard_map/ppermute | solution.py:63
  5.4 8.6 %collective-permute-start.7 = (bf16[6,2,32,2,128]{4,3,2,1,0:T(2,128)(2,1)S(1)}, bf16[6,2,32,2,128]{4,3,2,1,0:T(2,128)(2,1)S(1)}, u32[]{:S(2)}, u32[]{:S(2)}) collective-permute-start(bf16[6,2,32,2,128]{4,3,2,1,0:T(2,128)(2,1)S(1)} %shard_map.103), channel_id=1, source_target_pairs={{0,8},{8,0},{16,24},{24,16},{1,9},{9,1},{17,25},{25,17},{2,10},{10... | collective-permute-start | bytes 589832 | tf_op jit(solution)/shard_map/ppermute | solution.py:63
  5.9 8.8 %collective-permute-start.8 = (bf16[6,2,32,2,128]{4,3,2,1,0:T(2,128)(2,1)S(1)}, bf16[6,2,32,2,128]{4,3,2,1,0:T(2,128)(2,1)S(1)}, u32[]{:S(2)}, u32[]{:S(2)}) collective-permute-start(bf16[6,2,32,2,128]{4,3,2,1,0:T(2,128)(2,1)S(1)} %shard_map.104), channel_id=1, source_target_pairs={{0,16},{8,24},{16,0},{24,8},{1,17},{9,25},{17,1},{25,9},{2,18},{10... | collective-permute-start | bytes 589832 | tf_op jit(solution)/shard_map/ppermute | solution.py:63
  6.2 4.8 %copy-start.3 = (bf16[256,256]{1,0:T(8,128)(2,1)S(1)}, bf16[256,256]{1,0:T(8,128)(2,1)}, u32[]{:S(2)}) copy-start(bf16[256,256]{1,0:T(8,128)(2,1)} %constant.5.clone.refs_1_) | copy-start | bytes 393220
  6.2 4.8 %copy-start.4 = (bf16[256,256]{1,0:T(8,128)(2,1)S(1)}, bf16[256,256]{1,0:T(8,128)(2,1)}, u32[]{:S(2)}) copy-start(bf16[256,256]{1,0:T(8,128)(2,1)} %constant.4.clone.refs_0_) | copy-start | bytes 393220
  6.2 12.1 %collective-permute-start.1 = (bf16[6,2,32,2,128]{4,3,2,1,0:T(2,128)(2,1)S(1)}, bf16[6,2,32,2,128]{4,3,2,1,0:T(2,128)(2,1)S(1)}, u32[]{:S(2)}, u32[]{:S(2)}) collective-permute-start(bf16[6,2,32,2,128]{4,3,2,1,0:T(2,128)(2,1)S(1)} %shard_map.98), channel_id=1, source_target_pairs={{0,8},{8,0},{16,24},{24,16},{1,9},{9,1},{17,25},{25,17},{2,10},{10... | collective-permute-start | bytes 589832 | tf_op jit(solution)/shard_map/ppermute | solution.py:63
  7.9 14.7 %collective-permute-start = (bf16[6,2,32,2,128]{4,3,2,1,0:T(2,128)(2,1)S(1)}, bf16[6,2,32,2,128]{4,3,2,1,0:T(2,128)(2,1)S(1)}, u32[]{:S(2)}, u32[]{:S(2)}) collective-permute-start(bf16[6,2,32,2,128]{4,3,2,1,0:T(2,128)(2,1)S(1)} %shard_map.97), channel_id=1, source_target_pairs={{0,24},{8,16},{16,8},{24,0},{1,25},{9,17},{17,9},{25,1},{2,26},{10... | collective-permute-start | bytes 589832 | tf_op jit(solution)/shard_map/ppermute | solution.py:63
  9.1 10.6 %copy-start = (bf16[12,32,2,2048]{3,2,1,0:T(2,128)(2,1)S(1)}, bf16[12,32,2,2048]{3,2,1,0:T(2,128)(2,1)}, u32[]{:S(2)}) copy-start(bf16[12,32,2,2048]{3,2,1,0:T(2,128)(2,1)} %fields_ref.3) | copy-start | bytes 9437188
  9.9 12.6 %collective-permute-start.2 = (bf16[6,2,32,2,128]{4,3,2,1,0:T(2,128)(2,1)S(1)}, bf16[6,2,32,2,128]{4,3,2,1,0:T(2,128)(2,1)S(1)}, u32[]{:S(2)}, u32[]{:S(2)}) collective-permute-start(bf16[6,2,32,2,128]{4,3,2,1,0:T(2,128)(2,1)S(1)} %shard_map.99), channel_id=1, source_target_pairs={{0,16},{8,24},{16,0},{24,8},{1,17},{9,25},{17,1},{25,9},{2,18},{10... | collective-permute-start | bytes 589832 | tf_op jit(solution)/shard_map/ppermute | solution.py:63
  15.5 10.3 %collective-permute-start.9 = (bf16[4,2,64,128]{3,2,1,0:T(8,128)(2,1)S(1)}, bf16[4,2,64,128]{3,2,1,0:T(8,128)(2,1)S(1)}, u32[]{:S(2)}, u32[]{:S(2)}) collective-permute-start(bf16[4,2,64,128]{3,2,1,0:T(8,128)(2,1)S(1)} %get-tuple-element.93), channel_id=1, source_target_pairs={{0,24},{8,16},{16,8},{24,0},{1,25},{9,17},{17,9},{25,1},{2,26},{10... | collective-permute-start | bytes 393224 | tf_op jit(solution)/shard_map/ppermute | solution.py:63
  18.3 9.9 %collective-permute-start.10 = (bf16[4,2,64,128]{3,2,1,0:T(8,128)(2,1)S(1)}, bf16[4,2,64,128]{3,2,1,0:T(8,128)(2,1)S(1)}, u32[]{:S(2)}, u32[]{:S(2)}) collective-permute-start(bf16[4,2,64,128]{3,2,1,0:T(8,128)(2,1)S(1)} %get-tuple-element.94), channel_id=1, source_target_pairs={{0,8},{8,0},{16,24},{24,16},{1,9},{9,1},{17,25},{25,17},{2,10},{10... | collective-permute-start | bytes 393224 | tf_op jit(solution)/shard_map/ppermute | solution.py:63
  19.5 18.2 %copy-start.7 = (s32[2,256]{1,0:T(2,128)S(1)}, s32[2,256]{1,0:T(2,128)}, u32[]{:S(2)}) copy-start(s32[2,256]{1,0:T(2,128)} %refs_8_.1) | copy-start | bytes 6148
  19.5 9.9 %collective-permute-start.11 = (bf16[4,2,64,128]{3,2,1,0:T(8,128)(2,1)S(1)}, bf16[4,2,64,128]{3,2,1,0:T(8,128)(2,1)S(1)}, u32[]{:S(2)}, u32[]{:S(2)}) collective-permute-start(bf16[4,2,64,128]{3,2,1,0:T(8,128)(2,1)S(1)} %get-tuple-element.95), channel_id=1, source_target_pairs={{0,16},{8,24},{16,0},{24,8},{1,17},{9,25},{17,1},{25,9},{2,18},{10... | collective-permute-start | bytes 393224 | tf_op jit(solution)/shard_map/ppermute | solution.py:63
  23.4 8.8 %collective-permute-start.3 = (bf16[4,2,64,128]{3,2,1,0:T(8,128)(2,1)S(1)}, bf16[4,2,64,128]{3,2,1,0:T(8,128)(2,1)S(1)}, u32[]{:S(2)}, u32[]{:S(2)}) collective-permute-start(bf16[4,2,64,128]{3,2,1,0:T(8,128)(2,1)S(1)} %get-tuple-element.88), channel_id=1, source_target_pairs={{0,24},{8,16},{16,8},{24,0},{1,25},{9,17},{17,9},{25,1},{2,26},{10... | collective-permute-start | bytes 393224 | tf_op jit(solution)/shard_map/ppermute | solution.py:63
  25.6 8.2 %collective-permute-start.4 = (bf16[4,2,64,128]{3,2,1,0:T(8,128)(2,1)S(1)}, bf16[4,2,64,128]{3,2,1,0:T(8,128)(2,1)S(1)}, u32[]{:S(2)}, u32[]{:S(2)}) collective-permute-start(bf16[4,2,64,128]{3,2,1,0:T(8,128)(2,1)S(1)} %get-tuple-element.89), channel_id=1, source_target_pairs={{0,8},{8,0},{16,24},{24,16},{1,9},{9,1},{17,25},{25,17},{2,10},{10... | collective-permute-start | bytes 393224 | tf_op jit(solution)/shard_map/ppermute | solution.py:63
  25.8 8.2 %collective-permute-start.5 = (bf16[4,2,64,128]{3,2,1,0:T(8,128)(2,1)S(1)}, bf16[4,2,64,128]{3,2,1,0:T(8,128)(2,1)S(1)}, u32[]{:S(2)}, u32[]{:S(2)}) collective-permute-start(bf16[4,2,64,128]{3,2,1,0:T(8,128)(2,1)S(1)} %get-tuple-element.90), channel_id=1, source_target_pairs={{0,16},{8,24},{16,0},{24,8},{1,17},{9,25},{17,1},{25,9},{2,18},{10... | collective-permute-start | bytes 393224 | tf_op jit(solution)/shard_map/ppermute | solution.py:63
  29.4 14.6 %collective-permute-start.17 = (bf16[6,2,32,2,128]{4,3,2,1,0:T(2,128)(2,1)S(1)}, bf16[6,2,32,2,128]{4,3,2,1,0:T(2,128)(2,1)S(1)}, u32[]{:S(2)}, u32[]{:S(2)}) collective-permute-start(bf16[6,2,32,2,128]{4,3,2,1,0:T(2,128)(2,1)S(1)} %get-tuple-element.144), channel_id=1, source_target_pairs={{0,24},{8,16},{16,8},{24,0},{1,25},{9,17},{17,9},{25,1},{2,26},{10... | collective-permute-start | bytes 589832 | tf_op jit(solution)/shard_map/ppermute | solution.py:63
  34.0 11.4 %collective-permute-start.18 = (bf16[6,2,32,2,128]{4,3,2,1,0:T(2,128)(2,1)S(1)}, bf16[6,2,32,2,128]{4,3,2,1,0:T(2,128)(2,1)S(1)}, u32[]{:S(2)}, u32[]{:S(2)}) collective-permute-start(bf16[6,2,32,2,128]{4,3,2,1,0:T(2,128)(2,1)S(1)} %get-tuple-element.145), channel_id=1, source_target_pairs={{0,8},{8,0},{16,24},{24,16},{1,9},{9,1},{17,25},{25,17},{2,10},{10... | collective-permute-start | bytes 589832 | tf_op jit(solution)/shard_map/ppermute | solution.py:63
  35.4 10.9 %collective-permute-start.19 = (bf16[6,2,32,2,128]{4,3,2,1,0:T(2,128)(2,1)S(1)}, bf16[6,2,32,2,128]{4,3,2,1,0:T(2,128)(2,1)S(1)}, u32[]{:S(2)}, u32[]{:S(2)}) collective-permute-start(bf16[6,2,32,2,128]{4,3,2,1,0:T(2,128)(2,1)S(1)} %get-tuple-element.146), channel_id=1, source_target_pairs={{0,16},{8,24},{16,0},{24,8},{1,17},{9,25},{17,1},{25,9},{2,18},{10... | collective-permute-start | bytes 589832 | tf_op jit(solution)/shard_map/ppermute | solution.py:63
  38.9 10.2 %collective-permute-start.15 = (bf16[4,2,64,128]{3,2,1,0:T(8,128)(2,1)S(1)}, bf16[4,2,64,128]{3,2,1,0:T(8,128)(2,1)S(1)}, u32[]{:S(2)}, u32[]{:S(2)}) collective-permute-start(bf16[4,2,64,128]{3,2,1,0:T(8,128)(2,1)S(1)} %get-tuple-element.127), channel_id=1, source_target_pairs={{0,1},{1,2},{2,3},{3,4},{4,5},{5,6},{6,7},{8,9},{9,10},{10,11},{11... | collective-permute-start | bytes 393224 | tf_op jit(solution)/shard_map/ppermute | solution.py:70
  43.6 9.6 %collective-permute-start.12 = (bf16[6,2,32,2,128]{4,3,2,1,0:T(2,128)(2,1)S(1)}, bf16[6,2,32,2,128]{4,3,2,1,0:T(2,128)(2,1)S(1)}, u32[]{:S(2)}, u32[]{:S(2)}) collective-permute-start(bf16[6,2,32,2,128]{4,3,2,1,0:T(2,128)(2,1)S(1)} %get-tuple-element.124), channel_id=1, source_target_pairs={{0,24},{8,16},{16,8},{24,0},{1,25},{9,17},{17,9},{25,1},{2,26},{10... | collective-permute-start | bytes 589832 | tf_op jit(solution)/shard_map/ppermute | solution.py:63
  44.0 11.0 %collective-permute-start.13 = (bf16[6,2,32,2,128]{4,3,2,1,0:T(2,128)(2,1)S(1)}, bf16[6,2,32,2,128]{4,3,2,1,0:T(2,128)(2,1)S(1)}, u32[]{:S(2)}, u32[]{:S(2)}) collective-permute-start(bf16[6,2,32,2,128]{4,3,2,1,0:T(2,128)(2,1)S(1)} %get-tuple-element.125), channel_id=1, source_target_pairs={{0,8},{8,0},{16,24},{24,16},{1,9},{9,1},{17,25},{25,17},{2,10},{10... | collective-permute-start | bytes 589832 | tf_op jit(solution)/shard_map/ppermute | solution.py:63
  45.3 10.2 %collective-permute-start.14 = (bf16[6,2,32,2,128]{4,3,2,1,0:T(2,128)(2,1)S(1)}, bf16[6,2,32,2,128]{4,3,2,1,0:T(2,128)(2,1)S(1)}, u32[]{:S(2)}, u32[]{:S(2)}) collective-permute-start(bf16[6,2,32,2,128]{4,3,2,1,0:T(2,128)(2,1)S(1)} %get-tuple-element.126), channel_id=1, source_target_pairs={{0,16},{8,24},{16,0},{24,8},{1,17},{9,25},{17,1},{25,9},{2,18},{10... | collective-permute-start | bytes 589832 | tf_op jit(solution)/shard_map/ppermute | solution.py:63
  46.3 6.6 %collective-permute-start.16 = (bf16[4,2,64,128]{3,2,1,0:T(8,128)(2,1)S(1)}, bf16[4,2,64,128]{3,2,1,0:T(8,128)(2,1)S(1)}, u32[]{:S(2)}, u32[]{:S(2)}) collective-permute-start(bf16[4,2,64,128]{3,2,1,0:T(8,128)(2,1)S(1)} %get-tuple-element.128), channel_id=1, source_target_pairs={{1,0},{2,1},{3,2},{4,3},{5,4},{6,5},{7,6},{9,8},{10,9},{11,10},{12... | collective-permute-start | bytes 393224 | tf_op jit(solution)/shard_map/ppermute | solution.py:70
  49.2 9.1 %collective-permute-start.20 = (bf16[3,2,64,128]{3,2,1,0:T(8,128)(2,1)S(1)}, bf16[3,2,64,128]{3,2,1,0:T(8,128)(2,1)S(1)}, u32[]{:S(2)}, u32[]{:S(2)}) collective-permute-start(bf16[3,2,64,128]{3,2,1,0:T(8,128)(2,1)S(1)} %get-tuple-element.148), channel_id=1, source_target_pairs={{0,24},{8,16},{16,8},{24,0},{1,25},{9,17},{17,9},{25,1},{2,26},{10... | collective-permute-start | bytes 294920 | tf_op jit(solution)/shard_map/ppermute | solution.py:63
  52.9 11.0 %collective-permute-start.21 = (bf16[3,2,64,128]{3,2,1,0:T(8,128)(2,1)S(1)}, bf16[3,2,64,128]{3,2,1,0:T(8,128)(2,1)S(1)}, u32[]{:S(2)}, u32[]{:S(2)}) collective-permute-start(bf16[3,2,64,128]{3,2,1,0:T(8,128)(2,1)S(1)} %get-tuple-element.149), channel_id=1, source_target_pairs={{0,8},{8,0},{16,24},{24,16},{1,9},{9,1},{17,25},{25,17},{2,10},{10... | collective-permute-start | bytes 294920 | tf_op jit(solution)/shard_map/ppermute | solution.py:63
  53.2 10.7 %collective-permute-start.22 = (bf16[3,2,64,128]{3,2,1,0:T(8,128)(2,1)S(1)}, bf16[3,2,64,128]{3,2,1,0:T(8,128)(2,1)S(1)}, u32[]{:S(2)}, u32[]{:S(2)}) collective-permute-start(bf16[3,2,64,128]{3,2,1,0:T(8,128)(2,1)S(1)} %get-tuple-element.150), channel_id=1, source_target_pairs={{0,16},{8,24},{16,0},{24,8},{1,17},{9,25},{17,1},{25,9},{2,18},{10... | collective-permute-start | bytes 294920 | tf_op jit(solution)/shard_map/ppermute | solution.py:63
  55.5 3.7 %copy-start.1 = (bf16[5,64,2048]{2,1,0:T(8,128)(2,1)S(1)}, bf16[5,64,2048]{2,1,0:T(8,128)(2,1)}, u32[]{:S(2)}) copy-start(bf16[5,64,2048]{2,1,0:T(8,128)(2,1)} %refs_10_.1) | copy-start | bytes 3932164
  55.5 3.7 %copy-start.2 = (bf16[5,64,2048]{2,1,0:T(8,128)(2,1)S(1)}, bf16[5,64,2048]{2,1,0:T(8,128)(2,1)}, u32[]{:S(2)}) copy-start(bf16[5,64,2048]{2,1,0:T(8,128)(2,1)} %refs_11_.1) | copy-start | bytes 3932164
  55.5 3.7 %copy-start.5 = (f32[2048]{0:T(1024)S(1)}, f32[2048]{0:T(1024)}, u32[]{:S(2)}) copy-start(f32[2048]{0:T(1024)} %param.9) | copy-start | bytes 24580
  55.5 3.7 %copy-start.6 = (s32[32,5]{0,1:T(8,128)S(1)}, s32[32,5]{0,1:T(8,128)}, u32[]{:S(2)}) copy-start(s32[32,5]{0,1:T(8,128)} %param.12) | copy-start | bytes 1924
  56.4 7.4 %collective-permute-start.23 = (bf16[3,2,64,128]{3,2,1,0:T(8,128)(2,1)S(1)}, bf16[3,2,64,128]{3,2,1,0:T(8,128)(2,1)S(1)}, u32[]{:S(2)}, u32[]{:S(2)}) collective-permute-start(bf16[3,2,64,128]{3,2,1,0:T(8,128)(2,1)S(1)} %get-tuple-element.152), channel_id=1, source_target_pairs={{0,24},{8,16},{16,8},{24,0},{1,25},{9,17},{17,9},{25,1},{2,26},{10... | collective-permute-start | bytes 294920 | tf_op jit(solution)/shard_map/ppermute | solution.py:63
  57.0 6.8 %collective-permute-start.24 = (bf16[3,2,64,128]{3,2,1,0:T(8,128)(2,1)S(1)}, bf16[3,2,64,128]{3,2,1,0:T(8,128)(2,1)S(1)}, u32[]{:S(2)}, u32[]{:S(2)}) collective-permute-start(bf16[3,2,64,128]{3,2,1,0:T(8,128)(2,1)S(1)} %get-tuple-element.153), channel_id=1, source_target_pairs={{0,8},{8,0},{16,24},{24,16},{1,9},{9,1},{17,25},{25,17},{2,10},{10... | collective-permute-start | bytes 294920 | tf_op jit(solution)/shard_map/ppermute | solution.py:63
  58.2 5.8 %collective-permute-start.25 = (bf16[3,2,64,128]{3,2,1,0:T(8,128)(2,1)S(1)}, bf16[3,2,64,128]{3,2,1,0:T(8,128)(2,1)S(1)}, u32[]{:S(2)}, u32[]{:S(2)}) collective-permute-start(bf16[3,2,64,128]{3,2,1,0:T(8,128)(2,1)S(1)} %get-tuple-element.154), channel_id=1, source_target_pairs={{0,16},{8,24},{16,0},{24,8},{1,17},{9,25},{17,1},{25,9},{2,18},{10... | collective-permute-start | bytes 294920 | tf_op jit(solution)/shard_map/ppermute | solution.py:63
